TPU v7x, 32 devices: a whole 2x2x4 slice. The times are simulated.
32 devices in a mesh: groups: 2 (over x), store: 16 (over z, y, core).
Axes of the slice: x: 2, y: 2, z: 4, core: 2. Of those that a mesh axis runs over, the one named last changes fastest.
Arguments:
- sources: bfloat16 [16384, 512], P(('groups', 'store')), parts along dimension 0, may hold values from -1800 to 1800
- self_terms: float32 [2, 8192], P(None, 'store'), may hold values from 0.5 to 2
- near_tiles: bfloat16 [2, 32, 5, 256, 256], P(None, 'store'), may hold values from -1 to 1
- near_cols: int32 [32, 5], P('store'), may hold values from 0 to 31, as said below
- near_count: int32 [32], P('store'), may hold values from 1 to 5, as said below
- far_cols: int32 [32, 6], P('store'), may hold values from 0 to 31, as said below
- basis_left: bfloat16 [32, 256, 32], P('store'), may hold values from -2 to 2
- basis_right: bfloat16 [32, 256, 32], P('store'), may hold values from -2 to 2
- couplings: bfloat16 [2, 32, 6, 32, 32], P(None, 'store'), may hold values from -1 to 1
Outputs:
- images: float32 [2, 16384, 512], P(None, ('groups', 'store')), parts along dimension 1
- heights: float32 [4, 512], P('groups'), parts along dimension 0
- norms: float32 [4, 512], P('groups'), parts along dimension 0
There are 2 independent parts, one for each index of `groups`. A program takes and returns all parts, laid end to end along the dimension named above; an argument that names none is the same for every part. Nothing has to cross between parts.
Inputs may be any that keep to these rules, and one draw needn't show every extreme that they name: `near_cols`: the slots of row block i name the blocks i - 2 to i + 2, cyclically, each once, in a drawn order. Slots 0 to near_count - 1 of a row block are live; block 0 has all 5. `far_cols`: a far-field block lies more than 2 blocks from its row block, cyclically.
All inputs are finite; a program needn't handle non-finite values.
Results may differ from a plain program's by a relative error of at most 0.011.
Values may be sent and summed in bfloat16 or wider, within the bound.
No kernel may reach another device: no remote copies, remote signals or barrier semaphores. Data moves between devices by JAX's collectives and lax.ppermute only.
A program may use at most 128 MiB of HBM per device.

v0:
```python
import jax
import jax.numpy as jnp
from jax import lax
from jax.sharding import PartitionSpec as P

REACH = 2


EPSILON = 1e-06


def padded_2(block, sides, width):
    for axis, dim in sides:
        count = lax.axis_size(axis)
        forward = [(i, i + 1) for i in range(count - 1)]
        forward.append((count - 1, 0))
        backward = [(target, source) for source, target in forward]
        low = lax.ppermute(
            lax.slice_in_dim(block, block.shape[dim] - width, None, axis=dim), axis, forward
        )
        high = lax.ppermute(lax.slice_in_dim(block, 0, width, axis=dim), axis, backward)
        block = jnp.concatenate([low, block, high], axis=dim)
    return block


def shards(
    sources,
    self_terms,
    near_tiles,
    near_cols,
    near_count,
    far_cols,
    basis_left,
    basis_right,
    couplings,
):
    local_blocks = near_cols.shape[0]
    block_size = near_tiles.shape[-1]
    columns = sources.shape[1]
    all_blocks = local_blocks * lax.axis_size("store")
    all_panels = all_blocks * block_size
    first_block = lax.axis_index("store") * local_blocks
    global_rows = first_block + jnp.arange(local_blocks, dtype=jnp.int32)
    relative = (near_cols - global_rows[:, None] + REACH) % all_blocks - REACH
    extended = jnp.arange(local_blocks, dtype=jnp.int32)[:, None] + REACH + relative
    highest = jnp.max(near_count)
    diagonal = self_terms.reshape(2, local_blocks, block_size)

    def far_rows(inputs):
        coeffs = jnp.einsum(
            "bpr,kbps->kbrs", basis_right, inputs, preferred_element_type=jnp.float32
        ).astype(jnp.bfloat16)
        gathered = lax.all_gather(coeffs, "store", axis=1, tiled=True)
        picked = gathered[:, far_cols]
        picked = jnp.broadcast_to(picked, (2,) + picked.shape[1:])
        reduced = jnp.einsum(
            "obfrq,obfqs->obrs", couplings, picked, preferred_element_type=jnp.float32
        ).astype(jnp.bfloat16)
        return jnp.einsum(
            "bpr,obrs->obps", basis_left, reduced, preferred_element_type=jnp.float32
        ).astype(jnp.bfloat16)

    def operate(inputs):
        padded = padded_2(inputs, (("store", 1),), REACH)

        def add_slot(position, accum):
            which = lax.dynamic_index_in_dim(extended, position, 1, keepdims=False)
            taken = jnp.take(padded, which, axis=1)
            taken = jnp.broadcast_to(taken, (2,) + taken.shape[1:])
            tiles_now = lax.dynamic_index_in_dim(near_tiles, position, 2, keepdims=False)
            product = jnp.einsum(
                "obpq,obqs->obps", tiles_now, taken, preferred_element_type=jnp.float32
            )
            weight = (position < near_count).astype(jnp.float32)
            return accum + product * weight[None, :, None, None]

        start = jnp.zeros((2, local_blocks, block_size, columns), jnp.float32)
        near_part = lax.fori_loop(0, highest, add_slot, start)
        far_part = far_rows(inputs)
        return (
            near_part
            + diagonal[..., None] * inputs.astype(jnp.float32)
            + far_part.astype(jnp.float32)
        )

    source_f = sources.astype(jnp.float32).reshape(local_blocks, block_size, columns)
    scale_sq = lax.psum(jnp.sum(source_f * source_f, axis=(0, 1)), "store") / all_panels
    first_vec = (source_f / jnp.sqrt(scale_sq + EPSILON)).astype(jnp.bfloat16)
    image_one = operate(first_vec[None])
    first_f = first_vec.astype(jnp.float32)
    heights = lax.psum(jnp.sum(first_f[None] * image_one, axis=(1, 2)), "store") / all_panels
    remain = image_one - heights[:, None, None, :] * first_f[None]
    spread = lax.psum(jnp.sum(remain * remain, axis=(1, 2)), "store") / all_panels
    norms = jnp.sqrt(spread + EPSILON)
    second_vec = (remain / norms[:, None, None, :]).astype(jnp.bfloat16)
    image_two = operate(second_vec)
    return (image_two.reshape(2, local_blocks * block_size, columns), heights, norms)


def solution(mesh):
    placed = (
        P(("groups", "store"), None),
        P(None, "store"),
        P(None, "store", None, None, None),
        P("store", None),
        P("store"),
        P("store", None),
        P("store", None, None),
        P("store", None, None),
        P(None, "store", None, None, None),
    )
    return jax.shard_map(
        shards,
        mesh=mesh,
        in_specs=placed,
        out_specs=(P(None, ("groups", "store"), None), P("groups", None), P("groups", None)),
        check_vma=False,
    )
```

profile of v0, /device:TPU:0, one launch (start us, length us, event | category | flops | bytes accessed | tf_op | source)
XLA Modules:
  0.0 223.3 jit_solution(12892225822094660299)
XLA Ops:
  7.2 0.0 all-gather.3.cloned.1.call-start
  7.2 1.2 convert_element_type.97
  8.4 1.2 multiply_reduce_fusion.2
  9.6 34.9 %psum.21 = f32[512]{0:T(512)S(1)} all-reduce(f32[512]{0:T(512)S(1)} %multiply_reduce_fusion.2), channel_id=1, replica_groups=mesh['groups'=2,'store'=16] {'store'}, use_global_device_ids=true, to_apply=%region_2.3 | all-reduce | flops 512 | bytes 4096 | tf_op jit(solution)/shard_map/psum | solution.py:87
  44.5 0.1 divide_convert_fusion.2
  44.7 0.1 collective-permute-start
  44.7 4.4 %collective-permute-start.1 = (bf16[1,2,256,512]{3,2,1,0:T(8,128)(2,1)S(1)}, bf16[1,2,256,512]{3,2,1,0:T(8,128)(2,1)S(1)}, u32[]{:S(2)}, u32[]{:S(2)}) collective-permute-start(bf16[1,2,256,512]{3,2,1,0:T(8,128)(2,1)S(1)} %divide_convert_fusion.2), channel_id=1, source_target_pairs={{1,0},{2,1},{3,2},{4,3},{5,4},{6,5},{7,6},{8,7},{9,8},{10,9},{11,1... | collective-permute-start | bytes 1572872 | tf_op jit(solution)/shard_map/ppermute | solution.py:21
  49.2 1.2 fusion.30
  50.3 0.8 fusion.13
  51.2 0.0 all-gather.3.cloned.1.call-update
  51.2 0.0 all-gather.5.cloned.1.call-start
  51.3 0.1 copy.30
  51.4 3.5 %copy.36 = bf16[2,2,5,256,256]{4,3,1,0,2:T(8,128)(2,1)} copy(bf16[2,2,5,256,256]{4,3,2,1,0:T(8,128)(2,1)} %param.15) | data formatting | bytes 5242880 | tf_op jit(solution)/shard_map/while | solution.py:78
  54.9 0.1 reshape.96
  55.0 0.7 reduce_max.9
  55.7 0.5 collective-permute-done
  56.1 1.3 pad_maximum_fusion.1
  57.5 0.2 broadcast.104.clone
  57.7 23.1 %while.20 = (s32[]{:T(128)}, f32[2,2,256,512]{3,2,1,0:T(8,128)S(1)}, s32[]{:T(128)}, bf16[2,2,5,256,256]{4,3,1,0,2:T(8,128)(2,1)}, s32[2,5]{0,1:T(8,128)S(1)}, /...) while((s32[]{:T(128)}, f32[2,2,256,512]{3,2,1,0:T(8,128)S(1)}, ...), condition=%wide.region_4.5_spmd, body=%wide.region_3.4_spmd.sunk | while | flops 269747232 | bytes 7344335 | solution.py:78
  58.5 2.0 gather_fusion
  60.5 0.1 broadcast_select_fusion.2
  60.6 1.6 multiply_add_fusion.4
  63.0 2.0 gather_fusion
  65.0 0.1 broadcast_select_fusion.2
  65.1 1.6 multiply_add_fusion.4
  67.4 2.0 gather_fusion
  69.4 0.1 broadcast_select_fusion.2
  69.5 1.6 multiply_add_fusion.4
  71.9 2.0 gather_fusion
  73.9 0.1 broadcast_select_fusion.2
  74.1 1.6 multiply_add_fusion.4
  76.4 2.0 gather_fusion
  78.4 0.1 broadcast_select_fusion.2
  78.5 1.6 multiply_add_fusion.4
  80.8 5.7 %all-gather.3.cloned.1.call-done = bf16[1,32,32,512]{3,2,0,1:T(8,128)(2,1)} async-done(((bf16[1,2,32,512]{3,2,0,1:T(8,128)(2,1)}), bf16[1,32,32,512]{3,2,0,1:T(8,128)(2,1)}) %all-gather.3.cloned.1.call-update) | async-done | bytes 1048592 | tf_op jit(solution)/shard_map/all_gather | solution.py:53
  86.5 2.5 %gather_fusion.2 = bf16[12,32,512]{2,1,0:T(8,128)(2,1)} fusion(bf16[32,32,512]{2,1,0:T(8,128)(2,1)} %bitcast.109, s32[1024]{0:T(1024)S(1)} %pad_clamp_fusion.2), kind=kCustom, calls=%fused_computation.2 | custom fusion | bytes 786480 | tf_op jit(solution)/shard_map/gather | solution.py:54
  89.1 3.7 %multiply_reduce_fusion.1 = (f32[2,512]{1,0:T(2,128)S(1)}, f32[2,2,256,512]{3,2,0,1:T(8,128)}) fusion(f32[2,256,512]{2,1,0:T(8,128)} %get-tuple-element.155, bf16[2,256,32]{1,2,0:T(8,128)(2,1)S(1)} %copy-done, bf16[2,6,32,512]{3,2,1,0:T(8,128)(2,1)} %bitcast.108, bf16[2,2,6,32,32]{4,3,2,1,0:T(8,128)(2,1)S(1)} %copy-done.3, f32[2,2,256]{2,0,1:T(2,128)S(1)} %bitcast.112, ...), kind=kOutput, calls=%fused_computation.32 | convolution fusion | flops 62454784 | bytes 5726208 | tf_op jit(solution)/shard_map/bpr,obrs->obps/dot_general | solution.py:59
  92.8 31.7 %psum.22 = f32[2,512]{1,0:T(2,128)S(1)} all-reduce(f32[2,512]{1,0:T(2,128)S(1)} %get-tuple-element.157), channel_id=1, replica_groups=mesh['groups'=2,'store'=16] {'store'}, use_global_device_ids=true, to_apply=%region_6.7 | all-reduce | flops 1024 | bytes 8192 | tf_op jit(solution)/shard_map/psum | solution.py:91
  124.6 2.0 multiply_reduce_fusion
  126.6 29.5 %psum.23 = f32[2,512]{1,0:T(2,128)S(1)} all-reduce(f32[2,512]{1,0:T(2,128)S(1)} %multiply_reduce_fusion), channel_id=1, replica_groups=mesh['groups'=2,'store'=16] {'store'}, use_global_device_ids=true, to_apply=%region_8.9 | all-reduce | flops 1024 | bytes 8192 | tf_op jit(solution)/shard_map/psum | solution.py:93
  156.1 1.4 divide_convert_fusion
  157.5 4.4 %collective-permute-start.3 = (bf16[2,2,256,512]{3,2,0,1:T(8,128)(2,1)}, bf16[2,2,256,512]{3,2,0,1:T(8,128)(2,1)S(1)}, u32[]{:S(2)}, u32[]{:S(2)}) collective-permute-start(bf16[2,2,256,512]{3,2,0,1:T(8,128)(2,1)} %divide_convert_fusion), channel_id=1, source_target_pairs={{1,0},{2,1},{3,2},{4,3},{5,4},{6,5},{7,6},{8,7},{9,8},{10,9},{11,1... | collective-permute-start | bytes 3145736 | tf_op jit(solution)/shard_map/ppermute | solution.py:21
  161.9 2.2 fusion.12
  164.1 0.0 all-gather.5.cloned.1.call-update
  164.1 10.7 %collective-permute-done.2 = bf16[2,2,256,512]{3,2,0,1:T(8,128)(2,1)S(1)} collective-permute-done((bf16[2,2,256,512]{3,2,0,1:T(8,128)(2,1)}, bf16[2,2,256,512]{3,2,0,1:T(8,128)(2,1)S(1)}, u32[]{:S(2)}, u32[]{:S(2)}) %collective-permute-start.2) | collective-permute-done | bytes 1048608 | tf_op jit(solution)/shard_map/ppermute | solution.py:18
  174.9 1.1 collective-permute-done.3
  176.0 1.4 pad_maximum_fusion
  177.4 1.8 copy.37
  179.2 0.2 broadcast.104
  179.5 25.8 %while.21 = (s32[]{:T(128)}, f32[2,2,256,512]{3,2,1,0:T(8,128)S(1)}, s32[]{:T(128)}, bf16[2,2,5,256,256]{4,3,1,0,2:T(8,128)(2,1)}, s32[2,5]{0,1:T(8,128)S(1)}, /...) while((s32[]{:T(128)}, f32[2,2,256,512]{3,2,1,0:T(8,128)S(1)}, ...), condition=%wide.region_10.11_spmd, body=%wide.region_9.10_spmd.sunk | while | flops 270009376 | bytes 7868623 | solution.py:78
  180.2 2.5 %gather_fusion.1 = bf16[2,2,256,512]{3,2,1,0:T(8,128)(2,1)S(1)} fusion(bf16[2,6,256,512]{3,2,1,0:T(8,128)(2,1)} %get-tuple-element.312, s32[1024]{0:T(1024)S(1)} %pad_clamp_fusion.6), kind=kCustom, calls=%fused_computation.1.clone.1 | custom fusion | bytes 2097160 | tf_op jit(solution)/shard_map/while/body/jit(_take)/gather | solution.py:68
  182.8 1.7 multiply_add_fusion.5
  185.2 2.5 %gather_fusion.1 = bf16[2,2,256,512]{3,2,1,0:T(8,128)(2,1)S(1)} fusion(bf16[2,6,256,512]{3,2,1,0:T(8,128)(2,1)} %get-tuple-element.312, s32[1024]{0:T(1024)S(1)} %pad_clamp_fusion.6), kind=kCustom, calls=%fused_computation.1.clone.1 | custom fusion | bytes 2097160 | tf_op jit(solution)/shard_map/while/body/jit(_take)/gather | solution.py:68
  187.7 1.7 multiply_add_fusion.5
  190.1 2.8 %gather_fusion.1 = bf16[2,2,256,512]{3,2,1,0:T(8,128)(2,1)S(1)} fusion(bf16[2,6,256,512]{3,2,1,0:T(8,128)(2,1)} %get-tuple-element.312, s32[1024]{0:T(1024)S(1)} %pad_clamp_fusion.6), kind=kCustom, calls=%fused_computation.1.clone.1 | custom fusion | bytes 2097160 | tf_op jit(solution)/shard_map/while/body/jit(_take)/gather | solution.py:68
  192.9 1.7 multiply_add_fusion.5
  195.4 2.5 %gather_fusion.1 = bf16[2,2,256,512]{3,2,1,0:T(8,128)(2,1)S(1)} fusion(bf16[2,6,256,512]{3,2,1,0:T(8,128)(2,1)} %get-tuple-element.312, s32[1024]{0:T(1024)S(1)} %pad_clamp_fusion.6), kind=kCustom, calls=%fused_computation.1.clone.1 | custom fusion | bytes 2097160 | tf_op jit(solution)/shard_map/while/body/jit(_take)/gather | solution.py:68
  197.9 1.7 multiply_add_fusion.5
  200.3 2.5 %gather_fusion.1 = bf16[2,2,256,512]{3,2,1,0:T(8,128)(2,1)S(1)} fusion(bf16[2,6,256,512]{3,2,1,0:T(8,128)(2,1)} %get-tuple-element.312, s32[1024]{0:T(1024)S(1)} %pad_clamp_fusion.6), kind=kCustom, calls=%fused_computation.1.clone.1 | custom fusion | bytes 2097160 | tf_op jit(solution)/shard_map/while/body/jit(_take)/gather | solution.py:68
  202.9 1.7 multiply_add_fusion.5
  205.3 2.4 %all-gather.5.cloned.1.call-done = bf16[2,32,32,512]{3,2,0,1:T(8,128)(2,1)} async-done(((bf16[2,2,32,512]{3,2,0,1:T(8,128)(2,1)}), bf16[2,32,32,512]{3,2,0,1:T(8,128)(2,1)}) %all-gather.5.cloned.1.call-update) | async-done | bytes 2097168 | tf_op jit(solution)/shard_map/all_gather | solution.py:53
  207.7 2.2 gather_fusion.3
  209.9 3.5 %bitcast_add_fusion = f32[2,2,256,512]{3,2,0,1:T(8,128)} fusion(f32[2,2,256,512]{3,2,1,0:T(8,128)S(1)} %get-tuple-element.80, bf16[2,2,256,512]{3,2,0,1:T(8,128)(2,1)} %divide_convert_fusion, f32[2,2,256]{2,0,1:T(2,128)S(1)} %bitcast.113, bf16[2,6,2,32,512]{4,3,2,1,0:T(8,128)(2,1)S(1)} %bitcast.106, bf16[2,2,6,32,32]{4,3,2,1,0:T(8,128)(2,1)S(1)} %copy-done.3, ...), kind=kOutput, calls=%fused_computation.25 | convolution fusion | flops 61931520 | bytes 6115328 | tf_op jit(solution)/shard_map/bpr,obrs->obps/dot_general | solution.py:59
  213.3 3.1 %copy.41 = f32[2,2,256,512]{3,2,1,0:T(8,128)} copy(f32[2,2,256,512]{3,2,0,1:T(8,128)} %bitcast_add_fusion) | data formatting | bytes 4194304 | tf_op jit(solution)/shard_map/add | solution.py:81
  (61 shorter events, 0.4 us)
Async XLA Ops:
  7.2 81.9 %copy-start = (bf16[2,256,32]{1,2,0:T(8,128)(2,1)S(1)}, bf16[2,256,32]{1,2,0:T(8,128)(2,1)}, u32[]{:S(2)}) copy-start(bf16[2,256,32]{1,2,0:T(8,128)(2,1)} %param.19) | copy-start | bytes 98308
  7.2 79.4 %all-gather.3.cloned.1.call-start = ((), (), s32[]{:S(2)}) async-start(), calls=%async_computation | async-start | bytes 1114112 | tf_op jit(solution)/shard_map/all_gather | solution.py:53
  44.5 5.8 %copy-start.4 = (bf16[2,256,32]{1,2,0:T(8,128)(2,1)S(1)}, bf16[2,256,32]{1,2,0:T(8,128)(2,1)}, u32[]{:S(2)}) copy-start(bf16[2,256,32]{1,2,0:T(8,128)(2,1)} %param.20) | copy-start | bytes 98308
  44.5 6.7 %copy-start.9 = (s32[2,6]{1,0:T(2,128)S(1)}, s32[2,6]{1,0:T(2,128)}, u32[]{:S(2)}) copy-start(s32[2,6]{1,0:T(2,128)} %param.18) | copy-start | bytes 148
  44.5 6.7 %copy-start.8 = (s32[2,5]{1,0:T(2,128)S(1)}, s32[2,5]{1,0:T(2,128)}, u32[]{:S(2)}) copy-start(s32[2,5]{1,0:T(2,128)} %param.16) | copy-start | bytes 124
  44.7 11.5 %collective-permute-start = (bf16[1,2,256,512]{3,2,1,0:T(8,128)(2,1)S(1)}, bf16[1,2,256,512]{3,2,1,0:T(8,128)(2,1)S(1)}, u32[]{:S(2)}, u32[]{:S(2)}) collective-permute-start(bf16[1,2,256,512]{3,2,1,0:T(8,128)(2,1)S(1)} %divide_convert_fusion.2), channel_id=1, source_target_pairs={{0,1},{1,2},{2,3},{3,4},{4,5},{5,6},{6,7},{7,8},{8,9},{9,10},{10,1... | collective-permute-start | bytes 1572872 | tf_op jit(solution)/shard_map/ppermute | solution.py:18
  44.7 11.4 %collective-permute-start.1 = (bf16[1,2,256,512]{3,2,1,0:T(8,128)(2,1)S(1)}, bf16[1,2,256,512]{3,2,1,0:T(8,128)(2,1)S(1)}, u32[]{:S(2)}, u32[]{:S(2)}) collective-permute-start(bf16[1,2,256,512]{3,2,1,0:T(8,128)(2,1)S(1)} %divide_convert_fusion.2), channel_id=1, source_target_pairs={{1,0},{2,1},{3,2},{4,3},{5,4},{6,5},{7,6},{8,7},{9,8},{10,9},{11,1... | collective-permute-start | bytes 1572872 | tf_op jit(solution)/shard_map/ppermute | solution.py:21
  51.2 156.5 %all-gather.5.cloned.1.call-start = ((), (), s32[]{:S(2)}) async-start(), calls=%async_computation.1 | async-start | bytes 2228224 | tf_op jit(solution)/shard_map/all_gather | solution.py:53
  51.4 3.6 %copy-start.10 = (s32[2]{0:T(128)S(1)}, s32[2]{0:T(128)}, u32[]{:S(2)}) copy-start(s32[2]{0:T(128)} %param.17) | copy-start | bytes 28
  57.7 31.4 %copy-start.3 = (bf16[2,2,6,32,32]{4,3,2,1,0:T(8,128)(2,1)S(1)}, bf16[2,2,6,32,32]{4,3,2,1,0:T(8,128)(2,1)}, u32[]{:S(2)}) copy-start(bf16[2,2,6,32,32]{4,3,2,1,0:T(8,128)(2,1)} %param.21) | copy-start | bytes 147460
  57.7 31.4 %copy-start.7 = (f32[2,512]{1,0:T(2,128)S(1)}, f32[2,512]{1,0:T(2,128)}, u32[]{:S(2)}) copy-start(f32[2,512]{1,0:T(2,128)} %param.14) | copy-start | bytes 12292
  89.1 35.5 %copy-start.2 = (f32[2,256,512]{2,1,0:T(8,128)S(1)}, f32[2,256,512]{2,1,0:T(8,128)}, u32[]{:S(2)}) copy-start(f32[2,256,512]{2,1,0:T(8,128)} %get-tuple-element.155) | copy-start | bytes 3145732
  92.8 63.2 %copy-start.1 = (f32[2,2,256,512]{3,2,0,1:T(8,128)S(1)}, f32[2,2,256,512]{3,2,0,1:T(8,128)}, u32[]{:S(2)}) copy-start(f32[2,2,256,512]{3,2,0,1:T(8,128)} %get-tuple-element.158) | copy-start | bytes 6291460
  124.6 32.9 %copy-start.5 = (f32[2,512]{1,0:T(2,128)}, f32[2,512]{1,0:T(2,128)S(1)}, u32[]{:S(2)}) copy-start(f32[2,512]{1,0:T(2,128)S(1)} %broadcast_multiply_fusion) | copy-start | bytes 12292
  156.1 1.4 copy-start.6
  157.5 17.4 %collective-permute-start.2 = (bf16[2,2,256,512]{3,2,0,1:T(8,128)(2,1)}, bf16[2,2,256,512]{3,2,0,1:T(8,128)(2,1)S(1)}, u32[]{:S(2)}, u32[]{:S(2)}) collective-permute-start(bf16[2,2,256,512]{3,2,0,1:T(8,128)(2,1)} %divide_convert_fusion), channel_id=1, source_target_pairs={{0,1},{1,2},{2,3},{3,4},{4,5},{5,6},{6,7},{7,8},{8,9},{9,10},{10,1... | collective-permute-start | bytes 3145736 | tf_op jit(solution)/shard_map/ppermute | solution.py:18
  157.5 18.5 %collective-permute-start.3 = (bf16[2,2,256,512]{3,2,0,1:T(8,128)(2,1)}, bf16[2,2,256,512]{3,2,0,1:T(8,128)(2,1)S(1)}, u32[]{:S(2)}, u32[]{:S(2)}) collective-permute-start(bf16[2,2,256,512]{3,2,0,1:T(8,128)(2,1)} %divide_convert_fusion), channel_id=1, source_target_pairs={{1,0},{2,1},{3,2},{4,3},{5,4},{6,5},{7,6},{8,7},{9,8},{10,9},{11,1... | collective-permute-start | bytes 3145736 | tf_op jit(solution)/shard_map/ppermute | solution.py:21
Sparse Core Ops, SparseCore 0:
  51.3 35.1 all-gather.2
  164.3 43.3 all-gather.4
where the time goes:
time: 225 us; the launch traced here: 223 us
  blocking collectives  96.1 us (43%)
  local copies, waits for them, and re-layouts  36.8 us (16%)
  matrix products  26.7 us (12%)
  waiting for transfers between devices  20.4 us (9%)
  between operations  14.2 us (6%)
  other arithmetic  11.3 us (5%)
  starting transfers between devices  9.01 us (4%)
  loops' own time  8.67 us (4%)
    psum x1, blocking collectives, shards(): lax.psum(jnp.sum(source_f * source_f, axis=(0, 1)), 'store') / all_panels  34.9 us
    psum x1, blocking collectives, shards(): lax.psum(jnp.sum(first_f[None] * image_one, axis=(1, 2)), 'store')  31.7 us
    psum x1, blocking collectives, shards(): lax.psum(jnp.sum(remain * remain, axis=(1, 2)), 'store') / all_panels  29.5 us
    gather x10, local copies, waits for them, and re-layouts, add_slot(): taken = jnp.take(padded, which, axis=1)  22.8 us
    dot_general x10, matrix products, add_slot(): jnp.einsum('obpq,obqs->obps', tiles_now, taken, preferred_element_type=jn...  16.5 us
    ppermute x2, waiting for transfers between devices, padded_2(): lax.ppermute(lax.slice_in_dim(block, block.shape[dim] - width, None, axis...  11.2 us
    ppermute x2, starting transfers between devices, padded_2(): lax.ppermute(lax.slice_in_dim(block, 0, width, axis=dim), axis, backward)  8.87 us
    another operation x2, loops' own time, operate(): near_part = lax.fori_loop(0, highest, add_slot, start)  8.67 us
  transfers between devices with their start and end apart: 6, of which 5 were waited for; matrix products, arithmetic and copies ran while one was open for 24% of the time, Pallas kernels for 0%

commit v1 on v0

v1 whole, which is shorter than its diff:
```python
import functools

import jax
import jax.numpy as jnp
from jax import lax
from jax.experimental import pallas as pl
from jax.experimental.pallas import tpu as pltpu
from jax.sharding import PartitionSpec as P

REACH = 2
EPSILON = 1e-06
SLICE = 128
STATS = 16
F32 = jnp.float32
BF16 = jnp.bfloat16

VMEM = pl.BlockSpec(memory_space=pltpu.VMEM)
SMEM = pl.BlockSpec(memory_space=pltpu.SMEM)


def call(body, out_shape, in_specs, scratch=(), flops=0, nbytes=0):
    many = isinstance(out_shape, (list, tuple))
    return pl.pallas_call(
        body,
        out_shape=out_shape,
        in_specs=in_specs,
        out_specs=[VMEM] * len(out_shape) if many else VMEM,
        scratch_shapes=list(scratch),
        compiler_params=pltpu.CompilerParams(vmem_limit_bytes=40 * 1024 * 1024),
        cost_estimate=pl.CostEstimate(flops=flops, bytes_accessed=nbytes, transcendentals=0),
    )


def dot(a, b, dims=((1,), (0,))):
    return lax.dot_general(a, b, (dims, ((), ())), preferred_element_type=F32)


def split3(row):
    high = row.astype(BF16)
    rest = row - high.astype(F32)
    middle = rest.astype(BF16)
    low = (rest - middle.astype(F32)).astype(BF16)
    return [high, middle, low]


def join3(rows, at):
    return rows[..., 3 * at, :] + rows[..., 3 * at + 1, :] + rows[..., 3 * at + 2, :]


def order_tiles(all_blocks, cols, count, row0, tiles, out):
    ops, blocks, near, size, _ = tiles.shape
    for b in range(blocks):
        for k in range(near):
            rel = lax.rem(cols[b, k] - (row0[0] + b) + REACH + all_blocks, all_blocks)
            rel = lax.rem(rel, all_blocks)
            at = pl.multiple_of(rel * size, size)
            live = k < count[b]
            for o in range(ops):
                tile = tiles[o, b, k]
                out[b, o * size:(o + 1) * size, pl.ds(at, size)] = jnp.where(
                    live, tile, jnp.zeros_like(tile)
                )


def coeff_kernel(u, right, out):
    blocks, size, rank = right.shape
    n = out.shape[0]
    slices = u.shape[1] // SLICE
    for b in range(blocks):
        z = dot(right[b], u[b * size:(b + 1) * size, :], ((0,), (0,))).astype(BF16)
        for a in range(slices):
            part = z[:, a * SLICE:(a + 1) * SLICE]

            def put(g, _, part=part, a=a, b=b):
                out[a * (n // slices) + g, b * rank:(b + 1) * rank, :] = part
                return 0

            lax.fori_loop(0, n // slices, put, 0)


def couple(cols, coup, a, b, blocks, ops, rank, source):
    far = coup.shape[2] // rank
    at = (a * blocks + b) * far
    picked = []
    for f in range(far):
        start = pl.multiple_of(cols[at + f] * rank, rank)
        picked.append(source(start))
    return jnp.concatenate(picked, axis=0)


def first_couple(ops, blocks, rank, cols, z, coup, out):
    slices = out.shape[0]
    for a in range(slices):
        for b in range(blocks):
            picked = couple(cols, coup, a, b, blocks, ops, rank, lambda s: z[pl.ds(s, rank), :])
            lhs = coup[a, b * ops * rank:(b + 1) * ops * rank, :]
            res = dot(lhs, picked).astype(BF16)
            for o in range(ops):
                row = (o * blocks + b) * rank
                out[a, row:row + rank, :] = res[o * rank:(o + 1) * rank]


def image_kernel(n, w, low, own, high, diag, left, right, cmsg, vout, mout, ext, image, coef):
    ops = vout.shape[0] // own.shape[0]
    blocks, size, rank = right.shape
    rows, columns = own.shape
    slices = columns // SLICE
    ext[0:rows, :] = low[...]
    ext[rows:2 * rows, :] = own[...]
    ext[2 * rows:, :] = high[...]
    for a in range(slices):
        coef[:, a * SLICE:(a + 1) * SLICE] = cmsg[a]
    near = w.shape[2]
    inner = [None] * ops
    squares = None
    for b in range(blocks):
        base = rows + (b - REACH) * size
        product = dot(w[b], ext[base:base + near, :])
        ub = own[b * size:(b + 1) * size, :].astype(F32)
        part = jnp.sum(ub * ub, axis=0, keepdims=True)
        squares = part if squares is None else squares + part
        for o in range(ops):
            row = (o * blocks + b) * rank
            far = dot(left[b], coef[row:row + rank, :]).astype(BF16).astype(F32)
            value = (
                product[o * size:(o + 1) * size]
                + diag[b * size:(b + 1) * size, o:o + 1] * ub
                + far
            )
            image[o, b * size:(b + 1) * size, :] = value
            part = jnp.sum(ub * value, axis=0, keepdims=True)
            inner[o] = part if inner[o] is None else inner[o] + part
    stats = []
    shifts = []
    spreads = []
    good = squares > 0
    for o in range(ops):
        shift = jnp.where(good, inner[o] / jnp.where(good, squares, 1.0), 0.0)
        pieces = split3(shift)
        stats += pieces
        shift = pieces[0].astype(F32) + pieces[1].astype(F32) + pieces[2].astype(F32)
        shifts.append(pieces)
        spread = None
        for b in range(blocks):
            ub = own[b * size:(b + 1) * size, :].astype(F32)
            v = image[o, b * size:(b + 1) * size, :] - shift * ub
            part = jnp.sum(v * v, axis=0, keepdims=True)
            spread = part if spread is None else spread + part
            v = v.astype(BF16)
            vout[(o * blocks + b) * size:(o * blocks + b + 1) * size, :] = v
            z = dot(right[b], v, ((0,), (0,))).astype(BF16)
            row = (o * blocks + b) * rank
            for a in range(slices):
                part = z[:, a * SLICE:(a + 1) * SLICE]

                def put(g, _, part=part, a=a, row=row):
                    mout[a * (n // slices) + g, row:row + rank, :] = part
                    return 0

                lax.fori_loop(0, n // slices, put, 0)
        spreads.append(spread)
    zero = jnp.zeros((1, columns), BF16)
    edge = sum(shifts, [])
    vout[ops * rows:, :] = jnp.concatenate(edge + [zero] * (STATS - len(edge)), axis=0)
    stats += split3(squares)
    for spread in spreads:
        stats += split3(spread)
    stats = jnp.concatenate(stats + [zero] * (STATS - len(stats)), axis=0)
    base = ops * blocks * rank
    for a in range(slices):
        part = stats[:, a * SLICE:(a + 1) * SLICE]

        def put_stats(g, _, part=part, a=a):
            mout[a * (n // slices) + g, base:base + STATS, :] = part
            return 0

        lax.fori_loop(0, n // slices, put_stats, 0)


def second_couple(panels, ops, blocks, rank, cols, z1, msg, coup, out, zs):
    n = msg.shape[0]
    slices = out.shape[0]
    body = ops * blocks * rank
    st = msg[:, body:body + STATS, :].astype(F32)
    shift = [join3(st, o) for o in range(ops)]
    squares = join3(st, ops)
    scale_sq = jnp.sum(squares, axis=0, keepdims=True) / panels + EPSILON
    reverse = 1.0 / jnp.sqrt(scale_sq)
    heights, norms = [], []
    for o in range(ops):
        total = jnp.sum(shift[o] * squares, axis=0, keepdims=True) / panels
        height = total / scale_sq
        delta = shift[o] - height
        spread = join3(st, ops + 1 + o) + delta * delta * squares
        norm = jnp.sqrt(jnp.sum(spread, axis=0, keepdims=True) / panels / scale_sq + EPSILON)
        heights.append(height)
        norms.append(norm)
        factor = reverse / norm
        zs[ops, 0:n, :] = delta

        def put(d, _, o=o, factor=factor):
            change = zs[ops, pl.ds(d, 1), :]
            for b in range(blocks):
                row = (o * blocks + b) * rank
                at = pl.multiple_of((d * blocks + b) * rank, rank)
                z = msg[d, row:row + rank, :].astype(F32) + change * z1[pl.ds(at, rank), :].astype(F32)
                zs[o, pl.ds(at, rank), :] = z * factor
            return 0

        lax.fori_loop(0, n, put, 0, unroll=4)
    for a in range(slices):
        for b in range(blocks):
            for o in range(ops):
                picked = couple(
                    cols, coup, a, b, blocks, ops, rank, lambda s, o=o: zs[o, pl.ds(s, rank), :]
                ).astype(BF16)
                row = (b * ops + o) * rank
                res = dot(coup[a, row:row + rank, :], picked).astype(BF16)
                row = (o * blocks + b) * rank
                out[a, row:row + rank, :] = res
    rows = []
    for row in heights + norms + [reverse]:
        rows += split3(row)
    rows += [jnp.zeros_like(rows[0])] * (STATS - len(rows))
    rows = jnp.concatenate(rows, axis=0)
    for a in range(slices):
        out[a, body:body + STATS, :] = rows


def final_kernel(
    w, ulow, uown, uhigh, vlow, vown, vhigh, diag, left, cmsg, images, heights, norms, ext, coef, stat
):
    ops = images.shape[0]
    blocks, size, rank = left.shape
    rows, columns = uown.shape
    slices = columns // SLICE
    body = ops * blocks * rank
    for a in range(slices):
        coef[:, a * SLICE:(a + 1) * SLICE] = cmsg[a, 0:body, :]
        stat[:, a * SLICE:(a + 1) * SLICE] = cmsg[a, body:, :].astype(F32)
    st = stat[...]

    def row3(values, at):
        return values[3 * at:3 * at + 1] + values[3 * at + 1:3 * at + 2] + values[3 * at + 2:3 * at + 3]

    reverse = row3(st, 2 * ops)
    near = w.shape[2]
    for o in range(ops):
        height = row3(st, o)
        norm = row3(st, ops + o)
        heights[o:o + 1, :] = height
        norms[o:o + 1, :] = norm
        factor = reverse / norm
        for at, (u, v) in enumerate(((ulow, vlow), (uown, vown), (uhigh, vhigh))):
            shift = row3(v[ops * rows:, :].astype(F32), o)
            change = (shift - height) * factor
            value = v[o * rows:(o + 1) * rows, :].astype(F32) * factor + u[...].astype(F32) * change
            ext[at * rows:(at + 1) * rows, :] = value.astype(BF16)
        for b in range(blocks):
            base = rows + (b - REACH) * size
            product = dot(w[b, o * size:(o + 1) * size, :], ext[base:base + near, :])
            row = (o * blocks + b) * rank
            far = dot(left[b], coef[row:row + rank, :]).astype(BF16).astype(F32)
            mine = ext[rows + b * size:rows + (b + 1) * size, :].astype(F32)
            images[o, b * size:(b + 1) * size, :] = (
                product + diag[b * size:(b + 1) * size, o:o + 1] * mine + far
            )


def ring(block):
    count = lax.axis_size("store")
    forward = [(i, (i + 1) % count) for i in range(count)]
    backward = [(target, source) for source, target in forward]
    return lax.ppermute(block, "store", forward), lax.ppermute(block, "store", backward)


def shards(
    sources,
    self_terms,
    near_tiles,
    near_cols,
    near_count,
    far_cols,
    basis_left,
    basis_right,
    couplings,
):
    n = lax.axis_size("store")
    ops, blocks, near, size, _ = near_tiles.shape
    rank = basis_left.shape[2]
    far = far_cols.shape[1]
    rows, columns = sources.shape
    slices = columns // SLICE
    lanes = n // slices
    all_blocks = blocks * n
    groups = [[a * lanes + g for a in range(slices)] for g in range(lanes)]
    sds = jax.ShapeDtypeStruct

    def exchange(x, part):
        return lax.all_to_all(
            x, "store", 0, 0, axis_index_groups=groups if part else None, tiled=True
        )

    row0 = (lax.axis_index("store") * blocks).astype(jnp.int32).reshape(1)
    diag = self_terms.T

    z_out = call(coeff_kernel, sds((n, blocks * rank, SLICE), BF16), [VMEM, VMEM])(
        sources, basis_right
    )
    z1 = exchange(z_out, False).reshape(n * blocks * rank, SLICE)
    low, high = ring(sources)

    mine = jnp.transpose(couplings, (1, 0, 3, 2, 4)).reshape(blocks * ops * rank, far * rank)
    names = jnp.pad(far_cols.astype(BF16).reshape(1, blocks * far), ((0, STATS - 1), (0, far * rank - blocks * far)))
    mine = jnp.concatenate([mine, names], axis=0)
    held = exchange(jnp.broadcast_to(mine[None], (slices,) + mine.shape), True)
    cols = held[:, blocks * ops * rank, :blocks * far].astype(jnp.int32).reshape(-1)

    w = call(
        functools.partial(order_tiles, all_blocks),
        sds((blocks, ops * size, near * size), BF16),
        [SMEM, SMEM, SMEM, VMEM],
    )(near_cols, near_count, row0, near_tiles)

    body = ops * blocks * rank
    c1 = call(
        functools.partial(first_couple, ops, blocks, rank),
        sds((slices, body, SLICE), BF16),
        [SMEM, VMEM, VMEM],
    )(cols, z1, held)
    c1 = exchange(c1, True)

    v, msg = call(
        functools.partial(image_kernel, n),
        [sds((ops * rows + STATS, columns), BF16), sds((n, body + STATS, SLICE), BF16)],
        [VMEM] * 8,
        [
            pltpu.VMEM((3 * rows, columns), BF16),
            pltpu.VMEM((ops, rows, columns), F32),
            pltpu.VMEM((body, columns), BF16),
        ],
        flops=2 * ops * rows * near * size * columns,
    )(w, low, sources, high, diag, basis_left, basis_right, c1)
    msg = exchange(msg, False)
    vlow, vhigh = ring(v)

    c2 = call(
        functools.partial(second_couple, all_blocks * size, ops, blocks, rank),
        sds((slices, body + STATS, SLICE), BF16),
        [SMEM, VMEM, VMEM, VMEM],
        [pltpu.VMEM((ops + 1, n * blocks * rank, SLICE), F32)],
    )(cols, z1, msg, held)
    c2 = exchange(c2, True)

    images, heights, norms = call(
        final_kernel,
        [sds((ops, rows, columns), F32), sds((ops, columns), F32), sds((ops, columns), F32)],
        [VMEM] * 10,
        [
            pltpu.VMEM((3 * rows, columns), BF16),
            pltpu.VMEM((body, columns), BF16),
            pltpu.VMEM((STATS, columns), F32),
        ],
        flops=2 * ops * rows * near * size * columns,
    )(w, low, sources, high, vlow, v, vhigh, diag, basis_left, c2)
    return images, heights, norms


def solution(mesh):
    placed = (
        P(("groups", "store"), None),
        P(None, "store"),
        P(None, "store", None, None, None),
        P("store", None),
        P("store"),
        P("store", None),
        P("store", None, None),
        P("store", None, None),
        P(None, "store", None, None, None),
    )
    return jax.shard_map(
        shards,
        mesh=mesh,
        in_specs=placed,
        out_specs=(P(None, ("groups", "store"), None), P("groups", None), P("groups", None)),
        check_vma=False,
    )
```

time: 225 us -> 113 us (0.50)
  blocking collectives: 96.1 us -> 0 us
  starting transfers between devices: 9.01 us -> 44.6 us
  matrix products: 26.7 us -> 0 us
  local copies, waits for them, and re-layouts: 36.8 us -> 16.8 us
  Pallas kernels: 0 us -> 15 us
  waiting for transfers between devices: 20.4 us -> 34 us
  between operations: 14.2 us -> 0.82 us
  other arithmetic: 11.3 us -> 0.78 us
  loops' own time: 8.67 us -> 0 us
    psum x3 -> x0, blocking collectives: 96.1 us -> none  [the longest x1 34.9 us: shards(): lax.psum(jnp.sum(source_f * source_f, axis=(0, 1)), 'store') / all_panels]
    all_to_all x0 -> x5, starting transfers between devices: none -> 35.8 us  [exchange(): lax.all_to_all(x, 'store', 0, 0, axis_index_groups=groups if part else No...]
    all_to_all x0 -> x5, waiting for transfers between devices: none -> 34 us  [exchange(): lax.all_to_all(x, 'store', 0, 0, axis_index_groups=groups if part else No...]
    gather x12 -> x0, local copies, waits for them, and re-layouts: 27.6 us -> none  [the longest x10 22.8 us: add_slot(): taken = jnp.take(padded, which, axis=1)]
    dot_general x14 -> x0, matrix products: 26.7 us -> none  [the longest x10 16.5 us: add_slot(): jnp.einsum('obpq,obqs->obps', tiles_now, taken, preferred_element_type=jn...]
    pallas_call x0 -> x6, Pallas kernels: none -> 15 us  [the longest x1 5.61 us: shards(): call(final_kernel, [sds((ops, rows, columns), F32), sds((ops, columns), F...]
    unnamed x23 -> x41, local copies, waits for them, and re-layouts: 0.15 us -> 14.5 us
    ppermute x4, waiting for transfers between devices: 12.3 us -> 0.01 us  [the longest x2 0.01 us: ring(): lax.ppermute(block, 'store', backward)]
  transfers between devices with their start and end apart: 6 -> 9, of which waited for: 5 -> 5; matrix products, arithmetic and copies ran while one was open for 24% -> 2% of each run, Pallas kernels for 0% -> 4%
where the time goes in v1:
time: 113 us; the launch traced here: 112 us
  starting transfers between devices  44.6 us (39%)
  waiting for transfers between devices  34 us (30%)
  local copies, waits for them, and re-layouts  16.8 us (15%)
  Pallas kernels  15 us (13%)
    all_to_all x5, starting transfers between devices, exchange(): lax.all_to_all(x, 'store', 0, 0, axis_index_groups=groups if part else No...  35.8 us
    all_to_all x5, waiting for transfers between devices, exchange(): lax.all_to_all(x, 'store', 0, 0, axis_index_groups=groups if part else No...  34 us
    unnamed x41, local copies, waits for them, and re-layouts  14.5 us
    ppermute x2, starting transfers between devices, ring(): lax.ppermute(block, 'store', backward)  8.77 us
    pallas_call x1, Pallas kernels, shards(): call(final_kernel, [sds((ops, rows, columns), F32), sds((ops, columns), F...  5.61 us
    pallas_call x1, Pallas kernels, shards(): call(functools.partial(image_kernel, n), [sds((ops * rows + STATS, column...  4.57 us
  transfers between devices with their start and end apart: 9, of which 5 were waited for; matrix products, arithmetic and copies ran while one was open for 2% of the time, Pallas kernels for 4%

profile of v1, /device:TPU:0, one launch (start us, length us, event | category | flops | bytes accessed | tf_op | source)
XLA Modules:
  0.0 111.9 jit_solution(11263984037184906154)
XLA Ops:
  0.6 0.0 copy-start.3
  0.6 0.7 convert_element_type.12
  1.4 0.1 reshape.28
  1.5 1.1 copy.18
  2.5 0.0 copy-start.17
  2.6 0.0 copy-start.18
  2.6 0.1 reshape.24
  2.7 0.0 copy-start.15
  2.8 0.0 copy-start.16
  2.8 0.1 copy.20
  2.9 0.7 broadcast_in_dim.2
  3.6 6.3 %all-to-all-start = ((bf16[4,144,192]{2,1,0:T(8,128)(2,1)}), bf16[4,144,192]{2,1,0:T(8,128)(2,1)S(1)}, u32[]{:S(2)}, u32[]{:S(2)}) async-start(bf16[4,144,192]{2,1,0:T(8,128)(2,1)} %broadcast_in_dim.2), calls=%async_computation | async-start | bytes 589824 | tf_op jit(solution)/shard_map/all_to_all | solution.py:300
  9.9 0.9 copy.23.right
  10.8 0.0 copy-done.3
  10.8 0.0 copy-start.13
  10.8 1.2 %shard_map.113 = bf16[16,64,128]{2,1,0:T(8,128)(2,1)} custom-call(bf16[512,512]{1,0:T(8,128)(2,1)S(1)} %copy-done.3, bf16[2,256,32]{2,1,0:T(8,128)(2,1)S(1)} %copy.23.right), custom_call_target="tpu_custom_call" | custom-call | tf_op jit(solution)/shard_map/pallas_call | solution.py:307
  12.0 7.6 %all-to-all-done.coup = bf16[4,144,192]{2,1,0:T(8,128)(2,1)S(1)} async-done(((bf16[4,144,192]{2,1,0:T(8,128)(2,1)}), bf16[4,144,192]{2,1,0:T(8,128)(2,1)S(1)}, u32[]{:S(2)}, u32[]{:S(2)}) %all-to-all-start) | async-done | bytes 221216 | tf_op jit(solution)/shard_map/all_to_all | solution.py:300
  19.5 0.0 copy-done.13
  19.5 3.8 %all-to-all-start.1 = ((bf16[16,64,128]{2,1,0:T(8,128)(2,1)}), bf16[16,64,128]{2,1,0:T(8,128)(2,1)S(1)}, u32[]{:S(2)}, u32[]{:S(2)}) async-start(bf16[16,64,128]{2,1,0:T(8,128)(2,1)} %shard_map.113), calls=%async_computation.1 | async-start | bytes 524288 | tf_op jit(solution)/shard_map/all_to_all | solution.py:300
  23.3 4.4 %collective-permute-start.1 = (bf16[512,512]{1,0:T(8,128)(2,1)S(1)}, bf16[512,512]{1,0:T(8,128)(2,1)}, u32[]{:S(2)}, u32[]{:S(2)}) collective-permute-start(bf16[512,512]{1,0:T(8,128)(2,1)S(1)} %copy-done.3), channel_id=1, source_target_pairs={{1,0},{2,1},{3,2},{4,3},{5,4},{6,5},{7,6},{8,7},{9,8},{10,9},{11,1... | collective-permute-start | bytes 1572872 | tf_op jit(solution)/shard_map/ppermute | solution.py:274
  27.7 0.0 collective-permute-start
  27.7 0.1 reshape.27.cols
  27.8 5.6 %all-to-all-done.1 = bf16[16,64,128]{2,1,0:T(8,128)(2,1)S(1)} async-done(((bf16[16,64,128]{2,1,0:T(8,128)(2,1)}), bf16[16,64,128]{2,1,0:T(8,128)(2,1)S(1)}, u32[]{:S(2)}, u32[]{:S(2)}) %all-to-all-start.1) | async-done | bytes 262176 | tf_op jit(solution)/shard_map/all_to_all | solution.py:300
  33.4 1.5 %shard_map.114 = bf16[4,128,128]{2,1,0:T(8,128)(2,1)} custom-call(s32[48]{0:T(128)S(1)} %reshape.27.cols, bf16[1024,128]{1,0:T(8,128)(2,1)S(1)} %bitcast.6, bf16[4,144,192]{2,1,0:T(8,128)(2,1)S(1)} %all-to-all-done.coup), custom_call_target="tpu_custom_call" | custom-call | tf_op jit(solution)/shard_map/pallas_call | solution.py:326
  34.8 7.2 %all-to-all-start.2 = ((bf16[4,128,128]{2,1,0:T(8,128)(2,1)}), bf16[4,128,128]{2,1,0:T(8,128)(2,1)}, u32[]{:S(2)}, u32[]{:S(2)}) async-start(bf16[4,128,128]{2,1,0:T(8,128)(2,1)} %shard_map.114), calls=%async_computation.2 | async-start | bytes 262144 | tf_op jit(solution)/shard_map/all_to_all | solution.py:300
  42.1 0.0 copy-done.17
  42.1 0.7 copy.22.left
  42.8 0.0 copy-done.18
  42.8 0.9 copy.17
  43.7 0.0 copy-done.1
  43.7 0.0 copy-done.15
  43.7 0.0 copy-done.16
  43.7 0.0 copy-start
  43.7 1.7 %copy-done = bf16[2,2,5,256,256]{4,3,2,1,0:T(8,128)(2,1)S(1)} copy-done((bf16[2,2,5,256,256]{4,3,2,1,0:T(8,128)(2,1)S(1)}, bf16[2,2,5,256,256]{4,3,2,1,0:T(8,128)(2,1)}, u32[]{:S(2)}) %copy-start) | copy-done | bytes 2621464
  45.4 0.9 shard_map.112.w
  46.3 0.0 collective-permute-done.1.high.uhigh
  46.3 0.0 collective-permute-done.low.ulow
  46.3 2.3 %all-to-all-done.2.cmsg = bf16[4,128,128]{2,1,0:T(8,128)(2,1)} async-done(((bf16[4,128,128]{2,1,0:T(8,128)(2,1)}), bf16[4,128,128]{2,1,0:T(8,128)(2,1)}, u32[]{:S(2)}, u32[]{:S(2)}) %all-to-all-start.2) | async-done | bytes 131104 | tf_op jit(solution)/shard_map/all_to_all | solution.py:300
  48.6 0.9 copy-done.7
  49.5 0.0 copy-start.11
  49.5 0.9 copy-done.11
  50.4 0.0 copy-start.14
  50.4 0.9 copy-done.14
  51.3 4.6 %shard_map.115 = (bf16[1040,512]{1,0:T(8,128)(2,1)S(1)}, bf16[16,144,128]{2,1,0:T(8,128)(2,1)S(1)}) custom-call(bf16[2,512,1280]{2,1,0:T(8,128)(2,1)S(1)} %shard_map.112.w, bf16[512,512]{1,0:T(8,128)(2,1)} %collective-permute-done.low.ulow, bf16[512,512]{1,0:T(8,128)(2,1)S(1)} %copy-done.3, bf16[512,512]{1,0:T(8,128)(2,1)} %collective-permute-done.1.high.uhigh, ...), custom_call_target="tpu_custom_call" | custom-call | flops 1342177280 | tf_op jit(solution)/shard_map/pallas_call | solution.py:333
  55.9 0.0 copy-start.5
  55.9 1.0 copy-done.5
  56.9 0.8 copy-done.10
  57.7 5.0 %all-to-all-start.3 = ((bf16[16,144,128]{2,1,0:T(8,128)(2,1)}), bf16[16,144,128]{2,1,0:T(8,128)(2,1)S(1)}, u32[]{:S(2)}, u32[]{:S(2)}) async-start(bf16[16,144,128]{2,1,0:T(8,128)(2,1)} %copy-done.10), calls=%async_computation.3 | async-start | bytes 1179648 | tf_op jit(solution)/shard_map/all_to_all | solution.py:300
  62.8 4.4 %collective-permute-start.3 = (bf16[1040,512]{1,0:T(8,128)(2,1)}, bf16[1040,512]{1,0:T(8,128)(2,1)}, u32[]{:S(2)}, u32[]{:S(2)}) collective-permute-start(bf16[1040,512]{1,0:T(8,128)(2,1)} %copy-done.5), channel_id=1, source_target_pairs={{1,0},{2,1},{3,2},{4,3},{5,4},{6,5},{7,6},{8,7},{9,8},{10,9},{11,1... | collective-permute-start | bytes 3194888 | tf_op jit(solution)/shard_map/ppermute | solution.py:274
  67.2 0.0 collective-permute-start.2
  67.2 11.7 %all-to-all-done.3.msg = bf16[16,144,128]{2,1,0:T(8,128)(2,1)S(1)} async-done(((bf16[16,144,128]{2,1,0:T(8,128)(2,1)}), bf16[16,144,128]{2,1,0:T(8,128)(2,1)S(1)}, u32[]{:S(2)}, u32[]{:S(2)}) %all-to-all-start.3) | async-done | bytes 589856 | tf_op jit(solution)/shard_map/all_to_all | solution.py:300
  78.8 0.9 copy-done.2
  79.8 1.3 %shard_map.116 = bf16[4,144,128]{2,1,0:T(8,128)(2,1)S(1)} custom-call(s32[48]{0:T(128)S(1)} %reshape.27.cols, bf16[1024,128]{1,0:T(8,128)(2,1)S(1)} %bitcast.7, bf16[16,144,128]{2,1,0:T(8,128)(2,1)S(1)} %all-to-all-done.3.msg, bf16[4,144,192]{2,1,0:T(8,128)(2,1)S(1)} %all-to-all-done.coup), custom_call_target="tpu_custom_call" | custom-call | tf_op jit(solution)/shard_map/pallas_call | solution.py:347
  81.1 0.0 copy-start.9
  81.1 0.7 copy-done.9
  81.8 13.5 %all-to-all-start.4 = ((bf16[4,144,128]{2,1,0:T(8,128)(2,1)}), bf16[4,144,128]{2,1,0:T(8,128)(2,1)S(1)}, u32[]{:S(2)}, u32[]{:S(2)}) async-start(bf16[4,144,128]{2,1,0:T(8,128)(2,1)} %copy-done.9), calls=%async_computation.4 | async-start | bytes 294912 | tf_op jit(solution)/shard_map/all_to_all | solution.py:300
  95.3 0.0 collective-permute-done.3.vhigh
  95.3 0.0 collective-permute-done.2.vlow
  95.3 6.9 %all-to-all-done.4.cmsg = bf16[4,144,128]{2,1,0:T(8,128)(2,1)S(1)} async-done(((bf16[4,144,128]{2,1,0:T(8,128)(2,1)}), bf16[4,144,128]{2,1,0:T(8,128)(2,1)S(1)}, u32[]{:S(2)}, u32[]{:S(2)}) %all-to-all-start.4) | async-done | bytes 147488 | tf_op jit(solution)/shard_map/all_to_all | solution.py:300
  102.2 1.0 copy-done.4
  103.2 1.2 %copy-done.6 = bf16[1040,512]{1,0:T(8,128)(2,1)S(1)} copy-done((bf16[1040,512]{1,0:T(8,128)(2,1)S(1)}, bf16[1040,512]{1,0:T(8,128)(2,1)}, u32[]{:S(2)}) %copy-start.6) | copy-done | bytes 1064984
  104.5 0.9 copy-done.8
  105.4 0.9 copy-done.12
  106.3 5.6 %shard_map.117 = (f32[2,512,512]{2,1,0:T(8,128)}, f32[2,512]{1,0:T(2,128)}, f32[2,512]{1,0:T(2,128)}) custom-call(bf16[2,512,1280]{2,1,0:T(8,128)(2,1)S(1)} %shard_map.112.w, bf16[512,512]{1,0:T(8,128)(2,1)} %collective-permute-done.low.ulow, bf16[512,512]{1,0:T(8,128)(2,1)S(1)} %copy-done.4, bf16[512,512]{1,0:T(8,128)(2,1)} %collective-permute-done.1.high.uhigh, ...), custom_call_target="tpu_custom_call" | custom-call | flops 1342177280 | tf_op jit(solution)/shard_map/pallas_call | solution.py:355
  (10 shorter events, 0.0 us)
Async XLA Ops:
  0.6 10.2 %copy-start.3 = (bf16[512,512]{1,0:T(8,128)(2,1)S(1)}, bf16[512,512]{1,0:T(8,128)(2,1)}, u32[]{:S(2)}) copy-start(bf16[512,512]{1,0:T(8,128)(2,1)} %uown.1) | copy-start | bytes 1572868
  2.5 39.5 %copy-start.17 = (bf16[2,256,32]{1,2,0:T(8,128)(2,1)S(1)}, bf16[2,256,32]{1,2,0:T(8,128)(2,1)}, u32[]{:S(2)}) copy-start(bf16[2,256,32]{1,2,0:T(8,128)(2,1)} %param.15) | copy-start | bytes 98308
  2.6 40.2 %copy-start.18 = (f32[2,512]{1,0:T(2,128)S(1)}, f32[2,512]{1,0:T(2,128)}, u32[]{:S(2)}) copy-start(f32[2,512]{1,0:T(2,128)} %param.10) | copy-start | bytes 12292
  2.7 40.9 %copy-start.15 = (s32[2,5]{1,0:T(2,128)S(1)}, s32[2,5]{1,0:T(2,128)}, u32[]{:S(2)}) copy-start(s32[2,5]{1,0:T(2,128)} %cols.1) | copy-start | bytes 124
  2.8 40.9 %copy-start.16 = (s32[2]{0:T(128)S(1)}, s32[2]{0:T(128)}, u32[]{:S(2)}) copy-start(s32[2]{0:T(128)} %count.1) | copy-start | bytes 28
  3.6 15.9 %all-to-all-start = ((bf16[4,144,192]{2,1,0:T(8,128)(2,1)}), bf16[4,144,192]{2,1,0:T(8,128)(2,1)S(1)}, u32[]{:S(2)}, u32[]{:S(2)}) async-start(bf16[4,144,192]{2,1,0:T(8,128)(2,1)} %broadcast_in_dim.2), calls=%async_computation | async-start | bytes 589824 | tf_op jit(solution)/shard_map/all_to_all | solution.py:300
  10.8 8.7 %copy-start.13 = (bf16[2,256,32]{2,1,0:T(8,128)(2,1)}, bf16[2,256,32]{2,1,0:T(8,128)(2,1)S(1)}, u32[]{:S(2)}) copy-start(bf16[2,256,32]{2,1,0:T(8,128)(2,1)S(1)} %copy.23.right) | copy-start | bytes 98308
  19.5 13.8 %all-to-all-start.1 = ((bf16[16,64,128]{2,1,0:T(8,128)(2,1)}), bf16[16,64,128]{2,1,0:T(8,128)(2,1)S(1)}, u32[]{:S(2)}, u32[]{:S(2)}) async-start(bf16[16,64,128]{2,1,0:T(8,128)(2,1)} %shard_map.113), calls=%async_computation.1 | async-start | bytes 524288 | tf_op jit(solution)/shard_map/all_to_all | solution.py:300
  23.3 23.0 %collective-permute-start.1 = (bf16[512,512]{1,0:T(8,128)(2,1)S(1)}, bf16[512,512]{1,0:T(8,128)(2,1)}, u32[]{:S(2)}, u32[]{:S(2)}) collective-permute-start(bf16[512,512]{1,0:T(8,128)(2,1)S(1)} %copy-done.3), channel_id=1, source_target_pairs={{1,0},{2,1},{3,2},{4,3},{5,4},{6,5},{7,6},{8,7},{9,8},{10,9},{11,1... | collective-permute-start | bytes 1572872 | tf_op jit(solution)/shard_map/ppermute | solution.py:274
  27.7 18.6 %collective-permute-start = (bf16[512,512]{1,0:T(8,128)(2,1)S(1)}, bf16[512,512]{1,0:T(8,128)(2,1)}, u32[]{:S(2)}, u32[]{:S(2)}) collective-permute-start(bf16[512,512]{1,0:T(8,128)(2,1)S(1)} %copy-done.3), channel_id=1, source_target_pairs={{0,1},{1,2},{2,3},{3,4},{4,5},{5,6},{6,7},{7,8},{8,9},{9,10},{10,1... | collective-permute-start | bytes 1572872 | tf_op jit(solution)/shard_map/ppermute | solution.py:274
  33.4 10.3 %copy-start.1 = (bf16[16,64,128]{2,1,0:T(8,128)(2,1)}, bf16[16,64,128]{2,1,0:T(8,128)(2,1)S(1)}, u32[]{:S(2)}) copy-start(bf16[16,64,128]{2,1,0:T(8,128)(2,1)S(1)} %all-to-all-done.1) | copy-start | bytes 786436
  34.8 13.7 %all-to-all-start.2 = ((bf16[4,128,128]{2,1,0:T(8,128)(2,1)}), bf16[4,128,128]{2,1,0:T(8,128)(2,1)}, u32[]{:S(2)}, u32[]{:S(2)}) async-start(bf16[4,128,128]{2,1,0:T(8,128)(2,1)} %shard_map.114), calls=%async_computation.2 | async-start | bytes 262144 | tf_op jit(solution)/shard_map/all_to_all | solution.py:300
  43.7 1.7 %copy-start = (bf16[2,2,5,256,256]{4,3,2,1,0:T(8,128)(2,1)S(1)}, bf16[2,2,5,256,256]{4,3,2,1,0:T(8,128)(2,1)}, u32[]{:S(2)}) copy-start(bf16[2,2,5,256,256]{4,3,2,1,0:T(8,128)(2,1)} %tiles.1) | copy-start | bytes 7864324
  48.6 1.0 copy-start.7
  49.5 0.9 copy-start.11
  50.4 0.9 copy-start.14
  55.9 1.0 copy-start.5
  56.9 0.8 copy-start.10
  57.7 21.1 %all-to-all-start.3 = ((bf16[16,144,128]{2,1,0:T(8,128)(2,1)}), bf16[16,144,128]{2,1,0:T(8,128)(2,1)S(1)}, u32[]{:S(2)}, u32[]{:S(2)}) async-start(bf16[16,144,128]{2,1,0:T(8,128)(2,1)} %copy-done.10), calls=%async_computation.3 | async-start | bytes 1179648 | tf_op jit(solution)/shard_map/all_to_all | solution.py:300
  62.8 32.5 %collective-permute-start.3 = (bf16[1040,512]{1,0:T(8,128)(2,1)}, bf16[1040,512]{1,0:T(8,128)(2,1)}, u32[]{:S(2)}, u32[]{:S(2)}) collective-permute-start(bf16[1040,512]{1,0:T(8,128)(2,1)} %copy-done.5), channel_id=1, source_target_pairs={{1,0},{2,1},{3,2},{4,3},{5,4},{6,5},{7,6},{8,7},{9,8},{10,9},{11,1... | collective-permute-start | bytes 3194888 | tf_op jit(solution)/shard_map/ppermute | solution.py:274
  67.2 28.1 %collective-permute-start.2 = (bf16[1040,512]{1,0:T(8,128)(2,1)}, bf16[1040,512]{1,0:T(8,128)(2,1)}, u32[]{:S(2)}, u32[]{:S(2)}) collective-permute-start(bf16[1040,512]{1,0:T(8,128)(2,1)} %copy-done.5), channel_id=1, source_target_pairs={{0,1},{1,2},{2,3},{3,4},{4,5},{5,6},{6,7},{7,8},{8,9},{9,10},{10,1... | collective-permute-start | bytes 3194888 | tf_op jit(solution)/shard_map/ppermute | solution.py:274
  78.8 1.0 copy-start.2
  81.1 0.7 copy-start.9
  81.8 20.4 %all-to-all-start.4 = ((bf16[4,144,128]{2,1,0:T(8,128)(2,1)}), bf16[4,144,128]{2,1,0:T(8,128)(2,1)S(1)}, u32[]{:S(2)}, u32[]{:S(2)}) async-start(bf16[4,144,128]{2,1,0:T(8,128)(2,1)} %copy-done.9), calls=%async_computation.4 | async-start | bytes 294912 | tf_op jit(solution)/shard_map/all_to_all | solution.py:300
  102.2 1.0 copy-start.4
  103.2 1.2 %copy-start.6 = (bf16[1040,512]{1,0:T(8,128)(2,1)S(1)}, bf16[1040,512]{1,0:T(8,128)(2,1)}, u32[]{:S(2)}) copy-start(bf16[1040,512]{1,0:T(8,128)(2,1)} %copy-done.5) | copy-start | bytes 3194884
  104.5 0.9 copy-start.8
  105.4 0.9 copy-start.12

commit v2 on v1

v2 whole, which is shorter than its diff:
```python
import functools

import jax
import jax.numpy as jnp
from jax import lax
from jax.experimental import pallas as pl
from jax.experimental.pallas import tpu as pltpu
from jax.sharding import PartitionSpec as P

REACH = 2
EPSILON = 1e-06
LANES = 128
HALF = 64
SLICES = 8
STATS = 16
F32 = jnp.float32
BF16 = jnp.bfloat16

VMEM = pl.BlockSpec(memory_space=pltpu.VMEM)
SMEM = pl.BlockSpec(memory_space=pltpu.SMEM)


def call(body, out_shape, in_specs, scratch=(), flops=0, nbytes=0):
    many = isinstance(out_shape, (list, tuple))
    return pl.pallas_call(
        body,
        out_shape=out_shape,
        in_specs=in_specs,
        out_specs=[VMEM] * len(out_shape) if many else VMEM,
        scratch_shapes=list(scratch),
        compiler_params=pltpu.CompilerParams(vmem_limit_bytes=20 * 1024 * 1024),
        cost_estimate=pl.CostEstimate(flops=flops, bytes_accessed=nbytes, transcendentals=0),
    )


def dot(a, b, dims=((1,), (0,))):
    return lax.dot_general(a, b, (dims, ((), ())), preferred_element_type=F32)


def split3(row):
    high = row.astype(BF16)
    rest = row - high.astype(F32)
    middle = rest.astype(BF16)
    low = (rest - middle.astype(F32)).astype(BF16)
    return [high, middle, low]


def join3(rows, at):
    return rows[..., 3 * at, :] + rows[..., 3 * at + 1, :] + rows[..., 3 * at + 2, :]


def row3(values, at):
    return values[3 * at:3 * at + 1] + values[3 * at + 1:3 * at + 2] + values[3 * at + 2:3 * at + 3]


def halves(x, y):
    left = lax.broadcasted_iota(jnp.int32, x.shape, x.ndim - 1) < HALF
    first = jnp.where(left, x, pltpu.roll(y, HALF, x.ndim - 1))
    second = jnp.where(left, pltpu.roll(x, HALF, x.ndim - 1), y)
    return first, second


def chunk(x, pair):
    return x[:, pair * LANES:(pair + 1) * LANES]


def send_all(out, rows, at, part):
    n = out.shape[0]

    def put(g, _):
        out[g * SLICES + at, rows, :] = part
        return 0

    lax.fori_loop(0, n // SLICES, put, 0, unroll=n == 2 * SLICES)


def order_tiles(all_blocks, cols, count, row0, tiles, out):
    ops, blocks, near, size, _ = tiles.shape
    for b in range(blocks):
        for k in range(near):
            rel = lax.rem(cols[b, k] - (row0[0] + b) + REACH + all_blocks, all_blocks)
            rel = lax.rem(rel, all_blocks)
            at = pl.multiple_of(rel * size, size)
            live = k < count[b]
            for o in range(ops):
                tile = tiles[o, b, k]
                out[b, o * size:(o + 1) * size, pl.ds(at, size)] = jnp.where(
                    live, tile, jnp.zeros_like(tile)
                )


def coeff_kernel(u, right, out):
    blocks, rank, size = right.shape
    z = [dot(right[b], u[b * size:(b + 1) * size, :]) for b in range(blocks)]
    for pair in range(SLICES // 2):
        first, second = halves(chunk(z[0], pair), chunk(z[1], pair))
        send_all(out, slice(0, rank), 2 * pair, first.astype(BF16))
        send_all(out, slice(0, rank), 2 * pair + 1, second.astype(BF16))


def share_kernel(far_cols, coup, out):
    ops, blocks, far, rank, _ = coup.shape
    rows = blocks * ops * rank
    parts = []
    for b in range(blocks):
        for o in range(ops):
            parts.append(jnp.concatenate([coup[o, b, f] for f in range(far)], axis=1))
    lane = lax.broadcasted_iota(jnp.int32, (STATS, far * rank), 1)
    names = jnp.zeros((STATS, far * rank), F32)
    for b in range(blocks):
        for f in range(far):
            names = jnp.where(lane == b * far + f, far_cols[b, f].astype(F32), names)
    whole = jnp.concatenate(parts + [names.astype(BF16)], axis=0)
    for s in range(out.shape[0]):
        out[s] = whole


def couple(cols, coup, s, b, ops, rank, z):
    blocks = 2
    far = coup.shape[2] // rank
    at = (s * blocks + b) * far
    picked = []
    for f in range(far):
        start = pl.multiple_of(cols[at + f] * rank, rank)
        picked.append([x[pl.ds(start, rank), :] for x in z])
    res = []
    if len(z) == 1:
        lhs = coup[s, b * ops * rank:(b + 1) * ops * rank, :]
        return dot(lhs, jnp.concatenate([p[0] for p in picked], axis=0))
    for o in range(ops):
        row = (b * ops + o) * rank
        rhs = jnp.concatenate([p[o] for p in picked], axis=0)
        res.append(dot(coup[s, row:row + rank, :], rhs))
    return jnp.concatenate(res, axis=0)


def spread_rows(source, target, rank):
    n = source.shape[0]
    x = source.reshape(n, rank, LANES)
    y = pltpu.roll(x, HALF, 2)
    both = jnp.concatenate([x[:, None], y[:, None]], axis=1)
    target[...] = both.reshape(n * 2 * rank, LANES).astype(BF16)


def first_couple(ops, rank, cols, z1, coup, out, zs):
    spread_rows(z1[...].astype(F32), zs, rank)
    for s in range(out.shape[0]):
        c = [couple(cols, coup, s, b, ops, rank, [zs]) for b in range(2)]
        out[s] = halves(c[0], c[1])[0].astype(BF16)


def take_coefs(cmsg, coef, rows):
    for pair in range(SLICES // 2):
        parts = halves(
            cmsg[2 * pair, 0:rows, :].astype(F32), cmsg[2 * pair + 1, 0:rows, :].astype(F32)
        )
        for b in range(2):
            coef[b, :, pair * LANES:(pair + 1) * LANES] = parts[b].astype(BF16)


def near_product(tiles, parts, b, blocks, size):
    total = None
    first = b - REACH
    at = 0
    for d, part in enumerate(parts):
        start = max((d - 1) * blocks, first)
        stop = min(d * blocks, first + 2 * REACH + 1)
        if stop <= start:
            continue
        begin = (start - (d - 1) * blocks) * size
        width = (stop - start) * size
        value = dot(tiles[:, at:at + width], part[begin:begin + width, :])
        total = value if total is None else total + value
        at += width
    return total


def diagonal_of(diag, o, b, size, columns):
    row = diag[o:o + 1, b * size:(b + 1) * size]
    column = jnp.transpose(jnp.broadcast_to(row, (LANES, size)))
    return jnp.concatenate([column] * (columns // LANES), axis=1)


def image_kernel(w, low, own, high, diag, left, right, cmsg, vout, mout, image, coef):
    ops = image.shape[0]
    blocks, rank, size = right.shape
    rows, columns = own.shape
    take_coefs(cmsg, coef, ops * rank)
    inner = [None] * ops
    squares = None
    for b in range(blocks):
        product = near_product(w.at[b], (low, own, high), b, blocks, size)
        ub = own[b * size:(b + 1) * size, :].astype(F32)
        part = jnp.sum(ub * ub, axis=0, keepdims=True)
        squares = part if squares is None else squares + part
        for o in range(ops):
            far = dot(left[b], coef[b, o * rank:(o + 1) * rank, :], ((0,), (0,)))
            value = (
                product[o * size:(o + 1) * size]
                + diagonal_of(diag, o, b, size, columns) * ub
                + far.astype(BF16).astype(F32)
            )
            image[o, b * size:(b + 1) * size, :] = value
            part = jnp.sum(ub * value, axis=0, keepdims=True)
            inner[o] = part if inner[o] is None else inner[o] + part
    stats = []
    spreads = []
    good = squares > 0
    for o in range(ops):
        shift = jnp.where(good, inner[o] / jnp.where(good, squares, 1.0), 0.0)
        pieces = split3(shift)
        stats += pieces
        shift = pieces[0].astype(F32) + pieces[1].astype(F32) + pieces[2].astype(F32)
        spread = None
        z = []
        for b in range(blocks):
            ub = own[b * size:(b + 1) * size, :].astype(F32)
            v = image[o, b * size:(b + 1) * size, :] - shift * ub
            part = jnp.sum(v * v, axis=0, keepdims=True)
            spread = part if spread is None else spread + part
            v = v.astype(BF16)
            vout[(o * blocks + b) * size:(o * blocks + b + 1) * size, :] = v
            z.append(dot(right[b], v))
        for pair in range(SLICES // 2):
            first, second = halves(chunk(z[0], pair), chunk(z[1], pair))
            send_all(mout, slice(o * rank, (o + 1) * rank), 2 * pair, first.astype(BF16))
            send_all(mout, slice(o * rank, (o + 1) * rank), 2 * pair + 1, second.astype(BF16))
        spreads.append(spread)
    zero = jnp.zeros((1, columns), BF16)
    vout[ops * rows:, :] = jnp.concatenate(stats + [zero] * (STATS - len(stats)), axis=0)
    stats += split3(squares)
    for spread in spreads:
        stats += split3(spread)
    stats = jnp.concatenate(stats + [zero] * (STATS - len(stats)), axis=0).astype(F32)
    for pair in range(SLICES // 2):
        part = chunk(stats, pair)
        first, second = halves(part, part)
        send_all(mout, slice(ops * rank, ops * rank + STATS), 2 * pair, first.astype(BF16))
        send_all(mout, slice(ops * rank, ops * rank + STATS), 2 * pair + 1, second.astype(BF16))


def second_couple(panels, ops, rank, cols, z1, msg, coup, out, zs):
    body = ops * rank
    st = msg[:, body:body + STATS, :].astype(F32)
    shift = [join3(st, o) for o in range(ops)]
    squares = join3(st, ops)
    scale_sq = jnp.sum(squares, axis=0, keepdims=True) / panels + EPSILON
    reverse = 1.0 / jnp.sqrt(scale_sq)
    heights, norms = [], []
    base = z1[...].astype(F32)
    for o in range(ops):
        total = jnp.sum(shift[o] * squares, axis=0, keepdims=True) / panels
        height = total / scale_sq
        delta = shift[o] - height
        spread = join3(st, ops + 1 + o) + delta * delta * squares
        norm = jnp.sqrt(jnp.sum(spread, axis=0, keepdims=True) / panels / scale_sq + EPSILON)
        heights.append(height)
        norms.append(norm)
        factor = reverse / norm
        z = msg[:, o * rank:(o + 1) * rank, :].astype(F32) + delta[:, None, :] * base
        spread_rows(z * factor[None], zs.at[o], rank)
    rows = []
    for row in heights + norms + [reverse]:
        rows += split3(row)
    rows += [jnp.zeros_like(rows[0])] * (STATS - len(rows))
    rows = jnp.concatenate(rows, axis=0)
    for s in range(out.shape[0]):
        c = [couple(cols, coup, s, b, ops, rank, [zs.at[o] for o in range(ops)]) for b in range(2)]
        out[s, 0:body, :] = halves(c[0], c[1])[0].astype(BF16)
        out[s, body:body + STATS, :] = rows


def final_kernel(
    w, ulow, uown, uhigh, vlow, vown, vhigh, diag, left, cmsg, images, heights, norms, ext, coef, stat
):
    ops = images.shape[0]
    blocks, rank, size = left.shape
    rows, columns = uown.shape
    body = ops * rank
    take_coefs(cmsg, coef, body)
    for pair in range(SLICES // 2):
        stat[:, pair * LANES:(pair + 1) * LANES] = halves(
            cmsg[2 * pair, body:body + STATS, :].astype(F32),
            cmsg[2 * pair + 1, body:body + STATS, :].astype(F32),
        )[0]
    st = stat[...]
    reverse = row3(st, 2 * ops)
    for o in range(ops):
        height = row3(st, o)
        norm = row3(st, ops + o)
        heights[o:o + 1, :] = height
        norms[o:o + 1, :] = norm
        factor = reverse / norm
        for at, (u, v) in enumerate(((ulow, vlow), (uown, vown), (uhigh, vhigh))):
            shift = row3(v[ops * rows:, :].astype(F32), o)
            change = (shift - height) * factor
            value = v[o * rows:(o + 1) * rows, :].astype(F32) * factor + u[...].astype(F32) * change
            ext[o, at] = value.astype(BF16)
        for b in range(blocks):
            parts = [ext.at[o, at] for at in range(3)]
            product = near_product(w.at[b, o * size:(o + 1) * size], parts, b, blocks, size)
            far = dot(left[b], coef[b, o * rank:(o + 1) * rank, :], ((0,), (0,)))
            mine = ext[o, 1, b * size:(b + 1) * size, :].astype(F32)
            images[o, b * size:(b + 1) * size, :] = (
                product
                + diagonal_of(diag, o, b, size, columns) * mine
                + far.astype(BF16).astype(F32)
            )


def ring(block):
    count = lax.axis_size("store")
    forward = [(i, (i + 1) % count) for i in range(count)]
    backward = [(target, source) for source, target in forward]
    return lax.ppermute(block, "store", forward), lax.ppermute(block, "store", backward)


def shards(
    sources,
    self_terms,
    near_tiles,
    near_cols,
    near_count,
    far_cols,
    basis_left,
    basis_right,
    couplings,
):
    n = lax.axis_size("store")
    ops, blocks, near, size, _ = near_tiles.shape
    rank = basis_left.shape[2]
    far = far_cols.shape[1]
    rows, columns = sources.shape
    all_blocks = blocks * n
    groups = [[g * SLICES + s for s in range(SLICES)] for g in range(n // SLICES)]
    sds = jax.ShapeDtypeStruct
    body = ops * rank

    def exchange(x, part):
        return lax.all_to_all(
            x, "store", 0, 0, axis_index_groups=groups if part else None, tiled=True
        )

    row0 = (lax.axis_index("store") * blocks).astype(jnp.int32).reshape(1)
    left = jnp.transpose(basis_left, (0, 2, 1))
    right = jnp.transpose(basis_right, (0, 2, 1))

    z1 = call(coeff_kernel, sds((n, rank, LANES), BF16), [VMEM, VMEM])(sources, right)
    z1 = exchange(z1, False)
    low, high = ring(sources)

    held = call(
        share_kernel, sds((SLICES, blocks * body + STATS, far * rank), BF16), [SMEM, VMEM]
    )(far_cols, couplings)
    held = exchange(held, True)
    cols = held[:, blocks * body, :blocks * far].astype(jnp.int32).reshape(-1)

    w = call(
        functools.partial(order_tiles, all_blocks),
        sds((blocks, ops * size, near * size), BF16),
        [SMEM, SMEM, SMEM, VMEM],
    )(near_cols, near_count, row0, near_tiles)

    c1 = call(
        functools.partial(first_couple, ops, rank),
        sds((SLICES, body, LANES), BF16),
        [SMEM, VMEM, VMEM],
        [pltpu.VMEM((n * blocks * rank, LANES), BF16)],
    )(cols, z1, held)
    c1 = exchange(c1, True)

    v, msg = call(
        image_kernel,
        [sds((ops * rows + STATS, columns), BF16), sds((n, body + STATS, LANES), BF16)],
        [VMEM] * 8,
        [
            pltpu.VMEM((ops, rows, columns), F32),
            pltpu.VMEM((blocks, body, columns), BF16),
        ],
        flops=2 * ops * rows * near * size * columns,
    )(w, low, sources, high, self_terms, left, right, c1)
    msg = exchange(msg, False)
    vlow, vhigh = ring(v)

    c2 = call(
        functools.partial(second_couple, all_blocks * size, ops, rank),
        sds((SLICES, body + STATS, LANES), BF16),
        [SMEM, VMEM, VMEM, VMEM],
        [pltpu.VMEM((ops, n * blocks * rank, LANES), BF16)],
    )(cols, z1, msg, held)
    c2 = exchange(c2, True)

    images, heights, norms = call(
        final_kernel,
        [sds((ops, rows, columns), F32), sds((ops, columns), F32), sds((ops, columns), F32)],
        [VMEM] * 10,
        [
            pltpu.VMEM((ops, 3, rows, columns), BF16),
            pltpu.VMEM((blocks, body, columns), BF16),
            pltpu.VMEM((STATS, columns), F32),
        ],
        flops=2 * ops * rows * near * size * columns,
    )(w, low, sources, high, vlow, v, vhigh, self_terms, left, c2)
    return images, heights, norms


def solution(mesh):
    placed = (
        P(("groups", "store"), None),
        P(None, "store"),
        P(None, "store", None, None, None),
        P("store", None),
        P("store"),
        P("store", None),
        P("store", None, None),
        P("store", None, None),
        P(None, "store", None, None, None),
    )
    return jax.shard_map(
        shards,
        mesh=mesh,
        in_specs=placed,
        out_specs=(P(None, ("groups", "store"), None), P("groups", None), P("groups", None)),
        check_vma=False,
    )
```

time: 113 us -> 97.3 us (0.86)
  blocking collectives: 0 us -> 37 us
  waiting for transfers between devices: 34 us -> 13.4 us
  starting transfers between devices: 44.6 us -> 24.6 us
  local copies, waits for them, and re-layouts: 16.8 us -> 5.3 us
    all_to_all x0 -> x2, blocking collectives: none -> 37 us  [exchange(): lax.all_to_all(x, 'store', 0, 0, axis_index_groups=groups if part else No...]
    all_to_all x5 -> x3, waiting for transfers between devices: 34 us -> 13.4 us  [exchange(): lax.all_to_all(x, 'store', 0, 0, axis_index_groups=groups if part else No...]
    all_to_all x5 -> x3, starting transfers between devices: 35.8 us -> 19.4 us  [exchange(): lax.all_to_all(x, 'store', 0, 0, axis_index_groups=groups if part else No...]
    unnamed x41 -> x24, local copies, waits for them, and re-layouts: 14.5 us -> 5.22 us
    ppermute x2, starting transfers between devices: 8.77 us -> 5.05 us  [ring(): lax.ppermute(block, 'store', backward)]
    pallas_call x4 -> x5, Pallas kernels: 8.48 us -> 9.69 us  [the longest x1 3.91 us: shards(): call(image_kernel, [sds((ops * rows + STATS, columns), BF16), sds((n, bod...]
  transfers between devices with their start and end apart: 9 -> 7, of which waited for: 5 -> 3; matrix products, arithmetic and copies ran while one was open for 2% -> 0% of each run, Pallas kernels for 4% -> 5%
where the time goes in v2:
time: 97.3 us; the launch traced here: 96.6 us
  blocking collectives  37 us (38%)
  starting transfers between devices  24.6 us (25%)
  Pallas kernels  15.5 us (16%)
  waiting for transfers between devices  13.4 us (14%)
  local copies, waits for them, and re-layouts  5.3 us (5%)
    all_to_all x2, blocking collectives, exchange(): lax.all_to_all(x, 'store', 0, 0, axis_index_groups=groups if part else No...  37 us
    all_to_all x3, starting transfers between devices, exchange(): lax.all_to_all(x, 'store', 0, 0, axis_index_groups=groups if part else No...  19.4 us
    all_to_all x3, waiting for transfers between devices, exchange(): lax.all_to_all(x, 'store', 0, 0, axis_index_groups=groups if part else No...  13.4 us
    unnamed x24, local copies, waits for them, and re-layouts  5.22 us
    ppermute x2, starting transfers between devices, ring(): lax.ppermute(block, 'store', backward)  5.05 us
    pallas_call x1, Pallas kernels, shards(): call(final_kernel, [sds((ops, rows, columns), F32), sds((ops, columns), F...  4.94 us
    pallas_call x1, Pallas kernels, shards(): call(image_kernel, [sds((ops * rows + STATS, columns), BF16), sds((n, bod...  3.91 us
  transfers between devices with their start and end apart: 7, of which 3 were waited for; matrix products, arithmetic and copies ran while one was open for 0% of the time, Pallas kernels for 5%

profile of v2, /device:TPU:0, one launch (start us, length us, event | category | flops | bytes accessed | tf_op | source)
XLA Modules:
  0.0 96.6 jit_solution(13104952936805261661)
XLA Ops:
  0.6 0.0 copy-start.1
  0.6 0.0 copy-start.4
  0.7 1.0 %copy-done.4 = bf16[2,2,6,32,32]{4,3,2,1,0:T(8,128)(2,1)S(1)} copy-done((bf16[2,2,6,32,32]{4,3,2,1,0:T(8,128)(2,1)S(1)}, bf16[2,2,6,32,32]{4,3,2,1,0:T(8,128)(2,1)}, u32[]{:S(2)}) %copy-start.4) | copy-done | bytes 49176
  1.6 0.0 copy-start.9
  1.6 0.7 copy-done.9
  2.3 0.0 copy-start.10
  2.3 0.0 copy-start.11
  2.3 1.5 %shard_map.113 = bf16[8,144,192]{2,1,0:T(8,128)(2,1)} custom-call(s32[2,6]{1,0:T(2,128)S(1)} %copy-done.9, bf16[2,2,6,32,32]{4,3,2,1,0:T(8,128)(2,1)S(1)} %copy-done.4), custom_call_target="tpu_custom_call" | custom-call | tf_op jit(solution)/shard_map/pallas_call | solution.py:352
  3.8 5.3 %all-to-all-start = ((bf16[8,144,192]{2,1,0:T(8,128)(2,1)}), bf16[8,144,192]{2,1,0:T(8,128)(2,1)S(1)}, u32[]{:S(2)}, u32[]{:S(2)}) async-start(bf16[8,144,192]{2,1,0:T(8,128)(2,1)} %shard_map.113), calls=%async_computation | async-start | bytes 1179648 | tf_op jit(solution)/shard_map/all_to_all | solution.py:340
  9.1 4.7 %collective-permute-start.1 = (bf16[512,512]{1,0:T(8,128)(2,1)}, bf16[512,512]{1,0:T(8,128)(2,1)}, u32[]{:S(2)}, u32[]{:S(2)}) collective-permute-start(bf16[512,512]{1,0:T(8,128)(2,1)} %uown.1), channel_id=1, source_target_pairs={{1,0},{2,1},{3,2},{4,3},{5,4},{6,5},{7,6},{8,7},{9,8},{10,9},{11,1... | collective-permute-start | bytes 1572872 | tf_op jit(solution)/shard_map/ppermute | solution.py:315
  13.8 0.0 collective-permute-start
  13.8 0.0 copy-done.1
  13.8 0.0 copy-start.6
  13.8 0.8 copy-done.6
  14.5 0.9 shard_map.114
  15.4 3.1 %all-to-all-done.coup = bf16[8,144,192]{2,1,0:T(8,128)(2,1)S(1)} async-done(((bf16[8,144,192]{2,1,0:T(8,128)(2,1)}), bf16[8,144,192]{2,1,0:T(8,128)(2,1)S(1)}, u32[]{:S(2)}, u32[]{:S(2)}) %all-to-all-start) | async-done | bytes 442400 | tf_op jit(solution)/shard_map/all_to_all | solution.py:340
  18.6 10.7 %all-to-all-start.1 = ((bf16[16,32,128]{2,1,0:T(8,128)(2,1)}), bf16[16,32,128]{2,1,0:T(8,128)(2,1)S(1)}, u32[]{:S(2)}, u32[]{:S(2)}) async-start(bf16[16,32,128]{2,1,0:T(8,128)(2,1)} %shard_map.114), calls=%async_computation.1 | async-start | bytes 262144 | tf_op jit(solution)/shard_map/all_to_all | solution.py:340
  29.4 0.1 reshape.14.cols
  29.5 7.8 %all-to-all-done.1.z1 = bf16[16,32,128]{2,1,0:T(8,128)(2,1)S(1)} async-done(((bf16[16,32,128]{2,1,0:T(8,128)(2,1)}), bf16[16,32,128]{2,1,0:T(8,128)(2,1)S(1)}, u32[]{:S(2)}, u32[]{:S(2)}) %all-to-all-start.1) | async-done | bytes 131104 | tf_op jit(solution)/shard_map/all_to_all | solution.py:340
  37.3 1.8 %shard_map.115 = bf16[8,64,128]{2,1,0:T(8,128)(2,1)} custom-call(s32[96]{0:T(128)S(1)} %reshape.14.cols, bf16[16,32,128]{2,1,0:T(8,128)(2,1)S(1)} %all-to-all-done.1.z1, bf16[8,144,192]{2,1,0:T(8,128)(2,1)S(1)} %all-to-all-done.coup), custom_call_target="tpu_custom_call" | custom-call | tf_op jit(solution)/shard_map/pallas_call | solution.py:364
  39.1 3.4 %all-to-all-start.2 = ((bf16[8,64,128]{2,1,0:T(8,128)(2,1)}), bf16[8,64,128]{2,1,0:T(8,128)(2,1)S(1)}, u32[]{:S(2)}, u32[]{:S(2)}) async-start(bf16[8,64,128]{2,1,0:T(8,128)(2,1)} %shard_map.115), calls=%async_computation.2 | async-start | bytes 262144 | tf_op jit(solution)/shard_map/all_to_all | solution.py:340
  42.5 0.0 copy-done.10
  42.5 0.0 copy-done.11
  42.5 0.0 copy-start
  42.5 1.7 %copy-done = bf16[2,2,5,256,256]{4,3,2,1,0:T(8,128)(2,1)S(1)} copy-done((bf16[2,2,5,256,256]{4,3,2,1,0:T(8,128)(2,1)S(1)}, bf16[2,2,5,256,256]{4,3,2,1,0:T(8,128)(2,1)}, u32[]{:S(2)}) %copy-start) | copy-done | bytes 2621464
  44.2 0.0 copy-start.5
  44.2 0.0 copy-start.7
  44.2 0.0 copy-start.8
  44.2 0.9 shard_map.112.w
  45.1 0.0 collective-permute-done.1.high.uhigh
  45.1 0.0 collective-permute-done.low.ulow
  45.2 2.4 %all-to-all-done.2.cmsg = bf16[8,64,128]{2,1,0:T(8,128)(2,1)S(1)} async-done(((bf16[8,64,128]{2,1,0:T(8,128)(2,1)}), bf16[8,64,128]{2,1,0:T(8,128)(2,1)S(1)}, u32[]{:S(2)}, u32[]{:S(2)}) %all-to-all-start.2) | async-done | bytes 131104 | tf_op jit(solution)/shard_map/all_to_all | solution.py:340
  47.6 0.0 copy-done.5
  47.6 0.0 copy-done.7
  47.6 0.0 copy-done.8
  47.6 0.0 copy-start.2
  47.6 1.0 %copy-done.2 = bf16[512,512]{1,0:T(8,128)(2,1)S(1)} copy-done((bf16[512,512]{1,0:T(8,128)(2,1)S(1)}, bf16[512,512]{1,0:T(8,128)(2,1)}, u32[]{:S(2)}) %copy-start.2) | copy-done | bytes 524312
  48.6 3.9 %shard_map.116 = (bf16[1040,512]{1,0:T(8,128)(2,1)S(1)}, bf16[16,80,128]{2,1,0:T(8,128)(2,1)S(1)}) custom-call(bf16[2,512,1280]{2,1,0:T(8,128)(2,1)S(1)} %shard_map.112.w, bf16[512,512]{1,0:T(8,128)(2,1)} %collective-permute-done.low.ulow, bf16[512,512]{1,0:T(8,128)(2,1)S(1)} %copy-done.2, bf16[512,512]{1,0:T(8,128)(2,1)} %collective-permute-done.1.high.uhigh, ...), custom_call_target="tpu_custom_call" | custom-call | flops 1342177280 | tf_op jit(solution)/shard_map/pallas_call | solution.py:372
  52.5 0.0 copy-start.3
  52.5 0.3 collective-permute-start.3
  52.9 0.2 collective-permute-start.2
  53.1 28.4 %all_to_all.25.msg = bf16[16,80,128]{2,1,0:T(8,128)(2,1)S(1)} all-to-all(bf16[16,80,128]{2,1,0:T(8,128)(2,1)S(1)} %get-tuple-element.6), channel_id=1, replica_groups=mesh['groups'=2,'store'=16] {'store'}, dimensions={0} | all-to-all | bytes 655360 | tf_op jit(solution)/shard_map/all_to_all | solution.py:340
  81.5 1.6 %shard_map.117 = bf16[8,80,128]{2,1,0:T(8,128)(2,1)S(1)} custom-call(s32[96]{0:T(128)S(1)} %reshape.14.cols, bf16[16,32,128]{2,1,0:T(8,128)(2,1)S(1)} %all-to-all-done.1.z1, bf16[16,80,128]{2,1,0:T(8,128)(2,1)S(1)} %all_to_all.25.msg, bf16[8,144,192]{2,1,0:T(8,128)(2,1)S(1)} %all-to-all-done.coup), custom_call_target="tpu_custom_call" | custom-call | tf_op jit(solution)/shard_map/pallas_call | solution.py:385
  83.1 8.6 %all_to_all.26.cmsg = bf16[8,80,128]{2,1,0:T(8,128)(2,1)S(1)} all-to-all(bf16[8,80,128]{2,1,0:T(8,128)(2,1)S(1)} %shard_map.117), channel_id=1, replica_groups={{0,1,2,3,4,5,6,7},{8,9,10,11,12,13,14,15},{16,17,18,19,20,21,22,23},{24..., dimensions={0} | all-to-all | bytes 327680 | tf_op jit(solution)/shard_map/all_to_all | solution.py:340
  91.7 0.0 collective-permute-done.3.vhigh
  91.7 0.0 collective-permute-done.2.vlow
  91.7 0.0 copy-done.3
  91.7 4.9 %shard_map.118 = (f32[2,512,512]{2,1,0:T(8,128)}, f32[2,512]{1,0:T(2,128)}, f32[2,512]{1,0:T(2,128)}) custom-call(bf16[2,512,1280]{2,1,0:T(8,128)(2,1)S(1)} %shard_map.112.w, bf16[512,512]{1,0:T(8,128)(2,1)} %collective-permute-done.low.ulow, bf16[512,512]{1,0:T(8,128)(2,1)S(1)} %copy-done.3, bf16[512,512]{1,0:T(8,128)(2,1)} %collective-permute-done.1.high.uhigh, ...), custom_call_target="tpu_custom_call" | custom-call | flops 1342177280 | tf_op jit(solution)/shard_map/pallas_call | solution.py:393
  (1 shorter events, 0.0 us)
Async XLA Ops:
  0.6 13.1 %copy-start.1 = (bf16[512,512]{1,0:T(8,128)(2,1)S(1)}, bf16[512,512]{1,0:T(8,128)(2,1)}, u32[]{:S(2)}) copy-start(bf16[512,512]{1,0:T(8,128)(2,1)} %uown.1) | copy-start | bytes 1572868
  0.6 1.0 %copy-start.4 = (bf16[2,2,6,32,32]{4,3,2,1,0:T(8,128)(2,1)S(1)}, bf16[2,2,6,32,32]{4,3,2,1,0:T(8,128)(2,1)}, u32[]{:S(2)}) copy-start(bf16[2,2,6,32,32]{4,3,2,1,0:T(8,128)(2,1)} %coup.1) | copy-start | bytes 147460
  1.6 0.7 copy-start.9
  2.3 40.2 %copy-start.10 = (s32[2,5]{1,0:T(2,128)S(1)}, s32[2,5]{1,0:T(2,128)}, u32[]{:S(2)}) copy-start(s32[2,5]{1,0:T(2,128)} %cols.1) | copy-start | bytes 124
  2.3 40.2 %copy-start.11 = (s32[2]{0:T(128)S(1)}, s32[2]{0:T(128)}, u32[]{:S(2)}) copy-start(s32[2]{0:T(128)} %count.1) | copy-start | bytes 28
  3.8 14.8 %all-to-all-start = ((bf16[8,144,192]{2,1,0:T(8,128)(2,1)}), bf16[8,144,192]{2,1,0:T(8,128)(2,1)S(1)}, u32[]{:S(2)}, u32[]{:S(2)}) async-start(bf16[8,144,192]{2,1,0:T(8,128)(2,1)} %shard_map.113), calls=%async_computation | async-start | bytes 1179648 | tf_op jit(solution)/shard_map/all_to_all | solution.py:340
  9.1 36.1 %collective-permute-start.1 = (bf16[512,512]{1,0:T(8,128)(2,1)}, bf16[512,512]{1,0:T(8,128)(2,1)}, u32[]{:S(2)}, u32[]{:S(2)}) collective-permute-start(bf16[512,512]{1,0:T(8,128)(2,1)} %uown.1), channel_id=1, source_target_pairs={{1,0},{2,1},{3,2},{4,3},{5,4},{6,5},{7,6},{8,7},{9,8},{10,9},{11,1... | collective-permute-start | bytes 1572872 | tf_op jit(solution)/shard_map/ppermute | solution.py:315
  13.8 31.4 %collective-permute-start = (bf16[512,512]{1,0:T(8,128)(2,1)}, bf16[512,512]{1,0:T(8,128)(2,1)}, u32[]{:S(2)}, u32[]{:S(2)}) collective-permute-start(bf16[512,512]{1,0:T(8,128)(2,1)} %uown.1), channel_id=1, source_target_pairs={{0,1},{1,2},{2,3},{3,4},{4,5},{5,6},{6,7},{7,8},{8,9},{9,10},{10,1... | collective-permute-start | bytes 1572872 | tf_op jit(solution)/shard_map/ppermute | solution.py:315
  13.8 0.8 copy-start.6
  18.6 18.7 %all-to-all-start.1 = ((bf16[16,32,128]{2,1,0:T(8,128)(2,1)}), bf16[16,32,128]{2,1,0:T(8,128)(2,1)S(1)}, u32[]{:S(2)}, u32[]{:S(2)}) async-start(bf16[16,32,128]{2,1,0:T(8,128)(2,1)} %shard_map.114), calls=%async_computation.1 | async-start | bytes 262144 | tf_op jit(solution)/shard_map/all_to_all | solution.py:340
  39.1 8.5 %all-to-all-start.2 = ((bf16[8,64,128]{2,1,0:T(8,128)(2,1)}), bf16[8,64,128]{2,1,0:T(8,128)(2,1)S(1)}, u32[]{:S(2)}, u32[]{:S(2)}) async-start(bf16[8,64,128]{2,1,0:T(8,128)(2,1)} %shard_map.115), calls=%async_computation.2 | async-start | bytes 262144 | tf_op jit(solution)/shard_map/all_to_all | solution.py:340
  42.5 1.7 %copy-start = (bf16[2,2,5,256,256]{4,3,2,1,0:T(8,128)(2,1)S(1)}, bf16[2,2,5,256,256]{4,3,2,1,0:T(8,128)(2,1)}, u32[]{:S(2)}) copy-start(bf16[2,2,5,256,256]{4,3,2,1,0:T(8,128)(2,1)} %tiles.1) | copy-start | bytes 7864324
  44.2 3.3 %copy-start.5 = (bf16[2,256,32]{1,2,0:T(8,128)(2,1)S(1)}, bf16[2,256,32]{1,2,0:T(8,128)(2,1)}, u32[]{:S(2)}) copy-start(bf16[2,256,32]{1,2,0:T(8,128)(2,1)} %param.15) | copy-start | bytes 98308
  44.2 3.3 %copy-start.7 = (bf16[2,256,32]{1,2,0:T(8,128)(2,1)S(1)}, bf16[2,256,32]{1,2,0:T(8,128)(2,1)}, u32[]{:S(2)}) copy-start(bf16[2,256,32]{1,2,0:T(8,128)(2,1)} %param.16) | copy-start | bytes 98308
  44.2 3.3 %copy-start.8 = (f32[2,512]{1,0:T(2,128)S(1)}, f32[2,512]{1,0:T(2,128)}, u32[]{:S(2)}) copy-start(f32[2,512]{1,0:T(2,128)} %diag.3) | copy-start | bytes 12292
  47.6 1.0 %copy-start.2 = (bf16[512,512]{1,0:T(8,128)(2,1)S(1)}, bf16[512,512]{1,0:T(8,128)(2,1)}, u32[]{:S(2)}) copy-start(bf16[512,512]{1,0:T(8,128)(2,1)} %uown.1) | copy-start | bytes 1572868
  52.5 39.1 %copy-start.3 = (bf16[512,512]{1,0:T(8,128)(2,1)S(1)}, bf16[512,512]{1,0:T(8,128)(2,1)}, u32[]{:S(2)}) copy-start(bf16[512,512]{1,0:T(8,128)(2,1)} %uown.1) | copy-start | bytes 1572868
  52.5 39.1 %collective-permute-start.3 = (bf16[1040,512]{1,0:T(8,128)(2,1)S(1)}, bf16[1040,512]{1,0:T(8,128)(2,1)S(1)}, u32[]{:S(2)}, u32[]{:S(2)}) collective-permute-start(bf16[1040,512]{1,0:T(8,128)(2,1)S(1)} %get-tuple-element.5.vown), channel_id=1, source_target_pairs={{1,0},{2,1},{3,2},{4,3},{5,4},{6,5},{7,6},{8,7},{9,8},{10,9},{11,1... | collective-permute-start | bytes 3194888 | tf_op jit(solution)/shard_map/ppermute | solution.py:315
  52.9 38.8 %collective-permute-start.2 = (bf16[1040,512]{1,0:T(8,128)(2,1)S(1)}, bf16[1040,512]{1,0:T(8,128)(2,1)S(1)}, u32[]{:S(2)}, u32[]{:S(2)}) collective-permute-start(bf16[1040,512]{1,0:T(8,128)(2,1)S(1)} %get-tuple-element.5.vown), channel_id=1, source_target_pairs={{0,1},{1,2},{2,3},{3,4},{4,5},{5,6},{6,7},{7,8},{8,9},{9,10},{10,1... | collective-permute-start | bytes 3194888 | tf_op jit(solution)/shard_map/ppermute | solution.py:315

commit v3 on v2

--- a/solution.py
+++ b/solution.py
@@ -98,40 +98,49 @@
         send_all(out, slice(0, rank), 2 * pair + 1, second.astype(BF16))
 
 
-def share_kernel(far_cols, coup, out):
+def share_kernel(far_cols, coup, after, out):
     ops, blocks, far, rank, _ = coup.shape
-    rows = blocks * ops * rank
-    parts = []
+    body = ops * rank
+    whole, rest = [], []
     for b in range(blocks):
-        for o in range(ops):
-            parts.append(jnp.concatenate([coup[o, b, f] for f in range(far)], axis=1))
-    lane = lax.broadcasted_iota(jnp.int32, (STATS, far * rank), 1)
-    names = jnp.zeros((STATS, far * rank), F32)
+        tiles = [
+            jnp.concatenate([coup[o, b, f] for f in range(far)], axis=1) for o in range(ops)
+        ]
+        tiles = jnp.concatenate(tiles, axis=0)
+        whole.append(tiles[:, :LANES])
+        rest.append(tiles[:, LANES:])
+    lane = lax.broadcasted_iota(jnp.int32, (STATS, LANES), 1)
+    names = jnp.zeros((STATS, LANES), F32)
     for b in range(blocks):
         for f in range(far):
             names = jnp.where(lane == b * far + f, far_cols[b, f].astype(F32), names)
-    whole = jnp.concatenate(parts + [names.astype(BF16)], axis=0)
+    whole = jnp.concatenate(
+        whole + [jnp.concatenate(rest, axis=1), names.astype(BF16)], axis=0
+    )
     for s in range(out.shape[0]):
         out[s] = whole
 
 
-def couple(cols, coup, s, b, ops, rank, z):
+def coupling_rows(coup, s, b, ops, rank):
+    body = ops * rank
+    first = coup[s, b * body:(b + 1) * body, :]
+    rest = coup[s, 2 * body:3 * body, b * HALF:(b + 1) * HALF]
+    return jnp.concatenate([first, rest], axis=1)
+
+
+def couple(cols, coup, s, b, ops, rank, far, z):
     blocks = 2
-    far = coup.shape[2] // rank
     at = (s * blocks + b) * far
-    picked = []
-    for f in range(far):
-        start = pl.multiple_of(cols[at + f] * rank, rank)
-        picked.append([x[pl.ds(start, rank), :] for x in z])
-    res = []
+    lhs = coupling_rows(coup, s, b, ops, rank)
+    starts = [pl.multiple_of(cols[at + f] * rank, rank) for f in range(far)]
+    picked = [
+        jnp.concatenate([x[pl.ds(start, rank), :] for start in starts], axis=0) for x in z
+    ]
     if len(z) == 1:
-        lhs = coup[s, b * ops * rank:(b + 1) * ops * rank, :]
-        return dot(lhs, jnp.concatenate([p[0] for p in picked], axis=0))
-    for o in range(ops):
-        row = (b * ops + o) * rank
-        rhs = jnp.concatenate([p[o] for p in picked], axis=0)
-        res.append(dot(coup[s, row:row + rank, :], rhs))
-    return jnp.concatenate(res, axis=0)
+        return dot(lhs, picked[0])
+    return jnp.concatenate(
+        [dot(lhs[o * rank:(o + 1) * rank], picked[o]) for o in range(ops)], axis=0
+    )
 
 
 def spread_rows(source, target, rank):
@@ -142,10 +151,10 @@
     target[...] = both.reshape(n * 2 * rank, LANES).astype(BF16)
 
 
-def first_couple(ops, rank, cols, z1, coup, out, zs):
+def first_couple(ops, rank, far, cols, z1, coup, out, zs):
     spread_rows(z1[...].astype(F32), zs, rank)
     for s in range(out.shape[0]):
-        c = [couple(cols, coup, s, b, ops, rank, [zs]) for b in range(2)]
+        c = [couple(cols, coup, s, b, ops, rank, far, [zs]) for b in range(2)]
         out[s] = halves(c[0], c[1])[0].astype(BF16)
 
 
@@ -181,11 +190,10 @@
     return jnp.concatenate([column] * (columns // LANES), axis=1)
 
 
-def image_kernel(w, low, own, high, diag, left, right, cmsg, vout, mout, image, coef):
+def near_kernel(w, low, own, high, diag, left, image, vout):
     ops = image.shape[0]
-    blocks, rank, size = right.shape
+    blocks, rank, size = left.shape
     rows, columns = own.shape
-    take_coefs(cmsg, coef, ops * rank)
     inner = [None] * ops
     squares = None
     for b in range(blocks):
@@ -194,23 +202,59 @@
         part = jnp.sum(ub * ub, axis=0, keepdims=True)
         squares = part if squares is None else squares + part
         for o in range(ops):
-            far = dot(left[b], coef[b, o * rank:(o + 1) * rank, :], ((0,), (0,)))
             value = (
                 product[o * size:(o + 1) * size]
                 + diagonal_of(diag, o, b, size, columns) * ub
-                + far.astype(BF16).astype(F32)
             )
+            image[o, b * size:(b + 1) * size, :] = value
+            part = jnp.sum(ub * value, axis=0, keepdims=True)
+            inner[o] = part if inner[o] is None else inner[o] + part
+    stats = []
+    good = squares > 0
+    for o in range(ops):
+        shift = jnp.where(good, inner[o] / jnp.where(good, squares, 1.0), 0.0)
+        pieces = split3(shift)
+        stats += pieces
+        shift = pieces[0].astype(F32) + pieces[1].astype(F32) + pieces[2].astype(F32)
+        for b in range(blocks):
+            ub = own[b * size:(b + 1) * size, :].astype(F32)
+            v = image[o, b * size:(b + 1) * size, :] - shift * ub
+            image[o, b * size:(b + 1) * size, :] = v
+            vout[(o * blocks + b) * size:(o * blocks + b + 1) * size, :] = v.astype(BF16)
+    zero = jnp.zeros((1, columns), BF16)
+    at = ops * rows
+    vout[at:at + STATS, :] = jnp.concatenate(stats + [zero] * (STATS - len(stats)), axis=0)
+    for b in range(blocks):
+        vout[at + STATS:at + STATS + rank, b * size:(b + 1) * size] = left[b]
+
+
+def image_kernel(own, near, edge, left, right, cmsg, vout, mout, image, coef):
+    ops = image.shape[0]
+    blocks, rank, size = right.shape
+    rows, columns = own.shape
+    take_coefs(cmsg, coef, ops * rank)
+    inner = [None] * ops
+    squares = None
+    for b in range(blocks):
+        ub = own[b * size:(b + 1) * size, :].astype(F32)
+        part = jnp.sum(ub * ub, axis=0, keepdims=True)
+        squares = part if squares is None else squares + part
+        for o in range(ops):
+            far = dot(left[b], coef[b, o * rank:(o + 1) * rank, :], ((0,), (0,)))
+            value = near[o, b * size:(b + 1) * size, :] + far.astype(BF16).astype(F32)
             image[o, b * size:(b + 1) * size, :] = value
             part = jnp.sum(ub * value, axis=0, keepdims=True)
             inner[o] = part if inner[o] is None else inner[o] + part
     stats = []
     spreads = []
     good = squares > 0
+    edges = edge[0:STATS, :].astype(F32)
     for o in range(ops):
-        shift = jnp.where(good, inner[o] / jnp.where(good, squares, 1.0), 0.0)
-        pieces = split3(shift)
+        before = row3(edges, o)
+        change = jnp.where(good, inner[o] / jnp.where(good, squares, 1.0), 0.0)
+        pieces = split3(before + change)
         stats += pieces
-        shift = pieces[0].astype(F32) + pieces[1].astype(F32) + pieces[2].astype(F32)
+        shift = pieces[0].astype(F32) + pieces[1].astype(F32) + pieces[2].astype(F32) - before
         spread = None
         z = []
         for b in range(blocks):
@@ -239,7 +283,25 @@
         send_all(mout, slice(ops * rank, ops * rank + STATS), 2 * pair + 1, second.astype(BF16))
 
 
-def second_couple(panels, ops, rank, cols, z1, msg, coup, out, zs):
+def neighbour_kernel(size, low, high, clow, chigh, olow, ohigh, coef):
+    blocks, body, columns = coef.shape
+    rows = blocks * size
+    ops = (low.shape[0] - STATS) // rows
+    rank = body // ops
+    for v, cmsg, out in ((low, clow, olow), (high, chigh, ohigh)):
+        take_coefs(cmsg, coef, body)
+        for b in range(blocks):
+            left = v[ops * rows + STATS:, b * size:(b + 1) * size]
+            for o in range(ops):
+                far = dot(left, coef[b, o * rank:(o + 1) * rank, :], ((0,), (0,)))
+                at = (o * blocks + b) * size
+                out[at:at + size, :] = (
+                    v[at:at + size, :].astype(F32) + far.astype(BF16).astype(F32)
+                ).astype(BF16)
+        out[ops * rows:, :] = v[ops * rows:ops * rows + STATS, :]
+
+
+def second_couple(panels, ops, rank, far, cols, z1, msg, coup, out, zs):
     body = ops * rank
     st = msg[:, body:body + STATS, :].astype(F32)
     shift = [join3(st, o) for o in range(ops)]
@@ -265,7 +327,7 @@
     rows += [jnp.zeros_like(rows[0])] * (STATS - len(rows))
     rows = jnp.concatenate(rows, axis=0)
     for s in range(out.shape[0]):
-        c = [couple(cols, coup, s, b, ops, rank, [zs.at[o] for o in range(ops)]) for b in range(2)]
+        c = [couple(cols, coup, s, b, ops, rank, far, [zs.at[o] for o in range(ops)]) for b in range(2)]
         out[s, 0:body, :] = halves(c[0], c[1])[0].astype(BF16)
         out[s, body:body + STATS, :] = rows
 
@@ -345,15 +407,17 @@
     left = jnp.transpose(basis_left, (0, 2, 1))
     right = jnp.transpose(basis_right, (0, 2, 1))
 
+    low, high = ring(sources)
     z1 = call(coeff_kernel, sds((n, rank, LANES), BF16), [VMEM, VMEM])(sources, right)
     z1 = exchange(z1, False)
-    low, high = ring(sources)
 
     held = call(
-        share_kernel, sds((SLICES, blocks * body + STATS, far * rank), BF16), [SMEM, VMEM]
-    )(far_cols, couplings)
+        share_kernel,
+        sds((SLICES, (blocks + 1) * body + STATS, LANES), BF16),
+        [SMEM, VMEM, pl.BlockSpec(memory_space=pl.ANY)],
+    )(far_cols, couplings, z1)
     held = exchange(held, True)
-    cols = held[:, blocks * body, :blocks * far].astype(jnp.int32).reshape(-1)
+    cols = held[:, (blocks + 1) * body, :blocks * far].astype(jnp.int32).reshape(-1)
 
     w = call(
         functools.partial(order_tiles, all_blocks),
@@ -361,34 +425,49 @@
         [SMEM, SMEM, SMEM, VMEM],
     )(near_cols, near_count, row0, near_tiles)
 
+    work = 2 * ops * rows * near * size * columns
+    image, edge = call(
+        near_kernel,
+        [sds((ops, rows, columns), F32), sds((ops * rows + STATS + rank, columns), BF16)],
+        [VMEM] * 6,
+        flops=work,
+    )(w, low, sources, high, self_terms, left)
+    vlow, vhigh = ring(edge)
+
     c1 = call(
-        functools.partial(first_couple, ops, rank),
+        functools.partial(first_couple, ops, rank, far),
         sds((SLICES, body, LANES), BF16),
         [SMEM, VMEM, VMEM],
         [pltpu.VMEM((n * blocks * rank, LANES), BF16)],
     )(cols, z1, held)
     c1 = exchange(c1, True)
+    clow, chigh = ring(c1)
 
     v, msg = call(
         image_kernel,
         [sds((ops * rows + STATS, columns), BF16), sds((n, body + STATS, LANES), BF16)],
-        [VMEM] * 8,
+        [VMEM, VMEM, pl.BlockSpec(memory_space=pltpu.VMEM), VMEM, VMEM, VMEM],
         [
             pltpu.VMEM((ops, rows, columns), F32),
             pltpu.VMEM((blocks, body, columns), BF16),
         ],
-        flops=2 * ops * rows * near * size * columns,
-    )(w, low, sources, high, self_terms, left, right, c1)
+    )(sources, image, edge[ops * rows:ops * rows + STATS], left, right, c1)
     msg = exchange(msg, False)
-    vlow, vhigh = ring(v)
 
     c2 = call(
-        functools.partial(second_couple, all_blocks * size, ops, rank),
+        functools.partial(second_couple, all_blocks * size, ops, rank, far),
         sds((SLICES, body + STATS, LANES), BF16),
         [SMEM, VMEM, VMEM, VMEM],
         [pltpu.VMEM((ops, n * blocks * rank, LANES), BF16)],
     )(cols, z1, msg, held)
     c2 = exchange(c2, True)
+
+    vlow, vhigh = call(
+        functools.partial(neighbour_kernel, size),
+        [sds((ops * rows + STATS, columns), BF16)] * 2,
+        [VMEM] * 4,
+        [pltpu.VMEM((blocks, body, columns), BF16)],
+    )(vlow, vhigh, clow, chigh)
 
     images, heights, norms = call(
         final_kernel,
@@ -399,7 +478,7 @@
             pltpu.VMEM((blocks, body, columns), BF16),
             pltpu.VMEM((STATS, columns), F32),
         ],
-        flops=2 * ops * rows * near * size * columns,
+        flops=work,
     )(w, low, sources, high, vlow, v, vhigh, self_terms, left, c2)
     return images, heights, norms
 

time: 97.3 us -> 112 us (1.15)
  local copies, waits for them, and re-layouts: 5.3 us -> 16.2 us
  Pallas kernels: 15.5 us -> 20.3 us
  waiting for transfers between devices: 13.4 us -> 9.8 us
  blocking collectives: 37 us -> 38.3 us
    all_to_all x3, waiting for transfers between devices: 13.4 us -> 2.71 us  [exchange(): lax.all_to_all(x, 'store', 0, 0, axis_index_groups=groups if part else No...]
    unnamed x24 -> x40, local copies, waits for them, and re-layouts: 5.22 us -> 15.4 us
    pallas_call x3 -> x5, Pallas kernels: 4.85 us -> 12.7 us  [the longest x1 4.43 us: shards(): call(near_kernel, [sds((ops, rows, columns), F32), sds((ops * rows + STAT...]
    ppermute x2 -> x3, waiting for transfers between devices: 0.01 us -> 4.57 us  [ring(): lax.ppermute(block, 'store', forward)]
    ppermute x2 -> x3, starting transfers between devices: 5.05 us -> 8.04 us  [ring(): lax.ppermute(block, 'store', backward)]
    all_to_all x3, starting transfers between devices: 19.4 us -> 16.6 us  [exchange(): lax.all_to_all(x, 'store', 0, 0, axis_index_groups=groups if part else No...]
    ppermute x2 -> x3, waiting for transfers between devices: 0.01 us -> 2.52 us  [ring(): lax.ppermute(block, 'store', backward)]
    pallas_call x1, Pallas kernels: 3.91 us -> 1.46 us  [shards(): call(image_kernel, [sds((ops * rows + STATS, columns), BF16), sds((n, bod...]
  transfers between devices with their start and end apart: 7 -> 9, of which waited for: 3 -> 3; matrix products, arithmetic and copies ran while one was open for 0% -> 1% of each run, Pallas kernels for 5% -> 12%
where the time goes in v3:
time: 112 us; the launch traced here: 111 us
  blocking collectives  38.3 us (34%)
  starting transfers between devices  24.6 us (22%)
  Pallas kernels  20.3 us (18%)
  local copies, waits for them, and re-layouts  16.2 us (14%)
  waiting for transfers between devices  9.8 us (9%)
    all_to_all x2, blocking collectives, exchange(): lax.all_to_all(x, 'store', 0, 0, axis_index_groups=groups if part else No...  38.3 us
    all_to_all x3, starting transfers between devices, exchange(): lax.all_to_all(x, 'store', 0, 0, axis_index_groups=groups if part else No...  16.6 us
    unnamed x40, local copies, waits for them, and re-layouts  15.4 us
    ppermute x3, starting transfers between devices, ring(): lax.ppermute(block, 'store', backward)  8.04 us
    pallas_call x1, Pallas kernels, shards(): call(final_kernel, [sds((ops, rows, columns), F32), sds((ops, columns), F...  4.93 us
    ppermute x3, waiting for transfers between devices, ring(): lax.ppermute(block, 'store', forward)  4.57 us
    pallas_call x1, Pallas kernels, shards(): call(near_kernel, [sds((ops, rows, columns), F32), sds((ops * rows + STAT...  4.43 us
    pallas_call x1, Pallas kernels, shards(): call(functools.partial(second_couple, all_blocks * size, ops, rank, far),...  2.75 us
  transfers between devices with their start and end apart: 9, of which 3 were waited for; matrix products, arithmetic and copies ran while one was open for 1% of the time, Pallas kernels for 12%

profile of v3, /device:TPU:0, one launch (start us, length us, event | category | flops | bytes accessed | tf_op | source)
XLA Modules:
  0.0 110.7 jit_solution(17055076651679409630)
XLA Ops:
  0.6 0.0 copy-start
  0.6 1.0 copy-done
  1.7 0.0 copy-start.14
  1.7 0.8 copy-done.14
  2.4 0.3 shard_map.114
  2.7 0.0 copy-start.1
  2.7 15.3 %all_to_all.25.after.z1 = bf16[16,32,128]{2,1,0:T(8,128)(2,1)S(1)} all-to-all(bf16[16,32,128]{2,1,0:T(8,128)(2,1)S(1)} %shard_map.114), channel_id=1, replica_groups=mesh['groups'=2,'store'=16] {'store'}, dimensions={0} | all-to-all | bytes 262144 | tf_op jit(solution)/shard_map/all_to_all | solution.py:402
  18.0 0.0 copy-start.12
  18.0 0.9 copy-done.12
  18.9 0.0 copy-start.17
  18.9 0.7 copy-done.17
  19.6 0.0 copy-start.18
  19.6 0.0 copy-start.19
  19.6 1.5 %shard_map.115 = bf16[8,208,128]{2,1,0:T(8,128)(2,1)} custom-call(s32[2,6]{1,0:T(2,128)S(1)} %copy-done.17, bf16[2,2,6,32,32]{4,3,2,1,0:T(8,128)(2,1)S(1)} %copy-done.12, bf16[16,32,128]{2,1,0:T(8,128)(2,1)S(1)} %all_to_all.25.after.z1), custom_call_target="tpu_custom_call" | custom-call | tf_op jit(solution)/shard_map/pallas_call | solution.py:414
  21.0 4.1 %all-to-all-start.1 = ((bf16[8,208,128]{2,1,0:T(8,128)(2,1)}), bf16[8,208,128]{2,1,0:T(8,128)(2,1)}, u32[]{:S(2)}, u32[]{:S(2)}) async-start(bf16[8,208,128]{2,1,0:T(8,128)(2,1)} %shard_map.115), calls=%async_computation.1 | async-start | bytes 851968 | tf_op jit(solution)/shard_map/all_to_all | solution.py:402
  25.2 0.0 copy-done.1
  25.2 2.4 %collective-permute-start.1 = (bf16[512,512]{1,0:T(8,128)(2,1)S(1)}, bf16[512,512]{1,0:T(8,128)(2,1)}, u32[]{:S(2)}, u32[]{:S(2)}) collective-permute-start(bf16[512,512]{1,0:T(8,128)(2,1)S(1)} %copy-done.1), channel_id=1, source_target_pairs={{1,0},{2,1},{3,2},{4,3},{5,4},{6,5},{7,6},{8,7},{9,8},{10,9},{11,1... | collective-permute-start | bytes 1572872 | tf_op jit(solution)/shard_map/ppermute | solution.py:377
  27.6 0.0 collective-permute-start
  27.6 0.0 copy-done.18
  27.6 0.0 copy-done.19
  27.6 0.0 copy-start.2
  27.6 1.7 %copy-done.2 = bf16[2,2,5,256,256]{4,3,2,1,0:T(8,128)(2,1)S(1)} copy-done((bf16[2,2,5,256,256]{4,3,2,1,0:T(8,128)(2,1)S(1)}, bf16[2,2,5,256,256]{4,3,2,1,0:T(8,128)(2,1)}, u32[]{:S(2)}) %copy-start.2) | copy-done | bytes 2621464
  29.4 0.9 shard_map.112.w
  30.3 2.7 %all-to-all-done.1.coup = bf16[8,208,128]{2,1,0:T(8,128)(2,1)} async-done(((bf16[8,208,128]{2,1,0:T(8,128)(2,1)}), bf16[8,208,128]{2,1,0:T(8,128)(2,1)}, u32[]{:S(2)}, u32[]{:S(2)}) %all-to-all-start.1) | async-done | bytes 426016 | tf_op jit(solution)/shard_map/all_to_all | solution.py:402
  33.0 0.7 fusion
  33.7 0.1 reshape.14.cols
  33.8 1.6 %shard_map.116 = bf16[8,64,128]{2,1,0:T(8,128)(2,1)S(1)} custom-call(s32[96]{0:T(128)S(1)} %reshape.14.cols, bf16[16,32,128]{2,1,0:T(8,128)(2,1)S(1)} %all_to_all.25.after.z1, bf16[8,208,128]{2,1,0:T(8,128)(2,1)} %all-to-all-done.1.coup), custom_call_target="tpu_custom_call" | custom-call | tf_op jit(solution)/shard_map/pallas_call | solution.py:437
  35.4 0.0 copy-start.11
  35.4 0.6 copy-done.11
  36.1 8.6 %all-to-all-start.2 = ((bf16[8,64,128]{2,1,0:T(8,128)(2,1)}), bf16[8,64,128]{2,1,0:T(8,128)(2,1)S(1)}, u32[]{:S(2)}, u32[]{:S(2)}) async-start(bf16[8,64,128]{2,1,0:T(8,128)(2,1)} %copy-done.11), calls=%async_computation.2 | async-start | bytes 262144 | tf_op jit(solution)/shard_map/all_to_all | solution.py:402
  44.7 0.0 collective-permute-done.1.high.uhigh
  44.7 0.0 collective-permute-done.low.ulow
  44.7 0.0 copy-done.13
  44.7 0.0 copy-done.16
  44.7 0.0 copy-start.15
  44.7 4.4 %shard_map.113 = (f32[2,512,512]{2,1,0:T(8,128)S(1)}, bf16[1072,512]{1,0:T(8,128)(2,1)}) custom-call(bf16[2,512,1280]{2,1,0:T(8,128)(2,1)S(1)} %shard_map.112.w, bf16[512,512]{1,0:T(8,128)(2,1)} %collective-permute-done.low.ulow, bf16[512,512]{1,0:T(8,128)(2,1)S(1)} %copy-done.1, bf16[512,512]{1,0:T(8,128)(2,1)} %collective-permute-done.1.high.uhigh, ...), custom_call_target="tpu_custom_call" | custom-call | flops 1342177280 | tf_op jit(solution)/shard_map/pallas_call | solution.py:429
  49.2 1.3 %copy-done.3 = f32[2,512,512]{2,1,0:T(8,128)} copy-done((f32[2,512,512]{2,1,0:T(8,128)}, f32[2,512,512]{2,1,0:T(8,128)S(1)}, u32[]{:S(2)}) %copy-start.3) | copy-done | bytes 2097176
  50.5 2.8 %collective-permute-start.3 = (bf16[1072,512]{1,0:T(8,128)(2,1)}, bf16[1072,512]{1,0:T(8,128)(2,1)}, u32[]{:S(2)}, u32[]{:S(2)}) collective-permute-start(bf16[1072,512]{1,0:T(8,128)(2,1)} %get-tuple-element.9), channel_id=1, source_target_pairs={{1,0},{2,1},{3,2},{4,3},{5,4},{6,5},{7,6},{8,7},{9,8},{10,9},{11,1... | collective-permute-start | bytes 3293192 | tf_op jit(solution)/shard_map/ppermute | solution.py:377
  53.3 0.0 collective-permute-start.2
  53.3 0.7 slice.7.edge
  54.0 0.0 all-to-all-done.2.cmsg
  54.0 0.0 copy-done.15
  54.0 1.6 %copy-done.4 = f32[2,512,512]{2,1,0:T(8,128)S(1)} copy-done((f32[2,512,512]{2,1,0:T(8,128)S(1)}, f32[2,512,512]{2,1,0:T(8,128)}, u32[]{:S(2)}) %copy-start.4) | copy-done | bytes 2097176
  55.6 1.5 %shard_map.118 = (bf16[1040,512]{1,0:T(8,128)(2,1)S(1)}, bf16[16,80,128]{2,1,0:T(8,128)(2,1)S(1)}) custom-call(bf16[512,512]{1,0:T(8,128)(2,1)S(1)} %copy-done.1, f32[2,512,512]{2,1,0:T(8,128)S(1)} %copy-done.4, bf16[16,512]{1,0:T(8,128)(2,1)S(1)} %slice.7.edge, bf16[2,32,256]{2,1,0:T(8,128)(2,1)S(1)} %bitcast.4, bf16[2,32,256]{2,1,0:T(8,128)(2,1)S(1)} %bitcast.7, ...), custom_call_target="tpu_custom_call" | custom-call | tf_op jit(solution)/shard_map/pallas_call | solution.py:446
  57.1 0.0 copy-start.5
  57.1 1.0 copy-done.5
  58.1 23.1 %all_to_all.26.msg = bf16[16,80,128]{2,1,0:T(8,128)(2,1)S(1)} all-to-all(bf16[16,80,128]{2,1,0:T(8,128)(2,1)S(1)} %get-tuple-element.14), channel_id=1, replica_groups=mesh['groups'=2,'store'=16] {'store'}, dimensions={0} | all-to-all | bytes 655360 | tf_op jit(solution)/shard_map/all_to_all | solution.py:402
  81.2 2.7 %shard_map.119 = bf16[8,80,128]{2,1,0:T(8,128)(2,1)} custom-call(s32[96]{0:T(128)S(1)} %reshape.14.cols, bf16[16,32,128]{2,1,0:T(8,128)(2,1)S(1)} %all_to_all.25.after.z1, bf16[16,80,128]{2,1,0:T(8,128)(2,1)S(1)} %all_to_all.26.msg, bf16[8,208,128]{2,1,0:T(8,128)(2,1)} %all-to-all-done.1.coup), custom_call_target="tpu_custom_call" | custom-call | tf_op jit(solution)/shard_map/pallas_call | solution.py:457
  83.9 3.8 %all-to-all-start.4 = ((bf16[8,80,128]{2,1,0:T(8,128)(2,1)}), bf16[8,80,128]{2,1,0:T(8,128)(2,1)S(1)}, u32[]{:S(2)}, u32[]{:S(2)}) async-start(bf16[8,80,128]{2,1,0:T(8,128)(2,1)} %shard_map.119), calls=%async_computation.4 | async-start | bytes 327680 | tf_op jit(solution)/shard_map/all_to_all | solution.py:402
  87.7 2.8 %collective-permute-start.5 = (bf16[8,64,128]{2,1,0:T(8,128)(2,1)S(1)}, bf16[8,64,128]{2,1,0:T(8,128)(2,1)S(1)}, u32[]{:S(2)}, u32[]{:S(2)}) collective-permute-start(bf16[8,64,128]{2,1,0:T(8,128)(2,1)S(1)} %all-to-all-done.2.cmsg), channel_id=1, source_target_pairs={{1,0},{2,1},{3,2},{4,3},{5,4},{6,5},{7,6},{8,7},{9,8},{10,9},{11,1... | collective-permute-start | bytes 393224 | tf_op jit(solution)/shard_map/ppermute | solution.py:377
  90.5 0.0 collective-permute-start.4
  90.5 2.5 %collective-permute-done.5.chigh = bf16[8,64,128]{2,1,0:T(8,128)(2,1)S(1)} collective-permute-done((bf16[8,64,128]{2,1,0:T(8,128)(2,1)S(1)}, bf16[8,64,128]{2,1,0:T(8,128)(2,1)S(1)}, u32[]{:S(2)}, u32[]{:S(2)}) %collective-permute-start.5) | collective-permute-done | bytes 131104 | tf_op jit(solution)/shard_map/ppermute | solution.py:377
  93.1 4.6 %collective-permute-done.4.clow = bf16[8,64,128]{2,1,0:T(8,128)(2,1)S(1)} collective-permute-done((bf16[8,64,128]{2,1,0:T(8,128)(2,1)S(1)}, bf16[8,64,128]{2,1,0:T(8,128)(2,1)S(1)}, u32[]{:S(2)}, u32[]{:S(2)}) %collective-permute-start.4) | collective-permute-done | bytes 131104 | tf_op jit(solution)/shard_map/ppermute | solution.py:377
  97.6 0.0 collective-permute-done.3.high
  97.6 0.0 collective-permute-done.2.low
  97.6 2.5 %shard_map.117 = (bf16[1040,512]{1,0:T(8,128)(2,1)S(1)}, bf16[1040,512]{1,0:T(8,128)(2,1)S(1)}) custom-call(bf16[1072,512]{1,0:T(8,128)(2,1)} %collective-permute-done.2.low, bf16[1072,512]{1,0:T(8,128)(2,1)} %collective-permute-done.3.high, bf16[8,64,128]{2,1,0:T(8,128)(2,1)S(1)} %collective-permute-done.4.clow, ...), custom_call_target="tpu_custom_call" | custom-call | tf_op jit(solution)/shard_map/pallas_call | solution.py:465
  100.1 0.0 copy-start.7
  100.1 1.0 copy-done.7
  101.1 1.0 copy-done.9
  102.1 0.0 all-to-all-done.4.cmsg
  102.1 1.2 %copy-done.6 = bf16[1040,512]{1,0:T(8,128)(2,1)S(1)} copy-done((bf16[1040,512]{1,0:T(8,128)(2,1)S(1)}, bf16[1040,512]{1,0:T(8,128)(2,1)}, u32[]{:S(2)}) %copy-start.6) | copy-done | bytes 1064984
  103.3 1.2 %copy-done.8 = bf16[1040,512]{1,0:T(8,128)(2,1)S(1)} copy-done((bf16[1040,512]{1,0:T(8,128)(2,1)S(1)}, bf16[1040,512]{1,0:T(8,128)(2,1)}, u32[]{:S(2)}) %copy-start.8) | copy-done | bytes 1064984
  104.5 1.2 %copy-done.10 = bf16[1040,512]{1,0:T(8,128)(2,1)S(1)} copy-done((bf16[1040,512]{1,0:T(8,128)(2,1)S(1)}, bf16[1040,512]{1,0:T(8,128)(2,1)}, u32[]{:S(2)}) %copy-start.10) | copy-done | bytes 1064984
  105.8 4.9 %shard_map.120 = (f32[2,512,512]{2,1,0:T(8,128)}, f32[2,512]{1,0:T(2,128)}, f32[2,512]{1,0:T(2,128)}) custom-call(bf16[2,512,1280]{2,1,0:T(8,128)(2,1)S(1)} %shard_map.112.w, bf16[512,512]{1,0:T(8,128)(2,1)} %collective-permute-done.low.ulow, bf16[512,512]{1,0:T(8,128)(2,1)S(1)} %copy-done.1, bf16[512,512]{1,0:T(8,128)(2,1)} %collective-permute-done.1.high.uhigh, ...), custom_call_target="tpu_custom_call" | custom-call | flops 1342177280 | tf_op jit(solution)/shard_map/pallas_call | solution.py:472
  (8 shorter events, 0.0 us)
Async XLA Ops:
  0.6 1.0 copy-start
  1.7 0.8 copy-start.14
  2.7 22.5 %copy-start.1 = (bf16[512,512]{1,0:T(8,128)(2,1)S(1)}, bf16[512,512]{1,0:T(8,128)(2,1)}, u32[]{:S(2)}) copy-start(bf16[512,512]{1,0:T(8,128)(2,1)} %uown.1) | copy-start | bytes 1572868
  18.0 0.9 copy-start.12
  18.9 0.7 copy-start.17
  19.6 8.0 %copy-start.18 = (s32[2,5]{1,0:T(2,128)S(1)}, s32[2,5]{1,0:T(2,128)}, u32[]{:S(2)}) copy-start(s32[2,5]{1,0:T(2,128)} %cols.1) | copy-start | bytes 124
  19.6 8.0 %copy-start.19 = (s32[2]{0:T(128)S(1)}, s32[2]{0:T(128)}, u32[]{:S(2)}) copy-start(s32[2]{0:T(128)} %count.1) | copy-start | bytes 28
  21.0 11.9 %all-to-all-start.1 = ((bf16[8,208,128]{2,1,0:T(8,128)(2,1)}), bf16[8,208,128]{2,1,0:T(8,128)(2,1)}, u32[]{:S(2)}, u32[]{:S(2)}) async-start(bf16[8,208,128]{2,1,0:T(8,128)(2,1)} %shard_map.115), calls=%async_computation.1 | async-start | bytes 851968 | tf_op jit(solution)/shard_map/all_to_all | solution.py:402
  25.2 19.5 %collective-permute-start.1 = (bf16[512,512]{1,0:T(8,128)(2,1)S(1)}, bf16[512,512]{1,0:T(8,128)(2,1)}, u32[]{:S(2)}, u32[]{:S(2)}) collective-permute-start(bf16[512,512]{1,0:T(8,128)(2,1)S(1)} %copy-done.1), channel_id=1, source_target_pairs={{1,0},{2,1},{3,2},{4,3},{5,4},{6,5},{7,6},{8,7},{9,8},{10,9},{11,1... | collective-permute-start | bytes 1572872 | tf_op jit(solution)/shard_map/ppermute | solution.py:377
  27.6 17.1 %collective-permute-start = (bf16[512,512]{1,0:T(8,128)(2,1)S(1)}, bf16[512,512]{1,0:T(8,128)(2,1)}, u32[]{:S(2)}, u32[]{:S(2)}) collective-permute-start(bf16[512,512]{1,0:T(8,128)(2,1)S(1)} %copy-done.1), channel_id=1, source_target_pairs={{0,1},{1,2},{2,3},{3,4},{4,5},{5,6},{6,7},{7,8},{8,9},{9,10},{10,1... | collective-permute-start | bytes 1572872 | tf_op jit(solution)/shard_map/ppermute | solution.py:377
  27.6 1.7 %copy-start.2 = (bf16[2,2,5,256,256]{4,3,2,1,0:T(8,128)(2,1)S(1)}, bf16[2,2,5,256,256]{4,3,2,1,0:T(8,128)(2,1)}, u32[]{:S(2)}) copy-start(bf16[2,2,5,256,256]{4,3,2,1,0:T(8,128)(2,1)} %tiles.1) | copy-start | bytes 7864324
  29.4 15.3 %copy-start.13 = (bf16[2,256,32]{1,2,0:T(8,128)(2,1)S(1)}, bf16[2,256,32]{1,2,0:T(8,128)(2,1)}, u32[]{:S(2)}) copy-start(bf16[2,256,32]{1,2,0:T(8,128)(2,1)} %param.15) | copy-start | bytes 98308
  29.4 15.3 %copy-start.16 = (f32[2,512]{1,0:T(2,128)S(1)}, f32[2,512]{1,0:T(2,128)}, u32[]{:S(2)}) copy-start(f32[2,512]{1,0:T(2,128)} %diag.3) | copy-start | bytes 12292
  35.4 0.6 copy-start.11
  36.1 18.0 %all-to-all-start.2 = ((bf16[8,64,128]{2,1,0:T(8,128)(2,1)}), bf16[8,64,128]{2,1,0:T(8,128)(2,1)S(1)}, u32[]{:S(2)}, u32[]{:S(2)}) async-start(bf16[8,64,128]{2,1,0:T(8,128)(2,1)} %copy-done.11), calls=%async_computation.2 | async-start | bytes 262144 | tf_op jit(solution)/shard_map/all_to_all | solution.py:402
  44.7 9.3 %copy-start.15 = (bf16[2,256,32]{1,2,0:T(8,128)(2,1)S(1)}, bf16[2,256,32]{1,2,0:T(8,128)(2,1)}, u32[]{:S(2)}) copy-start(bf16[2,256,32]{1,2,0:T(8,128)(2,1)} %param.16) | copy-start | bytes 98308
  49.1 1.3 %copy-start.3 = (f32[2,512,512]{2,1,0:T(8,128)}, f32[2,512,512]{2,1,0:T(8,128)S(1)}, u32[]{:S(2)}) copy-start(f32[2,512,512]{2,1,0:T(8,128)S(1)} %get-tuple-element.11.near) | copy-start | bytes 6291460
  50.5 47.2 %collective-permute-start.3 = (bf16[1072,512]{1,0:T(8,128)(2,1)}, bf16[1072,512]{1,0:T(8,128)(2,1)}, u32[]{:S(2)}, u32[]{:S(2)}) collective-permute-start(bf16[1072,512]{1,0:T(8,128)(2,1)} %get-tuple-element.9), channel_id=1, source_target_pairs={{1,0},{2,1},{3,2},{4,3},{5,4},{6,5},{7,6},{8,7},{9,8},{10,9},{11,1... | collective-permute-start | bytes 3293192 | tf_op jit(solution)/shard_map/ppermute | solution.py:377
  53.3 44.4 %collective-permute-start.2 = (bf16[1072,512]{1,0:T(8,128)(2,1)}, bf16[1072,512]{1,0:T(8,128)(2,1)}, u32[]{:S(2)}, u32[]{:S(2)}) collective-permute-start(bf16[1072,512]{1,0:T(8,128)(2,1)} %get-tuple-element.9), channel_id=1, source_target_pairs={{0,1},{1,2},{2,3},{3,4},{4,5},{5,6},{6,7},{7,8},{8,9},{9,10},{10,1... | collective-permute-start | bytes 3293192 | tf_op jit(solution)/shard_map/ppermute | solution.py:377
  54.0 1.6 %copy-start.4 = (f32[2,512,512]{2,1,0:T(8,128)S(1)}, f32[2,512,512]{2,1,0:T(8,128)}, u32[]{:S(2)}) copy-start(f32[2,512,512]{2,1,0:T(8,128)} %copy-done.3) | copy-start | bytes 6291460
  57.1 1.0 copy-start.5
  83.9 18.2 %all-to-all-start.4 = ((bf16[8,80,128]{2,1,0:T(8,128)(2,1)}), bf16[8,80,128]{2,1,0:T(8,128)(2,1)S(1)}, u32[]{:S(2)}, u32[]{:S(2)}) async-start(bf16[8,80,128]{2,1,0:T(8,128)(2,1)} %shard_map.119), calls=%async_computation.4 | async-start | bytes 327680 | tf_op jit(solution)/shard_map/all_to_all | solution.py:402
  87.7 5.3 %collective-permute-start.5 = (bf16[8,64,128]{2,1,0:T(8,128)(2,1)S(1)}, bf16[8,64,128]{2,1,0:T(8,128)(2,1)S(1)}, u32[]{:S(2)}, u32[]{:S(2)}) collective-permute-start(bf16[8,64,128]{2,1,0:T(8,128)(2,1)S(1)} %all-to-all-done.2.cmsg), channel_id=1, source_target_pairs={{1,0},{2,1},{3,2},{4,3},{5,4},{6,5},{7,6},{8,7},{9,8},{10,9},{11,1... | collective-permute-start | bytes 393224 | tf_op jit(solution)/shard_map/ppermute | solution.py:377
  90.5 7.1 %collective-permute-start.4 = (bf16[8,64,128]{2,1,0:T(8,128)(2,1)S(1)}, bf16[8,64,128]{2,1,0:T(8,128)(2,1)S(1)}, u32[]{:S(2)}, u32[]{:S(2)}) collective-permute-start(bf16[8,64,128]{2,1,0:T(8,128)(2,1)S(1)} %all-to-all-done.2.cmsg), channel_id=1, source_target_pairs={{0,1},{1,2},{2,3},{3,4},{4,5},{5,6},{6,7},{7,8},{8,9},{9,10},{10,1... | collective-permute-start | bytes 393224 | tf_op jit(solution)/shard_map/ppermute | solution.py:377
  100.1 1.0 copy-start.7
  101.1 1.0 copy-start.9
  102.1 1.2 %copy-start.6 = (bf16[1040,512]{1,0:T(8,128)(2,1)S(1)}, bf16[1040,512]{1,0:T(8,128)(2,1)}, u32[]{:S(2)}) copy-start(bf16[1040,512]{1,0:T(8,128)(2,1)} %copy-done.5) | copy-start | bytes 3194884
  103.3 1.2 %copy-start.8 = (bf16[1040,512]{1,0:T(8,128)(2,1)S(1)}, bf16[1040,512]{1,0:T(8,128)(2,1)}, u32[]{:S(2)}) copy-start(bf16[1040,512]{1,0:T(8,128)(2,1)} %copy-done.7) | copy-start | bytes 3194884
  104.5 1.2 %copy-start.10 = (bf16[1040,512]{1,0:T(8,128)(2,1)S(1)}, bf16[1040,512]{1,0:T(8,128)(2,1)}, u32[]{:S(2)}) copy-start(bf16[1040,512]{1,0:T(8,128)(2,1)} %copy-done.9) | copy-start | bytes 3194884

commit v4 on v2

--- a/solution.py
+++ b/solution.py
@@ -62,16 +62,6 @@
 
 def chunk(x, pair):
     return x[:, pair * LANES:(pair + 1) * LANES]
-
-
-def send_all(out, rows, at, part):
-    n = out.shape[0]
-
-    def put(g, _):
-        out[g * SLICES + at, rows, :] = part
-        return 0
-
-    lax.fori_loop(0, n // SLICES, put, 0, unroll=n == 2 * SLICES)
 
 
 def order_tiles(all_blocks, cols, count, row0, tiles, out):
@@ -89,63 +79,79 @@
                 )
 
 
-def coeff_kernel(u, right, out):
-    blocks, rank, size = right.shape
+def share_kernel(far_cols, u, right, coup, out):
+    ops, blocks, far, rank, _ = coup.shape
+    size = right.shape[2]
     z = [dot(right[b], u[b * size:(b + 1) * size, :]) for b in range(blocks)]
     for pair in range(SLICES // 2):
         first, second = halves(chunk(z[0], pair), chunk(z[1], pair))
-        send_all(out, slice(0, rank), 2 * pair, first.astype(BF16))
-        send_all(out, slice(0, rank), 2 * pair + 1, second.astype(BF16))
-
-
-def share_kernel(far_cols, coup, out):
-    ops, blocks, far, rank, _ = coup.shape
-    rows = blocks * ops * rank
-    parts = []
+        out[2 * pair, 0:rank, :] = first.astype(BF16)
+        out[2 * pair + 1, 0:rank, :] = second.astype(BF16)
+    whole, rest = [], []
     for b in range(blocks):
-        for o in range(ops):
-            parts.append(jnp.concatenate([coup[o, b, f] for f in range(far)], axis=1))
-    lane = lax.broadcasted_iota(jnp.int32, (STATS, far * rank), 1)
-    names = jnp.zeros((STATS, far * rank), F32)
+        tiles = [
+            jnp.concatenate([coup[o, b, f] for f in range(far)], axis=1) for o in range(ops)
+        ]
+        tiles = jnp.concatenate(tiles, axis=0)
+        whole.append(tiles[:, :LANES])
+        rest.append(tiles[:, LANES:])
+    lane = lax.broadcasted_iota(jnp.int32, (STATS, LANES), 1)
+    names = jnp.zeros((STATS, LANES), F32)
     for b in range(blocks):
         for f in range(far):
             names = jnp.where(lane == b * far + f, far_cols[b, f].astype(F32), names)
-    whole = jnp.concatenate(parts + [names.astype(BF16)], axis=0)
-    for s in range(out.shape[0]):
-        out[s] = whole
-
-
-def couple(cols, coup, s, b, ops, rank, z):
-    blocks = 2
-    far = coup.shape[2] // rank
-    at = (s * blocks + b) * far
-    picked = []
-    for f in range(far):
-        start = pl.multiple_of(cols[at + f] * rank, rank)
-        picked.append([x[pl.ds(start, rank), :] for x in z])
-    res = []
+    whole = jnp.concatenate(
+        whole + [jnp.concatenate(rest, axis=1), names.astype(BF16)], axis=0
+    )
+    for s in range(SLICES):
+        out[s, rank:, :] = whole
+
+
+def relay_kernel(first, u, z, uout):
+    z[...] = first[:, 0:z.shape[1], :]
+    uout[...] = u[...]
+
+
+def coupling_rows(held, s, b, ops, rank):
+    body = ops * rank
+    first = held[s, rank + b * body:rank + (b + 1) * body, :]
+    rest = held[s, rank + 2 * body:rank + 3 * body, b * HALF:(b + 1) * HALF]
+    return jnp.concatenate([first, rest], axis=1)
+
+
+def couple(cols, held, s, b, ops, rank, far, z):
+    at = (s * 2 + b) * far
+    lhs = coupling_rows(held, s, b, ops, rank)
+    starts = [pl.multiple_of(cols[at + f] * rank, rank) for f in range(far)]
+    picked = [
+        jnp.concatenate([x[pl.ds(start, rank), :] for start in starts], axis=0) for x in z
+    ]
     if len(z) == 1:
-        lhs = coup[s, b * ops * rank:(b + 1) * ops * rank, :]
-        return dot(lhs, jnp.concatenate([p[0] for p in picked], axis=0))
-    for o in range(ops):
-        row = (b * ops + o) * rank
-        rhs = jnp.concatenate([p[o] for p in picked], axis=0)
-        res.append(dot(coup[s, row:row + rank, :], rhs))
-    return jnp.concatenate(res, axis=0)
-
-
-def spread_rows(source, target, rank):
-    n = source.shape[0]
-    x = source.reshape(n, rank, LANES)
-    y = pltpu.roll(x, HALF, 2)
-    both = jnp.concatenate([x[:, None], y[:, None]], axis=1)
-    target[...] = both.reshape(n * 2 * rank, LANES).astype(BF16)
-
-
-def first_couple(ops, rank, cols, z1, coup, out, zs):
-    spread_rows(z1[...].astype(F32), zs, rank)
-    for s in range(out.shape[0]):
-        c = [couple(cols, coup, s, b, ops, rank, [zs]) for b in range(2)]
+        return dot(lhs, picked[0])
+    return jnp.concatenate(
+        [dot(lhs[o * rank:(o + 1) * rank], picked[o]) for o in range(ops)], axis=0
+    )
+
+
+def spread_rows(source, rank):
+    count = source.shape[0]
+    turned = pltpu.roll(source, HALF, 2)
+    both = jnp.concatenate([source[:, None], turned[:, None]], axis=1)
+    return both.reshape(count * 2 * rank, LANES).astype(BF16)
+
+
+def group_at(group, m, groups, step):
+    return pl.multiple_of(lax.rem(group[0] + (groups - m), groups) * step, step)
+
+
+def first_couple(ops, rank, far, cols, group, held, *refs):
+    parts, (out, zs) = refs[:-2], refs[-2:]
+    step = SLICES * 2 * rank
+    for m, part in enumerate(parts):
+        at = group_at(group, m, len(parts), step)
+        zs[pl.ds(at, step), :] = spread_rows(part[...].astype(F32), rank)
+    for s in range(SLICES):
+        c = [couple(cols, held, s, b, ops, rank, far, [zs]) for b in range(2)]
         out[s] = halves(c[0], c[1])[0].astype(BF16)
 
 
@@ -223,8 +229,8 @@
             z.append(dot(right[b], v))
         for pair in range(SLICES // 2):
             first, second = halves(chunk(z[0], pair), chunk(z[1], pair))
-            send_all(mout, slice(o * rank, (o + 1) * rank), 2 * pair, first.astype(BF16))
-            send_all(mout, slice(o * rank, (o + 1) * rank), 2 * pair + 1, second.astype(BF16))
+            mout[2 * pair, o * rank:(o + 1) * rank, :] = first.astype(BF16)
+            mout[2 * pair + 1, o * rank:(o + 1) * rank, :] = second.astype(BF16)
         spreads.append(spread)
     zero = jnp.zeros((1, columns), BF16)
     vout[ops * rows:, :] = jnp.concatenate(stats + [zero] * (STATS - len(stats)), axis=0)
@@ -235,37 +241,48 @@
     for pair in range(SLICES // 2):
         part = chunk(stats, pair)
         first, second = halves(part, part)
-        send_all(mout, slice(ops * rank, ops * rank + STATS), 2 * pair, first.astype(BF16))
-        send_all(mout, slice(ops * rank, ops * rank + STATS), 2 * pair + 1, second.astype(BF16))
-
-
-def second_couple(panels, ops, rank, cols, z1, msg, coup, out, zs):
+        mout[2 * pair, ops * rank:ops * rank + STATS, :] = first.astype(BF16)
+        mout[2 * pair + 1, ops * rank:ops * rank + STATS, :] = second.astype(BF16)
+
+
+def second_couple(panels, ops, rank, far, cols, group, held, *refs):
+    out, zs, st = refs[-3:]
+    count = (len(refs) - 3) // 2
+    z1, msgs = refs[:count], refs[count:2 * count]
     body = ops * rank
-    st = msg[:, body:body + STATS, :].astype(F32)
-    shift = [join3(st, o) for o in range(ops)]
-    squares = join3(st, ops)
+    step = SLICES * 2 * rank
+    for m, msg in enumerate(msgs):
+        at = group_at(group, m, count, SLICES)
+        st[pl.ds(at, SLICES)] = msg[:, body:body + STATS, :].astype(F32)
+    every = st[...]
+    squares = join3(every, ops)
     scale_sq = jnp.sum(squares, axis=0, keepdims=True) / panels + EPSILON
     reverse = 1.0 / jnp.sqrt(scale_sq)
     heights, norms = [], []
-    base = z1[...].astype(F32)
     for o in range(ops):
-        total = jnp.sum(shift[o] * squares, axis=0, keepdims=True) / panels
-        height = total / scale_sq
-        delta = shift[o] - height
-        spread = join3(st, ops + 1 + o) + delta * delta * squares
+        shift = join3(every, o)
+        height = jnp.sum(shift * squares, axis=0, keepdims=True) / panels / scale_sq
+        delta = shift - height
+        spread = join3(every, ops + 1 + o) + delta * delta * squares
         norm = jnp.sqrt(jnp.sum(spread, axis=0, keepdims=True) / panels / scale_sq + EPSILON)
         heights.append(height)
         norms.append(norm)
-        factor = reverse / norm
-        z = msg[:, o * rank:(o + 1) * rank, :].astype(F32) + delta[:, None, :] * base
-        spread_rows(z * factor[None], zs.at[o], rank)
+    for m, (base, msg) in enumerate(zip(z1, msgs)):
+        at = group_at(group, m, count, step)
+        mine = msg[:, body:body + STATS, :].astype(F32)
+        base = base[...].astype(F32)
+        for o in range(ops):
+            delta = join3(mine, o) - heights[o]
+            z = msg[:, o * rank:(o + 1) * rank, :].astype(F32) + delta[:, None, :] * base
+            z = z * (reverse / norms[o])[None]
+            zs[o, pl.ds(at, step), :] = spread_rows(z, rank)
     rows = []
     for row in heights + norms + [reverse]:
         rows += split3(row)
     rows += [jnp.zeros_like(rows[0])] * (STATS - len(rows))
     rows = jnp.concatenate(rows, axis=0)
-    for s in range(out.shape[0]):
-        c = [couple(cols, coup, s, b, ops, rank, [zs.at[o] for o in range(ops)]) for b in range(2)]
+    for s in range(SLICES):
+        c = [couple(cols, held, s, b, ops, rank, far, [zs.at[o] for o in range(ops)]) for b in range(2)]
         out[s, 0:body, :] = halves(c[0], c[1])[0].astype(BF16)
         out[s, body:body + STATS, :] = rows
 
@@ -332,28 +349,40 @@
     far = far_cols.shape[1]
     rows, columns = sources.shape
     all_blocks = blocks * n
-    groups = [[g * SLICES + s for s in range(SLICES)] for g in range(n // SLICES)]
+    count = n // SLICES
+    groups = [[g * SLICES + s for s in range(SLICES)] for g in range(count)]
     sds = jax.ShapeDtypeStruct
     body = ops * rank
 
-    def exchange(x, part):
-        return lax.all_to_all(
-            x, "store", 0, 0, axis_index_groups=groups if part else None, tiled=True
-        )
-
-    row0 = (lax.axis_index("store") * blocks).astype(jnp.int32).reshape(1)
+    def exchange(x):
+        return lax.all_to_all(x, "store", 0, 0, axis_index_groups=groups, tiled=True)
+
+    def across(x):
+        parts = [x]
+        for m in range(1, count):
+            pairs = [(i, (i + m * SLICES) % n) for i in range(n)]
+            parts.append(lax.ppermute(x, "store", pairs))
+        return parts
+
+    place = lax.axis_index("store").astype(jnp.int32)
+    row0 = (place * blocks).reshape(1)
+    group = lax.div(place, jnp.int32(SLICES)).reshape(1)
     left = jnp.transpose(basis_left, (0, 2, 1))
     right = jnp.transpose(basis_right, (0, 2, 1))
 
-    z1 = call(coeff_kernel, sds((n, rank, LANES), BF16), [VMEM, VMEM])(sources, right)
-    z1 = exchange(z1, False)
-    low, high = ring(sources)
-
+    shared = rank + (blocks + 1) * body
     held = call(
-        share_kernel, sds((SLICES, blocks * body + STATS, far * rank), BF16), [SMEM, VMEM]
-    )(far_cols, couplings)
-    held = exchange(held, True)
-    cols = held[:, blocks * body, :blocks * far].astype(jnp.int32).reshape(-1)
+        share_kernel, sds((SLICES, shared + STATS, LANES), BF16), [SMEM, VMEM, VMEM, VMEM]
+    )(far_cols, sources, right, couplings)
+    held = exchange(held)
+    cols = held[:, shared, :blocks * far].astype(jnp.int32).reshape(-1)
+    z1, own = call(
+        relay_kernel,
+        [sds((SLICES, rank, LANES), BF16), sds((rows, columns), BF16)],
+        [VMEM, VMEM],
+    )(held, sources)
+    z1 = across(z1)
+    low, high = ring(own)
 
     w = call(
         functools.partial(order_tiles, all_blocks),
@@ -362,33 +391,37 @@
     )(near_cols, near_count, row0, near_tiles)
 
     c1 = call(
-        functools.partial(first_couple, ops, rank),
+        functools.partial(first_couple, ops, rank, far),
         sds((SLICES, body, LANES), BF16),
-        [SMEM, VMEM, VMEM],
+        [SMEM, SMEM] + [VMEM] * (1 + count),
         [pltpu.VMEM((n * blocks * rank, LANES), BF16)],
-    )(cols, z1, held)
-    c1 = exchange(c1, True)
-
+    )(cols, group, held, *z1)
+    c1 = exchange(c1)
+
+    work = 2 * ops * rows * near * size * columns
     v, msg = call(
         image_kernel,
-        [sds((ops * rows + STATS, columns), BF16), sds((n, body + STATS, LANES), BF16)],
+        [sds((ops * rows + STATS, columns), BF16), sds((SLICES, body + STATS, LANES), BF16)],
         [VMEM] * 8,
         [
             pltpu.VMEM((ops, rows, columns), F32),
             pltpu.VMEM((blocks, body, columns), BF16),
         ],
-        flops=2 * ops * rows * near * size * columns,
-    )(w, low, sources, high, self_terms, left, right, c1)
-    msg = exchange(msg, False)
+        flops=work,
+    )(w, low, own, high, self_terms, left, right, c1)
+    msgs = across(exchange(msg))
     vlow, vhigh = ring(v)
 
     c2 = call(
-        functools.partial(second_couple, all_blocks * size, ops, rank),
+        functools.partial(second_couple, all_blocks * size, ops, rank, far),
         sds((SLICES, body + STATS, LANES), BF16),
-        [SMEM, VMEM, VMEM, VMEM],
-        [pltpu.VMEM((ops, n * blocks * rank, LANES), BF16)],
-    )(cols, z1, msg, held)
-    c2 = exchange(c2, True)
+        [SMEM, SMEM] + [VMEM] * (1 + 2 * count),
+        [
+            pltpu.VMEM((ops, n * blocks * rank, LANES), BF16),
+            pltpu.VMEM((n, STATS, LANES), F32),
+        ],
+    )(cols, group, held, *z1, *msgs)
+    c2 = exchange(c2)
 
     images, heights, norms = call(
         final_kernel,
@@ -399,8 +432,8 @@
             pltpu.VMEM((blocks, body, columns), BF16),
             pltpu.VMEM((STATS, columns), F32),
         ],
-        flops=2 * ops * rows * near * size * columns,
-    )(w, low, sources, high, vlow, v, vhigh, self_terms, left, c2)
+        flops=work,
+    )(w, low, own, high, vlow, v, vhigh, self_terms, left, c2)
     return images, heights, norms
 
 

time: 97.3 us -> 99.6 us (1.024)
  starting transfers between devices: 24.6 us -> 11.8 us
  blocking collectives: 37 us -> 46.9 us
  waiting for transfers between devices: 13.4 us -> 19.2 us
    ppermute x0 -> x2, waiting for transfers between devices: none -> 16.7 us  [across(): parts.append(lax.ppermute(x, 'store', pairs))]
    all_to_all x3 -> x1, starting transfers between devices: 19.4 us -> 4.16 us  [exchange(): lax.all_to_all(x, 'store', 0, 0, axis_index_groups=groups, tiled=True)]
    all_to_all x3 -> x1, waiting for transfers between devices: 13.4 us -> 2.51 us  [exchange(): lax.all_to_all(x, 'store', 0, 0, axis_index_groups=groups, tiled=True)]
    all_to_all x2 -> x3, blocking collectives: 37 us -> 46.9 us  [exchange(): lax.all_to_all(x, 'store', 0, 0, axis_index_groups=groups, tiled=True)]
    ppermute x0 -> x2, starting transfers between devices: none -> 2.64 us  [across(): parts.append(lax.ppermute(x, 'store', pairs))]
    unnamed x24 -> x20, local copies, waits for them, and re-layouts: 5.22 us -> 5.15 us
  transfers between devices with their start and end apart: 7 -> 7, of which waited for: 3 -> 3; matrix products, arithmetic and copies ran while one was open for 0% -> 0% of each run, Pallas kernels for 5% -> 4%
where the time goes in v4:
time: 99.6 us; the launch traced here: 99 us
  blocking collectives  46.9 us (47%)
  waiting for transfers between devices  19.2 us (19%)
  Pallas kernels  15.1 us (15%)
  starting transfers between devices  11.8 us (12%)
  local copies, waits for them, and re-layouts  5.23 us (5%)
    all_to_all x3, blocking collectives, exchange(): lax.all_to_all(x, 'store', 0, 0, axis_index_groups=groups, tiled=True)  46.9 us
    ppermute x2, waiting for transfers between devices, across(): parts.append(lax.ppermute(x, 'store', pairs))  16.7 us
    unnamed x20, local copies, waits for them, and re-layouts  5.15 us
    pallas_call x1, Pallas kernels, shards(): call(final_kernel, [sds((ops, rows, columns), F32), sds((ops, columns), F...  5.09 us
    ppermute x2, starting transfers between devices, ring(): lax.ppermute(block, 'store', backward)  5 us
    all_to_all x1, starting transfers between devices, exchange(): lax.all_to_all(x, 'store', 0, 0, axis_index_groups=groups, tiled=True)  4.16 us
    pallas_call x1, Pallas kernels, shards(): call(image_kernel, [sds((ops * rows + STATS, columns), BF16), sds((SLICES...  4.08 us
    ppermute x2, starting transfers between devices, across(): parts.append(lax.ppermute(x, 'store', pairs))  2.64 us
  transfers between devices with their start and end apart: 7, of which 3 were waited for; matrix products, arithmetic and copies ran while one was open for 0% of the time, Pallas kernels for 4%

profile of v4, /device:TPU:0, one launch (start us, length us, event | category | flops | bytes accessed | tf_op | source)
XLA Modules:
  0.0 99.0 jit_solution(325838524864839997)
XLA Ops:
  0.6 0.0 copy-start.1
  0.6 1.0 %copy-done.1 = bf16[512,512]{1,0:T(8,128)(2,1)S(1)} copy-done((bf16[512,512]{1,0:T(8,128)(2,1)S(1)}, bf16[512,512]{1,0:T(8,128)(2,1)}, u32[]{:S(2)}) %copy-start.1) | copy-done | bytes 524312
  1.7 0.0 copy-start.2
  1.7 0.9 copy-done.2
  2.6 0.0 copy-start.4
  2.6 0.8 copy-done.4
  3.4 0.0 copy-start.8
  3.4 0.7 copy-done.8
  4.0 0.0 copy-start.7
  4.0 0.0 copy-start.9
  4.0 0.8 shard_map.113
  4.9 13.7 %all_to_all.20.first.held = bf16[8,240,128]{2,1,0:T(8,128)(2,1)S(1)} all-to-all(bf16[8,240,128]{2,1,0:T(8,128)(2,1)S(1)} %shard_map.113), channel_id=1, replica_groups={{0,1,2,3,4,5,6,7},{8,9,10,11,12,13,14,15},{16,17,18,19,20,21,22,23},{24..., dimensions={0} | all-to-all | bytes 983040 | tf_op jit(solution)/shard_map/all_to_all | solution.py:358
  18.6 0.8 shard_map.114
  19.4 2.8 %collective-permute-start.1 = (bf16[512,512]{1,0:T(8,128)(2,1)}, bf16[512,512]{1,0:T(8,128)(2,1)}, u32[]{:S(2)}, u32[]{:S(2)}) collective-permute-start(bf16[512,512]{1,0:T(8,128)(2,1)} %get-tuple-element.7.own.uown), channel_id=1, source_target_pairs={{1,0},{2,1},{3,2},{4,3},{5,4},{6,5},{7,6},{8,7},{9,8},{10,9},{11,1... | collective-permute-start | bytes 1572872 | tf_op jit(solution)/shard_map/ppermute | solution.py:332
  22.2 0.0 collective-permute-start
  22.2 0.3 collective-permute-start.2
  22.6 0.1 reshape.18.cols
  22.6 8.9 %collective-permute-done.2.refs_1_ = bf16[8,32,128]{2,1,0:T(8,128)(2,1)S(1)} collective-permute-done((bf16[8,32,128]{2,1,0:T(8,128)(2,1)S(1)}, bf16[8,32,128]{2,1,0:T(8,128)(2,1)S(1)}, u32[]{:S(2)}, u32[]{:S(2)}) %collective-permute-start.2) | collective-permute-done | bytes 65568 | tf_op jit(solution)/shard_map/ppermute | solution.py:364
  31.5 1.8 %shard_map.115 = bf16[8,64,128]{2,1,0:T(8,128)(2,1)} custom-call(s32[96]{0:T(128)S(1)} %reshape.18.cols, s32[1]{0:T(128)} %bitcast.3.group, bf16[8,240,128]{2,1,0:T(8,128)(2,1)S(1)} %all_to_all.20.first.held, bf16[8,32,128]{2,1,0:T(8,128)(2,1)S(1)} %get-tuple-element.8.refs_0_, bf16[8,32,128]{2,1,0:T(8,128)(2,1)S(1)} %collective-permute-done.2.refs_1_), custom_call_target="tpu_custom_call" | custom-call | tf_op jit(solution)/shard_map/pallas_call | solution.py:393
  33.3 4.2 %all-to-all-start.1 = ((bf16[8,64,128]{2,1,0:T(8,128)(2,1)}), bf16[8,64,128]{2,1,0:T(8,128)(2,1)S(1)}, u32[]{:S(2)}, u32[]{:S(2)}) async-start(bf16[8,64,128]{2,1,0:T(8,128)(2,1)} %shard_map.115), calls=%async_computation.1 | async-start | bytes 262144 | tf_op jit(solution)/shard_map/all_to_all | solution.py:358
  37.5 0.0 copy-done.7
  37.5 0.0 copy-done.9
  37.5 0.0 copy-start
  37.5 1.7 %copy-done = bf16[2,2,5,256,256]{4,3,2,1,0:T(8,128)(2,1)S(1)} copy-done((bf16[2,2,5,256,256]{4,3,2,1,0:T(8,128)(2,1)S(1)}, bf16[2,2,5,256,256]{4,3,2,1,0:T(8,128)(2,1)}, u32[]{:S(2)}) %copy-start) | copy-done | bytes 2621464
  39.2 0.0 copy-start.3
  39.2 0.0 copy-start.5
  39.2 0.0 copy-start.6
  39.2 0.9 shard_map.112.w
  40.1 2.5 %all-to-all-done.1.cmsg = bf16[8,64,128]{2,1,0:T(8,128)(2,1)S(1)} async-done(((bf16[8,64,128]{2,1,0:T(8,128)(2,1)}), bf16[8,64,128]{2,1,0:T(8,128)(2,1)S(1)}, u32[]{:S(2)}, u32[]{:S(2)}) %all-to-all-start.1) | async-done | bytes 131104 | tf_op jit(solution)/shard_map/all_to_all | solution.py:358
  42.7 0.0 collective-permute-done.1.high.uhigh
  42.7 0.0 collective-permute-done.low.ulow
  42.7 0.0 copy-done.3
  42.7 0.0 copy-done.5
  42.7 0.0 copy-done.6
  42.7 4.1 %shard_map.116 = (bf16[1040,512]{1,0:T(8,128)(2,1)S(1)}, bf16[8,80,128]{2,1,0:T(8,128)(2,1)S(1)}) custom-call(bf16[2,512,1280]{2,1,0:T(8,128)(2,1)S(1)} %shard_map.112.w, bf16[512,512]{1,0:T(8,128)(2,1)} %collective-permute-done.low.ulow, bf16[512,512]{1,0:T(8,128)(2,1)} %get-tuple-element.7.own.uown, bf16[512,512]{1,0:T(8,128)(2,1)} %collective-permute-done.1.high.uhigh, ...), custom_call_target="tpu_custom_call" | custom-call | flops 1342177280 | tf_op jit(solution)/shard_map/pallas_call | solution.py:402
  46.8 2.2 %collective-permute-start.4 = (bf16[1040,512]{1,0:T(8,128)(2,1)S(1)}, bf16[1040,512]{1,0:T(8,128)(2,1)S(1)}, u32[]{:S(2)}, u32[]{:S(2)}) collective-permute-start(bf16[1040,512]{1,0:T(8,128)(2,1)S(1)} %get-tuple-element.9.vown), channel_id=1, source_target_pairs={{1,0},{2,1},{3,2},{4,3},{5,4},{6,5},{7,6},{8,7},{9,8},{10,9},{11,1... | collective-permute-start | bytes 3194888 | tf_op jit(solution)/shard_map/ppermute | solution.py:332
  49.0 0.0 collective-permute-start.3
  49.0 25.1 %all_to_all.21.refs_2_ = bf16[8,80,128]{2,1,0:T(8,128)(2,1)S(1)} all-to-all(bf16[8,80,128]{2,1,0:T(8,128)(2,1)S(1)} %get-tuple-element.10), channel_id=1, replica_groups={{0,1,2,3,4,5,6,7},{8,9,10,11,12,13,14,15},{16,17,18,19,20,21,22,23},{24..., dimensions={0} | all-to-all | bytes 327680 | tf_op jit(solution)/shard_map/all_to_all | solution.py:358
  74.2 2.3 %collective-permute-start.5 = (bf16[8,80,128]{2,1,0:T(8,128)(2,1)S(1)}, bf16[8,80,128]{2,1,0:T(8,128)(2,1)S(1)}, u32[]{:S(2)}, u32[]{:S(2)}) collective-permute-start(bf16[8,80,128]{2,1,0:T(8,128)(2,1)S(1)} %all_to_all.21.refs_2_), channel_id=1, source_target_pairs={{0,8},{1,9},{2,10},{3,11},{4,12},{5,13},{6,14},{7,15},{8,0},{9,1},... | collective-permute-start | bytes 491528 | tf_op jit(solution)/shard_map/ppermute | solution.py:364
  76.5 7.8 %collective-permute-done.5.refs_3_ = bf16[8,80,128]{2,1,0:T(8,128)(2,1)S(1)} collective-permute-done((bf16[8,80,128]{2,1,0:T(8,128)(2,1)S(1)}, bf16[8,80,128]{2,1,0:T(8,128)(2,1)S(1)}, u32[]{:S(2)}, u32[]{:S(2)}) %collective-permute-start.5) | collective-permute-done | bytes 163872 | tf_op jit(solution)/shard_map/ppermute | solution.py:364
  84.3 1.6 %shard_map.117 = bf16[8,80,128]{2,1,0:T(8,128)(2,1)S(1)} custom-call(s32[96]{0:T(128)S(1)} %reshape.18.cols, s32[1]{0:T(128)} %bitcast.3.group, bf16[8,240,128]{2,1,0:T(8,128)(2,1)S(1)} %all_to_all.20.first.held, bf16[8,32,128]{2,1,0:T(8,128)(2,1)S(1)} %get-tuple-element.8.refs_0_, bf16[8,32,128]{2,1,0:T(8,128)(2,1)S(1)} %collective-permute-done.2.refs_1_, ...), custom_call_target="tpu_custom_call" | custom-call | tf_op jit(solution)/shard_map/pallas_call | solution.py:415
  85.9 8.0 %all_to_all.22.cmsg = bf16[8,80,128]{2,1,0:T(8,128)(2,1)S(1)} all-to-all(bf16[8,80,128]{2,1,0:T(8,128)(2,1)S(1)} %shard_map.117), channel_id=1, replica_groups={{0,1,2,3,4,5,6,7},{8,9,10,11,12,13,14,15},{16,17,18,19,20,21,22,23},{24..., dimensions={0} | all-to-all | bytes 327680 | tf_op jit(solution)/shard_map/all_to_all | solution.py:358
  93.9 0.0 collective-permute-done.4.vhigh
  93.9 0.0 collective-permute-done.3.vlow
  93.9 5.1 %shard_map.118 = (f32[2,512,512]{2,1,0:T(8,128)}, f32[2,512]{1,0:T(2,128)}, f32[2,512]{1,0:T(2,128)}) custom-call(bf16[2,512,1280]{2,1,0:T(8,128)(2,1)S(1)} %shard_map.112.w, bf16[512,512]{1,0:T(8,128)(2,1)} %collective-permute-done.low.ulow, bf16[512,512]{1,0:T(8,128)(2,1)} %get-tuple-element.7.own.uown, ...), custom_call_target="tpu_custom_call" | custom-call | flops 1342177280 | tf_op jit(solution)/shard_map/pallas_call | solution.py:426
  (1 shorter events, 0.0 us)
Async XLA Ops:
  0.6 1.0 %copy-start.1 = (bf16[512,512]{1,0:T(8,128)(2,1)S(1)}, bf16[512,512]{1,0:T(8,128)(2,1)}, u32[]{:S(2)}) copy-start(bf16[512,512]{1,0:T(8,128)(2,1)} %u.3) | copy-start | bytes 1572868
  1.7 0.9 copy-start.2
  2.6 0.8 copy-start.4
  3.4 0.7 copy-start.8
  4.0 33.4 %copy-start.7 = (s32[2,5]{1,0:T(2,128)S(1)}, s32[2,5]{1,0:T(2,128)}, u32[]{:S(2)}) copy-start(s32[2,5]{1,0:T(2,128)} %cols.1) | copy-start | bytes 124
  4.0 33.4 %copy-start.9 = (s32[2]{0:T(128)S(1)}, s32[2]{0:T(128)}, u32[]{:S(2)}) copy-start(s32[2]{0:T(128)} %count.1) | copy-start | bytes 28
  19.4 23.2 %collective-permute-start.1 = (bf16[512,512]{1,0:T(8,128)(2,1)}, bf16[512,512]{1,0:T(8,128)(2,1)}, u32[]{:S(2)}, u32[]{:S(2)}) collective-permute-start(bf16[512,512]{1,0:T(8,128)(2,1)} %get-tuple-element.7.own.uown), channel_id=1, source_target_pairs={{1,0},{2,1},{3,2},{4,3},{5,4},{6,5},{7,6},{8,7},{9,8},{10,9},{11,1... | collective-permute-start | bytes 1572872 | tf_op jit(solution)/shard_map/ppermute | solution.py:332
  22.2 20.5 %collective-permute-start = (bf16[512,512]{1,0:T(8,128)(2,1)}, bf16[512,512]{1,0:T(8,128)(2,1)}, u32[]{:S(2)}, u32[]{:S(2)}) collective-permute-start(bf16[512,512]{1,0:T(8,128)(2,1)} %get-tuple-element.7.own.uown), channel_id=1, source_target_pairs={{0,1},{1,2},{2,3},{3,4},{4,5},{5,6},{6,7},{7,8},{8,9},{9,10},{10,1... | collective-permute-start | bytes 1572872 | tf_op jit(solution)/shard_map/ppermute | solution.py:332
  22.2 9.3 %collective-permute-start.2 = (bf16[8,32,128]{2,1,0:T(8,128)(2,1)S(1)}, bf16[8,32,128]{2,1,0:T(8,128)(2,1)S(1)}, u32[]{:S(2)}, u32[]{:S(2)}) collective-permute-start(bf16[8,32,128]{2,1,0:T(8,128)(2,1)S(1)} %get-tuple-element.8.refs_0_), channel_id=1, source_target_pairs={{0,8},{1,9},{2,10},{3,11},{4,12},{5,13},{6,14},{7,15},{8,0},{9,1},... | collective-permute-start | bytes 196616 | tf_op jit(solution)/shard_map/ppermute | solution.py:364
  33.3 9.3 %all-to-all-start.1 = ((bf16[8,64,128]{2,1,0:T(8,128)(2,1)}), bf16[8,64,128]{2,1,0:T(8,128)(2,1)S(1)}, u32[]{:S(2)}, u32[]{:S(2)}) async-start(bf16[8,64,128]{2,1,0:T(8,128)(2,1)} %shard_map.115), calls=%async_computation.1 | async-start | bytes 262144 | tf_op jit(solution)/shard_map/all_to_all | solution.py:358
  37.5 1.7 %copy-start = (bf16[2,2,5,256,256]{4,3,2,1,0:T(8,128)(2,1)S(1)}, bf16[2,2,5,256,256]{4,3,2,1,0:T(8,128)(2,1)}, u32[]{:S(2)}) copy-start(bf16[2,2,5,256,256]{4,3,2,1,0:T(8,128)(2,1)} %tiles.1) | copy-start | bytes 7864324
  39.2 3.4 %copy-start.3 = (bf16[2,256,32]{1,2,0:T(8,128)(2,1)S(1)}, bf16[2,256,32]{1,2,0:T(8,128)(2,1)}, u32[]{:S(2)}) copy-start(bf16[2,256,32]{1,2,0:T(8,128)(2,1)} %param.15) | copy-start | bytes 98308
  39.2 3.4 %copy-start.5 = (bf16[2,256,32]{1,2,0:T(8,128)(2,1)S(1)}, bf16[2,256,32]{1,2,0:T(8,128)(2,1)}, u32[]{:S(2)}) copy-start(bf16[2,256,32]{1,2,0:T(8,128)(2,1)} %param.16) | copy-start | bytes 98308
  39.2 3.4 %copy-start.6 = (f32[2,512]{1,0:T(2,128)S(1)}, f32[2,512]{1,0:T(2,128)}, u32[]{:S(2)}) copy-start(f32[2,512]{1,0:T(2,128)} %diag.3) | copy-start | bytes 12292
  46.8 47.2 %collective-permute-start.4 = (bf16[1040,512]{1,0:T(8,128)(2,1)S(1)}, bf16[1040,512]{1,0:T(8,128)(2,1)S(1)}, u32[]{:S(2)}, u32[]{:S(2)}) collective-permute-start(bf16[1040,512]{1,0:T(8,128)(2,1)S(1)} %get-tuple-element.9.vown), channel_id=1, source_target_pairs={{1,0},{2,1},{3,2},{4,3},{5,4},{6,5},{7,6},{8,7},{9,8},{10,9},{11,1... | collective-permute-start | bytes 3194888 | tf_op jit(solution)/shard_map/ppermute | solution.py:332
  49.0 44.9 %collective-permute-start.3 = (bf16[1040,512]{1,0:T(8,128)(2,1)S(1)}, bf16[1040,512]{1,0:T(8,128)(2,1)S(1)}, u32[]{:S(2)}, u32[]{:S(2)}) collective-permute-start(bf16[1040,512]{1,0:T(8,128)(2,1)S(1)} %get-tuple-element.9.vown), channel_id=1, source_target_pairs={{0,1},{1,2},{2,3},{3,4},{4,5},{5,6},{6,7},{7,8},{8,9},{9,10},{10,1... | collective-permute-start | bytes 3194888 | tf_op jit(solution)/shard_map/ppermute | solution.py:332
  74.2 10.1 %collective-permute-start.5 = (bf16[8,80,128]{2,1,0:T(8,128)(2,1)S(1)}, bf16[8,80,128]{2,1,0:T(8,128)(2,1)S(1)}, u32[]{:S(2)}, u32[]{:S(2)}) collective-permute-start(bf16[8,80,128]{2,1,0:T(8,128)(2,1)S(1)} %all_to_all.21.refs_2_), channel_id=1, source_target_pairs={{0,8},{1,9},{2,10},{3,11},{4,12},{5,13},{6,14},{7,15},{8,0},{9,1},... | collective-permute-start | bytes 491528 | tf_op jit(solution)/shard_map/ppermute | solution.py:364

commit v5 on v4

--- a/solution.py
+++ b/solution.py
@@ -13,14 +13,16 @@
 HALF = 64
 SLICES = 8
 STATS = 16
+HBM_RATE = 3690000
 F32 = jnp.float32
 BF16 = jnp.bfloat16
 
 VMEM = pl.BlockSpec(memory_space=pltpu.VMEM)
 SMEM = pl.BlockSpec(memory_space=pltpu.SMEM)
-
-
-def call(body, out_shape, in_specs, scratch=(), flops=0, nbytes=0):
+HBM = pl.BlockSpec(memory_space=pltpu.HBM)
+
+
+def call(body, out_shape, in_specs, scratch=(), micros=1.0):
     many = isinstance(out_shape, (list, tuple))
     return pl.pallas_call(
         body,
@@ -29,7 +31,9 @@
         out_specs=[VMEM] * len(out_shape) if many else VMEM,
         scratch_shapes=list(scratch),
         compiler_params=pltpu.CompilerParams(vmem_limit_bytes=20 * 1024 * 1024),
-        cost_estimate=pl.CostEstimate(flops=flops, bytes_accessed=nbytes, transcendentals=0),
+        cost_estimate=pl.CostEstimate(
+            flops=0, bytes_accessed=int(micros * HBM_RATE), transcendentals=0
+        ),
     )
 
 
@@ -79,7 +83,15 @@
                 )
 
 
-def share_kernel(far_cols, u, right, coup, out):
+def share_kernel(far_cols, u_in, right_in, coup_in, out, u, right, coup, sems):
+    copies = [
+        pltpu.make_async_copy(source, target, sems.at[i])
+        for i, (source, target) in enumerate(((u_in, u), (right_in, right), (coup_in, coup)))
+    ]
+    for copy in copies:
+        copy.start()
+    for copy in copies:
+        copy.wait()
     ops, blocks, far, rank, _ = coup.shape
     size = right.shape[2]
     z = [dot(right[b], u[b * size:(b + 1) * size, :]) for b in range(blocks)]
@@ -107,9 +119,12 @@
         out[s, rank:, :] = whole
 
 
-def relay_kernel(first, u, z, uout):
+def relay_kernel(first, z):
     z[...] = first[:, 0:z.shape[1], :]
-    uout[...] = u[...]
+
+
+def copy_kernel(source, target):
+    target[...] = source[...]
 
 
 def coupling_rows(held, s, b, ops, rank):
@@ -372,22 +387,27 @@
 
     shared = rank + (blocks + 1) * body
     held = call(
-        share_kernel, sds((SLICES, shared + STATS, LANES), BF16), [SMEM, VMEM, VMEM, VMEM]
+        share_kernel,
+        sds((SLICES, shared + STATS, LANES), BF16),
+        [SMEM, HBM, HBM, HBM],
+        [
+            pltpu.VMEM(sources.shape, BF16),
+            pltpu.VMEM(right.shape, BF16),
+            pltpu.VMEM(couplings.shape, BF16),
+            pltpu.SemaphoreType.DMA((3,)),
+        ],
     )(far_cols, sources, right, couplings)
     held = exchange(held)
     cols = held[:, shared, :blocks * far].astype(jnp.int32).reshape(-1)
-    z1, own = call(
-        relay_kernel,
-        [sds((SLICES, rank, LANES), BF16), sds((rows, columns), BF16)],
-        [VMEM, VMEM],
-    )(held, sources)
-    z1 = across(z1)
+    z1 = across(call(relay_kernel, sds((SLICES, rank, LANES), BF16), [VMEM])(held))
+    own = sources
     low, high = ring(own)
 
     w = call(
         functools.partial(order_tiles, all_blocks),
         sds((blocks, ops * size, near * size), BF16),
         [SMEM, SMEM, SMEM, VMEM],
+        micros=2.5,
     )(near_cols, near_count, row0, near_tiles)
 
     c1 = call(
@@ -398,7 +418,6 @@
     )(cols, group, held, *z1)
     c1 = exchange(c1)
 
-    work = 2 * ops * rows * near * size * columns
     v, msg = call(
         image_kernel,
         [sds((ops * rows + STATS, columns), BF16), sds((SLICES, body + STATS, LANES), BF16)],
@@ -407,10 +426,11 @@
             pltpu.VMEM((ops, rows, columns), F32),
             pltpu.VMEM((blocks, body, columns), BF16),
         ],
-        flops=work,
+        micros=4.0,
     )(w, low, own, high, self_terms, left, right, c1)
     msgs = across(exchange(msg))
-    vlow, vhigh = ring(v)
+    bulk = call(copy_kernel, sds(v.shape, BF16), [VMEM], micros=4.0)(v)
+    vlow, vhigh = ring(bulk)
 
     c2 = call(
         functools.partial(second_couple, all_blocks * size, ops, rank, far),
@@ -432,7 +452,7 @@
             pltpu.VMEM((blocks, body, columns), BF16),
             pltpu.VMEM((STATS, columns), F32),
         ],
-        flops=work,
+        micros=4.0,
     )(w, low, own, high, vlow, v, vhigh, self_terms, left, c2)
     return images, heights, norms
 

time: 99.6 us -> 97.8 us (0.982)
  starting transfers between devices: 11.8 us -> 26.2 us
  blocking collectives: 46.9 us -> 33.1 us
  waiting for transfers between devices: 19.2 us -> 16.6 us
  Pallas kernels: 15.1 us -> 16.2 us
  local copies, waits for them, and re-layouts: 5.23 us -> 4.19 us
    all_to_all x3 -> x2, blocking collectives: 46.9 us -> 33.1 us  [exchange(): lax.all_to_all(x, 'store', 0, 0, axis_index_groups=groups, tiled=True)]
    ppermute x2, starting transfers between devices: 2.64 us -> 10.6 us  [across(): parts.append(lax.ppermute(x, 'store', pairs))]
    ppermute x2, waiting for transfers between devices: 16.7 us -> 10.4 us  [across(): parts.append(lax.ppermute(x, 'store', pairs))]
    all_to_all x1 -> x2, starting transfers between devices: 4.16 us -> 8.64 us  [exchange(): lax.all_to_all(x, 'store', 0, 0, axis_index_groups=groups, tiled=True)]
    all_to_all x1 -> x2, waiting for transfers between devices: 2.51 us -> 6.2 us  [exchange(): lax.all_to_all(x, 'store', 0, 0, axis_index_groups=groups, tiled=True)]
    ppermute x2, starting transfers between devices: 5 us -> 7 us  [ring(): lax.ppermute(block, 'store', backward)]
    pallas_call x2 -> x3, Pallas kernels: 1.65 us -> 2.75 us  [the longest x1 2.68 us: shards(): call(share_kernel, sds((SLICES, shared + STATS, LANES), BF16), [SMEM, HBM...]
    unnamed x20 -> x18, local copies, waits for them, and re-layouts: 5.15 us -> 4.11 us
  transfers between devices with their start and end apart: 7 -> 8, of which waited for: 3 -> 4; matrix products, arithmetic and copies ran while one was open for 0% -> 0% of each run, Pallas kernels for 4% -> 4%
where the time goes in v5:
time: 97.8 us; the launch traced here: 97.2 us
  blocking collectives  33.1 us (34%)
  starting transfers between devices  26.2 us (27%)
  waiting for transfers between devices  16.6 us (17%)
  Pallas kernels  16.2 us (17%)
  local copies, waits for them, and re-layouts  4.19 us (4%)
    all_to_all x2, blocking collectives, exchange(): lax.all_to_all(x, 'store', 0, 0, axis_index_groups=groups, tiled=True)  33.1 us
    ppermute x2, starting transfers between devices, across(): parts.append(lax.ppermute(x, 'store', pairs))  10.6 us
    ppermute x2, waiting for transfers between devices, across(): parts.append(lax.ppermute(x, 'store', pairs))  10.4 us
    all_to_all x2, starting transfers between devices, exchange(): lax.all_to_all(x, 'store', 0, 0, axis_index_groups=groups, tiled=True)  8.64 us
    ppermute x2, starting transfers between devices, ring(): lax.ppermute(block, 'store', backward)  7 us
    all_to_all x2, waiting for transfers between devices, exchange(): lax.all_to_all(x, 'store', 0, 0, axis_index_groups=groups, tiled=True)  6.2 us
    pallas_call x1, Pallas kernels, shards(): call(final_kernel, [sds((ops, rows, columns), F32), sds((ops, columns), F...  5.09 us
    unnamed x18, local copies, waits for them, and re-layouts  4.11 us
  transfers between devices with their start and end apart: 8, of which 4 were waited for; matrix products, arithmetic and copies ran while one was open for 0% of the time, Pallas kernels for 4%

profile of v5, /device:TPU:0, one launch (start us, length us, event | category | flops | bytes accessed | tf_op | source)
XLA Modules:
  0.0 97.2 jit_solution(2643831706056355344)
XLA Ops:
  0.6 0.0 copy-start.1
  0.6 0.9 copy-done.1
  1.6 0.0 copy-start.3
  1.6 0.8 copy-done.3
  2.3 0.0 copy-start.7
  2.3 0.7 copy-done.7
  3.0 2.7 %shard_map.113 = bf16[8,240,128]{2,1,0:T(8,128)(2,1)} custom-call(s32[2,6]{1,0:T(2,128)S(1)} %copy-done.7, bf16[512,512]{1,0:T(8,128)(2,1)} %uown.1, bf16[2,32,256]{2,1,0:T(8,128)(2,1)S(1)} %bitcast.6, bf16[2,2,6,32,32]{4,3,2,1,0:T(8,128)(2,1)S(1)} %copy-done.1), custom_call_target="tpu_custom_call" | custom-call | bytes 3690000 | tf_op jit(solution)/shard_map/pallas_call | solution.py:389
  5.7 0.0 copy-start.6
  5.7 0.0 copy-start.8
  5.7 5.3 %all-to-all-start = ((bf16[8,240,128]{2,1,0:T(8,128)(2,1)}), bf16[8,240,128]{2,1,0:T(8,128)(2,1)S(1)}, u32[]{:S(2)}, u32[]{:S(2)}) async-start(bf16[8,240,128]{2,1,0:T(8,128)(2,1)} %shard_map.113), calls=%async_computation | async-start | bytes 983040 | tf_op jit(solution)/shard_map/all_to_all | solution.py:373
  11.0 4.7 %collective-permute-start.1 = (bf16[512,512]{1,0:T(8,128)(2,1)}, bf16[512,512]{1,0:T(8,128)(2,1)}, u32[]{:S(2)}, u32[]{:S(2)}) collective-permute-start(bf16[512,512]{1,0:T(8,128)(2,1)} %uown.1), channel_id=1, source_target_pairs={{1,0},{2,1},{3,2},{4,3},{5,4},{6,5},{7,6},{8,7},{9,8},{10,9},{11,1... | collective-permute-start | bytes 1572872 | tf_op jit(solution)/shard_map/ppermute | solution.py:347
  15.7 0.0 collective-permute-start
  15.7 3.8 %all-to-all-done.first.held = bf16[8,240,128]{2,1,0:T(8,128)(2,1)S(1)} async-done(((bf16[8,240,128]{2,1,0:T(8,128)(2,1)}), bf16[8,240,128]{2,1,0:T(8,128)(2,1)S(1)}, u32[]{:S(2)}, u32[]{:S(2)}) %all-to-all-start) | async-done | bytes 491552 | tf_op jit(solution)/shard_map/all_to_all | solution.py:373
  19.5 8.2 %collective-permute-start.2 = (bf16[8,32,128]{2,1,0:T(8,128)(2,1)S(1)}, bf16[8,32,128]{2,1,0:T(8,128)(2,1)S(1)}, u32[]{:S(2)}, u32[]{:S(2)}) collective-permute-start(bf16[8,32,128]{2,1,0:T(8,128)(2,1)S(1)} %shard_map.114.refs_0_), channel_id=1, source_target_pairs={{0,8},{1,9},{2,10},{3,11},{4,12},{5,13},{6,14},{7,15},{8,0},{9,1},... | collective-permute-start | bytes 196616 | tf_op jit(solution)/shard_map/ppermute | solution.py:379
  27.7 0.1 reshape.18.cols
  27.8 2.7 %collective-permute-done.2.refs_1_ = bf16[8,32,128]{2,1,0:T(8,128)(2,1)S(1)} collective-permute-done((bf16[8,32,128]{2,1,0:T(8,128)(2,1)S(1)}, bf16[8,32,128]{2,1,0:T(8,128)(2,1)S(1)}, u32[]{:S(2)}, u32[]{:S(2)}) %collective-permute-start.2) | collective-permute-done | bytes 65568 | tf_op jit(solution)/shard_map/ppermute | solution.py:379
  30.5 1.8 %shard_map.115 = bf16[8,64,128]{2,1,0:T(8,128)(2,1)} custom-call(s32[96]{0:T(128)S(1)} %reshape.18.cols, s32[1]{0:T(128)} %bitcast.3.group, bf16[8,240,128]{2,1,0:T(8,128)(2,1)S(1)} %all-to-all-done.first.held, bf16[8,32,128]{2,1,0:T(8,128)(2,1)S(1)} %shard_map.114.refs_0_, bf16[8,32,128]{2,1,0:T(8,128)(2,1)S(1)} %collective-permute-done.2.refs_1_), custom_call_target="tpu_custom_call" | custom-call | bytes 3690000 | tf_op jit(solution)/shard_map/pallas_call | solution.py:413
  32.3 3.4 %all-to-all-start.1 = ((bf16[8,64,128]{2,1,0:T(8,128)(2,1)}), bf16[8,64,128]{2,1,0:T(8,128)(2,1)S(1)}, u32[]{:S(2)}, u32[]{:S(2)}) async-start(bf16[8,64,128]{2,1,0:T(8,128)(2,1)} %shard_map.115), calls=%async_computation.1 | async-start | bytes 262144 | tf_op jit(solution)/shard_map/all_to_all | solution.py:373
  35.6 0.0 copy-done.6
  35.6 0.0 copy-done.8
  35.7 0.0 copy-start
  35.7 1.7 %copy-done = bf16[2,2,5,256,256]{4,3,2,1,0:T(8,128)(2,1)S(1)} copy-done((bf16[2,2,5,256,256]{4,3,2,1,0:T(8,128)(2,1)S(1)}, bf16[2,2,5,256,256]{4,3,2,1,0:T(8,128)(2,1)}, u32[]{:S(2)}) %copy-start) | copy-done | bytes 2621464
  37.4 0.0 copy-start.2
  37.4 0.0 copy-start.4
  37.4 0.0 copy-start.5
  37.4 0.9 shard_map.112.w
  38.3 0.0 collective-permute-done.1.high.uhigh
  38.3 0.0 collective-permute-done.low.ulow
  38.3 2.4 %all-to-all-done.1.cmsg = bf16[8,64,128]{2,1,0:T(8,128)(2,1)S(1)} async-done(((bf16[8,64,128]{2,1,0:T(8,128)(2,1)}), bf16[8,64,128]{2,1,0:T(8,128)(2,1)S(1)}, u32[]{:S(2)}, u32[]{:S(2)}) %all-to-all-start.1) | async-done | bytes 131104 | tf_op jit(solution)/shard_map/all_to_all | solution.py:373
  40.7 0.0 copy-done.2
  40.7 0.0 copy-done.4
  40.8 0.0 copy-done.5
  40.8 4.1 %shard_map.116 = (bf16[1040,512]{1,0:T(8,128)(2,1)S(1)}, bf16[8,80,128]{2,1,0:T(8,128)(2,1)S(1)}) custom-call(bf16[2,512,1280]{2,1,0:T(8,128)(2,1)S(1)} %shard_map.112.w, bf16[512,512]{1,0:T(8,128)(2,1)} %collective-permute-done.low.ulow, bf16[512,512]{1,0:T(8,128)(2,1)} %uown.1, bf16[512,512]{1,0:T(8,128)(2,1)} %collective-permute-done.1.high.uhigh, ...), custom_call_target="tpu_custom_call" | custom-call | bytes 14760000 | tf_op jit(solution)/shard_map/pallas_call | solution.py:421
  44.8 0.1 shard_map.117
  44.9 2.3 %collective-permute-start.4 = (bf16[1040,512]{1,0:T(8,128)(2,1)S(1)}, bf16[1040,512]{1,0:T(8,128)(2,1)S(1)}, u32[]{:S(2)}, u32[]{:S(2)}) collective-permute-start(bf16[1040,512]{1,0:T(8,128)(2,1)S(1)} %shard_map.117), channel_id=1, source_target_pairs={{1,0},{2,1},{3,2},{4,3},{5,4},{6,5},{7,6},{8,7},{9,8},{10,9},{11,1... | collective-permute-start | bytes 3194888 | tf_op jit(solution)/shard_map/ppermute | solution.py:347
  47.2 0.0 collective-permute-start.3
  47.2 25.1 %all_to_all.20.refs_2_ = bf16[8,80,128]{2,1,0:T(8,128)(2,1)S(1)} all-to-all(bf16[8,80,128]{2,1,0:T(8,128)(2,1)S(1)} %get-tuple-element.6), channel_id=1, replica_groups={{0,1,2,3,4,5,6,7},{8,9,10,11,12,13,14,15},{16,17,18,19,20,21,22,23},{24..., dimensions={0} | all-to-all | bytes 327680 | tf_op jit(solution)/shard_map/all_to_all | solution.py:373
  72.3 2.4 %collective-permute-start.5 = (bf16[8,80,128]{2,1,0:T(8,128)(2,1)S(1)}, bf16[8,80,128]{2,1,0:T(8,128)(2,1)S(1)}, u32[]{:S(2)}, u32[]{:S(2)}) collective-permute-start(bf16[8,80,128]{2,1,0:T(8,128)(2,1)S(1)} %all_to_all.20.refs_2_), channel_id=1, source_target_pairs={{0,8},{1,9},{2,10},{3,11},{4,12},{5,13},{6,14},{7,15},{8,0},{9,1},... | collective-permute-start | bytes 491528 | tf_op jit(solution)/shard_map/ppermute | solution.py:379
  74.7 7.7 %collective-permute-done.5.refs_3_ = bf16[8,80,128]{2,1,0:T(8,128)(2,1)S(1)} collective-permute-done((bf16[8,80,128]{2,1,0:T(8,128)(2,1)S(1)}, bf16[8,80,128]{2,1,0:T(8,128)(2,1)S(1)}, u32[]{:S(2)}, u32[]{:S(2)}) %collective-permute-start.5) | collective-permute-done | bytes 163872 | tf_op jit(solution)/shard_map/ppermute | solution.py:379
  82.4 1.6 %shard_map.118 = bf16[8,80,128]{2,1,0:T(8,128)(2,1)S(1)} custom-call(s32[96]{0:T(128)S(1)} %reshape.18.cols, s32[1]{0:T(128)} %bitcast.3.group, bf16[8,240,128]{2,1,0:T(8,128)(2,1)S(1)} %all-to-all-done.first.held, bf16[8,32,128]{2,1,0:T(8,128)(2,1)S(1)} %shard_map.114.refs_0_, bf16[8,32,128]{2,1,0:T(8,128)(2,1)S(1)} %collective-permute-done.2.refs_1_, ...), custom_call_target="tpu_custom_call" | custom-call | bytes 3690000 | tf_op jit(solution)/shard_map/pallas_call | solution.py:435
  84.0 8.0 %all_to_all.21.cmsg = bf16[8,80,128]{2,1,0:T(8,128)(2,1)S(1)} all-to-all(bf16[8,80,128]{2,1,0:T(8,128)(2,1)S(1)} %shard_map.118), channel_id=1, replica_groups={{0,1,2,3,4,5,6,7},{8,9,10,11,12,13,14,15},{16,17,18,19,20,21,22,23},{24..., dimensions={0} | all-to-all | bytes 327680 | tf_op jit(solution)/shard_map/all_to_all | solution.py:373
  92.1 0.0 collective-permute-done.4.vhigh
  92.1 0.0 collective-permute-done.3.vlow
  92.1 5.1 %shard_map.119 = (f32[2,512,512]{2,1,0:T(8,128)}, f32[2,512]{1,0:T(2,128)}, f32[2,512]{1,0:T(2,128)}) custom-call(bf16[2,512,1280]{2,1,0:T(8,128)(2,1)S(1)} %shard_map.112.w, bf16[512,512]{1,0:T(8,128)(2,1)} %collective-permute-done.low.ulow, bf16[512,512]{1,0:T(8,128)(2,1)} %uown.1, bf16[512,512]{1,0:T(8,128)(2,1)} %collective-permute-done.1.high.uhigh, ...), custom_call_target="tpu_custom_call" | custom-call | bytes 14760000 | tf_op jit(solution)/shard_map/pallas_call | solution.py:446
  (2 shorter events, 0.0 us)
Async XLA Ops:
  0.6 0.9 copy-start.1
  1.6 0.8 copy-start.3
  2.3 0.7 copy-start.7
  5.7 30.0 %copy-start.6 = (s32[2,5]{1,0:T(2,128)S(1)}, s32[2,5]{1,0:T(2,128)}, u32[]{:S(2)}) copy-start(s32[2,5]{1,0:T(2,128)} %cols.1) | copy-start | bytes 124
  5.7 30.0 %copy-start.8 = (s32[2]{0:T(128)S(1)}, s32[2]{0:T(128)}, u32[]{:S(2)}) copy-start(s32[2]{0:T(128)} %count.1) | copy-start | bytes 28
  5.7 13.8 %all-to-all-start = ((bf16[8,240,128]{2,1,0:T(8,128)(2,1)}), bf16[8,240,128]{2,1,0:T(8,128)(2,1)S(1)}, u32[]{:S(2)}, u32[]{:S(2)}) async-start(bf16[8,240,128]{2,1,0:T(8,128)(2,1)} %shard_map.113), calls=%async_computation | async-start | bytes 983040 | tf_op jit(solution)/shard_map/all_to_all | solution.py:373
  11.0 27.3 %collective-permute-start.1 = (bf16[512,512]{1,0:T(8,128)(2,1)}, bf16[512,512]{1,0:T(8,128)(2,1)}, u32[]{:S(2)}, u32[]{:S(2)}) collective-permute-start(bf16[512,512]{1,0:T(8,128)(2,1)} %uown.1), channel_id=1, source_target_pairs={{1,0},{2,1},{3,2},{4,3},{5,4},{6,5},{7,6},{8,7},{9,8},{10,9},{11,1... | collective-permute-start | bytes 1572872 | tf_op jit(solution)/shard_map/ppermute | solution.py:347
  15.7 22.6 %collective-permute-start = (bf16[512,512]{1,0:T(8,128)(2,1)}, bf16[512,512]{1,0:T(8,128)(2,1)}, u32[]{:S(2)}, u32[]{:S(2)}) collective-permute-start(bf16[512,512]{1,0:T(8,128)(2,1)} %uown.1), channel_id=1, source_target_pairs={{0,1},{1,2},{2,3},{3,4},{4,5},{5,6},{6,7},{7,8},{8,9},{9,10},{10,1... | collective-permute-start | bytes 1572872 | tf_op jit(solution)/shard_map/ppermute | solution.py:347
  19.5 11.0 %collective-permute-start.2 = (bf16[8,32,128]{2,1,0:T(8,128)(2,1)S(1)}, bf16[8,32,128]{2,1,0:T(8,128)(2,1)S(1)}, u32[]{:S(2)}, u32[]{:S(2)}) collective-permute-start(bf16[8,32,128]{2,1,0:T(8,128)(2,1)S(1)} %shard_map.114.refs_0_), channel_id=1, source_target_pairs={{0,8},{1,9},{2,10},{3,11},{4,12},{5,13},{6,14},{7,15},{8,0},{9,1},... | collective-permute-start | bytes 196616 | tf_op jit(solution)/shard_map/ppermute | solution.py:379
  32.3 8.5 %all-to-all-start.1 = ((bf16[8,64,128]{2,1,0:T(8,128)(2,1)}), bf16[8,64,128]{2,1,0:T(8,128)(2,1)S(1)}, u32[]{:S(2)}, u32[]{:S(2)}) async-start(bf16[8,64,128]{2,1,0:T(8,128)(2,1)} %shard_map.115), calls=%async_computation.1 | async-start | bytes 262144 | tf_op jit(solution)/shard_map/all_to_all | solution.py:373
  35.7 1.7 %copy-start = (bf16[2,2,5,256,256]{4,3,2,1,0:T(8,128)(2,1)S(1)}, bf16[2,2,5,256,256]{4,3,2,1,0:T(8,128)(2,1)}, u32[]{:S(2)}) copy-start(bf16[2,2,5,256,256]{4,3,2,1,0:T(8,128)(2,1)} %tiles.1) | copy-start | bytes 7864324
  37.4 3.3 %copy-start.2 = (bf16[2,256,32]{1,2,0:T(8,128)(2,1)S(1)}, bf16[2,256,32]{1,2,0:T(8,128)(2,1)}, u32[]{:S(2)}) copy-start(bf16[2,256,32]{1,2,0:T(8,128)(2,1)} %param.15) | copy-start | bytes 98308
  37.4 3.3 %copy-start.4 = (bf16[2,256,32]{1,2,0:T(8,128)(2,1)S(1)}, bf16[2,256,32]{1,2,0:T(8,128)(2,1)}, u32[]{:S(2)}) copy-start(bf16[2,256,32]{1,2,0:T(8,128)(2,1)} %param.16) | copy-start | bytes 98308
  37.4 3.3 %copy-start.5 = (f32[2,512]{1,0:T(2,128)S(1)}, f32[2,512]{1,0:T(2,128)}, u32[]{:S(2)}) copy-start(f32[2,512]{1,0:T(2,128)} %diag.3) | copy-start | bytes 12292
  44.9 47.2 %collective-permute-start.4 = (bf16[1040,512]{1,0:T(8,128)(2,1)S(1)}, bf16[1040,512]{1,0:T(8,128)(2,1)S(1)}, u32[]{:S(2)}, u32[]{:S(2)}) collective-permute-start(bf16[1040,512]{1,0:T(8,128)(2,1)S(1)} %shard_map.117), channel_id=1, source_target_pairs={{1,0},{2,1},{3,2},{4,3},{5,4},{6,5},{7,6},{8,7},{9,8},{10,9},{11,1... | collective-permute-start | bytes 3194888 | tf_op jit(solution)/shard_map/ppermute | solution.py:347
  47.2 44.9 %collective-permute-start.3 = (bf16[1040,512]{1,0:T(8,128)(2,1)S(1)}, bf16[1040,512]{1,0:T(8,128)(2,1)S(1)}, u32[]{:S(2)}, u32[]{:S(2)}) collective-permute-start(bf16[1040,512]{1,0:T(8,128)(2,1)S(1)} %shard_map.117), channel_id=1, source_target_pairs={{0,1},{1,2},{2,3},{3,4},{4,5},{5,6},{6,7},{7,8},{8,9},{9,10},{10,1... | collective-permute-start | bytes 3194888 | tf_op jit(solution)/shard_map/ppermute | solution.py:347
  72.3 10.1 %collective-permute-start.5 = (bf16[8,80,128]{2,1,0:T(8,128)(2,1)S(1)}, bf16[8,80,128]{2,1,0:T(8,128)(2,1)S(1)}, u32[]{:S(2)}, u32[]{:S(2)}) collective-permute-start(bf16[8,80,128]{2,1,0:T(8,128)(2,1)S(1)} %all_to_all.20.refs_2_), channel_id=1, source_target_pairs={{0,8},{1,9},{2,10},{3,11},{4,12},{5,13},{6,14},{7,15},{8,0},{9,1},... | collective-permute-start | bytes 491528 | tf_op jit(solution)/shard_map/ppermute | solution.py:379

commit v6 on v5

--- a/solution.py
+++ b/solution.py
@@ -19,10 +19,9 @@
 
 VMEM = pl.BlockSpec(memory_space=pltpu.VMEM)
 SMEM = pl.BlockSpec(memory_space=pltpu.SMEM)
-HBM = pl.BlockSpec(memory_space=pltpu.HBM)
-
-
-def call(body, out_shape, in_specs, scratch=(), micros=1.0):
+
+
+def call(body, out_shape, in_specs, scratch=(), micros=1.0, megabytes=20):
     many = isinstance(out_shape, (list, tuple))
     return pl.pallas_call(
         body,
@@ -30,7 +29,7 @@
         in_specs=in_specs,
         out_specs=[VMEM] * len(out_shape) if many else VMEM,
         scratch_shapes=list(scratch),
-        compiler_params=pltpu.CompilerParams(vmem_limit_bytes=20 * 1024 * 1024),
+        compiler_params=pltpu.CompilerParams(vmem_limit_bytes=megabytes * 1024 * 1024),
         cost_estimate=pl.CostEstimate(
             flops=0, bytes_accessed=int(micros * HBM_RATE), transcendentals=0
         ),
@@ -83,15 +82,7 @@
                 )
 
 
-def share_kernel(far_cols, u_in, right_in, coup_in, out, u, right, coup, sems):
-    copies = [
-        pltpu.make_async_copy(source, target, sems.at[i])
-        for i, (source, target) in enumerate(((u_in, u), (right_in, right), (coup_in, coup)))
-    ]
-    for copy in copies:
-        copy.start()
-    for copy in copies:
-        copy.wait()
+def share_kernel(far_cols, u, right, coup, out):
     ops, blocks, far, rank, _ = coup.shape
     size = right.shape[2]
     z = [dot(right[b], u[b * size:(b + 1) * size, :]) for b in range(blocks)]
@@ -389,13 +380,8 @@
     held = call(
         share_kernel,
         sds((SLICES, shared + STATS, LANES), BF16),
-        [SMEM, HBM, HBM, HBM],
-        [
-            pltpu.VMEM(sources.shape, BF16),
-            pltpu.VMEM(right.shape, BF16),
-            pltpu.VMEM(couplings.shape, BF16),
-            pltpu.SemaphoreType.DMA((3,)),
-        ],
+        [SMEM, VMEM, VMEM, VMEM],
+        megabytes=60,
     )(far_cols, sources, right, couplings)
     held = exchange(held)
     cols = held[:, shared, :blocks * far].astype(jnp.int32).reshape(-1)
@@ -428,9 +414,9 @@
         ],
         micros=4.0,
     )(w, low, own, high, self_terms, left, right, c1)
-    msgs = across(exchange(msg))
-    bulk = call(copy_kernel, sds(v.shape, BF16), [VMEM], micros=4.0)(v)
-    vlow, vhigh = ring(bulk)
+    msg = exchange(msg)
+    msgs = across(call(copy_kernel, sds(msg.shape, BF16), [VMEM], micros=40.0)(msg))
+    vlow, vhigh = ring(v)
 
     c2 = call(
         functools.partial(second_couple, all_blocks * size, ops, rank, far),

time: 97.8 us -> 94.9 us (0.970)
  local copies, waits for them, and re-layouts: 4.19 us -> 1.83 us
    unnamed x18 -> x12, local copies, waits for them, and re-layouts: 4.11 us -> 1.75 us
  transfers between devices with their start and end apart: 8 -> 8, of which waited for: 4 -> 4; matrix products, arithmetic and copies ran while one was open for 0% -> 0% of each run, Pallas kernels for 4% -> 5%
where the time goes in v6:
time: 94.9 us; the launch traced here: 94.4 us
  blocking collectives  33.1 us (35%)
  starting transfers between devices  26.3 us (28%)
  waiting for transfers between devices  16.6 us (17%)
  Pallas kernels  15.8 us (17%)
  local copies, waits for them, and re-layouts  1.83 us (2%)
    all_to_all x2, blocking collectives, exchange(): lax.all_to_all(x, 'store', 0, 0, axis_index_groups=groups, tiled=True)  33.1 us
    ppermute x2, starting transfers between devices, across(): parts.append(lax.ppermute(x, 'store', pairs))  10.6 us
    ppermute x2, waiting for transfers between devices, across(): parts.append(lax.ppermute(x, 'store', pairs))  10.4 us
    all_to_all x2, starting transfers between devices, exchange(): lax.all_to_all(x, 'store', 0, 0, axis_index_groups=groups, tiled=True)  8.63 us
    ppermute x2, starting transfers between devices, ring(): lax.ppermute(block, 'store', backward)  7 us
    all_to_all x2, waiting for transfers between devices, exchange(): lax.all_to_all(x, 'store', 0, 0, axis_index_groups=groups, tiled=True)  6.2 us
    pallas_call x1, Pallas kernels, shards(): call(final_kernel, [sds((ops, rows, columns), F32), sds((ops, columns), F...  5.18 us
    pallas_call x1, Pallas kernels, shards(): call(image_kernel, [sds((ops * rows + STATS, columns), BF16), sds((SLICES...  4.1 us
  transfers between devices with their start and end apart: 8, of which 4 were waited for; matrix products, arithmetic and copies ran while one was open for 0% of the time, Pallas kernels for 5%

profile of v6, /device:TPU:0, one launch (start us, length us, event | category | flops | bytes accessed | tf_op | source)
XLA Modules:
  0.0 94.4 jit_solution(6812888071887666148)
XLA Ops:
  0.6 0.0 copy-start.5
  0.6 0.0 copy-start.4
  0.7 2.2 %shard_map.113 = bf16[8,240,128]{2,1,0:T(8,128)(2,1)} custom-call(s32[2,6]{1,0:T(2,128)} %far_cols.1, bf16[512,512]{1,0:T(8,128)(2,1)} %uown.1, bf16[2,32,256]{2,1,0:T(8,128)(2,1)} %bitcast.6, bf16[2,2,6,32,32]{4,3,2,1,0:T(8,128)(2,1)} %coup.1), custom_call_target="tpu_custom_call" | custom-call | bytes 3690000 | tf_op jit(solution)/shard_map/pallas_call | solution.py:380
  2.8 5.3 %all-to-all-start = ((bf16[8,240,128]{2,1,0:T(8,128)(2,1)}), bf16[8,240,128]{2,1,0:T(8,128)(2,1)S(1)}, u32[]{:S(2)}, u32[]{:S(2)}) async-start(bf16[8,240,128]{2,1,0:T(8,128)(2,1)} %shard_map.113), calls=%async_computation | async-start | bytes 983040 | tf_op jit(solution)/shard_map/all_to_all | solution.py:364
  8.1 4.7 %collective-permute-start.1 = (bf16[512,512]{1,0:T(8,128)(2,1)}, bf16[512,512]{1,0:T(8,128)(2,1)}, u32[]{:S(2)}, u32[]{:S(2)}) collective-permute-start(bf16[512,512]{1,0:T(8,128)(2,1)} %uown.1), channel_id=1, source_target_pairs={{1,0},{2,1},{3,2},{4,3},{5,4},{6,5},{7,6},{8,7},{9,8},{10,9},{11,1... | collective-permute-start | bytes 1572872 | tf_op jit(solution)/shard_map/ppermute | solution.py:338
  12.8 0.0 collective-permute-start
  12.8 3.8 %all-to-all-done.first.held = bf16[8,240,128]{2,1,0:T(8,128)(2,1)S(1)} async-done(((bf16[8,240,128]{2,1,0:T(8,128)(2,1)}), bf16[8,240,128]{2,1,0:T(8,128)(2,1)S(1)}, u32[]{:S(2)}, u32[]{:S(2)}) %all-to-all-start) | async-done | bytes 491552 | tf_op jit(solution)/shard_map/all_to_all | solution.py:364
  16.6 8.2 %collective-permute-start.2 = (bf16[8,32,128]{2,1,0:T(8,128)(2,1)S(1)}, bf16[8,32,128]{2,1,0:T(8,128)(2,1)S(1)}, u32[]{:S(2)}, u32[]{:S(2)}) collective-permute-start(bf16[8,32,128]{2,1,0:T(8,128)(2,1)S(1)} %shard_map.114.refs_0_), channel_id=1, source_target_pairs={{0,8},{1,9},{2,10},{3,11},{4,12},{5,13},{6,14},{7,15},{8,0},{9,1},... | collective-permute-start | bytes 196616 | tf_op jit(solution)/shard_map/ppermute | solution.py:370
  24.8 0.1 reshape.18.cols
  24.9 2.7 %collective-permute-done.2.refs_1_ = bf16[8,32,128]{2,1,0:T(8,128)(2,1)S(1)} collective-permute-done((bf16[8,32,128]{2,1,0:T(8,128)(2,1)S(1)}, bf16[8,32,128]{2,1,0:T(8,128)(2,1)S(1)}, u32[]{:S(2)}, u32[]{:S(2)}) %collective-permute-start.2) | collective-permute-done | bytes 65568 | tf_op jit(solution)/shard_map/ppermute | solution.py:370
  27.6 1.8 %shard_map.115 = bf16[8,64,128]{2,1,0:T(8,128)(2,1)} custom-call(s32[96]{0:T(128)S(1)} %reshape.18.cols, s32[1]{0:T(128)} %bitcast.3.group, bf16[8,240,128]{2,1,0:T(8,128)(2,1)S(1)} %all-to-all-done.first.held, bf16[8,32,128]{2,1,0:T(8,128)(2,1)S(1)} %shard_map.114.refs_0_, bf16[8,32,128]{2,1,0:T(8,128)(2,1)S(1)} %collective-permute-done.2.refs_1_), custom_call_target="tpu_custom_call" | custom-call | bytes 3690000 | tf_op jit(solution)/shard_map/pallas_call | solution.py:399
  29.4 3.4 %all-to-all-start.1 = ((bf16[8,64,128]{2,1,0:T(8,128)(2,1)}), bf16[8,64,128]{2,1,0:T(8,128)(2,1)S(1)}, u32[]{:S(2)}, u32[]{:S(2)}) async-start(bf16[8,64,128]{2,1,0:T(8,128)(2,1)} %shard_map.115), calls=%async_computation.1 | async-start | bytes 262144 | tf_op jit(solution)/shard_map/all_to_all | solution.py:364
  32.8 0.0 copy-done.5
  32.8 0.0 copy-done.4
  32.8 0.0 copy-start
  32.8 1.7 %copy-done = bf16[2,2,5,256,256]{4,3,2,1,0:T(8,128)(2,1)S(1)} copy-done((bf16[2,2,5,256,256]{4,3,2,1,0:T(8,128)(2,1)S(1)}, bf16[2,2,5,256,256]{4,3,2,1,0:T(8,128)(2,1)}, u32[]{:S(2)}) %copy-start) | copy-done | bytes 2621464
  34.5 0.0 copy-start.1
  34.5 0.0 copy-start.2
  34.5 0.0 copy-start.3
  34.5 0.9 shard_map.112.w
  35.4 0.0 collective-permute-done.1.high.uhigh
  35.4 0.0 collective-permute-done.low.ulow
  35.5 2.4 %all-to-all-done.1.cmsg = bf16[8,64,128]{2,1,0:T(8,128)(2,1)S(1)} async-done(((bf16[8,64,128]{2,1,0:T(8,128)(2,1)}), bf16[8,64,128]{2,1,0:T(8,128)(2,1)S(1)}, u32[]{:S(2)}, u32[]{:S(2)}) %all-to-all-start.1) | async-done | bytes 131104 | tf_op jit(solution)/shard_map/all_to_all | solution.py:364
  37.9 0.0 copy-done.1
  37.9 0.0 copy-done.2
  37.9 0.0 copy-done.3
  37.9 4.1 %shard_map.116 = (bf16[1040,512]{1,0:T(8,128)(2,1)S(1)}, bf16[8,80,128]{2,1,0:T(8,128)(2,1)S(1)}) custom-call(bf16[2,512,1280]{2,1,0:T(8,128)(2,1)S(1)} %shard_map.112.w, bf16[512,512]{1,0:T(8,128)(2,1)} %collective-permute-done.low.ulow, bf16[512,512]{1,0:T(8,128)(2,1)} %uown.1, bf16[512,512]{1,0:T(8,128)(2,1)} %collective-permute-done.1.high.uhigh, ...), custom_call_target="tpu_custom_call" | custom-call | bytes 14760000 | tf_op jit(solution)/shard_map/pallas_call | solution.py:407
  42.0 2.3 %collective-permute-start.4 = (bf16[1040,512]{1,0:T(8,128)(2,1)S(1)}, bf16[1040,512]{1,0:T(8,128)(2,1)S(1)}, u32[]{:S(2)}, u32[]{:S(2)}) collective-permute-start(bf16[1040,512]{1,0:T(8,128)(2,1)S(1)} %get-tuple-element.5.vown), channel_id=1, source_target_pairs={{1,0},{2,1},{3,2},{4,3},{5,4},{6,5},{7,6},{8,7},{9,8},{10,9},{11,1... | collective-permute-start | bytes 3194888 | tf_op jit(solution)/shard_map/ppermute | solution.py:338
  44.3 0.0 collective-permute-start.3
  44.3 25.1 %all_to_all.20.source = bf16[8,80,128]{2,1,0:T(8,128)(2,1)S(1)} all-to-all(bf16[8,80,128]{2,1,0:T(8,128)(2,1)S(1)} %get-tuple-element.6), channel_id=1, replica_groups={{0,1,2,3,4,5,6,7},{8,9,10,11,12,13,14,15},{16,17,18,19,20,21,22,23},{24..., dimensions={0} | all-to-all | bytes 327680 | tf_op jit(solution)/shard_map/all_to_all | solution.py:364
  69.4 2.4 %collective-permute-start.5 = (bf16[8,80,128]{2,1,0:T(8,128)(2,1)S(1)}, bf16[8,80,128]{2,1,0:T(8,128)(2,1)S(1)}, u32[]{:S(2)}, u32[]{:S(2)}) collective-permute-start(bf16[8,80,128]{2,1,0:T(8,128)(2,1)S(1)} %shard_map.117.refs_2_), channel_id=1, source_target_pairs={{0,8},{1,9},{2,10},{3,11},{4,12},{5,13},{6,14},{7,15},{8,0},{9,1},... | collective-permute-start | bytes 491528 | tf_op jit(solution)/shard_map/ppermute | solution.py:370
  71.8 7.7 %collective-permute-done.5.refs_3_ = bf16[8,80,128]{2,1,0:T(8,128)(2,1)S(1)} collective-permute-done((bf16[8,80,128]{2,1,0:T(8,128)(2,1)S(1)}, bf16[8,80,128]{2,1,0:T(8,128)(2,1)S(1)}, u32[]{:S(2)}, u32[]{:S(2)}) %collective-permute-start.5) | collective-permute-done | bytes 163872 | tf_op jit(solution)/shard_map/ppermute | solution.py:370
  79.6 1.6 %shard_map.118 = bf16[8,80,128]{2,1,0:T(8,128)(2,1)S(1)} custom-call(s32[96]{0:T(128)S(1)} %reshape.18.cols, s32[1]{0:T(128)} %bitcast.3.group, bf16[8,240,128]{2,1,0:T(8,128)(2,1)S(1)} %all-to-all-done.first.held, bf16[8,32,128]{2,1,0:T(8,128)(2,1)S(1)} %shard_map.114.refs_0_, bf16[8,32,128]{2,1,0:T(8,128)(2,1)S(1)} %collective-permute-done.2.refs_1_, ...), custom_call_target="tpu_custom_call" | custom-call | bytes 3690000 | tf_op jit(solution)/shard_map/pallas_call | solution.py:421
  81.2 8.0 %all_to_all.21.cmsg = bf16[8,80,128]{2,1,0:T(8,128)(2,1)S(1)} all-to-all(bf16[8,80,128]{2,1,0:T(8,128)(2,1)S(1)} %shard_map.118), channel_id=1, replica_groups={{0,1,2,3,4,5,6,7},{8,9,10,11,12,13,14,15},{16,17,18,19,20,21,22,23},{24..., dimensions={0} | all-to-all | bytes 327680 | tf_op jit(solution)/shard_map/all_to_all | solution.py:364
  89.2 0.0 collective-permute-done.4.vhigh
  89.2 0.0 collective-permute-done.3.vlow
  89.2 5.2 %shard_map.119 = (f32[2,512,512]{2,1,0:T(8,128)}, f32[2,512]{1,0:T(2,128)}, f32[2,512]{1,0:T(2,128)}) custom-call(bf16[2,512,1280]{2,1,0:T(8,128)(2,1)S(1)} %shard_map.112.w, bf16[512,512]{1,0:T(8,128)(2,1)} %collective-permute-done.low.ulow, bf16[512,512]{1,0:T(8,128)(2,1)} %uown.1, bf16[512,512]{1,0:T(8,128)(2,1)} %collective-permute-done.1.high.uhigh, ...), custom_call_target="tpu_custom_call" | custom-call | bytes 14760000 | tf_op jit(solution)/shard_map/pallas_call | solution.py:432
  (3 shorter events, 0.0 us)
Async XLA Ops:
  0.6 32.1 %copy-start.5 = (s32[2]{0:T(128)S(1)}, s32[2]{0:T(128)}, u32[]{:S(2)}) copy-start(s32[2]{0:T(128)} %count.1) | copy-start | bytes 28
  0.6 32.1 %copy-start.4 = (s32[2,5]{1,0:T(2,128)S(1)}, s32[2,5]{1,0:T(2,128)}, u32[]{:S(2)}) copy-start(s32[2,5]{1,0:T(2,128)} %cols.1) | copy-start | bytes 124
  2.8 13.7 %all-to-all-start = ((bf16[8,240,128]{2,1,0:T(8,128)(2,1)}), bf16[8,240,128]{2,1,0:T(8,128)(2,1)S(1)}, u32[]{:S(2)}, u32[]{:S(2)}) async-start(bf16[8,240,128]{2,1,0:T(8,128)(2,1)} %shard_map.113), calls=%async_computation | async-start | bytes 983040 | tf_op jit(solution)/shard_map/all_to_all | solution.py:364
  8.1 27.3 %collective-permute-start.1 = (bf16[512,512]{1,0:T(8,128)(2,1)}, bf16[512,512]{1,0:T(8,128)(2,1)}, u32[]{:S(2)}, u32[]{:S(2)}) collective-permute-start(bf16[512,512]{1,0:T(8,128)(2,1)} %uown.1), channel_id=1, source_target_pairs={{1,0},{2,1},{3,2},{4,3},{5,4},{6,5},{7,6},{8,7},{9,8},{10,9},{11,1... | collective-permute-start | bytes 1572872 | tf_op jit(solution)/shard_map/ppermute | solution.py:338
  12.8 22.7 %collective-permute-start = (bf16[512,512]{1,0:T(8,128)(2,1)}, bf16[512,512]{1,0:T(8,128)(2,1)}, u32[]{:S(2)}, u32[]{:S(2)}) collective-permute-start(bf16[512,512]{1,0:T(8,128)(2,1)} %uown.1), channel_id=1, source_target_pairs={{0,1},{1,2},{2,3},{3,4},{4,5},{5,6},{6,7},{7,8},{8,9},{9,10},{10,1... | collective-permute-start | bytes 1572872 | tf_op jit(solution)/shard_map/ppermute | solution.py:338
  16.6 11.0 %collective-permute-start.2 = (bf16[8,32,128]{2,1,0:T(8,128)(2,1)S(1)}, bf16[8,32,128]{2,1,0:T(8,128)(2,1)S(1)}, u32[]{:S(2)}, u32[]{:S(2)}) collective-permute-start(bf16[8,32,128]{2,1,0:T(8,128)(2,1)S(1)} %shard_map.114.refs_0_), channel_id=1, source_target_pairs={{0,8},{1,9},{2,10},{3,11},{4,12},{5,13},{6,14},{7,15},{8,0},{9,1},... | collective-permute-start | bytes 196616 | tf_op jit(solution)/shard_map/ppermute | solution.py:370
  29.4 8.5 %all-to-all-start.1 = ((bf16[8,64,128]{2,1,0:T(8,128)(2,1)}), bf16[8,64,128]{2,1,0:T(8,128)(2,1)S(1)}, u32[]{:S(2)}, u32[]{:S(2)}) async-start(bf16[8,64,128]{2,1,0:T(8,128)(2,1)} %shard_map.115), calls=%async_computation.1 | async-start | bytes 262144 | tf_op jit(solution)/shard_map/all_to_all | solution.py:364
  32.8 1.7 %copy-start = (bf16[2,2,5,256,256]{4,3,2,1,0:T(8,128)(2,1)S(1)}, bf16[2,2,5,256,256]{4,3,2,1,0:T(8,128)(2,1)}, u32[]{:S(2)}) copy-start(bf16[2,2,5,256,256]{4,3,2,1,0:T(8,128)(2,1)} %tiles.1) | copy-start | bytes 7864324
  34.5 3.3 %copy-start.1 = (bf16[2,256,32]{1,2,0:T(8,128)(2,1)S(1)}, bf16[2,256,32]{1,2,0:T(8,128)(2,1)}, u32[]{:S(2)}) copy-start(bf16[2,256,32]{1,2,0:T(8,128)(2,1)} %param.15) | copy-start | bytes 98308
  34.5 3.3 %copy-start.2 = (bf16[2,256,32]{1,2,0:T(8,128)(2,1)S(1)}, bf16[2,256,32]{1,2,0:T(8,128)(2,1)}, u32[]{:S(2)}) copy-start(bf16[2,256,32]{1,2,0:T(8,128)(2,1)} %param.16) | copy-start | bytes 98308
  34.5 3.3 %copy-start.3 = (f32[2,512]{1,0:T(2,128)S(1)}, f32[2,512]{1,0:T(2,128)}, u32[]{:S(2)}) copy-start(f32[2,512]{1,0:T(2,128)} %diag.3) | copy-start | bytes 12292
  42.0 47.2 %collective-permute-start.4 = (bf16[1040,512]{1,0:T(8,128)(2,1)S(1)}, bf16[1040,512]{1,0:T(8,128)(2,1)S(1)}, u32[]{:S(2)}, u32[]{:S(2)}) collective-permute-start(bf16[1040,512]{1,0:T(8,128)(2,1)S(1)} %get-tuple-element.5.vown), channel_id=1, source_target_pairs={{1,0},{2,1},{3,2},{4,3},{5,4},{6,5},{7,6},{8,7},{9,8},{10,9},{11,1... | collective-permute-start | bytes 3194888 | tf_op jit(solution)/shard_map/ppermute | solution.py:338
  44.3 44.9 %collective-permute-start.3 = (bf16[1040,512]{1,0:T(8,128)(2,1)S(1)}, bf16[1040,512]{1,0:T(8,128)(2,1)S(1)}, u32[]{:S(2)}, u32[]{:S(2)}) collective-permute-start(bf16[1040,512]{1,0:T(8,128)(2,1)S(1)} %get-tuple-element.5.vown), channel_id=1, source_target_pairs={{0,1},{1,2},{2,3},{3,4},{4,5},{5,6},{6,7},{7,8},{8,9},{9,10},{10,1... | collective-permute-start | bytes 3194888 | tf_op jit(solution)/shard_map/ppermute | solution.py:338
  69.4 10.2 %collective-permute-start.5 = (bf16[8,80,128]{2,1,0:T(8,128)(2,1)S(1)}, bf16[8,80,128]{2,1,0:T(8,128)(2,1)S(1)}, u32[]{:S(2)}, u32[]{:S(2)}) collective-permute-start(bf16[8,80,128]{2,1,0:T(8,128)(2,1)S(1)} %shard_map.117.refs_2_), channel_id=1, source_target_pairs={{0,8},{1,9},{2,10},{3,11},{4,12},{5,13},{6,14},{7,15},{8,0},{9,1},... | collective-permute-start | bytes 491528 | tf_op jit(solution)/shard_map/ppermute | solution.py:370

commit v7 on v6

--- a/solution.py
+++ b/solution.py
@@ -82,14 +82,17 @@
                 )
 
 
-def share_kernel(far_cols, u, right, coup, out):
-    ops, blocks, far, rank, _ = coup.shape
-    size = right.shape[2]
+def coeff_kernel(u, right, out):
+    blocks, rank, size = right.shape
     z = [dot(right[b], u[b * size:(b + 1) * size, :]) for b in range(blocks)]
     for pair in range(SLICES // 2):
         first, second = halves(chunk(z[0], pair), chunk(z[1], pair))
-        out[2 * pair, 0:rank, :] = first.astype(BF16)
-        out[2 * pair + 1, 0:rank, :] = second.astype(BF16)
+        out[2 * pair] = first.astype(BF16)
+        out[2 * pair + 1] = second.astype(BF16)
+
+
+def pack_kernel(far_cols, coup, out):
+    ops, blocks, far, rank, _ = coup.shape
     whole, rest = [], []
     for b in range(blocks):
         tiles = [
@@ -103,25 +106,29 @@
     for b in range(blocks):
         for f in range(far):
             names = jnp.where(lane == b * far + f, far_cols[b, f].astype(F32), names)
-    whole = jnp.concatenate(
+    out[...] = jnp.concatenate(
         whole + [jnp.concatenate(rest, axis=1), names.astype(BF16)], axis=0
     )
+
+
+def share_kernel(packed, *refs):
+    parts, out = refs[:-1], refs[-1]
+    rows = packed.shape[0]
+    rank = parts[0].shape[1]
     for s in range(SLICES):
-        out[s, rank:, :] = whole
-
-
-def relay_kernel(first, z):
-    z[...] = first[:, 0:z.shape[1], :]
-
-
-def copy_kernel(source, target):
+        out[s, 0:rows, :] = packed[...]
+    for m, part in enumerate(parts):
+        out[:, rows + m * rank:rows + (m + 1) * rank, :] = part[...]
+
+
+def copy_kernel(source, after, target):
     target[...] = source[...]
 
 
 def coupling_rows(held, s, b, ops, rank):
     body = ops * rank
-    first = held[s, rank + b * body:rank + (b + 1) * body, :]
-    rest = held[s, rank + 2 * body:rank + 3 * body, b * HALF:(b + 1) * HALF]
+    first = held[s, b * body:(b + 1) * body, :]
+    rest = held[s, 2 * body:3 * body, b * HALF:(b + 1) * HALF]
     return jnp.concatenate([first, rest], axis=1)
 
 
@@ -146,16 +153,21 @@
     return both.reshape(count * 2 * rank, LANES).astype(BF16)
 
 
+def held_part(held, m, ops, rank):
+    at = 3 * ops * rank + STATS + m * rank
+    return held[:, at:at + rank, :].astype(F32)
+
+
 def group_at(group, m, groups, step):
     return pl.multiple_of(lax.rem(group[0] + (groups - m), groups) * step, step)
 
 
-def first_couple(ops, rank, far, cols, group, held, *refs):
-    parts, (out, zs) = refs[:-2], refs[-2:]
+def first_couple(ops, rank, far, cols, group, held, out, zs):
     step = SLICES * 2 * rank
-    for m, part in enumerate(parts):
-        at = group_at(group, m, len(parts), step)
-        zs[pl.ds(at, step), :] = spread_rows(part[...].astype(F32), rank)
+    count = zs.shape[0] // step
+    for m in range(count):
+        at = group_at(group, m, count, step)
+        zs[pl.ds(at, step), :] = spread_rows(held_part(held, m, ops, rank), rank)
     for s in range(SLICES):
         c = [couple(cols, held, s, b, ops, rank, far, [zs]) for b in range(2)]
         out[s] = halves(c[0], c[1])[0].astype(BF16)
@@ -252,9 +264,8 @@
 
 
 def second_couple(panels, ops, rank, far, cols, group, held, *refs):
-    out, zs, st = refs[-3:]
-    count = (len(refs) - 3) // 2
-    z1, msgs = refs[:count], refs[count:2 * count]
+    msgs, (out, zs, st) = refs[:-3], refs[-3:]
+    count = len(msgs)
     body = ops * rank
     step = SLICES * 2 * rank
     for m, msg in enumerate(msgs):
@@ -273,10 +284,10 @@
         norm = jnp.sqrt(jnp.sum(spread, axis=0, keepdims=True) / panels / scale_sq + EPSILON)
         heights.append(height)
         norms.append(norm)
-    for m, (base, msg) in enumerate(zip(z1, msgs)):
+    for m, msg in enumerate(msgs):
         at = group_at(group, m, count, step)
         mine = msg[:, body:body + STATS, :].astype(F32)
-        base = base[...].astype(F32)
+        base = held_part(held, m, ops, rank)
         for o in range(ops):
             delta = join3(mine, o) - heights[o]
             z = msg[:, o * rank:(o + 1) * rank, :].astype(F32) + delta[:, None, :] * base
@@ -376,18 +387,22 @@
     left = jnp.transpose(basis_left, (0, 2, 1))
     right = jnp.transpose(basis_right, (0, 2, 1))
 
-    shared = rank + (blocks + 1) * body
+    low, high = ring(sources)
+    z1 = call(coeff_kernel, sds((SLICES, rank, LANES), BF16), [VMEM, VMEM], megabytes=60)(
+        sources, right
+    )
+    z1 = across(z1)
+    shared = (blocks + 1) * body
+    packed = call(pack_kernel, sds((shared + STATS, LANES), BF16), [SMEM, VMEM])(
+        far_cols, couplings
+    )
     held = call(
         share_kernel,
-        sds((SLICES, shared + STATS, LANES), BF16),
-        [SMEM, VMEM, VMEM, VMEM],
-        megabytes=60,
-    )(far_cols, sources, right, couplings)
+        sds((SLICES, shared + STATS + count * rank, LANES), BF16),
+        [VMEM] * (1 + count),
+    )(packed, *z1)
     held = exchange(held)
     cols = held[:, shared, :blocks * far].astype(jnp.int32).reshape(-1)
-    z1 = across(call(relay_kernel, sds((SLICES, rank, LANES), BF16), [VMEM])(held))
-    own = sources
-    low, high = ring(own)
 
     w = call(
         functools.partial(order_tiles, all_blocks),
@@ -399,9 +414,9 @@
     c1 = call(
         functools.partial(first_couple, ops, rank, far),
         sds((SLICES, body, LANES), BF16),
-        [SMEM, SMEM] + [VMEM] * (1 + count),
+        [SMEM, SMEM, VMEM],
         [pltpu.VMEM((n * blocks * rank, LANES), BF16)],
-    )(cols, group, held, *z1)
+    )(cols, group, held)
     c1 = exchange(c1)
 
     v, msg = call(
@@ -413,20 +428,23 @@
             pltpu.VMEM((blocks, body, columns), BF16),
         ],
         micros=4.0,
-    )(w, low, own, high, self_terms, left, right, c1)
+    )(w, low, sources, high, self_terms, left, right, c1)
     msg = exchange(msg)
-    msgs = across(call(copy_kernel, sds(msg.shape, BF16), [VMEM], micros=40.0)(msg))
-    vlow, vhigh = ring(v)
+    msgs = across(msg)
+    bulk = call(
+        copy_kernel, sds(v.shape, BF16), [VMEM, pl.BlockSpec(memory_space=pl.ANY)], micros=8.0
+    )(v, msg)
+    vlow, vhigh = ring(bulk)
 
     c2 = call(
         functools.partial(second_couple, all_blocks * size, ops, rank, far),
         sds((SLICES, body + STATS, LANES), BF16),
-        [SMEM, SMEM] + [VMEM] * (1 + 2 * count),
+        [SMEM, SMEM] + [VMEM] * (1 + count),
         [
             pltpu.VMEM((ops, n * blocks * rank, LANES), BF16),
             pltpu.VMEM((n, STATS, LANES), F32),
         ],
-    )(cols, group, held, *z1, *msgs)
+    )(cols, group, held, *msgs)
     c2 = exchange(c2)
 
     images, heights, norms = call(
@@ -439,7 +457,7 @@
             pltpu.VMEM((STATS, columns), F32),
         ],
         micros=4.0,
-    )(w, low, own, high, vlow, v, vhigh, self_terms, left, c2)
+    )(w, low, sources, high, vlow, v, vhigh, self_terms, left, c2)
     return images, heights, norms
 
 

time: 94.9 us -> 90.8 us (0.957)
  blocking collectives: 33.1 us -> 15.7 us
  waiting for transfers between devices: 16.6 us -> 27.9 us
  local copies, waits for them, and re-layouts: 1.83 us -> 4.28 us
  starting transfers between devices: 26.3 us -> 24.7 us
  Pallas kernels: 15.8 us -> 17 us
    all_to_all x2, blocking collectives: 33.1 us -> 15.7 us  [exchange(): lax.all_to_all(x, 'store', 0, 0, axis_index_groups=groups, tiled=True)]
    ppermute x2, waiting for transfers between devices: 10.4 us -> 21 us  [across(): parts.append(lax.ppermute(x, 'store', pairs))]
    ppermute x2, starting transfers between devices: 10.6 us -> 4.62 us  [across(): parts.append(lax.ppermute(x, 'store', pairs))]
    all_to_all x2, starting transfers between devices: 8.63 us -> 12.3 us  [exchange(): lax.all_to_all(x, 'store', 0, 0, axis_index_groups=groups, tiled=True)]
    unnamed x12 -> x18, local copies, waits for them, and re-layouts: 1.75 us -> 4.2 us
    pallas_call x3 -> x4, Pallas kernels: 2.2 us -> 3.57 us  [the longest x1 1.95 us: shards(): call(coeff_kernel, sds((SLICES, rank, LANES), BF16), [VMEM, VMEM], megaby...]
  transfers between devices with their start and end apart: 8 -> 8, of which waited for: 4 -> 4; matrix products, arithmetic and copies ran while one was open for 0% -> 0% of each run, Pallas kernels for 5% -> 6%
where the time goes in v7:
time: 90.8 us; the launch traced here: 90.2 us
  waiting for transfers between devices  27.9 us (31%)
  starting transfers between devices  24.7 us (27%)
  Pallas kernels  17 us (19%)
  blocking collectives  15.7 us (17%)
  local copies, waits for them, and re-layouts  4.28 us (5%)
    ppermute x2, waiting for transfers between devices, across(): parts.append(lax.ppermute(x, 'store', pairs))  21 us
    all_to_all x2, blocking collectives, exchange(): lax.all_to_all(x, 'store', 0, 0, axis_index_groups=groups, tiled=True)  15.7 us
    all_to_all x2, starting transfers between devices, exchange(): lax.all_to_all(x, 'store', 0, 0, axis_index_groups=groups, tiled=True)  12.3 us
    ppermute x2, starting transfers between devices, ring(): lax.ppermute(block, 'store', backward)  7.75 us
    all_to_all x2, waiting for transfers between devices, exchange(): lax.all_to_all(x, 'store', 0, 0, axis_index_groups=groups, tiled=True)  6.85 us
    pallas_call x1, Pallas kernels, shards(): call(final_kernel, [sds((ops, rows, columns), F32), sds((ops, columns), F...  5.02 us
    ppermute x2, starting transfers between devices, across(): parts.append(lax.ppermute(x, 'store', pairs))  4.62 us
    unnamed x18, local copies, waits for them, and re-layouts  4.2 us
  transfers between devices with their start and end apart: 8, of which 4 were waited for; matrix products, arithmetic and copies ran while one was open for 0% of the time, Pallas kernels for 6%

profile of v7, /device:TPU:0, one launch (start us, length us, event | category | flops | bytes accessed | tf_op | source)
XLA Modules:
  0.0 90.2 jit_solution(7992547123473384880)
XLA Ops:
  0.6 1.9 %shard_map.114.refs_0_ = bf16[8,32,128]{2,1,0:T(8,128)(2,1)} custom-call(bf16[512,512]{1,0:T(8,128)(2,1)} %uown.1, bf16[2,32,256]{2,1,0:T(8,128)(2,1)} %bitcast.6), custom_call_target="tpu_custom_call" | custom-call | bytes 3690000 | tf_op jit(solution)/shard_map/pallas_call | solution.py:391
  2.6 4.0 %collective-permute-start.2 = (bf16[8,32,128]{2,1,0:T(8,128)(2,1)}, bf16[8,32,128]{2,1,0:T(8,128)(2,1)S(1)}, u32[]{:S(2)}, u32[]{:S(2)}) collective-permute-start(bf16[8,32,128]{2,1,0:T(8,128)(2,1)} %shard_map.114.refs_0_), channel_id=1, source_target_pairs={{0,8},{1,9},{2,10},{3,11},{4,12},{5,13},{6,14},{7,15},{8,0},{9,1},... | collective-permute-start | bytes 196616 | tf_op jit(solution)/shard_map/ppermute | solution.py:381
  6.6 0.0 copy-start.2
  6.6 0.9 %copy-done.2 = bf16[2,2,6,32,32]{4,3,2,1,0:T(8,128)(2,1)S(1)} copy-done((bf16[2,2,6,32,32]{4,3,2,1,0:T(8,128)(2,1)S(1)}, bf16[2,2,6,32,32]{4,3,2,1,0:T(8,128)(2,1)}, u32[]{:S(2)}) %copy-start.2) | copy-done | bytes 49176
  7.5 0.0 copy-start.6
  7.5 0.7 copy-done.6
  8.2 0.7 shard_map.113.packed
  8.9 1.6 %collective-permute-done.2.refs_1_ = bf16[8,32,128]{2,1,0:T(8,128)(2,1)S(1)} collective-permute-done((bf16[8,32,128]{2,1,0:T(8,128)(2,1)}, bf16[8,32,128]{2,1,0:T(8,128)(2,1)S(1)}, u32[]{:S(2)}, u32[]{:S(2)}) %collective-permute-start.2) | collective-permute-done | bytes 65568 | tf_op jit(solution)/shard_map/ppermute | solution.py:381
  10.5 0.0 copy-start.1
  10.5 0.8 copy-done.1
  11.3 0.9 shard_map.115
  12.2 0.0 copy-start.7
  12.2 0.0 copy-start.8
  12.2 3.7 %all-to-all-start = ((bf16[8,272,128]{2,1,0:T(8,128)(2,1)}), bf16[8,272,128]{2,1,0:T(8,128)(2,1)S(1)}, u32[]{:S(2)}, u32[]{:S(2)}) async-start(bf16[8,272,128]{2,1,0:T(8,128)(2,1)} %shard_map.115), calls=%async_computation | async-start | bytes 1114112 | tf_op jit(solution)/shard_map/all_to_all | solution.py:375
  15.9 4.8 %collective-permute-start.1 = (bf16[512,512]{1,0:T(8,128)(2,1)}, bf16[512,512]{1,0:T(8,128)(2,1)}, u32[]{:S(2)}, u32[]{:S(2)}) collective-permute-start(bf16[512,512]{1,0:T(8,128)(2,1)} %uown.1), channel_id=1, source_target_pairs={{1,0},{2,1},{3,2},{4,3},{5,4},{6,5},{7,6},{8,7},{9,8},{10,9},{11,1... | collective-permute-start | bytes 1572872 | tf_op jit(solution)/shard_map/ppermute | solution.py:349
  20.6 0.0 collective-permute-start
  20.6 4.4 %all-to-all-done.held = bf16[8,272,128]{2,1,0:T(8,128)(2,1)S(1)} async-done(((bf16[8,272,128]{2,1,0:T(8,128)(2,1)}), bf16[8,272,128]{2,1,0:T(8,128)(2,1)S(1)}, u32[]{:S(2)}, u32[]{:S(2)}) %all-to-all-start) | async-done | bytes 557088 | tf_op jit(solution)/shard_map/all_to_all | solution.py:375
  25.0 0.1 reshape.18.cols
  25.1 1.8 %shard_map.116 = bf16[8,64,128]{2,1,0:T(8,128)(2,1)} custom-call(s32[96]{0:T(128)S(1)} %reshape.18.cols, s32[1]{0:T(128)} %bitcast.3.group, bf16[8,272,128]{2,1,0:T(8,128)(2,1)S(1)} %all-to-all-done.held), custom_call_target="tpu_custom_call" | custom-call | bytes 3690000 | tf_op jit(solution)/shard_map/pallas_call | solution.py:414
  26.9 8.6 %all-to-all-start.1 = ((bf16[8,64,128]{2,1,0:T(8,128)(2,1)}), bf16[8,64,128]{2,1,0:T(8,128)(2,1)S(1)}, u32[]{:S(2)}, u32[]{:S(2)}) async-start(bf16[8,64,128]{2,1,0:T(8,128)(2,1)} %shard_map.116), calls=%async_computation.1 | async-start | bytes 262144 | tf_op jit(solution)/shard_map/all_to_all | solution.py:375
  35.5 0.0 copy-done.7
  35.5 0.0 copy-done.8
  35.5 0.0 copy-start
  35.5 1.7 %copy-done = bf16[2,2,5,256,256]{4,3,2,1,0:T(8,128)(2,1)S(1)} copy-done((bf16[2,2,5,256,256]{4,3,2,1,0:T(8,128)(2,1)S(1)}, bf16[2,2,5,256,256]{4,3,2,1,0:T(8,128)(2,1)}, u32[]{:S(2)}) %copy-start) | copy-done | bytes 2621464
  37.3 0.0 copy-start.3
  37.3 0.0 copy-start.4
  37.3 0.0 copy-start.5
  37.3 0.9 shard_map.112.w
  38.2 0.0 collective-permute-done.1.high.uhigh
  38.2 0.0 collective-permute-done.low.ulow
  38.2 2.5 %all-to-all-done.1.cmsg = bf16[8,64,128]{2,1,0:T(8,128)(2,1)S(1)} async-done(((bf16[8,64,128]{2,1,0:T(8,128)(2,1)}), bf16[8,64,128]{2,1,0:T(8,128)(2,1)S(1)}, u32[]{:S(2)}, u32[]{:S(2)}) %all-to-all-start.1) | async-done | bytes 131104 | tf_op jit(solution)/shard_map/all_to_all | solution.py:375
  40.7 0.0 copy-done.3
  40.7 0.0 copy-done.4
  40.7 0.0 copy-done.5
  40.7 4.1 %shard_map.117 = (bf16[1040,512]{1,0:T(8,128)(2,1)S(1)}, bf16[8,80,128]{2,1,0:T(8,128)(2,1)S(1)}) custom-call(bf16[2,512,1280]{2,1,0:T(8,128)(2,1)S(1)} %shard_map.112.w, bf16[512,512]{1,0:T(8,128)(2,1)} %collective-permute-done.low.ulow, bf16[512,512]{1,0:T(8,128)(2,1)} %uown.1, bf16[512,512]{1,0:T(8,128)(2,1)} %collective-permute-done.1.high.uhigh, ...), custom_call_target="tpu_custom_call" | custom-call | bytes 14760000 | tf_op jit(solution)/shard_map/pallas_call | solution.py:422
  44.8 7.8 %all_to_all.20.after.refs_0_ = bf16[8,80,128]{2,1,0:T(8,128)(2,1)S(1)} all-to-all(bf16[8,80,128]{2,1,0:T(8,128)(2,1)S(1)} %get-tuple-element.6), channel_id=1, replica_groups={{0,1,2,3,4,5,6,7},{8,9,10,11,12,13,14,15},{16,17,18,19,20,21,22,23},{24..., dimensions={0} | all-to-all | bytes 327680 | tf_op jit(solution)/shard_map/all_to_all | solution.py:375
  52.6 0.1 shard_map.118
  52.7 3.0 %collective-permute-start.4 = (bf16[1040,512]{1,0:T(8,128)(2,1)S(1)}, bf16[1040,512]{1,0:T(8,128)(2,1)S(1)}, u32[]{:S(2)}, u32[]{:S(2)}) collective-permute-start(bf16[1040,512]{1,0:T(8,128)(2,1)S(1)} %shard_map.118), channel_id=1, source_target_pairs={{1,0},{2,1},{3,2},{4,3},{5,4},{6,5},{7,6},{8,7},{9,8},{10,9},{11,1... | collective-permute-start | bytes 3194888 | tf_op jit(solution)/shard_map/ppermute | solution.py:349
  55.7 0.0 collective-permute-start.3
  55.7 0.6 collective-permute-start.5
  56.3 19.5 %collective-permute-done.5.refs_1_ = bf16[8,80,128]{2,1,0:T(8,128)(2,1)S(1)} collective-permute-done((bf16[8,80,128]{2,1,0:T(8,128)(2,1)S(1)}, bf16[8,80,128]{2,1,0:T(8,128)(2,1)S(1)}, u32[]{:S(2)}, u32[]{:S(2)}) %collective-permute-start.5) | collective-permute-done | bytes 163872 | tf_op jit(solution)/shard_map/ppermute | solution.py:381
  75.7 1.6 %shard_map.119 = bf16[8,80,128]{2,1,0:T(8,128)(2,1)S(1)} custom-call(s32[96]{0:T(128)S(1)} %reshape.18.cols, s32[1]{0:T(128)} %bitcast.3.group, bf16[8,272,128]{2,1,0:T(8,128)(2,1)S(1)} %all-to-all-done.held, bf16[8,80,128]{2,1,0:T(8,128)(2,1)S(1)} %all_to_all.20.after.refs_0_, bf16[8,80,128]{2,1,0:T(8,128)(2,1)S(1)} %collective-permute-done.5.refs_1_), custom_call_target="tpu_custom_call" | custom-call | bytes 3690000 | tf_op jit(solution)/shard_map/pallas_call | solution.py:439
  77.3 7.8 %all_to_all.21.cmsg = bf16[8,80,128]{2,1,0:T(8,128)(2,1)S(1)} all-to-all(bf16[8,80,128]{2,1,0:T(8,128)(2,1)S(1)} %shard_map.119), channel_id=1, replica_groups={{0,1,2,3,4,5,6,7},{8,9,10,11,12,13,14,15},{16,17,18,19,20,21,22,23},{24..., dimensions={0} | all-to-all | bytes 327680 | tf_op jit(solution)/shard_map/all_to_all | solution.py:375
  85.2 0.0 collective-permute-done.4.vhigh
  85.2 0.0 collective-permute-done.3.vlow
  85.2 5.0 %shard_map.120 = (f32[2,512,512]{2,1,0:T(8,128)}, f32[2,512]{1,0:T(2,128)}, f32[2,512]{1,0:T(2,128)}) custom-call(bf16[2,512,1280]{2,1,0:T(8,128)(2,1)S(1)} %shard_map.112.w, bf16[512,512]{1,0:T(8,128)(2,1)} %collective-permute-done.low.ulow, bf16[512,512]{1,0:T(8,128)(2,1)} %uown.1, bf16[512,512]{1,0:T(8,128)(2,1)} %collective-permute-done.1.high.uhigh, ...), custom_call_target="tpu_custom_call" | custom-call | bytes 14760000 | tf_op jit(solution)/shard_map/pallas_call | solution.py:450
  (1 shorter events, 0.0 us)
Async XLA Ops:
  2.6 7.9 %collective-permute-start.2 = (bf16[8,32,128]{2,1,0:T(8,128)(2,1)}, bf16[8,32,128]{2,1,0:T(8,128)(2,1)S(1)}, u32[]{:S(2)}, u32[]{:S(2)}) collective-permute-start(bf16[8,32,128]{2,1,0:T(8,128)(2,1)} %shard_map.114.refs_0_), channel_id=1, source_target_pairs={{0,8},{1,9},{2,10},{3,11},{4,12},{5,13},{6,14},{7,15},{8,0},{9,1},... | collective-permute-start | bytes 196616 | tf_op jit(solution)/shard_map/ppermute | solution.py:381
  6.6 0.9 %copy-start.2 = (bf16[2,2,6,32,32]{4,3,2,1,0:T(8,128)(2,1)S(1)}, bf16[2,2,6,32,32]{4,3,2,1,0:T(8,128)(2,1)}, u32[]{:S(2)}) copy-start(bf16[2,2,6,32,32]{4,3,2,1,0:T(8,128)(2,1)} %coup.1) | copy-start | bytes 147460
  7.5 0.7 copy-start.6
  10.5 0.8 copy-start.1
  12.2 23.3 %copy-start.7 = (s32[2,5]{1,0:T(2,128)S(1)}, s32[2,5]{1,0:T(2,128)}, u32[]{:S(2)}) copy-start(s32[2,5]{1,0:T(2,128)} %cols.1) | copy-start | bytes 124
  12.2 23.3 %copy-start.8 = (s32[2]{0:T(128)S(1)}, s32[2]{0:T(128)}, u32[]{:S(2)}) copy-start(s32[2]{0:T(128)} %count.1) | copy-start | bytes 28
  12.2 12.8 %all-to-all-start = ((bf16[8,272,128]{2,1,0:T(8,128)(2,1)}), bf16[8,272,128]{2,1,0:T(8,128)(2,1)S(1)}, u32[]{:S(2)}, u32[]{:S(2)}) async-start(bf16[8,272,128]{2,1,0:T(8,128)(2,1)} %shard_map.115), calls=%async_computation | async-start | bytes 1114112 | tf_op jit(solution)/shard_map/all_to_all | solution.py:375
  15.9 22.3 %collective-permute-start.1 = (bf16[512,512]{1,0:T(8,128)(2,1)}, bf16[512,512]{1,0:T(8,128)(2,1)}, u32[]{:S(2)}, u32[]{:S(2)}) collective-permute-start(bf16[512,512]{1,0:T(8,128)(2,1)} %uown.1), channel_id=1, source_target_pairs={{1,0},{2,1},{3,2},{4,3},{5,4},{6,5},{7,6},{8,7},{9,8},{10,9},{11,1... | collective-permute-start | bytes 1572872 | tf_op jit(solution)/shard_map/ppermute | solution.py:349
  20.6 17.6 %collective-permute-start = (bf16[512,512]{1,0:T(8,128)(2,1)}, bf16[512,512]{1,0:T(8,128)(2,1)}, u32[]{:S(2)}, u32[]{:S(2)}) collective-permute-start(bf16[512,512]{1,0:T(8,128)(2,1)} %uown.1), channel_id=1, source_target_pairs={{0,1},{1,2},{2,3},{3,4},{4,5},{5,6},{6,7},{7,8},{8,9},{9,10},{10,1... | collective-permute-start | bytes 1572872 | tf_op jit(solution)/shard_map/ppermute | solution.py:349
  26.9 13.8 %all-to-all-start.1 = ((bf16[8,64,128]{2,1,0:T(8,128)(2,1)}), bf16[8,64,128]{2,1,0:T(8,128)(2,1)S(1)}, u32[]{:S(2)}, u32[]{:S(2)}) async-start(bf16[8,64,128]{2,1,0:T(8,128)(2,1)} %shard_map.116), calls=%async_computation.1 | async-start | bytes 262144 | tf_op jit(solution)/shard_map/all_to_all | solution.py:375
  35.5 1.7 %copy-start = (bf16[2,2,5,256,256]{4,3,2,1,0:T(8,128)(2,1)S(1)}, bf16[2,2,5,256,256]{4,3,2,1,0:T(8,128)(2,1)}, u32[]{:S(2)}) copy-start(bf16[2,2,5,256,256]{4,3,2,1,0:T(8,128)(2,1)} %tiles.1) | copy-start | bytes 7864324
  37.3 3.4 %copy-start.3 = (bf16[2,256,32]{1,2,0:T(8,128)(2,1)S(1)}, bf16[2,256,32]{1,2,0:T(8,128)(2,1)}, u32[]{:S(2)}) copy-start(bf16[2,256,32]{1,2,0:T(8,128)(2,1)} %param.15) | copy-start | bytes 98308
  37.3 3.4 %copy-start.4 = (bf16[2,256,32]{1,2,0:T(8,128)(2,1)S(1)}, bf16[2,256,32]{1,2,0:T(8,128)(2,1)}, u32[]{:S(2)}) copy-start(bf16[2,256,32]{1,2,0:T(8,128)(2,1)} %param.16) | copy-start | bytes 98308
  37.3 3.4 %copy-start.5 = (f32[2,512]{1,0:T(2,128)S(1)}, f32[2,512]{1,0:T(2,128)}, u32[]{:S(2)}) copy-start(f32[2,512]{1,0:T(2,128)} %diag.3) | copy-start | bytes 12292
  52.7 32.5 %collective-permute-start.4 = (bf16[1040,512]{1,0:T(8,128)(2,1)S(1)}, bf16[1040,512]{1,0:T(8,128)(2,1)S(1)}, u32[]{:S(2)}, u32[]{:S(2)}) collective-permute-start(bf16[1040,512]{1,0:T(8,128)(2,1)S(1)} %shard_map.118), channel_id=1, source_target_pairs={{1,0},{2,1},{3,2},{4,3},{5,4},{6,5},{7,6},{8,7},{9,8},{10,9},{11,1... | collective-permute-start | bytes 3194888 | tf_op jit(solution)/shard_map/ppermute | solution.py:349
  55.7 29.5 %collective-permute-start.3 = (bf16[1040,512]{1,0:T(8,128)(2,1)S(1)}, bf16[1040,512]{1,0:T(8,128)(2,1)S(1)}, u32[]{:S(2)}, u32[]{:S(2)}) collective-permute-start(bf16[1040,512]{1,0:T(8,128)(2,1)S(1)} %shard_map.118), channel_id=1, source_target_pairs={{0,1},{1,2},{2,3},{3,4},{4,5},{5,6},{6,7},{7,8},{8,9},{9,10},{10,1... | collective-permute-start | bytes 3194888 | tf_op jit(solution)/shard_map/ppermute | solution.py:349
  55.7 20.0 %collective-permute-start.5 = (bf16[8,80,128]{2,1,0:T(8,128)(2,1)S(1)}, bf16[8,80,128]{2,1,0:T(8,128)(2,1)S(1)}, u32[]{:S(2)}, u32[]{:S(2)}) collective-permute-start(bf16[8,80,128]{2,1,0:T(8,128)(2,1)S(1)} %all_to_all.20.after.refs_0_), channel_id=1, source_target_pairs={{0,8},{1,9},{2,10},{3,11},{4,12},{5,13},{6,14},{7,15},{8,0},{9,1},... | collective-permute-start | bytes 491528 | tf_op jit(solution)/shard_map/ppermute | solution.py:381

commit v8 on v7

--- a/solution.py
+++ b/solution.py
@@ -91,7 +91,7 @@
         out[2 * pair + 1] = second.astype(BF16)
 
 
-def pack_kernel(far_cols, coup, out):
+def pack_kernel(far_cols, coup, left, right, out):
     ops, blocks, far, rank, _ = coup.shape
     whole, rest = [], []
     for b in range(blocks):
@@ -106,8 +106,13 @@
     for b in range(blocks):
         for f in range(far):
             names = jnp.where(lane == b * far + f, far_cols[b, f].astype(F32), names)
+    mixed = [dot(right[b], left[b], ((1,), (1,))) for b in range(blocks)]
+    high = [m.astype(BF16) for m in mixed]
+    low = [(m - h.astype(F32)).astype(BF16) for m, h in zip(mixed, high)]
     out[...] = jnp.concatenate(
-        whole + [jnp.concatenate(rest, axis=1), names.astype(BF16)], axis=0
+        whole
+        + [jnp.concatenate(rest, axis=1), names.astype(BF16), jnp.concatenate(high + low, axis=1)],
+        axis=0,
     )
 
 
@@ -119,10 +124,6 @@
         out[s, 0:rows, :] = packed[...]
     for m, part in enumerate(parts):
         out[:, rows + m * rank:rows + (m + 1) * rank, :] = part[...]
-
-
-def copy_kernel(source, after, target):
-    target[...] = source[...]
 
 
 def coupling_rows(held, s, b, ops, rank):
@@ -154,7 +155,7 @@
 
 
 def held_part(held, m, ops, rank):
-    at = 3 * ops * rank + STATS + m * rank
+    at = 3 * ops * rank + STATS + (m + 1) * rank
     return held[:, at:at + rank, :].astype(F32)
 
 
@@ -162,15 +163,23 @@
     return pl.multiple_of(lax.rem(group[0] + (groups - m), groups) * step, step)
 
 
-def first_couple(ops, rank, far, cols, group, held, out, zs):
+def first_couple(ops, rank, far, cols, group, held, out, mixed, zs):
     step = SLICES * 2 * rank
     count = zs.shape[0] // step
     for m in range(count):
         at = group_at(group, m, count, step)
         zs[pl.ds(at, step), :] = spread_rows(held_part(held, m, ops, rank), rank)
+    at = 3 * ops * rank + STATS
+    first = lax.broadcasted_iota(jnp.int32, (rank, LANES), 1) < HALF
     for s in range(SLICES):
         c = [couple(cols, held, s, b, ops, rank, far, [zs]) for b in range(2)]
-        out[s] = halves(c[0], c[1])[0].astype(BF16)
+        c = halves(c[0], c[1])[0]
+        out[s] = c.astype(BF16)
+        for o in range(ops):
+            x = c[o * rank:(o + 1) * rank]
+            parts = [jnp.where(first, x, 0.0), jnp.where(first, 0.0, x)] * 2
+            parts = jnp.concatenate(parts, axis=0).astype(BF16)
+            mixed[s, o * rank:(o + 1) * rank, :] = dot(held[s, at:at + rank, :], parts)
 
 
 def take_coefs(cmsg, coef, rows):
@@ -205,11 +214,31 @@
     return jnp.concatenate([column] * (columns // LANES), axis=1)
 
 
-def image_kernel(w, low, own, high, diag, left, right, cmsg, vout, mout, image, coef):
+def pieces_of(values):
+    rows = []
+    for value in values:
+        rows += split3(value)
+    zero = jnp.zeros_like(rows[0])
+    return jnp.concatenate(rows + [zero] * (STATS - len(rows)), axis=0)
+
+
+def spread_pairs(out, rows, x, y):
+    for pair in range(SLICES // 2):
+        first, second = halves(chunk(x, pair), chunk(y, pair))
+        out[2 * pair, rows, :] = first.astype(BF16)
+        out[2 * pair + 1, rows, :] = second.astype(BF16)
+
+
+def ratio(inner, squares):
+    good = squares > 0
+    return jnp.where(good, inner / jnp.where(good, squares, 1.0), 0.0)
+
+
+def near_kernel(w, low, own, high, diag, right, c1, image, first, second, edge, msg):
     ops = image.shape[0]
     blocks, rank, size = right.shape
     rows, columns = own.shape
-    take_coefs(cmsg, coef, ops * rank)
+    body = ops * rank
     inner = [None] * ops
     squares = None
     for b in range(blocks):
@@ -218,126 +247,217 @@
         part = jnp.sum(ub * ub, axis=0, keepdims=True)
         squares = part if squares is None else squares + part
         for o in range(ops):
-            far = dot(left[b], coef[b, o * rank:(o + 1) * rank, :], ((0,), (0,)))
             value = (
                 product[o * size:(o + 1) * size]
                 + diagonal_of(diag, o, b, size, columns) * ub
-                + far.astype(BF16).astype(F32)
             )
             image[o, b * size:(b + 1) * size, :] = value
             part = jnp.sum(ub * value, axis=0, keepdims=True)
             inner[o] = part if inner[o] is None else inner[o] + part
-    stats = []
-    spreads = []
-    good = squares > 0
-    for o in range(ops):
-        shift = jnp.where(good, inner[o] / jnp.where(good, squares, 1.0), 0.0)
-        pieces = split3(shift)
-        stats += pieces
-        shift = pieces[0].astype(F32) + pieces[1].astype(F32) + pieces[2].astype(F32)
-        spread = None
+    shifts = [ratio(x, squares) for x in inner]
+    edges = pieces_of(shifts + [squares])
+    edge[...] = edges
+    first[rows:, :] = edges
+    edges = edges.astype(F32)
+    msg[:, 0:body, :] = c1[...]
+    for o, out in enumerate((first, second)):
+        shift = row3(edges, o)
         z = []
         for b in range(blocks):
             ub = own[b * size:(b + 1) * size, :].astype(F32)
             v = image[o, b * size:(b + 1) * size, :] - shift * ub
+            image[o, b * size:(b + 1) * size, :] = v
+            v = v.astype(BF16)
+            out[b * size:(b + 1) * size, :] = v
+            z.append(dot(right[b], v))
+        spread_pairs(msg, slice(body + o * rank, body + (o + 1) * rank), z[0], z[1])
+    spread_pairs(msg, slice(2 * body, 2 * body + STATS), edges, edges)
+
+
+def image_kernel(own, near, edge, left, got, mixed, after_low, after_high, vout, stats, cown, xmsg, image, coef):
+    ops = near.shape[0]
+    blocks, rank, size = left.shape
+    rows, columns = own.shape
+    body = ops * rank
+    for s in range(SLICES):
+        xmsg[s * body:(s + 1) * body, :] = (
+            got[s, body:2 * body, :].astype(F32) + mixed[s]
+        ).astype(BF16)
+        at = SLICES * body + s * STATS
+        xmsg[at:at + STATS, :] = got[s, 2 * body:2 * body + STATS, :]
+    take_coefs(got, coef, body)
+    edges = edge[...].astype(F32)
+    squares = row3(edges, ops)
+    shifts, spreads = [], []
+    for o in range(ops):
+        inner = None
+        for b in range(blocks):
+            cown[(o * blocks + b) * rank:(o * blocks + b + 1) * rank, :] = coef[
+                b, o * rank:(o + 1) * rank, :
+            ]
+            far = dot(left[b], coef[b, o * rank:(o + 1) * rank, :], ((0,), (0,)))
+            value = near[o, b * size:(b + 1) * size, :] + far.astype(BF16).astype(F32)
+            image[b * size:(b + 1) * size, :] = value
+            ub = own[b * size:(b + 1) * size, :].astype(F32)
+            part = jnp.sum(ub * value, axis=0, keepdims=True)
+            inner = part if inner is None else inner + part
+        before = row3(edges, o)
+        after = before + ratio(inner, squares)
+        shifts.append(after)
+        change = sum(x.astype(F32) for x in split3(after)) - before
+        spread = None
+        for b in range(blocks):
+            ub = own[b * size:(b + 1) * size, :].astype(F32)
+            v = image[b * size:(b + 1) * size, :] - change * ub
             part = jnp.sum(v * v, axis=0, keepdims=True)
             spread = part if spread is None else spread + part
-            v = v.astype(BF16)
-            vout[(o * blocks + b) * size:(o * blocks + b + 1) * size, :] = v
-            z.append(dot(right[b], v))
-        for pair in range(SLICES // 2):
-            first, second = halves(chunk(z[0], pair), chunk(z[1], pair))
-            mout[2 * pair, o * rank:(o + 1) * rank, :] = first.astype(BF16)
-            mout[2 * pair + 1, o * rank:(o + 1) * rank, :] = second.astype(BF16)
+            vout[(o * blocks + b) * size:(o * blocks + b + 1) * size, :] = v.astype(BF16)
         spreads.append(spread)
-    zero = jnp.zeros((1, columns), BF16)
-    vout[ops * rows:, :] = jnp.concatenate(stats + [zero] * (STATS - len(stats)), axis=0)
-    stats += split3(squares)
-    for spread in spreads:
-        stats += split3(spread)
-    stats = jnp.concatenate(stats + [zero] * (STATS - len(stats)), axis=0).astype(F32)
-    for pair in range(SLICES // 2):
-        part = chunk(stats, pair)
-        first, second = halves(part, part)
-        mout[2 * pair, ops * rank:ops * rank + STATS, :] = first.astype(BF16)
-        mout[2 * pair + 1, ops * rank:ops * rank + STATS, :] = second.astype(BF16)
+    every = pieces_of(shifts + [squares] + spreads)
+    stats[...] = every
+    at = SLICES * (body + STATS)
+    for j in range(columns // LANES):
+        xmsg[at + j * STATS:at + (j + 1) * STATS, :] = chunk(every, j)
+
+
+def bulk_kernel(near, cown, left, edge, after, out):
+    rows = near.shape[0]
+    blocks, rank, size = left.shape
+    at = rows + cown.shape[0]
+    out[0:rows, :] = near[...]
+    out[rows:at, :] = cown[...]
+    for b in range(blocks):
+        out[at:at + rank, b * size:(b + 1) * size] = left[b]
+    out[at + rank:, :] = edge[...]
 
 
 def second_couple(panels, ops, rank, far, cols, group, held, *refs):
-    msgs, (out, zs, st) = refs[:-3], refs[-3:]
-    count = len(msgs)
+    parts, (out, zs) = refs[:-2], refs[-2:]
+    count = len(parts)
     body = ops * rank
     step = SLICES * 2 * rank
-    for m, msg in enumerate(msgs):
-        at = group_at(group, m, count, SLICES)
-        st[pl.ds(at, SLICES)] = msg[:, body:body + STATS, :].astype(F32)
-    every = st[...]
-    squares = join3(every, ops)
-    scale_sq = jnp.sum(squares, axis=0, keepdims=True) / panels + EPSILON
-    reverse = 1.0 / jnp.sqrt(scale_sq)
-    heights, norms = [], []
-    for o in range(ops):
-        shift = join3(every, o)
-        height = jnp.sum(shift * squares, axis=0, keepdims=True) / panels / scale_sq
-        delta = shift - height
-        spread = join3(every, ops + 1 + o) + delta * delta * squares
-        norm = jnp.sqrt(jnp.sum(spread, axis=0, keepdims=True) / panels / scale_sq + EPSILON)
-        heights.append(height)
-        norms.append(norm)
-    for m, msg in enumerate(msgs):
-        at = group_at(group, m, count, step)
-        mine = msg[:, body:body + STATS, :].astype(F32)
+    at = SLICES * body
+    edges = [
+        x[at:at + SLICES * STATS, :].astype(F32).reshape(SLICES, STATS, LANES) for x in parts
+    ]
+    scale_sq = EPSILON
+    totals = [0.0] * ops
+    for x in edges:
+        squares = join3(x, ops)
+        scale_sq = scale_sq + jnp.sum(squares, axis=0, keepdims=True) / panels
+        for o in range(ops):
+            totals[o] = totals[o] + jnp.sum(join3(x, o) * squares, axis=0, keepdims=True) / panels
+    rough = pieces_of([total / scale_sq for total in totals])
+    for m, x in enumerate(parts):
+        row = group_at(group, m, count, step)
         base = held_part(held, m, ops, rank)
+        z = x[0:at, :].astype(F32).reshape(SLICES, body, LANES)
         for o in range(ops):
-            delta = join3(mine, o) - heights[o]
-            z = msg[:, o * rank:(o + 1) * rank, :].astype(F32) + delta[:, None, :] * base
-            z = z * (reverse / norms[o])[None]
-            zs[o, pl.ds(at, step), :] = spread_rows(z, rank)
-    rows = []
-    for row in heights + norms + [reverse]:
-        rows += split3(row)
-    rows += [jnp.zeros_like(rows[0])] * (STATS - len(rows))
-    rows = jnp.concatenate(rows, axis=0)
+            delta = join3(edges[m], o) - row3(rough.astype(F32), o)
+            value = z[:, o * rank:(o + 1) * rank, :] + delta[:, None, :] * base
+            zs[o, pl.ds(row, step), :] = spread_rows(value, rank)
+    start = at + SLICES * STATS
     for s in range(SLICES):
         c = [couple(cols, held, s, b, ops, rank, far, [zs.at[o] for o in range(ops)]) for b in range(2)]
         out[s, 0:body, :] = halves(c[0], c[1])[0].astype(BF16)
-        out[s, body:body + STATS, :] = rows
+        out[s, body:body + STATS, :] = rough
+        for m, x in enumerate(parts):
+            height = x.shape[0] - start
+            row = body + STATS + m * height
+            out[s, row:row + height, :] = x[start:, :]
 
 
 def final_kernel(
-    w, ulow, uown, uhigh, vlow, vown, vhigh, diag, left, cmsg, images, heights, norms, ext, coef, stat
+    panels,
+    group,
+    w,
+    ulow,
+    uown,
+    uhigh,
+    low0,
+    low1,
+    vown,
+    high0,
+    high1,
+    mine,
+    diag,
+    left,
+    cown,
+    cmsg,
+    images,
+    heights,
+    norms,
+    ext,
+    coef,
+    st,
 ):
     ops = images.shape[0]
     blocks, rank, size = left.shape
     rows, columns = uown.shape
     body = ops * rank
+    wide = columns // LANES
+    height = wide * STATS
+    count = (cmsg.shape[1] - body - STATS) // height
     take_coefs(cmsg, coef, body)
-    for pair in range(SLICES // 2):
-        stat[:, pair * LANES:(pair + 1) * LANES] = halves(
-            cmsg[2 * pair, body:body + STATS, :].astype(F32),
-            cmsg[2 * pair + 1, body:body + STATS, :].astype(F32),
-        )[0]
-    st = stat[...]
-    reverse = row3(st, 2 * ops)
+    for m in range(count):
+        at = group_at(group, m, count, SLICES)
+        for j in range(wide):
+            row = body + STATS + m * height + j * STATS
+            st[pl.ds(at, SLICES), :, j * LANES:(j + 1) * LANES] = cmsg[
+                :, row:row + STATS, :
+            ].astype(F32)
+    rough = jnp.concatenate(
+        [
+            halves(
+                cmsg[2 * pair, body:body + STATS, :].astype(F32),
+                cmsg[2 * pair + 1, body:body + STATS, :].astype(F32),
+            )[0]
+            for pair in range(wide)
+        ],
+        axis=1,
+    )
+    every = st[...]
+    squares = join3(every, ops)
+    scale_sq = jnp.sum(squares, axis=0, keepdims=True) / panels + EPSILON
+    reverse = 1.0 / jnp.sqrt(scale_sq)
     for o in range(ops):
-        height = row3(st, o)
-        norm = row3(st, ops + o)
-        heights[o:o + 1, :] = height
+        shift = join3(every, o)
+        high = jnp.sum(shift * squares, axis=0, keepdims=True) / panels / scale_sq
+        delta = shift - high
+        spread = join3(every, ops + 1 + o) + delta * delta * squares
+        norm = jnp.sqrt(jnp.sum(spread, axis=0, keepdims=True) / panels / scale_sq + EPSILON)
+        heights[o:o + 1, :] = high
         norms[o:o + 1, :] = norm
         factor = reverse / norm
-        for at, (u, v) in enumerate(((ulow, vlow), (uown, vown), (uhigh, vhigh))):
-            shift = row3(v[ops * rows:, :].astype(F32), o)
-            change = (shift - height) * factor
-            value = v[o * rows:(o + 1) * rows, :].astype(F32) * factor + u[...].astype(F32) * change
-            ext[o, at] = value.astype(BF16)
+        for at, u, v, more in ((0, ulow, (low0, low1)[o], low1), (2, uhigh, (high0, high1)[o], high1)):
+            start = rows + ops * blocks * rank
+            edges = more[start + rank:, :].astype(F32)
+            change = (row3(edges, o) - high) * factor
+            for b in range(blocks):
+                row = rows + (o * blocks + b) * rank
+                far = dot(
+                    more[start:start + rank, b * size:(b + 1) * size],
+                    more[row:row + rank, :],
+                    ((0,), (0,)),
+                ).astype(BF16).astype(F32)
+                here = slice(b * size, (b + 1) * size)
+                value = (v[here, :].astype(F32) + far) * factor + u[here, :].astype(F32) * change
+                ext[at, here, :] = value.astype(BF16)
+        change = (row3(mine[...].astype(F32), o) - high) * factor
+        value = vown[o * rows:(o + 1) * rows, :].astype(F32) * factor
+        ext[1] = (value + uown[...].astype(F32) * change).astype(BF16)
+        offset = high - row3(rough, o)
         for b in range(blocks):
-            parts = [ext.at[o, at] for at in range(3)]
+            parts = [ext.at[at] for at in range(3)]
             product = near_product(w.at[b, o * size:(o + 1) * size], parts, b, blocks, size)
-            far = dot(left[b], coef[b, o * rank:(o + 1) * rank, :], ((0,), (0,)))
-            mine = ext[o, 1, b * size:(b + 1) * size, :].astype(F32)
+            row = (o * blocks + b) * rank
+            c = coef[b, o * rank:(o + 1) * rank, :].astype(F32)
+            c = (c - offset * cown[row:row + rank, :].astype(F32)) * factor
+            far = dot(left[b], c.astype(BF16), ((0,), (0,)))
+            own = ext[1, b * size:(b + 1) * size, :].astype(F32)
             images[o, b * size:(b + 1) * size, :] = (
                 product
-                + diagonal_of(diag, o, b, size, columns) * mine
+                + diagonal_of(diag, o, b, size, columns) * own
                 + far.astype(BF16).astype(F32)
             )
 
@@ -393,13 +513,12 @@
     )
     z1 = across(z1)
     shared = (blocks + 1) * body
-    packed = call(pack_kernel, sds((shared + STATS, LANES), BF16), [SMEM, VMEM])(
-        far_cols, couplings
+    lead = shared + STATS + rank
+    packed = call(pack_kernel, sds((lead, LANES), BF16), [SMEM, VMEM, VMEM, VMEM])(
+        far_cols, couplings, left, right
     )
     held = call(
-        share_kernel,
-        sds((SLICES, shared + STATS + count * rank, LANES), BF16),
-        [VMEM] * (1 + count),
+        share_kernel, sds((SLICES, lead + count * rank, LANES), BF16), [VMEM] * (1 + count)
     )(packed, *z1)
     held = exchange(held)
     cols = held[:, shared, :blocks * far].astype(jnp.int32).reshape(-1)
@@ -411,53 +530,86 @@
         micros=2.5,
     )(near_cols, near_count, row0, near_tiles)
 
-    c1 = call(
+    c1, mixed = call(
         functools.partial(first_couple, ops, rank, far),
-        sds((SLICES, body, LANES), BF16),
+        [sds((SLICES, body, LANES), BF16), sds((SLICES, body, LANES), F32)],
         [SMEM, SMEM, VMEM],
         [pltpu.VMEM((n * blocks * rank, LANES), BF16)],
     )(cols, group, held)
-    c1 = exchange(c1)
-
-    v, msg = call(
+
+    image, first, second, edge, msg = call(
+        near_kernel,
+        [
+            sds((ops, rows, columns), F32),
+            sds((rows + STATS, columns), BF16),
+            sds((rows, columns), BF16),
+            sds((STATS, columns), BF16),
+            sds((SLICES, 2 * body + STATS, LANES), BF16),
+        ],
+        [VMEM] * 7,
+        micros=4.0,
+    )(w, low, sources, high, self_terms, right, c1)
+    low0, high0 = ring(first)
+    got = exchange(msg)
+
+    own_rows = ops * blocks * rank
+    v, stats, cown, xmsg = call(
         image_kernel,
-        [sds((ops * rows + STATS, columns), BF16), sds((SLICES, body + STATS, LANES), BF16)],
-        [VMEM] * 8,
         [
-            pltpu.VMEM((ops, rows, columns), F32),
+            sds((ops * rows, columns), BF16),
+            sds((STATS, columns), BF16),
+            sds((own_rows, columns), BF16),
+            sds((SLICES * (body + STATS) + columns // LANES * STATS, LANES), BF16),
+        ],
+        [VMEM] * 6 + [pl.BlockSpec(memory_space=pl.ANY)] * 2,
+        [pltpu.VMEM((rows, columns), F32), pltpu.VMEM((blocks, body, columns), BF16)],
+        micros=3.0,
+    )(sources, image, edge, left, got, mixed, low0, high0)
+    parts = across(xmsg)
+
+    bulk = call(
+        bulk_kernel,
+        sds((rows + own_rows + rank + STATS, columns), BF16),
+        [VMEM] * 4 + [pl.BlockSpec(memory_space=pl.ANY)],
+    )(second, cown, left, edge, parts[-1])
+    low1, high1 = ring(bulk)
+
+    panels = all_blocks * size
+    c2 = call(
+        functools.partial(second_couple, panels, ops, rank, far),
+        sds((SLICES, body + STATS + count * columns // LANES * STATS, LANES), BF16),
+        [SMEM, SMEM] + [VMEM] * (1 + count),
+        [pltpu.VMEM((ops, n * blocks * rank, LANES), BF16)],
+    )(cols, group, held, *parts)
+    c2 = exchange(c2)
+
+    images, heights, norms = call(
+        functools.partial(final_kernel, panels),
+        [sds((ops, rows, columns), F32), sds((ops, columns), F32), sds((ops, columns), F32)],
+        [SMEM] + [VMEM] * 14,
+        [
+            pltpu.VMEM((3, rows, columns), BF16),
             pltpu.VMEM((blocks, body, columns), BF16),
+            pltpu.VMEM((n, STATS, columns), F32),
         ],
-        micros=4.0,
-    )(w, low, sources, high, self_terms, left, right, c1)
-    msg = exchange(msg)
-    msgs = across(msg)
-    bulk = call(
-        copy_kernel, sds(v.shape, BF16), [VMEM, pl.BlockSpec(memory_space=pl.ANY)], micros=8.0
-    )(v, msg)
-    vlow, vhigh = ring(bulk)
-
-    c2 = call(
-        functools.partial(second_couple, all_blocks * size, ops, rank, far),
-        sds((SLICES, body + STATS, LANES), BF16),
-        [SMEM, SMEM] + [VMEM] * (1 + count),
-        [
-            pltpu.VMEM((ops, n * blocks * rank, LANES), BF16),
-            pltpu.VMEM((n, STATS, LANES), F32),
-        ],
-    )(cols, group, held, *msgs)
-    c2 = exchange(c2)
-
-    images, heights, norms = call(
-        final_kernel,
-        [sds((ops, rows, columns), F32), sds((ops, columns), F32), sds((ops, columns), F32)],
-        [VMEM] * 10,
-        [
-            pltpu.VMEM((ops, 3, rows, columns), BF16),
-            pltpu.VMEM((blocks, body, columns), BF16),
-            pltpu.VMEM((STATS, columns), F32),
-        ],
-        micros=4.0,
-    )(w, low, sources, high, vlow, v, vhigh, self_terms, left, c2)
+        micros=5.0,
+    )(
+        group,
+        w,
+        low,
+        sources,
+        high,
+        low0,
+        low1,
+        v,
+        high0,
+        high1,
+        stats,
+        self_terms,
+        left,
+        cown,
+        c2,
+    )
     return images, heights, norms
 
 

time: 90.8 us -> 117 us (1.29)
  the two profiles are of different devices: /device:TPU:0 before, /device:TPU:1 now
where the time goes in v8:
time: 117 us; the launch traced here: 116 us
  waiting for transfers between devices  41.1 us (35%)
  Pallas kernels  20.9 us (18%)
  starting transfers between devices  19.2 us (16%)
  local copies, waits for them, and re-layouts  16.7 us (14%)
  blocking collectives  16.2 us (14%)
    ppermute x3, waiting for transfers between devices, ring(): lax.ppermute(block, 'store', backward)  26.7 us
    unnamed x50, local copies, waits for them, and re-layouts  16.6 us
    all_to_all x1, blocking collectives, exchange(): lax.all_to_all(x, 'store', 0, 0, axis_index_groups=groups, tiled=True)  16.2 us
    ppermute x2, waiting for transfers between devices, across(): parts.append(lax.ppermute(x, 'store', pairs))  9.66 us
    all_to_all x2, starting transfers between devices, exchange(): lax.all_to_all(x, 'store', 0, 0, axis_index_groups=groups, tiled=True)  9.49 us
    pallas_call x1, Pallas kernels, shards(): call(functools.partial(final_kernel, panels), [sds((ops, rows, columns),...  6.08 us
    ppermute x3, starting transfers between devices, ring(): lax.ppermute(block, 'store', forward)  4.9 us
    all_to_all x2, waiting for transfers between devices, exchange(): lax.all_to_all(x, 'store', 0, 0, axis_index_groups=groups, tiled=True)  4.75 us
  transfers between devices with their start and end apart: 10, of which 4 were waited for; matrix products, arithmetic and copies ran while one was open for 1% of the time, Pallas kernels for 4%

profile of v8, /device:TPU:1, one launch (start us, length us, event | category | flops | bytes accessed | tf_op | source)
XLA Modules:
  0.0 115.6 jit_solution(4141202658733637494)
XLA Ops:
  0.6 0.0 copy-start
  0.6 0.0 copy-start.24
  0.7 0.0 copy-start.23
  0.7 2.0 %shard_map.114.refs_0_ = bf16[8,32,128]{2,1,0:T(8,128)(2,1)} custom-call(bf16[512,512]{1,0:T(8,128)(2,1)} %uown.1, bf16[2,32,256]{2,1,0:T(8,128)(2,1)} %bitcast.8), custom_call_target="tpu_custom_call" | custom-call | bytes 3690000 | tf_op jit(solution)/shard_map/pallas_call | solution.py:511
  2.7 3.1 %collective-permute-start.2 = (bf16[8,32,128]{2,1,0:T(8,128)(2,1)}, bf16[8,32,128]{2,1,0:T(8,128)(2,1)S(1)}, u32[]{:S(2)}, u32[]{:S(2)}) collective-permute-start(bf16[8,32,128]{2,1,0:T(8,128)(2,1)} %shard_map.114.refs_0_), channel_id=1, source_target_pairs={{0,8},{1,9},{2,10},{3,11},{4,12},{5,13},{6,14},{7,15},{8,0},{9,1},... | collective-permute-start | bytes 196616 | tf_op jit(solution)/shard_map/ppermute | solution.py:501
  5.8 0.8 copy-done.13
  6.6 0.8 copy-done.17
  7.3 0.9 copy-done.20
  8.2 0.7 copy-done.22
  8.9 0.7 shard_map.113.packed
  9.7 0.0 collective-permute-done.2.refs_1_
  9.7 0.0 copy-start.19
  9.7 0.8 copy-done.19
  10.5 0.9 shard_map.115
  11.4 5.0 %all-to-all-start = ((bf16[8,304,128]{2,1,0:T(8,128)(2,1)}), bf16[8,304,128]{2,1,0:T(8,128)(2,1)}, u32[]{:S(2)}, u32[]{:S(2)}) async-start(bf16[8,304,128]{2,1,0:T(8,128)(2,1)} %shard_map.115), calls=%async_computation | async-start | bytes 1245184 | tf_op jit(solution)/shard_map/all_to_all | solution.py:495
  16.5 0.0 copy-done
  16.5 0.2 collective-permute-start.1
  16.6 1.6 %collective-permute-start = (bf16[512,512]{1,0:T(8,128)(2,1)S(1)}, bf16[512,512]{1,0:T(8,128)(2,1)}, u32[]{:S(2)}, u32[]{:S(2)}) collective-permute-start(bf16[512,512]{1,0:T(8,128)(2,1)S(1)} %copy-done), channel_id=1, source_target_pairs={{0,1},{1,2},{2,3},{3,4},{4,5},{5,6},{6,7},{7,8},{8,9},{9,10},{10,1... | collective-permute-start | bytes 1572872 | tf_op jit(solution)/shard_map/ppermute | solution.py:469
  18.2 0.0 copy-done.24
  18.2 0.0 copy-done.23
  18.2 1.7 %copy-done.1 = bf16[2,2,5,256,256]{4,3,2,1,0:T(8,128)(2,1)S(1)} copy-done((bf16[2,2,5,256,256]{4,3,2,1,0:T(8,128)(2,1)S(1)}, bf16[2,2,5,256,256]{4,3,2,1,0:T(8,128)(2,1)}, u32[]{:S(2)}) %copy-start.1) | copy-done | bytes 2621464
  20.0 0.9 shard_map.112.w
  20.9 4.8 %all-to-all-done.held = bf16[8,304,128]{2,1,0:T(8,128)(2,1)} async-done(((bf16[8,304,128]{2,1,0:T(8,128)(2,1)}), bf16[8,304,128]{2,1,0:T(8,128)(2,1)}, u32[]{:S(2)}, u32[]{:S(2)}) %all-to-all-start) | async-done | bytes 622624 | tf_op jit(solution)/shard_map/all_to_all | solution.py:495
  25.6 0.7 fusion
  26.3 0.1 reshape.18.cols
  26.4 3.2 %shard_map.116 = (bf16[8,64,128]{2,1,0:T(8,128)(2,1)S(1)}, f32[8,64,128]{2,1,0:T(8,128)S(1)}) custom-call(s32[96]{0:T(128)S(1)} %reshape.18.cols, s32[1]{0:T(128)} %bitcast.group, bf16[8,304,128]{2,1,0:T(8,128)(2,1)} %all-to-all-done.held), custom_call_target="tpu_custom_call" | custom-call | bytes 3690000 | tf_op jit(solution)/shard_map/pallas_call | solution.py:533
  29.6 7.4 %collective-permute-done.1.high.uhigh = bf16[512,512]{1,0:T(8,128)(2,1)} collective-permute-done((bf16[512,512]{1,0:T(8,128)(2,1)S(1)}, bf16[512,512]{1,0:T(8,128)(2,1)}, u32[]{:S(2)}, u32[]{:S(2)}) %collective-permute-start.1) | collective-permute-done | bytes 524320 | tf_op jit(solution)/shard_map/ppermute | solution.py:469
  37.0 0.0 collective-permute-done.low.ulow
  37.0 0.0 copy-done.18
  37.0 0.0 copy-done.21
  37.0 3.7 %shard_map.117 = (f32[2,512,512]{2,1,0:T(8,128)S(1)}, bf16[528,512]{1,0:T(8,128)(2,1)S(1)}, bf16[512,512]{1,0:T(8,128)(2,1)S(1)}, bf16[16,512]{1,0:T(8,128)(2,1)S(1)}, bf16[8,144,128]{2,1,0:T(8,128)(2,1)S(1)}) custom-call(bf16[2,512,1280]{2,1,0:T(8,128)(2,1)S(1)} %shard_map.112.w, bf16[512,512]{1,0:T(8,128)(2,1)} %collective-permute-done.low.ulow, ...), custom_call_target="tpu_custom_call" | custom-call | bytes 14760000 | tf_op jit(solution)/shard_map/pallas_call | solution.py:540
  40.7 0.0 copy-start.15
  40.7 0.1 collective-permute-start.4
  40.8 1.7 %collective-permute-start.3 = (bf16[528,512]{1,0:T(8,128)(2,1)S(1)}, bf16[528,512]{1,0:T(8,128)(2,1)S(1)}, u32[]{:S(2)}, u32[]{:S(2)}) collective-permute-start(bf16[528,512]{1,0:T(8,128)(2,1)S(1)} %get-tuple-element.15), channel_id=1, source_target_pairs={{0,1},{1,2},{2,3},{3,4},{4,5},{5,6},{6,7},{7,8},{8,9},{9,10},{10,1... | collective-permute-start | bytes 1622024 | tf_op jit(solution)/shard_map/ppermute | solution.py:469
  42.5 16.2 %all_to_all.15.got = bf16[8,144,128]{2,1,0:T(8,128)(2,1)S(1)} all-to-all(bf16[8,144,128]{2,1,0:T(8,128)(2,1)S(1)} %get-tuple-element.19), channel_id=1, replica_groups={{0,1,2,3,4,5,6,7},{8,9,10,11,12,13,14,15},{16,17,18,19,20,21,22,23},{24..., dimensions={0} | all-to-all | bytes 589824 | tf_op jit(solution)/shard_map/all_to_all | solution.py:495
  58.7 0.0 collective-permute-done.4.after_high.high0
  58.7 0.0 collective-permute-done.3.after_low.low0
  58.7 0.0 copy-done.15
  58.8 0.0 copy-done.14
  58.8 1.2 %shard_map.118 = (bf16[1024,512]{1,0:T(8,128)(2,1)S(1)}, bf16[16,512]{1,0:T(8,128)(2,1)S(1)}, bf16[128,512]{1,0:T(8,128)(2,1)S(1)}, bf16[704,128]{1,0:T(8,128)(2,1)S(1)}) custom-call(bf16[512,512]{1,0:T(8,128)(2,1)S(1)} %copy-done, f32[2,512,512]{2,1,0:T(8,128)S(1)} %get-tuple-element.17.near, bf16[16,512]{1,0:T(8,128)(2,1)S(1)} %get-tuple-element.18.edge, ...), custom_call_target="tpu_custom_call" | custom-call | bytes 11070000 | tf_op jit(solution)/shard_map/pallas_call | solution.py:556
  60.0 0.0 copy-done.4
  60.0 0.0 copy-start.2
  60.0 0.8 copy-done.2
  60.8 1.0 copy-done.7
  61.8 1.2 %collective-permute-start.5 = (bf16[704,128]{1,0:T(8,128)(2,1)S(1)}, bf16[704,128]{1,0:T(8,128)(2,1)S(1)}, u32[]{:S(2)}, u32[]{:S(2)}) collective-permute-start(bf16[704,128]{1,0:T(8,128)(2,1)S(1)} %get-tuple-element.22.refs_0_), channel_id=1, source_target_pairs={{0,8},{1,9},{2,10},{3,11},{4,12},{5,13},{6,14},{7,15},{8,0},{9,1},... | collective-permute-start | bytes 540680 | tf_op jit(solution)/shard_map/ppermute | solution.py:501
  63.0 9.7 %collective-permute-done.5.after.refs_1_ = bf16[704,128]{1,0:T(8,128)(2,1)S(1)} collective-permute-done((bf16[704,128]{1,0:T(8,128)(2,1)S(1)}, bf16[704,128]{1,0:T(8,128)(2,1)S(1)}, u32[]{:S(2)}, u32[]{:S(2)}) %collective-permute-start.5) | collective-permute-done | bytes 180256 | tf_op jit(solution)/shard_map/ppermute | solution.py:501
  72.6 2.1 %shard_map.120 = bf16[8,208,128]{2,1,0:T(8,128)(2,1)S(1)} custom-call(s32[96]{0:T(128)S(1)} %reshape.18.cols, s32[1]{0:T(128)} %bitcast.group, bf16[8,304,128]{2,1,0:T(8,128)(2,1)} %all-to-all-done.held, bf16[704,128]{1,0:T(8,128)(2,1)S(1)} %get-tuple-element.22.refs_0_, bf16[704,128]{1,0:T(8,128)(2,1)S(1)} %collective-permute-done.5.after.refs_1_), custom_call_target="tpu_custom_call" | custom-call | bytes 3690000 | tf_op jit(solution)/shard_map/pallas_call | solution.py:578
  74.7 0.0 copy-start.6
  74.8 0.7 copy-done.6
  75.5 4.5 %all-to-all-start.2 = ((bf16[8,208,128]{2,1,0:T(8,128)(2,1)}), bf16[8,208,128]{2,1,0:T(8,128)(2,1)}, u32[]{:S(2)}, u32[]{:S(2)}) async-start(bf16[8,208,128]{2,1,0:T(8,128)(2,1)} %copy-done.6), calls=%async_computation.2 | async-start | bytes 851968 | tf_op jit(solution)/shard_map/all_to_all | solution.py:495
  80.0 1.0 copy-done.16
  81.1 0.2 collective-permute-start.7
  81.2 1.6 %collective-permute-start.6 = (bf16[688,512]{1,0:T(8,128)(2,1)S(1)}, bf16[688,512]{1,0:T(8,128)(2,1)S(1)}, u32[]{:S(2)}, u32[]{:S(2)}) collective-permute-start(bf16[688,512]{1,0:T(8,128)(2,1)S(1)} %shard_map.119), channel_id=1, source_target_pairs={{0,1},{1,2},{2,3},{3,4},{4,5},{5,6},{6,7},{7,8},{8,9},{9,10},{10,1... | collective-permute-start | bytes 2113544 | tf_op jit(solution)/shard_map/ppermute | solution.py:469
  82.9 19.3 %collective-permute-done.7.high1 = bf16[688,512]{1,0:T(8,128)(2,1)S(1)} collective-permute-done((bf16[688,512]{1,0:T(8,128)(2,1)S(1)}, bf16[688,512]{1,0:T(8,128)(2,1)S(1)}, u32[]{:S(2)}, u32[]{:S(2)}) %collective-permute-start.7) | collective-permute-done | bytes 704544 | tf_op jit(solution)/shard_map/ppermute | solution.py:469
  102.2 0.9 copy-done.9
  103.1 0.0 collective-permute-done.6.low1
  103.1 0.9 copy-done.11
  103.9 0.0 all-to-all-done.2.cmsg
  103.9 1.0 copy-done.3
  105.0 1.0 copy-done.5
  106.0 1.2 %copy-done.8 = bf16[1024,512]{1,0:T(8,128)(2,1)S(1)} copy-done((bf16[1024,512]{1,0:T(8,128)(2,1)S(1)}, bf16[1024,512]{1,0:T(8,128)(2,1)}, u32[]{:S(2)}) %copy-start.8) | copy-done | bytes 1048600
  107.3 1.1 copy-done.10
  108.4 1.1 copy-done.12
  109.5 6.1 %shard_map.121 = (f32[2,512,512]{2,1,0:T(8,128)}, f32[2,512]{1,0:T(2,128)}, f32[2,512]{1,0:T(2,128)}) custom-call(s32[1]{0:T(128)} %bitcast.group, bf16[2,512,1280]{2,1,0:T(8,128)(2,1)S(1)} %shard_map.112.w, bf16[512,512]{1,0:T(8,128)(2,1)} %collective-permute-done.low.ulow, bf16[512,512]{1,0:T(8,128)(2,1)S(1)} %copy-done, ...), custom_call_target="tpu_custom_call" | custom-call | bytes 18450000 | tf_op jit(solution)/shard_map/pallas_call | solution.py:586
  (19 shorter events, 0.1 us)
Async XLA Ops:
  0.6 15.8 %copy-start = (bf16[512,512]{1,0:T(8,128)(2,1)S(1)}, bf16[512,512]{1,0:T(8,128)(2,1)}, u32[]{:S(2)}) copy-start(bf16[512,512]{1,0:T(8,128)(2,1)} %uown.1) | copy-start | bytes 1572868
  0.6 17.6 %copy-start.24 = (s32[2]{0:T(128)S(1)}, s32[2]{0:T(128)}, u32[]{:S(2)}) copy-start(s32[2]{0:T(128)} %count.1) | copy-start | bytes 28
  0.7 17.6 %copy-start.23 = (s32[2,5]{1,0:T(2,128)S(1)}, s32[2,5]{1,0:T(2,128)}, u32[]{:S(2)}) copy-start(s32[2,5]{1,0:T(2,128)} %cols.1) | copy-start | bytes 124
  2.7 7.0 %collective-permute-start.2 = (bf16[8,32,128]{2,1,0:T(8,128)(2,1)}, bf16[8,32,128]{2,1,0:T(8,128)(2,1)S(1)}, u32[]{:S(2)}, u32[]{:S(2)}) collective-permute-start(bf16[8,32,128]{2,1,0:T(8,128)(2,1)} %shard_map.114.refs_0_), channel_id=1, source_target_pairs={{0,8},{1,9},{2,10},{3,11},{4,12},{5,13},{6,14},{7,15},{8,0},{9,1},... | collective-permute-start | bytes 196616 | tf_op jit(solution)/shard_map/ppermute | solution.py:501
  5.8 0.8 copy-start.13
  6.6 0.8 copy-start.17
  7.3 0.9 copy-start.20
  8.2 0.7 copy-start.22
  9.7 0.8 copy-start.19
  11.4 14.2 %all-to-all-start = ((bf16[8,304,128]{2,1,0:T(8,128)(2,1)}), bf16[8,304,128]{2,1,0:T(8,128)(2,1)}, u32[]{:S(2)}, u32[]{:S(2)}) async-start(bf16[8,304,128]{2,1,0:T(8,128)(2,1)} %shard_map.115), calls=%async_computation | async-start | bytes 1245184 | tf_op jit(solution)/shard_map/all_to_all | solution.py:495
  16.5 20.6 %collective-permute-start.1 = (bf16[512,512]{1,0:T(8,128)(2,1)S(1)}, bf16[512,512]{1,0:T(8,128)(2,1)}, u32[]{:S(2)}, u32[]{:S(2)}) collective-permute-start(bf16[512,512]{1,0:T(8,128)(2,1)S(1)} %copy-done), channel_id=1, source_target_pairs={{1,0},{2,1},{3,2},{4,3},{5,4},{6,5},{7,6},{8,7},{9,8},{10,9},{11,1... | collective-permute-start | bytes 1572872 | tf_op jit(solution)/shard_map/ppermute | solution.py:469
  16.6 20.4 %collective-permute-start = (bf16[512,512]{1,0:T(8,128)(2,1)S(1)}, bf16[512,512]{1,0:T(8,128)(2,1)}, u32[]{:S(2)}, u32[]{:S(2)}) collective-permute-start(bf16[512,512]{1,0:T(8,128)(2,1)S(1)} %copy-done), channel_id=1, source_target_pairs={{0,1},{1,2},{2,3},{3,4},{4,5},{5,6},{6,7},{7,8},{8,9},{9,10},{10,1... | collective-permute-start | bytes 1572872 | tf_op jit(solution)/shard_map/ppermute | solution.py:469
  18.2 1.7 %copy-start.1 = (bf16[2,2,5,256,256]{4,3,2,1,0:T(8,128)(2,1)S(1)}, bf16[2,2,5,256,256]{4,3,2,1,0:T(8,128)(2,1)}, u32[]{:S(2)}) copy-start(bf16[2,2,5,256,256]{4,3,2,1,0:T(8,128)(2,1)} %tiles.1) | copy-start | bytes 7864324
  19.9 17.1 %copy-start.18 = (bf16[2,256,32]{1,2,0:T(8,128)(2,1)S(1)}, bf16[2,256,32]{1,2,0:T(8,128)(2,1)}, u32[]{:S(2)}) copy-start(bf16[2,256,32]{1,2,0:T(8,128)(2,1)} %param.16) | copy-start | bytes 98308
  19.9 17.1 %copy-start.21 = (f32[2,512]{1,0:T(2,128)S(1)}, f32[2,512]{1,0:T(2,128)}, u32[]{:S(2)}) copy-start(f32[2,512]{1,0:T(2,128)} %diag.3) | copy-start | bytes 12292
  29.6 29.1 %copy-start.14 = (bf16[2,256,32]{1,2,0:T(8,128)(2,1)S(1)}, bf16[2,256,32]{1,2,0:T(8,128)(2,1)}, u32[]{:S(2)}) copy-start(bf16[2,256,32]{1,2,0:T(8,128)(2,1)} %param.15) | copy-start | bytes 98308
  40.7 18.0 %copy-start.15 = (bf16[512,512]{1,0:T(8,128)(2,1)}, bf16[512,512]{1,0:T(8,128)(2,1)S(1)}, u32[]{:S(2)}) copy-start(bf16[512,512]{1,0:T(8,128)(2,1)S(1)} %get-tuple-element.16.near) | copy-start | bytes 1572868
  40.7 18.0 %collective-permute-start.4 = (bf16[528,512]{1,0:T(8,128)(2,1)S(1)}, bf16[528,512]{1,0:T(8,128)(2,1)S(1)}, u32[]{:S(2)}, u32[]{:S(2)}) collective-permute-start(bf16[528,512]{1,0:T(8,128)(2,1)S(1)} %get-tuple-element.15), channel_id=1, source_target_pairs={{1,0},{2,1},{3,2},{4,3},{5,4},{6,5},{7,6},{8,7},{9,8},{10,9},{11,1... | collective-permute-start | bytes 1622024 | tf_op jit(solution)/shard_map/ppermute | solution.py:469
  40.8 17.9 %collective-permute-start.3 = (bf16[528,512]{1,0:T(8,128)(2,1)S(1)}, bf16[528,512]{1,0:T(8,128)(2,1)S(1)}, u32[]{:S(2)}, u32[]{:S(2)}) collective-permute-start(bf16[528,512]{1,0:T(8,128)(2,1)S(1)} %get-tuple-element.15), channel_id=1, source_target_pairs={{0,1},{1,2},{2,3},{3,4},{4,5},{5,6},{6,7},{7,8},{8,9},{9,10},{10,1... | collective-permute-start | bytes 1622024 | tf_op jit(solution)/shard_map/ppermute | solution.py:469
  58.7 1.2 %copy-start.4 = (bf16[528,512]{1,0:T(8,128)(2,1)}, bf16[528,512]{1,0:T(8,128)(2,1)S(1)}, u32[]{:S(2)}) copy-start(bf16[528,512]{1,0:T(8,128)(2,1)S(1)} %collective-permute-done.3.after_low.low0) | copy-start | bytes 1622020
  60.0 0.8 copy-start.2
  60.8 1.0 copy-start.7
  61.8 10.9 %collective-permute-start.5 = (bf16[704,128]{1,0:T(8,128)(2,1)S(1)}, bf16[704,128]{1,0:T(8,128)(2,1)S(1)}, u32[]{:S(2)}, u32[]{:S(2)}) collective-permute-start(bf16[704,128]{1,0:T(8,128)(2,1)S(1)} %get-tuple-element.22.refs_0_), channel_id=1, source_target_pairs={{0,8},{1,9},{2,10},{3,11},{4,12},{5,13},{6,14},{7,15},{8,0},{9,1},... | collective-permute-start | bytes 540680 | tf_op jit(solution)/shard_map/ppermute | solution.py:501
  74.7 0.8 copy-start.6
  75.5 28.4 %all-to-all-start.2 = ((bf16[8,208,128]{2,1,0:T(8,128)(2,1)}), bf16[8,208,128]{2,1,0:T(8,128)(2,1)}, u32[]{:S(2)}, u32[]{:S(2)}) async-start(bf16[8,208,128]{2,1,0:T(8,128)(2,1)} %copy-done.6), calls=%async_computation.2 | async-start | bytes 851968 | tf_op jit(solution)/shard_map/all_to_all | solution.py:495
  80.0 1.0 copy-start.16
  81.1 21.1 %collective-permute-start.7 = (bf16[688,512]{1,0:T(8,128)(2,1)S(1)}, bf16[688,512]{1,0:T(8,128)(2,1)S(1)}, u32[]{:S(2)}, u32[]{:S(2)}) collective-permute-start(bf16[688,512]{1,0:T(8,128)(2,1)S(1)} %shard_map.119), channel_id=1, source_target_pairs={{1,0},{2,1},{3,2},{4,3},{5,4},{6,5},{7,6},{8,7},{9,8},{10,9},{11,1... | collective-permute-start | bytes 2113544 | tf_op jit(solution)/shard_map/ppermute | solution.py:469
  81.2 21.8 %collective-permute-start.6 = (bf16[688,512]{1,0:T(8,128)(2,1)S(1)}, bf16[688,512]{1,0:T(8,128)(2,1)S(1)}, u32[]{:S(2)}, u32[]{:S(2)}) collective-permute-start(bf16[688,512]{1,0:T(8,128)(2,1)S(1)} %shard_map.119), channel_id=1, source_target_pairs={{0,1},{1,2},{2,3},{3,4},{4,5},{5,6},{6,7},{7,8},{8,9},{9,10},{10,1... | collective-permute-start | bytes 2113544 | tf_op jit(solution)/shard_map/ppermute | solution.py:469
  102.2 0.9 copy-start.9
  103.1 0.9 copy-start.11
  103.9 1.0 copy-start.3
  105.0 1.0 copy-start.5
  106.0 1.2 %copy-start.8 = (bf16[1024,512]{1,0:T(8,128)(2,1)S(1)}, bf16[1024,512]{1,0:T(8,128)(2,1)}, u32[]{:S(2)}) copy-start(bf16[1024,512]{1,0:T(8,128)(2,1)} %copy-done.7) | copy-start | bytes 3145732
  107.3 1.1 copy-start.10
  108.4 1.1 copy-start.12

commit v9 on v8

--- a/solution.py
+++ b/solution.py
@@ -19,15 +19,19 @@
 
 VMEM = pl.BlockSpec(memory_space=pltpu.VMEM)
 SMEM = pl.BlockSpec(memory_space=pltpu.SMEM)
-
-
-def call(body, out_shape, in_specs, scratch=(), micros=1.0, megabytes=20):
+ANY = pl.BlockSpec(memory_space=pl.ANY)
+
+
+def call(body, out_shape, in_specs, scratch=(), micros=1.0, megabytes=20, out_specs=None, alias=None):
     many = isinstance(out_shape, (list, tuple))
+    if out_specs is None:
+        out_specs = [VMEM] * len(out_shape) if many else VMEM
     return pl.pallas_call(
         body,
         out_shape=out_shape,
         in_specs=in_specs,
-        out_specs=[VMEM] * len(out_shape) if many else VMEM,
+        out_specs=out_specs,
+        input_output_aliases=alias or {},
         scratch_shapes=list(scratch),
         compiler_params=pltpu.CompilerParams(vmem_limit_bytes=megabytes * 1024 * 1024),
         cost_estimate=pl.CostEstimate(
@@ -82,17 +86,14 @@
                 )
 
 
-def coeff_kernel(u, right, out):
-    blocks, rank, size = right.shape
+def coeff_kernel(far_cols, u, left, right, coup, z_out, out):
+    ops, blocks, far, rank, _ = coup.shape
+    size = right.shape[2]
     z = [dot(right[b], u[b * size:(b + 1) * size, :]) for b in range(blocks)]
     for pair in range(SLICES // 2):
         first, second = halves(chunk(z[0], pair), chunk(z[1], pair))
-        out[2 * pair] = first.astype(BF16)
-        out[2 * pair + 1] = second.astype(BF16)
-
-
-def pack_kernel(far_cols, coup, left, right, out):
-    ops, blocks, far, rank, _ = coup.shape
+        z_out[2 * pair] = first.astype(BF16)
+        z_out[2 * pair + 1] = second.astype(BF16)
     whole, rest = [], []
     for b in range(blocks):
         tiles = [
@@ -116,7 +117,7 @@
     )
 
 
-def share_kernel(packed, *refs):
+def share_kernel(packed, after_low, after_high, *refs):
     parts, out = refs[:-1], refs[-1]
     rows = packed.shape[0]
     rank = parts[0].shape[1]
@@ -234,7 +235,7 @@
     return jnp.where(good, inner / jnp.where(good, squares, 1.0), 0.0)
 
 
-def near_kernel(w, low, own, high, diag, right, c1, image, first, second, edge, msg):
+def near_kernel(w, low, own, high, diag, right, c1, image, edge, msg):
     ops = image.shape[0]
     blocks, rank, size = right.shape
     rows, columns = own.shape
@@ -257,24 +258,21 @@
     shifts = [ratio(x, squares) for x in inner]
     edges = pieces_of(shifts + [squares])
     edge[...] = edges
-    first[rows:, :] = edges
     edges = edges.astype(F32)
     msg[:, 0:body, :] = c1[...]
-    for o, out in enumerate((first, second)):
+    for o in range(ops):
         shift = row3(edges, o)
         z = []
         for b in range(blocks):
             ub = own[b * size:(b + 1) * size, :].astype(F32)
             v = image[o, b * size:(b + 1) * size, :] - shift * ub
             image[o, b * size:(b + 1) * size, :] = v
-            v = v.astype(BF16)
-            out[b * size:(b + 1) * size, :] = v
-            z.append(dot(right[b], v))
+            z.append(dot(right[b], v.astype(BF16)))
         spread_pairs(msg, slice(body + o * rank, body + (o + 1) * rank), z[0], z[1])
     spread_pairs(msg, slice(2 * body, 2 * body + STATS), edges, edges)
 
 
-def image_kernel(own, near, edge, left, got, mixed, after_low, after_high, vout, stats, cown, xmsg, image, coef):
+def image_kernel(own, near, edge, left, got, mixed, first, second, cown, xmsg, image, coef):
     ops = near.shape[0]
     blocks, rank, size = left.shape
     rows, columns = own.shape
@@ -311,24 +309,13 @@
             v = image[b * size:(b + 1) * size, :] - change * ub
             part = jnp.sum(v * v, axis=0, keepdims=True)
             spread = part if spread is None else spread + part
-            vout[(o * blocks + b) * size:(o * blocks + b + 1) * size, :] = v.astype(BF16)
+            (first, second)[o][b * size:(b + 1) * size, :] = v.astype(BF16)
         spreads.append(spread)
     every = pieces_of(shifts + [squares] + spreads)
-    stats[...] = every
+    first[rows:, :] = every
     at = SLICES * (body + STATS)
     for j in range(columns // LANES):
         xmsg[at + j * STATS:at + (j + 1) * STATS, :] = chunk(every, j)
-
-
-def bulk_kernel(near, cown, left, edge, after, out):
-    rows = near.shape[0]
-    blocks, rank, size = left.shape
-    at = rows + cown.shape[0]
-    out[0:rows, :] = near[...]
-    out[rows:at, :] = cown[...]
-    for b in range(blocks):
-        out[at:at + rank, b * size:(b + 1) * size] = left[b]
-    out[at + rank:, :] = edge[...]
 
 
 def second_couple(panels, ops, rank, far, cols, group, held, *refs):
@@ -367,19 +354,45 @@
             out[s, row:row + height, :] = x[start:, :]
 
 
-def final_kernel(
+def apply_second(o, rows3, u3, v3, w, diag, left, cown, cmsg, images, ext, coef, out, sem):
+    blocks, rank, size = left.shape
+    rows, columns = u3[1].shape
+    ops = w.shape[1] // size
+    factor, changes, offset = rows3
+    copies = []
+    for at, (u, v) in enumerate(zip(u3, v3)):
+        value = v[0:rows, :].astype(F32) * factor + u[...].astype(F32) * changes[at]
+        ext[at] = value.astype(BF16)
+    take_coefs(cmsg, coef, ops * rank)
+    for b in range(blocks):
+        parts = [ext.at[at] for at in range(3)]
+        product = near_product(w.at[b, o * size:(o + 1) * size], parts, b, blocks, size)
+        row = (o * blocks + b) * rank
+        c = coef[b, o * rank:(o + 1) * rank, :].astype(F32) * factor
+        c = c - offset * cown[row:row + rank, :].astype(F32)
+        far = dot(left[b], c.astype(BF16), ((0,), (0,)))
+        here = slice(b * size, (b + 1) * size)
+        out[here, :] = (
+            product
+            + diagonal_of(diag, o, b, size, columns) * ext[1, here, :].astype(F32)
+            + far.astype(BF16).astype(F32)
+        )
+        copies.append(pltpu.make_async_copy(out.at[here], images.at[o, here], sem.at[b]))
+        copies[-1].start()
+    for copy in copies:
+        copy.wait()
+
+
+def final_first(
     panels,
     group,
     w,
     ulow,
     uown,
     uhigh,
-    low0,
-    low1,
+    vlow,
     vown,
-    high0,
-    high1,
-    mine,
+    vhigh,
     diag,
     left,
     cown,
@@ -387,18 +400,20 @@
     images,
     heights,
     norms,
+    aux,
     ext,
     coef,
+    out,
     st,
+    sem,
 ):
-    ops = images.shape[0]
     blocks, rank, size = left.shape
     rows, columns = uown.shape
+    ops = w.shape[1] // size
     body = ops * rank
     wide = columns // LANES
     height = wide * STATS
     count = (cmsg.shape[1] - body - STATS) // height
-    take_coefs(cmsg, coef, body)
     for m in range(count):
         at = group_at(group, m, count, SLICES)
         for j in range(wide):
@@ -420,6 +435,7 @@
     squares = join3(every, ops)
     scale_sq = jnp.sum(squares, axis=0, keepdims=True) / panels + EPSILON
     reverse = 1.0 / jnp.sqrt(scale_sq)
+    found = []
     for o in range(ops):
         shift = join3(every, o)
         high = jnp.sum(shift * squares, axis=0, keepdims=True) / panels / scale_sq
@@ -429,37 +445,71 @@
         heights[o:o + 1, :] = high
         norms[o:o + 1, :] = norm
         factor = reverse / norm
-        for at, u, v, more in ((0, ulow, (low0, low1)[o], low1), (2, uhigh, (high0, high1)[o], high1)):
-            start = rows + ops * blocks * rank
-            edges = more[start + rank:, :].astype(F32)
-            change = (row3(edges, o) - high) * factor
-            for b in range(blocks):
-                row = rows + (o * blocks + b) * rank
-                far = dot(
-                    more[start:start + rank, b * size:(b + 1) * size],
-                    more[row:row + rank, :],
-                    ((0,), (0,)),
-                ).astype(BF16).astype(F32)
-                here = slice(b * size, (b + 1) * size)
-                value = (v[here, :].astype(F32) + far) * factor + u[here, :].astype(F32) * change
-                ext[at, here, :] = value.astype(BF16)
-        change = (row3(mine[...].astype(F32), o) - high) * factor
-        value = vown[o * rows:(o + 1) * rows, :].astype(F32) * factor
-        ext[1] = (value + uown[...].astype(F32) * change).astype(BF16)
-        offset = high - row3(rough, o)
-        for b in range(blocks):
-            parts = [ext.at[at] for at in range(3)]
-            product = near_product(w.at[b, o * size:(o + 1) * size], parts, b, blocks, size)
-            row = (o * blocks + b) * rank
-            c = coef[b, o * rank:(o + 1) * rank, :].astype(F32)
-            c = (c - offset * cown[row:row + rank, :].astype(F32)) * factor
-            far = dot(left[b], c.astype(BF16), ((0,), (0,)))
-            own = ext[1, b * size:(b + 1) * size, :].astype(F32)
-            images[o, b * size:(b + 1) * size, :] = (
-                product
-                + diagonal_of(diag, o, b, size, columns) * own
-                + far.astype(BF16).astype(F32)
-            )
+        changes = [
+            (row3(v[rows:rows + STATS, :].astype(F32), o) - high) * factor
+            for v in (vlow, vown, vhigh)
+        ]
+        found.append((factor, changes, (high - row3(rough, o)) * factor))
+    factor, changes, offset = found[1]
+    aux[0:1, :] = factor
+    aux[1:2, :] = offset
+    for at in range(3):
+        aux[2 + at:3 + at, :] = changes[at]
+    apply_second(
+        0,
+        found[0],
+        (ulow, uown, uhigh),
+        (vlow, vown, vhigh),
+        w,
+        diag,
+        left,
+        cown,
+        cmsg,
+        images,
+        ext,
+        coef,
+        out,
+        sem,
+    )
+
+
+def final_second(
+    begun,
+    w,
+    ulow,
+    uown,
+    uhigh,
+    vlow,
+    vown,
+    vhigh,
+    diag,
+    left,
+    cown,
+    cmsg,
+    aux,
+    images,
+    ext,
+    coef,
+    out,
+    sem,
+):
+    rows3 = aux[0:1, :], [aux[2 + at:3 + at, :] for at in range(3)], aux[1:2, :]
+    apply_second(
+        1,
+        rows3,
+        (ulow, uown, uhigh),
+        (vlow, vown, vhigh),
+        w,
+        diag,
+        left,
+        cown,
+        cmsg,
+        images,
+        ext,
+        coef,
+        out,
+        sem,
+    )
 
 
 def ring(block):
@@ -508,18 +558,21 @@
     right = jnp.transpose(basis_right, (0, 2, 1))
 
     low, high = ring(sources)
-    z1 = call(coeff_kernel, sds((SLICES, rank, LANES), BF16), [VMEM, VMEM], megabytes=60)(
-        sources, right
-    )
-    z1 = across(z1)
     shared = (blocks + 1) * body
     lead = shared + STATS + rank
-    packed = call(pack_kernel, sds((lead, LANES), BF16), [SMEM, VMEM, VMEM, VMEM])(
-        far_cols, couplings, left, right
-    )
+    z1, packed = call(
+        coeff_kernel,
+        [sds((SLICES, rank, LANES), BF16), sds((lead, LANES), BF16)],
+        [SMEM] + [VMEM] * 4,
+        megabytes=60,
+    )(far_cols, sources, left, right, couplings)
+    z1 = across(z1)
     held = call(
-        share_kernel, sds((SLICES, lead + count * rank, LANES), BF16), [VMEM] * (1 + count)
-    )(packed, *z1)
+        share_kernel,
+        sds((SLICES, lead + count * rank, LANES), BF16),
+        [VMEM, ANY, ANY] + [VMEM] * count,
+        megabytes=60,
+    )(packed, low, high, *z1)
     held = exchange(held)
     cols = held[:, shared, :blocks * far].astype(jnp.int32).reshape(-1)
 
@@ -537,42 +590,33 @@
         [pltpu.VMEM((n * blocks * rank, LANES), BF16)],
     )(cols, group, held)
 
-    image, first, second, edge, msg = call(
+    image, edge, msg = call(
         near_kernel,
         [
             sds((ops, rows, columns), F32),
-            sds((rows + STATS, columns), BF16),
-            sds((rows, columns), BF16),
             sds((STATS, columns), BF16),
             sds((SLICES, 2 * body + STATS, LANES), BF16),
         ],
         [VMEM] * 7,
         micros=4.0,
     )(w, low, sources, high, self_terms, right, c1)
-    low0, high0 = ring(first)
     got = exchange(msg)
 
-    own_rows = ops * blocks * rank
-    v, stats, cown, xmsg = call(
+    first, second, cown, xmsg = call(
         image_kernel,
         [
-            sds((ops * rows, columns), BF16),
-            sds((STATS, columns), BF16),
-            sds((own_rows, columns), BF16),
+            sds((rows + STATS, columns), BF16),
+            sds((rows, columns), BF16),
+            sds((ops * blocks * rank, columns), BF16),
             sds((SLICES * (body + STATS) + columns // LANES * STATS, LANES), BF16),
         ],
-        [VMEM] * 6 + [pl.BlockSpec(memory_space=pl.ANY)] * 2,
+        [VMEM] * 6,
         [pltpu.VMEM((rows, columns), F32), pltpu.VMEM((blocks, body, columns), BF16)],
         micros=3.0,
-    )(sources, image, edge, left, got, mixed, low0, high0)
+    )(sources, image, edge, left, got, mixed)
     parts = across(xmsg)
-
-    bulk = call(
-        bulk_kernel,
-        sds((rows + own_rows + rank + STATS, columns), BF16),
-        [VMEM] * 4 + [pl.BlockSpec(memory_space=pl.ANY)],
-    )(second, cown, left, edge, parts[-1])
-    low1, high1 = ring(bulk)
+    low0, high0 = ring(first)
+    low1, high1 = ring(second)
 
     panels = all_blocks * size
     c2 = call(
@@ -583,33 +627,31 @@
     )(cols, group, held, *parts)
     c2 = exchange(c2)
 
-    images, heights, norms = call(
-        functools.partial(final_kernel, panels),
-        [sds((ops, rows, columns), F32), sds((ops, columns), F32), sds((ops, columns), F32)],
-        [SMEM] + [VMEM] * 14,
-        [
-            pltpu.VMEM((3, rows, columns), BF16),
-            pltpu.VMEM((blocks, body, columns), BF16),
-            pltpu.VMEM((n, STATS, columns), F32),
-        ],
-        micros=5.0,
-    )(
-        group,
-        w,
-        low,
-        sources,
-        high,
-        low0,
-        low1,
-        v,
-        high0,
-        high1,
-        stats,
-        self_terms,
-        left,
-        cown,
-        c2,
-    )
+    outs = sds((ops, rows, columns), F32)
+    scratch = [
+        pltpu.VMEM((3, rows, columns), BF16),
+        pltpu.VMEM((blocks, body, columns), BF16),
+        pltpu.VMEM((rows, columns), F32),
+    ]
+    images, heights, norms, aux = call(
+        functools.partial(final_first, panels),
+        [outs, sds((ops, columns), F32), sds((ops, columns), F32), sds((8, columns), F32)],
+        [SMEM] + [VMEM] * 11,
+        scratch + [pltpu.VMEM((n, STATS, columns), F32), pltpu.SemaphoreType.DMA((blocks,))],
+        micros=4.0,
+        megabytes=60,
+        out_specs=[ANY, VMEM, VMEM, VMEM],
+    )(group, w, low, sources, high, low0, first, high0, self_terms, left, cown, c2)
+    images = call(
+        final_second,
+        outs,
+        [ANY] + [VMEM] * 12,
+        scratch + [pltpu.SemaphoreType.DMA((blocks,))],
+        micros=4.0,
+        megabytes=60,
+        out_specs=ANY,
+        alias={0: 0},
+    )(images, w, low, sources, high, low1, second, high1, self_terms, left, cown, c2, aux)
     return images, heights, norms
 
 

time: 117 us -> 110 us (0.940)
  local copies, waits for them, and re-layouts: 16.7 us -> 7.26 us
  blocking collectives: 16.2 us -> 9.93 us
  Pallas kernels: 20.9 us -> 25.1 us
  waiting for transfers between devices: 41.1 us -> 45.1 us
    unnamed x50 -> x40, local copies, waits for them, and re-layouts: 16.6 us -> 7.18 us
    all_to_all x1, blocking collectives: 16.2 us -> 9.93 us  [exchange(): lax.all_to_all(x, 'store', 0, 0, axis_index_groups=groups, tiled=True)]
    ppermute x3, waiting for transfers between devices: 26.7 us -> 20.8 us  [ring(): lax.ppermute(block, 'store', backward)]
    ppermute x3, waiting for transfers between devices: 0.01 us -> 4.63 us  [ring(): lax.ppermute(block, 'store', forward)]
    ppermute x2, waiting for transfers between devices: 9.66 us -> 13.1 us  [across(): parts.append(lax.ppermute(x, 'store', pairs))]
    pallas_call x6 -> x5, Pallas kernels: 13.8 us -> 16.3 us  [the longest x1 5.97 us: shards(): call(functools.partial(final_first, panels), [outs, sds((ops, columns), F...]
    all_to_all x2, waiting for transfers between devices: 4.75 us -> 6.49 us  [exchange(): lax.all_to_all(x, 'store', 0, 0, axis_index_groups=groups, tiled=True)]
  transfers between devices with their start and end apart: 10 -> 10, of which waited for: 4 -> 5; matrix products, arithmetic and copies ran while one was open for 1% -> 0% of each run, Pallas kernels for 4% -> 8%
where the time goes in v9:
time: 110 us; the launch traced here: 109 us
  waiting for transfers between devices  45.1 us (41%)
  Pallas kernels  25.1 us (23%)
  starting transfers between devices  20 us (18%)
  blocking collectives  9.93 us (9%)
  local copies, waits for them, and re-layouts  7.26 us (7%)
    ppermute x3, waiting for transfers between devices, ring(): lax.ppermute(block, 'store', backward)  20.8 us
    ppermute x2, waiting for transfers between devices, across(): parts.append(lax.ppermute(x, 'store', pairs))  13.1 us
    all_to_all x2, starting transfers between devices, exchange(): lax.all_to_all(x, 'store', 0, 0, axis_index_groups=groups, tiled=True)  10.6 us
    all_to_all x1, blocking collectives, exchange(): lax.all_to_all(x, 'store', 0, 0, axis_index_groups=groups, tiled=True)  9.93 us
    unnamed x40, local copies, waits for them, and re-layouts  7.18 us
    all_to_all x2, waiting for transfers between devices, exchange(): lax.all_to_all(x, 'store', 0, 0, axis_index_groups=groups, tiled=True)  6.49 us
    pallas_call x1, Pallas kernels, shards(): call(functools.partial(final_first, panels), [outs, sds((ops, columns), F...  5.97 us
    ppermute x3, starting transfers between devices, ring(): lax.ppermute(block, 'store', forward)  5.61 us
  transfers between devices with their start and end apart: 10, of which 5 were waited for; matrix products, arithmetic and copies ran while one was open for 0% of the time, Pallas kernels for 8%

profile of v9, /device:TPU:1, one launch (start us, length us, event | category | flops | bytes accessed | tf_op | source)
XLA Modules:
  0.0 108.9 jit_solution(9437876812336106428)
XLA Ops:
  0.6 0.0 copy-start.14
  0.6 0.0 copy-start.13
  0.7 0.1 collective-permute-start.1
  0.8 2.6 %collective-permute-start = (bf16[512,512]{1,0:T(8,128)(2,1)}, bf16[512,512]{1,0:T(8,128)(2,1)S(1)}, u32[]{:S(2)}, u32[]{:S(2)}) collective-permute-start(bf16[512,512]{1,0:T(8,128)(2,1)} %uown.3), channel_id=1, source_target_pairs={{0,1},{1,2},{2,3},{3,4},{4,5},{5,6},{6,7},{7,8},{8,9},{9,10},{10,1... | collective-permute-start | bytes 1572872 | tf_op jit(solution)/shard_map/ppermute | solution.py:519
  3.4 2.1 %shard_map.113 = (bf16[8,32,128]{2,1,0:T(8,128)(2,1)}, bf16[240,128]{1,0:T(8,128)(2,1)}) custom-call(s32[2,6]{1,0:T(2,128)} %far_cols.1, bf16[512,512]{1,0:T(8,128)(2,1)} %uown.3, bf16[2,32,256]{2,1,0:T(8,128)(2,1)} %bitcast.4, bf16[2,32,256]{2,1,0:T(8,128)(2,1)} %bitcast.8, bf16[2,2,6,32,32]{4,3,2,1,0:T(8,128)(2,1)} %coup.1), custom_call_target="tpu_custom_call" | custom-call | bytes 3690000 | tf_op jit(solution)/shard_map/pallas_call | solution.py:563
  5.5 2.3 %collective-permute-start.2 = (bf16[8,32,128]{2,1,0:T(8,128)(2,1)}, bf16[8,32,128]{2,1,0:T(8,128)(2,1)S(1)}, u32[]{:S(2)}, u32[]{:S(2)}) collective-permute-start(bf16[8,32,128]{2,1,0:T(8,128)(2,1)} %get-tuple-element.19.refs_0_), channel_id=1, source_target_pairs={{0,8},{1,9},{2,10},{3,11},{4,12},{5,13},{6,14},{7,15},{8,0},{9,1},... | collective-permute-start | bytes 196616 | tf_op jit(solution)/shard_map/ppermute | solution.py:551
  7.8 3.1 %collective-permute-done.2.refs_1_ = bf16[8,32,128]{2,1,0:T(8,128)(2,1)S(1)} collective-permute-done((bf16[8,32,128]{2,1,0:T(8,128)(2,1)}, bf16[8,32,128]{2,1,0:T(8,128)(2,1)S(1)}, u32[]{:S(2)}, u32[]{:S(2)}) %collective-permute-start.2) | collective-permute-done | bytes 65568 | tf_op jit(solution)/shard_map/ppermute | solution.py:551
  10.8 0.0 copy-start.19
  10.8 0.0 collective-permute-done.1.after_high.high.uhigh
  10.8 0.0 copy-start.2
  10.8 4.6 %collective-permute-done.after_low.low.ulow = bf16[512,512]{1,0:T(8,128)(2,1)S(1)} collective-permute-done((bf16[512,512]{1,0:T(8,128)(2,1)}, bf16[512,512]{1,0:T(8,128)(2,1)S(1)}, u32[]{:S(2)}, u32[]{:S(2)}) %collective-permute-start) | collective-permute-done | bytes 524320 | tf_op jit(solution)/shard_map/ppermute | solution.py:519
  15.5 0.0 copy-start.4
  15.5 0.0 copy-done.19
  15.5 0.0 copy-done.2
  15.5 0.8 copy-done.4
  16.3 1.8 %shard_map.114 = bf16[8,304,128]{2,1,0:T(8,128)(2,1)} custom-call(bf16[240,128]{1,0:T(8,128)(2,1)} %get-tuple-element.18.packed, bf16[512,512]{1,0:T(8,128)(2,1)} %copy-done.4, bf16[512,512]{1,0:T(8,128)(2,1)} %copy-done.2, bf16[8,32,128]{2,1,0:T(8,128)(2,1)} %get-tuple-element.19.refs_0_, bf16[8,32,128]{2,1,0:T(8,128)(2,1)} %copy-done.19), custom_call_target="tpu_custom_call" | custom-call | bytes 3690000 | tf_op jit(solution)/shard_map/pallas_call | solution.py:570
  18.1 6.5 %all-to-all-start = ((bf16[8,304,128]{2,1,0:T(8,128)(2,1)}), bf16[8,304,128]{2,1,0:T(8,128)(2,1)}, u32[]{:S(2)}, u32[]{:S(2)}) async-start(bf16[8,304,128]{2,1,0:T(8,128)(2,1)} %shard_map.114), calls=%async_computation | async-start | bytes 1245184 | tf_op jit(solution)/shard_map/all_to_all | solution.py:545
  24.5 0.0 copy-done.14
  24.5 0.0 copy-done.13
  24.5 0.0 copy-start.6
  24.5 1.7 %copy-done.6 = bf16[2,2,5,256,256]{4,3,2,1,0:T(8,128)(2,1)S(1)} copy-done((bf16[2,2,5,256,256]{4,3,2,1,0:T(8,128)(2,1)S(1)}, bf16[2,2,5,256,256]{4,3,2,1,0:T(8,128)(2,1)}, u32[]{:S(2)}) %copy-start.6) | copy-done | bytes 2621464
  26.3 0.0 copy-start.1
  26.3 0.0 copy-start.11
  26.3 0.9 shard_map.112.w
  27.2 0.0 copy-start
  27.2 6.5 %all-to-all-done.held = bf16[8,304,128]{2,1,0:T(8,128)(2,1)} async-done(((bf16[8,304,128]{2,1,0:T(8,128)(2,1)}), bf16[8,304,128]{2,1,0:T(8,128)(2,1)}, u32[]{:S(2)}, u32[]{:S(2)}) %all-to-all-start) | async-done | bytes 622624 | tf_op jit(solution)/shard_map/all_to_all | solution.py:545
  33.7 0.7 fusion
  34.4 0.1 reshape.18.cols
  34.5 3.2 %shard_map.115 = (bf16[8,64,128]{2,1,0:T(8,128)(2,1)S(1)}, f32[8,64,128]{2,1,0:T(8,128)S(1)}) custom-call(s32[96]{0:T(128)S(1)} %reshape.18.cols, s32[1]{0:T(128)} %bitcast.group, bf16[8,304,128]{2,1,0:T(8,128)(2,1)} %all-to-all-done.held), custom_call_target="tpu_custom_call" | custom-call | bytes 3690000 | tf_op jit(solution)/shard_map/pallas_call | solution.py:586
  37.7 0.0 copy-done.1
  37.7 0.0 copy-done.11
  37.7 0.0 copy-done.12
  37.7 0.0 copy-start.3
  37.7 1.0 copy-done.3
  38.8 1.0 copy-done.5
  39.8 2.2 %shard_map.116 = (f32[2,512,512]{2,1,0:T(8,128)S(1)}, bf16[16,512]{1,0:T(8,128)(2,1)S(1)}, bf16[8,144,128]{2,1,0:T(8,128)(2,1)S(1)}) custom-call(bf16[2,512,1280]{2,1,0:T(8,128)(2,1)S(1)} %shard_map.112.w, bf16[512,512]{1,0:T(8,128)(2,1)S(1)} %copy-done.5, bf16[512,512]{1,0:T(8,128)(2,1)S(1)} %copy-done.1, bf16[512,512]{1,0:T(8,128)(2,1)S(1)} %copy-done.3, ...), custom_call_target="tpu_custom_call" | custom-call | bytes 14760000 | tf_op jit(solution)/shard_map/pallas_call | solution.py:593
  42.0 0.0 copy-done
  42.0 9.9 %all_to_all.15.got = bf16[8,144,128]{2,1,0:T(8,128)(2,1)S(1)} all-to-all(bf16[8,144,128]{2,1,0:T(8,128)(2,1)S(1)} %get-tuple-element.23), channel_id=1, replica_groups={{0,1,2,3,4,5,6,7},{8,9,10,11,12,13,14,15},{16,17,18,19,20,21,22,23},{24..., dimensions={0} | all-to-all | bytes 589824 | tf_op jit(solution)/shard_map/all_to_all | solution.py:545
  51.9 0.0 copy-done.8
  51.9 1.2 %shard_map.117 = (bf16[528,512]{1,0:T(8,128)(2,1)S(1)}, bf16[512,512]{1,0:T(8,128)(2,1)S(1)}, bf16[128,512]{1,0:T(8,128)(2,1)S(1)}, bf16[704,128]{1,0:T(8,128)(2,1)S(1)}) custom-call(bf16[512,512]{1,0:T(8,128)(2,1)S(1)} %copy-done.1, f32[2,512,512]{2,1,0:T(8,128)S(1)} %get-tuple-element.21.near, bf16[16,512]{1,0:T(8,128)(2,1)S(1)} %get-tuple-element.22.edge, ...), custom_call_target="tpu_custom_call" | custom-call | bytes 11070000 | tf_op jit(solution)/shard_map/pallas_call | solution.py:605
  53.2 0.6 copy-done.9
  53.8 0.9 collective-permute-start.5
  54.7 10.1 %collective-permute-done.5.refs_1_ = bf16[704,128]{1,0:T(8,128)(2,1)S(1)} collective-permute-done((bf16[704,128]{1,0:T(8,128)(2,1)S(1)}, bf16[704,128]{1,0:T(8,128)(2,1)S(1)}, u32[]{:S(2)}, u32[]{:S(2)}) %collective-permute-start.5) | collective-permute-done | bytes 180256 | tf_op jit(solution)/shard_map/ppermute | solution.py:551
  64.8 2.9 %shard_map.118 = bf16[8,208,128]{2,1,0:T(8,128)(2,1)} custom-call(s32[96]{0:T(128)S(1)} %reshape.18.cols, s32[1]{0:T(128)} %bitcast.group, bf16[8,304,128]{2,1,0:T(8,128)(2,1)} %all-to-all-done.held, bf16[704,128]{1,0:T(8,128)(2,1)S(1)} %get-tuple-element.27.refs_0_, bf16[704,128]{1,0:T(8,128)(2,1)S(1)} %collective-permute-done.5.refs_1_), custom_call_target="tpu_custom_call" | custom-call | bytes 3690000 | tf_op jit(solution)/shard_map/pallas_call | solution.py:622
  67.6 4.1 %all-to-all-start.2 = ((bf16[8,208,128]{2,1,0:T(8,128)(2,1)}), bf16[8,208,128]{2,1,0:T(8,128)(2,1)S(1)}, u32[]{:S(2)}, u32[]{:S(2)}) async-start(bf16[8,208,128]{2,1,0:T(8,128)(2,1)} %shard_map.118), calls=%async_computation.2 | async-start | bytes 851968 | tf_op jit(solution)/shard_map/all_to_all | solution.py:545
  71.8 0.2 collective-permute-start.4
  71.9 1.6 %collective-permute-start.3 = (bf16[528,512]{1,0:T(8,128)(2,1)S(1)}, bf16[528,512]{1,0:T(8,128)(2,1)S(1)}, u32[]{:S(2)}, u32[]{:S(2)}) collective-permute-start(bf16[528,512]{1,0:T(8,128)(2,1)S(1)} %get-tuple-element.25.vown), channel_id=1, source_target_pairs={{0,1},{1,2},{2,3},{3,4},{4,5},{5,6},{6,7},{7,8},{8,9},{9,10},{10,1... | collective-permute-start | bytes 1622024 | tf_op jit(solution)/shard_map/ppermute | solution.py:519
  73.5 0.4 collective-permute-start.7
  73.9 1.4 %collective-permute-start.6 = (bf16[512,512]{1,0:T(8,128)(2,1)S(1)}, bf16[512,512]{1,0:T(8,128)(2,1)}, u32[]{:S(2)}, u32[]{:S(2)}) collective-permute-start(bf16[512,512]{1,0:T(8,128)(2,1)S(1)} %get-tuple-element.29.vown), channel_id=1, source_target_pairs={{0,1},{1,2},{2,3},{3,4},{4,5},{5,6},{6,7},{7,8},{8,9},{9,10},{10,1... | collective-permute-start | bytes 1572872 | tf_op jit(solution)/shard_map/ppermute | solution.py:519
  75.3 20.8 %collective-permute-done.4.vhigh = bf16[528,512]{1,0:T(8,128)(2,1)S(1)} collective-permute-done((bf16[528,512]{1,0:T(8,128)(2,1)S(1)}, bf16[528,512]{1,0:T(8,128)(2,1)S(1)}, u32[]{:S(2)}, u32[]{:S(2)}) %collective-permute-start.4) | collective-permute-done | bytes 540704 | tf_op jit(solution)/shard_map/ppermute | solution.py:519
  96.1 0.0 collective-permute-done.3.vlow
  96.1 0.0 all-to-all-done.2.cmsg
  96.1 0.0 copy-start.15
  96.1 0.0 copy-done.7
  96.1 0.8 copy-done.16
  96.9 0.2 copy-done.17
  97.1 0.2 copy-done.15
  97.3 6.0 %shard_map.119 = (f32[2,512,512]{2,1,0:T(8,128)}, f32[2,512]{1,0:T(2,128)}, f32[2,512]{1,0:T(2,128)}, f32[8,512]{1,0:T(8,128)}) custom-call(s32[1]{0:T(128)} %bitcast.group, bf16[2,512,1280]{2,1,0:T(8,128)(2,1)} %copy-done, bf16[512,512]{1,0:T(8,128)(2,1)} %copy-done.4, bf16[512,512]{1,0:T(8,128)(2,1)} %uown.3, bf16[512,512]{1,0:T(8,128)(2,1)} %copy-done.2, ...), custom_call_target="tpu_custom_call" | custom-call | bytes 14760000 | tf_op jit(solution)/shard_map/pallas_call | solution.py:636
  103.2 0.0 copy-done.10
  103.2 0.0 collective-permute-done.7.vhigh
  103.2 0.0 copy-start.18
  103.3 0.0 collective-permute-done.6.vlow
  103.3 0.8 copy-done.18
  104.0 4.9 %shard_map.120 = f32[2,512,512]{2,1,0:T(8,128)} custom-call(f32[2,512,512]{2,1,0:T(8,128)} %get-tuple-element.28.begun, bf16[2,512,1280]{2,1,0:T(8,128)(2,1)} %copy-done, bf16[512,512]{1,0:T(8,128)(2,1)} %copy-done.4, bf16[512,512]{1,0:T(8,128)(2,1)} %uown.3, bf16[512,512]{1,0:T(8,128)(2,1)} %copy-done.2, ...), custom_call_target="tpu_custom_call", output_to_operand_aliasing={{}: (0, {})} | custom-call | bytes 14760000 | tf_op jit(solution)/shard_map/pallas_call | solution.py:645
  (8 shorter events, 0.0 us)
Async XLA Ops:
  0.6 23.9 %copy-start.14 = (s32[2]{0:T(128)S(1)}, s32[2]{0:T(128)}, u32[]{:S(2)}) copy-start(s32[2]{0:T(128)} %count.1) | copy-start | bytes 28
  0.6 23.9 %copy-start.13 = (s32[2,5]{1,0:T(2,128)S(1)}, s32[2,5]{1,0:T(2,128)}, u32[]{:S(2)}) copy-start(s32[2,5]{1,0:T(2,128)} %cols.1) | copy-start | bytes 124
  0.7 10.2 %collective-permute-start.1 = (bf16[512,512]{1,0:T(8,128)(2,1)}, bf16[512,512]{1,0:T(8,128)(2,1)S(1)}, u32[]{:S(2)}, u32[]{:S(2)}) collective-permute-start(bf16[512,512]{1,0:T(8,128)(2,1)} %uown.3), channel_id=1, source_target_pairs={{1,0},{2,1},{3,2},{4,3},{5,4},{6,5},{7,6},{8,7},{9,8},{10,9},{11,1... | collective-permute-start | bytes 1572872 | tf_op jit(solution)/shard_map/ppermute | solution.py:519
  0.8 14.7 %collective-permute-start = (bf16[512,512]{1,0:T(8,128)(2,1)}, bf16[512,512]{1,0:T(8,128)(2,1)S(1)}, u32[]{:S(2)}, u32[]{:S(2)}) collective-permute-start(bf16[512,512]{1,0:T(8,128)(2,1)} %uown.3), channel_id=1, source_target_pairs={{0,1},{1,2},{2,3},{3,4},{4,5},{5,6},{6,7},{7,8},{8,9},{9,10},{10,1... | collective-permute-start | bytes 1572872 | tf_op jit(solution)/shard_map/ppermute | solution.py:519
  5.5 5.4 %collective-permute-start.2 = (bf16[8,32,128]{2,1,0:T(8,128)(2,1)}, bf16[8,32,128]{2,1,0:T(8,128)(2,1)S(1)}, u32[]{:S(2)}, u32[]{:S(2)}) collective-permute-start(bf16[8,32,128]{2,1,0:T(8,128)(2,1)} %get-tuple-element.19.refs_0_), channel_id=1, source_target_pairs={{0,8},{1,9},{2,10},{3,11},{4,12},{5,13},{6,14},{7,15},{8,0},{9,1},... | collective-permute-start | bytes 196616 | tf_op jit(solution)/shard_map/ppermute | solution.py:551
  10.8 4.6 %copy-start.19 = (bf16[8,32,128]{2,1,0:T(8,128)(2,1)}, bf16[8,32,128]{2,1,0:T(8,128)(2,1)S(1)}, u32[]{:S(2)}) copy-start(bf16[8,32,128]{2,1,0:T(8,128)(2,1)S(1)} %collective-permute-done.2.refs_1_) | copy-start | bytes 196612
  10.8 4.6 %copy-start.2 = (bf16[512,512]{1,0:T(8,128)(2,1)}, bf16[512,512]{1,0:T(8,128)(2,1)S(1)}, u32[]{:S(2)}) copy-start(bf16[512,512]{1,0:T(8,128)(2,1)S(1)} %collective-permute-done.1.after_high.high.uhigh) | copy-start | bytes 1572868
  15.5 0.8 copy-start.4
  18.1 15.6 %all-to-all-start = ((bf16[8,304,128]{2,1,0:T(8,128)(2,1)}), bf16[8,304,128]{2,1,0:T(8,128)(2,1)}, u32[]{:S(2)}, u32[]{:S(2)}) async-start(bf16[8,304,128]{2,1,0:T(8,128)(2,1)} %shard_map.114), calls=%async_computation | async-start | bytes 1245184 | tf_op jit(solution)/shard_map/all_to_all | solution.py:545
  24.5 1.7 %copy-start.6 = (bf16[2,2,5,256,256]{4,3,2,1,0:T(8,128)(2,1)S(1)}, bf16[2,2,5,256,256]{4,3,2,1,0:T(8,128)(2,1)}, u32[]{:S(2)}) copy-start(bf16[2,2,5,256,256]{4,3,2,1,0:T(8,128)(2,1)} %tiles.1) | copy-start | bytes 7864324
  26.3 11.4 %copy-start.1 = (bf16[512,512]{1,0:T(8,128)(2,1)S(1)}, bf16[512,512]{1,0:T(8,128)(2,1)}, u32[]{:S(2)}) copy-start(bf16[512,512]{1,0:T(8,128)(2,1)} %uown.3) | copy-start | bytes 1572868
  26.3 11.4 %copy-start.11 = (bf16[2,256,32]{1,2,0:T(8,128)(2,1)S(1)}, bf16[2,256,32]{1,2,0:T(8,128)(2,1)}, u32[]{:S(2)}) copy-start(bf16[2,256,32]{1,2,0:T(8,128)(2,1)} %param.16) | copy-start | bytes 98308
  26.3 11.4 %copy-start.12 = (f32[2,512]{1,0:T(2,128)S(1)}, f32[2,512]{1,0:T(2,128)}, u32[]{:S(2)}) copy-start(f32[2,512]{1,0:T(2,128)} %diag.5) | copy-start | bytes 12292
  27.2 14.8 %copy-start = (bf16[2,512,1280]{2,1,0:T(8,128)(2,1)}, bf16[2,512,1280]{2,1,0:T(8,128)(2,1)S(1)}, u32[]{:S(2)}) copy-start(bf16[2,512,1280]{2,1,0:T(8,128)(2,1)S(1)} %shard_map.112.w) | copy-start | bytes 7864324
  37.7 1.0 copy-start.3
  38.8 1.0 copy-start.5
  39.8 12.1 %copy-start.8 = (bf16[2,256,32]{1,2,0:T(8,128)(2,1)S(1)}, bf16[2,256,32]{1,2,0:T(8,128)(2,1)}, u32[]{:S(2)}) copy-start(bf16[2,256,32]{1,2,0:T(8,128)(2,1)} %param.15) | copy-start | bytes 98308
  53.2 0.6 copy-start.9
  53.8 42.3 %copy-start.7 = (bf16[528,512]{1,0:T(8,128)(2,1)}, bf16[528,512]{1,0:T(8,128)(2,1)S(1)}, u32[]{:S(2)}) copy-start(bf16[528,512]{1,0:T(8,128)(2,1)S(1)} %get-tuple-element.25.vown) | copy-start | bytes 1622020
  53.8 49.4 %copy-start.10 = (bf16[512,512]{1,0:T(8,128)(2,1)}, bf16[512,512]{1,0:T(8,128)(2,1)S(1)}, u32[]{:S(2)}) copy-start(bf16[512,512]{1,0:T(8,128)(2,1)S(1)} %get-tuple-element.29.vown) | copy-start | bytes 1572868
  53.8 11.0 %collective-permute-start.5 = (bf16[704,128]{1,0:T(8,128)(2,1)S(1)}, bf16[704,128]{1,0:T(8,128)(2,1)S(1)}, u32[]{:S(2)}, u32[]{:S(2)}) collective-permute-start(bf16[704,128]{1,0:T(8,128)(2,1)S(1)} %get-tuple-element.27.refs_0_), channel_id=1, source_target_pairs={{0,8},{1,9},{2,10},{3,11},{4,12},{5,13},{6,14},{7,15},{8,0},{9,1},... | collective-permute-start | bytes 540680 | tf_op jit(solution)/shard_map/ppermute | solution.py:551
  67.6 28.5 %all-to-all-start.2 = ((bf16[8,208,128]{2,1,0:T(8,128)(2,1)}), bf16[8,208,128]{2,1,0:T(8,128)(2,1)S(1)}, u32[]{:S(2)}, u32[]{:S(2)}) async-start(bf16[8,208,128]{2,1,0:T(8,128)(2,1)} %shard_map.118), calls=%async_computation.2 | async-start | bytes 851968 | tf_op jit(solution)/shard_map/all_to_all | solution.py:545
  71.8 24.3 %collective-permute-start.4 = (bf16[528,512]{1,0:T(8,128)(2,1)S(1)}, bf16[528,512]{1,0:T(8,128)(2,1)S(1)}, u32[]{:S(2)}, u32[]{:S(2)}) collective-permute-start(bf16[528,512]{1,0:T(8,128)(2,1)S(1)} %get-tuple-element.25.vown), channel_id=1, source_target_pairs={{1,0},{2,1},{3,2},{4,3},{5,4},{6,5},{7,6},{8,7},{9,8},{10,9},{11,1... | collective-permute-start | bytes 1622024 | tf_op jit(solution)/shard_map/ppermute | solution.py:519
  71.9 24.2 %collective-permute-start.3 = (bf16[528,512]{1,0:T(8,128)(2,1)S(1)}, bf16[528,512]{1,0:T(8,128)(2,1)S(1)}, u32[]{:S(2)}, u32[]{:S(2)}) collective-permute-start(bf16[528,512]{1,0:T(8,128)(2,1)S(1)} %get-tuple-element.25.vown), channel_id=1, source_target_pairs={{0,1},{1,2},{2,3},{3,4},{4,5},{5,6},{6,7},{7,8},{8,9},{9,10},{10,1... | collective-permute-start | bytes 1622024 | tf_op jit(solution)/shard_map/ppermute | solution.py:519
  73.5 29.7 %collective-permute-start.7 = (bf16[512,512]{1,0:T(8,128)(2,1)S(1)}, bf16[512,512]{1,0:T(8,128)(2,1)S(1)}, u32[]{:S(2)}, u32[]{:S(2)}) collective-permute-start(bf16[512,512]{1,0:T(8,128)(2,1)S(1)} %get-tuple-element.29.vown), channel_id=1, source_target_pairs={{1,0},{2,1},{3,2},{4,3},{5,4},{6,5},{7,6},{8,7},{9,8},{10,9},{11,1... | collective-permute-start | bytes 1572872 | tf_op jit(solution)/shard_map/ppermute | solution.py:519
  73.9 29.4 %collective-permute-start.6 = (bf16[512,512]{1,0:T(8,128)(2,1)S(1)}, bf16[512,512]{1,0:T(8,128)(2,1)}, u32[]{:S(2)}, u32[]{:S(2)}) collective-permute-start(bf16[512,512]{1,0:T(8,128)(2,1)S(1)} %get-tuple-element.29.vown), channel_id=1, source_target_pairs={{0,1},{1,2},{2,3},{3,4},{4,5},{5,6},{6,7},{7,8},{8,9},{9,10},{10,1... | collective-permute-start | bytes 1572872 | tf_op jit(solution)/shard_map/ppermute | solution.py:519
  96.1 0.8 copy-start.16
  96.1 1.0 copy-start.17
  96.1 1.2 %copy-start.15 = (bf16[8,208,128]{2,1,0:T(8,128)(2,1)}, bf16[8,208,128]{2,1,0:T(8,128)(2,1)S(1)}, u32[]{:S(2)}) copy-start(bf16[8,208,128]{2,1,0:T(8,128)(2,1)S(1)} %all-to-all-done.2.cmsg) | copy-start | bytes 1277956
  103.2 0.8 copy-start.18

commit v10 on v7

--- a/solution.py
+++ b/solution.py
@@ -13,12 +13,13 @@
 HALF = 64
 SLICES = 8
 STATS = 16
-HBM_RATE = 3690000
+FLOP_RATE = 1150000000
 F32 = jnp.float32
 BF16 = jnp.bfloat16
 
 VMEM = pl.BlockSpec(memory_space=pltpu.VMEM)
 SMEM = pl.BlockSpec(memory_space=pltpu.SMEM)
+ANY = pl.BlockSpec(memory_space=pl.ANY)
 
 
 def call(body, out_shape, in_specs, scratch=(), micros=1.0, megabytes=20):
@@ -31,7 +32,7 @@
         scratch_shapes=list(scratch),
         compiler_params=pltpu.CompilerParams(vmem_limit_bytes=megabytes * 1024 * 1024),
         cost_estimate=pl.CostEstimate(
-            flops=0, bytes_accessed=int(micros * HBM_RATE), transcendentals=0
+            flops=int(micros * FLOP_RATE), bytes_accessed=0, transcendentals=0
         ),
     )
 
@@ -121,7 +122,7 @@
         out[:, rows + m * rank:rows + (m + 1) * rank, :] = part[...]
 
 
-def copy_kernel(source, after, target):
+def copy_kernel(source, target):
     target[...] = source[...]
 
 
@@ -205,7 +206,21 @@
     return jnp.concatenate([column] * (columns // LANES), axis=1)
 
 
-def image_kernel(w, low, own, high, diag, left, right, cmsg, vout, mout, image, coef):
+def near_kernel(w, low, own, high, diag, image):
+    ops, rows, columns = image.shape
+    size = w.shape[1] // ops
+    blocks = rows // size
+    for b in range(blocks):
+        product = near_product(w.at[b], (low, own, high), b, blocks, size)
+        here = slice(b * size, (b + 1) * size)
+        ub = own[here, :].astype(F32)
+        for o in range(ops):
+            image[o, here, :] = (
+                product[o * size:(o + 1) * size] + diagonal_of(diag, o, b, size, columns) * ub
+            )
+
+
+def image_kernel(own, near, left, right, cmsg, out0, out1, mout, image, coef):
     ops = image.shape[0]
     blocks, rank, size = right.shape
     rows, columns = own.shape
@@ -213,18 +228,14 @@
     inner = [None] * ops
     squares = None
     for b in range(blocks):
-        product = near_product(w.at[b], (low, own, high), b, blocks, size)
-        ub = own[b * size:(b + 1) * size, :].astype(F32)
+        here = slice(b * size, (b + 1) * size)
+        ub = own[here, :].astype(F32)
         part = jnp.sum(ub * ub, axis=0, keepdims=True)
         squares = part if squares is None else squares + part
         for o in range(ops):
             far = dot(left[b], coef[b, o * rank:(o + 1) * rank, :], ((0,), (0,)))
-            value = (
-                product[o * size:(o + 1) * size]
-                + diagonal_of(diag, o, b, size, columns) * ub
-                + far.astype(BF16).astype(F32)
-            )
-            image[o, b * size:(b + 1) * size, :] = value
+            value = near[o, here, :] + far.astype(BF16).astype(F32)
+            image[o, here, :] = value
             part = jnp.sum(ub * value, axis=0, keepdims=True)
             inner[o] = part if inner[o] is None else inner[o] + part
     stats = []
@@ -243,7 +254,7 @@
             part = jnp.sum(v * v, axis=0, keepdims=True)
             spread = part if spread is None else spread + part
             v = v.astype(BF16)
-            vout[(o * blocks + b) * size:(o * blocks + b + 1) * size, :] = v
+            (out0, out1)[o][b * size:(b + 1) * size, :] = v
             z.append(dot(right[b], v))
         for pair in range(SLICES // 2):
             first, second = halves(chunk(z[0], pair), chunk(z[1], pair))
@@ -251,7 +262,7 @@
             mout[2 * pair + 1, o * rank:(o + 1) * rank, :] = second.astype(BF16)
         spreads.append(spread)
     zero = jnp.zeros((1, columns), BF16)
-    vout[ops * rows:, :] = jnp.concatenate(stats + [zero] * (STATS - len(stats)), axis=0)
+    out0[rows:, :] = jnp.concatenate(stats + [zero] * (STATS - len(stats)), axis=0)
     stats += split3(squares)
     for spread in spreads:
         stats += split3(spread)
@@ -263,7 +274,7 @@
         mout[2 * pair + 1, ops * rank:ops * rank + STATS, :] = second.astype(BF16)
 
 
-def second_couple(panels, ops, rank, far, cols, group, held, *refs):
+def second_couple(panels, ops, rank, far, cols, group, after_low, after_high, held, *refs):
     msgs, (out, zs, st) = refs[:-3], refs[-3:]
     count = len(msgs)
     body = ops * rank
@@ -305,7 +316,25 @@
 
 
 def final_kernel(
-    w, ulow, uown, uhigh, vlow, vown, vhigh, diag, left, cmsg, images, heights, norms, ext, coef, stat
+    w,
+    ulow,
+    uown,
+    uhigh,
+    low0,
+    first,
+    high0,
+    low1,
+    second,
+    high1,
+    diag,
+    left,
+    cmsg,
+    images,
+    heights,
+    norms,
+    ext,
+    coef,
+    stat,
 ):
     ops = images.shape[0]
     blocks, rank, size = left.shape
@@ -325,10 +354,12 @@
         heights[o:o + 1, :] = height
         norms[o:o + 1, :] = norm
         factor = reverse / norm
-        for at, (u, v) in enumerate(((ulow, vlow), (uown, vown), (uhigh, vhigh))):
-            shift = row3(v[ops * rows:, :].astype(F32), o)
+        triples = (ulow, low0, low1), (uown, first, second), (uhigh, high0, high1)
+        for at, (u, v0, v1) in enumerate(triples):
+            shift = row3(v0[rows:, :].astype(F32), o)
             change = (shift - height) * factor
-            value = v[o * rows:(o + 1) * rows, :].astype(F32) * factor + u[...].astype(F32) * change
+            v = (v0, v1)[o][0:rows, :].astype(F32)
+            value = v * factor + u[...].astype(F32) * change
             ext[o, at] = value.astype(BF16)
         for b in range(blocks):
             parts = [ext.at[o, at] for at in range(3)]
@@ -419,45 +450,51 @@
     )(cols, group, held)
     c1 = exchange(c1)
 
-    v, msg = call(
+    image = call(near_kernel, sds((ops, rows, columns), F32), [VMEM] * 5, micros=3.0)(
+        w, low, sources, high, self_terms
+    )
+    first, second, msg = call(
         image_kernel,
-        [sds((ops * rows + STATS, columns), BF16), sds((SLICES, body + STATS, LANES), BF16)],
-        [VMEM] * 8,
+        [
+            sds((rows + STATS, columns), BF16),
+            sds((rows, columns), BF16),
+            sds((SLICES, body + STATS, LANES), BF16),
+        ],
+        [VMEM] * 5,
         [
             pltpu.VMEM((ops, rows, columns), F32),
             pltpu.VMEM((blocks, body, columns), BF16),
         ],
-        micros=4.0,
-    )(w, low, sources, high, self_terms, left, right, c1)
+        micros=2.0,
+    )(sources, image, left, right, c1)
     msg = exchange(msg)
-    msgs = across(msg)
-    bulk = call(
-        copy_kernel, sds(v.shape, BF16), [VMEM, pl.BlockSpec(memory_space=pl.ANY)], micros=8.0
-    )(v, msg)
-    vlow, vhigh = ring(bulk)
+    msgs = across(call(copy_kernel, sds(msg.shape, BF16), [VMEM], micros=30.0)(msg))
+    low0, high0 = ring(first)
+    low1, high1 = ring(second)
 
     c2 = call(
         functools.partial(second_couple, all_blocks * size, ops, rank, far),
         sds((SLICES, body + STATS, LANES), BF16),
-        [SMEM, SMEM] + [VMEM] * (1 + count),
+        [SMEM, SMEM, ANY, ANY] + [VMEM] * (1 + count),
         [
             pltpu.VMEM((ops, n * blocks * rank, LANES), BF16),
             pltpu.VMEM((n, STATS, LANES), F32),
         ],
-    )(cols, group, held, *msgs)
+        micros=30.0,
+    )(cols, group, low0, high0, held, *msgs)
     c2 = exchange(c2)
 
     images, heights, norms = call(
         final_kernel,
         [sds((ops, rows, columns), F32), sds((ops, columns), F32), sds((ops, columns), F32)],
-        [VMEM] * 10,
+        [VMEM] * 13,
         [
             pltpu.VMEM((ops, 3, rows, columns), BF16),
             pltpu.VMEM((blocks, body, columns), BF16),
             pltpu.VMEM((STATS, columns), F32),
         ],
         micros=4.0,
-    )(w, low, sources, high, vlow, v, vhigh, self_terms, left, c2)
+    )(w, low, sources, high, low0, first, high0, low1, second, high1, self_terms, left, c2)
     return images, heights, norms
 
 

time: 90.8 us -> 93.8 us (1.033)
  starting transfers between devices: 24.7 us -> 45.7 us
  blocking collectives: 15.7 us -> 0 us
  waiting for transfers between devices: 27.9 us -> 20 us
  local copies, waits for them, and re-layouts: 4.28 us -> 8.01 us
  Pallas kernels: 17 us -> 18.6 us
    all_to_all x2 -> x0, blocking collectives: 15.7 us -> none  [exchange(): lax.all_to_all(x, 'store', 0, 0, axis_index_groups=groups, tiled=True)]
    all_to_all x2 -> x4, starting transfers between devices: 12.3 us -> 27.7 us  [exchange(): lax.all_to_all(x, 'store', 0, 0, axis_index_groups=groups, tiled=True)]
    ppermute x2, waiting for transfers between devices: 21 us -> 12.2 us  [across(): parts.append(lax.ppermute(x, 'store', pairs))]
    unnamed x18 -> x30, local copies, waits for them, and re-layouts: 4.2 us -> 7.93 us
    ppermute x2 -> x3, starting transfers between devices: 7.75 us -> 10.7 us  [ring(): lax.ppermute(block, 'store', backward)]
    ppermute x2, starting transfers between devices: 4.62 us -> 7.28 us  [across(): parts.append(lax.ppermute(x, 'store', pairs))]
    all_to_all x2 -> x4, waiting for transfers between devices: 6.85 us -> 7.79 us  [exchange(): lax.all_to_all(x, 'store', 0, 0, axis_index_groups=groups, tiled=True)]
    pallas_call x2 -> x3, Pallas kernels: 4.15 us -> 4.9 us  [the longest x1 2.72 us: shards(): call(near_kernel, sds((ops, rows, columns), F32), [VMEM] * 5, micros=3.0)]
  transfers between devices with their start and end apart: 8 -> 12, of which waited for: 4 -> 5; matrix products, arithmetic and copies ran while one was open for 0% -> 0% of each run, Pallas kernels for 6% -> 9%
where the time goes in v10:
time: 93.8 us; the launch traced here: 93.1 us
  starting transfers between devices  45.7 us (49%)
  waiting for transfers between devices  20 us (21%)
  Pallas kernels  18.6 us (20%)
  local copies, waits for them, and re-layouts  8.01 us (9%)
    all_to_all x4, starting transfers between devices, exchange(): lax.all_to_all(x, 'store', 0, 0, axis_index_groups=groups, tiled=True)  27.7 us
    ppermute x2, waiting for transfers between devices, across(): parts.append(lax.ppermute(x, 'store', pairs))  12.2 us
    ppermute x3, starting transfers between devices, ring(): lax.ppermute(block, 'store', backward)  10.7 us
    unnamed x30, local copies, waits for them, and re-layouts  7.93 us
    all_to_all x4, waiting for transfers between devices, exchange(): lax.all_to_all(x, 'store', 0, 0, axis_index_groups=groups, tiled=True)  7.79 us
    ppermute x2, starting transfers between devices, across(): parts.append(lax.ppermute(x, 'store', pairs))  7.28 us
    pallas_call x1, Pallas kernels, shards(): call(final_kernel, [sds((ops, rows, columns), F32), sds((ops, columns), F...  5.23 us
    pallas_call x1, Pallas kernels, shards(): call(near_kernel, sds((ops, rows, columns), F32), [VMEM] * 5, micros=3.0)  2.72 us
  transfers between devices with their start and end apart: 12, of which 5 were waited for; matrix products, arithmetic and copies ran while one was open for 0% of the time, Pallas kernels for 9%

profile of v10, /device:TPU:0, one launch (start us, length us, event | category | flops | bytes accessed | tf_op | source)
XLA Modules:
  0.0 93.1 jit_solution(2696537684553168809)
XLA Ops:
  0.6 0.0 copy-start.2
  0.6 0.0 copy-start.7
  0.7 2.0 %shard_map.115.refs_0_ = bf16[8,32,128]{2,1,0:T(8,128)(2,1)} custom-call(bf16[512,512]{1,0:T(8,128)(2,1)} %uown.1, bf16[2,32,256]{2,1,0:T(8,128)(2,1)} %bitcast.4), custom_call_target="tpu_custom_call" | custom-call | flops 1150000000 | tf_op jit(solution)/shard_map/pallas_call | solution.py:422
  2.6 0.0 copy-start.3
  2.6 4.0 %collective-permute-start.2 = (bf16[8,32,128]{2,1,0:T(8,128)(2,1)}, bf16[8,32,128]{2,1,0:T(8,128)(2,1)S(1)}, u32[]{:S(2)}, u32[]{:S(2)}) collective-permute-start(bf16[8,32,128]{2,1,0:T(8,128)(2,1)} %shard_map.115.refs_0_), channel_id=1, source_target_pairs={{0,8},{1,9},{2,10},{3,11},{4,12},{5,13},{6,14},{7,15},{8,0},{9,1},... | collective-permute-start | bytes 196616 | tf_op jit(solution)/shard_map/ppermute | solution.py:412
  6.7 0.0 copy-done.2
  6.7 0.0 copy-done.7
  6.7 0.7 shard_map.114.packed
  7.4 0.0 copy-start
  7.4 0.0 copy-start.8
  7.4 0.0 copy-start.9
  7.4 3.2 %collective-permute-done.2.refs_1_ = bf16[8,32,128]{2,1,0:T(8,128)(2,1)S(1)} collective-permute-done((bf16[8,32,128]{2,1,0:T(8,128)(2,1)}, bf16[8,32,128]{2,1,0:T(8,128)(2,1)S(1)}, u32[]{:S(2)}, u32[]{:S(2)}) %collective-permute-start.2) | collective-permute-done | bytes 65568 | tf_op jit(solution)/shard_map/ppermute | solution.py:412
  10.6 0.0 copy-done.3
  10.6 0.9 shard_map.116
  11.5 3.5 %all-to-all-start = ((bf16[8,272,128]{2,1,0:T(8,128)(2,1)}), bf16[8,272,128]{2,1,0:T(8,128)(2,1)S(1)}, u32[]{:S(2)}, u32[]{:S(2)}) async-start(bf16[8,272,128]{2,1,0:T(8,128)(2,1)} %shard_map.116), calls=%async_computation | async-start | bytes 1114112 | tf_op jit(solution)/shard_map/all_to_all | solution.py:406
  15.0 4.7 %collective-permute-start.1 = (bf16[512,512]{1,0:T(8,128)(2,1)}, bf16[512,512]{1,0:T(8,128)(2,1)}, u32[]{:S(2)}, u32[]{:S(2)}) collective-permute-start(bf16[512,512]{1,0:T(8,128)(2,1)} %uown.1), channel_id=1, source_target_pairs={{1,0},{2,1},{3,2},{4,3},{5,4},{6,5},{7,6},{8,7},{9,8},{10,9},{11,1... | collective-permute-start | bytes 1572872 | tf_op jit(solution)/shard_map/ppermute | solution.py:380
  19.7 0.0 collective-permute-start
  19.7 0.0 copy-done
  19.7 0.0 copy-done.8
  19.7 0.0 copy-done.9
  19.7 0.9 shard_map.112.w
  20.6 0.0 copy-start.10
  20.6 1.5 %copy-done.10 = bf16[2,512,1280]{2,1,0:T(8,128)(2,1)} copy-done((bf16[2,512,1280]{2,1,0:T(8,128)(2,1)}, bf16[2,512,1280]{2,1,0:T(8,128)(2,1)S(1)}, u32[]{:S(2)}) %copy-start.10) | copy-done | bytes 2621464
  22.2 0.0 copy-start.1
  22.2 0.0 copy-start.6
  22.2 2.0 %all-to-all-done.held = bf16[8,272,128]{2,1,0:T(8,128)(2,1)S(1)} async-done(((bf16[8,272,128]{2,1,0:T(8,128)(2,1)}), bf16[8,272,128]{2,1,0:T(8,128)(2,1)S(1)}, u32[]{:S(2)}, u32[]{:S(2)}) %all-to-all-start) | async-done | bytes 557088 | tf_op jit(solution)/shard_map/all_to_all | solution.py:406
  24.2 0.1 reshape.18.cols
  24.2 1.8 %shard_map.117 = bf16[8,64,128]{2,1,0:T(8,128)(2,1)} custom-call(s32[96]{0:T(128)S(1)} %reshape.18.cols, s32[1]{0:T(128)} %bitcast.3.group, bf16[8,272,128]{2,1,0:T(8,128)(2,1)S(1)} %all-to-all-done.held), custom_call_target="tpu_custom_call" | custom-call | flops 1150000000 | tf_op jit(solution)/shard_map/pallas_call | solution.py:445
  26.0 8.6 %all-to-all-start.1 = ((bf16[8,64,128]{2,1,0:T(8,128)(2,1)}), bf16[8,64,128]{2,1,0:T(8,128)(2,1)S(1)}, u32[]{:S(2)}, u32[]{:S(2)}) async-start(bf16[8,64,128]{2,1,0:T(8,128)(2,1)} %shard_map.117), calls=%async_computation.1 | async-start | bytes 262144 | tf_op jit(solution)/shard_map/all_to_all | solution.py:406
  34.7 0.0 copy-start.4
  34.7 0.0 copy-start.5
  34.7 0.0 collective-permute-done.1.high.uhigh
  34.7 0.0 collective-permute-done.low.ulow
  34.7 0.0 copy-done.1
  34.7 0.0 copy-done.6
  34.7 0.0 copy-start.11
  34.7 1.7 %copy-done.11 = bf16[2,512,1280]{2,1,0:T(8,128)(2,1)S(1)} copy-done((bf16[2,512,1280]{2,1,0:T(8,128)(2,1)S(1)}, bf16[2,512,1280]{2,1,0:T(8,128)(2,1)}, u32[]{:S(2)}) %copy-start.11) | copy-done | bytes 2621464
  36.5 2.7 %shard_map.113.near = f32[2,512,512]{2,1,0:T(8,128)S(1)} custom-call(bf16[2,512,1280]{2,1,0:T(8,128)(2,1)S(1)} %copy-done.11, bf16[512,512]{1,0:T(8,128)(2,1)} %collective-permute-done.low.ulow, bf16[512,512]{1,0:T(8,128)(2,1)S(1)} %copy-done.1, bf16[512,512]{1,0:T(8,128)(2,1)} %collective-permute-done.1.high.uhigh, f32[2,512]{1,0:T(2,128)S(1)} %copy-done.6), custom_call_target="tpu_custom_call" | custom-call | flops 3449999872 | tf_op jit(solution)/shard_map/pallas_call | solution.py:453
  39.2 0.0 copy-start.13
  39.2 1.3 %copy-done.13 = f32[2,512,512]{2,1,0:T(8,128)} copy-done((f32[2,512,512]{2,1,0:T(8,128)}, f32[2,512,512]{2,1,0:T(8,128)S(1)}, u32[]{:S(2)}) %copy-start.13) | copy-done | bytes 2097176
  40.5 0.0 all-to-all-done.1.cmsg
  40.5 0.0 copy-done.4
  40.5 0.0 copy-done.5
  40.5 0.0 copy-start.14
  40.5 1.6 %copy-done.14 = f32[2,512,512]{2,1,0:T(8,128)S(1)} copy-done((f32[2,512,512]{2,1,0:T(8,128)S(1)}, f32[2,512,512]{2,1,0:T(8,128)}, u32[]{:S(2)}) %copy-start.14) | copy-done | bytes 2097176
  42.1 2.2 %shard_map.118 = (bf16[528,512]{1,0:T(8,128)(2,1)S(1)}, bf16[512,512]{1,0:T(8,128)(2,1)S(1)}, bf16[8,80,128]{2,1,0:T(8,128)(2,1)}) custom-call(bf16[512,512]{1,0:T(8,128)(2,1)S(1)} %copy-done.1, f32[2,512,512]{2,1,0:T(8,128)S(1)} %copy-done.14, bf16[2,32,256]{2,1,0:T(8,128)(2,1)S(1)} %bitcast.6, bf16[2,32,256]{2,1,0:T(8,128)(2,1)S(1)} %bitcast.5, ...), custom_call_target="tpu_custom_call" | custom-call | flops 2300000000 | tf_op jit(solution)/shard_map/pallas_call | solution.py:456
  44.3 4.2 %all-to-all-start.2 = ((bf16[8,80,128]{2,1,0:T(8,128)(2,1)}), bf16[8,80,128]{2,1,0:T(8,128)(2,1)S(1)}, u32[]{:S(2)}, u32[]{:S(2)}) async-start(bf16[8,80,128]{2,1,0:T(8,128)(2,1)} %get-tuple-element.8), calls=%async_computation.2 | async-start | bytes 327680 | tf_op jit(solution)/shard_map/all_to_all | solution.py:406
  48.5 5.1 %collective-permute-start.4 = (bf16[528,512]{1,0:T(8,128)(2,1)S(1)}, bf16[528,512]{1,0:T(8,128)(2,1)S(1)}, u32[]{:S(2)}, u32[]{:S(2)}) collective-permute-start(bf16[528,512]{1,0:T(8,128)(2,1)S(1)} %get-tuple-element.6.first), channel_id=1, source_target_pairs={{1,0},{2,1},{3,2},{4,3},{5,4},{6,5},{7,6},{8,7},{9,8},{10,9},{11,1... | collective-permute-start | bytes 1622024 | tf_op jit(solution)/shard_map/ppermute | solution.py:380
  53.5 0.0 collective-permute-start.3
  53.5 0.4 all-to-all-done.2.source
  53.9 3.2 %collective-permute-start.7 = (bf16[8,80,128]{2,1,0:T(8,128)(2,1)S(1)}, bf16[8,80,128]{2,1,0:T(8,128)(2,1)S(1)}, u32[]{:S(2)}, u32[]{:S(2)}) collective-permute-start(bf16[8,80,128]{2,1,0:T(8,128)(2,1)S(1)} %shard_map.119.refs_0_), channel_id=1, source_target_pairs={{0,8},{1,9},{2,10},{3,11},{4,12},{5,13},{6,14},{7,15},{8,0},{9,1},... | collective-permute-start | bytes 491528 | tf_op jit(solution)/shard_map/ppermute | solution.py:412
  57.2 0.9 %collective-permute-start.6 = (bf16[512,512]{1,0:T(8,128)(2,1)S(1)}, bf16[512,512]{1,0:T(8,128)(2,1)}, u32[]{:S(2)}, u32[]{:S(2)}) collective-permute-start(bf16[512,512]{1,0:T(8,128)(2,1)S(1)} %get-tuple-element.7.second), channel_id=1, source_target_pairs={{1,0},{2,1},{3,2},{4,3},{5,4},{6,5},{7,6},{8,7},{9,8},{10,9},{11,1... | collective-permute-start | bytes 1572872 | tf_op jit(solution)/shard_map/ppermute | solution.py:380
  58.1 0.0 collective-permute-start.5
  58.1 9.0 %collective-permute-done.7.refs_1_ = bf16[8,80,128]{2,1,0:T(8,128)(2,1)S(1)} collective-permute-done((bf16[8,80,128]{2,1,0:T(8,128)(2,1)S(1)}, bf16[8,80,128]{2,1,0:T(8,128)(2,1)S(1)}, u32[]{:S(2)}, u32[]{:S(2)}) %collective-permute-start.7) | collective-permute-done | bytes 163872 | tf_op jit(solution)/shard_map/ppermute | solution.py:412
  67.1 0.0 collective-permute-done.4.after_high.high0
  67.1 0.0 collective-permute-done.3.after_low.low0
  67.1 2.3 %shard_map.120 = bf16[8,80,128]{2,1,0:T(8,128)(2,1)} custom-call(s32[96]{0:T(128)S(1)} %reshape.18.cols, s32[1]{0:T(128)} %bitcast.3.group, bf16[528,512]{1,0:T(8,128)(2,1)S(1)} %collective-permute-done.3.after_low.low0, bf16[528,512]{1,0:T(8,128)(2,1)S(1)} %collective-permute-done.4.after_high.high0, bf16[8,272,128]{2,1,0:T(8,128)(2,1)S(1)} %all-to-all-done.held, ...), custom_call_target="tpu_custom_call" | custom-call | flops 34500001792 | tf_op jit(solution)/shard_map/pallas_call | solution.py:475
  69.4 11.3 %all-to-all-start.3 = ((bf16[8,80,128]{2,1,0:T(8,128)(2,1)}), bf16[8,80,128]{2,1,0:T(8,128)(2,1)S(1)}, u32[]{:S(2)}, u32[]{:S(2)}) async-start(bf16[8,80,128]{2,1,0:T(8,128)(2,1)} %shard_map.120), calls=%async_computation.3 | async-start | bytes 327680 | tf_op jit(solution)/shard_map/all_to_all | solution.py:406
  80.7 0.0 collective-permute-done.6.high1
  80.7 0.0 collective-permute-done.5.low1
  80.7 5.4 %all-to-all-done.3.cmsg = bf16[8,80,128]{2,1,0:T(8,128)(2,1)S(1)} async-done(((bf16[8,80,128]{2,1,0:T(8,128)(2,1)}), bf16[8,80,128]{2,1,0:T(8,128)(2,1)S(1)}, u32[]{:S(2)}, u32[]{:S(2)}) %all-to-all-start.3) | async-done | bytes 163872 | tf_op jit(solution)/shard_map/all_to_all | solution.py:406
  86.2 0.0 copy-start.12
  86.2 1.7 %copy-done.12 = bf16[2,512,1280]{2,1,0:T(8,128)(2,1)S(1)} copy-done((bf16[2,512,1280]{2,1,0:T(8,128)(2,1)S(1)}, bf16[2,512,1280]{2,1,0:T(8,128)(2,1)}, u32[]{:S(2)}) %copy-start.12) | copy-done | bytes 2621464
  87.9 5.2 %shard_map.121 = (f32[2,512,512]{2,1,0:T(8,128)}, f32[2,512]{1,0:T(2,128)}, f32[2,512]{1,0:T(2,128)}) custom-call(bf16[2,512,1280]{2,1,0:T(8,128)(2,1)S(1)} %copy-done.12, bf16[512,512]{1,0:T(8,128)(2,1)} %collective-permute-done.low.ulow, bf16[512,512]{1,0:T(8,128)(2,1)S(1)} %copy-done.1, bf16[512,512]{1,0:T(8,128)(2,1)} %collective-permute-done.1.high.uhigh, ...), custom_call_target="tpu_custom_call" | custom-call | flops 4600000000 | tf_op jit(solution)/shard_map/pallas_call | solution.py:487
  (2 shorter events, 0.0 us)
Async XLA Ops:
  0.6 6.0 %copy-start.2 = (bf16[2,2,6,32,32]{4,3,2,1,0:T(8,128)(2,1)S(1)}, bf16[2,2,6,32,32]{4,3,2,1,0:T(8,128)(2,1)}, u32[]{:S(2)}) copy-start(bf16[2,2,6,32,32]{4,3,2,1,0:T(8,128)(2,1)} %coup.1) | copy-start | bytes 147460
  0.6 6.0 %copy-start.7 = (s32[2,6]{1,0:T(2,128)S(1)}, s32[2,6]{1,0:T(2,128)}, u32[]{:S(2)}) copy-start(s32[2,6]{1,0:T(2,128)} %far_cols.1) | copy-start | bytes 148
  2.6 8.0 %copy-start.3 = (bf16[8,32,128]{2,1,0:T(8,128)(2,1)S(1)}, bf16[8,32,128]{2,1,0:T(8,128)(2,1)}, u32[]{:S(2)}) copy-start(bf16[8,32,128]{2,1,0:T(8,128)(2,1)} %shard_map.115.refs_0_) | copy-start | bytes 196612
  2.6 8.0 %collective-permute-start.2 = (bf16[8,32,128]{2,1,0:T(8,128)(2,1)}, bf16[8,32,128]{2,1,0:T(8,128)(2,1)S(1)}, u32[]{:S(2)}, u32[]{:S(2)}) collective-permute-start(bf16[8,32,128]{2,1,0:T(8,128)(2,1)} %shard_map.115.refs_0_), channel_id=1, source_target_pairs={{0,8},{1,9},{2,10},{3,11},{4,12},{5,13},{6,14},{7,15},{8,0},{9,1},... | collective-permute-start | bytes 196616 | tf_op jit(solution)/shard_map/ppermute | solution.py:412
  7.4 12.3 %copy-start = (bf16[2,2,5,256,256]{4,3,2,1,0:T(8,128)(2,1)S(1)}, bf16[2,2,5,256,256]{4,3,2,1,0:T(8,128)(2,1)}, u32[]{:S(2)}) copy-start(bf16[2,2,5,256,256]{4,3,2,1,0:T(8,128)(2,1)} %tiles.1) | copy-start | bytes 7864324
  7.4 12.3 %copy-start.8 = (s32[2,5]{1,0:T(2,128)S(1)}, s32[2,5]{1,0:T(2,128)}, u32[]{:S(2)}) copy-start(s32[2,5]{1,0:T(2,128)} %cols.1) | copy-start | bytes 124
  7.4 12.3 %copy-start.9 = (s32[2]{0:T(128)S(1)}, s32[2]{0:T(128)}, u32[]{:S(2)}) copy-start(s32[2]{0:T(128)} %count.1) | copy-start | bytes 28
  11.5 12.7 %all-to-all-start = ((bf16[8,272,128]{2,1,0:T(8,128)(2,1)}), bf16[8,272,128]{2,1,0:T(8,128)(2,1)S(1)}, u32[]{:S(2)}, u32[]{:S(2)}) async-start(bf16[8,272,128]{2,1,0:T(8,128)(2,1)} %shard_map.116), calls=%async_computation | async-start | bytes 1114112 | tf_op jit(solution)/shard_map/all_to_all | solution.py:406
  15.0 19.7 %collective-permute-start.1 = (bf16[512,512]{1,0:T(8,128)(2,1)}, bf16[512,512]{1,0:T(8,128)(2,1)}, u32[]{:S(2)}, u32[]{:S(2)}) collective-permute-start(bf16[512,512]{1,0:T(8,128)(2,1)} %uown.1), channel_id=1, source_target_pairs={{1,0},{2,1},{3,2},{4,3},{5,4},{6,5},{7,6},{8,7},{9,8},{10,9},{11,1... | collective-permute-start | bytes 1572872 | tf_op jit(solution)/shard_map/ppermute | solution.py:380
  19.7 15.0 %collective-permute-start = (bf16[512,512]{1,0:T(8,128)(2,1)}, bf16[512,512]{1,0:T(8,128)(2,1)}, u32[]{:S(2)}, u32[]{:S(2)}) collective-permute-start(bf16[512,512]{1,0:T(8,128)(2,1)} %uown.1), channel_id=1, source_target_pairs={{0,1},{1,2},{2,3},{3,4},{4,5},{5,6},{6,7},{7,8},{8,9},{9,10},{10,1... | collective-permute-start | bytes 1572872 | tf_op jit(solution)/shard_map/ppermute | solution.py:380
  20.6 1.5 %copy-start.10 = (bf16[2,512,1280]{2,1,0:T(8,128)(2,1)}, bf16[2,512,1280]{2,1,0:T(8,128)(2,1)S(1)}, u32[]{:S(2)}) copy-start(bf16[2,512,1280]{2,1,0:T(8,128)(2,1)S(1)} %shard_map.112.w) | copy-start | bytes 7864324
  22.2 12.6 %copy-start.1 = (bf16[512,512]{1,0:T(8,128)(2,1)S(1)}, bf16[512,512]{1,0:T(8,128)(2,1)}, u32[]{:S(2)}) copy-start(bf16[512,512]{1,0:T(8,128)(2,1)} %uown.1) | copy-start | bytes 1572868
  22.2 12.6 %copy-start.6 = (f32[2,512]{1,0:T(2,128)S(1)}, f32[2,512]{1,0:T(2,128)}, u32[]{:S(2)}) copy-start(f32[2,512]{1,0:T(2,128)} %diag.3) | copy-start | bytes 12292
  26.0 14.5 %all-to-all-start.1 = ((bf16[8,64,128]{2,1,0:T(8,128)(2,1)}), bf16[8,64,128]{2,1,0:T(8,128)(2,1)S(1)}, u32[]{:S(2)}, u32[]{:S(2)}) async-start(bf16[8,64,128]{2,1,0:T(8,128)(2,1)} %shard_map.117), calls=%async_computation.1 | async-start | bytes 262144 | tf_op jit(solution)/shard_map/all_to_all | solution.py:406
  34.7 5.9 %copy-start.4 = (bf16[2,256,32]{1,2,0:T(8,128)(2,1)S(1)}, bf16[2,256,32]{1,2,0:T(8,128)(2,1)}, u32[]{:S(2)}) copy-start(bf16[2,256,32]{1,2,0:T(8,128)(2,1)} %param.16) | copy-start | bytes 98308
  34.7 5.8 %copy-start.5 = (bf16[2,256,32]{1,2,0:T(8,128)(2,1)S(1)}, bf16[2,256,32]{1,2,0:T(8,128)(2,1)}, u32[]{:S(2)}) copy-start(bf16[2,256,32]{1,2,0:T(8,128)(2,1)} %param.15) | copy-start | bytes 98308
  34.7 1.7 %copy-start.11 = (bf16[2,512,1280]{2,1,0:T(8,128)(2,1)S(1)}, bf16[2,512,1280]{2,1,0:T(8,128)(2,1)}, u32[]{:S(2)}) copy-start(bf16[2,512,1280]{2,1,0:T(8,128)(2,1)} %copy-done.10) | copy-start | bytes 7864324
  39.2 1.3 %copy-start.13 = (f32[2,512,512]{2,1,0:T(8,128)}, f32[2,512,512]{2,1,0:T(8,128)S(1)}, u32[]{:S(2)}) copy-start(f32[2,512,512]{2,1,0:T(8,128)S(1)} %shard_map.113.near) | copy-start | bytes 6291460
  40.5 1.6 %copy-start.14 = (f32[2,512,512]{2,1,0:T(8,128)S(1)}, f32[2,512,512]{2,1,0:T(8,128)}, u32[]{:S(2)}) copy-start(f32[2,512,512]{2,1,0:T(8,128)} %copy-done.13) | copy-start | bytes 6291460
  44.3 9.6 %all-to-all-start.2 = ((bf16[8,80,128]{2,1,0:T(8,128)(2,1)}), bf16[8,80,128]{2,1,0:T(8,128)(2,1)S(1)}, u32[]{:S(2)}, u32[]{:S(2)}) async-start(bf16[8,80,128]{2,1,0:T(8,128)(2,1)} %get-tuple-element.8), calls=%async_computation.2 | async-start | bytes 327680 | tf_op jit(solution)/shard_map/all_to_all | solution.py:406
  48.5 18.6 %collective-permute-start.4 = (bf16[528,512]{1,0:T(8,128)(2,1)S(1)}, bf16[528,512]{1,0:T(8,128)(2,1)S(1)}, u32[]{:S(2)}, u32[]{:S(2)}) collective-permute-start(bf16[528,512]{1,0:T(8,128)(2,1)S(1)} %get-tuple-element.6.first), channel_id=1, source_target_pairs={{1,0},{2,1},{3,2},{4,3},{5,4},{6,5},{7,6},{8,7},{9,8},{10,9},{11,1... | collective-permute-start | bytes 1622024 | tf_op jit(solution)/shard_map/ppermute | solution.py:380
  53.5 13.6 %collective-permute-start.3 = (bf16[528,512]{1,0:T(8,128)(2,1)S(1)}, bf16[528,512]{1,0:T(8,128)(2,1)S(1)}, u32[]{:S(2)}, u32[]{:S(2)}) collective-permute-start(bf16[528,512]{1,0:T(8,128)(2,1)S(1)} %get-tuple-element.6.first), channel_id=1, source_target_pairs={{0,1},{1,2},{2,3},{3,4},{4,5},{5,6},{6,7},{7,8},{8,9},{9,10},{10,1... | collective-permute-start | bytes 1622024 | tf_op jit(solution)/shard_map/ppermute | solution.py:380
  53.9 13.2 %collective-permute-start.7 = (bf16[8,80,128]{2,1,0:T(8,128)(2,1)S(1)}, bf16[8,80,128]{2,1,0:T(8,128)(2,1)S(1)}, u32[]{:S(2)}, u32[]{:S(2)}) collective-permute-start(bf16[8,80,128]{2,1,0:T(8,128)(2,1)S(1)} %shard_map.119.refs_0_), channel_id=1, source_target_pairs={{0,8},{1,9},{2,10},{3,11},{4,12},{5,13},{6,14},{7,15},{8,0},{9,1},... | collective-permute-start | bytes 491528 | tf_op jit(solution)/shard_map/ppermute | solution.py:412
  57.2 23.6 %collective-permute-start.6 = (bf16[512,512]{1,0:T(8,128)(2,1)S(1)}, bf16[512,512]{1,0:T(8,128)(2,1)}, u32[]{:S(2)}, u32[]{:S(2)}) collective-permute-start(bf16[512,512]{1,0:T(8,128)(2,1)S(1)} %get-tuple-element.7.second), channel_id=1, source_target_pairs={{1,0},{2,1},{3,2},{4,3},{5,4},{6,5},{7,6},{8,7},{9,8},{10,9},{11,1... | collective-permute-start | bytes 1572872 | tf_op jit(solution)/shard_map/ppermute | solution.py:380
  58.1 22.6 %collective-permute-start.5 = (bf16[512,512]{1,0:T(8,128)(2,1)S(1)}, bf16[512,512]{1,0:T(8,128)(2,1)}, u32[]{:S(2)}, u32[]{:S(2)}) collective-permute-start(bf16[512,512]{1,0:T(8,128)(2,1)S(1)} %get-tuple-element.7.second), channel_id=1, source_target_pairs={{0,1},{1,2},{2,3},{3,4},{4,5},{5,6},{6,7},{7,8},{8,9},{9,10},{10,1... | collective-permute-start | bytes 1572872 | tf_op jit(solution)/shard_map/ppermute | solution.py:380
  69.4 16.8 %all-to-all-start.3 = ((bf16[8,80,128]{2,1,0:T(8,128)(2,1)}), bf16[8,80,128]{2,1,0:T(8,128)(2,1)S(1)}, u32[]{:S(2)}, u32[]{:S(2)}) async-start(bf16[8,80,128]{2,1,0:T(8,128)(2,1)} %shard_map.120), calls=%async_computation.3 | async-start | bytes 327680 | tf_op jit(solution)/shard_map/all_to_all | solution.py:406
  86.2 1.7 %copy-start.12 = (bf16[2,512,1280]{2,1,0:T(8,128)(2,1)S(1)}, bf16[2,512,1280]{2,1,0:T(8,128)(2,1)}, u32[]{:S(2)}) copy-start(bf16[2,512,1280]{2,1,0:T(8,128)(2,1)} %copy-done.10) | copy-start | bytes 7864324

commit v11 on v7

--- a/solution.py
+++ b/solution.py
@@ -13,25 +13,28 @@
 HALF = 64
 SLICES = 8
 STATS = 16
-HBM_RATE = 3690000
+FLOP_RATE = 1150000000
 F32 = jnp.float32
 BF16 = jnp.bfloat16
 
 VMEM = pl.BlockSpec(memory_space=pltpu.VMEM)
 SMEM = pl.BlockSpec(memory_space=pltpu.SMEM)
-
-
-def call(body, out_shape, in_specs, scratch=(), micros=1.0, megabytes=20):
+ANY = pl.BlockSpec(memory_space=pl.ANY)
+
+
+def call(body, out_shape, in_specs, scratch=(), micros=1.0, megabytes=20, out_specs=None):
     many = isinstance(out_shape, (list, tuple))
+    if out_specs is None:
+        out_specs = [VMEM] * len(out_shape) if many else VMEM
     return pl.pallas_call(
         body,
         out_shape=out_shape,
         in_specs=in_specs,
-        out_specs=[VMEM] * len(out_shape) if many else VMEM,
+        out_specs=out_specs,
         scratch_shapes=list(scratch),
         compiler_params=pltpu.CompilerParams(vmem_limit_bytes=megabytes * 1024 * 1024),
         cost_estimate=pl.CostEstimate(
-            flops=0, bytes_accessed=int(micros * HBM_RATE), transcendentals=0
+            flops=int(micros * FLOP_RATE), bytes_accessed=0, transcendentals=0
         ),
     )
 
@@ -67,32 +70,46 @@
     return x[:, pair * LANES:(pair + 1) * LANES]
 
 
-def order_tiles(all_blocks, cols, count, row0, tiles, out):
+def fetch_tiles(all_blocks, cols, count, row0, tiles, w, sems):
     ops, blocks, near, size, _ = tiles.shape
+    steps = []
     for b in range(blocks):
         for k in range(near):
             rel = lax.rem(cols[b, k] - (row0[0] + b) + REACH + all_blocks, all_blocks)
-            rel = lax.rem(rel, all_blocks)
-            at = pl.multiple_of(rel * size, size)
+            at = pl.multiple_of(lax.rem(rel, all_blocks) * size, size)
             live = k < count[b]
             for o in range(ops):
-                tile = tiles[o, b, k]
-                out[b, o * size:(o + 1) * size, pl.ds(at, size)] = jnp.where(
-                    live, tile, jnp.zeros_like(tile)
-                )
-
-
-def coeff_kernel(u, right, out):
-    blocks, rank, size = right.shape
+                place = w.at[b, o * size:(o + 1) * size, pl.ds(at, size)]
+                copy = pltpu.make_async_copy(tiles.at[o, b, k], place, sems.at[b, k, o])
+                steps.append((live, copy, place))
+    for live, copy, place in steps:
+
+        @pl.when(live)
+        def _(copy=copy):
+            copy.start()
+
+        @pl.when(jnp.logical_not(live))
+        def _(place=place):
+            place[...] = jnp.zeros_like(place)
+
+    def wait():
+        for live, copy, _ in steps:
+
+            @pl.when(live)
+            def _(copy=copy):
+                copy.wait()
+
+    return wait
+
+
+def coeff_kernel(far_cols, u, right, coup, z_out, out):
+    ops, blocks, far, rank, _ = coup.shape
+    size = right.shape[2]
     z = [dot(right[b], u[b * size:(b + 1) * size, :]) for b in range(blocks)]
     for pair in range(SLICES // 2):
         first, second = halves(chunk(z[0], pair), chunk(z[1], pair))
-        out[2 * pair] = first.astype(BF16)
-        out[2 * pair + 1] = second.astype(BF16)
-
-
-def pack_kernel(far_cols, coup, out):
-    ops, blocks, far, rank, _ = coup.shape
+        z_out[2 * pair] = first.astype(BF16)
+        z_out[2 * pair + 1] = second.astype(BF16)
     whole, rest = [], []
     for b in range(blocks):
         tiles = [
@@ -121,10 +138,6 @@
         out[:, rows + m * rank:rows + (m + 1) * rank, :] = part[...]
 
 
-def copy_kernel(source, after, target):
-    target[...] = source[...]
-
-
 def coupling_rows(held, s, b, ops, rank):
     body = ops * rank
     first = held[s, b * body:(b + 1) * body, :]
@@ -205,11 +218,32 @@
     return jnp.concatenate([column] * (columns // LANES), axis=1)
 
 
-def image_kernel(w, low, own, high, diag, left, right, cmsg, vout, mout, image, coef):
+def image_kernel(
+    all_blocks,
+    cols,
+    count,
+    row0,
+    tiles,
+    low,
+    own,
+    high,
+    diag,
+    left,
+    right,
+    cmsg,
+    vout,
+    mout,
+    image,
+    coef,
+    w,
+    sems,
+):
+    wait = fetch_tiles(all_blocks, cols, count, row0, tiles, w, sems)
     ops = image.shape[0]
     blocks, rank, size = right.shape
     rows, columns = own.shape
     take_coefs(cmsg, coef, ops * rank)
+    wait()
     inner = [None] * ops
     squares = None
     for b in range(blocks):
@@ -305,8 +339,33 @@
 
 
 def final_kernel(
-    w, ulow, uown, uhigh, vlow, vown, vhigh, diag, left, cmsg, images, heights, norms, ext, coef, stat
+    all_blocks,
+    cols,
+    count,
+    row0,
+    tiles,
+    ulow,
+    uown,
+    uhigh,
+    vlow,
+    vown,
+    vhigh,
+    diag,
+    left,
+    cmsg,
+    images,
+    heights,
+    norms,
+    ext,
+    coef,
+    stat,
+    out,
+    w,
+    sems,
+    outs,
 ):
+    wait = fetch_tiles(all_blocks, cols, count, row0, tiles, w, sems)
+    copies = []
     ops = images.shape[0]
     blocks, rank, size = left.shape
     rows, columns = uown.shape
@@ -330,16 +389,24 @@
             change = (shift - height) * factor
             value = v[o * rows:(o + 1) * rows, :].astype(F32) * factor + u[...].astype(F32) * change
             ext[o, at] = value.astype(BF16)
+        if o == 0:
+            wait()
         for b in range(blocks):
             parts = [ext.at[o, at] for at in range(3)]
             product = near_product(w.at[b, o * size:(o + 1) * size], parts, b, blocks, size)
             far = dot(left[b], coef[b, o * rank:(o + 1) * rank, :], ((0,), (0,)))
             mine = ext[o, 1, b * size:(b + 1) * size, :].astype(F32)
-            images[o, b * size:(b + 1) * size, :] = (
+            here = slice(b * size, (b + 1) * size)
+            out[o, here, :] = (
                 product
                 + diagonal_of(diag, o, b, size, columns) * mine
                 + far.astype(BF16).astype(F32)
             )
+            copy = pltpu.make_async_copy(out.at[o, here], images.at[o, here], outs.at[o, b])
+            copy.start()
+            copies.append(copy)
+    for copy in copies:
+        copy.wait()
 
 
 def ring(block):
@@ -388,14 +455,14 @@
     right = jnp.transpose(basis_right, (0, 2, 1))
 
     low, high = ring(sources)
-    z1 = call(coeff_kernel, sds((SLICES, rank, LANES), BF16), [VMEM, VMEM], megabytes=60)(
-        sources, right
-    )
+    shared = (blocks + 1) * body
+    z1, packed = call(
+        coeff_kernel,
+        [sds((SLICES, rank, LANES), BF16), sds((shared + STATS, LANES), BF16)],
+        [SMEM, VMEM, VMEM, VMEM],
+        megabytes=60,
+    )(far_cols, sources, right, couplings)
     z1 = across(z1)
-    shared = (blocks + 1) * body
-    packed = call(pack_kernel, sds((shared + STATS, LANES), BF16), [SMEM, VMEM])(
-        far_cols, couplings
-    )
     held = call(
         share_kernel,
         sds((SLICES, shared + STATS + count * rank, LANES), BF16),
@@ -404,13 +471,6 @@
     held = exchange(held)
     cols = held[:, shared, :blocks * far].astype(jnp.int32).reshape(-1)
 
-    w = call(
-        functools.partial(order_tiles, all_blocks),
-        sds((blocks, ops * size, near * size), BF16),
-        [SMEM, SMEM, SMEM, VMEM],
-        micros=2.5,
-    )(near_cols, near_count, row0, near_tiles)
-
     c1 = call(
         functools.partial(first_couple, ops, rank, far),
         sds((SLICES, body, LANES), BF16),
@@ -419,22 +479,24 @@
     )(cols, group, held)
     c1 = exchange(c1)
 
+    places = [SMEM, SMEM, SMEM, ANY]
+    tile_scratch = [
+        pltpu.VMEM((blocks, ops * size, near * size), BF16),
+        pltpu.SemaphoreType.DMA((blocks, near, ops)),
+    ]
     v, msg = call(
-        image_kernel,
+        functools.partial(image_kernel, all_blocks),
         [sds((ops * rows + STATS, columns), BF16), sds((SLICES, body + STATS, LANES), BF16)],
-        [VMEM] * 8,
+        places + [VMEM] * 7,
         [
             pltpu.VMEM((ops, rows, columns), F32),
             pltpu.VMEM((blocks, body, columns), BF16),
-        ],
+        ]
+        + tile_scratch,
         micros=4.0,
-    )(w, low, sources, high, self_terms, left, right, c1)
-    msg = exchange(msg)
-    msgs = across(msg)
-    bulk = call(
-        copy_kernel, sds(v.shape, BF16), [VMEM, pl.BlockSpec(memory_space=pl.ANY)], micros=8.0
-    )(v, msg)
-    vlow, vhigh = ring(bulk)
+    )(near_cols, near_count, row0, near_tiles, low, sources, high, self_terms, left, right, c1)
+    msgs = across(exchange(msg))
+    vlow, vhigh = ring(v)
 
     c2 = call(
         functools.partial(second_couple, all_blocks * size, ops, rank, far),
@@ -444,20 +506,39 @@
             pltpu.VMEM((ops, n * blocks * rank, LANES), BF16),
             pltpu.VMEM((n, STATS, LANES), F32),
         ],
+        micros=30.0,
     )(cols, group, held, *msgs)
     c2 = exchange(c2)
 
     images, heights, norms = call(
-        final_kernel,
+        functools.partial(final_kernel, all_blocks),
         [sds((ops, rows, columns), F32), sds((ops, columns), F32), sds((ops, columns), F32)],
-        [VMEM] * 10,
+        places + [VMEM] * 9,
         [
             pltpu.VMEM((ops, 3, rows, columns), BF16),
             pltpu.VMEM((blocks, body, columns), BF16),
             pltpu.VMEM((STATS, columns), F32),
-        ],
+            pltpu.VMEM((ops, rows, columns), F32),
+        ]
+        + tile_scratch
+        + [pltpu.SemaphoreType.DMA((ops, blocks))],
         micros=4.0,
-    )(w, low, sources, high, vlow, v, vhigh, self_terms, left, c2)
+        out_specs=[ANY, VMEM, VMEM],
+    )(
+        near_cols,
+        near_count,
+        row0,
+        near_tiles,
+        low,
+        sources,
+        high,
+        vlow,
+        v,
+        vhigh,
+        self_terms,
+        left,
+        c2,
+    )
     return images, heights, norms
 
 

time: 90.8 us -> 92.3 us (1.017)
  blocking collectives: 15.7 us -> 26.7 us
  waiting for transfers between devices: 27.9 us -> 20.5 us
  local copies, waits for them, and re-layouts: 4.28 us -> 1.76 us
    all_to_all x2, blocking collectives: 15.7 us -> 26.7 us  [exchange(): lax.all_to_all(x, 'store', 0, 0, axis_index_groups=groups, tiled=True)]
    ppermute x2, waiting for transfers between devices: 21 us -> 11 us  [across(): parts.append(lax.ppermute(x, 'store', pairs))]
    ppermute x2, starting transfers between devices: 7.75 us -> 4.75 us  [ring(): lax.ppermute(block, 'store', backward)]
    all_to_all x2, waiting for transfers between devices: 6.85 us -> 9.52 us  [exchange(): lax.all_to_all(x, 'store', 0, 0, axis_index_groups=groups, tiled=True)]
    unnamed x18 -> x16, local copies, waits for them, and re-layouts: 4.2 us -> 1.68 us
    ppermute x2, starting transfers between devices: 4.62 us -> 7.04 us  [across(): parts.append(lax.ppermute(x, 'store', pairs))]
    pallas_call x6 -> x3, Pallas kernels: 12.7 us -> 13.3 us  [the longest x1 6.58 us: shards(): call(functools.partial(final_kernel, all_blocks), [sds((ops, rows, column...]
  transfers between devices with their start and end apart: 8 -> 8, of which waited for: 4 -> 4; matrix products, arithmetic and copies ran while one was open for 0% -> 0% of each run, Pallas kernels for 6% -> 4%
where the time goes in v11:
time: 92.3 us; the launch traced here: 91.8 us
  blocking collectives  26.7 us (29%)
  starting transfers between devices  24.5 us (27%)
  waiting for transfers between devices  20.5 us (22%)
  Pallas kernels  17.6 us (19%)
  local copies, waits for them, and re-layouts  1.76 us (2%)
    all_to_all x2, blocking collectives, exchange(): lax.all_to_all(x, 'store', 0, 0, axis_index_groups=groups, tiled=True)  26.7 us
    all_to_all x2, starting transfers between devices, exchange(): lax.all_to_all(x, 'store', 0, 0, axis_index_groups=groups, tiled=True)  12.2 us
    ppermute x2, waiting for transfers between devices, across(): parts.append(lax.ppermute(x, 'store', pairs))  11 us
    all_to_all x2, waiting for transfers between devices, exchange(): lax.all_to_all(x, 'store', 0, 0, axis_index_groups=groups, tiled=True)  9.52 us
    ppermute x2, starting transfers between devices, across(): parts.append(lax.ppermute(x, 'store', pairs))  7.04 us
    pallas_call x1, Pallas kernels, shards(): call(functools.partial(final_kernel, all_blocks), [sds((ops, rows, column...  6.58 us
    ppermute x2, starting transfers between devices, ring(): lax.ppermute(block, 'store', backward)  4.75 us
    pallas_call x1, Pallas kernels, shards(): call(functools.partial(image_kernel, all_blocks), [sds((ops * rows + STAT...  4.69 us
  transfers between devices with their start and end apart: 8, of which 4 were waited for; matrix products, arithmetic and copies ran while one was open for 0% of the time, Pallas kernels for 4%

profile of v11, /device:TPU:0, one launch (start us, length us, event | category | flops | bytes accessed | tf_op | source)
XLA Modules:
  0.0 91.8 jit_solution(2822517269869145762)
XLA Ops:
  0.6 2.0 %shard_map.112 = (bf16[8,32,128]{2,1,0:T(8,128)(2,1)}, bf16[208,128]{1,0:T(8,128)(2,1)}) custom-call(s32[2,6]{1,0:T(2,128)} %far_cols.1, bf16[512,512]{1,0:T(8,128)(2,1)} %uown.1, bf16[2,32,256]{2,1,0:T(8,128)(2,1)} %bitcast.4, bf16[2,2,6,32,32]{4,3,2,1,0:T(8,128)(2,1)} %coup.1), custom_call_target="tpu_custom_call" | custom-call | flops 1150000000 | tf_op jit(solution)/shard_map/pallas_call | solution.py:459
  2.7 4.0 %collective-permute-start.2 = (bf16[8,32,128]{2,1,0:T(8,128)(2,1)}, bf16[8,32,128]{2,1,0:T(8,128)(2,1)S(1)}, u32[]{:S(2)}, u32[]{:S(2)}) collective-permute-start(bf16[8,32,128]{2,1,0:T(8,128)(2,1)} %get-tuple-element.8.refs_0_), channel_id=1, source_target_pairs={{0,8},{1,9},{2,10},{3,11},{4,12},{5,13},{6,14},{7,15},{8,0},{9,1},... | collective-permute-start | bytes 196616 | tf_op jit(solution)/shard_map/ppermute | solution.py:448
  6.7 3.9 %collective-permute-done.2.refs_1_ = bf16[8,32,128]{2,1,0:T(8,128)(2,1)S(1)} collective-permute-done((bf16[8,32,128]{2,1,0:T(8,128)(2,1)}, bf16[8,32,128]{2,1,0:T(8,128)(2,1)S(1)}, u32[]{:S(2)}, u32[]{:S(2)}) %collective-permute-start.2) | collective-permute-done | bytes 65568 | tf_op jit(solution)/shard_map/ppermute | solution.py:448
  10.6 0.0 copy-start.1
  10.6 0.8 copy-done.1
  11.4 0.0 copy-start.7
  11.4 0.8 copy-done.7
  12.2 0.9 shard_map.113
  13.1 3.5 %all-to-all-start = ((bf16[8,272,128]{2,1,0:T(8,128)(2,1)}), bf16[8,272,128]{2,1,0:T(8,128)(2,1)S(1)}, u32[]{:S(2)}, u32[]{:S(2)}) async-start(bf16[8,272,128]{2,1,0:T(8,128)(2,1)} %shard_map.113), calls=%async_computation | async-start | bytes 1114112 | tf_op jit(solution)/shard_map/all_to_all | solution.py:442
  16.6 4.8 %collective-permute-start.1 = (bf16[512,512]{1,0:T(8,128)(2,1)}, bf16[512,512]{1,0:T(8,128)(2,1)}, u32[]{:S(2)}, u32[]{:S(2)}) collective-permute-start(bf16[512,512]{1,0:T(8,128)(2,1)} %uown.1), channel_id=1, source_target_pairs={{1,0},{2,1},{3,2},{4,3},{5,4},{6,5},{7,6},{8,7},{9,8},{10,9},{11,1... | collective-permute-start | bytes 1572872 | tf_op jit(solution)/shard_map/ppermute | solution.py:416
  21.4 0.0 collective-permute-start
  21.4 4.4 %all-to-all-done.held = bf16[8,272,128]{2,1,0:T(8,128)(2,1)S(1)} async-done(((bf16[8,272,128]{2,1,0:T(8,128)(2,1)}), bf16[8,272,128]{2,1,0:T(8,128)(2,1)S(1)}, u32[]{:S(2)}, u32[]{:S(2)}) %all-to-all-start) | async-done | bytes 557088 | tf_op jit(solution)/shard_map/all_to_all | solution.py:442
  25.8 0.1 reshape.18.cols
  25.8 0.0 copy-start
  25.8 0.0 copy-start.2
  25.9 0.0 copy-start.3
  25.9 0.0 copy-start.4
  25.9 0.0 copy-start.5
  25.9 0.0 copy-start.6
  25.9 1.8 %shard_map.114 = bf16[8,64,128]{2,1,0:T(8,128)(2,1)} custom-call(s32[96]{0:T(128)S(1)} %reshape.18.cols, s32[1]{0:T(128)} %bitcast.3.group, bf16[8,272,128]{2,1,0:T(8,128)(2,1)S(1)} %all-to-all-done.held), custom_call_target="tpu_custom_call" | custom-call | flops 1150000000 | tf_op jit(solution)/shard_map/pallas_call | solution.py:474
  27.7 8.6 %all-to-all-start.1 = ((bf16[8,64,128]{2,1,0:T(8,128)(2,1)}), bf16[8,64,128]{2,1,0:T(8,128)(2,1)S(1)}, u32[]{:S(2)}, u32[]{:S(2)}) async-start(bf16[8,64,128]{2,1,0:T(8,128)(2,1)} %shard_map.114), calls=%async_computation.1 | async-start | bytes 262144 | tf_op jit(solution)/shard_map/all_to_all | solution.py:442
  36.3 0.0 collective-permute-done.1.high.uhigh
  36.3 0.0 collective-permute-done.low.ulow
  36.3 5.2 %all-to-all-done.1.cmsg = bf16[8,64,128]{2,1,0:T(8,128)(2,1)S(1)} async-done(((bf16[8,64,128]{2,1,0:T(8,128)(2,1)}), bf16[8,64,128]{2,1,0:T(8,128)(2,1)S(1)}, u32[]{:S(2)}, u32[]{:S(2)}) %all-to-all-start.1) | async-done | bytes 131104 | tf_op jit(solution)/shard_map/all_to_all | solution.py:442
  41.5 0.0 copy-done
  41.5 0.0 copy-done.2
  41.5 0.0 copy-done.3
  41.5 0.0 copy-done.4
  41.5 0.0 copy-done.5
  41.5 0.0 copy-done.6
  41.5 4.7 %shard_map.115 = (bf16[1040,512]{1,0:T(8,128)(2,1)S(1)}, bf16[8,80,128]{2,1,0:T(8,128)(2,1)S(1)}) custom-call(s32[2,5]{1,0:T(2,128)S(1)} %copy-done.5, s32[2]{0:T(128)S(1)} %copy-done.6, s32[1]{0:T(128)} %bitcast.row0, bf16[2,2,5,256,256]{4,3,2,1,0:T(8,128)(2,1)S(1)} %copy-done, bf16[512,512]{1,0:T(8,128)(2,1)} %collective-permute-done.low.ulow, ...), custom_call_target="tpu_custom_call" | custom-call | flops 4600000000 | tf_op jit(solution)/shard_map/pallas_call | solution.py:487
  46.2 7.8 %all_to_all.20.refs_0_ = bf16[8,80,128]{2,1,0:T(8,128)(2,1)S(1)} all-to-all(bf16[8,80,128]{2,1,0:T(8,128)(2,1)S(1)} %get-tuple-element.10), channel_id=1, replica_groups={{0,1,2,3,4,5,6,7},{8,9,10,11,12,13,14,15},{16,17,18,19,20,21,22,23},{24..., dimensions={0} | all-to-all | bytes 327680 | tf_op jit(solution)/shard_map/all_to_all | solution.py:442
  54.1 3.0 %collective-permute-start.5 = (bf16[8,80,128]{2,1,0:T(8,128)(2,1)S(1)}, bf16[8,80,128]{2,1,0:T(8,128)(2,1)S(1)}, u32[]{:S(2)}, u32[]{:S(2)}) collective-permute-start(bf16[8,80,128]{2,1,0:T(8,128)(2,1)S(1)} %all_to_all.20.refs_0_), channel_id=1, source_target_pairs={{0,8},{1,9},{2,10},{3,11},{4,12},{5,13},{6,14},{7,15},{8,0},{9,1},... | collective-permute-start | bytes 491528 | tf_op jit(solution)/shard_map/ppermute | solution.py:448
  57.1 0.0 collective-permute-start.4
  57.1 0.5 collective-permute-start.3
  57.6 7.1 %collective-permute-done.5.refs_1_ = bf16[8,80,128]{2,1,0:T(8,128)(2,1)S(1)} collective-permute-done((bf16[8,80,128]{2,1,0:T(8,128)(2,1)S(1)}, bf16[8,80,128]{2,1,0:T(8,128)(2,1)S(1)}, u32[]{:S(2)}, u32[]{:S(2)}) %collective-permute-start.5) | collective-permute-done | bytes 163872 | tf_op jit(solution)/shard_map/ppermute | solution.py:448
  64.7 1.6 %shard_map.116 = bf16[8,80,128]{2,1,0:T(8,128)(2,1)S(1)} custom-call(s32[96]{0:T(128)S(1)} %reshape.18.cols, s32[1]{0:T(128)} %bitcast.3.group, bf16[8,272,128]{2,1,0:T(8,128)(2,1)S(1)} %all-to-all-done.held, bf16[8,80,128]{2,1,0:T(8,128)(2,1)S(1)} %all_to_all.20.refs_0_, bf16[8,80,128]{2,1,0:T(8,128)(2,1)S(1)} %collective-permute-done.5.refs_1_), custom_call_target="tpu_custom_call" | custom-call | flops 34500001792 | tf_op jit(solution)/shard_map/pallas_call | solution.py:501
  66.3 18.9 %all_to_all.21.cmsg = bf16[8,80,128]{2,1,0:T(8,128)(2,1)S(1)} all-to-all(bf16[8,80,128]{2,1,0:T(8,128)(2,1)S(1)} %shard_map.116), channel_id=1, replica_groups={{0,1,2,3,4,5,6,7},{8,9,10,11,12,13,14,15},{16,17,18,19,20,21,22,23},{24..., dimensions={0} | all-to-all | bytes 327680 | tf_op jit(solution)/shard_map/all_to_all | solution.py:442
  85.2 0.0 collective-permute-done.4.vhigh
  85.2 0.0 collective-permute-done.3.vlow
  85.2 6.6 %shard_map.117 = (f32[2,512,512]{2,1,0:T(8,128)}, f32[2,512]{1,0:T(2,128)}, f32[2,512]{1,0:T(2,128)}) custom-call(s32[2,5]{1,0:T(2,128)S(1)} %copy-done.5, s32[2]{0:T(128)S(1)} %copy-done.6, s32[1]{0:T(128)} %bitcast.row0, bf16[2,2,5,256,256]{4,3,2,1,0:T(8,128)(2,1)S(1)} %copy-done, bf16[512,512]{1,0:T(8,128)(2,1)} %collective-permute-done.low.ulow, ...), custom_call_target="tpu_custom_call" | custom-call | flops 4600000000 | tf_op jit(solution)/shard_map/pallas_call | solution.py:513
  (1 shorter events, 0.0 us)
Async XLA Ops:
  2.7 7.9 %collective-permute-start.2 = (bf16[8,32,128]{2,1,0:T(8,128)(2,1)}, bf16[8,32,128]{2,1,0:T(8,128)(2,1)S(1)}, u32[]{:S(2)}, u32[]{:S(2)}) collective-permute-start(bf16[8,32,128]{2,1,0:T(8,128)(2,1)} %get-tuple-element.8.refs_0_), channel_id=1, source_target_pairs={{0,8},{1,9},{2,10},{3,11},{4,12},{5,13},{6,14},{7,15},{8,0},{9,1},... | collective-permute-start | bytes 196616 | tf_op jit(solution)/shard_map/ppermute | solution.py:448
  10.6 0.8 copy-start.1
  11.4 0.8 copy-start.7
  13.1 12.7 %all-to-all-start = ((bf16[8,272,128]{2,1,0:T(8,128)(2,1)}), bf16[8,272,128]{2,1,0:T(8,128)(2,1)S(1)}, u32[]{:S(2)}, u32[]{:S(2)}) async-start(bf16[8,272,128]{2,1,0:T(8,128)(2,1)} %shard_map.113), calls=%async_computation | async-start | bytes 1114112 | tf_op jit(solution)/shard_map/all_to_all | solution.py:442
  16.6 19.7 %collective-permute-start.1 = (bf16[512,512]{1,0:T(8,128)(2,1)}, bf16[512,512]{1,0:T(8,128)(2,1)}, u32[]{:S(2)}, u32[]{:S(2)}) collective-permute-start(bf16[512,512]{1,0:T(8,128)(2,1)} %uown.1), channel_id=1, source_target_pairs={{1,0},{2,1},{3,2},{4,3},{5,4},{6,5},{7,6},{8,7},{9,8},{10,9},{11,1... | collective-permute-start | bytes 1572872 | tf_op jit(solution)/shard_map/ppermute | solution.py:416
  21.4 15.0 %collective-permute-start = (bf16[512,512]{1,0:T(8,128)(2,1)}, bf16[512,512]{1,0:T(8,128)(2,1)}, u32[]{:S(2)}, u32[]{:S(2)}) collective-permute-start(bf16[512,512]{1,0:T(8,128)(2,1)} %uown.1), channel_id=1, source_target_pairs={{0,1},{1,2},{2,3},{3,4},{4,5},{5,6},{6,7},{7,8},{8,9},{9,10},{10,1... | collective-permute-start | bytes 1572872 | tf_op jit(solution)/shard_map/ppermute | solution.py:416
  25.8 15.7 %copy-start = (bf16[2,2,5,256,256]{4,3,2,1,0:T(8,128)(2,1)S(1)}, bf16[2,2,5,256,256]{4,3,2,1,0:T(8,128)(2,1)}, u32[]{:S(2)}) copy-start(bf16[2,2,5,256,256]{4,3,2,1,0:T(8,128)(2,1)} %tiles.3) | copy-start | bytes 7864324
  25.8 15.7 %copy-start.2 = (bf16[2,256,32]{1,2,0:T(8,128)(2,1)S(1)}, bf16[2,256,32]{1,2,0:T(8,128)(2,1)}, u32[]{:S(2)}) copy-start(bf16[2,256,32]{1,2,0:T(8,128)(2,1)} %param.16) | copy-start | bytes 98308
  25.9 15.7 %copy-start.3 = (bf16[2,256,32]{1,2,0:T(8,128)(2,1)S(1)}, bf16[2,256,32]{1,2,0:T(8,128)(2,1)}, u32[]{:S(2)}) copy-start(bf16[2,256,32]{1,2,0:T(8,128)(2,1)} %param.15) | copy-start | bytes 98308
  25.9 15.7 %copy-start.4 = (f32[2,512]{1,0:T(2,128)S(1)}, f32[2,512]{1,0:T(2,128)}, u32[]{:S(2)}) copy-start(f32[2,512]{1,0:T(2,128)} %diag.3) | copy-start | bytes 12292
  25.9 15.7 %copy-start.5 = (s32[2,5]{1,0:T(2,128)S(1)}, s32[2,5]{1,0:T(2,128)}, u32[]{:S(2)}) copy-start(s32[2,5]{1,0:T(2,128)} %cols.3) | copy-start | bytes 124
  25.9 15.7 %copy-start.6 = (s32[2]{0:T(128)S(1)}, s32[2]{0:T(128)}, u32[]{:S(2)}) copy-start(s32[2]{0:T(128)} %count.3) | copy-start | bytes 28
  27.7 13.8 %all-to-all-start.1 = ((bf16[8,64,128]{2,1,0:T(8,128)(2,1)}), bf16[8,64,128]{2,1,0:T(8,128)(2,1)S(1)}, u32[]{:S(2)}, u32[]{:S(2)}) async-start(bf16[8,64,128]{2,1,0:T(8,128)(2,1)} %shard_map.114), calls=%async_computation.1 | async-start | bytes 262144 | tf_op jit(solution)/shard_map/all_to_all | solution.py:442
  54.1 10.6 %collective-permute-start.5 = (bf16[8,80,128]{2,1,0:T(8,128)(2,1)S(1)}, bf16[8,80,128]{2,1,0:T(8,128)(2,1)S(1)}, u32[]{:S(2)}, u32[]{:S(2)}) collective-permute-start(bf16[8,80,128]{2,1,0:T(8,128)(2,1)S(1)} %all_to_all.20.refs_0_), channel_id=1, source_target_pairs={{0,8},{1,9},{2,10},{3,11},{4,12},{5,13},{6,14},{7,15},{8,0},{9,1},... | collective-permute-start | bytes 491528 | tf_op jit(solution)/shard_map/ppermute | solution.py:448
  57.1 28.1 %collective-permute-start.4 = (bf16[1040,512]{1,0:T(8,128)(2,1)S(1)}, bf16[1040,512]{1,0:T(8,128)(2,1)S(1)}, u32[]{:S(2)}, u32[]{:S(2)}) collective-permute-start(bf16[1040,512]{1,0:T(8,128)(2,1)S(1)} %get-tuple-element.9.vown), channel_id=1, source_target_pairs={{1,0},{2,1},{3,2},{4,3},{5,4},{6,5},{7,6},{8,7},{9,8},{10,9},{11,1... | collective-permute-start | bytes 3194888 | tf_op jit(solution)/shard_map/ppermute | solution.py:416
  57.1 28.1 %collective-permute-start.3 = (bf16[1040,512]{1,0:T(8,128)(2,1)S(1)}, bf16[1040,512]{1,0:T(8,128)(2,1)S(1)}, u32[]{:S(2)}, u32[]{:S(2)}) collective-permute-start(bf16[1040,512]{1,0:T(8,128)(2,1)S(1)} %get-tuple-element.9.vown), channel_id=1, source_target_pairs={{0,1},{1,2},{2,3},{3,4},{4,5},{5,6},{6,7},{7,8},{8,9},{9,10},{10,1... | collective-permute-start | bytes 3194888 | tf_op jit(solution)/shard_map/ppermute | solution.py:416

commit v12 on v7

--- a/solution.py
+++ b/solution.py
@@ -13,25 +13,28 @@
 HALF = 64
 SLICES = 8
 STATS = 16
-HBM_RATE = 3690000
+FLOP_RATE = 1150000000
 F32 = jnp.float32
 BF16 = jnp.bfloat16
 
 VMEM = pl.BlockSpec(memory_space=pltpu.VMEM)
 SMEM = pl.BlockSpec(memory_space=pltpu.SMEM)
-
-
-def call(body, out_shape, in_specs, scratch=(), micros=1.0, megabytes=20):
+ANY = pl.BlockSpec(memory_space=pl.ANY)
+
+
+def call(body, out_shape, in_specs, scratch=(), micros=1.0, megabytes=20, out_specs=None):
     many = isinstance(out_shape, (list, tuple))
+    if out_specs is None:
+        out_specs = [VMEM] * len(out_shape) if many else VMEM
     return pl.pallas_call(
         body,
         out_shape=out_shape,
         in_specs=in_specs,
-        out_specs=[VMEM] * len(out_shape) if many else VMEM,
+        out_specs=out_specs,
         scratch_shapes=list(scratch),
         compiler_params=pltpu.CompilerParams(vmem_limit_bytes=megabytes * 1024 * 1024),
         cost_estimate=pl.CostEstimate(
-            flops=0, bytes_accessed=int(micros * HBM_RATE), transcendentals=0
+            flops=int(micros * FLOP_RATE), bytes_accessed=0, transcendentals=0
         ),
     )
 
@@ -82,17 +85,14 @@
                 )
 
 
-def coeff_kernel(u, right, out):
-    blocks, rank, size = right.shape
+def coeff_kernel(count, far_cols, u, right, coup, z_out, out):
+    ops, blocks, far, rank, _ = coup.shape
+    size = right.shape[2]
     z = [dot(right[b], u[b * size:(b + 1) * size, :]) for b in range(blocks)]
     for pair in range(SLICES // 2):
         first, second = halves(chunk(z[0], pair), chunk(z[1], pair))
-        out[2 * pair] = first.astype(BF16)
-        out[2 * pair + 1] = second.astype(BF16)
-
-
-def pack_kernel(far_cols, coup, out):
-    ops, blocks, far, rank, _ = coup.shape
+        z_out[2 * pair] = first.astype(BF16)
+        z_out[2 * pair + 1] = second.astype(BF16)
     whole, rest = [], []
     for b in range(blocks):
         tiles = [
@@ -105,7 +105,11 @@
     names = jnp.zeros((STATS, LANES), F32)
     for b in range(blocks):
         for f in range(far):
-            names = jnp.where(lane == b * far + f, far_cols[b, f].astype(F32), names)
+            col = far_cols[b, f]
+            device = lax.div(col, blocks)
+            slot = lax.rem(device, count) * SLICES + lax.div(device, count)
+            name = (slot * blocks + lax.rem(col, blocks)).astype(F32)
+            names = jnp.where(lane == b * far + f, name, names)
     out[...] = jnp.concatenate(
         whole + [jnp.concatenate(rest, axis=1), names.astype(BF16)], axis=0
     )
@@ -119,10 +123,6 @@
         out[s, 0:rows, :] = packed[...]
     for m, part in enumerate(parts):
         out[:, rows + m * rank:rows + (m + 1) * rank, :] = part[...]
-
-
-def copy_kernel(source, after, target):
-    target[...] = source[...]
 
 
 def coupling_rows(held, s, b, ops, rank):
@@ -305,8 +305,26 @@
 
 
 def final_kernel(
-    w, ulow, uown, uhigh, vlow, vown, vhigh, diag, left, cmsg, images, heights, norms, ext, coef, stat
+    w,
+    ulow,
+    uown,
+    uhigh,
+    vlow,
+    vown,
+    vhigh,
+    diag,
+    left,
+    cmsg,
+    images,
+    heights,
+    norms,
+    ext,
+    coef,
+    stat,
+    out,
+    outs,
 ):
+    copies = []
     ops = images.shape[0]
     blocks, rank, size = left.shape
     rows, columns = uown.shape
@@ -335,11 +353,17 @@
             product = near_product(w.at[b, o * size:(o + 1) * size], parts, b, blocks, size)
             far = dot(left[b], coef[b, o * rank:(o + 1) * rank, :], ((0,), (0,)))
             mine = ext[o, 1, b * size:(b + 1) * size, :].astype(F32)
-            images[o, b * size:(b + 1) * size, :] = (
+            here = slice(b * size, (b + 1) * size)
+            out[o, here, :] = (
                 product
                 + diagonal_of(diag, o, b, size, columns) * mine
                 + far.astype(BF16).astype(F32)
             )
+            copy = pltpu.make_async_copy(out.at[o, here], images.at[o, here], outs.at[o, b])
+            copy.start()
+            copies.append(copy)
+    for copy in copies:
+        copy.wait()
 
 
 def ring(block):
@@ -367,7 +391,7 @@
     rows, columns = sources.shape
     all_blocks = blocks * n
     count = n // SLICES
-    groups = [[g * SLICES + s for s in range(SLICES)] for g in range(count)]
+    groups = [[s * count + g for s in range(SLICES)] for g in range(count)]
     sds = jax.ShapeDtypeStruct
     body = ops * rank
 
@@ -377,25 +401,25 @@
     def across(x):
         parts = [x]
         for m in range(1, count):
-            pairs = [(i, (i + m * SLICES) % n) for i in range(n)]
+            pairs = [(i, i - i % count + (i + m) % count) for i in range(n)]
             parts.append(lax.ppermute(x, "store", pairs))
         return parts
 
     place = lax.axis_index("store").astype(jnp.int32)
     row0 = (place * blocks).reshape(1)
-    group = lax.div(place, jnp.int32(SLICES)).reshape(1)
+    group = lax.rem(place, jnp.int32(count)).reshape(1)
     left = jnp.transpose(basis_left, (0, 2, 1))
     right = jnp.transpose(basis_right, (0, 2, 1))
 
     low, high = ring(sources)
-    z1 = call(coeff_kernel, sds((SLICES, rank, LANES), BF16), [VMEM, VMEM], megabytes=60)(
-        sources, right
-    )
+    shared = (blocks + 1) * body
+    z1, packed = call(
+        functools.partial(coeff_kernel, count),
+        [sds((SLICES, rank, LANES), BF16), sds((shared + STATS, LANES), BF16)],
+        [SMEM, VMEM, VMEM, VMEM],
+        megabytes=60,
+    )(far_cols, sources, right, couplings)
     z1 = across(z1)
-    shared = (blocks + 1) * body
-    packed = call(pack_kernel, sds((shared + STATS, LANES), BF16), [SMEM, VMEM])(
-        far_cols, couplings
-    )
     held = call(
         share_kernel,
         sds((SLICES, shared + STATS + count * rank, LANES), BF16),
@@ -404,13 +428,6 @@
     held = exchange(held)
     cols = held[:, shared, :blocks * far].astype(jnp.int32).reshape(-1)
 
-    w = call(
-        functools.partial(order_tiles, all_blocks),
-        sds((blocks, ops * size, near * size), BF16),
-        [SMEM, SMEM, SMEM, VMEM],
-        micros=2.5,
-    )(near_cols, near_count, row0, near_tiles)
-
     c1 = call(
         functools.partial(first_couple, ops, rank, far),
         sds((SLICES, body, LANES), BF16),
@@ -418,6 +435,13 @@
         [pltpu.VMEM((n * blocks * rank, LANES), BF16)],
     )(cols, group, held)
     c1 = exchange(c1)
+
+    w = call(
+        functools.partial(order_tiles, all_blocks),
+        sds((blocks, ops * size, near * size), BF16),
+        [SMEM, SMEM, SMEM, VMEM],
+        micros=2.5,
+    )(near_cols, near_count, row0, near_tiles)
 
     v, msg = call(
         image_kernel,
@@ -429,12 +453,8 @@
         ],
         micros=4.0,
     )(w, low, sources, high, self_terms, left, right, c1)
-    msg = exchange(msg)
-    msgs = across(msg)
-    bulk = call(
-        copy_kernel, sds(v.shape, BF16), [VMEM, pl.BlockSpec(memory_space=pl.ANY)], micros=8.0
-    )(v, msg)
-    vlow, vhigh = ring(bulk)
+    msgs = across(exchange(msg))
+    vlow, vhigh = ring(v)
 
     c2 = call(
         functools.partial(second_couple, all_blocks * size, ops, rank, far),
@@ -444,6 +464,7 @@
             pltpu.VMEM((ops, n * blocks * rank, LANES), BF16),
             pltpu.VMEM((n, STATS, LANES), F32),
         ],
+        micros=30.0,
     )(cols, group, held, *msgs)
     c2 = exchange(c2)
 
@@ -455,8 +476,11 @@
             pltpu.VMEM((ops, 3, rows, columns), BF16),
             pltpu.VMEM((blocks, body, columns), BF16),
             pltpu.VMEM((STATS, columns), F32),
+            pltpu.VMEM((ops, rows, columns), F32),
+            pltpu.SemaphoreType.DMA((ops, blocks)),
         ],
         micros=4.0,
+        out_specs=[ANY, VMEM, VMEM],
     )(w, low, sources, high, vlow, v, vhigh, self_terms, left, c2)
     return images, heights, norms
 

time: 90.8 us -> 96.9 us (1.067)
  blocking collectives: 15.7 us -> 35.2 us
  waiting for transfers between devices: 27.9 us -> 17.8 us
  starting transfers between devices: 24.7 us -> 21.1 us
    ppermute x2, waiting for transfers between devices: 21 us -> 1.18 us  [across(): parts.append(lax.ppermute(x, 'store', pairs))]
    all_to_all x2, blocking collectives: 15.7 us -> 35.2 us  [exchange(): lax.all_to_all(x, 'store', 0, 0, axis_index_groups=groups, tiled=True)]
    all_to_all x2, waiting for transfers between devices: 6.85 us -> 16.6 us  [exchange(): lax.all_to_all(x, 'store', 0, 0, axis_index_groups=groups, tiled=True)]
    ppermute x2, starting transfers between devices: 4.62 us -> 0.46 us  [across(): parts.append(lax.ppermute(x, 'store', pairs))]
    all_to_all x2, starting transfers between devices: 12.3 us -> 15.4 us  [exchange(): lax.all_to_all(x, 'store', 0, 0, axis_index_groups=groups, tiled=True)]
    ppermute x2, starting transfers between devices: 7.75 us -> 5.24 us  [ring(): lax.ppermute(block, 'store', backward)]
    unnamed x18 -> x22, local copies, waits for them, and re-layouts: 4.2 us -> 4.9 us
    pallas_call x3 -> x1, Pallas kernels: 2.7 us -> 2.02 us  [shards(): call(functools.partial(coeff_kernel, count), [sds((SLICES, rank, LANES),...]
  transfers between devices with their start and end apart: 8 -> 8, of which waited for: 4 -> 4; matrix products, arithmetic and copies ran while one was open for 0% -> 0% of each run, Pallas kernels for 6% -> 4%
where the time goes in v12:
time: 96.9 us; the launch traced here: 96.4 us
  blocking collectives  35.2 us (36%)
  starting transfers between devices  21.1 us (22%)
  waiting for transfers between devices  17.8 us (18%)
  Pallas kernels  16.5 us (17%)
  local copies, waits for them, and re-layouts  4.98 us (5%)
    all_to_all x2, blocking collectives, exchange(): lax.all_to_all(x, 'store', 0, 0, axis_index_groups=groups, tiled=True)  35.2 us
    all_to_all x2, waiting for transfers between devices, exchange(): lax.all_to_all(x, 'store', 0, 0, axis_index_groups=groups, tiled=True)  16.6 us
    all_to_all x2, starting transfers between devices, exchange(): lax.all_to_all(x, 'store', 0, 0, axis_index_groups=groups, tiled=True)  15.4 us
    pallas_call x1, Pallas kernels, shards(): call(final_kernel, [sds((ops, rows, columns), F32), sds((ops, columns), F...  5.25 us
    ppermute x2, starting transfers between devices, ring(): lax.ppermute(block, 'store', backward)  5.24 us
    unnamed x22, local copies, waits for them, and re-layouts  4.9 us
    pallas_call x1, Pallas kernels, shards(): call(image_kernel, [sds((ops * rows + STATS, columns), BF16), sds((SLICES...  4.08 us
    pallas_call x1, Pallas kernels, shards(): call(functools.partial(coeff_kernel, count), [sds((SLICES, rank, LANES),...  2.02 us
  transfers between devices with their start and end apart: 8, of which 4 were waited for; matrix products, arithmetic and copies ran while one was open for 0% of the time, Pallas kernels for 4%

profile of v12, /device:TPU:0, one launch (start us, length us, event | category | flops | bytes accessed | tf_op | source)
XLA Modules:
  0.0 96.4 jit_solution(17524520896415328764)
XLA Ops:
  0.6 2.0 %shard_map.113 = (bf16[8,32,128]{2,1,0:T(8,128)(2,1)}, bf16[208,128]{1,0:T(8,128)(2,1)}) custom-call(s32[2,6]{1,0:T(2,128)} %far_cols.1, bf16[512,512]{1,0:T(8,128)(2,1)} %uown.1, bf16[2,32,256]{2,1,0:T(8,128)(2,1)} %bitcast.4, bf16[2,2,6,32,32]{4,3,2,1,0:T(8,128)(2,1)} %coup.1), custom_call_target="tpu_custom_call" | custom-call | flops 1150000000 | tf_op jit(solution)/shard_map/pallas_call | solution.py:416
  2.7 0.5 collective-permute-start.2
  3.1 1.1 %collective-permute-done.2.refs_1_ = bf16[8,32,128]{2,1,0:T(8,128)(2,1)S(1)} collective-permute-done((bf16[8,32,128]{2,1,0:T(8,128)(2,1)}, bf16[8,32,128]{2,1,0:T(8,128)(2,1)S(1)}, u32[]{:S(2)}, u32[]{:S(2)}) %collective-permute-start.2) | collective-permute-done | bytes 65568 | tf_op jit(solution)/shard_map/ppermute | solution.py:405
  4.2 0.0 copy-start.1
  4.2 0.8 copy-done.1
  5.1 0.0 copy-start.10
  5.1 0.8 copy-done.10
  5.9 0.9 shard_map.114
  6.7 7.2 %all-to-all-start = ((bf16[8,272,128]{2,1,0:T(8,128)(2,1)}), bf16[8,272,128]{2,1,0:T(8,128)(2,1)S(1)}, u32[]{:S(2)}, u32[]{:S(2)}) async-start(bf16[8,272,128]{2,1,0:T(8,128)(2,1)} %shard_map.114), calls=%async_computation | async-start | bytes 1114112 | tf_op jit(solution)/shard_map/all_to_all | solution.py:399
  13.9 3.9 %collective-permute-start.1 = (bf16[512,512]{1,0:T(8,128)(2,1)}, bf16[512,512]{1,0:T(8,128)(2,1)}, u32[]{:S(2)}, u32[]{:S(2)}) collective-permute-start(bf16[512,512]{1,0:T(8,128)(2,1)} %uown.1), channel_id=1, source_target_pairs={{1,0},{2,1},{3,2},{4,3},{5,4},{6,5},{7,6},{8,7},{9,8},{10,9},{11,1... | collective-permute-start | bytes 1572872 | tf_op jit(solution)/shard_map/ppermute | solution.py:373
  17.8 0.0 collective-permute-start
  17.8 11.7 %all-to-all-done.held = bf16[8,272,128]{2,1,0:T(8,128)(2,1)S(1)} async-done(((bf16[8,272,128]{2,1,0:T(8,128)(2,1)}), bf16[8,272,128]{2,1,0:T(8,128)(2,1)S(1)}, u32[]{:S(2)}, u32[]{:S(2)}) %all-to-all-start) | async-done | bytes 557088 | tf_op jit(solution)/shard_map/all_to_all | solution.py:399
  29.6 0.1 reshape.18.cols
  29.6 0.0 copy-start
  29.6 0.0 copy-start.5
  29.6 0.0 copy-start.6
  29.7 1.8 %shard_map.115 = bf16[8,64,128]{2,1,0:T(8,128)(2,1)} custom-call(s32[96]{0:T(128)S(1)} %reshape.18.cols, s32[1]{0:T(128)} %bitcast.3.group, bf16[8,272,128]{2,1,0:T(8,128)(2,1)S(1)} %all-to-all-done.held), custom_call_target="tpu_custom_call" | custom-call | flops 1150000000 | tf_op jit(solution)/shard_map/pallas_call | solution.py:431
  31.4 8.3 %all-to-all-start.1 = ((bf16[8,64,128]{2,1,0:T(8,128)(2,1)}), bf16[8,64,128]{2,1,0:T(8,128)(2,1)S(1)}, u32[]{:S(2)}, u32[]{:S(2)}) async-start(bf16[8,64,128]{2,1,0:T(8,128)(2,1)} %shard_map.115), calls=%async_computation.1 | async-start | bytes 262144 | tf_op jit(solution)/shard_map/all_to_all | solution.py:399
  39.7 0.0 copy-done
  39.7 0.0 copy-done.5
  39.7 0.0 copy-done.6
  39.7 0.0 copy-start.2
  39.7 0.0 copy-start.3
  39.8 0.0 copy-start.4
  39.8 0.9 shard_map.112.w
  40.7 0.0 copy-start.7
  40.7 1.5 %copy-done.7 = bf16[2,512,1280]{2,1,0:T(8,128)(2,1)} copy-done((bf16[2,512,1280]{2,1,0:T(8,128)(2,1)}, bf16[2,512,1280]{2,1,0:T(8,128)(2,1)S(1)}, u32[]{:S(2)}) %copy-start.7) | copy-done | bytes 2621464
  42.2 0.0 collective-permute-done.1.high.uhigh
  42.2 0.0 collective-permute-done.low.ulow
  42.2 4.9 %all-to-all-done.1.cmsg = bf16[8,64,128]{2,1,0:T(8,128)(2,1)S(1)} async-done(((bf16[8,64,128]{2,1,0:T(8,128)(2,1)}), bf16[8,64,128]{2,1,0:T(8,128)(2,1)S(1)}, u32[]{:S(2)}, u32[]{:S(2)}) %all-to-all-start.1) | async-done | bytes 131104 | tf_op jit(solution)/shard_map/all_to_all | solution.py:399
  47.0 0.0 copy-done.2
  47.0 0.0 copy-done.3
  47.1 0.0 copy-done.4
  47.1 0.0 copy-start.8
  47.1 1.7 %copy-done.8 = bf16[2,512,1280]{2,1,0:T(8,128)(2,1)S(1)} copy-done((bf16[2,512,1280]{2,1,0:T(8,128)(2,1)S(1)}, bf16[2,512,1280]{2,1,0:T(8,128)(2,1)}, u32[]{:S(2)}) %copy-start.8) | copy-done | bytes 2621464
  48.8 4.1 %shard_map.116 = (bf16[1040,512]{1,0:T(8,128)(2,1)S(1)}, bf16[8,80,128]{2,1,0:T(8,128)(2,1)S(1)}) custom-call(bf16[2,512,1280]{2,1,0:T(8,128)(2,1)S(1)} %copy-done.8, bf16[512,512]{1,0:T(8,128)(2,1)} %collective-permute-done.low.ulow, bf16[512,512]{1,0:T(8,128)(2,1)} %uown.1, bf16[512,512]{1,0:T(8,128)(2,1)} %collective-permute-done.1.high.uhigh, ...), custom_call_target="tpu_custom_call" | custom-call | flops 4600000000 | tf_op jit(solution)/shard_map/pallas_call | solution.py:446
  52.9 10.0 %all_to_all.20.refs_0_ = bf16[8,80,128]{2,1,0:T(8,128)(2,1)S(1)} all-to-all(bf16[8,80,128]{2,1,0:T(8,128)(2,1)S(1)} %get-tuple-element.10), channel_id=1, replica_groups={{0,2,4,6,8,10,12,14},{1,3,5,7,9,11,13,15},{16,18,20,22,24,26,28,30},{17..., dimensions={0} | all-to-all | bytes 327680 | tf_op jit(solution)/shard_map/all_to_all | solution.py:399
  62.8 0.0 collective-permute-start.5
  62.9 0.0 copy-start.9
  62.9 1.3 %collective-permute-start.4 = (bf16[1040,512]{1,0:T(8,128)(2,1)S(1)}, bf16[1040,512]{1,0:T(8,128)(2,1)S(1)}, u32[]{:S(2)}, u32[]{:S(2)}) collective-permute-start(bf16[1040,512]{1,0:T(8,128)(2,1)S(1)} %get-tuple-element.9.vown), channel_id=1, source_target_pairs={{1,0},{2,1},{3,2},{4,3},{5,4},{6,5},{7,6},{8,7},{9,8},{10,9},{11,1... | collective-permute-start | bytes 3194888 | tf_op jit(solution)/shard_map/ppermute | solution.py:373
  64.2 0.0 collective-permute-start.3
  64.2 0.1 collective-permute-done.5.refs_1_
  64.2 1.6 %shard_map.117 = bf16[8,80,128]{2,1,0:T(8,128)(2,1)S(1)} custom-call(s32[96]{0:T(128)S(1)} %reshape.18.cols, s32[1]{0:T(128)} %bitcast.3.group, bf16[8,272,128]{2,1,0:T(8,128)(2,1)S(1)} %all-to-all-done.held, bf16[8,80,128]{2,1,0:T(8,128)(2,1)S(1)} %all_to_all.20.refs_0_, bf16[8,80,128]{2,1,0:T(8,128)(2,1)S(1)} %collective-permute-done.5.refs_1_), custom_call_target="tpu_custom_call" | custom-call | flops 34500001792 | tf_op jit(solution)/shard_map/pallas_call | solution.py:459
  65.8 25.3 %all_to_all.21.cmsg = bf16[8,80,128]{2,1,0:T(8,128)(2,1)S(1)} all-to-all(bf16[8,80,128]{2,1,0:T(8,128)(2,1)S(1)} %shard_map.117), channel_id=1, replica_groups={{0,2,4,6,8,10,12,14},{1,3,5,7,9,11,13,15},{16,18,20,22,24,26,28,30},{17..., dimensions={0} | all-to-all | bytes 327680 | tf_op jit(solution)/shard_map/all_to_all | solution.py:399
  91.1 0.0 collective-permute-done.4.vhigh
  91.1 0.0 collective-permute-done.3.vlow
  91.1 0.0 copy-done.9
  91.1 5.2 %shard_map.118 = (f32[2,512,512]{2,1,0:T(8,128)}, f32[2,512]{1,0:T(2,128)}, f32[2,512]{1,0:T(2,128)}) custom-call(bf16[2,512,1280]{2,1,0:T(8,128)(2,1)S(1)} %copy-done.9, bf16[512,512]{1,0:T(8,128)(2,1)} %collective-permute-done.low.ulow, bf16[512,512]{1,0:T(8,128)(2,1)} %uown.1, bf16[512,512]{1,0:T(8,128)(2,1)} %collective-permute-done.1.high.uhigh, ...), custom_call_target="tpu_custom_call" | custom-call | flops 4600000000 | tf_op jit(solution)/shard_map/pallas_call | solution.py:471
  (1 shorter events, 0.0 us)
Async XLA Ops:
  2.7 1.6 %collective-permute-start.2 = (bf16[8,32,128]{2,1,0:T(8,128)(2,1)}, bf16[8,32,128]{2,1,0:T(8,128)(2,1)S(1)}, u32[]{:S(2)}, u32[]{:S(2)}) collective-permute-start(bf16[8,32,128]{2,1,0:T(8,128)(2,1)} %get-tuple-element.8.refs_0_), channel_id=1, source_target_pairs={{0,1},{1,0},{2,3},{3,2},{4,5},{5,4},{6,7},{7,6},{8,9},{9,8},{10,11... | collective-permute-start | bytes 196616 | tf_op jit(solution)/shard_map/ppermute | solution.py:405
  4.2 0.8 copy-start.1
  5.1 0.8 copy-start.10
  6.7 22.8 %all-to-all-start = ((bf16[8,272,128]{2,1,0:T(8,128)(2,1)}), bf16[8,272,128]{2,1,0:T(8,128)(2,1)S(1)}, u32[]{:S(2)}, u32[]{:S(2)}) async-start(bf16[8,272,128]{2,1,0:T(8,128)(2,1)} %shard_map.114), calls=%async_computation | async-start | bytes 1114112 | tf_op jit(solution)/shard_map/all_to_all | solution.py:399
  13.9 28.3 %collective-permute-start.1 = (bf16[512,512]{1,0:T(8,128)(2,1)}, bf16[512,512]{1,0:T(8,128)(2,1)}, u32[]{:S(2)}, u32[]{:S(2)}) collective-permute-start(bf16[512,512]{1,0:T(8,128)(2,1)} %uown.1), channel_id=1, source_target_pairs={{1,0},{2,1},{3,2},{4,3},{5,4},{6,5},{7,6},{8,7},{9,8},{10,9},{11,1... | collective-permute-start | bytes 1572872 | tf_op jit(solution)/shard_map/ppermute | solution.py:373
  17.8 24.3 %collective-permute-start = (bf16[512,512]{1,0:T(8,128)(2,1)}, bf16[512,512]{1,0:T(8,128)(2,1)}, u32[]{:S(2)}, u32[]{:S(2)}) collective-permute-start(bf16[512,512]{1,0:T(8,128)(2,1)} %uown.1), channel_id=1, source_target_pairs={{0,1},{1,2},{2,3},{3,4},{4,5},{5,6},{6,7},{7,8},{8,9},{9,10},{10,1... | collective-permute-start | bytes 1572872 | tf_op jit(solution)/shard_map/ppermute | solution.py:373
  29.6 10.1 %copy-start = (bf16[2,2,5,256,256]{4,3,2,1,0:T(8,128)(2,1)S(1)}, bf16[2,2,5,256,256]{4,3,2,1,0:T(8,128)(2,1)}, u32[]{:S(2)}) copy-start(bf16[2,2,5,256,256]{4,3,2,1,0:T(8,128)(2,1)} %tiles.1) | copy-start | bytes 7864324
  29.6 10.1 %copy-start.5 = (s32[2,5]{1,0:T(2,128)S(1)}, s32[2,5]{1,0:T(2,128)}, u32[]{:S(2)}) copy-start(s32[2,5]{1,0:T(2,128)} %cols.1) | copy-start | bytes 124
  29.6 10.1 %copy-start.6 = (s32[2]{0:T(128)S(1)}, s32[2]{0:T(128)}, u32[]{:S(2)}) copy-start(s32[2]{0:T(128)} %count.1) | copy-start | bytes 28
  31.4 15.6 %all-to-all-start.1 = ((bf16[8,64,128]{2,1,0:T(8,128)(2,1)}), bf16[8,64,128]{2,1,0:T(8,128)(2,1)S(1)}, u32[]{:S(2)}, u32[]{:S(2)}) async-start(bf16[8,64,128]{2,1,0:T(8,128)(2,1)} %shard_map.115), calls=%async_computation.1 | async-start | bytes 262144 | tf_op jit(solution)/shard_map/all_to_all | solution.py:399
  39.7 7.3 %copy-start.2 = (bf16[2,256,32]{1,2,0:T(8,128)(2,1)S(1)}, bf16[2,256,32]{1,2,0:T(8,128)(2,1)}, u32[]{:S(2)}) copy-start(bf16[2,256,32]{1,2,0:T(8,128)(2,1)} %param.16) | copy-start | bytes 98308
  39.7 7.3 %copy-start.3 = (bf16[2,256,32]{1,2,0:T(8,128)(2,1)S(1)}, bf16[2,256,32]{1,2,0:T(8,128)(2,1)}, u32[]{:S(2)}) copy-start(bf16[2,256,32]{1,2,0:T(8,128)(2,1)} %param.15) | copy-start | bytes 98308
  39.8 7.3 %copy-start.4 = (f32[2,512]{1,0:T(2,128)S(1)}, f32[2,512]{1,0:T(2,128)}, u32[]{:S(2)}) copy-start(f32[2,512]{1,0:T(2,128)} %diag.3) | copy-start | bytes 12292
  40.7 1.5 %copy-start.7 = (bf16[2,512,1280]{2,1,0:T(8,128)(2,1)}, bf16[2,512,1280]{2,1,0:T(8,128)(2,1)S(1)}, u32[]{:S(2)}) copy-start(bf16[2,512,1280]{2,1,0:T(8,128)(2,1)S(1)} %shard_map.112.w) | copy-start | bytes 7864324
  47.1 1.7 %copy-start.8 = (bf16[2,512,1280]{2,1,0:T(8,128)(2,1)S(1)}, bf16[2,512,1280]{2,1,0:T(8,128)(2,1)}, u32[]{:S(2)}) copy-start(bf16[2,512,1280]{2,1,0:T(8,128)(2,1)} %copy-done.7) | copy-start | bytes 7864324
  62.8 1.4 %collective-permute-start.5 = (bf16[8,80,128]{2,1,0:T(8,128)(2,1)S(1)}, bf16[8,80,128]{2,1,0:T(8,128)(2,1)S(1)}, u32[]{:S(2)}, u32[]{:S(2)}) collective-permute-start(bf16[8,80,128]{2,1,0:T(8,128)(2,1)S(1)} %all_to_all.20.refs_0_), channel_id=1, source_target_pairs={{0,1},{1,0},{2,3},{3,2},{4,5},{5,4},{6,7},{7,6},{8,9},{9,8},{10,11... | collective-permute-start | bytes 491528 | tf_op jit(solution)/shard_map/ppermute | solution.py:405
  62.9 28.3 %copy-start.9 = (bf16[2,512,1280]{2,1,0:T(8,128)(2,1)S(1)}, bf16[2,512,1280]{2,1,0:T(8,128)(2,1)}, u32[]{:S(2)}) copy-start(bf16[2,512,1280]{2,1,0:T(8,128)(2,1)} %copy-done.7) | copy-start | bytes 7864324
  62.9 28.3 %collective-permute-start.4 = (bf16[1040,512]{1,0:T(8,128)(2,1)S(1)}, bf16[1040,512]{1,0:T(8,128)(2,1)S(1)}, u32[]{:S(2)}, u32[]{:S(2)}) collective-permute-start(bf16[1040,512]{1,0:T(8,128)(2,1)S(1)} %get-tuple-element.9.vown), channel_id=1, source_target_pairs={{1,0},{2,1},{3,2},{4,3},{5,4},{6,5},{7,6},{8,7},{9,8},{10,9},{11,1... | collective-permute-start | bytes 3194888 | tf_op jit(solution)/shard_map/ppermute | solution.py:373
  64.2 26.9 %collective-permute-start.3 = (bf16[1040,512]{1,0:T(8,128)(2,1)S(1)}, bf16[1040,512]{1,0:T(8,128)(2,1)S(1)}, u32[]{:S(2)}, u32[]{:S(2)}) collective-permute-start(bf16[1040,512]{1,0:T(8,128)(2,1)S(1)} %get-tuple-element.9.vown), channel_id=1, source_target_pairs={{0,1},{1,2},{2,3},{3,4},{4,5},{5,6},{6,7},{7,8},{8,9},{9,10},{10,1... | collective-permute-start | bytes 3194888 | tf_op jit(solution)/shard_map/ppermute | solution.py:373

commit v13 on v10

--- a/solution.py
+++ b/solution.py
@@ -22,13 +22,15 @@
 ANY = pl.BlockSpec(memory_space=pl.ANY)
 
 
-def call(body, out_shape, in_specs, scratch=(), micros=1.0, megabytes=20):
+def call(body, out_shape, in_specs, scratch=(), micros=1.0, megabytes=20, out_specs=None):
     many = isinstance(out_shape, (list, tuple))
+    if out_specs is None:
+        out_specs = [VMEM] * len(out_shape) if many else VMEM
     return pl.pallas_call(
         body,
         out_shape=out_shape,
         in_specs=in_specs,
-        out_specs=[VMEM] * len(out_shape) if many else VMEM,
+        out_specs=out_specs,
         scratch_shapes=list(scratch),
         compiler_params=pltpu.CompilerParams(vmem_limit_bytes=megabytes * 1024 * 1024),
         cost_estimate=pl.CostEstimate(
@@ -83,17 +85,14 @@
                 )
 
 
-def coeff_kernel(u, right, out):
-    blocks, rank, size = right.shape
+def coeff_kernel(count, far_cols, u, right, coup, z_out, out):
+    ops, blocks, far, rank, _ = coup.shape
+    size = right.shape[2]
     z = [dot(right[b], u[b * size:(b + 1) * size, :]) for b in range(blocks)]
     for pair in range(SLICES // 2):
         first, second = halves(chunk(z[0], pair), chunk(z[1], pair))
-        out[2 * pair] = first.astype(BF16)
-        out[2 * pair + 1] = second.astype(BF16)
-
-
-def pack_kernel(far_cols, coup, out):
-    ops, blocks, far, rank, _ = coup.shape
+        z_out[2 * pair] = first.astype(BF16)
+        z_out[2 * pair + 1] = second.astype(BF16)
     whole, rest = [], []
     for b in range(blocks):
         tiles = [
@@ -106,7 +105,11 @@
     names = jnp.zeros((STATS, LANES), F32)
     for b in range(blocks):
         for f in range(far):
-            names = jnp.where(lane == b * far + f, far_cols[b, f].astype(F32), names)
+            col = far_cols[b, f]
+            device = lax.div(col, blocks)
+            slot = lax.rem(device, count) * SLICES + lax.div(device, count)
+            name = (slot * blocks + lax.rem(col, blocks)).astype(F32)
+            names = jnp.where(lane == b * far + f, name, names)
     out[...] = jnp.concatenate(
         whole + [jnp.concatenate(rest, axis=1), names.astype(BF16)], axis=0
     )
@@ -120,10 +123,6 @@
         out[s, 0:rows, :] = packed[...]
     for m, part in enumerate(parts):
         out[:, rows + m * rank:rows + (m + 1) * rank, :] = part[...]
-
-
-def copy_kernel(source, target):
-    target[...] = source[...]
 
 
 def coupling_rows(held, s, b, ops, rank):
@@ -163,7 +162,7 @@
     return pl.multiple_of(lax.rem(group[0] + (groups - m), groups) * step, step)
 
 
-def first_couple(ops, rank, far, cols, group, held, out, zs):
+def first_couple(ops, rank, far, cols, group, after, held, out, zs):
     step = SLICES * 2 * rank
     count = zs.shape[0] // step
     for m in range(count):
@@ -335,7 +334,10 @@
     ext,
     coef,
     stat,
+    out,
+    outs,
 ):
+    copies = []
     ops = images.shape[0]
     blocks, rank, size = left.shape
     rows, columns = uown.shape
@@ -366,11 +368,17 @@
             product = near_product(w.at[b, o * size:(o + 1) * size], parts, b, blocks, size)
             far = dot(left[b], coef[b, o * rank:(o + 1) * rank, :], ((0,), (0,)))
             mine = ext[o, 1, b * size:(b + 1) * size, :].astype(F32)
-            images[o, b * size:(b + 1) * size, :] = (
+            here = slice(b * size, (b + 1) * size)
+            out[o, here, :] = (
                 product
                 + diagonal_of(diag, o, b, size, columns) * mine
                 + far.astype(BF16).astype(F32)
             )
+            copy = pltpu.make_async_copy(out.at[o, here], images.at[o, here], outs.at[o, b])
+            copy.start()
+            copies.append(copy)
+    for copy in copies:
+        copy.wait()
 
 
 def ring(block):
@@ -398,7 +406,7 @@
     rows, columns = sources.shape
     all_blocks = blocks * n
     count = n // SLICES
-    groups = [[g * SLICES + s for s in range(SLICES)] for g in range(count)]
+    groups = [[s * count + g for s in range(SLICES)] for g in range(count)]
     sds = jax.ShapeDtypeStruct
     body = ops * rank
 
@@ -408,25 +416,25 @@
     def across(x):
         parts = [x]
         for m in range(1, count):
-            pairs = [(i, (i + m * SLICES) % n) for i in range(n)]
+            pairs = [(i, i - i % count + (i + m) % count) for i in range(n)]
             parts.append(lax.ppermute(x, "store", pairs))
         return parts
 
     place = lax.axis_index("store").astype(jnp.int32)
     row0 = (place * blocks).reshape(1)
-    group = lax.div(place, jnp.int32(SLICES)).reshape(1)
+    group = lax.rem(place, jnp.int32(count)).reshape(1)
     left = jnp.transpose(basis_left, (0, 2, 1))
     right = jnp.transpose(basis_right, (0, 2, 1))
 
     low, high = ring(sources)
-    z1 = call(coeff_kernel, sds((SLICES, rank, LANES), BF16), [VMEM, VMEM], megabytes=60)(
-        sources, right
-    )
+    shared = (blocks + 1) * body
+    z1, packed = call(
+        functools.partial(coeff_kernel, count),
+        [sds((SLICES, rank, LANES), BF16), sds((shared + STATS, LANES), BF16)],
+        [SMEM, VMEM, VMEM, VMEM],
+        megabytes=60,
+    )(far_cols, sources, right, couplings)
     z1 = across(z1)
-    shared = (blocks + 1) * body
-    packed = call(pack_kernel, sds((shared + STATS, LANES), BF16), [SMEM, VMEM])(
-        far_cols, couplings
-    )
     held = call(
         share_kernel,
         sds((SLICES, shared + STATS + count * rank, LANES), BF16),
@@ -441,18 +449,18 @@
         [SMEM, SMEM, SMEM, VMEM],
         micros=2.5,
     )(near_cols, near_count, row0, near_tiles)
+    image = call(near_kernel, sds((ops, rows, columns), F32), [VMEM] * 5, micros=3.0)(
+        w, low, sources, high, self_terms
+    )
 
     c1 = call(
         functools.partial(first_couple, ops, rank, far),
         sds((SLICES, body, LANES), BF16),
-        [SMEM, SMEM, VMEM],
+        [SMEM, SMEM, ANY, VMEM],
         [pltpu.VMEM((n * blocks * rank, LANES), BF16)],
-    )(cols, group, held)
+    )(cols, group, image, held)
     c1 = exchange(c1)
 
-    image = call(near_kernel, sds((ops, rows, columns), F32), [VMEM] * 5, micros=3.0)(
-        w, low, sources, high, self_terms
-    )
     first, second, msg = call(
         image_kernel,
         [
@@ -467,10 +475,9 @@
         ],
         micros=2.0,
     )(sources, image, left, right, c1)
-    msg = exchange(msg)
-    msgs = across(call(copy_kernel, sds(msg.shape, BF16), [VMEM], micros=30.0)(msg))
     low0, high0 = ring(first)
     low1, high1 = ring(second)
+    msgs = across(exchange(msg))
 
     c2 = call(
         functools.partial(second_couple, all_blocks * size, ops, rank, far),
@@ -492,8 +499,11 @@
             pltpu.VMEM((ops, 3, rows, columns), BF16),
             pltpu.VMEM((blocks, body, columns), BF16),
             pltpu.VMEM((STATS, columns), F32),
+            pltpu.VMEM((ops, rows, columns), F32),
+            pltpu.SemaphoreType.DMA((ops, blocks)),
         ],
         micros=4.0,
+        out_specs=[ANY, VMEM, VMEM],
     )(w, low, sources, high, low0, first, high0, low1, second, high1, self_terms, left, c2)
     return images, heights, norms
 

time: 93.8 us -> 95 us (1.013)
  starting transfers between devices: 45.7 us -> 18 us
  blocking collectives: 0 us -> 25.8 us
  waiting for transfers between devices: 20 us -> 25.1 us
  Pallas kernels: 18.6 us -> 16.8 us
    all_to_all x0 -> x2, blocking collectives: none -> 25.8 us  [exchange(): lax.all_to_all(x, 'store', 0, 0, axis_index_groups=groups, tiled=True)]
    all_to_all x4 -> x2, starting transfers between devices: 27.7 us -> 10.7 us  [exchange(): lax.all_to_all(x, 'store', 0, 0, axis_index_groups=groups, tiled=True)]
    ppermute x3, waiting for transfers between devices: 0.01 us -> 11.3 us  [ring(): lax.ppermute(block, 'store', backward)]
    ppermute x2, waiting for transfers between devices: 12.2 us -> 1.12 us  [across(): parts.append(lax.ppermute(x, 'store', pairs))]
    ppermute x3, waiting for transfers between devices: 0.01 us -> 9.88 us  [ring(): lax.ppermute(block, 'store', forward)]
    ppermute x2, starting transfers between devices: 7.28 us -> 0.46 us  [across(): parts.append(lax.ppermute(x, 'store', pairs))]
    all_to_all x4 -> x2, waiting for transfers between devices: 7.79 us -> 2.78 us  [exchange(): lax.all_to_all(x, 'store', 0, 0, axis_index_groups=groups, tiled=True)]
    ppermute x3, starting transfers between devices: 10.7 us -> 6.84 us  [ring(): lax.ppermute(block, 'store', backward)]
  transfers between devices with their start and end apart: 12 -> 10, of which waited for: 5 -> 6; matrix products, arithmetic and copies ran while one was open for 0% -> 0% of each run, Pallas kernels for 9% -> 6%
where the time goes in v13:
time: 95 us; the launch traced here: 94.4 us
  blocking collectives  25.8 us (27%)
  waiting for transfers between devices  25.1 us (26%)
  starting transfers between devices  18 us (19%)
  Pallas kernels  16.8 us (18%)
  local copies, waits for them, and re-layouts  8 us (8%)
    all_to_all x2, blocking collectives, exchange(): lax.all_to_all(x, 'store', 0, 0, axis_index_groups=groups, tiled=True)  25.8 us
    ppermute x3, waiting for transfers between devices, ring(): lax.ppermute(block, 'store', backward)  11.3 us
    all_to_all x2, starting transfers between devices, exchange(): lax.all_to_all(x, 'store', 0, 0, axis_index_groups=groups, tiled=True)  10.7 us
    ppermute x3, waiting for transfers between devices, ring(): lax.ppermute(block, 'store', forward)  9.88 us
    unnamed x30, local copies, waits for them, and re-layouts  7.92 us
    ppermute x3, starting transfers between devices, ring(): lax.ppermute(block, 'store', backward)  6.84 us
    pallas_call x1, Pallas kernels, shards(): call(final_kernel, [sds((ops, rows, columns), F32), sds((ops, columns), F...  5.32 us
    all_to_all x2, waiting for transfers between devices, exchange(): lax.all_to_all(x, 'store', 0, 0, axis_index_groups=groups, tiled=True)  2.78 us
  transfers between devices with their start and end apart: 10, of which 6 were waited for; matrix products, arithmetic and copies ran while one was open for 0% of the time, Pallas kernels for 6%

profile of v13, /device:TPU:0, one launch (start us, length us, event | category | flops | bytes accessed | tf_op | source)
XLA Modules:
  0.0 94.4 jit_solution(12071713632060929361)
XLA Ops:
  0.6 2.0 %shard_map.114 = (bf16[8,32,128]{2,1,0:T(8,128)(2,1)}, bf16[208,128]{1,0:T(8,128)(2,1)}) custom-call(s32[2,6]{1,0:T(2,128)} %far_cols.1, bf16[512,512]{1,0:T(8,128)(2,1)} %uown.1, bf16[2,32,256]{2,1,0:T(8,128)(2,1)} %bitcast.4, bf16[2,2,6,32,32]{4,3,2,1,0:T(8,128)(2,1)} %coup.1), custom_call_target="tpu_custom_call" | custom-call | flops 1150000000 | tf_op jit(solution)/shard_map/pallas_call | solution.py:431
  2.7 0.5 collective-permute-start.2
  3.1 1.1 %collective-permute-done.2.refs_1_ = bf16[8,32,128]{2,1,0:T(8,128)(2,1)S(1)} collective-permute-done((bf16[8,32,128]{2,1,0:T(8,128)(2,1)}, bf16[8,32,128]{2,1,0:T(8,128)(2,1)S(1)}, u32[]{:S(2)}, u32[]{:S(2)}) %collective-permute-start.2) | collective-permute-done | bytes 65568 | tf_op jit(solution)/shard_map/ppermute | solution.py:420
  4.2 0.0 copy-start.3
  4.2 0.8 copy-done.3
  5.1 0.0 copy-start.14
  5.1 0.8 copy-done.14
  5.9 0.0 copy-start
  5.9 0.0 copy-start.7
  5.9 0.0 copy-start.8
  5.9 0.9 shard_map.115
  6.8 7.3 %all-to-all-start = ((bf16[8,272,128]{2,1,0:T(8,128)(2,1)}), bf16[8,272,128]{2,1,0:T(8,128)(2,1)S(1)}, u32[]{:S(2)}, u32[]{:S(2)}) async-start(bf16[8,272,128]{2,1,0:T(8,128)(2,1)} %shard_map.115), calls=%async_computation | async-start | bytes 1114112 | tf_op jit(solution)/shard_map/all_to_all | solution.py:414
  14.1 3.9 %collective-permute-start.1 = (bf16[512,512]{1,0:T(8,128)(2,1)}, bf16[512,512]{1,0:T(8,128)(2,1)}, u32[]{:S(2)}, u32[]{:S(2)}) collective-permute-start(bf16[512,512]{1,0:T(8,128)(2,1)} %uown.1), channel_id=1, source_target_pairs={{1,0},{2,1},{3,2},{4,3},{5,4},{6,5},{7,6},{8,7},{9,8},{10,9},{11,1... | collective-permute-start | bytes 1572872 | tf_op jit(solution)/shard_map/ppermute | solution.py:388
  18.0 0.0 collective-permute-start
  18.0 0.0 copy-done
  18.0 0.0 copy-done.7
  18.0 0.0 copy-done.8
  18.0 0.0 copy-start.1
  18.0 0.0 copy-start.6
  18.0 0.9 shard_map.112.w
  18.9 10.3 %collective-permute-done.1.high.uhigh = bf16[512,512]{1,0:T(8,128)(2,1)} collective-permute-done((bf16[512,512]{1,0:T(8,128)(2,1)}, bf16[512,512]{1,0:T(8,128)(2,1)}, u32[]{:S(2)}, u32[]{:S(2)}) %collective-permute-start.1) | collective-permute-done | bytes 524320 | tf_op jit(solution)/shard_map/ppermute | solution.py:388
  29.2 5.0 %collective-permute-done.low.ulow = bf16[512,512]{1,0:T(8,128)(2,1)} collective-permute-done((bf16[512,512]{1,0:T(8,128)(2,1)}, bf16[512,512]{1,0:T(8,128)(2,1)}, u32[]{:S(2)}, u32[]{:S(2)}) %collective-permute-start) | collective-permute-done | bytes 524320 | tf_op jit(solution)/shard_map/ppermute | solution.py:388
  34.2 0.0 copy-done.1
  34.2 0.0 copy-done.6
  34.2 2.7 %shard_map.113.after.near = f32[2,512,512]{2,1,0:T(8,128)S(1)} custom-call(bf16[2,512,1280]{2,1,0:T(8,128)(2,1)S(1)} %shard_map.112.w, bf16[512,512]{1,0:T(8,128)(2,1)} %collective-permute-done.low.ulow, bf16[512,512]{1,0:T(8,128)(2,1)S(1)} %copy-done.1, bf16[512,512]{1,0:T(8,128)(2,1)} %collective-permute-done.1.high.uhigh, f32[2,512]{1,0:T(2,128)S(1)} %copy-done.6), custom_call_target="tpu_custom_call" | custom-call | flops 3449999872 | tf_op jit(solution)/shard_map/pallas_call | solution.py:452
  36.9 0.0 copy-start.9
  36.9 1.3 %copy-done.9 = f32[2,512,512]{2,1,0:T(8,128)} copy-done((f32[2,512,512]{2,1,0:T(8,128)}, f32[2,512,512]{2,1,0:T(8,128)S(1)}, u32[]{:S(2)}) %copy-start.9) | copy-done | bytes 2097176
  38.2 0.0 copy-start.12
  38.2 1.5 %copy-done.12 = bf16[2,512,1280]{2,1,0:T(8,128)(2,1)} copy-done((bf16[2,512,1280]{2,1,0:T(8,128)(2,1)}, bf16[2,512,1280]{2,1,0:T(8,128)(2,1)S(1)}, u32[]{:S(2)}) %copy-start.12) | copy-done | bytes 2621464
  39.8 0.0 copy-start.2
  39.8 0.0 copy-start.4
  39.8 0.0 copy-start.5
  39.8 0.0 all-to-all-done.held
  39.8 0.1 reshape.18.cols
  39.9 0.0 copy-start.10
  39.9 1.7 %copy-done.10 = f32[2,512,512]{2,1,0:T(8,128)S(1)} copy-done((f32[2,512,512]{2,1,0:T(8,128)S(1)}, f32[2,512,512]{2,1,0:T(8,128)}, u32[]{:S(2)}) %copy-start.10) | copy-done | bytes 2097176
  41.5 0.0 copy-start.11
  41.5 1.1 %shard_map.116 = bf16[8,64,128]{2,1,0:T(8,128)(2,1)S(1)} custom-call(s32[96]{0:T(128)S(1)} %reshape.18.cols, s32[1]{0:T(128)} %bitcast.3.group, f32[2,512,512]{2,1,0:T(8,128)S(1)} %copy-done.10, bf16[8,272,128]{2,1,0:T(8,128)(2,1)S(1)} %all-to-all-done.held), custom_call_target="tpu_custom_call" | custom-call | flops 1150000000 | tf_op jit(solution)/shard_map/pallas_call | solution.py:456
  42.7 11.3 %all_to_all.20.cmsg = bf16[8,64,128]{2,1,0:T(8,128)(2,1)S(1)} all-to-all(bf16[8,64,128]{2,1,0:T(8,128)(2,1)S(1)} %shard_map.116), channel_id=1, replica_groups={{0,2,4,6,8,10,12,14},{1,3,5,7,9,11,13,15},{16,18,20,22,24,26,28,30},{17..., dimensions={0} | all-to-all | bytes 262144 | tf_op jit(solution)/shard_map/all_to_all | solution.py:414
  54.0 0.0 copy-done.2
  54.0 0.0 copy-done.4
  54.0 0.0 copy-done.5
  54.0 0.0 copy-done.11
  54.0 1.5 %shard_map.117 = (bf16[528,512]{1,0:T(8,128)(2,1)S(1)}, bf16[512,512]{1,0:T(8,128)(2,1)S(1)}, bf16[8,80,128]{2,1,0:T(8,128)(2,1)S(1)}) custom-call(bf16[512,512]{1,0:T(8,128)(2,1)S(1)} %copy-done.2, f32[2,512,512]{2,1,0:T(8,128)S(1)} %copy-done.11, bf16[2,32,256]{2,1,0:T(8,128)(2,1)S(1)} %bitcast.6, bf16[2,32,256]{2,1,0:T(8,128)(2,1)S(1)} %bitcast.5, ...), custom_call_target="tpu_custom_call" | custom-call | flops 2300000000 | tf_op jit(solution)/shard_map/pallas_call | solution.py:464
  55.5 0.9 collective-permute-start.4
  56.4 0.0 collective-permute-start.3
  56.4 14.5 %all_to_all.21.refs_0_ = bf16[8,80,128]{2,1,0:T(8,128)(2,1)S(1)} all-to-all(bf16[8,80,128]{2,1,0:T(8,128)(2,1)S(1)} %get-tuple-element.12), channel_id=1, replica_groups={{0,2,4,6,8,10,12,14},{1,3,5,7,9,11,13,15},{16,18,20,22,24,26,28,30},{17..., dimensions={0} | all-to-all | bytes 327680 | tf_op jit(solution)/shard_map/all_to_all | solution.py:414
  70.9 0.0 collective-permute-start.7
  70.9 2.1 %collective-permute-start.6 = (bf16[512,512]{1,0:T(8,128)(2,1)S(1)}, bf16[512,512]{1,0:T(8,128)(2,1)}, u32[]{:S(2)}, u32[]{:S(2)}) collective-permute-start(bf16[512,512]{1,0:T(8,128)(2,1)S(1)} %get-tuple-element.11.second), channel_id=1, source_target_pairs={{1,0},{2,1},{3,2},{4,3},{5,4},{6,5},{7,6},{8,7},{9,8},{10,9},{11,1... | collective-permute-start | bytes 1572872 | tf_op jit(solution)/shard_map/ppermute | solution.py:388
  72.9 0.0 collective-permute-start.5
  72.9 0.0 collective-permute-done.7.refs_1_
  72.9 0.0 collective-permute-done.4.after_high.high0
  72.9 0.0 collective-permute-done.3.after_low.low0
  73.0 2.3 %shard_map.118 = bf16[8,80,128]{2,1,0:T(8,128)(2,1)} custom-call(s32[96]{0:T(128)S(1)} %reshape.18.cols, s32[1]{0:T(128)} %bitcast.3.group, bf16[528,512]{1,0:T(8,128)(2,1)S(1)} %collective-permute-done.3.after_low.low0, bf16[528,512]{1,0:T(8,128)(2,1)S(1)} %collective-permute-done.4.after_high.high0, bf16[8,272,128]{2,1,0:T(8,128)(2,1)S(1)} %all-to-all-done.held, ...), custom_call_target="tpu_custom_call" | custom-call | flops 34500001792 | tf_op jit(solution)/shard_map/pallas_call | solution.py:482
  75.2 3.4 %all-to-all-start.3 = ((bf16[8,80,128]{2,1,0:T(8,128)(2,1)}), bf16[8,80,128]{2,1,0:T(8,128)(2,1)S(1)}, u32[]{:S(2)}, u32[]{:S(2)}) async-start(bf16[8,80,128]{2,1,0:T(8,128)(2,1)} %shard_map.118), calls=%async_computation.3 | async-start | bytes 327680 | tf_op jit(solution)/shard_map/all_to_all | solution.py:414
  78.6 1.0 %collective-permute-done.6.high1 = bf16[512,512]{1,0:T(8,128)(2,1)} collective-permute-done((bf16[512,512]{1,0:T(8,128)(2,1)S(1)}, bf16[512,512]{1,0:T(8,128)(2,1)}, u32[]{:S(2)}, u32[]{:S(2)}) %collective-permute-start.6) | collective-permute-done | bytes 524320 | tf_op jit(solution)/shard_map/ppermute | solution.py:388
  79.6 4.9 %collective-permute-done.5.low1 = bf16[512,512]{1,0:T(8,128)(2,1)} collective-permute-done((bf16[512,512]{1,0:T(8,128)(2,1)S(1)}, bf16[512,512]{1,0:T(8,128)(2,1)}, u32[]{:S(2)}, u32[]{:S(2)}) %collective-permute-start.5) | collective-permute-done | bytes 524320 | tf_op jit(solution)/shard_map/ppermute | solution.py:388
  84.5 2.8 %all-to-all-done.3.cmsg = bf16[8,80,128]{2,1,0:T(8,128)(2,1)S(1)} async-done(((bf16[8,80,128]{2,1,0:T(8,128)(2,1)}), bf16[8,80,128]{2,1,0:T(8,128)(2,1)S(1)}, u32[]{:S(2)}, u32[]{:S(2)}) %all-to-all-start.3) | async-done | bytes 163872 | tf_op jit(solution)/shard_map/all_to_all | solution.py:414
  87.3 0.0 copy-start.13
  87.3 1.7 %copy-done.13 = bf16[2,512,1280]{2,1,0:T(8,128)(2,1)S(1)} copy-done((bf16[2,512,1280]{2,1,0:T(8,128)(2,1)S(1)}, bf16[2,512,1280]{2,1,0:T(8,128)(2,1)}, u32[]{:S(2)}) %copy-start.13) | copy-done | bytes 2621464
  89.1 5.3 %shard_map.119 = (f32[2,512,512]{2,1,0:T(8,128)}, f32[2,512]{1,0:T(2,128)}, f32[2,512]{1,0:T(2,128)}) custom-call(bf16[2,512,1280]{2,1,0:T(8,128)(2,1)S(1)} %copy-done.13, bf16[512,512]{1,0:T(8,128)(2,1)} %collective-permute-done.low.ulow, bf16[512,512]{1,0:T(8,128)(2,1)S(1)} %copy-done.2, bf16[512,512]{1,0:T(8,128)(2,1)} %collective-permute-done.1.high.uhigh, ...), custom_call_target="tpu_custom_call" | custom-call | flops 4600000000 | tf_op jit(solution)/shard_map/pallas_call | solution.py:494
  (1 shorter events, 0.0 us)
Async XLA Ops:
  2.7 1.6 %collective-permute-start.2 = (bf16[8,32,128]{2,1,0:T(8,128)(2,1)}, bf16[8,32,128]{2,1,0:T(8,128)(2,1)S(1)}, u32[]{:S(2)}, u32[]{:S(2)}) collective-permute-start(bf16[8,32,128]{2,1,0:T(8,128)(2,1)} %get-tuple-element.9.refs_0_), channel_id=1, source_target_pairs={{0,1},{1,0},{2,3},{3,2},{4,5},{5,4},{6,7},{7,6},{8,9},{9,8},{10,11... | collective-permute-start | bytes 196616 | tf_op jit(solution)/shard_map/ppermute | solution.py:420
  4.2 0.8 copy-start.3
  5.1 0.8 copy-start.14
  5.9 12.1 %copy-start = (bf16[2,2,5,256,256]{4,3,2,1,0:T(8,128)(2,1)S(1)}, bf16[2,2,5,256,256]{4,3,2,1,0:T(8,128)(2,1)}, u32[]{:S(2)}) copy-start(bf16[2,2,5,256,256]{4,3,2,1,0:T(8,128)(2,1)} %tiles.1) | copy-start | bytes 7864324
  5.9 12.1 %copy-start.7 = (s32[2,5]{1,0:T(2,128)S(1)}, s32[2,5]{1,0:T(2,128)}, u32[]{:S(2)}) copy-start(s32[2,5]{1,0:T(2,128)} %cols.1) | copy-start | bytes 124
  5.9 12.1 %copy-start.8 = (s32[2]{0:T(128)S(1)}, s32[2]{0:T(128)}, u32[]{:S(2)}) copy-start(s32[2]{0:T(128)} %count.1) | copy-start | bytes 28
  6.8 33.0 %all-to-all-start = ((bf16[8,272,128]{2,1,0:T(8,128)(2,1)}), bf16[8,272,128]{2,1,0:T(8,128)(2,1)S(1)}, u32[]{:S(2)}, u32[]{:S(2)}) async-start(bf16[8,272,128]{2,1,0:T(8,128)(2,1)} %shard_map.115), calls=%async_computation | async-start | bytes 1114112 | tf_op jit(solution)/shard_map/all_to_all | solution.py:414
  14.1 15.2 %collective-permute-start.1 = (bf16[512,512]{1,0:T(8,128)(2,1)}, bf16[512,512]{1,0:T(8,128)(2,1)}, u32[]{:S(2)}, u32[]{:S(2)}) collective-permute-start(bf16[512,512]{1,0:T(8,128)(2,1)} %uown.1), channel_id=1, source_target_pairs={{1,0},{2,1},{3,2},{4,3},{5,4},{6,5},{7,6},{8,7},{9,8},{10,9},{11,1... | collective-permute-start | bytes 1572872 | tf_op jit(solution)/shard_map/ppermute | solution.py:388
  18.0 16.2 %collective-permute-start = (bf16[512,512]{1,0:T(8,128)(2,1)}, bf16[512,512]{1,0:T(8,128)(2,1)}, u32[]{:S(2)}, u32[]{:S(2)}) collective-permute-start(bf16[512,512]{1,0:T(8,128)(2,1)} %uown.1), channel_id=1, source_target_pairs={{0,1},{1,2},{2,3},{3,4},{4,5},{5,6},{6,7},{7,8},{8,9},{9,10},{10,1... | collective-permute-start | bytes 1572872 | tf_op jit(solution)/shard_map/ppermute | solution.py:388
  18.0 16.2 %copy-start.1 = (bf16[512,512]{1,0:T(8,128)(2,1)S(1)}, bf16[512,512]{1,0:T(8,128)(2,1)}, u32[]{:S(2)}) copy-start(bf16[512,512]{1,0:T(8,128)(2,1)} %uown.1) | copy-start | bytes 1572868
  18.0 16.2 %copy-start.6 = (f32[2,512]{1,0:T(2,128)S(1)}, f32[2,512]{1,0:T(2,128)}, u32[]{:S(2)}) copy-start(f32[2,512]{1,0:T(2,128)} %diag.3) | copy-start | bytes 12292
  36.9 1.3 %copy-start.9 = (f32[2,512,512]{2,1,0:T(8,128)}, f32[2,512,512]{2,1,0:T(8,128)S(1)}, u32[]{:S(2)}) copy-start(f32[2,512,512]{2,1,0:T(8,128)S(1)} %shard_map.113.after.near) | copy-start | bytes 6291460
  38.2 1.5 %copy-start.12 = (bf16[2,512,1280]{2,1,0:T(8,128)(2,1)}, bf16[2,512,1280]{2,1,0:T(8,128)(2,1)S(1)}, u32[]{:S(2)}) copy-start(bf16[2,512,1280]{2,1,0:T(8,128)(2,1)S(1)} %shard_map.112.w) | copy-start | bytes 7864324
  39.8 14.3 %copy-start.2 = (bf16[512,512]{1,0:T(8,128)(2,1)S(1)}, bf16[512,512]{1,0:T(8,128)(2,1)}, u32[]{:S(2)}) copy-start(bf16[512,512]{1,0:T(8,128)(2,1)} %uown.1) | copy-start | bytes 1572868
  39.8 14.3 %copy-start.4 = (bf16[2,256,32]{1,2,0:T(8,128)(2,1)S(1)}, bf16[2,256,32]{1,2,0:T(8,128)(2,1)}, u32[]{:S(2)}) copy-start(bf16[2,256,32]{1,2,0:T(8,128)(2,1)} %param.16) | copy-start | bytes 98308
  39.8 14.3 %copy-start.5 = (bf16[2,256,32]{1,2,0:T(8,128)(2,1)S(1)}, bf16[2,256,32]{1,2,0:T(8,128)(2,1)}, u32[]{:S(2)}) copy-start(bf16[2,256,32]{1,2,0:T(8,128)(2,1)} %param.15) | copy-start | bytes 98308
  39.9 1.7 %copy-start.10 = (f32[2,512,512]{2,1,0:T(8,128)S(1)}, f32[2,512,512]{2,1,0:T(8,128)}, u32[]{:S(2)}) copy-start(f32[2,512,512]{2,1,0:T(8,128)} %copy-done.9) | copy-start | bytes 6291460
  41.5 12.5 %copy-start.11 = (f32[2,512,512]{2,1,0:T(8,128)S(1)}, f32[2,512,512]{2,1,0:T(8,128)}, u32[]{:S(2)}) copy-start(f32[2,512,512]{2,1,0:T(8,128)} %copy-done.9) | copy-start | bytes 6291460
  55.5 17.4 %collective-permute-start.4 = (bf16[528,512]{1,0:T(8,128)(2,1)S(1)}, bf16[528,512]{1,0:T(8,128)(2,1)S(1)}, u32[]{:S(2)}, u32[]{:S(2)}) collective-permute-start(bf16[528,512]{1,0:T(8,128)(2,1)S(1)} %get-tuple-element.10.first), channel_id=1, source_target_pairs={{1,0},{2,1},{3,2},{4,3},{5,4},{6,5},{7,6},{8,7},{9,8},{10,9},{11,1... | collective-permute-start | bytes 1622024 | tf_op jit(solution)/shard_map/ppermute | solution.py:388
  56.4 16.5 %collective-permute-start.3 = (bf16[528,512]{1,0:T(8,128)(2,1)S(1)}, bf16[528,512]{1,0:T(8,128)(2,1)S(1)}, u32[]{:S(2)}, u32[]{:S(2)}) collective-permute-start(bf16[528,512]{1,0:T(8,128)(2,1)S(1)} %get-tuple-element.10.first), channel_id=1, source_target_pairs={{0,1},{1,2},{2,3},{3,4},{4,5},{5,6},{6,7},{7,8},{8,9},{9,10},{10,1... | collective-permute-start | bytes 1622024 | tf_op jit(solution)/shard_map/ppermute | solution.py:388
  70.9 2.1 %collective-permute-start.7 = (bf16[8,80,128]{2,1,0:T(8,128)(2,1)S(1)}, bf16[8,80,128]{2,1,0:T(8,128)(2,1)S(1)}, u32[]{:S(2)}, u32[]{:S(2)}) collective-permute-start(bf16[8,80,128]{2,1,0:T(8,128)(2,1)S(1)} %all_to_all.21.refs_0_), channel_id=1, source_target_pairs={{0,1},{1,0},{2,3},{3,2},{4,5},{5,4},{6,7},{7,6},{8,9},{9,8},{10,11... | collective-permute-start | bytes 491528 | tf_op jit(solution)/shard_map/ppermute | solution.py:420
  70.9 8.8 %collective-permute-start.6 = (bf16[512,512]{1,0:T(8,128)(2,1)S(1)}, bf16[512,512]{1,0:T(8,128)(2,1)}, u32[]{:S(2)}, u32[]{:S(2)}) collective-permute-start(bf16[512,512]{1,0:T(8,128)(2,1)S(1)} %get-tuple-element.11.second), channel_id=1, source_target_pairs={{1,0},{2,1},{3,2},{4,3},{5,4},{6,5},{7,6},{8,7},{9,8},{10,9},{11,1... | collective-permute-start | bytes 1572872 | tf_op jit(solution)/shard_map/ppermute | solution.py:388
  72.9 11.6 %collective-permute-start.5 = (bf16[512,512]{1,0:T(8,128)(2,1)S(1)}, bf16[512,512]{1,0:T(8,128)(2,1)}, u32[]{:S(2)}, u32[]{:S(2)}) collective-permute-start(bf16[512,512]{1,0:T(8,128)(2,1)S(1)} %get-tuple-element.11.second), channel_id=1, source_target_pairs={{0,1},{1,2},{2,3},{3,4},{4,5},{5,6},{6,7},{7,8},{8,9},{9,10},{10,1... | collective-permute-start | bytes 1572872 | tf_op jit(solution)/shard_map/ppermute | solution.py:388
  75.2 12.1 %all-to-all-start.3 = ((bf16[8,80,128]{2,1,0:T(8,128)(2,1)}), bf16[8,80,128]{2,1,0:T(8,128)(2,1)S(1)}, u32[]{:S(2)}, u32[]{:S(2)}) async-start(bf16[8,80,128]{2,1,0:T(8,128)(2,1)} %shard_map.118), calls=%async_computation.3 | async-start | bytes 327680 | tf_op jit(solution)/shard_map/all_to_all | solution.py:414
  87.3 1.7 %copy-start.13 = (bf16[2,512,1280]{2,1,0:T(8,128)(2,1)S(1)}, bf16[2,512,1280]{2,1,0:T(8,128)(2,1)}, u32[]{:S(2)}) copy-start(bf16[2,512,1280]{2,1,0:T(8,128)(2,1)} %copy-done.12) | copy-start | bytes 7864324

commit v14 on v13

--- a/solution.py
+++ b/solution.py
@@ -22,7 +22,7 @@
 ANY = pl.BlockSpec(memory_space=pl.ANY)
 
 
-def call(body, out_shape, in_specs, scratch=(), micros=1.0, megabytes=20, out_specs=None):
+def call(body, out_shape, in_specs, scratch=(), micros=0.0, megabytes=20, out_specs=None):
     many = isinstance(out_shape, (list, tuple))
     if out_specs is None:
         out_specs = [VMEM] * len(out_shape) if many else VMEM
@@ -205,7 +205,8 @@
     return jnp.concatenate([column] * (columns // LANES), axis=1)
 
 
-def near_kernel(w, low, own, high, diag, image):
+def near_kernel(w, low, own, high, diag, image, token):
+    token[...] = jnp.zeros_like(token)
     ops, rows, columns = image.shape
     size = w.shape[1] // ops
     blocks = rows // size
@@ -447,18 +448,23 @@
         functools.partial(order_tiles, all_blocks),
         sds((blocks, ops * size, near * size), BF16),
         [SMEM, SMEM, SMEM, VMEM],
-        micros=2.5,
+        micros=0.0,
+        megabytes=60,
     )(near_cols, near_count, row0, near_tiles)
-    image = call(near_kernel, sds((ops, rows, columns), F32), [VMEM] * 5, micros=3.0)(
-        w, low, sources, high, self_terms
-    )
+    image, token = call(
+        near_kernel,
+        [sds((ops, rows, columns), F32), sds((8, LANES), F32)],
+        [VMEM] * 5,
+        micros=10.0,
+        megabytes=60,
+    )(w, low, sources, high, self_terms)
 
     c1 = call(
         functools.partial(first_couple, ops, rank, far),
         sds((SLICES, body, LANES), BF16),
         [SMEM, SMEM, ANY, VMEM],
         [pltpu.VMEM((n * blocks * rank, LANES), BF16)],
-    )(cols, group, image, held)
+    )(cols, group, token, held)
     c1 = exchange(c1)
 
     first, second, msg = call(

time: 95 us -> 95.4 us (level); the launches traced: 94.4 us -> 93.8 us
  waiting for transfers between devices: 25.1 us -> 16.3 us
  Pallas kernels: 16.8 us -> 22 us
  local copies, waits for them, and re-layouts: 8 us -> 12.6 us
  blocking collectives: 25.8 us -> 24.7 us
    ppermute x3, waiting for transfers between devices: 11.3 us -> 0.01 us  [ring(): lax.ppermute(block, 'store', backward)]
    all_to_all x2, waiting for transfers between devices: 2.78 us -> 11.8 us  [exchange(): lax.all_to_all(x, 'store', 0, 0, axis_index_groups=groups, tiled=True)]
    ppermute x3, waiting for transfers between devices: 9.88 us -> 4.42 us  [ring(): lax.ppermute(block, 'store', forward)]
    unnamed x30 -> x40, local copies, waits for them, and re-layouts: 7.92 us -> 12.6 us
    pallas_call x1, Pallas kernels: 0.9 us -> 3.47 us  [shards(): call(functools.partial(order_tiles, all_blocks), sds((blocks, ops * size,...]
    pallas_call x1, Pallas kernels: 2.72 us -> 4.99 us  [shards(): call(near_kernel, [sds((ops, rows, columns), F32), sds((8, LANES), F32)],...]
    all_to_all x2, starting transfers between devices: 10.7 us -> 9.48 us  [exchange(): lax.all_to_all(x, 'store', 0, 0, axis_index_groups=groups, tiled=True)]
    ppermute x2, waiting for transfers between devices: 1.12 us -> 0.01 us  [across(): parts.append(lax.ppermute(x, 'store', pairs))]
  transfers between devices with their start and end apart: 10 -> 10, of which waited for: 6 -> 3; matrix products, arithmetic and copies ran while one was open for 0% -> 0% of each run, Pallas kernels for 6% -> 15%
where the time goes in v14:
time: 95.4 us; the launch traced here: 93.8 us
  blocking collectives  24.7 us (26%)
  Pallas kernels  22 us (23%)
  starting transfers between devices  17.4 us (18%)
  waiting for transfers between devices  16.3 us (17%)
  local copies, waits for them, and re-layouts  12.6 us (13%)
    all_to_all x2, blocking collectives, exchange(): lax.all_to_all(x, 'store', 0, 0, axis_index_groups=groups, tiled=True)  24.7 us
    unnamed x40, local copies, waits for them, and re-layouts  12.6 us
    all_to_all x2, waiting for transfers between devices, exchange(): lax.all_to_all(x, 'store', 0, 0, axis_index_groups=groups, tiled=True)  11.8 us
    all_to_all x2, starting transfers between devices, exchange(): lax.all_to_all(x, 'store', 0, 0, axis_index_groups=groups, tiled=True)  9.48 us
    ppermute x3, starting transfers between devices, ring(): lax.ppermute(block, 'store', backward)  7.63 us
    pallas_call x1, Pallas kernels, shards(): call(final_kernel, [sds((ops, rows, columns), F32), sds((ops, columns), F...  5.15 us
    pallas_call x1, Pallas kernels, shards(): call(near_kernel, [sds((ops, rows, columns), F32), sds((8, LANES), F32)],...  4.99 us
    ppermute x3, waiting for transfers between devices, ring(): lax.ppermute(block, 'store', forward)  4.42 us
  transfers between devices with their start and end apart: 10, of which 3 were waited for; matrix products, arithmetic and copies ran while one was open for 0% of the time, Pallas kernels for 15%

profile of v14, /device:TPU:0, one launch (start us, length us, event | category | flops | bytes accessed | tf_op | source)
XLA Modules:
  0.0 93.8 jit_solution(4243251286055404154)
XLA Ops:
  0.6 5.5 %collective-permute-start.1 = (bf16[512,512]{1,0:T(8,128)(2,1)}, bf16[512,512]{1,0:T(8,128)(2,1)S(1)}, u32[]{:S(2)}, u32[]{:S(2)}) collective-permute-start(bf16[512,512]{1,0:T(8,128)(2,1)} %uown.1), channel_id=1, source_target_pairs={{1,0},{2,1},{3,2},{4,3},{5,4},{6,5},{7,6},{8,7},{9,8},{10,9},{11,1... | collective-permute-start | bytes 1572872 | tf_op jit(solution)/shard_map/ppermute | solution.py:389
  6.1 0.0 collective-permute-start
  6.1 2.0 %shard_map.114 = (bf16[8,32,128]{2,1,0:T(8,128)(2,1)}, bf16[208,128]{1,0:T(8,128)(2,1)}) custom-call(s32[2,6]{1,0:T(2,128)} %far_cols.1, bf16[512,512]{1,0:T(8,128)(2,1)} %uown.1, bf16[2,32,256]{2,1,0:T(8,128)(2,1)} %bitcast.4, bf16[2,2,6,32,32]{4,3,2,1,0:T(8,128)(2,1)} %coup.1), custom_call_target="tpu_custom_call" | custom-call | tf_op jit(solution)/shard_map/pallas_call | solution.py:432
  8.2 0.0 collective-permute-start.2
  8.2 0.0 copy-start.3
  8.2 3.5 %shard_map.112.w = bf16[2,512,1280]{2,1,0:T(8,128)(2,1)} custom-call(s32[2,5]{1,0:T(2,128)} %cols.1, s32[2]{0:T(128)} %count.1, s32[1]{0:T(128)} %bitcast.row0, bf16[2,2,5,256,256]{4,3,2,1,0:T(8,128)(2,1)} %tiles.1), custom_call_target="tpu_custom_call" | custom-call | tf_op jit(solution)/shard_map/pallas_call | solution.py:447
  11.6 0.0 collective-permute-done.2.refs_1_
  11.6 0.0 copy-done.3
  11.6 0.0 copy-done.4
  11.7 0.9 shard_map.115
  12.5 6.1 %all-to-all-start = ((bf16[8,272,128]{2,1,0:T(8,128)(2,1)}), bf16[8,272,128]{2,1,0:T(8,128)(2,1)S(1)}, u32[]{:S(2)}, u32[]{:S(2)}) async-start(bf16[8,272,128]{2,1,0:T(8,128)(2,1)} %shard_map.115), calls=%async_computation | async-start | bytes 1114112 | tf_op jit(solution)/shard_map/all_to_all | solution.py:415
  18.6 0.0 copy-start.1
  18.6 0.0 copy-start.5
  18.6 0.0 copy-start.17
  18.7 0.0 collective-permute-done.1.high.uhigh
  18.7 0.0 copy-start.13
  18.7 0.0 collective-permute-done.low.ulow
  18.7 0.8 copy-done.13
  19.5 0.0 copy-start.15
  19.5 0.8 copy-done.15
  20.3 5.0 %shard_map.113 = (f32[2,512,512]{2,1,0:T(8,128)}, f32[8,128]{1,0:T(8,128)}) custom-call(bf16[2,512,1280]{2,1,0:T(8,128)(2,1)} %shard_map.112.w, bf16[512,512]{1,0:T(8,128)(2,1)} %copy-done.15, bf16[512,512]{1,0:T(8,128)(2,1)} %uown.1, bf16[512,512]{1,0:T(8,128)(2,1)} %copy-done.13, f32[2,512]{1,0:T(2,128)} %diag.3), custom_call_target="tpu_custom_call" | custom-call | flops 11500000256 | tf_op jit(solution)/shard_map/pallas_call | solution.py:454
  25.3 8.7 %all-to-all-done.held = bf16[8,272,128]{2,1,0:T(8,128)(2,1)S(1)} async-done(((bf16[8,272,128]{2,1,0:T(8,128)(2,1)}), bf16[8,272,128]{2,1,0:T(8,128)(2,1)S(1)}, u32[]{:S(2)}, u32[]{:S(2)}) %all-to-all-start) | async-done | bytes 557088 | tf_op jit(solution)/shard_map/all_to_all | solution.py:415
  34.0 0.1 reshape.18.cols
  34.1 0.0 copy-start.6
  34.1 0.7 copy-done.6
  34.8 1.1 %shard_map.116 = bf16[8,64,128]{2,1,0:T(8,128)(2,1)S(1)} custom-call(s32[96]{0:T(128)S(1)} %reshape.18.cols, s32[1]{0:T(128)} %bitcast.3.group, f32[8,128]{1,0:T(8,128)S(1)} %copy-done.6, bf16[8,272,128]{2,1,0:T(8,128)(2,1)S(1)} %all-to-all-done.held), custom_call_target="tpu_custom_call" | custom-call | tf_op jit(solution)/shard_map/pallas_call | solution.py:462
  35.9 10.8 %all_to_all.20.cmsg = bf16[8,64,128]{2,1,0:T(8,128)(2,1)S(1)} all-to-all(bf16[8,64,128]{2,1,0:T(8,128)(2,1)S(1)} %shard_map.116), channel_id=1, replica_groups={{0,2,4,6,8,10,12,14},{1,3,5,7,9,11,13,15},{16,18,20,22,24,26,28,30},{17..., dimensions={0} | all-to-all | bytes 262144 | tf_op jit(solution)/shard_map/all_to_all | solution.py:415
  46.7 0.0 copy-done.1
  46.7 0.0 copy-done.5
  46.7 0.0 copy-done.17
  46.7 0.0 copy-start.19
  46.7 1.6 %copy-done.19 = f32[2,512,512]{2,1,0:T(8,128)S(1)} copy-done((f32[2,512,512]{2,1,0:T(8,128)S(1)}, f32[2,512,512]{2,1,0:T(8,128)}, u32[]{:S(2)}) %copy-start.19) | copy-done | bytes 2097176
  48.3 2.1 %shard_map.117 = (bf16[528,512]{1,0:T(8,128)(2,1)S(1)}, bf16[512,512]{1,0:T(8,128)(2,1)}, bf16[8,80,128]{2,1,0:T(8,128)(2,1)S(1)}) custom-call(bf16[512,512]{1,0:T(8,128)(2,1)S(1)} %copy-done.1, f32[2,512,512]{2,1,0:T(8,128)S(1)} %copy-done.19, bf16[2,32,256]{2,1,0:T(8,128)(2,1)S(1)} %bitcast.6, bf16[2,32,256]{2,1,0:T(8,128)(2,1)S(1)} %bitcast.5, ...), custom_call_target="tpu_custom_call" | custom-call | flops 2300000000 | tf_op jit(solution)/shard_map/pallas_call | solution.py:470
  50.4 0.2 collective-permute-start.4
  50.6 0.3 collective-permute-start.3
  50.9 0.0 copy-start.7
  50.9 0.8 copy-done.7
  51.7 13.9 %all_to_all.21.refs_0_ = bf16[8,80,128]{2,1,0:T(8,128)(2,1)S(1)} all-to-all(bf16[8,80,128]{2,1,0:T(8,128)(2,1)S(1)} %get-tuple-element.16), channel_id=1, replica_groups={{0,2,4,6,8,10,12,14},{1,3,5,7,9,11,13,15},{16,18,20,22,24,26,28,30},{17..., dimensions={0} | all-to-all | bytes 327680 | tf_op jit(solution)/shard_map/all_to_all | solution.py:415
  65.6 0.0 collective-permute-start.7
  65.6 0.0 copy-start
  65.6 0.0 copy-start.18
  65.6 1.9 %collective-permute-start.6 = (bf16[512,512]{1,0:T(8,128)(2,1)}, bf16[512,512]{1,0:T(8,128)(2,1)}, u32[]{:S(2)}, u32[]{:S(2)}) collective-permute-start(bf16[512,512]{1,0:T(8,128)(2,1)} %get-tuple-element.15.second), channel_id=1, source_target_pairs={{1,0},{2,1},{3,2},{4,3},{5,4},{6,5},{7,6},{8,7},{9,8},{10,9},{11,1... | collective-permute-start | bytes 1572872 | tf_op jit(solution)/shard_map/ppermute | solution.py:389
  67.5 0.0 collective-permute-start.5
  67.5 0.0 collective-permute-done.7.refs_1_
  67.5 0.0 collective-permute-done.4.after_high.high0
  67.5 0.0 collective-permute-done.3.after_low.low0
  67.5 2.3 %shard_map.118 = bf16[8,80,128]{2,1,0:T(8,128)(2,1)} custom-call(s32[96]{0:T(128)S(1)} %reshape.18.cols, s32[1]{0:T(128)} %bitcast.3.group, bf16[528,512]{1,0:T(8,128)(2,1)S(1)} %collective-permute-done.3.after_low.low0, bf16[528,512]{1,0:T(8,128)(2,1)S(1)} %collective-permute-done.4.after_high.high0, bf16[8,272,128]{2,1,0:T(8,128)(2,1)S(1)} %all-to-all-done.held, ...), custom_call_target="tpu_custom_call" | custom-call | flops 34500001792 | tf_op jit(solution)/shard_map/pallas_call | solution.py:488
  69.8 0.8 copy-done.9
  70.6 0.8 copy-done.11
  71.4 3.4 %all-to-all-start.3 = ((bf16[8,80,128]{2,1,0:T(8,128)(2,1)}), bf16[8,80,128]{2,1,0:T(8,128)(2,1)S(1)}, u32[]{:S(2)}, u32[]{:S(2)}) async-start(bf16[8,80,128]{2,1,0:T(8,128)(2,1)} %shard_map.118), calls=%async_computation.3 | async-start | bytes 327680 | tf_op jit(solution)/shard_map/all_to_all | solution.py:415
  74.8 0.0 collective-permute-done.6.high1
  74.8 4.4 %collective-permute-done.5.low1 = bf16[512,512]{1,0:T(8,128)(2,1)} collective-permute-done((bf16[512,512]{1,0:T(8,128)(2,1)}, bf16[512,512]{1,0:T(8,128)(2,1)}, u32[]{:S(2)}, u32[]{:S(2)}) %collective-permute-start.5) | collective-permute-done | bytes 524320 | tf_op jit(solution)/shard_map/ppermute | solution.py:389
  79.2 3.1 %all-to-all-done.3.cmsg = bf16[8,80,128]{2,1,0:T(8,128)(2,1)S(1)} async-done(((bf16[8,80,128]{2,1,0:T(8,128)(2,1)}), bf16[8,80,128]{2,1,0:T(8,128)(2,1)S(1)}, u32[]{:S(2)}, u32[]{:S(2)}) %all-to-all-start.3) | async-done | bytes 163872 | tf_op jit(solution)/shard_map/all_to_all | solution.py:415
  82.3 0.0 copy-done
  82.3 0.0 copy-done.18
  82.3 0.0 copy-start.2
  82.3 1.0 %copy-done.2 = bf16[512,512]{1,0:T(8,128)(2,1)S(1)} copy-done((bf16[512,512]{1,0:T(8,128)(2,1)S(1)}, bf16[512,512]{1,0:T(8,128)(2,1)}, u32[]{:S(2)}) %copy-start.2) | copy-done | bytes 524312
  83.4 0.0 copy-start.8
  83.4 1.0 %copy-done.8 = bf16[528,512]{1,0:T(8,128)(2,1)S(1)} copy-done((bf16[528,512]{1,0:T(8,128)(2,1)S(1)}, bf16[528,512]{1,0:T(8,128)(2,1)}, u32[]{:S(2)}) %copy-start.8) | copy-done | bytes 540696
  84.4 1.0 %copy-done.10 = bf16[528,512]{1,0:T(8,128)(2,1)S(1)} copy-done((bf16[528,512]{1,0:T(8,128)(2,1)S(1)}, bf16[528,512]{1,0:T(8,128)(2,1)}, u32[]{:S(2)}) %copy-start.10) | copy-done | bytes 540696
  85.5 1.0 %copy-done.12 = bf16[528,512]{1,0:T(8,128)(2,1)S(1)} copy-done((bf16[528,512]{1,0:T(8,128)(2,1)S(1)}, bf16[528,512]{1,0:T(8,128)(2,1)}, u32[]{:S(2)}) %copy-start.12) | copy-done | bytes 540696
  86.5 1.0 %copy-done.14 = bf16[512,512]{1,0:T(8,128)(2,1)S(1)} copy-done((bf16[512,512]{1,0:T(8,128)(2,1)S(1)}, bf16[512,512]{1,0:T(8,128)(2,1)}, u32[]{:S(2)}) %copy-start.14) | copy-done | bytes 524312
  87.6 1.0 %copy-done.16 = bf16[512,512]{1,0:T(8,128)(2,1)S(1)} copy-done((bf16[512,512]{1,0:T(8,128)(2,1)S(1)}, bf16[512,512]{1,0:T(8,128)(2,1)}, u32[]{:S(2)}) %copy-start.16) | copy-done | bytes 524312
  88.6 5.2 %shard_map.119 = (f32[2,512,512]{2,1,0:T(8,128)}, f32[2,512]{1,0:T(2,128)}, f32[2,512]{1,0:T(2,128)}) custom-call(bf16[2,512,1280]{2,1,0:T(8,128)(2,1)S(1)} %copy-done, bf16[512,512]{1,0:T(8,128)(2,1)S(1)} %copy-done.16, bf16[512,512]{1,0:T(8,128)(2,1)S(1)} %copy-done.2, bf16[512,512]{1,0:T(8,128)(2,1)S(1)} %copy-done.14, bf16[528,512]{1,0:T(8,128)(2,1)S(1)} %copy-done.12, ...), custom_call_target="tpu_custom_call" | custom-call | flops 4600000000 | tf_op jit(solution)/shard_map/pallas_call | solution.py:500
  (8 shorter events, 0.0 us)
Async XLA Ops:
  0.6 18.0 %collective-permute-start.1 = (bf16[512,512]{1,0:T(8,128)(2,1)}, bf16[512,512]{1,0:T(8,128)(2,1)S(1)}, u32[]{:S(2)}, u32[]{:S(2)}) collective-permute-start(bf16[512,512]{1,0:T(8,128)(2,1)} %uown.1), channel_id=1, source_target_pairs={{1,0},{2,1},{3,2},{4,3},{5,4},{6,5},{7,6},{8,7},{9,8},{10,9},{11,1... | collective-permute-start | bytes 1572872 | tf_op jit(solution)/shard_map/ppermute | solution.py:389
  6.1 12.5 %collective-permute-start = (bf16[512,512]{1,0:T(8,128)(2,1)}, bf16[512,512]{1,0:T(8,128)(2,1)S(1)}, u32[]{:S(2)}, u32[]{:S(2)}) collective-permute-start(bf16[512,512]{1,0:T(8,128)(2,1)} %uown.1), channel_id=1, source_target_pairs={{0,1},{1,2},{2,3},{3,4},{4,5},{5,6},{6,7},{7,8},{8,9},{9,10},{10,1... | collective-permute-start | bytes 1572872 | tf_op jit(solution)/shard_map/ppermute | solution.py:389
  8.2 3.5 %collective-permute-start.2 = (bf16[8,32,128]{2,1,0:T(8,128)(2,1)}, bf16[8,32,128]{2,1,0:T(8,128)(2,1)S(1)}, u32[]{:S(2)}, u32[]{:S(2)}) collective-permute-start(bf16[8,32,128]{2,1,0:T(8,128)(2,1)} %get-tuple-element.12.refs_0_), channel_id=1, source_target_pairs={{0,1},{1,0},{2,3},{3,2},{4,5},{5,4},{6,7},{7,6},{8,9},{9,8},{10,11... | collective-permute-start | bytes 196616 | tf_op jit(solution)/shard_map/ppermute | solution.py:421
  8.2 3.5 %copy-start.3 = (bf16[8,32,128]{2,1,0:T(8,128)(2,1)S(1)}, bf16[8,32,128]{2,1,0:T(8,128)(2,1)}, u32[]{:S(2)}) copy-start(bf16[8,32,128]{2,1,0:T(8,128)(2,1)} %get-tuple-element.12.refs_0_) | copy-start | bytes 196612
  8.2 3.5 %copy-start.4 = (bf16[208,128]{1,0:T(8,128)(2,1)S(1)}, bf16[208,128]{1,0:T(8,128)(2,1)}, u32[]{:S(2)}) copy-start(bf16[208,128]{1,0:T(8,128)(2,1)} %get-tuple-element.11.packed) | copy-start | bytes 159748
  12.5 21.5 %all-to-all-start = ((bf16[8,272,128]{2,1,0:T(8,128)(2,1)}), bf16[8,272,128]{2,1,0:T(8,128)(2,1)S(1)}, u32[]{:S(2)}, u32[]{:S(2)}) async-start(bf16[8,272,128]{2,1,0:T(8,128)(2,1)} %shard_map.115), calls=%async_computation | async-start | bytes 1114112 | tf_op jit(solution)/shard_map/all_to_all | solution.py:415
  18.6 28.1 %copy-start.1 = (bf16[512,512]{1,0:T(8,128)(2,1)S(1)}, bf16[512,512]{1,0:T(8,128)(2,1)}, u32[]{:S(2)}) copy-start(bf16[512,512]{1,0:T(8,128)(2,1)} %uown.1) | copy-start | bytes 1572868
  18.6 28.1 %copy-start.5 = (bf16[2,256,32]{1,2,0:T(8,128)(2,1)S(1)}, bf16[2,256,32]{1,2,0:T(8,128)(2,1)}, u32[]{:S(2)}) copy-start(bf16[2,256,32]{1,2,0:T(8,128)(2,1)} %param.16) | copy-start | bytes 98308
  18.6 28.1 %copy-start.17 = (bf16[2,256,32]{1,2,0:T(8,128)(2,1)S(1)}, bf16[2,256,32]{1,2,0:T(8,128)(2,1)}, u32[]{:S(2)}) copy-start(bf16[2,256,32]{1,2,0:T(8,128)(2,1)} %param.15) | copy-start | bytes 98308
  18.7 0.8 copy-start.13
  19.5 0.8 copy-start.15
  34.1 0.7 copy-start.6
  46.7 1.6 %copy-start.19 = (f32[2,512,512]{2,1,0:T(8,128)S(1)}, f32[2,512,512]{2,1,0:T(8,128)}, u32[]{:S(2)}) copy-start(f32[2,512,512]{2,1,0:T(8,128)} %get-tuple-element.10.near) | copy-start | bytes 6291460
  50.4 17.2 %collective-permute-start.4 = (bf16[528,512]{1,0:T(8,128)(2,1)S(1)}, bf16[528,512]{1,0:T(8,128)(2,1)S(1)}, u32[]{:S(2)}, u32[]{:S(2)}) collective-permute-start(bf16[528,512]{1,0:T(8,128)(2,1)S(1)} %get-tuple-element.14.first), channel_id=1, source_target_pairs={{1,0},{2,1},{3,2},{4,3},{5,4},{6,5},{7,6},{8,7},{9,8},{10,9},{11,1... | collective-permute-start | bytes 1622024 | tf_op jit(solution)/shard_map/ppermute | solution.py:389
  50.6 16.9 %collective-permute-start.3 = (bf16[528,512]{1,0:T(8,128)(2,1)S(1)}, bf16[528,512]{1,0:T(8,128)(2,1)S(1)}, u32[]{:S(2)}, u32[]{:S(2)}) collective-permute-start(bf16[528,512]{1,0:T(8,128)(2,1)S(1)} %get-tuple-element.14.first), channel_id=1, source_target_pairs={{0,1},{1,2},{2,3},{3,4},{4,5},{5,6},{6,7},{7,8},{8,9},{9,10},{10,1... | collective-permute-start | bytes 1622024 | tf_op jit(solution)/shard_map/ppermute | solution.py:389
  50.9 0.8 copy-start.7
  65.6 1.9 %collective-permute-start.7 = (bf16[8,80,128]{2,1,0:T(8,128)(2,1)S(1)}, bf16[8,80,128]{2,1,0:T(8,128)(2,1)S(1)}, u32[]{:S(2)}, u32[]{:S(2)}) collective-permute-start(bf16[8,80,128]{2,1,0:T(8,128)(2,1)S(1)} %all_to_all.21.refs_0_), channel_id=1, source_target_pairs={{0,1},{1,0},{2,3},{3,2},{4,5},{5,4},{6,7},{7,6},{8,9},{9,8},{10,11... | collective-permute-start | bytes 491528 | tf_op jit(solution)/shard_map/ppermute | solution.py:421
  65.6 16.7 %copy-start = (bf16[2,512,1280]{2,1,0:T(8,128)(2,1)S(1)}, bf16[2,512,1280]{2,1,0:T(8,128)(2,1)}, u32[]{:S(2)}) copy-start(bf16[2,512,1280]{2,1,0:T(8,128)(2,1)} %shard_map.112.w) | copy-start | bytes 7864324
  65.6 16.7 %copy-start.18 = (f32[2,512]{1,0:T(2,128)S(1)}, f32[2,512]{1,0:T(2,128)}, u32[]{:S(2)}) copy-start(f32[2,512]{1,0:T(2,128)} %diag.3) | copy-start | bytes 12292
  65.6 9.2 %collective-permute-start.6 = (bf16[512,512]{1,0:T(8,128)(2,1)}, bf16[512,512]{1,0:T(8,128)(2,1)}, u32[]{:S(2)}, u32[]{:S(2)}) collective-permute-start(bf16[512,512]{1,0:T(8,128)(2,1)} %get-tuple-element.15.second), channel_id=1, source_target_pairs={{1,0},{2,1},{3,2},{4,3},{5,4},{6,5},{7,6},{8,7},{9,8},{10,9},{11,1... | collective-permute-start | bytes 1572872 | tf_op jit(solution)/shard_map/ppermute | solution.py:389
  67.5 11.7 %collective-permute-start.5 = (bf16[512,512]{1,0:T(8,128)(2,1)}, bf16[512,512]{1,0:T(8,128)(2,1)}, u32[]{:S(2)}, u32[]{:S(2)}) collective-permute-start(bf16[512,512]{1,0:T(8,128)(2,1)} %get-tuple-element.15.second), channel_id=1, source_target_pairs={{0,1},{1,2},{2,3},{3,4},{4,5},{5,6},{6,7},{7,8},{8,9},{9,10},{10,1... | collective-permute-start | bytes 1572872 | tf_op jit(solution)/shard_map/ppermute | solution.py:389
  69.8 0.8 copy-start.9
  70.6 0.8 copy-start.11
  71.4 10.9 %all-to-all-start.3 = ((bf16[8,80,128]{2,1,0:T(8,128)(2,1)}), bf16[8,80,128]{2,1,0:T(8,128)(2,1)S(1)}, u32[]{:S(2)}, u32[]{:S(2)}) async-start(bf16[8,80,128]{2,1,0:T(8,128)(2,1)} %shard_map.118), calls=%async_computation.3 | async-start | bytes 327680 | tf_op jit(solution)/shard_map/all_to_all | solution.py:415
  82.3 1.0 %copy-start.2 = (bf16[512,512]{1,0:T(8,128)(2,1)S(1)}, bf16[512,512]{1,0:T(8,128)(2,1)}, u32[]{:S(2)}) copy-start(bf16[512,512]{1,0:T(8,128)(2,1)} %uown.1) | copy-start | bytes 1572868
  83.4 1.0 %copy-start.8 = (bf16[528,512]{1,0:T(8,128)(2,1)S(1)}, bf16[528,512]{1,0:T(8,128)(2,1)}, u32[]{:S(2)}) copy-start(bf16[528,512]{1,0:T(8,128)(2,1)} %copy-done.7) | copy-start | bytes 1622020
  84.4 1.0 %copy-start.10 = (bf16[528,512]{1,0:T(8,128)(2,1)S(1)}, bf16[528,512]{1,0:T(8,128)(2,1)}, u32[]{:S(2)}) copy-start(bf16[528,512]{1,0:T(8,128)(2,1)} %copy-done.9) | copy-start | bytes 1622020
  85.5 1.0 %copy-start.12 = (bf16[528,512]{1,0:T(8,128)(2,1)S(1)}, bf16[528,512]{1,0:T(8,128)(2,1)}, u32[]{:S(2)}) copy-start(bf16[528,512]{1,0:T(8,128)(2,1)} %copy-done.11) | copy-start | bytes 1622020
  86.5 1.0 %copy-start.14 = (bf16[512,512]{1,0:T(8,128)(2,1)S(1)}, bf16[512,512]{1,0:T(8,128)(2,1)}, u32[]{:S(2)}) copy-start(bf16[512,512]{1,0:T(8,128)(2,1)} %copy-done.13) | copy-start | bytes 1572868
  87.6 1.0 %copy-start.16 = (bf16[512,512]{1,0:T(8,128)(2,1)S(1)}, bf16[512,512]{1,0:T(8,128)(2,1)}, u32[]{:S(2)}) copy-start(bf16[512,512]{1,0:T(8,128)(2,1)} %copy-done.15) | copy-start | bytes 1572868

commit v15 on v14

--- a/solution.py
+++ b/solution.py
@@ -22,7 +22,7 @@
 ANY = pl.BlockSpec(memory_space=pl.ANY)
 
 
-def call(body, out_shape, in_specs, scratch=(), micros=0.0, megabytes=20, out_specs=None):
+def call(body, out_shape, in_specs, scratch=(), micros=0.0, megabytes=20, out_specs=None, alias=None):
     many = isinstance(out_shape, (list, tuple))
     if out_specs is None:
         out_specs = [VMEM] * len(out_shape) if many else VMEM
@@ -31,6 +31,7 @@
         out_shape=out_shape,
         in_specs=in_specs,
         out_specs=out_specs,
+        input_output_aliases=alias or {},
         scratch_shapes=list(scratch),
         compiler_params=pltpu.CompilerParams(vmem_limit_bytes=megabytes * 1024 * 1024),
         cost_estimate=pl.CostEstimate(
@@ -70,7 +71,7 @@
     return x[:, pair * LANES:(pair + 1) * LANES]
 
 
-def order_tiles(all_blocks, cols, count, row0, tiles, out):
+def order_tiles(all_blocks, cols, count, row0, tiles, after, out):
     ops, blocks, near, size, _ = tiles.shape
     for b in range(blocks):
         for k in range(near):
@@ -315,35 +316,56 @@
         out[s, body:body + STATS, :] = rows
 
 
-def final_kernel(
+def apply_second(o, factor, changes, u3, v3, w, diag, left, cmsg, images, ext, coef, out, sems):
+    blocks, rank, size = left.shape
+    rows, columns = u3[1].shape
+    ops = w.shape[1] // size
+    take_coefs(cmsg, coef, ops * rank)
+    for at, (u, v) in enumerate(zip(u3, v3)):
+        value = v[0:rows, :].astype(F32) * factor + u[...].astype(F32) * changes[at]
+        ext[at] = value.astype(BF16)
+    copies = []
+    for b in range(blocks):
+        parts = [ext.at[at] for at in range(3)]
+        product = near_product(w.at[b, o * size:(o + 1) * size], parts, b, blocks, size)
+        far = dot(left[b], coef[b, o * rank:(o + 1) * rank, :], ((0,), (0,)))
+        here = slice(b * size, (b + 1) * size)
+        out[here, :] = (
+            product
+            + diagonal_of(diag, o, b, size, columns) * ext[1, here, :].astype(F32)
+            + far.astype(BF16).astype(F32)
+        )
+        copies.append(pltpu.make_async_copy(out.at[here], images.at[o, here], sems.at[b]))
+        copies[-1].start()
+    for copy in copies:
+        copy.wait()
+
+
+def final_first(
     w,
     ulow,
     uown,
     uhigh,
-    low0,
-    first,
-    high0,
-    low1,
-    second,
-    high1,
+    vlow,
+    vown,
+    vhigh,
     diag,
     left,
     cmsg,
     images,
     heights,
     norms,
+    aux,
     ext,
     coef,
+    out,
     stat,
-    out,
-    outs,
+    sems,
 ):
-    copies = []
-    ops = images.shape[0]
     blocks, rank, size = left.shape
     rows, columns = uown.shape
+    ops = w.shape[1] // size
     body = ops * rank
-    take_coefs(cmsg, coef, body)
     for pair in range(SLICES // 2):
         stat[:, pair * LANES:(pair + 1) * LANES] = halves(
             cmsg[2 * pair, body:body + STATS, :].astype(F32),
@@ -351,35 +373,48 @@
         )[0]
     st = stat[...]
     reverse = row3(st, 2 * ops)
+    scales = []
     for o in range(ops):
         height = row3(st, o)
         norm = row3(st, ops + o)
         heights[o:o + 1, :] = height
         norms[o:o + 1, :] = norm
         factor = reverse / norm
-        triples = (ulow, low0, low1), (uown, first, second), (uhigh, high0, high1)
-        for at, (u, v0, v1) in enumerate(triples):
-            shift = row3(v0[rows:, :].astype(F32), o)
-            change = (shift - height) * factor
-            v = (v0, v1)[o][0:rows, :].astype(F32)
-            value = v * factor + u[...].astype(F32) * change
-            ext[o, at] = value.astype(BF16)
-        for b in range(blocks):
-            parts = [ext.at[o, at] for at in range(3)]
-            product = near_product(w.at[b, o * size:(o + 1) * size], parts, b, blocks, size)
-            far = dot(left[b], coef[b, o * rank:(o + 1) * rank, :], ((0,), (0,)))
-            mine = ext[o, 1, b * size:(b + 1) * size, :].astype(F32)
-            here = slice(b * size, (b + 1) * size)
-            out[o, here, :] = (
-                product
-                + diagonal_of(diag, o, b, size, columns) * mine
-                + far.astype(BF16).astype(F32)
-            )
-            copy = pltpu.make_async_copy(out.at[o, here], images.at[o, here], outs.at[o, b])
-            copy.start()
-            copies.append(copy)
-    for copy in copies:
-        copy.wait()
+        changes = [
+            (row3(v[rows:, :].astype(F32), o) - height) * factor for v in (vlow, vown, vhigh)
+        ]
+        scales.append((factor, changes))
+    factor, changes = scales[1]
+    aux[0:1, :] = factor
+    for at in range(3):
+        aux[1 + at:2 + at, :] = changes[at]
+    factor, changes = scales[0]
+    u3, v3 = (ulow, uown, uhigh), (vlow, vown, vhigh)
+    apply_second(0, factor, changes, u3, v3, w, diag, left, cmsg, images, ext, coef, out, sems)
+
+
+def final_second(
+    begun,
+    w,
+    ulow,
+    uown,
+    uhigh,
+    vlow,
+    vown,
+    vhigh,
+    diag,
+    left,
+    cmsg,
+    aux,
+    images,
+    ext,
+    coef,
+    out,
+    sems,
+):
+    factor, changes = aux[0:1, :], [aux[1 + at:2 + at, :] for at in range(3)]
+    u3, v3 = (ulow, uown, uhigh), (vlow, vown, vhigh)
+    apply_second(1, factor, changes, u3, v3, w, diag, left, cmsg, images, ext, coef, out, sems)
 
 
 def ring(block):
@@ -436,21 +471,20 @@
         megabytes=60,
     )(far_cols, sources, right, couplings)
     z1 = across(z1)
-    held = call(
+    mine = call(
         share_kernel,
         sds((SLICES, shared + STATS + count * rank, LANES), BF16),
         [VMEM] * (1 + count),
     )(packed, *z1)
-    held = exchange(held)
+    held = exchange(mine)
     cols = held[:, shared, :blocks * far].astype(jnp.int32).reshape(-1)
 
     w = call(
         functools.partial(order_tiles, all_blocks),
         sds((blocks, ops * size, near * size), BF16),
-        [SMEM, SMEM, SMEM, VMEM],
-        micros=0.0,
+        [SMEM, SMEM, SMEM, VMEM, ANY],
         megabytes=60,
-    )(near_cols, near_count, row0, near_tiles)
+    )(near_cols, near_count, row0, near_tiles, mine)
     image, token = call(
         near_kernel,
         [sds((ops, rows, columns), F32), sds((8, LANES), F32)],
@@ -497,20 +531,29 @@
     )(cols, group, low0, high0, held, *msgs)
     c2 = exchange(c2)
 
-    images, heights, norms = call(
-        final_kernel,
-        [sds((ops, rows, columns), F32), sds((ops, columns), F32), sds((ops, columns), F32)],
-        [VMEM] * 13,
-        [
-            pltpu.VMEM((ops, 3, rows, columns), BF16),
-            pltpu.VMEM((blocks, body, columns), BF16),
-            pltpu.VMEM((STATS, columns), F32),
-            pltpu.VMEM((ops, rows, columns), F32),
-            pltpu.SemaphoreType.DMA((ops, blocks)),
-        ],
+    outs = sds((ops, rows, columns), F32)
+    scratch = [
+        pltpu.VMEM((3, rows, columns), BF16),
+        pltpu.VMEM((blocks, body, columns), BF16),
+        pltpu.VMEM((rows, columns), F32),
+    ]
+    images, heights, norms, aux = call(
+        final_first,
+        [outs, sds((ops, columns), F32), sds((ops, columns), F32), sds((8, columns), F32)],
+        [VMEM] * 10,
+        scratch + [pltpu.VMEM((STATS, columns), F32), pltpu.SemaphoreType.DMA((blocks,))],
+        micros=10.0,
+        out_specs=[ANY, VMEM, VMEM, VMEM],
+    )(w, low, sources, high, low0, first, high0, self_terms, left, c2)
+    images = call(
+        final_second,
+        outs,
+        [ANY] + [VMEM] * 11,
+        scratch + [pltpu.SemaphoreType.DMA((blocks,))],
         micros=4.0,
-        out_specs=[ANY, VMEM, VMEM],
-    )(w, low, sources, high, low0, first, high0, low1, second, high1, self_terms, left, c2)
+        out_specs=ANY,
+        alias={0: 0},
+    )(images, w, low, sources, high, low1, second, high1, self_terms, left, c2, aux)
     return images, heights, norms
 
 

time: 95.4 us -> 94.8 us (level)
  waiting for transfers between devices: 16.3 us -> 12.5 us
  starting transfers between devices: 17.4 us -> 19.3 us
  local copies, waits for them, and re-layouts: 12.6 us -> 14.3 us
    ppermute x3, waiting for transfers between devices: 4.42 us -> 0.01 us  [ring(): lax.ppermute(block, 'store', forward)]
    ppermute x2, waiting for transfers between devices: 0.01 us -> 2.85 us  [across(): parts.append(lax.ppermute(x, 'store', pairs))]
    ppermute x3, starting transfers between devices: 7.63 us -> 9.94 us  [ring(): lax.ppermute(block, 'store', backward)]
    all_to_all x2, waiting for transfers between devices: 11.8 us -> 9.64 us  [exchange(): lax.all_to_all(x, 'store', 0, 0, axis_index_groups=groups, tiled=True)]
    unnamed x40 -> x44, local copies, waits for them, and re-layouts: 12.6 us -> 14.2 us
    pallas_call x1 -> x2, Pallas kernels: 5.15 us -> 6 us  [the longest x1 3.16 us: shards(): call(final_second, outs, [ANY] + [VMEM] * 11, scratch + [pltpu.SemaphoreT...]
  transfers between devices with their start and end apart: 10 -> 10, of which waited for: 3 -> 4; matrix products, arithmetic and copies ran while one was open for 0% -> 0% of each run, Pallas kernels for 15% -> 15%
where the time goes in v15:
time: 94.8 us; the launch traced here: 93.8 us
  blocking collectives  24.7 us (26%)
  Pallas kernels  22.2 us (23%)
  starting transfers between devices  19.3 us (20%)
  local copies, waits for them, and re-layouts  14.3 us (15%)
  waiting for transfers between devices  12.5 us (13%)
    all_to_all x2, blocking collectives, exchange(): lax.all_to_all(x, 'store', 0, 0, axis_index_groups=groups, tiled=True)  24.7 us
    unnamed x44, local copies, waits for them, and re-layouts  14.2 us
    ppermute x3, starting transfers between devices, ring(): lax.ppermute(block, 'store', backward)  9.94 us
    all_to_all x2, waiting for transfers between devices, exchange(): lax.all_to_all(x, 'store', 0, 0, axis_index_groups=groups, tiled=True)  9.64 us
    all_to_all x2, starting transfers between devices, exchange(): lax.all_to_all(x, 'store', 0, 0, axis_index_groups=groups, tiled=True)  9.14 us
    pallas_call x1, Pallas kernels, shards(): call(near_kernel, [sds((ops, rows, columns), F32), sds((8, LANES), F32)],...  4.99 us
    pallas_call x1, Pallas kernels, shards(): call(functools.partial(order_tiles, all_blocks), sds((blocks, ops * size,...  3.42 us
    pallas_call x1, Pallas kernels, shards(): call(final_second, outs, [ANY] + [VMEM] * 11, scratch + [pltpu.SemaphoreT...  3.16 us
  transfers between devices with their start and end apart: 10, of which 4 were waited for; matrix products, arithmetic and copies ran while one was open for 0% of the time, Pallas kernels for 15%

profile of v15, /device:TPU:0, one launch (start us, length us, event | category | flops | bytes accessed | tf_op | source)
XLA Modules:
  0.0 93.8 jit_solution(17138474488729800697)
XLA Ops:
  0.6 5.5 %collective-permute-start.2 = (bf16[512,512]{1,0:T(8,128)(2,1)}, bf16[512,512]{1,0:T(8,128)(2,1)S(1)}, u32[]{:S(2)}, u32[]{:S(2)}) collective-permute-start(bf16[512,512]{1,0:T(8,128)(2,1)} %uown.3), channel_id=1, source_target_pairs={{1,0},{2,1},{3,2},{4,3},{5,4},{6,5},{7,6},{8,7},{9,8},{10,9},{11,1... | collective-permute-start | bytes 1572872 | tf_op jit(solution)/shard_map/ppermute | solution.py:424
  6.1 0.0 collective-permute-start.1
  6.1 2.0 %shard_map.112 = (bf16[8,32,128]{2,1,0:T(8,128)(2,1)}, bf16[208,128]{1,0:T(8,128)(2,1)}) custom-call(s32[2,6]{1,0:T(2,128)} %far_cols.1, bf16[512,512]{1,0:T(8,128)(2,1)} %uown.3, bf16[2,32,256]{2,1,0:T(8,128)(2,1)} %bitcast.4, bf16[2,2,6,32,32]{4,3,2,1,0:T(8,128)(2,1)} %coup.1), custom_call_target="tpu_custom_call" | custom-call | tf_op jit(solution)/shard_map/pallas_call | solution.py:467
  8.2 0.0 collective-permute-start
  8.2 1.5 %collective-permute-done.refs_1_ = bf16[8,32,128]{2,1,0:T(8,128)(2,1)S(1)} collective-permute-done((bf16[8,32,128]{2,1,0:T(8,128)(2,1)}, bf16[8,32,128]{2,1,0:T(8,128)(2,1)S(1)}, u32[]{:S(2)}, u32[]{:S(2)}) %collective-permute-start) | collective-permute-done | bytes 65568 | tf_op jit(solution)/shard_map/ppermute | solution.py:456
  9.6 0.0 copy-start.3
  9.6 0.8 copy-done.3
  10.5 0.0 copy-start.4
  10.5 0.8 copy-done.4
  11.3 0.9 shard_map.113.after
  12.1 5.8 %all-to-all-start = ((bf16[8,272,128]{2,1,0:T(8,128)(2,1)}), bf16[8,272,128]{2,1,0:T(8,128)(2,1)S(1)}, u32[]{:S(2)}, u32[]{:S(2)}) async-start(bf16[8,272,128]{2,1,0:T(8,128)(2,1)} %shard_map.113.after), calls=%async_computation | async-start | bytes 1114112 | tf_op jit(solution)/shard_map/all_to_all | solution.py:450
  17.9 3.4 %shard_map.114.w = bf16[2,512,1280]{2,1,0:T(8,128)(2,1)} custom-call(s32[2,5]{1,0:T(2,128)} %cols.1, s32[2]{0:T(128)} %count.1, s32[1]{0:T(128)} %bitcast.row0, bf16[2,2,5,256,256]{4,3,2,1,0:T(8,128)(2,1)} %tiles.1, bf16[8,272,128]{2,1,0:T(8,128)(2,1)} %shard_map.113.after), custom_call_target="tpu_custom_call" | custom-call | tf_op jit(solution)/shard_map/pallas_call | solution.py:482
  21.3 0.0 copy-start.1
  21.3 0.0 copy-start.5
  21.3 0.0 copy-start.19
  21.3 0.0 collective-permute-done.2.high.uhigh
  21.3 0.0 copy-start.13
  21.3 0.0 collective-permute-done.1.low.ulow
  21.4 0.8 copy-done.13
  22.1 0.0 copy-start.15
  22.1 0.8 copy-done.15
  23.0 5.0 %shard_map.115 = (f32[2,512,512]{2,1,0:T(8,128)}, f32[8,128]{1,0:T(8,128)}) custom-call(bf16[2,512,1280]{2,1,0:T(8,128)(2,1)} %shard_map.114.w, bf16[512,512]{1,0:T(8,128)(2,1)} %copy-done.15, bf16[512,512]{1,0:T(8,128)(2,1)} %uown.3, bf16[512,512]{1,0:T(8,128)(2,1)} %copy-done.13, f32[2,512]{1,0:T(2,128)} %diag.5), custom_call_target="tpu_custom_call" | custom-call | flops 11500000256 | tf_op jit(solution)/shard_map/pallas_call | solution.py:488
  27.9 5.7 %all-to-all-done.held = bf16[8,272,128]{2,1,0:T(8,128)(2,1)S(1)} async-done(((bf16[8,272,128]{2,1,0:T(8,128)(2,1)}), bf16[8,272,128]{2,1,0:T(8,128)(2,1)S(1)}, u32[]{:S(2)}, u32[]{:S(2)}) %all-to-all-start) | async-done | bytes 557088 | tf_op jit(solution)/shard_map/all_to_all | solution.py:450
  33.6 0.1 reshape.18.cols
  33.7 0.0 copy-start.6
  33.7 0.7 copy-done.6
  34.4 1.1 %shard_map.116 = bf16[8,64,128]{2,1,0:T(8,128)(2,1)S(1)} custom-call(s32[96]{0:T(128)S(1)} %reshape.18.cols, s32[1]{0:T(128)} %bitcast.3.group, f32[8,128]{1,0:T(8,128)S(1)} %copy-done.6, bf16[8,272,128]{2,1,0:T(8,128)(2,1)S(1)} %all-to-all-done.held), custom_call_target="tpu_custom_call" | custom-call | tf_op jit(solution)/shard_map/pallas_call | solution.py:496
  35.5 10.8 %all_to_all.20.cmsg = bf16[8,64,128]{2,1,0:T(8,128)(2,1)S(1)} all-to-all(bf16[8,64,128]{2,1,0:T(8,128)(2,1)S(1)} %shard_map.116), channel_id=1, replica_groups={{0,2,4,6,8,10,12,14},{1,3,5,7,9,11,13,15},{16,18,20,22,24,26,28,30},{17..., dimensions={0} | all-to-all | bytes 262144 | tf_op jit(solution)/shard_map/all_to_all | solution.py:450
  46.3 0.0 copy-done.1
  46.3 0.0 copy-done.5
  46.3 0.0 copy-done.19
  46.3 0.0 copy-start.21
  46.3 1.6 %copy-done.21 = f32[2,512,512]{2,1,0:T(8,128)S(1)} copy-done((f32[2,512,512]{2,1,0:T(8,128)S(1)}, f32[2,512,512]{2,1,0:T(8,128)}, u32[]{:S(2)}) %copy-start.21) | copy-done | bytes 2097176
  47.9 1.5 %shard_map.117 = (bf16[528,512]{1,0:T(8,128)(2,1)S(1)}, bf16[512,512]{1,0:T(8,128)(2,1)S(1)}, bf16[8,80,128]{2,1,0:T(8,128)(2,1)S(1)}) custom-call(bf16[512,512]{1,0:T(8,128)(2,1)S(1)} %copy-done.1, f32[2,512,512]{2,1,0:T(8,128)S(1)} %copy-done.21, bf16[2,32,256]{2,1,0:T(8,128)(2,1)S(1)} %bitcast.6, bf16[2,32,256]{2,1,0:T(8,128)(2,1)S(1)} %bitcast.5, ...), custom_call_target="tpu_custom_call" | custom-call | flops 2300000000 | tf_op jit(solution)/shard_map/pallas_call | solution.py:504
  49.4 0.0 copy-start.17
  49.4 0.3 collective-permute-start.4
  49.8 0.2 collective-permute-start.3
  50.0 0.8 copy-done.7
  50.8 0.0 copy-done.17
  50.8 13.9 %all_to_all.21.refs_0_ = bf16[8,80,128]{2,1,0:T(8,128)(2,1)S(1)} all-to-all(bf16[8,80,128]{2,1,0:T(8,128)(2,1)S(1)} %get-tuple-element.19), channel_id=1, replica_groups={{0,2,4,6,8,10,12,14},{1,3,5,7,9,11,13,15},{16,18,20,22,24,26,28,30},{17..., dimensions={0} | all-to-all | bytes 327680 | tf_op jit(solution)/shard_map/all_to_all | solution.py:450
  64.7 0.0 collective-permute-start.5
  64.7 1.4 %collective-permute-done.5.refs_1_ = bf16[8,80,128]{2,1,0:T(8,128)(2,1)S(1)} collective-permute-done((bf16[8,80,128]{2,1,0:T(8,128)(2,1)S(1)}, bf16[8,80,128]{2,1,0:T(8,128)(2,1)S(1)}, u32[]{:S(2)}, u32[]{:S(2)}) %collective-permute-start.5) | collective-permute-done | bytes 163872 | tf_op jit(solution)/shard_map/ppermute | solution.py:456
  66.1 0.0 collective-permute-done.4.after_high.vhigh
  66.1 0.0 collective-permute-done.3.after_low.vlow
  66.1 2.3 %shard_map.118 = bf16[8,80,128]{2,1,0:T(8,128)(2,1)} custom-call(s32[96]{0:T(128)S(1)} %reshape.18.cols, s32[1]{0:T(128)} %bitcast.3.group, bf16[528,512]{1,0:T(8,128)(2,1)S(1)} %collective-permute-done.3.after_low.vlow, bf16[528,512]{1,0:T(8,128)(2,1)S(1)} %collective-permute-done.4.after_high.vhigh, bf16[8,272,128]{2,1,0:T(8,128)(2,1)S(1)} %all-to-all-done.held, ...), custom_call_target="tpu_custom_call" | custom-call | flops 34500001792 | tf_op jit(solution)/shard_map/pallas_call | solution.py:522
  68.4 0.8 copy-done.9
  69.2 0.8 copy-done.11
  70.0 3.4 %all-to-all-start.3 = ((bf16[8,80,128]{2,1,0:T(8,128)(2,1)}), bf16[8,80,128]{2,1,0:T(8,128)(2,1)S(1)}, u32[]{:S(2)}, u32[]{:S(2)}) async-start(bf16[8,80,128]{2,1,0:T(8,128)(2,1)} %shard_map.118), calls=%async_computation.3 | async-start | bytes 327680 | tf_op jit(solution)/shard_map/all_to_all | solution.py:450
  73.4 4.1 %collective-permute-start.7 = (bf16[512,512]{1,0:T(8,128)(2,1)}, bf16[512,512]{1,0:T(8,128)(2,1)S(1)}, u32[]{:S(2)}, u32[]{:S(2)}) collective-permute-start(bf16[512,512]{1,0:T(8,128)(2,1)} %copy-done.17), channel_id=1, source_target_pairs={{1,0},{2,1},{3,2},{4,3},{5,4},{6,5},{7,6},{8,7},{9,8},{10,9},{11,1... | collective-permute-start | bytes 1572872 | tf_op jit(solution)/shard_map/ppermute | solution.py:424
  77.5 0.0 collective-permute-start.6
  77.5 4.0 %all-to-all-done.3.cmsg = bf16[8,80,128]{2,1,0:T(8,128)(2,1)S(1)} async-done(((bf16[8,80,128]{2,1,0:T(8,128)(2,1)}), bf16[8,80,128]{2,1,0:T(8,128)(2,1)S(1)}, u32[]{:S(2)}, u32[]{:S(2)}) %all-to-all-start.3) | async-done | bytes 163872 | tf_op jit(solution)/shard_map/all_to_all | solution.py:450
  81.5 0.0 copy-done
  81.5 0.0 copy-done.20
  81.5 1.0 %copy-done.2 = bf16[512,512]{1,0:T(8,128)(2,1)S(1)} copy-done((bf16[512,512]{1,0:T(8,128)(2,1)S(1)}, bf16[512,512]{1,0:T(8,128)(2,1)}, u32[]{:S(2)}) %copy-start.2) | copy-done | bytes 524312
  82.6 1.0 %copy-done.8 = bf16[528,512]{1,0:T(8,128)(2,1)S(1)} copy-done((bf16[528,512]{1,0:T(8,128)(2,1)S(1)}, bf16[528,512]{1,0:T(8,128)(2,1)}, u32[]{:S(2)}) %copy-start.8) | copy-done | bytes 540696
  83.6 1.0 %copy-done.10 = bf16[528,512]{1,0:T(8,128)(2,1)S(1)} copy-done((bf16[528,512]{1,0:T(8,128)(2,1)S(1)}, bf16[528,512]{1,0:T(8,128)(2,1)}, u32[]{:S(2)}) %copy-start.10) | copy-done | bytes 540696
  84.7 1.0 %copy-done.12 = bf16[528,512]{1,0:T(8,128)(2,1)S(1)} copy-done((bf16[528,512]{1,0:T(8,128)(2,1)S(1)}, bf16[528,512]{1,0:T(8,128)(2,1)}, u32[]{:S(2)}) %copy-start.12) | copy-done | bytes 540696
  85.7 1.0 %copy-done.14 = bf16[512,512]{1,0:T(8,128)(2,1)S(1)} copy-done((bf16[512,512]{1,0:T(8,128)(2,1)S(1)}, bf16[512,512]{1,0:T(8,128)(2,1)}, u32[]{:S(2)}) %copy-start.14) | copy-done | bytes 524312
  86.8 1.0 %copy-done.16 = bf16[512,512]{1,0:T(8,128)(2,1)S(1)} copy-done((bf16[512,512]{1,0:T(8,128)(2,1)S(1)}, bf16[512,512]{1,0:T(8,128)(2,1)}, u32[]{:S(2)}) %copy-start.16) | copy-done | bytes 524312
  87.8 2.8 %shard_map.119 = (f32[2,512,512]{2,1,0:T(8,128)}, f32[2,512]{1,0:T(2,128)}, f32[2,512]{1,0:T(2,128)}, f32[8,512]{1,0:T(8,128)S(1)}) custom-call(bf16[2,512,1280]{2,1,0:T(8,128)(2,1)S(1)} %copy-done, bf16[512,512]{1,0:T(8,128)(2,1)S(1)} %copy-done.16, bf16[512,512]{1,0:T(8,128)(2,1)S(1)} %copy-done.2, bf16[512,512]{1,0:T(8,128)(2,1)S(1)} %copy-done.14, ...), custom_call_target="tpu_custom_call" | custom-call | flops 11500000256 | tf_op jit(solution)/shard_map/pallas_call | solution.py:540
  90.6 0.0 collective-permute-done.7.vhigh
  90.7 0.0 collective-permute-done.6.vlow
  90.7 0.0 copy-done.18
  90.7 3.2 %shard_map.120 = f32[2,512,512]{2,1,0:T(8,128)} custom-call(f32[2,512,512]{2,1,0:T(8,128)} %get-tuple-element.20.begun, bf16[2,512,1280]{2,1,0:T(8,128)(2,1)S(1)} %copy-done, bf16[512,512]{1,0:T(8,128)(2,1)S(1)} %copy-done.16, bf16[512,512]{1,0:T(8,128)(2,1)S(1)} %copy-done.2, bf16[512,512]{1,0:T(8,128)(2,1)S(1)} %copy-done.14, ...), custom_call_target="tpu_custom_call", output_to_operand_aliasing={{}: (0, {})} | custom-call | flops 4600000000 | tf_op jit(solution)/shard_map/pallas_call | solution.py:548
  (13 shorter events, 0.0 us)
Async XLA Ops:
  0.6 20.7 %collective-permute-start.2 = (bf16[512,512]{1,0:T(8,128)(2,1)}, bf16[512,512]{1,0:T(8,128)(2,1)S(1)}, u32[]{:S(2)}, u32[]{:S(2)}) collective-permute-start(bf16[512,512]{1,0:T(8,128)(2,1)} %uown.3), channel_id=1, source_target_pairs={{1,0},{2,1},{3,2},{4,3},{5,4},{6,5},{7,6},{8,7},{9,8},{10,9},{11,1... | collective-permute-start | bytes 1572872 | tf_op jit(solution)/shard_map/ppermute | solution.py:424
  6.1 15.2 %collective-permute-start.1 = (bf16[512,512]{1,0:T(8,128)(2,1)}, bf16[512,512]{1,0:T(8,128)(2,1)S(1)}, u32[]{:S(2)}, u32[]{:S(2)}) collective-permute-start(bf16[512,512]{1,0:T(8,128)(2,1)} %uown.3), channel_id=1, source_target_pairs={{0,1},{1,2},{2,3},{3,4},{4,5},{5,6},{6,7},{7,8},{8,9},{9,10},{10,1... | collective-permute-start | bytes 1572872 | tf_op jit(solution)/shard_map/ppermute | solution.py:424
  8.2 1.5 %collective-permute-start = (bf16[8,32,128]{2,1,0:T(8,128)(2,1)}, bf16[8,32,128]{2,1,0:T(8,128)(2,1)S(1)}, u32[]{:S(2)}, u32[]{:S(2)}) collective-permute-start(bf16[8,32,128]{2,1,0:T(8,128)(2,1)} %get-tuple-element.15.refs_0_), channel_id=1, source_target_pairs={{0,1},{1,0},{2,3},{3,2},{4,5},{5,4},{6,7},{7,6},{8,9},{9,8},{10,11... | collective-permute-start | bytes 196616 | tf_op jit(solution)/shard_map/ppermute | solution.py:456
  9.6 0.8 copy-start.3
  10.5 0.8 copy-start.4
  12.1 21.5 %all-to-all-start = ((bf16[8,272,128]{2,1,0:T(8,128)(2,1)}), bf16[8,272,128]{2,1,0:T(8,128)(2,1)S(1)}, u32[]{:S(2)}, u32[]{:S(2)}) async-start(bf16[8,272,128]{2,1,0:T(8,128)(2,1)} %shard_map.113.after), calls=%async_computation | async-start | bytes 1114112 | tf_op jit(solution)/shard_map/all_to_all | solution.py:450
  21.3 25.0 %copy-start.1 = (bf16[512,512]{1,0:T(8,128)(2,1)S(1)}, bf16[512,512]{1,0:T(8,128)(2,1)}, u32[]{:S(2)}) copy-start(bf16[512,512]{1,0:T(8,128)(2,1)} %uown.3) | copy-start | bytes 1572868
  21.3 25.0 %copy-start.5 = (bf16[2,256,32]{1,2,0:T(8,128)(2,1)S(1)}, bf16[2,256,32]{1,2,0:T(8,128)(2,1)}, u32[]{:S(2)}) copy-start(bf16[2,256,32]{1,2,0:T(8,128)(2,1)} %param.16) | copy-start | bytes 98308
  21.3 25.0 %copy-start.19 = (bf16[2,256,32]{1,2,0:T(8,128)(2,1)S(1)}, bf16[2,256,32]{1,2,0:T(8,128)(2,1)}, u32[]{:S(2)}) copy-start(bf16[2,256,32]{1,2,0:T(8,128)(2,1)} %param.15) | copy-start | bytes 98308
  21.3 0.8 copy-start.13
  22.1 0.8 copy-start.15
  33.7 0.7 copy-start.6
  46.3 1.6 %copy-start.21 = (f32[2,512,512]{2,1,0:T(8,128)S(1)}, f32[2,512,512]{2,1,0:T(8,128)}, u32[]{:S(2)}) copy-start(f32[2,512,512]{2,1,0:T(8,128)} %get-tuple-element.16.near) | copy-start | bytes 6291460
  49.4 1.4 %copy-start.17 = (bf16[512,512]{1,0:T(8,128)(2,1)}, bf16[512,512]{1,0:T(8,128)(2,1)S(1)}, u32[]{:S(2)}) copy-start(bf16[512,512]{1,0:T(8,128)(2,1)S(1)} %get-tuple-element.21.vown) | copy-start | bytes 1572868
  49.4 16.7 %collective-permute-start.4 = (bf16[528,512]{1,0:T(8,128)(2,1)S(1)}, bf16[528,512]{1,0:T(8,128)(2,1)S(1)}, u32[]{:S(2)}, u32[]{:S(2)}) collective-permute-start(bf16[528,512]{1,0:T(8,128)(2,1)S(1)} %get-tuple-element.18.vown), channel_id=1, source_target_pairs={{1,0},{2,1},{3,2},{4,3},{5,4},{6,5},{7,6},{8,7},{9,8},{10,9},{11,1... | collective-permute-start | bytes 1622024 | tf_op jit(solution)/shard_map/ppermute | solution.py:424
  49.8 16.4 %collective-permute-start.3 = (bf16[528,512]{1,0:T(8,128)(2,1)S(1)}, bf16[528,512]{1,0:T(8,128)(2,1)S(1)}, u32[]{:S(2)}, u32[]{:S(2)}) collective-permute-start(bf16[528,512]{1,0:T(8,128)(2,1)S(1)} %get-tuple-element.18.vown), channel_id=1, source_target_pairs={{0,1},{1,2},{2,3},{3,4},{4,5},{5,6},{6,7},{7,8},{8,9},{9,10},{10,1... | collective-permute-start | bytes 1622024 | tf_op jit(solution)/shard_map/ppermute | solution.py:424
  50.0 0.8 copy-start.7
  64.7 16.8 %copy-start = (bf16[2,512,1280]{2,1,0:T(8,128)(2,1)S(1)}, bf16[2,512,1280]{2,1,0:T(8,128)(2,1)}, u32[]{:S(2)}) copy-start(bf16[2,512,1280]{2,1,0:T(8,128)(2,1)} %shard_map.114.w) | copy-start | bytes 7864324
  64.7 16.8 %copy-start.20 = (f32[2,512]{1,0:T(2,128)S(1)}, f32[2,512]{1,0:T(2,128)}, u32[]{:S(2)}) copy-start(f32[2,512]{1,0:T(2,128)} %diag.5) | copy-start | bytes 12292
  64.7 1.4 %collective-permute-start.5 = (bf16[8,80,128]{2,1,0:T(8,128)(2,1)S(1)}, bf16[8,80,128]{2,1,0:T(8,128)(2,1)S(1)}, u32[]{:S(2)}, u32[]{:S(2)}) collective-permute-start(bf16[8,80,128]{2,1,0:T(8,128)(2,1)S(1)} %all_to_all.21.refs_0_), channel_id=1, source_target_pairs={{0,1},{1,0},{2,3},{3,2},{4,5},{5,4},{6,7},{7,6},{8,9},{9,8},{10,11... | collective-permute-start | bytes 491528 | tf_op jit(solution)/shard_map/ppermute | solution.py:456
  68.4 0.8 copy-start.9
  69.2 0.8 copy-start.11
  70.0 11.5 %all-to-all-start.3 = ((bf16[8,80,128]{2,1,0:T(8,128)(2,1)}), bf16[8,80,128]{2,1,0:T(8,128)(2,1)S(1)}, u32[]{:S(2)}, u32[]{:S(2)}) async-start(bf16[8,80,128]{2,1,0:T(8,128)(2,1)} %shard_map.118), calls=%async_computation.3 | async-start | bytes 327680 | tf_op jit(solution)/shard_map/all_to_all | solution.py:450
  73.4 17.2 %collective-permute-start.7 = (bf16[512,512]{1,0:T(8,128)(2,1)}, bf16[512,512]{1,0:T(8,128)(2,1)S(1)}, u32[]{:S(2)}, u32[]{:S(2)}) collective-permute-start(bf16[512,512]{1,0:T(8,128)(2,1)} %copy-done.17), channel_id=1, source_target_pairs={{1,0},{2,1},{3,2},{4,3},{5,4},{6,5},{7,6},{8,7},{9,8},{10,9},{11,1... | collective-permute-start | bytes 1572872 | tf_op jit(solution)/shard_map/ppermute | solution.py:424
  77.5 13.1 %collective-permute-start.6 = (bf16[512,512]{1,0:T(8,128)(2,1)}, bf16[512,512]{1,0:T(8,128)(2,1)}, u32[]{:S(2)}, u32[]{:S(2)}) collective-permute-start(bf16[512,512]{1,0:T(8,128)(2,1)} %copy-done.17), channel_id=1, source_target_pairs={{0,1},{1,2},{2,3},{3,4},{4,5},{5,6},{6,7},{7,8},{8,9},{9,10},{10,1... | collective-permute-start | bytes 1572872 | tf_op jit(solution)/shard_map/ppermute | solution.py:424
  81.5 1.0 %copy-start.2 = (bf16[512,512]{1,0:T(8,128)(2,1)S(1)}, bf16[512,512]{1,0:T(8,128)(2,1)}, u32[]{:S(2)}) copy-start(bf16[512,512]{1,0:T(8,128)(2,1)} %uown.3) | copy-start | bytes 1572868
  82.6 1.0 %copy-start.8 = (bf16[528,512]{1,0:T(8,128)(2,1)S(1)}, bf16[528,512]{1,0:T(8,128)(2,1)}, u32[]{:S(2)}) copy-start(bf16[528,512]{1,0:T(8,128)(2,1)} %copy-done.7) | copy-start | bytes 1622020
  83.6 1.0 %copy-start.10 = (bf16[528,512]{1,0:T(8,128)(2,1)S(1)}, bf16[528,512]{1,0:T(8,128)(2,1)}, u32[]{:S(2)}) copy-start(bf16[528,512]{1,0:T(8,128)(2,1)} %copy-done.9) | copy-start | bytes 1622020
  84.7 1.0 %copy-start.12 = (bf16[528,512]{1,0:T(8,128)(2,1)S(1)}, bf16[528,512]{1,0:T(8,128)(2,1)}, u32[]{:S(2)}) copy-start(bf16[528,512]{1,0:T(8,128)(2,1)} %copy-done.11) | copy-start | bytes 1622020
  85.7 1.0 %copy-start.14 = (bf16[512,512]{1,0:T(8,128)(2,1)S(1)}, bf16[512,512]{1,0:T(8,128)(2,1)}, u32[]{:S(2)}) copy-start(bf16[512,512]{1,0:T(8,128)(2,1)} %copy-done.13) | copy-start | bytes 1572868
  86.7 1.0 %copy-start.16 = (bf16[512,512]{1,0:T(8,128)(2,1)S(1)}, bf16[512,512]{1,0:T(8,128)(2,1)}, u32[]{:S(2)}) copy-start(bf16[512,512]{1,0:T(8,128)(2,1)} %copy-done.15) | copy-start | bytes 1572868
  87.8 2.9 %copy-start.18 = (bf16[512,512]{1,0:T(8,128)(2,1)S(1)}, bf16[512,512]{1,0:T(8,128)(2,1)}, u32[]{:S(2)}) copy-start(bf16[512,512]{1,0:T(8,128)(2,1)} %copy-done.17) | copy-start | bytes 1572868

commit v16 on v15

--- a/solution.py
+++ b/solution.py
@@ -475,6 +475,7 @@
         share_kernel,
         sds((SLICES, shared + STATS + count * rank, LANES), BF16),
         [VMEM] * (1 + count),
+        megabytes=60,
     )(packed, *z1)
     held = exchange(mine)
     cols = held[:, shared, :blocks * far].astype(jnp.int32).reshape(-1)
@@ -542,7 +543,6 @@
         [outs, sds((ops, columns), F32), sds((ops, columns), F32), sds((8, columns), F32)],
         [VMEM] * 10,
         scratch + [pltpu.VMEM((STATS, columns), F32), pltpu.SemaphoreType.DMA((blocks,))],
-        micros=10.0,
         out_specs=[ANY, VMEM, VMEM, VMEM],
     )(w, low, sources, high, low0, first, high0, self_terms, left, c2)
     images = call(
@@ -550,7 +550,6 @@
         outs,
         [ANY] + [VMEM] * 11,
         scratch + [pltpu.SemaphoreType.DMA((blocks,))],
-        micros=4.0,
         out_specs=ANY,
         alias={0: 0},
     )(images, w, low, sources, high, low1, second, high1, self_terms, left, c2, aux)

time: 94.8 us -> 86.7 us (0.915)
  blocking collectives: 24.7 us -> 38.6 us
  local copies, waits for them, and re-layouts: 14.3 us -> 4.55 us
  starting transfers between devices: 19.3 us -> 13.8 us
  waiting for transfers between devices: 12.5 us -> 7.19 us
    all_to_all x2 -> x3, blocking collectives: 24.7 us -> 38.6 us  [exchange(): lax.all_to_all(x, 'store', 0, 0, axis_index_groups=groups, tiled=True)]
    unnamed x44 -> x24, local copies, waits for them, and re-layouts: 14.2 us -> 4.47 us
    all_to_all x2 -> x1, waiting for transfers between devices: 9.64 us -> 5.71 us  [exchange(): lax.all_to_all(x, 'store', 0, 0, axis_index_groups=groups, tiled=True)]
    all_to_all x2 -> x1, starting transfers between devices: 9.14 us -> 5.76 us  [exchange(): lax.all_to_all(x, 'store', 0, 0, axis_index_groups=groups, tiled=True)]
    ppermute x3, starting transfers between devices: 9.94 us -> 7.78 us  [ring(): lax.ppermute(block, 'store', backward)]
    ppermute x2, waiting for transfers between devices: 2.85 us -> 1.46 us  [across(): parts.append(lax.ppermute(x, 'store', pairs))]
    pallas_call x1, Pallas kernels: 3.16 us -> 2.14 us  [shards(): call(final_second, outs, [ANY] + [VMEM] * 11, scratch + [pltpu.SemaphoreT...]
  transfers between devices with their start and end apart: 10 -> 9, of which waited for: 4 -> 2; matrix products, arithmetic and copies ran while one was open for 0% -> 0% of each run, Pallas kernels for 15% -> 19%
where the time goes in v16:
time: 86.7 us; the launch traced here: 86.3 us
  blocking collectives  38.6 us (45%)
  Pallas kernels  21.4 us (25%)
  starting transfers between devices  13.8 us (16%)
  waiting for transfers between devices  7.19 us (8%)
  local copies, waits for them, and re-layouts  4.55 us (5%)
    all_to_all x3, blocking collectives, exchange(): lax.all_to_all(x, 'store', 0, 0, axis_index_groups=groups, tiled=True)  38.6 us
    ppermute x3, starting transfers between devices, ring(): lax.ppermute(block, 'store', backward)  7.78 us
    all_to_all x1, starting transfers between devices, exchange(): lax.all_to_all(x, 'store', 0, 0, axis_index_groups=groups, tiled=True)  5.76 us
    all_to_all x1, waiting for transfers between devices, exchange(): lax.all_to_all(x, 'store', 0, 0, axis_index_groups=groups, tiled=True)  5.71 us
    pallas_call x1, Pallas kernels, shards(): call(near_kernel, [sds((ops, rows, columns), F32), sds((8, LANES), F32)],...  4.99 us
    unnamed x24, local copies, waits for them, and re-layouts  4.47 us
    pallas_call x1, Pallas kernels, shards(): call(functools.partial(order_tiles, all_blocks), sds((blocks, ops * size,...  3.43 us
    pallas_call x1, Pallas kernels, shards(): call(final_first, [outs, sds((ops, columns), F32), sds((ops, columns), F3...  2.85 us
  transfers between devices with their start and end apart: 9, of which 2 were waited for; matrix products, arithmetic and copies ran while one was open for 0% of the time, Pallas kernels for 19%

profile of v16, /device:TPU:0, one launch (start us, length us, event | category | flops | bytes accessed | tf_op | source)
XLA Modules:
  0.0 86.3 jit_solution(17429948152455993332)
XLA Ops:
  0.6 5.5 %collective-permute-start.2 = (bf16[512,512]{1,0:T(8,128)(2,1)}, bf16[512,512]{1,0:T(8,128)(2,1)S(1)}, u32[]{:S(2)}, u32[]{:S(2)}) collective-permute-start(bf16[512,512]{1,0:T(8,128)(2,1)} %uown.3), channel_id=1, source_target_pairs={{1,0},{2,1},{3,2},{4,3},{5,4},{6,5},{7,6},{8,7},{9,8},{10,9},{11,1... | collective-permute-start | bytes 1572872 | tf_op jit(solution)/shard_map/ppermute | solution.py:424
  6.1 0.0 collective-permute-start.1
  6.1 2.0 %shard_map.112 = (bf16[8,32,128]{2,1,0:T(8,128)(2,1)}, bf16[208,128]{1,0:T(8,128)(2,1)}) custom-call(s32[2,6]{1,0:T(2,128)} %far_cols.1, bf16[512,512]{1,0:T(8,128)(2,1)} %uown.3, bf16[2,32,256]{2,1,0:T(8,128)(2,1)} %bitcast.7, bf16[2,2,6,32,32]{4,3,2,1,0:T(8,128)(2,1)} %coup.1), custom_call_target="tpu_custom_call" | custom-call | tf_op jit(solution)/shard_map/pallas_call | solution.py:467
  8.2 0.0 collective-permute-start
  8.2 1.5 %collective-permute-done.refs_1_ = bf16[8,32,128]{2,1,0:T(8,128)(2,1)S(1)} collective-permute-done((bf16[8,32,128]{2,1,0:T(8,128)(2,1)}, bf16[8,32,128]{2,1,0:T(8,128)(2,1)S(1)}, u32[]{:S(2)}, u32[]{:S(2)}) %collective-permute-start) | collective-permute-done | bytes 65568 | tf_op jit(solution)/shard_map/ppermute | solution.py:456
  9.6 0.0 copy-start.11
  9.6 0.6 copy-done.11
  10.2 1.8 %shard_map.113.after = bf16[8,272,128]{2,1,0:T(8,128)(2,1)} custom-call(bf16[208,128]{1,0:T(8,128)(2,1)} %get-tuple-element.14.packed, bf16[8,32,128]{2,1,0:T(8,128)(2,1)} %get-tuple-element.15.refs_0_, bf16[8,32,128]{2,1,0:T(8,128)(2,1)} %copy-done.11), custom_call_target="tpu_custom_call" | custom-call | tf_op jit(solution)/shard_map/pallas_call | solution.py:474
  12.0 5.8 %all-to-all-start = ((bf16[8,272,128]{2,1,0:T(8,128)(2,1)}), bf16[8,272,128]{2,1,0:T(8,128)(2,1)S(1)}, u32[]{:S(2)}, u32[]{:S(2)}) async-start(bf16[8,272,128]{2,1,0:T(8,128)(2,1)} %shard_map.113.after), calls=%async_computation | async-start | bytes 1114112 | tf_op jit(solution)/shard_map/all_to_all | solution.py:450
  17.8 3.4 %shard_map.114.w = bf16[2,512,1280]{2,1,0:T(8,128)(2,1)} custom-call(s32[2,5]{1,0:T(2,128)} %cols.1, s32[2]{0:T(128)} %count.1, s32[1]{0:T(128)} %bitcast.row0, bf16[2,2,5,256,256]{4,3,2,1,0:T(8,128)(2,1)} %tiles.1, bf16[8,272,128]{2,1,0:T(8,128)(2,1)} %shard_map.113.after), custom_call_target="tpu_custom_call" | custom-call | tf_op jit(solution)/shard_map/pallas_call | solution.py:483
  21.2 0.0 copy-start.1
  21.2 0.0 copy-start.6
  21.2 0.0 copy-start.7
  21.2 0.0 collective-permute-done.2.high.uhigh
  21.2 0.0 copy-start.2
  21.2 0.0 collective-permute-done.1.low.ulow
  21.2 0.8 copy-done.2
  22.0 0.0 copy-start.4
  22.0 0.8 copy-done.4
  22.8 5.0 %shard_map.115 = (f32[2,512,512]{2,1,0:T(8,128)}, f32[8,128]{1,0:T(8,128)}) custom-call(bf16[2,512,1280]{2,1,0:T(8,128)(2,1)} %shard_map.114.w, bf16[512,512]{1,0:T(8,128)(2,1)} %copy-done.4, bf16[512,512]{1,0:T(8,128)(2,1)} %uown.3, bf16[512,512]{1,0:T(8,128)(2,1)} %copy-done.2, f32[2,512]{1,0:T(2,128)} %diag.5), custom_call_target="tpu_custom_call" | custom-call | flops 11500000256 | tf_op jit(solution)/shard_map/pallas_call | solution.py:489
  27.8 5.7 %all-to-all-done.held = bf16[8,272,128]{2,1,0:T(8,128)(2,1)S(1)} async-done(((bf16[8,272,128]{2,1,0:T(8,128)(2,1)}), bf16[8,272,128]{2,1,0:T(8,128)(2,1)S(1)}, u32[]{:S(2)}, u32[]{:S(2)}) %all-to-all-start) | async-done | bytes 557088 | tf_op jit(solution)/shard_map/all_to_all | solution.py:450
  33.5 0.1 reshape.18.cols
  33.6 0.0 copy-start.9
  33.6 0.7 copy-done.9
  34.3 1.1 %shard_map.116 = bf16[8,64,128]{2,1,0:T(8,128)(2,1)S(1)} custom-call(s32[96]{0:T(128)S(1)} %reshape.18.cols, s32[1]{0:T(128)} %bitcast.3.group, f32[8,128]{1,0:T(8,128)S(1)} %copy-done.9, bf16[8,272,128]{2,1,0:T(8,128)(2,1)S(1)} %all-to-all-done.held), custom_call_target="tpu_custom_call" | custom-call | tf_op jit(solution)/shard_map/pallas_call | solution.py:497
  35.4 10.8 %all_to_all.20.cmsg = bf16[8,64,128]{2,1,0:T(8,128)(2,1)S(1)} all-to-all(bf16[8,64,128]{2,1,0:T(8,128)(2,1)S(1)} %shard_map.116), channel_id=1, replica_groups={{0,2,4,6,8,10,12,14},{1,3,5,7,9,11,13,15},{16,18,20,22,24,26,28,30},{17..., dimensions={0} | all-to-all | bytes 262144 | tf_op jit(solution)/shard_map/all_to_all | solution.py:450
  46.2 0.0 copy-done.1
  46.2 0.0 copy-done.6
  46.2 0.0 copy-done.7
  46.2 0.0 copy-start.10
  46.2 1.6 %copy-done.10 = f32[2,512,512]{2,1,0:T(8,128)S(1)} copy-done((f32[2,512,512]{2,1,0:T(8,128)S(1)}, f32[2,512,512]{2,1,0:T(8,128)}, u32[]{:S(2)}) %copy-start.10) | copy-done | bytes 2097176
  47.8 1.4 %shard_map.117 = (bf16[528,512]{1,0:T(8,128)(2,1)S(1)}, bf16[512,512]{1,0:T(8,128)(2,1)S(1)}, bf16[8,80,128]{2,1,0:T(8,128)(2,1)S(1)}) custom-call(bf16[512,512]{1,0:T(8,128)(2,1)S(1)} %copy-done.1, f32[2,512,512]{2,1,0:T(8,128)S(1)} %copy-done.10, bf16[2,32,256]{2,1,0:T(8,128)(2,1)S(1)} %bitcast.4, bf16[2,32,256]{2,1,0:T(8,128)(2,1)S(1)} %bitcast.8, ...), custom_call_target="tpu_custom_call" | custom-call | flops 2300000000 | tf_op jit(solution)/shard_map/pallas_call | solution.py:505
  49.2 0.3 collective-permute-start.4
  49.5 0.2 collective-permute-start.3
  49.8 14.7 %all_to_all.21.refs_0_ = bf16[8,80,128]{2,1,0:T(8,128)(2,1)S(1)} all-to-all(bf16[8,80,128]{2,1,0:T(8,128)(2,1)S(1)} %get-tuple-element.19), channel_id=1, replica_groups={{0,2,4,6,8,10,12,14},{1,3,5,7,9,11,13,15},{16,18,20,22,24,26,28,30},{17..., dimensions={0} | all-to-all | bytes 327680 | tf_op jit(solution)/shard_map/all_to_all | solution.py:450
  64.5 0.0 collective-permute-start.5
  64.5 0.0 copy-start.3
  64.5 0.0 copy-start.5
  64.5 0.0 copy-start.8
  64.5 2.0 %collective-permute-start.7 = (bf16[512,512]{1,0:T(8,128)(2,1)S(1)}, bf16[512,512]{1,0:T(8,128)(2,1)S(1)}, u32[]{:S(2)}, u32[]{:S(2)}) collective-permute-start(bf16[512,512]{1,0:T(8,128)(2,1)S(1)} %get-tuple-element.21.vown), channel_id=1, source_target_pairs={{1,0},{2,1},{3,2},{4,3},{5,4},{6,5},{7,6},{8,7},{9,8},{10,9},{11,1... | collective-permute-start | bytes 1572872 | tf_op jit(solution)/shard_map/ppermute | solution.py:424
  66.5 0.0 collective-permute-start.6
  66.5 0.0 collective-permute-done.5.refs_1_
  66.5 0.0 collective-permute-done.4.after_high.vhigh
  66.5 0.0 collective-permute-done.3.after_low.vlow
  66.5 0.0 copy-start
  66.5 1.6 %shard_map.118 = bf16[8,80,128]{2,1,0:T(8,128)(2,1)S(1)} custom-call(s32[96]{0:T(128)S(1)} %reshape.18.cols, s32[1]{0:T(128)} %bitcast.3.group, bf16[528,512]{1,0:T(8,128)(2,1)S(1)} %collective-permute-done.3.after_low.vlow, bf16[528,512]{1,0:T(8,128)(2,1)S(1)} %collective-permute-done.4.after_high.vhigh, bf16[8,272,128]{2,1,0:T(8,128)(2,1)S(1)} %all-to-all-done.held, ...), custom_call_target="tpu_custom_call" | custom-call | flops 34500001792 | tf_op jit(solution)/shard_map/pallas_call | solution.py:523
  68.2 13.0 %all_to_all.22.cmsg = bf16[8,80,128]{2,1,0:T(8,128)(2,1)S(1)} all-to-all(bf16[8,80,128]{2,1,0:T(8,128)(2,1)S(1)} %shard_map.118), channel_id=1, replica_groups={{0,2,4,6,8,10,12,14},{1,3,5,7,9,11,13,15},{16,18,20,22,24,26,28,30},{17..., dimensions={0} | all-to-all | bytes 327680 | tf_op jit(solution)/shard_map/all_to_all | solution.py:450
  81.2 0.0 copy-done.3
  81.2 0.0 copy-done.5
  81.2 0.0 copy-done.8
  81.2 0.0 copy-done
  81.2 2.8 %shard_map.119 = (f32[2,512,512]{2,1,0:T(8,128)}, f32[2,512]{1,0:T(2,128)}, f32[2,512]{1,0:T(2,128)}, f32[8,512]{1,0:T(8,128)S(1)}) custom-call(bf16[2,512,1280]{2,1,0:T(8,128)(2,1)S(1)} %copy-done, bf16[512,512]{1,0:T(8,128)(2,1)S(1)} %copy-done.5, bf16[512,512]{1,0:T(8,128)(2,1)S(1)} %copy-done.1, bf16[512,512]{1,0:T(8,128)(2,1)S(1)} %copy-done.3, ...), custom_call_target="tpu_custom_call" | custom-call | tf_op jit(solution)/shard_map/pallas_call | solution.py:541
  84.1 0.0 collective-permute-done.7.vhigh
  84.1 0.0 collective-permute-done.6.vlow
  84.1 2.1 %shard_map.120 = f32[2,512,512]{2,1,0:T(8,128)} custom-call(f32[2,512,512]{2,1,0:T(8,128)} %get-tuple-element.20.begun, bf16[2,512,1280]{2,1,0:T(8,128)(2,1)S(1)} %copy-done, bf16[512,512]{1,0:T(8,128)(2,1)S(1)} %copy-done.5, bf16[512,512]{1,0:T(8,128)(2,1)S(1)} %copy-done.1, bf16[512,512]{1,0:T(8,128)(2,1)S(1)} %copy-done.3, ...), custom_call_target="tpu_custom_call", output_to_operand_aliasing={{}: (0, {})} | custom-call | tf_op jit(solution)/shard_map/pallas_call | solution.py:548
  (1 shorter events, 0.0 us)
Async XLA Ops:
  0.6 20.6 %collective-permute-start.2 = (bf16[512,512]{1,0:T(8,128)(2,1)}, bf16[512,512]{1,0:T(8,128)(2,1)S(1)}, u32[]{:S(2)}, u32[]{:S(2)}) collective-permute-start(bf16[512,512]{1,0:T(8,128)(2,1)} %uown.3), channel_id=1, source_target_pairs={{1,0},{2,1},{3,2},{4,3},{5,4},{6,5},{7,6},{8,7},{9,8},{10,9},{11,1... | collective-permute-start | bytes 1572872 | tf_op jit(solution)/shard_map/ppermute | solution.py:424
  6.1 15.1 %collective-permute-start.1 = (bf16[512,512]{1,0:T(8,128)(2,1)}, bf16[512,512]{1,0:T(8,128)(2,1)S(1)}, u32[]{:S(2)}, u32[]{:S(2)}) collective-permute-start(bf16[512,512]{1,0:T(8,128)(2,1)} %uown.3), channel_id=1, source_target_pairs={{0,1},{1,2},{2,3},{3,4},{4,5},{5,6},{6,7},{7,8},{8,9},{9,10},{10,1... | collective-permute-start | bytes 1572872 | tf_op jit(solution)/shard_map/ppermute | solution.py:424
  8.2 1.5 %collective-permute-start = (bf16[8,32,128]{2,1,0:T(8,128)(2,1)}, bf16[8,32,128]{2,1,0:T(8,128)(2,1)S(1)}, u32[]{:S(2)}, u32[]{:S(2)}) collective-permute-start(bf16[8,32,128]{2,1,0:T(8,128)(2,1)} %get-tuple-element.15.refs_0_), channel_id=1, source_target_pairs={{0,1},{1,0},{2,3},{3,2},{4,5},{5,4},{6,7},{7,6},{8,9},{9,8},{10,11... | collective-permute-start | bytes 196616 | tf_op jit(solution)/shard_map/ppermute | solution.py:456
  9.6 0.6 copy-start.11
  12.0 21.5 %all-to-all-start = ((bf16[8,272,128]{2,1,0:T(8,128)(2,1)}), bf16[8,272,128]{2,1,0:T(8,128)(2,1)S(1)}, u32[]{:S(2)}, u32[]{:S(2)}) async-start(bf16[8,272,128]{2,1,0:T(8,128)(2,1)} %shard_map.113.after), calls=%async_computation | async-start | bytes 1114112 | tf_op jit(solution)/shard_map/all_to_all | solution.py:450
  21.2 25.0 %copy-start.1 = (bf16[512,512]{1,0:T(8,128)(2,1)S(1)}, bf16[512,512]{1,0:T(8,128)(2,1)}, u32[]{:S(2)}) copy-start(bf16[512,512]{1,0:T(8,128)(2,1)} %uown.3) | copy-start | bytes 1572868
  21.2 25.0 %copy-start.6 = (bf16[2,256,32]{1,2,0:T(8,128)(2,1)S(1)}, bf16[2,256,32]{1,2,0:T(8,128)(2,1)}, u32[]{:S(2)}) copy-start(bf16[2,256,32]{1,2,0:T(8,128)(2,1)} %param.15) | copy-start | bytes 98308
  21.2 25.0 %copy-start.7 = (bf16[2,256,32]{1,2,0:T(8,128)(2,1)S(1)}, bf16[2,256,32]{1,2,0:T(8,128)(2,1)}, u32[]{:S(2)}) copy-start(bf16[2,256,32]{1,2,0:T(8,128)(2,1)} %param.16) | copy-start | bytes 98308
  21.2 0.8 copy-start.2
  22.0 0.8 copy-start.4
  33.6 0.7 copy-start.9
  46.2 1.6 %copy-start.10 = (f32[2,512,512]{2,1,0:T(8,128)S(1)}, f32[2,512,512]{2,1,0:T(8,128)}, u32[]{:S(2)}) copy-start(f32[2,512,512]{2,1,0:T(8,128)} %get-tuple-element.16.near) | copy-start | bytes 6291460
  49.2 17.3 %collective-permute-start.4 = (bf16[528,512]{1,0:T(8,128)(2,1)S(1)}, bf16[528,512]{1,0:T(8,128)(2,1)S(1)}, u32[]{:S(2)}, u32[]{:S(2)}) collective-permute-start(bf16[528,512]{1,0:T(8,128)(2,1)S(1)} %get-tuple-element.18.vown), channel_id=1, source_target_pairs={{1,0},{2,1},{3,2},{4,3},{5,4},{6,5},{7,6},{8,7},{9,8},{10,9},{11,1... | collective-permute-start | bytes 1622024 | tf_op jit(solution)/shard_map/ppermute | solution.py:424
  49.5 17.0 %collective-permute-start.3 = (bf16[528,512]{1,0:T(8,128)(2,1)S(1)}, bf16[528,512]{1,0:T(8,128)(2,1)S(1)}, u32[]{:S(2)}, u32[]{:S(2)}) collective-permute-start(bf16[528,512]{1,0:T(8,128)(2,1)S(1)} %get-tuple-element.18.vown), channel_id=1, source_target_pairs={{0,1},{1,2},{2,3},{3,4},{4,5},{5,6},{6,7},{7,8},{8,9},{9,10},{10,1... | collective-permute-start | bytes 1622024 | tf_op jit(solution)/shard_map/ppermute | solution.py:424
  64.5 2.0 %collective-permute-start.5 = (bf16[8,80,128]{2,1,0:T(8,128)(2,1)S(1)}, bf16[8,80,128]{2,1,0:T(8,128)(2,1)S(1)}, u32[]{:S(2)}, u32[]{:S(2)}) collective-permute-start(bf16[8,80,128]{2,1,0:T(8,128)(2,1)S(1)} %all_to_all.21.refs_0_), channel_id=1, source_target_pairs={{0,1},{1,0},{2,3},{3,2},{4,5},{5,4},{6,7},{7,6},{8,9},{9,8},{10,11... | collective-permute-start | bytes 491528 | tf_op jit(solution)/shard_map/ppermute | solution.py:456
  64.5 16.7 %copy-start.3 = (bf16[512,512]{1,0:T(8,128)(2,1)S(1)}, bf16[512,512]{1,0:T(8,128)(2,1)}, u32[]{:S(2)}) copy-start(bf16[512,512]{1,0:T(8,128)(2,1)} %copy-done.2) | copy-start | bytes 1572868
  64.5 16.7 %copy-start.5 = (bf16[512,512]{1,0:T(8,128)(2,1)S(1)}, bf16[512,512]{1,0:T(8,128)(2,1)}, u32[]{:S(2)}) copy-start(bf16[512,512]{1,0:T(8,128)(2,1)} %copy-done.4) | copy-start | bytes 1572868
  64.5 16.7 %copy-start.8 = (f32[2,512]{1,0:T(2,128)S(1)}, f32[2,512]{1,0:T(2,128)}, u32[]{:S(2)}) copy-start(f32[2,512]{1,0:T(2,128)} %diag.5) | copy-start | bytes 12292
  64.5 19.5 %collective-permute-start.7 = (bf16[512,512]{1,0:T(8,128)(2,1)S(1)}, bf16[512,512]{1,0:T(8,128)(2,1)S(1)}, u32[]{:S(2)}, u32[]{:S(2)}) collective-permute-start(bf16[512,512]{1,0:T(8,128)(2,1)S(1)} %get-tuple-element.21.vown), channel_id=1, source_target_pairs={{1,0},{2,1},{3,2},{4,3},{5,4},{6,5},{7,6},{8,7},{9,8},{10,9},{11,1... | collective-permute-start | bytes 1572872 | tf_op jit(solution)/shard_map/ppermute | solution.py:424
  66.5 17.6 %collective-permute-start.6 = (bf16[512,512]{1,0:T(8,128)(2,1)S(1)}, bf16[512,512]{1,0:T(8,128)(2,1)S(1)}, u32[]{:S(2)}, u32[]{:S(2)}) collective-permute-start(bf16[512,512]{1,0:T(8,128)(2,1)S(1)} %get-tuple-element.21.vown), channel_id=1, source_target_pairs={{0,1},{1,2},{2,3},{3,4},{4,5},{5,6},{6,7},{7,8},{8,9},{9,10},{10,1... | collective-permute-start | bytes 1572872 | tf_op jit(solution)/shard_map/ppermute | solution.py:424
  66.5 14.7 %copy-start = (bf16[2,512,1280]{2,1,0:T(8,128)(2,1)S(1)}, bf16[2,512,1280]{2,1,0:T(8,128)(2,1)}, u32[]{:S(2)}) copy-start(bf16[2,512,1280]{2,1,0:T(8,128)(2,1)} %shard_map.114.w) | copy-start | bytes 7864324

commit v17 on v9

--- a/solution.py
+++ b/solution.py
@@ -13,7 +13,7 @@
 HALF = 64
 SLICES = 8
 STATS = 16
-HBM_RATE = 3690000
+FLOP_RATE = 1150000000
 F32 = jnp.float32
 BF16 = jnp.bfloat16
 
@@ -22,7 +22,7 @@
 ANY = pl.BlockSpec(memory_space=pl.ANY)
 
 
-def call(body, out_shape, in_specs, scratch=(), micros=1.0, megabytes=20, out_specs=None, alias=None):
+def call(body, out_shape, in_specs, scratch=(), micros=0.0, megabytes=20, out_specs=None, alias=None):
     many = isinstance(out_shape, (list, tuple))
     if out_specs is None:
         out_specs = [VMEM] * len(out_shape) if many else VMEM
@@ -35,7 +35,7 @@
         scratch_shapes=list(scratch),
         compiler_params=pltpu.CompilerParams(vmem_limit_bytes=megabytes * 1024 * 1024),
         cost_estimate=pl.CostEstimate(
-            flops=0, bytes_accessed=int(micros * HBM_RATE), transcendentals=0
+            flops=int(micros * FLOP_RATE), bytes_accessed=0, transcendentals=0
         ),
     )
 
@@ -71,7 +71,7 @@
     return x[:, pair * LANES:(pair + 1) * LANES]
 
 
-def order_tiles(all_blocks, cols, count, row0, tiles, out):
+def order_tiles(all_blocks, cols, count, row0, tiles, after, out):
     ops, blocks, near, size, _ = tiles.shape
     for b in range(blocks):
         for k in range(near):
@@ -86,14 +86,16 @@
                 )
 
 
-def coeff_kernel(far_cols, u, left, right, coup, z_out, out):
+def coeff_kernel(count, far_cols, u, left, right, coup, out, u_out):
     ops, blocks, far, rank, _ = coup.shape
     size = right.shape[2]
+    u_out[...] = u[...]
     z = [dot(right[b], u[b * size:(b + 1) * size, :]) for b in range(blocks)]
+    at = 3 * ops * rank + STATS + rank
     for pair in range(SLICES // 2):
         first, second = halves(chunk(z[0], pair), chunk(z[1], pair))
-        z_out[2 * pair] = first.astype(BF16)
-        z_out[2 * pair + 1] = second.astype(BF16)
+        out[2 * pair, at:at + rank, :] = first.astype(BF16)
+        out[2 * pair + 1, at:at + rank, :] = second.astype(BF16)
     whole, rest = [], []
     for b in range(blocks):
         tiles = [
@@ -106,25 +108,25 @@
     names = jnp.zeros((STATS, LANES), F32)
     for b in range(blocks):
         for f in range(far):
-            names = jnp.where(lane == b * far + f, far_cols[b, f].astype(F32), names)
+            col = far_cols[b, f]
+            device = lax.div(col, blocks)
+            slot = lax.rem(device, count) * SLICES + lax.div(device, count)
+            name = (slot * blocks + lax.rem(col, blocks)).astype(F32)
+            names = jnp.where(lane == b * far + f, name, names)
     mixed = [dot(right[b], left[b], ((1,), (1,))) for b in range(blocks)]
     high = [m.astype(BF16) for m in mixed]
     low = [(m - h.astype(F32)).astype(BF16) for m, h in zip(mixed, high)]
-    out[...] = jnp.concatenate(
+    whole = jnp.concatenate(
         whole
         + [jnp.concatenate(rest, axis=1), names.astype(BF16), jnp.concatenate(high + low, axis=1)],
         axis=0,
     )
-
-
-def share_kernel(packed, after_low, after_high, *refs):
-    parts, out = refs[:-1], refs[-1]
-    rows = packed.shape[0]
-    rank = parts[0].shape[1]
     for s in range(SLICES):
-        out[s, 0:rows, :] = packed[...]
-    for m, part in enumerate(parts):
-        out[:, rows + m * rank:rows + (m + 1) * rank, :] = part[...]
+        out[s, 0:at, :] = whole
+
+
+def take_kernel(held, after, out):
+    out[...] = held[:, held.shape[1] - out.shape[1]:, :]
 
 
 def coupling_rows(held, s, b, ops, rank):
@@ -155,27 +157,24 @@
     return both.reshape(count * 2 * rank, LANES).astype(BF16)
 
 
-def held_part(held, m, ops, rank):
-    at = 3 * ops * rank + STATS + (m + 1) * rank
-    return held[:, at:at + rank, :].astype(F32)
-
-
 def group_at(group, m, groups, step):
     return pl.multiple_of(lax.rem(group[0] + (groups - m), groups) * step, step)
 
 
-def first_couple(ops, rank, far, cols, group, held, out, mixed, zs):
+def first_couple(ops, rank, far, cols, group, held, late, *refs):
+    parts, (out, mixed, zs) = refs[:-3], refs[-3:]
     step = SLICES * 2 * rank
-    count = zs.shape[0] // step
-    for m in range(count):
-        at = group_at(group, m, count, step)
-        zs[pl.ds(at, step), :] = spread_rows(held_part(held, m, ops, rank), rank)
+    body = ops * rank
+    for m, part in enumerate(parts):
+        at = group_at(group, m, len(parts), step)
+        zs[pl.ds(at, step), :] = spread_rows(part[...].astype(F32), rank)
+    out[:, body:, :] = late[...]
     at = 3 * ops * rank + STATS
     first = lax.broadcasted_iota(jnp.int32, (rank, LANES), 1) < HALF
     for s in range(SLICES):
         c = [couple(cols, held, s, b, ops, rank, far, [zs]) for b in range(2)]
         c = halves(c[0], c[1])[0]
-        out[s] = c.astype(BF16)
+        out[s, 0:body, :] = c.astype(BF16)
         for o in range(ops):
             x = c[o * rank:(o + 1) * rank]
             parts = [jnp.where(first, x, 0.0), jnp.where(first, 0.0, x)] * 2
@@ -235,7 +234,7 @@
     return jnp.where(good, inner / jnp.where(good, squares, 1.0), 0.0)
 
 
-def near_kernel(w, low, own, high, diag, right, c1, image, edge, msg):
+def near_kernel(w, low, own, high, diag, right, image, edge, msg):
     ops = image.shape[0]
     blocks, rank, size = right.shape
     rows, columns = own.shape
@@ -259,7 +258,6 @@
     edges = pieces_of(shifts + [squares])
     edge[...] = edges
     edges = edges.astype(F32)
-    msg[:, 0:body, :] = c1[...]
     for o in range(ops):
         shift = row3(edges, o)
         z = []
@@ -268,11 +266,11 @@
             v = image[o, b * size:(b + 1) * size, :] - shift * ub
             image[o, b * size:(b + 1) * size, :] = v
             z.append(dot(right[b], v.astype(BF16)))
-        spread_pairs(msg, slice(body + o * rank, body + (o + 1) * rank), z[0], z[1])
-    spread_pairs(msg, slice(2 * body, 2 * body + STATS), edges, edges)
-
-
-def image_kernel(own, near, edge, left, got, mixed, first, second, cown, xmsg, image, coef):
+        spread_pairs(msg, slice(o * rank, (o + 1) * rank), z[0], z[1])
+    spread_pairs(msg, slice(body, body + STATS), edges, edges)
+
+
+def image_kernel(own, near, edge, left, got, mixed, vout, cown, xmsg, image, coef):
     ops = near.shape[0]
     blocks, rank, size = left.shape
     rows, columns = own.shape
@@ -309,18 +307,19 @@
             v = image[b * size:(b + 1) * size, :] - change * ub
             part = jnp.sum(v * v, axis=0, keepdims=True)
             spread = part if spread is None else spread + part
-            (first, second)[o][b * size:(b + 1) * size, :] = v.astype(BF16)
+            vout[(o * blocks + b) * size:(o * blocks + b + 1) * size, :] = v.astype(BF16)
         spreads.append(spread)
     every = pieces_of(shifts + [squares] + spreads)
-    first[rows:, :] = every
+    vout[ops * rows:, :] = every
     at = SLICES * (body + STATS)
     for j in range(columns // LANES):
         xmsg[at + j * STATS:at + (j + 1) * STATS, :] = chunk(every, j)
 
 
 def second_couple(panels, ops, rank, far, cols, group, held, *refs):
-    parts, (out, zs) = refs[:-2], refs[-2:]
-    count = len(parts)
+    out, zs = refs[-2:]
+    count = (len(refs) - 2) // 2
+    z1, parts = refs[:count], refs[count:2 * count]
     body = ops * rank
     step = SLICES * 2 * rank
     at = SLICES * body
@@ -337,7 +336,7 @@
     rough = pieces_of([total / scale_sq for total in totals])
     for m, x in enumerate(parts):
         row = group_at(group, m, count, step)
-        base = held_part(held, m, ops, rank)
+        base = z1[m][...].astype(F32)
         z = x[0:at, :].astype(F32).reshape(SLICES, body, LANES)
         for o in range(ops):
             delta = join3(edges[m], o) - row3(rough.astype(F32), o)
@@ -361,7 +360,8 @@
     factor, changes, offset = rows3
     copies = []
     for at, (u, v) in enumerate(zip(u3, v3)):
-        value = v[0:rows, :].astype(F32) * factor + u[...].astype(F32) * changes[at]
+        v = v[o * rows:(o + 1) * rows, :].astype(F32)
+        value = v * factor + u[...].astype(F32) * changes[at]
         ext[at] = value.astype(BF16)
     take_coefs(cmsg, coef, ops * rank)
     for b in range(blocks):
@@ -372,18 +372,17 @@
         c = c - offset * cown[row:row + rank, :].astype(F32)
         far = dot(left[b], c.astype(BF16), ((0,), (0,)))
         here = slice(b * size, (b + 1) * size)
-        out[here, :] = (
+        out[o, here, :] = (
             product
             + diagonal_of(diag, o, b, size, columns) * ext[1, here, :].astype(F32)
             + far.astype(BF16).astype(F32)
         )
-        copies.append(pltpu.make_async_copy(out.at[here], images.at[o, here], sem.at[b]))
+        copies.append(pltpu.make_async_copy(out.at[o, here], images.at[o, here], sem.at[o, b]))
         copies[-1].start()
-    for copy in copies:
-        copy.wait()
-
-
-def final_first(
+    return copies
+
+
+def final_kernel(
     panels,
     group,
     w,
@@ -400,7 +399,6 @@
     images,
     heights,
     norms,
-    aux,
     ext,
     coef,
     out,
@@ -446,70 +444,30 @@
         norms[o:o + 1, :] = norm
         factor = reverse / norm
         changes = [
-            (row3(v[rows:rows + STATS, :].astype(F32), o) - high) * factor
+            (row3(v[ops * rows:, :].astype(F32), o) - high) * factor
             for v in (vlow, vown, vhigh)
         ]
         found.append((factor, changes, (high - row3(rough, o)) * factor))
-    factor, changes, offset = found[1]
-    aux[0:1, :] = factor
-    aux[1:2, :] = offset
-    for at in range(3):
-        aux[2 + at:3 + at, :] = changes[at]
-    apply_second(
-        0,
-        found[0],
-        (ulow, uown, uhigh),
-        (vlow, vown, vhigh),
-        w,
-        diag,
-        left,
-        cown,
-        cmsg,
-        images,
-        ext,
-        coef,
-        out,
-        sem,
-    )
-
-
-def final_second(
-    begun,
-    w,
-    ulow,
-    uown,
-    uhigh,
-    vlow,
-    vown,
-    vhigh,
-    diag,
-    left,
-    cown,
-    cmsg,
-    aux,
-    images,
-    ext,
-    coef,
-    out,
-    sem,
-):
-    rows3 = aux[0:1, :], [aux[2 + at:3 + at, :] for at in range(3)], aux[1:2, :]
-    apply_second(
-        1,
-        rows3,
-        (ulow, uown, uhigh),
-        (vlow, vown, vhigh),
-        w,
-        diag,
-        left,
-        cown,
-        cmsg,
-        images,
-        ext,
-        coef,
-        out,
-        sem,
-    )
+    copies = []
+    for o in range(ops):
+        copies += apply_second(
+            o,
+            found[o],
+            (ulow, uown, uhigh),
+            (vlow, vown, vhigh),
+            w,
+            diag,
+            left,
+            cown,
+            cmsg,
+            images,
+            ext,
+            coef,
+            out,
+            sem,
+        )
+    for copy in copies:
+        copy.wait()
 
 
 def ring(block):
@@ -537,7 +495,7 @@
     rows, columns = sources.shape
     all_blocks = blocks * n
     count = n // SLICES
-    groups = [[g * SLICES + s for s in range(SLICES)] for g in range(count)]
+    groups = [[s * count + g for s in range(SLICES)] for g in range(count)]
     sds = jax.ShapeDtypeStruct
     body = ops * rank
 
@@ -547,111 +505,92 @@
     def across(x):
         parts = [x]
         for m in range(1, count):
-            pairs = [(i, (i + m * SLICES) % n) for i in range(n)]
+            pairs = [(i, i - i % count + (i + m) % count) for i in range(n)]
             parts.append(lax.ppermute(x, "store", pairs))
         return parts
 
     place = lax.axis_index("store").astype(jnp.int32)
     row0 = (place * blocks).reshape(1)
-    group = lax.div(place, jnp.int32(SLICES)).reshape(1)
+    group = lax.rem(place, jnp.int32(count)).reshape(1)
     left = jnp.transpose(basis_left, (0, 2, 1))
     right = jnp.transpose(basis_right, (0, 2, 1))
 
-    low, high = ring(sources)
     shared = (blocks + 1) * body
     lead = shared + STATS + rank
-    z1, packed = call(
-        coeff_kernel,
-        [sds((SLICES, rank, LANES), BF16), sds((lead, LANES), BF16)],
+    mine, own = call(
+        functools.partial(coeff_kernel, count),
+        [sds((SLICES, lead + rank, LANES), BF16), sds(sources.shape, BF16)],
         [SMEM] + [VMEM] * 4,
         megabytes=60,
     )(far_cols, sources, left, right, couplings)
-    z1 = across(z1)
-    held = call(
-        share_kernel,
-        sds((SLICES, lead + count * rank, LANES), BF16),
-        [VMEM, ANY, ANY] + [VMEM] * count,
-        megabytes=60,
-    )(packed, low, high, *z1)
-    held = exchange(held)
+    low, high = ring(own)
+    held = exchange(mine)
     cols = held[:, shared, :blocks * far].astype(jnp.int32).reshape(-1)
 
     w = call(
         functools.partial(order_tiles, all_blocks),
         sds((blocks, ops * size, near * size), BF16),
-        [SMEM, SMEM, SMEM, VMEM],
-        micros=2.5,
-    )(near_cols, near_count, row0, near_tiles)
-
-    c1, mixed = call(
-        functools.partial(first_couple, ops, rank, far),
-        [sds((SLICES, body, LANES), BF16), sds((SLICES, body, LANES), F32)],
-        [SMEM, SMEM, VMEM],
-        [pltpu.VMEM((n * blocks * rank, LANES), BF16)],
-    )(cols, group, held)
-
-    image, edge, msg = call(
+        [SMEM, SMEM, SMEM, VMEM, ANY],
+        megabytes=60,
+    )(near_cols, near_count, row0, near_tiles, mine)
+    image, edge, late = call(
         near_kernel,
         [
             sds((ops, rows, columns), F32),
             sds((STATS, columns), BF16),
-            sds((SLICES, 2 * body + STATS, LANES), BF16),
+            sds((SLICES, body + STATS, LANES), BF16),
         ],
-        [VMEM] * 7,
-        micros=4.0,
-    )(w, low, sources, high, self_terms, right, c1)
+        [VMEM] * 6,
+        micros=10.0,
+        megabytes=60,
+    )(w, low, sources, high, self_terms, right)
+
+    z1 = across(call(take_kernel, sds((SLICES, rank, LANES), BF16), [VMEM, ANY])(held, edge))
+    msg, mixed = call(
+        functools.partial(first_couple, ops, rank, far),
+        [sds((SLICES, 2 * body + STATS, LANES), BF16), sds((SLICES, body, LANES), F32)],
+        [SMEM, SMEM] + [VMEM] * (2 + count),
+        [pltpu.VMEM((n * blocks * rank, LANES), BF16)],
+    )(cols, group, held, late, *z1)
     got = exchange(msg)
 
-    first, second, cown, xmsg = call(
+    v, cown, xmsg = call(
         image_kernel,
         [
-            sds((rows + STATS, columns), BF16),
-            sds((rows, columns), BF16),
+            sds((ops * rows + STATS, columns), BF16),
             sds((ops * blocks * rank, columns), BF16),
             sds((SLICES * (body + STATS) + columns // LANES * STATS, LANES), BF16),
         ],
         [VMEM] * 6,
         [pltpu.VMEM((rows, columns), F32), pltpu.VMEM((blocks, body, columns), BF16)],
-        micros=3.0,
+        micros=2.0,
     )(sources, image, edge, left, got, mixed)
     parts = across(xmsg)
-    low0, high0 = ring(first)
-    low1, high1 = ring(second)
+    vlow, vhigh = ring(v)
 
     panels = all_blocks * size
     c2 = call(
         functools.partial(second_couple, panels, ops, rank, far),
         sds((SLICES, body + STATS + count * columns // LANES * STATS, LANES), BF16),
-        [SMEM, SMEM] + [VMEM] * (1 + count),
+        [SMEM, SMEM] + [VMEM] * (1 + 2 * count),
         [pltpu.VMEM((ops, n * blocks * rank, LANES), BF16)],
-    )(cols, group, held, *parts)
+        micros=30.0,
+    )(cols, group, held, *z1, *parts)
     c2 = exchange(c2)
 
-    outs = sds((ops, rows, columns), F32)
-    scratch = [
-        pltpu.VMEM((3, rows, columns), BF16),
-        pltpu.VMEM((blocks, body, columns), BF16),
-        pltpu.VMEM((rows, columns), F32),
-    ]
-    images, heights, norms, aux = call(
-        functools.partial(final_first, panels),
-        [outs, sds((ops, columns), F32), sds((ops, columns), F32), sds((8, columns), F32)],
+    images, heights, norms = call(
+        functools.partial(final_kernel, panels),
+        [sds((ops, rows, columns), F32), sds((ops, columns), F32), sds((ops, columns), F32)],
         [SMEM] + [VMEM] * 11,
-        scratch + [pltpu.VMEM((n, STATS, columns), F32), pltpu.SemaphoreType.DMA((blocks,))],
-        micros=4.0,
-        megabytes=60,
-        out_specs=[ANY, VMEM, VMEM, VMEM],
-    )(group, w, low, sources, high, low0, first, high0, self_terms, left, cown, c2)
-    images = call(
-        final_second,
-        outs,
-        [ANY] + [VMEM] * 12,
-        scratch + [pltpu.SemaphoreType.DMA((blocks,))],
-        micros=4.0,
-        megabytes=60,
-        out_specs=ANY,
-        alias={0: 0},
-    )(images, w, low, sources, high, low1, second, high1, self_terms, left, cown, c2, aux)
+        [
+            pltpu.VMEM((3, rows, columns), BF16),
+            pltpu.VMEM((blocks, body, columns), BF16),
+            pltpu.VMEM((ops, rows, columns), F32),
+            pltpu.VMEM((n, STATS, columns), F32),
+            pltpu.SemaphoreType.DMA((ops, blocks)),
+        ],
+        out_specs=[ANY, VMEM, VMEM],
+    )(group, w, low, sources, high, vlow, v, vhigh, self_terms, left, cown, c2)
     return images, heights, norms
 
 

time: 110 us -> 90.7 us (0.82)
  the two profiles are of different devices: /device:TPU:1 before, /device:TPU:0 now
where the time goes in v17:
time: 90.7 us; the launch traced here: 90.3 us
  blocking collectives  45.5 us (50%)
  Pallas kernels  21.1 us (23%)
  starting transfers between devices  11.8 us (13%)
  waiting for transfers between devices  7.03 us (8%)
  local copies, waits for them, and re-layouts  4.16 us (5%)
    all_to_all x2, blocking collectives, exchange(): lax.all_to_all(x, 'store', 0, 0, axis_index_groups=groups, tiled=True)  45.5 us
    ppermute x2, starting transfers between devices, ring(): lax.ppermute(block, 'store', backward)  7.11 us
    ppermute x2, waiting for transfers between devices, ring(): lax.ppermute(block, 'store', forward)  5.74 us
    pallas_call x1, Pallas kernels, shards(): call(near_kernel, [sds((ops, rows, columns), F32), sds((STATS, columns),...  5.48 us
    pallas_call x1, Pallas kernels, shards(): call(functools.partial(final_kernel, panels), [sds((ops, rows, columns),...  4.36 us
    unnamed x24, local copies, waits for them, and re-layouts  4.08 us
    all_to_all x1, starting transfers between devices, exchange(): lax.all_to_all(x, 'store', 0, 0, axis_index_groups=groups, tiled=True)  3.54 us
    pallas_call x1, Pallas kernels, shards(): call(functools.partial(order_tiles, all_blocks), sds((blocks, ops * size,...  3.43 us
  transfers between devices with their start and end apart: 7, of which 3 were waited for; matrix products, arithmetic and copies ran while one was open for 0% of the time, Pallas kernels for 12%

profile of v17, /device:TPU:0, one launch (start us, length us, event | category | flops | bytes accessed | tf_op | source)
XLA Modules:
  0.0 90.3 jit_solution(16627938405978958989)
XLA Ops:
  0.6 2.4 %shard_map.112 = (bf16[8,272,128]{2,1,0:T(8,128)(2,1)}, bf16[512,512]{1,0:T(8,128)(2,1)}) custom-call(s32[2,6]{1,0:T(2,128)} %far_cols.1, bf16[512,512]{1,0:T(8,128)(2,1)} %uown.1, bf16[2,32,256]{2,1,0:T(8,128)(2,1)} %bitcast.4, bf16[2,32,256]{2,1,0:T(8,128)(2,1)} %bitcast.7, bf16[2,2,6,32,32]{4,3,2,1,0:T(8,128)(2,1)} %coup.1), custom_call_target="tpu_custom_call" | custom-call | tf_op jit(solution)/shard_map/pallas_call | solution.py:520
  3.0 5.4 %collective-permute-start.1 = (bf16[512,512]{1,0:T(8,128)(2,1)}, bf16[512,512]{1,0:T(8,128)(2,1)S(1)}, u32[]{:S(2)}, u32[]{:S(2)}) collective-permute-start(bf16[512,512]{1,0:T(8,128)(2,1)} %get-tuple-element.14), channel_id=1, source_target_pairs={{1,0},{2,1},{3,2},{4,3},{5,4},{6,5},{7,6},{8,7},{9,8},{10,9},{11,1... | collective-permute-start | bytes 1572872 | tf_op jit(solution)/shard_map/ppermute | solution.py:477
  8.5 0.0 collective-permute-start
  8.5 3.5 %all-to-all-start = ((bf16[8,272,128]{2,1,0:T(8,128)(2,1)}), bf16[8,272,128]{2,1,0:T(8,128)(2,1)S(1)}, u32[]{:S(2)}, u32[]{:S(2)}) async-start(bf16[8,272,128]{2,1,0:T(8,128)(2,1)} %get-tuple-element.13.after), calls=%async_computation | async-start | bytes 1114112 | tf_op jit(solution)/shard_map/all_to_all | solution.py:503
  12.0 3.4 %shard_map.113.w = bf16[2,512,1280]{2,1,0:T(8,128)(2,1)} custom-call(s32[2,5]{1,0:T(2,128)} %cols.1, s32[2]{0:T(128)} %count.1, s32[1]{0:T(128)} %bitcast.1.row0, bf16[2,2,5,256,256]{4,3,2,1,0:T(8,128)(2,1)} %tiles.1, bf16[8,272,128]{2,1,0:T(8,128)(2,1)} %get-tuple-element.13.after), custom_call_target="tpu_custom_call" | custom-call | tf_op jit(solution)/shard_map/pallas_call | solution.py:530
  15.5 0.5 collective-permute-done.1.high.uhigh
  15.9 0.0 copy-start.2
  15.9 5.7 %collective-permute-done.low.ulow = bf16[512,512]{1,0:T(8,128)(2,1)S(1)} collective-permute-done((bf16[512,512]{1,0:T(8,128)(2,1)}, bf16[512,512]{1,0:T(8,128)(2,1)S(1)}, u32[]{:S(2)}, u32[]{:S(2)}) %collective-permute-start) | collective-permute-done | bytes 524320 | tf_op jit(solution)/shard_map/ppermute | solution.py:477
  21.7 0.0 copy-done.2
  21.7 0.0 copy-start.4
  21.7 0.8 copy-done.4
  22.5 5.5 %shard_map.114 = (f32[2,512,512]{2,1,0:T(8,128)}, bf16[16,512]{1,0:T(8,128)(2,1)}, bf16[8,80,128]{2,1,0:T(8,128)(2,1)}) custom-call(bf16[2,512,1280]{2,1,0:T(8,128)(2,1)} %shard_map.113.w, bf16[512,512]{1,0:T(8,128)(2,1)} %copy-done.4, bf16[512,512]{1,0:T(8,128)(2,1)} %uown.1, bf16[512,512]{1,0:T(8,128)(2,1)} %copy-done.2, f32[2,512]{1,0:T(2,128)} %diag.3, ...), custom_call_target="tpu_custom_call" | custom-call | flops 11500000256 | tf_op jit(solution)/shard_map/pallas_call | solution.py:536
  27.9 0.0 copy-start.1
  27.9 0.0 copy-start.7
  27.9 0.0 all-to-all-done.held
  28.0 0.0 copy-start.8
  28.0 0.8 copy-done.8
  28.7 0.0 copy-start.9
  28.7 1.0 %collective-permute-start.2 = (bf16[8,32,128]{2,1,0:T(8,128)(2,1)S(1)}, bf16[8,32,128]{2,1,0:T(8,128)(2,1)S(1)}, u32[]{:S(2)}, u32[]{:S(2)}) collective-permute-start(bf16[8,32,128]{2,1,0:T(8,128)(2,1)S(1)} %shard_map.115.refs_0_), channel_id=1, source_target_pairs={{0,1},{1,0},{2,3},{3,2},{4,5},{5,4},{6,7},{7,6},{8,9},{9,8},{10,11... | collective-permute-start | bytes 196616 | tf_op jit(solution)/shard_map/ppermute | solution.py:509
  29.8 0.1 reshape.18.cols
  29.9 0.8 collective-permute-done.2.refs_1_
  30.7 0.0 copy-start.6
  30.7 0.9 %copy-done.6 = bf16[8,80,128]{2,1,0:T(8,128)(2,1)S(1)} copy-done((bf16[8,80,128]{2,1,0:T(8,128)(2,1)S(1)}, bf16[8,80,128]{2,1,0:T(8,128)(2,1)}, u32[]{:S(2)}) %copy-start.6) | copy-done | bytes 163864
  31.6 2.7 %shard_map.116 = (bf16[8,144,128]{2,1,0:T(8,128)(2,1)S(1)}, f32[8,64,128]{2,1,0:T(8,128)S(1)}) custom-call(s32[96]{0:T(128)S(1)} %reshape.18.cols, s32[1]{0:T(128)} %bitcast.group, bf16[8,272,128]{2,1,0:T(8,128)(2,1)S(1)} %all-to-all-done.held, bf16[8,80,128]{2,1,0:T(8,128)(2,1)S(1)} %copy-done.6, bf16[8,32,128]{2,1,0:T(8,128)(2,1)S(1)} %shard_map.115.refs_0_, ...), custom_call_target="tpu_custom_call" | custom-call | tf_op jit(solution)/shard_map/pallas_call | solution.py:549
  34.3 17.7 %all_to_all.15.got = bf16[8,144,128]{2,1,0:T(8,128)(2,1)S(1)} all-to-all(bf16[8,144,128]{2,1,0:T(8,128)(2,1)S(1)} %get-tuple-element.18), channel_id=1, replica_groups={{0,2,4,6,8,10,12,14},{1,3,5,7,9,11,13,15},{16,18,20,22,24,26,28,30},{17..., dimensions={0} | all-to-all | bytes 589824 | tf_op jit(solution)/shard_map/all_to_all | solution.py:503
  52.0 0.0 copy-done.1
  52.0 0.0 copy-done.7
  52.0 0.0 copy-done.9
  52.0 0.0 copy-start.11
  52.0 1.6 %copy-done.11 = f32[2,512,512]{2,1,0:T(8,128)S(1)} copy-done((f32[2,512,512]{2,1,0:T(8,128)S(1)}, f32[2,512,512]{2,1,0:T(8,128)}, u32[]{:S(2)}) %copy-start.11) | copy-done | bytes 2097176
  53.6 1.2 %shard_map.117 = (bf16[1040,512]{1,0:T(8,128)(2,1)S(1)}, bf16[128,512]{1,0:T(8,128)(2,1)S(1)}, bf16[704,128]{1,0:T(8,128)(2,1)S(1)}) custom-call(bf16[512,512]{1,0:T(8,128)(2,1)S(1)} %copy-done.1, f32[2,512,512]{2,1,0:T(8,128)S(1)} %copy-done.11, bf16[16,512]{1,0:T(8,128)(2,1)S(1)} %copy-done.9, bf16[2,32,256]{2,1,0:T(8,128)(2,1)S(1)} %bitcast.5, ...), custom_call_target="tpu_custom_call" | custom-call | flops 2300000000 | tf_op jit(solution)/shard_map/pallas_call | solution.py:557
  54.8 0.1 collective-permute-start.5
  54.9 0.0 copy-start.3
  54.9 0.0 copy-start.5
  54.9 0.0 copy-start.10
  54.9 1.7 %collective-permute-start.4 = (bf16[1040,512]{1,0:T(8,128)(2,1)S(1)}, bf16[1040,512]{1,0:T(8,128)(2,1)S(1)}, u32[]{:S(2)}, u32[]{:S(2)}) collective-permute-start(bf16[1040,512]{1,0:T(8,128)(2,1)S(1)} %get-tuple-element.20.vown), channel_id=1, source_target_pairs={{1,0},{2,1},{3,2},{4,3},{5,4},{6,5},{7,6},{8,7},{9,8},{10,9},{11,1... | collective-permute-start | bytes 3194888 | tf_op jit(solution)/shard_map/ppermute | solution.py:477
  56.6 0.0 collective-permute-start.3
  56.6 0.0 collective-permute-done.5.refs_3_
  56.6 0.0 copy-start
  56.6 1.5 %shard_map.118 = bf16[8,208,128]{2,1,0:T(8,128)(2,1)S(1)} custom-call(s32[96]{0:T(128)S(1)} %reshape.18.cols, s32[1]{0:T(128)} %bitcast.group, bf16[8,272,128]{2,1,0:T(8,128)(2,1)S(1)} %all-to-all-done.held, bf16[8,32,128]{2,1,0:T(8,128)(2,1)S(1)} %shard_map.115.refs_0_, bf16[8,32,128]{2,1,0:T(8,128)(2,1)S(1)} %collective-permute-done.2.refs_1_, ...), custom_call_target="tpu_custom_call" | custom-call | flops 34500001792 | tf_op jit(solution)/shard_map/pallas_call | solution.py:572
  58.1 27.8 %all_to_all.16.cmsg = bf16[8,208,128]{2,1,0:T(8,128)(2,1)S(1)} all-to-all(bf16[8,208,128]{2,1,0:T(8,128)(2,1)S(1)} %shard_map.118), channel_id=1, replica_groups={{0,2,4,6,8,10,12,14},{1,3,5,7,9,11,13,15},{16,18,20,22,24,26,28,30},{17..., dimensions={0} | all-to-all | bytes 851968 | tf_op jit(solution)/shard_map/all_to_all | solution.py:503
  85.9 0.0 collective-permute-done.4.vhigh
  85.9 0.0 collective-permute-done.3.vlow
  85.9 0.0 copy-done.3
  85.9 0.0 copy-done.5
  85.9 0.0 copy-done.10
  86.0 0.0 copy-done
  86.0 4.4 %shard_map.119 = (f32[2,512,512]{2,1,0:T(8,128)}, f32[2,512]{1,0:T(2,128)}, f32[2,512]{1,0:T(2,128)}) custom-call(s32[1]{0:T(128)} %bitcast.group, bf16[2,512,1280]{2,1,0:T(8,128)(2,1)S(1)} %copy-done, bf16[512,512]{1,0:T(8,128)(2,1)S(1)} %copy-done.5, bf16[512,512]{1,0:T(8,128)(2,1)S(1)} %copy-done.1, bf16[512,512]{1,0:T(8,128)(2,1)S(1)} %copy-done.3, ...), custom_call_target="tpu_custom_call" | custom-call | tf_op jit(solution)/shard_map/pallas_call | solution.py:581
  (2 shorter events, 0.0 us)
Async XLA Ops:
  3.0 12.9 %collective-permute-start.1 = (bf16[512,512]{1,0:T(8,128)(2,1)}, bf16[512,512]{1,0:T(8,128)(2,1)S(1)}, u32[]{:S(2)}, u32[]{:S(2)}) collective-permute-start(bf16[512,512]{1,0:T(8,128)(2,1)} %get-tuple-element.14), channel_id=1, source_target_pairs={{1,0},{2,1},{3,2},{4,3},{5,4},{6,5},{7,6},{8,7},{9,8},{10,9},{11,1... | collective-permute-start | bytes 1572872 | tf_op jit(solution)/shard_map/ppermute | solution.py:477
  8.5 13.2 %collective-permute-start = (bf16[512,512]{1,0:T(8,128)(2,1)}, bf16[512,512]{1,0:T(8,128)(2,1)S(1)}, u32[]{:S(2)}, u32[]{:S(2)}) collective-permute-start(bf16[512,512]{1,0:T(8,128)(2,1)} %get-tuple-element.14), channel_id=1, source_target_pairs={{0,1},{1,2},{2,3},{3,4},{4,5},{5,6},{6,7},{7,8},{8,9},{9,10},{10,1... | collective-permute-start | bytes 1572872 | tf_op jit(solution)/shard_map/ppermute | solution.py:477
  8.5 19.5 %all-to-all-start = ((bf16[8,272,128]{2,1,0:T(8,128)(2,1)}), bf16[8,272,128]{2,1,0:T(8,128)(2,1)S(1)}, u32[]{:S(2)}, u32[]{:S(2)}) async-start(bf16[8,272,128]{2,1,0:T(8,128)(2,1)} %get-tuple-element.13.after), calls=%async_computation | async-start | bytes 1114112 | tf_op jit(solution)/shard_map/all_to_all | solution.py:503
  15.9 5.7 %copy-start.2 = (bf16[512,512]{1,0:T(8,128)(2,1)}, bf16[512,512]{1,0:T(8,128)(2,1)S(1)}, u32[]{:S(2)}) copy-start(bf16[512,512]{1,0:T(8,128)(2,1)S(1)} %collective-permute-done.1.high.uhigh) | copy-start | bytes 1572868
  21.7 0.8 copy-start.4
  27.9 24.0 %copy-start.1 = (bf16[512,512]{1,0:T(8,128)(2,1)S(1)}, bf16[512,512]{1,0:T(8,128)(2,1)}, u32[]{:S(2)}) copy-start(bf16[512,512]{1,0:T(8,128)(2,1)} %uown.1) | copy-start | bytes 1572868
  27.9 24.0 %copy-start.7 = (bf16[2,256,32]{1,2,0:T(8,128)(2,1)S(1)}, bf16[2,256,32]{1,2,0:T(8,128)(2,1)}, u32[]{:S(2)}) copy-start(bf16[2,256,32]{1,2,0:T(8,128)(2,1)} %param.15) | copy-start | bytes 98308
  28.0 0.8 copy-start.8
  28.7 23.2 %copy-start.9 = (bf16[16,512]{1,0:T(8,128)(2,1)S(1)}, bf16[16,512]{1,0:T(8,128)(2,1)}, u32[]{:S(2)}) copy-start(bf16[16,512]{1,0:T(8,128)(2,1)} %get-tuple-element.16.after.edge) | copy-start | bytes 49156
  28.7 1.9 %collective-permute-start.2 = (bf16[8,32,128]{2,1,0:T(8,128)(2,1)S(1)}, bf16[8,32,128]{2,1,0:T(8,128)(2,1)S(1)}, u32[]{:S(2)}, u32[]{:S(2)}) collective-permute-start(bf16[8,32,128]{2,1,0:T(8,128)(2,1)S(1)} %shard_map.115.refs_0_), channel_id=1, source_target_pairs={{0,1},{1,0},{2,3},{3,2},{4,5},{5,4},{6,7},{7,6},{8,9},{9,8},{10,11... | collective-permute-start | bytes 196616 | tf_op jit(solution)/shard_map/ppermute | solution.py:509
  30.7 0.9 %copy-start.6 = (bf16[8,80,128]{2,1,0:T(8,128)(2,1)S(1)}, bf16[8,80,128]{2,1,0:T(8,128)(2,1)}, u32[]{:S(2)}) copy-start(bf16[8,80,128]{2,1,0:T(8,128)(2,1)} %get-tuple-element.17.late) | copy-start | bytes 491524
  52.0 1.6 %copy-start.11 = (f32[2,512,512]{2,1,0:T(8,128)S(1)}, f32[2,512,512]{2,1,0:T(8,128)}, u32[]{:S(2)}) copy-start(f32[2,512,512]{2,1,0:T(8,128)} %get-tuple-element.15.near) | copy-start | bytes 6291460
  54.8 1.8 %collective-permute-start.5 = (bf16[704,128]{1,0:T(8,128)(2,1)S(1)}, bf16[704,128]{1,0:T(8,128)(2,1)S(1)}, u32[]{:S(2)}, u32[]{:S(2)}) collective-permute-start(bf16[704,128]{1,0:T(8,128)(2,1)S(1)} %get-tuple-element.22.refs_2_), channel_id=1, source_target_pairs={{0,1},{1,0},{2,3},{3,2},{4,5},{5,4},{6,7},{7,6},{8,9},{9,8},{10,11... | collective-permute-start | bytes 540680 | tf_op jit(solution)/shard_map/ppermute | solution.py:509
  54.9 31.1 %copy-start.3 = (bf16[512,512]{1,0:T(8,128)(2,1)S(1)}, bf16[512,512]{1,0:T(8,128)(2,1)}, u32[]{:S(2)}) copy-start(bf16[512,512]{1,0:T(8,128)(2,1)} %copy-done.2) | copy-start | bytes 1572868
  54.9 31.1 %copy-start.5 = (bf16[512,512]{1,0:T(8,128)(2,1)S(1)}, bf16[512,512]{1,0:T(8,128)(2,1)}, u32[]{:S(2)}) copy-start(bf16[512,512]{1,0:T(8,128)(2,1)} %copy-done.4) | copy-start | bytes 1572868
  54.9 31.1 %copy-start.10 = (f32[2,512]{1,0:T(2,128)S(1)}, f32[2,512]{1,0:T(2,128)}, u32[]{:S(2)}) copy-start(f32[2,512]{1,0:T(2,128)} %diag.3) | copy-start | bytes 12292
  54.9 31.0 %collective-permute-start.4 = (bf16[1040,512]{1,0:T(8,128)(2,1)S(1)}, bf16[1040,512]{1,0:T(8,128)(2,1)S(1)}, u32[]{:S(2)}, u32[]{:S(2)}) collective-permute-start(bf16[1040,512]{1,0:T(8,128)(2,1)S(1)} %get-tuple-element.20.vown), channel_id=1, source_target_pairs={{1,0},{2,1},{3,2},{4,3},{5,4},{6,5},{7,6},{8,7},{9,8},{10,9},{11,1... | collective-permute-start | bytes 3194888 | tf_op jit(solution)/shard_map/ppermute | solution.py:477
  56.6 29.4 %collective-permute-start.3 = (bf16[1040,512]{1,0:T(8,128)(2,1)S(1)}, bf16[1040,512]{1,0:T(8,128)(2,1)S(1)}, u32[]{:S(2)}, u32[]{:S(2)}) collective-permute-start(bf16[1040,512]{1,0:T(8,128)(2,1)S(1)} %get-tuple-element.20.vown), channel_id=1, source_target_pairs={{0,1},{1,2},{2,3},{3,4},{4,5},{5,6},{6,7},{7,8},{8,9},{9,10},{10,1... | collective-permute-start | bytes 3194888 | tf_op jit(solution)/shard_map/ppermute | solution.py:477
  56.6 29.4 %copy-start = (bf16[2,512,1280]{2,1,0:T(8,128)(2,1)S(1)}, bf16[2,512,1280]{2,1,0:T(8,128)(2,1)}, u32[]{:S(2)}) copy-start(bf16[2,512,1280]{2,1,0:T(8,128)(2,1)} %shard_map.113.w) | copy-start | bytes 7864324

commit v18 on v16

--- a/solution.py
+++ b/solution.py
@@ -86,14 +86,16 @@
                 )
 
 
-def coeff_kernel(count, far_cols, u, right, coup, z_out, out):
+def coeff_kernel(count, far_cols, u, right, coup, out, u_out):
     ops, blocks, far, rank, _ = coup.shape
     size = right.shape[2]
+    u_out[...] = u[...]
     z = [dot(right[b], u[b * size:(b + 1) * size, :]) for b in range(blocks)]
+    at = 3 * ops * rank + STATS
     for pair in range(SLICES // 2):
         first, second = halves(chunk(z[0], pair), chunk(z[1], pair))
-        z_out[2 * pair] = first.astype(BF16)
-        z_out[2 * pair + 1] = second.astype(BF16)
+        out[2 * pair, at:at + rank, :] = first.astype(BF16)
+        out[2 * pair + 1, at:at + rank, :] = second.astype(BF16)
     whole, rest = [], []
     for b in range(blocks):
         tiles = [
@@ -111,19 +113,15 @@
             slot = lax.rem(device, count) * SLICES + lax.div(device, count)
             name = (slot * blocks + lax.rem(col, blocks)).astype(F32)
             names = jnp.where(lane == b * far + f, name, names)
-    out[...] = jnp.concatenate(
+    whole = jnp.concatenate(
         whole + [jnp.concatenate(rest, axis=1), names.astype(BF16)], axis=0
     )
-
-
-def share_kernel(packed, *refs):
-    parts, out = refs[:-1], refs[-1]
-    rows = packed.shape[0]
-    rank = parts[0].shape[1]
     for s in range(SLICES):
-        out[s, 0:rows, :] = packed[...]
-    for m, part in enumerate(parts):
-        out[:, rows + m * rank:rows + (m + 1) * rank, :] = part[...]
+        out[s, 0:at, :] = whole
+
+
+def take_kernel(held, after, out):
+    out[...] = held[:, held.shape[1] - out.shape[1]:, :]
 
 
 def coupling_rows(held, s, b, ops, rank):
@@ -154,21 +152,16 @@
     return both.reshape(count * 2 * rank, LANES).astype(BF16)
 
 
-def held_part(held, m, ops, rank):
-    at = 3 * ops * rank + STATS + m * rank
-    return held[:, at:at + rank, :].astype(F32)
-
-
 def group_at(group, m, groups, step):
     return pl.multiple_of(lax.rem(group[0] + (groups - m), groups) * step, step)
 
 
-def first_couple(ops, rank, far, cols, group, after, held, out, zs):
+def first_couple(ops, rank, far, cols, group, held, *refs):
+    parts, (out, zs) = refs[:-2], refs[-2:]
     step = SLICES * 2 * rank
-    count = zs.shape[0] // step
-    for m in range(count):
-        at = group_at(group, m, count, step)
-        zs[pl.ds(at, step), :] = spread_rows(held_part(held, m, ops, rank), rank)
+    for m, part in enumerate(parts):
+        at = group_at(group, m, len(parts), step)
+        zs[pl.ds(at, step), :] = spread_rows(part[...].astype(F32), rank)
     for s in range(SLICES):
         c = [couple(cols, held, s, b, ops, rank, far, [zs]) for b in range(2)]
         out[s] = halves(c[0], c[1])[0].astype(BF16)
@@ -276,8 +269,9 @@
 
 
 def second_couple(panels, ops, rank, far, cols, group, after_low, after_high, held, *refs):
-    msgs, (out, zs, st) = refs[:-3], refs[-3:]
-    count = len(msgs)
+    out, zs, st = refs[-3:]
+    count = (len(refs) - 3) // 2
+    z1, msgs = refs[:count], refs[count:2 * count]
     body = ops * rank
     step = SLICES * 2 * rank
     for m, msg in enumerate(msgs):
@@ -299,7 +293,7 @@
     for m, msg in enumerate(msgs):
         at = group_at(group, m, count, step)
         mine = msg[:, body:body + STATS, :].astype(F32)
-        base = held_part(held, m, ops, rank)
+        base = z1[m][...].astype(F32)
         for o in range(ops):
             delta = join3(mine, o) - heights[o]
             z = msg[:, o * rank:(o + 1) * rank, :].astype(F32) + delta[:, None, :] * base
@@ -462,21 +456,14 @@
     left = jnp.transpose(basis_left, (0, 2, 1))
     right = jnp.transpose(basis_right, (0, 2, 1))
 
-    low, high = ring(sources)
     shared = (blocks + 1) * body
-    z1, packed = call(
+    mine, own = call(
         functools.partial(coeff_kernel, count),
-        [sds((SLICES, rank, LANES), BF16), sds((shared + STATS, LANES), BF16)],
-        [SMEM, VMEM, VMEM, VMEM],
+        [sds((SLICES, shared + STATS + rank, LANES), BF16), sds(sources.shape, BF16)],
+        [SMEM] + [VMEM] * 3,
         megabytes=60,
     )(far_cols, sources, right, couplings)
-    z1 = across(z1)
-    mine = call(
-        share_kernel,
-        sds((SLICES, shared + STATS + count * rank, LANES), BF16),
-        [VMEM] * (1 + count),
-        megabytes=60,
-    )(packed, *z1)
+    low, high = ring(own)
     held = exchange(mine)
     cols = held[:, shared, :blocks * far].astype(jnp.int32).reshape(-1)
 
@@ -491,15 +478,15 @@
         [sds((ops, rows, columns), F32), sds((8, LANES), F32)],
         [VMEM] * 5,
         micros=10.0,
-        megabytes=60,
     )(w, low, sources, high, self_terms)
+    z1 = across(call(take_kernel, sds((SLICES, rank, LANES), BF16), [VMEM, ANY])(held, token))
 
     c1 = call(
         functools.partial(first_couple, ops, rank, far),
         sds((SLICES, body, LANES), BF16),
-        [SMEM, SMEM, ANY, VMEM],
+        [SMEM, SMEM] + [VMEM] * (1 + count),
         [pltpu.VMEM((n * blocks * rank, LANES), BF16)],
-    )(cols, group, token, held)
+    )(cols, group, held, *z1)
     c1 = exchange(c1)
 
     first, second, msg = call(
@@ -523,13 +510,13 @@
     c2 = call(
         functools.partial(second_couple, all_blocks * size, ops, rank, far),
         sds((SLICES, body + STATS, LANES), BF16),
-        [SMEM, SMEM, ANY, ANY] + [VMEM] * (1 + count),
+        [SMEM, SMEM, ANY, ANY] + [VMEM] * (1 + 2 * count),
         [
             pltpu.VMEM((ops, n * blocks * rank, LANES), BF16),
             pltpu.VMEM((n, STATS, LANES), F32),
         ],
         micros=30.0,
-    )(cols, group, low0, high0, held, *msgs)
+    )(cols, group, low0, high0, held, *z1, *msgs)
     c2 = exchange(c2)
 
     outs = sds((ops, rows, columns), F32)

time: 86.7 us -> 83 us (0.957)
  Pallas kernels: 21.4 us -> 16.6 us
  blocking collectives: 38.6 us -> 40.8 us
  starting transfers between devices: 13.8 us -> 12.7 us
    ppermute x3, waiting for transfers between devices: 0.01 us -> 5.74 us  [ring(): lax.ppermute(block, 'store', forward)]
    all_to_all x1, waiting for transfers between devices: 5.71 us -> 0.01 us  [exchange(): lax.all_to_all(x, 'store', 0, 0, axis_index_groups=groups, tiled=True)]
    pallas_call x1, Pallas kernels: 4.99 us -> 1.52 us  [shards(): call(near_kernel, [sds((ops, rows, columns), F32), sds((8, LANES), F32)],...]
    all_to_all x1, starting transfers between devices: 5.76 us -> 3.48 us  [exchange(): lax.all_to_all(x, 'store', 0, 0, axis_index_groups=groups, tiled=True)]
    all_to_all x3, blocking collectives: 38.6 us -> 40.8 us  [exchange(): lax.all_to_all(x, 'store', 0, 0, axis_index_groups=groups, tiled=True)]
    pallas_call x2, Pallas kernels: 3.79 us -> 2.34 us  [the longest x1 2.33 us: shards(): call(functools.partial(coeff_kernel, count), [sds((SLICES, shared + STATS...]
    ppermute x2, starting transfers between devices: 0.01 us -> 0.91 us  [across(): parts.append(lax.ppermute(x, 'store', pairs))]
    unnamed x24 -> x16, local copies, waits for them, and re-layouts: 4.47 us -> 4.68 us
  transfers between devices with their start and end apart: 9 -> 9, of which waited for: 2 -> 3; matrix products, arithmetic and copies ran while one was open for 0% -> 0% of each run, Pallas kernels for 19% -> 11%
where the time goes in v18:
time: 83 us; the launch traced here: 82.6 us
  blocking collectives  40.8 us (49%)
  Pallas kernels  16.6 us (20%)
  starting transfers between devices  12.7 us (15%)
  waiting for transfers between devices  6.99 us (8%)
  local copies, waits for them, and re-layouts  4.76 us (6%)
    all_to_all x3, blocking collectives, exchange(): lax.all_to_all(x, 'store', 0, 0, axis_index_groups=groups, tiled=True)  40.8 us
    ppermute x3, starting transfers between devices, ring(): lax.ppermute(block, 'store', backward)  8.25 us
    ppermute x3, waiting for transfers between devices, ring(): lax.ppermute(block, 'store', forward)  5.74 us
    unnamed x16, local copies, waits for them, and re-layouts  4.68 us
    all_to_all x1, starting transfers between devices, exchange(): lax.all_to_all(x, 'store', 0, 0, axis_index_groups=groups, tiled=True)  3.48 us
    pallas_call x1, Pallas kernels, shards(): call(functools.partial(order_tiles, all_blocks), sds((blocks, ops * size,...  3.48 us
    pallas_call x1, Pallas kernels, shards(): call(final_first, [outs, sds((ops, columns), F32), sds((ops, columns), F3...  2.86 us
    pallas_call x1, Pallas kernels, shards(): call(functools.partial(coeff_kernel, count), [sds((SLICES, shared + STATS...  2.33 us
  transfers between devices with their start and end apart: 9, of which 3 were waited for; matrix products, arithmetic and copies ran while one was open for 0% of the time, Pallas kernels for 11%

profile of v18, /device:TPU:0, one launch (start us, length us, event | category | flops | bytes accessed | tf_op | source)
XLA Modules:
  0.0 82.6 jit_solution(6271636350584544550)
XLA Ops:
  0.6 2.3 %shard_map.112 = (bf16[8,240,128]{2,1,0:T(8,128)(2,1)}, bf16[512,512]{1,0:T(8,128)(2,1)}) custom-call(s32[2,6]{1,0:T(2,128)} %far_cols.1, bf16[512,512]{1,0:T(8,128)(2,1)} %uown.3, bf16[2,32,256]{2,1,0:T(8,128)(2,1)} %bitcast.7, bf16[2,2,6,32,32]{4,3,2,1,0:T(8,128)(2,1)} %coup.1), custom_call_target="tpu_custom_call" | custom-call | tf_op jit(solution)/shard_map/pallas_call | solution.py:460
  3.0 5.4 %collective-permute-start.1 = (bf16[512,512]{1,0:T(8,128)(2,1)}, bf16[512,512]{1,0:T(8,128)(2,1)S(1)}, u32[]{:S(2)}, u32[]{:S(2)}) collective-permute-start(bf16[512,512]{1,0:T(8,128)(2,1)} %get-tuple-element.15), channel_id=1, source_target_pairs={{1,0},{2,1},{3,2},{4,3},{5,4},{6,5},{7,6},{8,7},{9,8},{10,9},{11,1... | collective-permute-start | bytes 1572872 | tf_op jit(solution)/shard_map/ppermute | solution.py:418
  8.4 0.0 collective-permute-start
  8.4 3.5 %all-to-all-start = ((bf16[8,240,128]{2,1,0:T(8,128)(2,1)}), bf16[8,240,128]{2,1,0:T(8,128)(2,1)S(1)}, u32[]{:S(2)}, u32[]{:S(2)}) async-start(bf16[8,240,128]{2,1,0:T(8,128)(2,1)} %get-tuple-element.14.after), calls=%async_computation | async-start | bytes 983040 | tf_op jit(solution)/shard_map/all_to_all | solution.py:444
  11.9 0.0 copy-start.2
  11.9 0.0 copy-start.5
  11.9 0.0 copy-start.3
  11.9 0.0 copy-start.4
  12.0 3.5 %shard_map.113.w = bf16[2,512,1280]{2,1,0:T(8,128)(2,1)} custom-call(s32[2,5]{1,0:T(2,128)} %cols.1, s32[2]{0:T(128)} %count.1, s32[1]{0:T(128)} %bitcast.row0, bf16[2,2,5,256,256]{4,3,2,1,0:T(8,128)(2,1)} %tiles.1, bf16[8,240,128]{2,1,0:T(8,128)(2,1)} %get-tuple-element.14.after), custom_call_target="tpu_custom_call" | custom-call | tf_op jit(solution)/shard_map/pallas_call | solution.py:470
  15.4 0.4 collective-permute-done.1.high.uhigh
  15.9 5.7 %collective-permute-done.low.ulow = bf16[512,512]{1,0:T(8,128)(2,1)S(1)} collective-permute-done((bf16[512,512]{1,0:T(8,128)(2,1)}, bf16[512,512]{1,0:T(8,128)(2,1)S(1)}, u32[]{:S(2)}, u32[]{:S(2)}) %collective-permute-start) | collective-permute-done | bytes 524320 | tf_op jit(solution)/shard_map/ppermute | solution.py:418
  21.6 0.0 copy-done.2
  21.6 0.0 copy-done.5
  21.6 0.0 copy-start
  21.6 1.7 %copy-done = bf16[2,512,1280]{2,1,0:T(8,128)(2,1)S(1)} copy-done((bf16[2,512,1280]{2,1,0:T(8,128)(2,1)S(1)}, bf16[2,512,1280]{2,1,0:T(8,128)(2,1)}, u32[]{:S(2)}) %copy-start) | copy-done | bytes 2621464
  23.4 1.5 %shard_map.114 = (f32[2,512,512]{2,1,0:T(8,128)S(1)}, f32[8,128]{1,0:T(8,128)S(1)}) custom-call(bf16[2,512,1280]{2,1,0:T(8,128)(2,1)S(1)} %copy-done, bf16[512,512]{1,0:T(8,128)(2,1)S(1)} %collective-permute-done.low.ulow, bf16[512,512]{1,0:T(8,128)(2,1)S(1)} %copy-done.2, bf16[512,512]{1,0:T(8,128)(2,1)S(1)} %collective-permute-done.1.high.uhigh, ...), custom_call_target="tpu_custom_call" | custom-call | flops 11500000256 | tf_op jit(solution)/shard_map/pallas_call | solution.py:476
  24.9 0.0 copy-start.6
  24.9 1.3 %copy-done.6 = f32[2,512,512]{2,1,0:T(8,128)} copy-done((f32[2,512,512]{2,1,0:T(8,128)}, f32[2,512,512]{2,1,0:T(8,128)S(1)}, u32[]{:S(2)}) %copy-start.6) | copy-done | bytes 2097176
  26.2 0.0 all-to-all-done.held
  26.2 0.9 %collective-permute-start.2 = (bf16[8,32,128]{2,1,0:T(8,128)(2,1)S(1)}, bf16[8,32,128]{2,1,0:T(8,128)(2,1)S(1)}, u32[]{:S(2)}, u32[]{:S(2)}) collective-permute-start(bf16[8,32,128]{2,1,0:T(8,128)(2,1)S(1)} %shard_map.115.refs_0_), channel_id=1, source_target_pairs={{0,1},{1,0},{2,3},{3,2},{4,5},{5,4},{6,7},{7,6},{8,9},{9,8},{10,11... | collective-permute-start | bytes 196616 | tf_op jit(solution)/shard_map/ppermute | solution.py:450
  27.1 0.1 reshape.18.cols
  27.2 0.8 collective-permute-done.2.refs_1_
  28.0 1.1 %shard_map.116 = bf16[8,64,128]{2,1,0:T(8,128)(2,1)S(1)} custom-call(s32[96]{0:T(128)S(1)} %reshape.18.cols, s32[1]{0:T(128)} %bitcast.3.group, bf16[8,240,128]{2,1,0:T(8,128)(2,1)S(1)} %all-to-all-done.held, bf16[8,32,128]{2,1,0:T(8,128)(2,1)S(1)} %shard_map.115.refs_0_, bf16[8,32,128]{2,1,0:T(8,128)(2,1)S(1)} %collective-permute-done.2.refs_1_), custom_call_target="tpu_custom_call" | custom-call | tf_op jit(solution)/shard_map/pallas_call | solution.py:484
  29.2 13.3 %all_to_all.20.cmsg = bf16[8,64,128]{2,1,0:T(8,128)(2,1)S(1)} all-to-all(bf16[8,64,128]{2,1,0:T(8,128)(2,1)S(1)} %shard_map.116), channel_id=1, replica_groups={{0,2,4,6,8,10,12,14},{1,3,5,7,9,11,13,15},{16,18,20,22,24,26,28,30},{17..., dimensions={0} | all-to-all | bytes 262144 | tf_op jit(solution)/shard_map/all_to_all | solution.py:444
  42.5 0.0 copy-done.3
  42.5 0.0 copy-done.4
  42.5 0.0 copy-start.7
  42.5 1.6 %copy-done.7 = f32[2,512,512]{2,1,0:T(8,128)S(1)} copy-done((f32[2,512,512]{2,1,0:T(8,128)S(1)}, f32[2,512,512]{2,1,0:T(8,128)}, u32[]{:S(2)}) %copy-start.7) | copy-done | bytes 2097176
  44.1 1.5 %shard_map.117 = (bf16[528,512]{1,0:T(8,128)(2,1)S(1)}, bf16[512,512]{1,0:T(8,128)(2,1)S(1)}, bf16[8,80,128]{2,1,0:T(8,128)(2,1)S(1)}) custom-call(bf16[512,512]{1,0:T(8,128)(2,1)S(1)} %copy-done.2, f32[2,512,512]{2,1,0:T(8,128)S(1)} %copy-done.7, bf16[2,32,256]{2,1,0:T(8,128)(2,1)S(1)} %bitcast.4, bf16[2,32,256]{2,1,0:T(8,128)(2,1)S(1)} %bitcast.8, ...), custom_call_target="tpu_custom_call" | custom-call | flops 2300000000 | tf_op jit(solution)/shard_map/pallas_call | solution.py:492
  45.6 0.8 collective-permute-start.4
  46.4 0.0 collective-permute-start.3
  46.4 14.5 %all_to_all.21.refs_2_ = bf16[8,80,128]{2,1,0:T(8,128)(2,1)S(1)} all-to-all(bf16[8,80,128]{2,1,0:T(8,128)(2,1)S(1)} %get-tuple-element.19), channel_id=1, replica_groups={{0,2,4,6,8,10,12,14},{1,3,5,7,9,11,13,15},{16,18,20,22,24,26,28,30},{17..., dimensions={0} | all-to-all | bytes 327680 | tf_op jit(solution)/shard_map/all_to_all | solution.py:444
  60.9 0.0 collective-permute-start.5
  60.9 2.0 %collective-permute-start.7 = (bf16[512,512]{1,0:T(8,128)(2,1)S(1)}, bf16[512,512]{1,0:T(8,128)(2,1)S(1)}, u32[]{:S(2)}, u32[]{:S(2)}) collective-permute-start(bf16[512,512]{1,0:T(8,128)(2,1)S(1)} %get-tuple-element.21.vown), channel_id=1, source_target_pairs={{1,0},{2,1},{3,2},{4,3},{5,4},{6,5},{7,6},{8,7},{9,8},{10,9},{11,1... | collective-permute-start | bytes 1572872 | tf_op jit(solution)/shard_map/ppermute | solution.py:418
  62.9 0.0 collective-permute-start.6
  62.9 0.0 collective-permute-done.5.refs_3_
  62.9 0.0 collective-permute-done.4.after_high.vhigh
  63.0 0.0 collective-permute-done.3.after_low.vlow
  63.0 0.0 copy-start.1
  63.0 1.6 %shard_map.118 = bf16[8,80,128]{2,1,0:T(8,128)(2,1)S(1)} custom-call(s32[96]{0:T(128)S(1)} %reshape.18.cols, s32[1]{0:T(128)} %bitcast.3.group, bf16[528,512]{1,0:T(8,128)(2,1)S(1)} %collective-permute-done.3.after_low.vlow, bf16[528,512]{1,0:T(8,128)(2,1)S(1)} %collective-permute-done.4.after_high.vhigh, bf16[8,240,128]{2,1,0:T(8,128)(2,1)S(1)} %all-to-all-done.held, ...), custom_call_target="tpu_custom_call" | custom-call | flops 34500001792 | tf_op jit(solution)/shard_map/pallas_call | solution.py:510
  64.6 13.0 %all_to_all.22.cmsg = bf16[8,80,128]{2,1,0:T(8,128)(2,1)S(1)} all-to-all(bf16[8,80,128]{2,1,0:T(8,128)(2,1)S(1)} %shard_map.118), channel_id=1, replica_groups={{0,2,4,6,8,10,12,14},{1,3,5,7,9,11,13,15},{16,18,20,22,24,26,28,30},{17..., dimensions={0} | all-to-all | bytes 327680 | tf_op jit(solution)/shard_map/all_to_all | solution.py:444
  77.6 0.0 copy-done.1
  77.6 2.9 %shard_map.119 = (f32[2,512,512]{2,1,0:T(8,128)}, f32[2,512]{1,0:T(2,128)}, f32[2,512]{1,0:T(2,128)}, f32[8,512]{1,0:T(8,128)S(1)}) custom-call(bf16[2,512,1280]{2,1,0:T(8,128)(2,1)S(1)} %copy-done.1, bf16[512,512]{1,0:T(8,128)(2,1)S(1)} %collective-permute-done.low.ulow, bf16[512,512]{1,0:T(8,128)(2,1)S(1)} %copy-done.2, ...), custom_call_target="tpu_custom_call" | custom-call | tf_op jit(solution)/shard_map/pallas_call | solution.py:528
  80.4 0.0 collective-permute-done.7.vhigh
  80.4 0.0 collective-permute-done.6.vlow
  80.5 2.2 %shard_map.120 = f32[2,512,512]{2,1,0:T(8,128)} custom-call(f32[2,512,512]{2,1,0:T(8,128)} %get-tuple-element.20.begun, bf16[2,512,1280]{2,1,0:T(8,128)(2,1)S(1)} %copy-done.1, bf16[512,512]{1,0:T(8,128)(2,1)S(1)} %collective-permute-done.low.ulow, bf16[512,512]{1,0:T(8,128)(2,1)S(1)} %copy-done.2, ...), custom_call_target="tpu_custom_call", output_to_operand_aliasing={{}: (0, {})} | custom-call | tf_op jit(solution)/shard_map/pallas_call | solution.py:535
  (2 shorter events, 0.0 us)
Async XLA Ops:
  3.0 12.9 %collective-permute-start.1 = (bf16[512,512]{1,0:T(8,128)(2,1)}, bf16[512,512]{1,0:T(8,128)(2,1)S(1)}, u32[]{:S(2)}, u32[]{:S(2)}) collective-permute-start(bf16[512,512]{1,0:T(8,128)(2,1)} %get-tuple-element.15), channel_id=1, source_target_pairs={{1,0},{2,1},{3,2},{4,3},{5,4},{6,5},{7,6},{8,7},{9,8},{10,9},{11,1... | collective-permute-start | bytes 1572872 | tf_op jit(solution)/shard_map/ppermute | solution.py:418
  8.4 13.2 %collective-permute-start = (bf16[512,512]{1,0:T(8,128)(2,1)}, bf16[512,512]{1,0:T(8,128)(2,1)S(1)}, u32[]{:S(2)}, u32[]{:S(2)}) collective-permute-start(bf16[512,512]{1,0:T(8,128)(2,1)} %get-tuple-element.15), channel_id=1, source_target_pairs={{0,1},{1,2},{2,3},{3,4},{4,5},{5,6},{6,7},{7,8},{8,9},{9,10},{10,1... | collective-permute-start | bytes 1572872 | tf_op jit(solution)/shard_map/ppermute | solution.py:418
  8.4 17.8 %all-to-all-start = ((bf16[8,240,128]{2,1,0:T(8,128)(2,1)}), bf16[8,240,128]{2,1,0:T(8,128)(2,1)S(1)}, u32[]{:S(2)}, u32[]{:S(2)}) async-start(bf16[8,240,128]{2,1,0:T(8,128)(2,1)} %get-tuple-element.14.after), calls=%async_computation | async-start | bytes 983040 | tf_op jit(solution)/shard_map/all_to_all | solution.py:444
  11.9 9.7 %copy-start.2 = (bf16[512,512]{1,0:T(8,128)(2,1)S(1)}, bf16[512,512]{1,0:T(8,128)(2,1)}, u32[]{:S(2)}) copy-start(bf16[512,512]{1,0:T(8,128)(2,1)} %uown.3) | copy-start | bytes 1572868
  11.9 9.7 %copy-start.5 = (f32[2,512]{1,0:T(2,128)S(1)}, f32[2,512]{1,0:T(2,128)}, u32[]{:S(2)}) copy-start(f32[2,512]{1,0:T(2,128)} %diag.5) | copy-start | bytes 12292
  11.9 30.6 %copy-start.3 = (bf16[2,256,32]{1,2,0:T(8,128)(2,1)S(1)}, bf16[2,256,32]{1,2,0:T(8,128)(2,1)}, u32[]{:S(2)}) copy-start(bf16[2,256,32]{1,2,0:T(8,128)(2,1)} %param.15) | copy-start | bytes 98308
  11.9 30.5 %copy-start.4 = (bf16[2,256,32]{1,2,0:T(8,128)(2,1)S(1)}, bf16[2,256,32]{1,2,0:T(8,128)(2,1)}, u32[]{:S(2)}) copy-start(bf16[2,256,32]{1,2,0:T(8,128)(2,1)} %param.16) | copy-start | bytes 98308
  21.6 1.7 %copy-start = (bf16[2,512,1280]{2,1,0:T(8,128)(2,1)S(1)}, bf16[2,512,1280]{2,1,0:T(8,128)(2,1)}, u32[]{:S(2)}) copy-start(bf16[2,512,1280]{2,1,0:T(8,128)(2,1)} %shard_map.113.w) | copy-start | bytes 7864324
  24.9 1.3 %copy-start.6 = (f32[2,512,512]{2,1,0:T(8,128)}, f32[2,512,512]{2,1,0:T(8,128)S(1)}, u32[]{:S(2)}) copy-start(f32[2,512,512]{2,1,0:T(8,128)S(1)} %get-tuple-element.16.near) | copy-start | bytes 6291460
  26.2 1.8 %collective-permute-start.2 = (bf16[8,32,128]{2,1,0:T(8,128)(2,1)S(1)}, bf16[8,32,128]{2,1,0:T(8,128)(2,1)S(1)}, u32[]{:S(2)}, u32[]{:S(2)}) collective-permute-start(bf16[8,32,128]{2,1,0:T(8,128)(2,1)S(1)} %shard_map.115.refs_0_), channel_id=1, source_target_pairs={{0,1},{1,0},{2,3},{3,2},{4,5},{5,4},{6,7},{7,6},{8,9},{9,8},{10,11... | collective-permute-start | bytes 196616 | tf_op jit(solution)/shard_map/ppermute | solution.py:450
  42.5 1.6 %copy-start.7 = (f32[2,512,512]{2,1,0:T(8,128)S(1)}, f32[2,512,512]{2,1,0:T(8,128)}, u32[]{:S(2)}) copy-start(f32[2,512,512]{2,1,0:T(8,128)} %copy-done.6) | copy-start | bytes 6291460
  45.6 17.4 %collective-permute-start.4 = (bf16[528,512]{1,0:T(8,128)(2,1)S(1)}, bf16[528,512]{1,0:T(8,128)(2,1)S(1)}, u32[]{:S(2)}, u32[]{:S(2)}) collective-permute-start(bf16[528,512]{1,0:T(8,128)(2,1)S(1)} %get-tuple-element.18.vown), channel_id=1, source_target_pairs={{1,0},{2,1},{3,2},{4,3},{5,4},{6,5},{7,6},{8,7},{9,8},{10,9},{11,1... | collective-permute-start | bytes 1622024 | tf_op jit(solution)/shard_map/ppermute | solution.py:418
  46.4 16.6 %collective-permute-start.3 = (bf16[528,512]{1,0:T(8,128)(2,1)S(1)}, bf16[528,512]{1,0:T(8,128)(2,1)S(1)}, u32[]{:S(2)}, u32[]{:S(2)}) collective-permute-start(bf16[528,512]{1,0:T(8,128)(2,1)S(1)} %get-tuple-element.18.vown), channel_id=1, source_target_pairs={{0,1},{1,2},{2,3},{3,4},{4,5},{5,6},{6,7},{7,8},{8,9},{9,10},{10,1... | collective-permute-start | bytes 1622024 | tf_op jit(solution)/shard_map/ppermute | solution.py:418
  60.9 2.1 %collective-permute-start.5 = (bf16[8,80,128]{2,1,0:T(8,128)(2,1)S(1)}, bf16[8,80,128]{2,1,0:T(8,128)(2,1)S(1)}, u32[]{:S(2)}, u32[]{:S(2)}) collective-permute-start(bf16[8,80,128]{2,1,0:T(8,128)(2,1)S(1)} %all_to_all.21.refs_2_), channel_id=1, source_target_pairs={{0,1},{1,0},{2,3},{3,2},{4,5},{5,4},{6,7},{7,6},{8,9},{9,8},{10,11... | collective-permute-start | bytes 491528 | tf_op jit(solution)/shard_map/ppermute | solution.py:450
  60.9 19.5 %collective-permute-start.7 = (bf16[512,512]{1,0:T(8,128)(2,1)S(1)}, bf16[512,512]{1,0:T(8,128)(2,1)S(1)}, u32[]{:S(2)}, u32[]{:S(2)}) collective-permute-start(bf16[512,512]{1,0:T(8,128)(2,1)S(1)} %get-tuple-element.21.vown), channel_id=1, source_target_pairs={{1,0},{2,1},{3,2},{4,3},{5,4},{6,5},{7,6},{8,7},{9,8},{10,9},{11,1... | collective-permute-start | bytes 1572872 | tf_op jit(solution)/shard_map/ppermute | solution.py:418
  62.9 17.5 %collective-permute-start.6 = (bf16[512,512]{1,0:T(8,128)(2,1)S(1)}, bf16[512,512]{1,0:T(8,128)(2,1)S(1)}, u32[]{:S(2)}, u32[]{:S(2)}) collective-permute-start(bf16[512,512]{1,0:T(8,128)(2,1)S(1)} %get-tuple-element.21.vown), channel_id=1, source_target_pairs={{0,1},{1,2},{2,3},{3,4},{4,5},{5,6},{6,7},{7,8},{8,9},{9,10},{10,1... | collective-permute-start | bytes 1572872 | tf_op jit(solution)/shard_map/ppermute | solution.py:418
  63.0 14.6 %copy-start.1 = (bf16[2,512,1280]{2,1,0:T(8,128)(2,1)S(1)}, bf16[2,512,1280]{2,1,0:T(8,128)(2,1)}, u32[]{:S(2)}) copy-start(bf16[2,512,1280]{2,1,0:T(8,128)(2,1)} %shard_map.113.w) | copy-start | bytes 7864324

commit v19 on v14

--- a/solution.py
+++ b/solution.py
@@ -22,7 +22,7 @@
 ANY = pl.BlockSpec(memory_space=pl.ANY)
 
 
-def call(body, out_shape, in_specs, scratch=(), micros=0.0, megabytes=20, out_specs=None):
+def call(body, out_shape, in_specs, scratch=(), micros=0.0, megabytes=20, out_specs=None, alias=None):
     many = isinstance(out_shape, (list, tuple))
     if out_specs is None:
         out_specs = [VMEM] * len(out_shape) if many else VMEM
@@ -31,6 +31,7 @@
         out_shape=out_shape,
         in_specs=in_specs,
         out_specs=out_specs,
+        input_output_aliases=alias or {},
         scratch_shapes=list(scratch),
         compiler_params=pltpu.CompilerParams(vmem_limit_bytes=megabytes * 1024 * 1024),
         cost_estimate=pl.CostEstimate(
@@ -70,7 +71,7 @@
     return x[:, pair * LANES:(pair + 1) * LANES]
 
 
-def order_tiles(all_blocks, cols, count, row0, tiles, out):
+def order_tiles(all_blocks, cols, count, row0, tiles, after, out):
     ops, blocks, near, size, _ = tiles.shape
     for b in range(blocks):
         for k in range(near):
@@ -85,14 +86,16 @@
                 )
 
 
-def coeff_kernel(count, far_cols, u, right, coup, z_out, out):
+def coeff_kernel(count, far_cols, u, right, coup, out, u_out):
     ops, blocks, far, rank, _ = coup.shape
     size = right.shape[2]
+    u_out[...] = u[...]
     z = [dot(right[b], u[b * size:(b + 1) * size, :]) for b in range(blocks)]
+    at = 3 * ops * rank + STATS
     for pair in range(SLICES // 2):
         first, second = halves(chunk(z[0], pair), chunk(z[1], pair))
-        z_out[2 * pair] = first.astype(BF16)
-        z_out[2 * pair + 1] = second.astype(BF16)
+        out[2 * pair, at:at + rank, :] = first.astype(BF16)
+        out[2 * pair + 1, at:at + rank, :] = second.astype(BF16)
     whole, rest = [], []
     for b in range(blocks):
         tiles = [
@@ -110,19 +113,15 @@
             slot = lax.rem(device, count) * SLICES + lax.div(device, count)
             name = (slot * blocks + lax.rem(col, blocks)).astype(F32)
             names = jnp.where(lane == b * far + f, name, names)
-    out[...] = jnp.concatenate(
+    whole = jnp.concatenate(
         whole + [jnp.concatenate(rest, axis=1), names.astype(BF16)], axis=0
     )
-
-
-def share_kernel(packed, *refs):
-    parts, out = refs[:-1], refs[-1]
-    rows = packed.shape[0]
-    rank = parts[0].shape[1]
     for s in range(SLICES):
-        out[s, 0:rows, :] = packed[...]
-    for m, part in enumerate(parts):
-        out[:, rows + m * rank:rows + (m + 1) * rank, :] = part[...]
+        out[s, 0:at, :] = whole
+
+
+def take_kernel(held, after, out):
+    out[...] = held[:, held.shape[1] - out.shape[1]:, :]
 
 
 def coupling_rows(held, s, b, ops, rank):
@@ -153,21 +152,16 @@
     return both.reshape(count * 2 * rank, LANES).astype(BF16)
 
 
-def held_part(held, m, ops, rank):
-    at = 3 * ops * rank + STATS + m * rank
-    return held[:, at:at + rank, :].astype(F32)
-
-
 def group_at(group, m, groups, step):
     return pl.multiple_of(lax.rem(group[0] + (groups - m), groups) * step, step)
 
 
-def first_couple(ops, rank, far, cols, group, after, held, out, zs):
+def first_couple(ops, rank, far, cols, group, after, held, *refs):
+    parts, (out, zs) = refs[:-2], refs[-2:]
     step = SLICES * 2 * rank
-    count = zs.shape[0] // step
-    for m in range(count):
-        at = group_at(group, m, count, step)
-        zs[pl.ds(at, step), :] = spread_rows(held_part(held, m, ops, rank), rank)
+    for m, part in enumerate(parts):
+        at = group_at(group, m, len(parts), step)
+        zs[pl.ds(at, step), :] = spread_rows(part[...].astype(F32), rank)
     for s in range(SLICES):
         c = [couple(cols, held, s, b, ops, rank, far, [zs]) for b in range(2)]
         out[s] = halves(c[0], c[1])[0].astype(BF16)
@@ -275,8 +269,9 @@
 
 
 def second_couple(panels, ops, rank, far, cols, group, after_low, after_high, held, *refs):
-    msgs, (out, zs, st) = refs[:-3], refs[-3:]
-    count = len(msgs)
+    out, zs, st = refs[-3:]
+    count = (len(refs) - 3) // 2
+    z1, msgs = refs[:count], refs[count:2 * count]
     body = ops * rank
     step = SLICES * 2 * rank
     for m, msg in enumerate(msgs):
@@ -298,7 +293,7 @@
     for m, msg in enumerate(msgs):
         at = group_at(group, m, count, step)
         mine = msg[:, body:body + STATS, :].astype(F32)
-        base = held_part(held, m, ops, rank)
+        base = z1[m][...].astype(F32)
         for o in range(ops):
             delta = join3(mine, o) - heights[o]
             z = msg[:, o * rank:(o + 1) * rank, :].astype(F32) + delta[:, None, :] * base
@@ -321,10 +316,10 @@
     uown,
     uhigh,
     low0,
-    first,
+    own0,
     high0,
     low1,
-    second,
+    own1,
     high1,
     diag,
     left,
@@ -334,48 +329,45 @@
     norms,
     ext,
     coef,
+    out,
     stat,
-    out,
-    outs,
+    sems,
 ):
-    copies = []
-    ops = images.shape[0]
     blocks, rank, size = left.shape
     rows, columns = uown.shape
+    ops = w.shape[1] // size
     body = ops * rank
-    take_coefs(cmsg, coef, body)
     for pair in range(SLICES // 2):
         stat[:, pair * LANES:(pair + 1) * LANES] = halves(
             cmsg[2 * pair, body:body + STATS, :].astype(F32),
             cmsg[2 * pair + 1, body:body + STATS, :].astype(F32),
         )[0]
     st = stat[...]
+    take_coefs(cmsg, coef, body)
     reverse = row3(st, 2 * ops)
+    copies = []
     for o in range(ops):
         height = row3(st, o)
         norm = row3(st, ops + o)
         heights[o:o + 1, :] = height
         norms[o:o + 1, :] = norm
         factor = reverse / norm
-        triples = (ulow, low0, low1), (uown, first, second), (uhigh, high0, high1)
+        triples = (ulow, low0, low1), (uown, own0, own1), (uhigh, high0, high1)
         for at, (u, v0, v1) in enumerate(triples):
-            shift = row3(v0[rows:, :].astype(F32), o)
-            change = (shift - height) * factor
+            change = (row3(v0[rows:, :].astype(F32), o) - height) * factor
             v = (v0, v1)[o][0:rows, :].astype(F32)
-            value = v * factor + u[...].astype(F32) * change
-            ext[o, at] = value.astype(BF16)
+            ext[o, at] = (v * factor + u[...].astype(F32) * change).astype(BF16)
         for b in range(blocks):
             parts = [ext.at[o, at] for at in range(3)]
             product = near_product(w.at[b, o * size:(o + 1) * size], parts, b, blocks, size)
             far = dot(left[b], coef[b, o * rank:(o + 1) * rank, :], ((0,), (0,)))
-            mine = ext[o, 1, b * size:(b + 1) * size, :].astype(F32)
             here = slice(b * size, (b + 1) * size)
             out[o, here, :] = (
                 product
-                + diagonal_of(diag, o, b, size, columns) * mine
+                + diagonal_of(diag, o, b, size, columns) * ext[o, 1, here, :].astype(F32)
                 + far.astype(BF16).astype(F32)
             )
-            copy = pltpu.make_async_copy(out.at[o, here], images.at[o, here], outs.at[o, b])
+            copy = pltpu.make_async_copy(out.at[o, here], images.at[o, here], sems.at[o, b])
             copy.start()
             copies.append(copy)
     for copy in copies:
@@ -427,44 +419,37 @@
     left = jnp.transpose(basis_left, (0, 2, 1))
     right = jnp.transpose(basis_right, (0, 2, 1))
 
-    low, high = ring(sources)
     shared = (blocks + 1) * body
-    z1, packed = call(
+    mine, own = call(
         functools.partial(coeff_kernel, count),
-        [sds((SLICES, rank, LANES), BF16), sds((shared + STATS, LANES), BF16)],
-        [SMEM, VMEM, VMEM, VMEM],
+        [sds((SLICES, shared + STATS + rank, LANES), BF16), sds(sources.shape, BF16)],
+        [SMEM] + [VMEM] * 3,
         megabytes=60,
     )(far_cols, sources, right, couplings)
-    z1 = across(z1)
-    held = call(
-        share_kernel,
-        sds((SLICES, shared + STATS + count * rank, LANES), BF16),
-        [VMEM] * (1 + count),
-    )(packed, *z1)
-    held = exchange(held)
+    low, high = ring(own)
+    held = exchange(mine)
     cols = held[:, shared, :blocks * far].astype(jnp.int32).reshape(-1)
 
     w = call(
         functools.partial(order_tiles, all_blocks),
         sds((blocks, ops * size, near * size), BF16),
-        [SMEM, SMEM, SMEM, VMEM],
-        micros=0.0,
+        [SMEM, SMEM, SMEM, VMEM, ANY],
         megabytes=60,
-    )(near_cols, near_count, row0, near_tiles)
+    )(near_cols, near_count, row0, near_tiles, mine)
     image, token = call(
         near_kernel,
         [sds((ops, rows, columns), F32), sds((8, LANES), F32)],
         [VMEM] * 5,
         micros=10.0,
-        megabytes=60,
     )(w, low, sources, high, self_terms)
+    z1 = across(call(take_kernel, sds((SLICES, rank, LANES), BF16), [VMEM, ANY])(held, token))
 
     c1 = call(
         functools.partial(first_couple, ops, rank, far),
         sds((SLICES, body, LANES), BF16),
-        [SMEM, SMEM, ANY, VMEM],
+        [SMEM, SMEM, ANY] + [VMEM] * (1 + count),
         [pltpu.VMEM((n * blocks * rank, LANES), BF16)],
-    )(cols, group, token, held)
+    )(cols, group, image, held, *z1)
     c1 = exchange(c1)
 
     first, second, msg = call(
@@ -488,13 +473,13 @@
     c2 = call(
         functools.partial(second_couple, all_blocks * size, ops, rank, far),
         sds((SLICES, body + STATS, LANES), BF16),
-        [SMEM, SMEM, ANY, ANY] + [VMEM] * (1 + count),
+        [SMEM, SMEM, ANY, ANY] + [VMEM] * (1 + 2 * count),
         [
             pltpu.VMEM((ops, n * blocks * rank, LANES), BF16),
             pltpu.VMEM((n, STATS, LANES), F32),
         ],
         micros=30.0,
-    )(cols, group, low0, high0, held, *msgs)
+    )(cols, group, low0, high0, held, *z1, *msgs)
     c2 = exchange(c2)
 
     images, heights, norms = call(
@@ -504,11 +489,10 @@
         [
             pltpu.VMEM((ops, 3, rows, columns), BF16),
             pltpu.VMEM((blocks, body, columns), BF16),
+            pltpu.VMEM((ops, rows, columns), F32),
             pltpu.VMEM((STATS, columns), F32),
-            pltpu.VMEM((ops, rows, columns), F32),
             pltpu.SemaphoreType.DMA((ops, blocks)),
         ],
-        micros=4.0,
         out_specs=[ANY, VMEM, VMEM],
     )(w, low, sources, high, low0, first, high0, low1, second, high1, self_terms, left, c2)
     return images, heights, norms

time: 95.4 us -> 91.9 us (0.963)
  Pallas kernels: 22 us -> 17.9 us
  blocking collectives: 24.7 us -> 28 us
  waiting for transfers between devices: 16.3 us -> 13.7 us
  starting transfers between devices: 17.4 us -> 15.6 us
  local copies, waits for them, and re-layouts: 12.6 us -> 14.2 us
    all_to_all x2, waiting for transfers between devices: 11.8 us -> 3.11 us  [exchange(): lax.all_to_all(x, 'store', 0, 0, axis_index_groups=groups, tiled=True)]
    ppermute x3, waiting for transfers between devices: 4.42 us -> 9.34 us  [ring(): lax.ppermute(block, 'store', forward)]
    pallas_call x1, Pallas kernels: 4.99 us -> 1.52 us  [shards(): call(near_kernel, [sds((ops, rows, columns), F32), sds((8, LANES), F32)],...]
    all_to_all x2, blocking collectives: 24.7 us -> 28 us  [exchange(): lax.all_to_all(x, 'store', 0, 0, axis_index_groups=groups, tiled=True)]
    all_to_all x2, starting transfers between devices: 9.48 us -> 6.86 us  [exchange(): lax.all_to_all(x, 'store', 0, 0, axis_index_groups=groups, tiled=True)]
    unnamed x40 -> x38, local copies, waits for them, and re-layouts: 12.6 us -> 14.1 us
  transfers between devices with their start and end apart: 10 -> 10, of which waited for: 3 -> 5; matrix products, arithmetic and copies ran while one was open for 0% -> 0% of each run, Pallas kernels for 15% -> 8%
where the time goes in v19:
time: 91.9 us; the launch traced here: 90.2 us
  blocking collectives  28 us (30%)
  Pallas kernels  17.9 us (19%)
  starting transfers between devices  15.6 us (17%)
  local copies, waits for them, and re-layouts  14.2 us (15%)
  waiting for transfers between devices  13.7 us (15%)
    all_to_all x2, blocking collectives, exchange(): lax.all_to_all(x, 'store', 0, 0, axis_index_groups=groups, tiled=True)  28 us
    unnamed x38, local copies, waits for them, and re-layouts  14.1 us
    ppermute x3, waiting for transfers between devices, ring(): lax.ppermute(block, 'store', forward)  9.34 us
    ppermute x3, starting transfers between devices, ring(): lax.ppermute(block, 'store', backward)  8.24 us
    all_to_all x2, starting transfers between devices, exchange(): lax.all_to_all(x, 'store', 0, 0, axis_index_groups=groups, tiled=True)  6.86 us
    pallas_call x1, Pallas kernels, shards(): call(final_kernel, [sds((ops, rows, columns), F32), sds((ops, columns), F...  5.15 us
    pallas_call x1, Pallas kernels, shards(): call(functools.partial(order_tiles, all_blocks), sds((blocks, ops * size,...  3.5 us
    all_to_all x2, waiting for transfers between devices, exchange(): lax.all_to_all(x, 'store', 0, 0, axis_index_groups=groups, tiled=True)  3.11 us
  transfers between devices with their start and end apart: 10, of which 5 were waited for; matrix products, arithmetic and copies ran while one was open for 0% of the time, Pallas kernels for 8%

profile of v19, /device:TPU:0, one launch (start us, length us, event | category | flops | bytes accessed | tf_op | source)
XLA Modules:
  0.0 90.2 jit_solution(12959150312159303783)
XLA Ops:
  0.6 2.3 %shard_map.112 = (bf16[8,240,128]{2,1,0:T(8,128)(2,1)}, bf16[512,512]{1,0:T(8,128)(2,1)}) custom-call(s32[2,6]{1,0:T(2,128)} %far_cols.1, bf16[512,512]{1,0:T(8,128)(2,1)} %uown.1, bf16[2,32,256]{2,1,0:T(8,128)(2,1)} %bitcast.6, bf16[2,2,6,32,32]{4,3,2,1,0:T(8,128)(2,1)} %coup.1), custom_call_target="tpu_custom_call" | custom-call | tf_op jit(solution)/shard_map/pallas_call | solution.py:423
  2.9 5.4 %collective-permute-start.1 = (bf16[512,512]{1,0:T(8,128)(2,1)}, bf16[512,512]{1,0:T(8,128)(2,1)S(1)}, u32[]{:S(2)}, u32[]{:S(2)}) collective-permute-start(bf16[512,512]{1,0:T(8,128)(2,1)} %get-tuple-element.11), channel_id=1, source_target_pairs={{1,0},{2,1},{3,2},{4,3},{5,4},{6,5},{7,6},{8,7},{9,8},{10,9},{11,1... | collective-permute-start | bytes 1572872 | tf_op jit(solution)/shard_map/ppermute | solution.py:381
  8.4 0.0 collective-permute-start
  8.4 3.5 %all-to-all-start = ((bf16[8,240,128]{2,1,0:T(8,128)(2,1)}), bf16[8,240,128]{2,1,0:T(8,128)(2,1)S(1)}, u32[]{:S(2)}, u32[]{:S(2)}) async-start(bf16[8,240,128]{2,1,0:T(8,128)(2,1)} %get-tuple-element.10.after), calls=%async_computation | async-start | bytes 983040 | tf_op jit(solution)/shard_map/all_to_all | solution.py:407
  11.9 0.0 copy-start.2
  11.9 0.0 copy-start.18
  11.9 3.5 %shard_map.113.w = bf16[2,512,1280]{2,1,0:T(8,128)(2,1)} custom-call(s32[2,5]{1,0:T(2,128)} %cols.1, s32[2]{0:T(128)} %count.1, s32[1]{0:T(128)} %bitcast.row0, bf16[2,2,5,256,256]{4,3,2,1,0:T(8,128)(2,1)} %tiles.1, bf16[8,240,128]{2,1,0:T(8,128)(2,1)} %get-tuple-element.10.after), custom_call_target="tpu_custom_call" | custom-call | tf_op jit(solution)/shard_map/pallas_call | solution.py:433
  15.4 0.4 collective-permute-done.1.high.uhigh
  15.9 0.0 copy-start.10
  15.9 0.8 copy-done.10
  16.7 4.9 %collective-permute-done.low.ulow = bf16[512,512]{1,0:T(8,128)(2,1)S(1)} collective-permute-done((bf16[512,512]{1,0:T(8,128)(2,1)}, bf16[512,512]{1,0:T(8,128)(2,1)S(1)}, u32[]{:S(2)}, u32[]{:S(2)}) %collective-permute-start) | collective-permute-done | bytes 524320 | tf_op jit(solution)/shard_map/ppermute | solution.py:381
  21.6 0.0 copy-start.13
  21.6 0.8 copy-done.13
  22.4 0.0 copy-done.2
  22.4 0.0 copy-done.18
  22.4 0.0 copy-start
  22.4 1.7 %copy-done = bf16[2,512,1280]{2,1,0:T(8,128)(2,1)S(1)} copy-done((bf16[2,512,1280]{2,1,0:T(8,128)(2,1)S(1)}, bf16[2,512,1280]{2,1,0:T(8,128)(2,1)}, u32[]{:S(2)}) %copy-start) | copy-done | bytes 2621464
  24.1 0.0 copy-start.11
  24.1 1.0 %copy-done.11 = bf16[512,512]{1,0:T(8,128)(2,1)S(1)} copy-done((bf16[512,512]{1,0:T(8,128)(2,1)S(1)}, bf16[512,512]{1,0:T(8,128)(2,1)}, u32[]{:S(2)}) %copy-start.11) | copy-done | bytes 524312
  25.2 0.0 copy-start.14
  25.2 1.0 %copy-done.14 = bf16[512,512]{1,0:T(8,128)(2,1)S(1)} copy-done((bf16[512,512]{1,0:T(8,128)(2,1)S(1)}, bf16[512,512]{1,0:T(8,128)(2,1)}, u32[]{:S(2)}) %copy-start.14) | copy-done | bytes 524312
  26.2 1.5 %shard_map.114 = (f32[2,512,512]{2,1,0:T(8,128)S(1)}, f32[8,128]{1,0:T(8,128)S(1)}) custom-call(bf16[2,512,1280]{2,1,0:T(8,128)(2,1)S(1)} %copy-done, bf16[512,512]{1,0:T(8,128)(2,1)S(1)} %copy-done.14, bf16[512,512]{1,0:T(8,128)(2,1)S(1)} %copy-done.2, bf16[512,512]{1,0:T(8,128)(2,1)S(1)} %copy-done.11, f32[2,512]{1,0:T(2,128)S(1)} %copy-done.18), custom_call_target="tpu_custom_call" | custom-call | flops 11500000256 | tf_op jit(solution)/shard_map/pallas_call | solution.py:439
  27.7 0.0 copy-start.16
  27.8 0.0 copy-start.17
  27.8 0.0 all-to-all-done.held
  27.8 0.5 collective-permute-start.2
  28.3 0.1 reshape.18.cols
  28.4 0.8 collective-permute-done.2.refs_1_
  29.2 1.1 %shard_map.116 = bf16[8,64,128]{2,1,0:T(8,128)(2,1)S(1)} custom-call(s32[96]{0:T(128)S(1)} %reshape.18.cols, s32[1]{0:T(128)} %bitcast.3.group, f32[2,512,512]{2,1,0:T(8,128)S(1)} %get-tuple-element.12.after.near, bf16[8,240,128]{2,1,0:T(8,128)(2,1)S(1)} %all-to-all-done.held, bf16[8,32,128]{2,1,0:T(8,128)(2,1)S(1)} %shard_map.115.refs_0_, ...), custom_call_target="tpu_custom_call" | custom-call | tf_op jit(solution)/shard_map/pallas_call | solution.py:447
  30.3 14.3 %all_to_all.20.cmsg = bf16[8,64,128]{2,1,0:T(8,128)(2,1)S(1)} all-to-all(bf16[8,64,128]{2,1,0:T(8,128)(2,1)S(1)} %shard_map.116), channel_id=1, replica_groups={{0,2,4,6,8,10,12,14},{1,3,5,7,9,11,13,15},{16,18,20,22,24,26,28,30},{17..., dimensions={0} | all-to-all | bytes 262144 | tf_op jit(solution)/shard_map/all_to_all | solution.py:407
  44.6 0.0 copy-done.16
  44.6 0.0 copy-done.17
  44.6 2.0 %shard_map.117 = (bf16[528,512]{1,0:T(8,128)(2,1)S(1)}, bf16[512,512]{1,0:T(8,128)(2,1)}, bf16[8,80,128]{2,1,0:T(8,128)(2,1)S(1)}) custom-call(bf16[512,512]{1,0:T(8,128)(2,1)S(1)} %copy-done.2, f32[2,512,512]{2,1,0:T(8,128)S(1)} %get-tuple-element.12.after.near, bf16[2,32,256]{2,1,0:T(8,128)(2,1)S(1)} %bitcast.4, bf16[2,32,256]{2,1,0:T(8,128)(2,1)S(1)} %bitcast.7, ...), custom_call_target="tpu_custom_call" | custom-call | flops 2300000000 | tf_op jit(solution)/shard_map/pallas_call | solution.py:455
  46.6 0.8 collective-permute-start.4
  47.4 0.0 collective-permute-start.3
  47.4 0.0 copy-start.4
  47.4 0.8 copy-done.4
  48.2 13.7 %all_to_all.21.refs_2_ = bf16[8,80,128]{2,1,0:T(8,128)(2,1)S(1)} all-to-all(bf16[8,80,128]{2,1,0:T(8,128)(2,1)S(1)} %get-tuple-element.16), channel_id=1, replica_groups={{0,2,4,6,8,10,12,14},{1,3,5,7,9,11,13,15},{16,18,20,22,24,26,28,30},{17..., dimensions={0} | all-to-all | bytes 327680 | tf_op jit(solution)/shard_map/all_to_all | solution.py:407
  61.9 0.0 collective-permute-start.7
  61.9 0.0 copy-start.1
  61.9 2.0 %collective-permute-start.6 = (bf16[512,512]{1,0:T(8,128)(2,1)}, bf16[512,512]{1,0:T(8,128)(2,1)}, u32[]{:S(2)}, u32[]{:S(2)}) collective-permute-start(bf16[512,512]{1,0:T(8,128)(2,1)} %get-tuple-element.15.own1), channel_id=1, source_target_pairs={{1,0},{2,1},{3,2},{4,3},{5,4},{6,5},{7,6},{8,7},{9,8},{10,9},{11,1... | collective-permute-start | bytes 1572872 | tf_op jit(solution)/shard_map/ppermute | solution.py:381
  63.9 0.0 collective-permute-start.5
  63.9 0.0 collective-permute-done.7.refs_3_
  63.9 0.0 collective-permute-done.4.after_high.high0
  63.9 0.0 collective-permute-done.3.after_low.low0
  63.9 2.3 %shard_map.118 = bf16[8,80,128]{2,1,0:T(8,128)(2,1)} custom-call(s32[96]{0:T(128)S(1)} %reshape.18.cols, s32[1]{0:T(128)} %bitcast.3.group, bf16[528,512]{1,0:T(8,128)(2,1)S(1)} %collective-permute-done.3.after_low.low0, bf16[528,512]{1,0:T(8,128)(2,1)S(1)} %collective-permute-done.4.after_high.high0, bf16[8,240,128]{2,1,0:T(8,128)(2,1)S(1)} %all-to-all-done.held, ...), custom_call_target="tpu_custom_call" | custom-call | flops 34500001792 | tf_op jit(solution)/shard_map/pallas_call | solution.py:473
  66.2 0.0 copy-start.6
  66.2 0.8 copy-done.6
  67.0 0.0 copy-start.8
  67.0 0.8 copy-done.8
  67.8 3.4 %all-to-all-start.3 = ((bf16[8,80,128]{2,1,0:T(8,128)(2,1)}), bf16[8,80,128]{2,1,0:T(8,128)(2,1)S(1)}, u32[]{:S(2)}, u32[]{:S(2)}) async-start(bf16[8,80,128]{2,1,0:T(8,128)(2,1)} %shard_map.118), calls=%async_computation.3 | async-start | bytes 327680 | tf_op jit(solution)/shard_map/all_to_all | solution.py:407
  71.2 0.0 collective-permute-done.6.high1
  71.2 4.4 %collective-permute-done.5.low1 = bf16[512,512]{1,0:T(8,128)(2,1)} collective-permute-done((bf16[512,512]{1,0:T(8,128)(2,1)}, bf16[512,512]{1,0:T(8,128)(2,1)}, u32[]{:S(2)}, u32[]{:S(2)}) %collective-permute-start.5) | collective-permute-done | bytes 524320 | tf_op jit(solution)/shard_map/ppermute | solution.py:381
  75.6 3.1 %all-to-all-done.3.cmsg = bf16[8,80,128]{2,1,0:T(8,128)(2,1)S(1)} async-done(((bf16[8,80,128]{2,1,0:T(8,128)(2,1)}), bf16[8,80,128]{2,1,0:T(8,128)(2,1)S(1)}, u32[]{:S(2)}, u32[]{:S(2)}) %all-to-all-start.3) | async-done | bytes 163872 | tf_op jit(solution)/shard_map/all_to_all | solution.py:407
  78.7 0.0 copy-done.1
  78.7 0.0 copy-start.3
  78.7 1.0 %copy-done.3 = bf16[512,512]{1,0:T(8,128)(2,1)S(1)} copy-done((bf16[512,512]{1,0:T(8,128)(2,1)S(1)}, bf16[512,512]{1,0:T(8,128)(2,1)}, u32[]{:S(2)}) %copy-start.3) | copy-done | bytes 524312
  79.8 0.0 copy-start.5
  79.8 1.0 %copy-done.5 = bf16[528,512]{1,0:T(8,128)(2,1)S(1)} copy-done((bf16[528,512]{1,0:T(8,128)(2,1)S(1)}, bf16[528,512]{1,0:T(8,128)(2,1)}, u32[]{:S(2)}) %copy-start.5) | copy-done | bytes 540696
  80.8 1.0 %copy-done.7 = bf16[528,512]{1,0:T(8,128)(2,1)S(1)} copy-done((bf16[528,512]{1,0:T(8,128)(2,1)S(1)}, bf16[528,512]{1,0:T(8,128)(2,1)}, u32[]{:S(2)}) %copy-start.7) | copy-done | bytes 540696
  81.9 1.0 %copy-done.9 = bf16[528,512]{1,0:T(8,128)(2,1)S(1)} copy-done((bf16[528,512]{1,0:T(8,128)(2,1)S(1)}, bf16[528,512]{1,0:T(8,128)(2,1)}, u32[]{:S(2)}) %copy-start.9) | copy-done | bytes 540696
  82.9 1.0 %copy-done.12 = bf16[512,512]{1,0:T(8,128)(2,1)S(1)} copy-done((bf16[512,512]{1,0:T(8,128)(2,1)S(1)}, bf16[512,512]{1,0:T(8,128)(2,1)}, u32[]{:S(2)}) %copy-start.12) | copy-done | bytes 524312
  84.0 1.0 %copy-done.15 = bf16[512,512]{1,0:T(8,128)(2,1)S(1)} copy-done((bf16[512,512]{1,0:T(8,128)(2,1)S(1)}, bf16[512,512]{1,0:T(8,128)(2,1)}, u32[]{:S(2)}) %copy-start.15) | copy-done | bytes 524312
  85.0 5.2 %shard_map.119 = (f32[2,512,512]{2,1,0:T(8,128)}, f32[2,512]{1,0:T(2,128)}, f32[2,512]{1,0:T(2,128)}) custom-call(bf16[2,512,1280]{2,1,0:T(8,128)(2,1)S(1)} %copy-done.1, bf16[512,512]{1,0:T(8,128)(2,1)S(1)} %copy-done.15, bf16[512,512]{1,0:T(8,128)(2,1)S(1)} %copy-done.3, bf16[512,512]{1,0:T(8,128)(2,1)S(1)} %copy-done.12, bf16[528,512]{1,0:T(8,128)(2,1)S(1)} %copy-done.9, ...), custom_call_target="tpu_custom_call" | custom-call | tf_op jit(solution)/shard_map/pallas_call | solution.py:485
  (6 shorter events, 0.0 us)
Async XLA Ops:
  2.9 12.9 %collective-permute-start.1 = (bf16[512,512]{1,0:T(8,128)(2,1)}, bf16[512,512]{1,0:T(8,128)(2,1)S(1)}, u32[]{:S(2)}, u32[]{:S(2)}) collective-permute-start(bf16[512,512]{1,0:T(8,128)(2,1)} %get-tuple-element.11), channel_id=1, source_target_pairs={{1,0},{2,1},{3,2},{4,3},{5,4},{6,5},{7,6},{8,7},{9,8},{10,9},{11,1... | collective-permute-start | bytes 1572872 | tf_op jit(solution)/shard_map/ppermute | solution.py:381
  8.4 13.2 %collective-permute-start = (bf16[512,512]{1,0:T(8,128)(2,1)}, bf16[512,512]{1,0:T(8,128)(2,1)S(1)}, u32[]{:S(2)}, u32[]{:S(2)}) collective-permute-start(bf16[512,512]{1,0:T(8,128)(2,1)} %get-tuple-element.11), channel_id=1, source_target_pairs={{0,1},{1,2},{2,3},{3,4},{4,5},{5,6},{6,7},{7,8},{8,9},{9,10},{10,1... | collective-permute-start | bytes 1572872 | tf_op jit(solution)/shard_map/ppermute | solution.py:381
  8.4 19.4 %all-to-all-start = ((bf16[8,240,128]{2,1,0:T(8,128)(2,1)}), bf16[8,240,128]{2,1,0:T(8,128)(2,1)S(1)}, u32[]{:S(2)}, u32[]{:S(2)}) async-start(bf16[8,240,128]{2,1,0:T(8,128)(2,1)} %get-tuple-element.10.after), calls=%async_computation | async-start | bytes 983040 | tf_op jit(solution)/shard_map/all_to_all | solution.py:407
  11.9 10.5 %copy-start.2 = (bf16[512,512]{1,0:T(8,128)(2,1)S(1)}, bf16[512,512]{1,0:T(8,128)(2,1)}, u32[]{:S(2)}) copy-start(bf16[512,512]{1,0:T(8,128)(2,1)} %uown.1) | copy-start | bytes 1572868
  11.9 10.5 %copy-start.18 = (f32[2,512]{1,0:T(2,128)S(1)}, f32[2,512]{1,0:T(2,128)}, u32[]{:S(2)}) copy-start(f32[2,512]{1,0:T(2,128)} %diag.3) | copy-start | bytes 12292
  15.9 0.8 copy-start.10
  21.6 0.8 copy-start.13
  22.4 1.7 %copy-start = (bf16[2,512,1280]{2,1,0:T(8,128)(2,1)S(1)}, bf16[2,512,1280]{2,1,0:T(8,128)(2,1)}, u32[]{:S(2)}) copy-start(bf16[2,512,1280]{2,1,0:T(8,128)(2,1)} %shard_map.113.w) | copy-start | bytes 7864324
  24.1 1.0 %copy-start.11 = (bf16[512,512]{1,0:T(8,128)(2,1)S(1)}, bf16[512,512]{1,0:T(8,128)(2,1)}, u32[]{:S(2)}) copy-start(bf16[512,512]{1,0:T(8,128)(2,1)} %copy-done.10) | copy-start | bytes 1572868
  25.2 1.0 %copy-start.14 = (bf16[512,512]{1,0:T(8,128)(2,1)S(1)}, bf16[512,512]{1,0:T(8,128)(2,1)}, u32[]{:S(2)}) copy-start(bf16[512,512]{1,0:T(8,128)(2,1)} %copy-done.13) | copy-start | bytes 1572868
  27.7 16.9 %copy-start.16 = (bf16[2,256,32]{1,2,0:T(8,128)(2,1)S(1)}, bf16[2,256,32]{1,2,0:T(8,128)(2,1)}, u32[]{:S(2)}) copy-start(bf16[2,256,32]{1,2,0:T(8,128)(2,1)} %param.15) | copy-start | bytes 98308
  27.8 16.9 %copy-start.17 = (bf16[2,256,32]{1,2,0:T(8,128)(2,1)S(1)}, bf16[2,256,32]{1,2,0:T(8,128)(2,1)}, u32[]{:S(2)}) copy-start(bf16[2,256,32]{1,2,0:T(8,128)(2,1)} %param.16) | copy-start | bytes 98308
  27.8 1.4 %collective-permute-start.2 = (bf16[8,32,128]{2,1,0:T(8,128)(2,1)S(1)}, bf16[8,32,128]{2,1,0:T(8,128)(2,1)S(1)}, u32[]{:S(2)}, u32[]{:S(2)}) collective-permute-start(bf16[8,32,128]{2,1,0:T(8,128)(2,1)S(1)} %shard_map.115.refs_0_), channel_id=1, source_target_pairs={{0,1},{1,0},{2,3},{3,2},{4,5},{5,4},{6,7},{7,6},{8,9},{9,8},{10,11... | collective-permute-start | bytes 196616 | tf_op jit(solution)/shard_map/ppermute | solution.py:413
  46.6 17.3 %collective-permute-start.4 = (bf16[528,512]{1,0:T(8,128)(2,1)S(1)}, bf16[528,512]{1,0:T(8,128)(2,1)S(1)}, u32[]{:S(2)}, u32[]{:S(2)}) collective-permute-start(bf16[528,512]{1,0:T(8,128)(2,1)S(1)} %get-tuple-element.14.own0), channel_id=1, source_target_pairs={{1,0},{2,1},{3,2},{4,3},{5,4},{6,5},{7,6},{8,7},{9,8},{10,9},{11,1... | collective-permute-start | bytes 1622024 | tf_op jit(solution)/shard_map/ppermute | solution.py:381
  47.4 16.5 %collective-permute-start.3 = (bf16[528,512]{1,0:T(8,128)(2,1)S(1)}, bf16[528,512]{1,0:T(8,128)(2,1)S(1)}, u32[]{:S(2)}, u32[]{:S(2)}) collective-permute-start(bf16[528,512]{1,0:T(8,128)(2,1)S(1)} %get-tuple-element.14.own0), channel_id=1, source_target_pairs={{0,1},{1,2},{2,3},{3,4},{4,5},{5,6},{6,7},{7,8},{8,9},{9,10},{10,1... | collective-permute-start | bytes 1622024 | tf_op jit(solution)/shard_map/ppermute | solution.py:381
  47.4 0.8 copy-start.4
  61.9 2.0 %collective-permute-start.7 = (bf16[8,80,128]{2,1,0:T(8,128)(2,1)S(1)}, bf16[8,80,128]{2,1,0:T(8,128)(2,1)S(1)}, u32[]{:S(2)}, u32[]{:S(2)}) collective-permute-start(bf16[8,80,128]{2,1,0:T(8,128)(2,1)S(1)} %all_to_all.21.refs_2_), channel_id=1, source_target_pairs={{0,1},{1,0},{2,3},{3,2},{4,5},{5,4},{6,7},{7,6},{8,9},{9,8},{10,11... | collective-permute-start | bytes 491528 | tf_op jit(solution)/shard_map/ppermute | solution.py:413
  61.9 16.8 %copy-start.1 = (bf16[2,512,1280]{2,1,0:T(8,128)(2,1)S(1)}, bf16[2,512,1280]{2,1,0:T(8,128)(2,1)}, u32[]{:S(2)}) copy-start(bf16[2,512,1280]{2,1,0:T(8,128)(2,1)} %shard_map.113.w) | copy-start | bytes 7864324
  61.9 9.3 %collective-permute-start.6 = (bf16[512,512]{1,0:T(8,128)(2,1)}, bf16[512,512]{1,0:T(8,128)(2,1)}, u32[]{:S(2)}, u32[]{:S(2)}) collective-permute-start(bf16[512,512]{1,0:T(8,128)(2,1)} %get-tuple-element.15.own1), channel_id=1, source_target_pairs={{1,0},{2,1},{3,2},{4,3},{5,4},{6,5},{7,6},{8,7},{9,8},{10,9},{11,1... | collective-permute-start | bytes 1572872 | tf_op jit(solution)/shard_map/ppermute | solution.py:381
  63.9 11.7 %collective-permute-start.5 = (bf16[512,512]{1,0:T(8,128)(2,1)}, bf16[512,512]{1,0:T(8,128)(2,1)}, u32[]{:S(2)}, u32[]{:S(2)}) collective-permute-start(bf16[512,512]{1,0:T(8,128)(2,1)} %get-tuple-element.15.own1), channel_id=1, source_target_pairs={{0,1},{1,2},{2,3},{3,4},{4,5},{5,6},{6,7},{7,8},{8,9},{9,10},{10,1... | collective-permute-start | bytes 1572872 | tf_op jit(solution)/shard_map/ppermute | solution.py:381
  66.2 0.8 copy-start.6
  67.0 0.8 copy-start.8
  67.8 10.9 %all-to-all-start.3 = ((bf16[8,80,128]{2,1,0:T(8,128)(2,1)}), bf16[8,80,128]{2,1,0:T(8,128)(2,1)S(1)}, u32[]{:S(2)}, u32[]{:S(2)}) async-start(bf16[8,80,128]{2,1,0:T(8,128)(2,1)} %shard_map.118), calls=%async_computation.3 | async-start | bytes 327680 | tf_op jit(solution)/shard_map/all_to_all | solution.py:407
  78.7 1.0 %copy-start.3 = (bf16[512,512]{1,0:T(8,128)(2,1)S(1)}, bf16[512,512]{1,0:T(8,128)(2,1)}, u32[]{:S(2)}) copy-start(bf16[512,512]{1,0:T(8,128)(2,1)} %uown.1) | copy-start | bytes 1572868
  79.8 1.0 %copy-start.5 = (bf16[528,512]{1,0:T(8,128)(2,1)S(1)}, bf16[528,512]{1,0:T(8,128)(2,1)}, u32[]{:S(2)}) copy-start(bf16[528,512]{1,0:T(8,128)(2,1)} %copy-done.4) | copy-start | bytes 1622020
  80.8 1.0 %copy-start.7 = (bf16[528,512]{1,0:T(8,128)(2,1)S(1)}, bf16[528,512]{1,0:T(8,128)(2,1)}, u32[]{:S(2)}) copy-start(bf16[528,512]{1,0:T(8,128)(2,1)} %copy-done.6) | copy-start | bytes 1622020
  81.9 1.0 %copy-start.9 = (bf16[528,512]{1,0:T(8,128)(2,1)S(1)}, bf16[528,512]{1,0:T(8,128)(2,1)}, u32[]{:S(2)}) copy-start(bf16[528,512]{1,0:T(8,128)(2,1)} %copy-done.8) | copy-start | bytes 1622020
  82.9 1.0 %copy-start.12 = (bf16[512,512]{1,0:T(8,128)(2,1)S(1)}, bf16[512,512]{1,0:T(8,128)(2,1)}, u32[]{:S(2)}) copy-start(bf16[512,512]{1,0:T(8,128)(2,1)} %copy-done.10) | copy-start | bytes 1572868
  84.0 1.0 %copy-start.15 = (bf16[512,512]{1,0:T(8,128)(2,1)S(1)}, bf16[512,512]{1,0:T(8,128)(2,1)}, u32[]{:S(2)}) copy-start(bf16[512,512]{1,0:T(8,128)(2,1)} %copy-done.13) | copy-start | bytes 1572868

commit v20 on v18

--- a/solution.py
+++ b/solution.py
@@ -156,7 +156,7 @@
     return pl.multiple_of(lax.rem(group[0] + (groups - m), groups) * step, step)
 
 
-def first_couple(ops, rank, far, cols, group, held, *refs):
+def first_couple(ops, rank, far, cols, group, after, held, *refs):
     parts, (out, zs) = refs[:-2], refs[-2:]
     step = SLICES * 2 * rank
     for m, part in enumerate(parts):
@@ -484,9 +484,9 @@
     c1 = call(
         functools.partial(first_couple, ops, rank, far),
         sds((SLICES, body, LANES), BF16),
-        [SMEM, SMEM] + [VMEM] * (1 + count),
+        [SMEM, SMEM, ANY] + [VMEM] * (1 + count),
         [pltpu.VMEM((n * blocks * rank, LANES), BF16)],
-    )(cols, group, held, *z1)
+    )(cols, group, image, held, *z1)
     c1 = exchange(c1)
 
     first, second, msg = call(

time: 83 us -> 83 us (level)
    unnamed x16 -> x18, local copies, waits for them, and re-layouts: 4.68 us -> 4.67 us
where the time goes in v20:
time: 83 us; the launch traced here: 82.6 us
  blocking collectives  40.8 us (49%)
  Pallas kernels  16.6 us (20%)
  starting transfers between devices  12.7 us (15%)
  waiting for transfers between devices  7.01 us (8%)
  local copies, waits for them, and re-layouts  4.75 us (6%)
    all_to_all x3, blocking collectives, exchange(): lax.all_to_all(x, 'store', 0, 0, axis_index_groups=groups, tiled=True)  40.8 us
    ppermute x3, starting transfers between devices, ring(): lax.ppermute(block, 'store', backward)  8.26 us
    ppermute x3, waiting for transfers between devices, ring(): lax.ppermute(block, 'store', forward)  5.74 us
    unnamed x18, local copies, waits for them, and re-layouts  4.67 us
    all_to_all x1, starting transfers between devices, exchange(): lax.all_to_all(x, 'store', 0, 0, axis_index_groups=groups, tiled=True)  3.48 us
    pallas_call x1, Pallas kernels, shards(): call(functools.partial(order_tiles, all_blocks), sds((blocks, ops * size,...  3.48 us
    pallas_call x1, Pallas kernels, shards(): call(final_first, [outs, sds((ops, columns), F32), sds((ops, columns), F3...  2.87 us
    pallas_call x1, Pallas kernels, shards(): call(functools.partial(coeff_kernel, count), [sds((SLICES, shared + STATS...  2.33 us
  transfers between devices with their start and end apart: 9, of which 3 were waited for; matrix products, arithmetic and copies ran while one was open for 0% of the time, Pallas kernels for 11%

profile of v20, /device:TPU:0, one launch (start us, length us, event | category | flops | bytes accessed | tf_op | source)
XLA Modules:
  0.0 82.6 jit_solution(5564757071710725670)
XLA Ops:
  0.6 2.3 %shard_map.112 = (bf16[8,240,128]{2,1,0:T(8,128)(2,1)}, bf16[512,512]{1,0:T(8,128)(2,1)}) custom-call(s32[2,6]{1,0:T(2,128)} %far_cols.1, bf16[512,512]{1,0:T(8,128)(2,1)} %uown.3, bf16[2,32,256]{2,1,0:T(8,128)(2,1)} %bitcast.7, bf16[2,2,6,32,32]{4,3,2,1,0:T(8,128)(2,1)} %coup.1), custom_call_target="tpu_custom_call" | custom-call | tf_op jit(solution)/shard_map/pallas_call | solution.py:460
  3.0 5.4 %collective-permute-start.1 = (bf16[512,512]{1,0:T(8,128)(2,1)}, bf16[512,512]{1,0:T(8,128)(2,1)S(1)}, u32[]{:S(2)}, u32[]{:S(2)}) collective-permute-start(bf16[512,512]{1,0:T(8,128)(2,1)} %get-tuple-element.15), channel_id=1, source_target_pairs={{1,0},{2,1},{3,2},{4,3},{5,4},{6,5},{7,6},{8,7},{9,8},{10,9},{11,1... | collective-permute-start | bytes 1572872 | tf_op jit(solution)/shard_map/ppermute | solution.py:418
  8.4 0.0 collective-permute-start
  8.4 3.5 %all-to-all-start = ((bf16[8,240,128]{2,1,0:T(8,128)(2,1)}), bf16[8,240,128]{2,1,0:T(8,128)(2,1)S(1)}, u32[]{:S(2)}, u32[]{:S(2)}) async-start(bf16[8,240,128]{2,1,0:T(8,128)(2,1)} %get-tuple-element.14.after), calls=%async_computation | async-start | bytes 983040 | tf_op jit(solution)/shard_map/all_to_all | solution.py:444
  11.9 0.0 copy-start.2
  11.9 0.0 copy-start.8
  11.9 3.5 %shard_map.113.w = bf16[2,512,1280]{2,1,0:T(8,128)(2,1)} custom-call(s32[2,5]{1,0:T(2,128)} %cols.1, s32[2]{0:T(128)} %count.1, s32[1]{0:T(128)} %bitcast.row0, bf16[2,2,5,256,256]{4,3,2,1,0:T(8,128)(2,1)} %tiles.1, bf16[8,240,128]{2,1,0:T(8,128)(2,1)} %get-tuple-element.14.after), custom_call_target="tpu_custom_call" | custom-call | tf_op jit(solution)/shard_map/pallas_call | solution.py:470
  15.4 0.5 collective-permute-done.1.high.uhigh
  15.9 5.7 %collective-permute-done.low.ulow = bf16[512,512]{1,0:T(8,128)(2,1)S(1)} collective-permute-done((bf16[512,512]{1,0:T(8,128)(2,1)}, bf16[512,512]{1,0:T(8,128)(2,1)S(1)}, u32[]{:S(2)}, u32[]{:S(2)}) %collective-permute-start) | collective-permute-done | bytes 524320 | tf_op jit(solution)/shard_map/ppermute | solution.py:418
  21.6 0.0 copy-done.2
  21.6 0.0 copy-done.8
  21.6 0.0 copy-start
  21.6 1.7 %copy-done = bf16[2,512,1280]{2,1,0:T(8,128)(2,1)S(1)} copy-done((bf16[2,512,1280]{2,1,0:T(8,128)(2,1)S(1)}, bf16[2,512,1280]{2,1,0:T(8,128)(2,1)}, u32[]{:S(2)}) %copy-start) | copy-done | bytes 2621464
  23.3 1.5 %shard_map.114 = (f32[2,512,512]{2,1,0:T(8,128)S(1)}, f32[8,128]{1,0:T(8,128)S(1)}) custom-call(bf16[2,512,1280]{2,1,0:T(8,128)(2,1)S(1)} %copy-done, bf16[512,512]{1,0:T(8,128)(2,1)S(1)} %collective-permute-done.low.ulow, bf16[512,512]{1,0:T(8,128)(2,1)S(1)} %copy-done.2, bf16[512,512]{1,0:T(8,128)(2,1)S(1)} %collective-permute-done.1.high.uhigh, ...), custom_call_target="tpu_custom_call" | custom-call | flops 11500000256 | tf_op jit(solution)/shard_map/pallas_call | solution.py:476
  24.9 0.0 copy-start.3
  24.9 1.3 %copy-done.3 = f32[2,512,512]{2,1,0:T(8,128)} copy-done((f32[2,512,512]{2,1,0:T(8,128)}, f32[2,512,512]{2,1,0:T(8,128)S(1)}, u32[]{:S(2)}) %copy-start.3) | copy-done | bytes 2097176
  26.2 0.0 copy-start.6
  26.2 0.0 copy-start.7
  26.2 0.0 all-to-all-done.held
  26.2 0.9 %collective-permute-start.2 = (bf16[8,32,128]{2,1,0:T(8,128)(2,1)S(1)}, bf16[8,32,128]{2,1,0:T(8,128)(2,1)S(1)}, u32[]{:S(2)}, u32[]{:S(2)}) collective-permute-start(bf16[8,32,128]{2,1,0:T(8,128)(2,1)S(1)} %shard_map.115.refs_0_), channel_id=1, source_target_pairs={{0,1},{1,0},{2,3},{3,2},{4,5},{5,4},{6,7},{7,6},{8,9},{9,8},{10,11... | collective-permute-start | bytes 196616 | tf_op jit(solution)/shard_map/ppermute | solution.py:450
  27.1 0.1 reshape.18.cols
  27.2 0.8 collective-permute-done.2.refs_1_
  28.0 0.0 copy-start.4
  28.0 1.6 %copy-done.4 = f32[2,512,512]{2,1,0:T(8,128)S(1)} copy-done((f32[2,512,512]{2,1,0:T(8,128)S(1)}, f32[2,512,512]{2,1,0:T(8,128)}, u32[]{:S(2)}) %copy-start.4) | copy-done | bytes 2097176
  29.6 0.0 copy-start.5
  29.6 1.1 %shard_map.116 = bf16[8,64,128]{2,1,0:T(8,128)(2,1)S(1)} custom-call(s32[96]{0:T(128)S(1)} %reshape.18.cols, s32[1]{0:T(128)} %bitcast.3.group, f32[2,512,512]{2,1,0:T(8,128)S(1)} %copy-done.4, bf16[8,240,128]{2,1,0:T(8,128)(2,1)S(1)} %all-to-all-done.held, bf16[8,32,128]{2,1,0:T(8,128)(2,1)S(1)} %shard_map.115.refs_0_, ...), custom_call_target="tpu_custom_call" | custom-call | tf_op jit(solution)/shard_map/pallas_call | solution.py:484
  30.7 13.3 %all_to_all.20.cmsg = bf16[8,64,128]{2,1,0:T(8,128)(2,1)S(1)} all-to-all(bf16[8,64,128]{2,1,0:T(8,128)(2,1)S(1)} %shard_map.116), channel_id=1, replica_groups={{0,2,4,6,8,10,12,14},{1,3,5,7,9,11,13,15},{16,18,20,22,24,26,28,30},{17..., dimensions={0} | all-to-all | bytes 262144 | tf_op jit(solution)/shard_map/all_to_all | solution.py:444
  44.1 0.0 copy-done.6
  44.1 0.0 copy-done.7
  44.1 0.0 copy-done.5
  44.1 1.5 %shard_map.117 = (bf16[528,512]{1,0:T(8,128)(2,1)S(1)}, bf16[512,512]{1,0:T(8,128)(2,1)S(1)}, bf16[8,80,128]{2,1,0:T(8,128)(2,1)S(1)}) custom-call(bf16[512,512]{1,0:T(8,128)(2,1)S(1)} %copy-done.2, f32[2,512,512]{2,1,0:T(8,128)S(1)} %copy-done.5, bf16[2,32,256]{2,1,0:T(8,128)(2,1)S(1)} %bitcast.4, bf16[2,32,256]{2,1,0:T(8,128)(2,1)S(1)} %bitcast.8, ...), custom_call_target="tpu_custom_call" | custom-call | flops 2300000000 | tf_op jit(solution)/shard_map/pallas_call | solution.py:492
  45.6 0.8 collective-permute-start.4
  46.4 0.0 collective-permute-start.3
  46.4 14.5 %all_to_all.21.refs_2_ = bf16[8,80,128]{2,1,0:T(8,128)(2,1)S(1)} all-to-all(bf16[8,80,128]{2,1,0:T(8,128)(2,1)S(1)} %get-tuple-element.19), channel_id=1, replica_groups={{0,2,4,6,8,10,12,14},{1,3,5,7,9,11,13,15},{16,18,20,22,24,26,28,30},{17..., dimensions={0} | all-to-all | bytes 327680 | tf_op jit(solution)/shard_map/all_to_all | solution.py:444
  60.9 0.0 collective-permute-start.5
  60.9 2.0 %collective-permute-start.7 = (bf16[512,512]{1,0:T(8,128)(2,1)S(1)}, bf16[512,512]{1,0:T(8,128)(2,1)S(1)}, u32[]{:S(2)}, u32[]{:S(2)}) collective-permute-start(bf16[512,512]{1,0:T(8,128)(2,1)S(1)} %get-tuple-element.21.vown), channel_id=1, source_target_pairs={{1,0},{2,1},{3,2},{4,3},{5,4},{6,5},{7,6},{8,7},{9,8},{10,9},{11,1... | collective-permute-start | bytes 1572872 | tf_op jit(solution)/shard_map/ppermute | solution.py:418
  62.9 0.0 collective-permute-start.6
  63.0 0.0 collective-permute-done.5.refs_3_
  63.0 0.0 collective-permute-done.4.after_high.vhigh
  63.0 0.0 collective-permute-done.3.after_low.vlow
  63.0 0.0 copy-start.1
  63.0 1.6 %shard_map.118 = bf16[8,80,128]{2,1,0:T(8,128)(2,1)S(1)} custom-call(s32[96]{0:T(128)S(1)} %reshape.18.cols, s32[1]{0:T(128)} %bitcast.3.group, bf16[528,512]{1,0:T(8,128)(2,1)S(1)} %collective-permute-done.3.after_low.vlow, bf16[528,512]{1,0:T(8,128)(2,1)S(1)} %collective-permute-done.4.after_high.vhigh, bf16[8,240,128]{2,1,0:T(8,128)(2,1)S(1)} %all-to-all-done.held, ...), custom_call_target="tpu_custom_call" | custom-call | flops 34500001792 | tf_op jit(solution)/shard_map/pallas_call | solution.py:510
  64.6 13.0 %all_to_all.22.cmsg = bf16[8,80,128]{2,1,0:T(8,128)(2,1)S(1)} all-to-all(bf16[8,80,128]{2,1,0:T(8,128)(2,1)S(1)} %shard_map.118), channel_id=1, replica_groups={{0,2,4,6,8,10,12,14},{1,3,5,7,9,11,13,15},{16,18,20,22,24,26,28,30},{17..., dimensions={0} | all-to-all | bytes 327680 | tf_op jit(solution)/shard_map/all_to_all | solution.py:444
  77.6 0.0 copy-done.1
  77.6 2.9 %shard_map.119 = (f32[2,512,512]{2,1,0:T(8,128)}, f32[2,512]{1,0:T(2,128)}, f32[2,512]{1,0:T(2,128)}, f32[8,512]{1,0:T(8,128)S(1)}) custom-call(bf16[2,512,1280]{2,1,0:T(8,128)(2,1)S(1)} %copy-done.1, bf16[512,512]{1,0:T(8,128)(2,1)S(1)} %collective-permute-done.low.ulow, bf16[512,512]{1,0:T(8,128)(2,1)S(1)} %copy-done.2, ...), custom_call_target="tpu_custom_call" | custom-call | tf_op jit(solution)/shard_map/pallas_call | solution.py:528
  80.4 0.0 collective-permute-done.7.vhigh
  80.5 0.0 collective-permute-done.6.vlow
  80.5 2.2 %shard_map.120 = f32[2,512,512]{2,1,0:T(8,128)} custom-call(f32[2,512,512]{2,1,0:T(8,128)} %get-tuple-element.20.begun, bf16[2,512,1280]{2,1,0:T(8,128)(2,1)S(1)} %copy-done.1, bf16[512,512]{1,0:T(8,128)(2,1)S(1)} %collective-permute-done.low.ulow, bf16[512,512]{1,0:T(8,128)(2,1)S(1)} %copy-done.2, ...), custom_call_target="tpu_custom_call", output_to_operand_aliasing={{}: (0, {})} | custom-call | tf_op jit(solution)/shard_map/pallas_call | solution.py:535
  (2 shorter events, 0.0 us)
Async XLA Ops:
  3.0 12.9 %collective-permute-start.1 = (bf16[512,512]{1,0:T(8,128)(2,1)}, bf16[512,512]{1,0:T(8,128)(2,1)S(1)}, u32[]{:S(2)}, u32[]{:S(2)}) collective-permute-start(bf16[512,512]{1,0:T(8,128)(2,1)} %get-tuple-element.15), channel_id=1, source_target_pairs={{1,0},{2,1},{3,2},{4,3},{5,4},{6,5},{7,6},{8,7},{9,8},{10,9},{11,1... | collective-permute-start | bytes 1572872 | tf_op jit(solution)/shard_map/ppermute | solution.py:418
  8.4 13.2 %collective-permute-start = (bf16[512,512]{1,0:T(8,128)(2,1)}, bf16[512,512]{1,0:T(8,128)(2,1)S(1)}, u32[]{:S(2)}, u32[]{:S(2)}) collective-permute-start(bf16[512,512]{1,0:T(8,128)(2,1)} %get-tuple-element.15), channel_id=1, source_target_pairs={{0,1},{1,2},{2,3},{3,4},{4,5},{5,6},{6,7},{7,8},{8,9},{9,10},{10,1... | collective-permute-start | bytes 1572872 | tf_op jit(solution)/shard_map/ppermute | solution.py:418
  8.4 17.8 %all-to-all-start = ((bf16[8,240,128]{2,1,0:T(8,128)(2,1)}), bf16[8,240,128]{2,1,0:T(8,128)(2,1)S(1)}, u32[]{:S(2)}, u32[]{:S(2)}) async-start(bf16[8,240,128]{2,1,0:T(8,128)(2,1)} %get-tuple-element.14.after), calls=%async_computation | async-start | bytes 983040 | tf_op jit(solution)/shard_map/all_to_all | solution.py:444
  11.9 9.7 %copy-start.2 = (bf16[512,512]{1,0:T(8,128)(2,1)S(1)}, bf16[512,512]{1,0:T(8,128)(2,1)}, u32[]{:S(2)}) copy-start(bf16[512,512]{1,0:T(8,128)(2,1)} %uown.3) | copy-start | bytes 1572868
  11.9 9.7 %copy-start.8 = (f32[2,512]{1,0:T(2,128)S(1)}, f32[2,512]{1,0:T(2,128)}, u32[]{:S(2)}) copy-start(f32[2,512]{1,0:T(2,128)} %diag.5) | copy-start | bytes 12292
  21.6 1.7 %copy-start = (bf16[2,512,1280]{2,1,0:T(8,128)(2,1)S(1)}, bf16[2,512,1280]{2,1,0:T(8,128)(2,1)}, u32[]{:S(2)}) copy-start(bf16[2,512,1280]{2,1,0:T(8,128)(2,1)} %shard_map.113.w) | copy-start | bytes 7864324
  24.9 1.3 %copy-start.3 = (f32[2,512,512]{2,1,0:T(8,128)}, f32[2,512,512]{2,1,0:T(8,128)S(1)}, u32[]{:S(2)}) copy-start(f32[2,512,512]{2,1,0:T(8,128)S(1)} %get-tuple-element.16.after.near) | copy-start | bytes 6291460
  26.2 17.9 %copy-start.6 = (bf16[2,256,32]{1,2,0:T(8,128)(2,1)S(1)}, bf16[2,256,32]{1,2,0:T(8,128)(2,1)}, u32[]{:S(2)}) copy-start(bf16[2,256,32]{1,2,0:T(8,128)(2,1)} %param.15) | copy-start | bytes 98308
  26.2 17.9 %copy-start.7 = (bf16[2,256,32]{1,2,0:T(8,128)(2,1)S(1)}, bf16[2,256,32]{1,2,0:T(8,128)(2,1)}, u32[]{:S(2)}) copy-start(bf16[2,256,32]{1,2,0:T(8,128)(2,1)} %param.16) | copy-start | bytes 98308
  26.2 1.8 %collective-permute-start.2 = (bf16[8,32,128]{2,1,0:T(8,128)(2,1)S(1)}, bf16[8,32,128]{2,1,0:T(8,128)(2,1)S(1)}, u32[]{:S(2)}, u32[]{:S(2)}) collective-permute-start(bf16[8,32,128]{2,1,0:T(8,128)(2,1)S(1)} %shard_map.115.refs_0_), channel_id=1, source_target_pairs={{0,1},{1,0},{2,3},{3,2},{4,5},{5,4},{6,7},{7,6},{8,9},{9,8},{10,11... | collective-permute-start | bytes 196616 | tf_op jit(solution)/shard_map/ppermute | solution.py:450
  28.0 1.6 %copy-start.4 = (f32[2,512,512]{2,1,0:T(8,128)S(1)}, f32[2,512,512]{2,1,0:T(8,128)}, u32[]{:S(2)}) copy-start(f32[2,512,512]{2,1,0:T(8,128)} %copy-done.3) | copy-start | bytes 6291460
  29.6 14.5 %copy-start.5 = (f32[2,512,512]{2,1,0:T(8,128)S(1)}, f32[2,512,512]{2,1,0:T(8,128)}, u32[]{:S(2)}) copy-start(f32[2,512,512]{2,1,0:T(8,128)} %copy-done.3) | copy-start | bytes 6291460
  45.6 17.4 %collective-permute-start.4 = (bf16[528,512]{1,0:T(8,128)(2,1)S(1)}, bf16[528,512]{1,0:T(8,128)(2,1)S(1)}, u32[]{:S(2)}, u32[]{:S(2)}) collective-permute-start(bf16[528,512]{1,0:T(8,128)(2,1)S(1)} %get-tuple-element.18.vown), channel_id=1, source_target_pairs={{1,0},{2,1},{3,2},{4,3},{5,4},{6,5},{7,6},{8,7},{9,8},{10,9},{11,1... | collective-permute-start | bytes 1622024 | tf_op jit(solution)/shard_map/ppermute | solution.py:418
  46.4 16.6 %collective-permute-start.3 = (bf16[528,512]{1,0:T(8,128)(2,1)S(1)}, bf16[528,512]{1,0:T(8,128)(2,1)S(1)}, u32[]{:S(2)}, u32[]{:S(2)}) collective-permute-start(bf16[528,512]{1,0:T(8,128)(2,1)S(1)} %get-tuple-element.18.vown), channel_id=1, source_target_pairs={{0,1},{1,2},{2,3},{3,4},{4,5},{5,6},{6,7},{7,8},{8,9},{9,10},{10,1... | collective-permute-start | bytes 1622024 | tf_op jit(solution)/shard_map/ppermute | solution.py:418
  60.9 2.1 %collective-permute-start.5 = (bf16[8,80,128]{2,1,0:T(8,128)(2,1)S(1)}, bf16[8,80,128]{2,1,0:T(8,128)(2,1)S(1)}, u32[]{:S(2)}, u32[]{:S(2)}) collective-permute-start(bf16[8,80,128]{2,1,0:T(8,128)(2,1)S(1)} %all_to_all.21.refs_2_), channel_id=1, source_target_pairs={{0,1},{1,0},{2,3},{3,2},{4,5},{5,4},{6,7},{7,6},{8,9},{9,8},{10,11... | collective-permute-start | bytes 491528 | tf_op jit(solution)/shard_map/ppermute | solution.py:450
  60.9 19.5 %collective-permute-start.7 = (bf16[512,512]{1,0:T(8,128)(2,1)S(1)}, bf16[512,512]{1,0:T(8,128)(2,1)S(1)}, u32[]{:S(2)}, u32[]{:S(2)}) collective-permute-start(bf16[512,512]{1,0:T(8,128)(2,1)S(1)} %get-tuple-element.21.vown), channel_id=1, source_target_pairs={{1,0},{2,1},{3,2},{4,3},{5,4},{6,5},{7,6},{8,7},{9,8},{10,9},{11,1... | collective-permute-start | bytes 1572872 | tf_op jit(solution)/shard_map/ppermute | solution.py:418
  62.9 17.5 %collective-permute-start.6 = (bf16[512,512]{1,0:T(8,128)(2,1)S(1)}, bf16[512,512]{1,0:T(8,128)(2,1)S(1)}, u32[]{:S(2)}, u32[]{:S(2)}) collective-permute-start(bf16[512,512]{1,0:T(8,128)(2,1)S(1)} %get-tuple-element.21.vown), channel_id=1, source_target_pairs={{0,1},{1,2},{2,3},{3,4},{4,5},{5,6},{6,7},{7,8},{8,9},{9,10},{10,1... | collective-permute-start | bytes 1572872 | tf_op jit(solution)/shard_map/ppermute | solution.py:418
  63.0 14.6 %copy-start.1 = (bf16[2,512,1280]{2,1,0:T(8,128)(2,1)S(1)}, bf16[2,512,1280]{2,1,0:T(8,128)(2,1)}, u32[]{:S(2)}) copy-start(bf16[2,512,1280]{2,1,0:T(8,128)(2,1)} %shard_map.113.w) | copy-start | bytes 7864324

commit v21 on v18

--- a/solution.py
+++ b/solution.py
@@ -199,22 +199,37 @@
     return jnp.concatenate([column] * (columns // LANES), axis=1)
 
 
-def near_kernel(w, low, own, high, diag, image, token):
+def ratio(inner, squares):
+    good = squares > 0
+    return jnp.where(good, inner / jnp.where(good, squares, 1.0), 0.0)
+
+
+def near_kernel(w, low, own, high, diag, image, token, early):
     token[...] = jnp.zeros_like(token)
     ops, rows, columns = image.shape
     size = w.shape[1] // ops
     blocks = rows // size
+    squares, inner = 0.0, 0.0
     for b in range(blocks):
         product = near_product(w.at[b], (low, own, high), b, blocks, size)
         here = slice(b * size, (b + 1) * size)
         ub = own[here, :].astype(F32)
+        squares = squares + jnp.sum(ub * ub, axis=0, keepdims=True)
         for o in range(ops):
-            image[o, here, :] = (
-                product[o * size:(o + 1) * size] + diagonal_of(diag, o, b, size, columns) * ub
-            )
-
-
-def image_kernel(own, near, left, right, cmsg, out0, out1, mout, image, coef):
+            value = product[o * size:(o + 1) * size] + diagonal_of(diag, o, b, size, columns) * ub
+            image[o, here, :] = value
+            if o == 0:
+                inner = inner + jnp.sum(ub * value, axis=0, keepdims=True)
+    pieces = split3(ratio(inner, squares))
+    shift = sum(x.astype(F32) for x in pieces)
+    early[0:rows, :] = (image[0] - shift * own[...].astype(F32)).astype(BF16)
+    zero = jnp.zeros_like(pieces[0])
+    early[rows:, :] = jnp.concatenate(pieces + [zero] * (STATS - len(pieces)), axis=0)
+
+
+def image_kernel(
+    own, near, left, right, cmsg, after_low, after_high, out0, half0, half1, mout, image, coef
+):
     ops = image.shape[0]
     blocks, rank, size = right.shape
     rows, columns = own.shape
@@ -248,7 +263,10 @@
             part = jnp.sum(v * v, axis=0, keepdims=True)
             spread = part if spread is None else spread + part
             v = v.astype(BF16)
-            (out0, out1)[o][b * size:(b + 1) * size, :] = v
+            if o == 0:
+                out0[b * size:(b + 1) * size, :] = v
+            else:
+                (half0, half1)[b][0:size, :] = v
             z.append(dot(right[b], v))
         for pair in range(SLICES // 2):
             first, second = halves(chunk(z[0], pair), chunk(z[1], pair))
@@ -256,7 +274,13 @@
             mout[2 * pair + 1, o * rank:(o + 1) * rank, :] = second.astype(BF16)
         spreads.append(spread)
     zero = jnp.zeros((1, columns), BF16)
-    out0[rows:, :] = jnp.concatenate(stats + [zero] * (STATS - len(stats)), axis=0)
+    edge = jnp.concatenate(stats + [zero] * (STATS - len(stats)), axis=0)
+    out0[rows:, :] = edge
+    half1[size:, :] = edge
+    at = size + blocks * rank
+    for b in range(blocks):
+        half0[size + b * rank:size + (b + 1) * rank, :] = coef[b, 0:rank, :]
+        half0[at:at + rank, b * size:(b + 1) * size] = left[b]
     stats += split3(squares)
     for spread in spreads:
         stats += split3(spread)
@@ -310,14 +334,16 @@
         out[s, body:body + STATS, :] = rows
 
 
-def apply_second(o, factor, changes, u3, v3, w, diag, left, cmsg, images, ext, coef, out, sems):
+def apply_second(o, factor, changes, u3, value_of, w, diag, left, cmsg, images, ext, coef, out, sems):
     blocks, rank, size = left.shape
-    rows, columns = u3[1].shape
     ops = w.shape[1] // size
+    columns = u3[1].shape[1]
     take_coefs(cmsg, coef, ops * rank)
-    for at, (u, v) in enumerate(zip(u3, v3)):
-        value = v[0:rows, :].astype(F32) * factor + u[...].astype(F32) * changes[at]
-        ext[at] = value.astype(BF16)
+    for at, u in enumerate(u3):
+        for b in range(blocks):
+            here = slice(b * size, (b + 1) * size)
+            value = value_of(at, b) * factor + u[here, :].astype(F32) * changes[at]
+            ext[at, here, :] = value.astype(BF16)
     copies = []
     for b in range(blocks):
         parts = [ext.at[at] for at in range(3)]
@@ -340,9 +366,11 @@
     ulow,
     uown,
     uhigh,
-    vlow,
-    vown,
-    vhigh,
+    elow,
+    own0,
+    ehigh,
+    halflow,
+    halfhigh,
     diag,
     left,
     cmsg,
@@ -367,24 +395,40 @@
         )[0]
     st = stat[...]
     reverse = row3(st, 2 * ops)
-    scales = []
+    own_edge = own0[rows:, :].astype(F32)
     for o in range(ops):
         height = row3(st, o)
         norm = row3(st, ops + o)
         heights[o:o + 1, :] = height
         norms[o:o + 1, :] = norm
-        factor = reverse / norm
-        changes = [
-            (row3(v[rows:, :].astype(F32), o) - height) * factor for v in (vlow, vown, vhigh)
-        ]
-        scales.append((factor, changes))
-    factor, changes = scales[1]
-    aux[0:1, :] = factor
-    for at in range(3):
-        aux[1 + at:2 + at, :] = changes[at]
-    factor, changes = scales[0]
-    u3, v3 = (ulow, uown, uhigh), (vlow, vown, vhigh)
-    apply_second(0, factor, changes, u3, v3, w, diag, left, cmsg, images, ext, coef, out, sems)
+        if o == 1:
+            aux[0:1, :] = reverse / norm
+            aux[1:2, :] = height
+            aux[2:3, :] = row3(own_edge, 1)
+    height = row3(st, 0)
+    factor = reverse / row3(st, ops)
+    changes = [
+        (row3(edge, 0) - height) * factor
+        for edge in (elow[rows:, :].astype(F32), own_edge, ehigh[rows:, :].astype(F32))
+    ]
+
+    def value_of(at, b):
+        here = slice(b * size, (b + 1) * size)
+        if at == 1:
+            return own0[here, :].astype(F32)
+        v, half = (elow, halflow) if at == 0 else (ehigh, halfhigh)
+        start = size + blocks * rank
+        far = dot(
+            half[start:start + rank, here],
+            half[size + b * rank:size + (b + 1) * rank, :],
+            ((0,), (0,)),
+        )
+        return v[here, :].astype(F32) + far.astype(BF16).astype(F32)
+
+    u3 = (ulow, uown, uhigh)
+    apply_second(
+        0, factor, changes, u3, value_of, w, diag, left, cmsg, images, ext, coef, out, sems
+    )
 
 
 def final_second(
@@ -393,9 +437,12 @@
     ulow,
     uown,
     uhigh,
-    vlow,
-    vown,
-    vhigh,
+    low0,
+    own0,
+    high0,
+    low1,
+    own1,
+    high1,
     diag,
     left,
     cmsg,
@@ -406,9 +453,25 @@
     out,
     sems,
 ):
-    factor, changes = aux[0:1, :], [aux[1 + at:2 + at, :] for at in range(3)]
-    u3, v3 = (ulow, uown, uhigh), (vlow, vown, vhigh)
-    apply_second(1, factor, changes, u3, v3, w, diag, left, cmsg, images, ext, coef, out, sems)
+    size = left.shape[2]
+    factor, height = aux[0:1, :], aux[1:2, :]
+    changes = [
+        (edge - height) * factor
+        for edge in (
+            row3(low1[size:, :].astype(F32), 1),
+            aux[2:3, :],
+            row3(high1[size:, :].astype(F32), 1),
+        )
+    ]
+    pieces = ((low0, low1), (own0, own1), (high0, high1))
+
+    def value_of(at, b):
+        return pieces[at][b][0:size, :].astype(F32)
+
+    u3 = (ulow, uown, uhigh)
+    apply_second(
+        1, factor, changes, u3, value_of, w, diag, left, cmsg, images, ext, coef, out, sems
+    )
 
 
 def ring(block):
@@ -473,12 +536,17 @@
         [SMEM, SMEM, SMEM, VMEM, ANY],
         megabytes=60,
     )(near_cols, near_count, row0, near_tiles, mine)
-    image, token = call(
+    image, token, early = call(
         near_kernel,
-        [sds((ops, rows, columns), F32), sds((8, LANES), F32)],
+        [
+            sds((ops, rows, columns), F32),
+            sds((8, LANES), F32),
+            sds((rows + STATS, columns), BF16),
+        ],
         [VMEM] * 5,
         micros=10.0,
     )(w, low, sources, high, self_terms)
+    elow, ehigh = ring(early)
     z1 = across(call(take_kernel, sds((SLICES, rank, LANES), BF16), [VMEM, ANY])(held, token))
 
     c1 = call(
@@ -486,25 +554,27 @@
         sds((SLICES, body, LANES), BF16),
         [SMEM, SMEM] + [VMEM] * (1 + count),
         [pltpu.VMEM((n * blocks * rank, LANES), BF16)],
+        micros=30.0,
     )(cols, group, held, *z1)
     c1 = exchange(c1)
 
-    first, second, msg = call(
+    own0, half0, half1, msg = call(
         image_kernel,
         [
             sds((rows + STATS, columns), BF16),
-            sds((rows, columns), BF16),
+            sds((size + (blocks + 1) * rank, columns), BF16),
+            sds((size + STATS, columns), BF16),
             sds((SLICES, body + STATS, LANES), BF16),
         ],
-        [VMEM] * 5,
+        [VMEM] * 5 + [ANY] * 2,
         [
             pltpu.VMEM((ops, rows, columns), F32),
             pltpu.VMEM((blocks, body, columns), BF16),
         ],
         micros=2.0,
-    )(sources, image, left, right, c1)
-    low0, high0 = ring(first)
-    low1, high1 = ring(second)
+    )(sources, image, left, right, c1, elow, ehigh)
+    low0, high0 = ring(half0)
+    low1, high1 = ring(half1)
     msgs = across(exchange(msg))
 
     c2 = call(
@@ -528,18 +598,34 @@
     images, heights, norms, aux = call(
         final_first,
         [outs, sds((ops, columns), F32), sds((ops, columns), F32), sds((8, columns), F32)],
-        [VMEM] * 10,
+        [VMEM] * 12,
         scratch + [pltpu.VMEM((STATS, columns), F32), pltpu.SemaphoreType.DMA((blocks,))],
         out_specs=[ANY, VMEM, VMEM, VMEM],
-    )(w, low, sources, high, low0, first, high0, self_terms, left, c2)
+    )(w, low, sources, high, elow, own0, ehigh, low0, high0, self_terms, left, c2)
     images = call(
         final_second,
         outs,
-        [ANY] + [VMEM] * 11,
+        [ANY] + [VMEM] * 14,
         scratch + [pltpu.SemaphoreType.DMA((blocks,))],
         out_specs=ANY,
         alias={0: 0},
-    )(images, w, low, sources, high, low1, second, high1, self_terms, left, c2, aux)
+    )(
+        images,
+        w,
+        low,
+        sources,
+        high,
+        low0,
+        half0,
+        high0,
+        low1,
+        half1,
+        high1,
+        self_terms,
+        left,
+        c2,
+        aux,
+    )
     return images, heights, norms
 
 

time: 83 us -> 101 us (1.22)
  blocking collectives: 40.8 us -> 0 us
  waiting for transfers between devices: 6.99 us -> 26.7 us
  starting transfers between devices: 12.7 us -> 32.2 us
  local copies, waits for them, and re-layouts: 4.76 us -> 20.9 us
  Pallas kernels: 16.6 us -> 19.4 us
    all_to_all x3 -> x0, blocking collectives: 40.8 us -> none  [exchange(): lax.all_to_all(x, 'store', 0, 0, axis_index_groups=groups, tiled=True)]
    unnamed x16 -> x76, local copies, waits for them, and re-layouts: 4.68 us -> 20.8 us
    all_to_all x1 -> x4, waiting for transfers between devices: 0.01 us -> 13.7 us  [exchange(): lax.all_to_all(x, 'store', 0, 0, axis_index_groups=groups, tiled=True)]
    all_to_all x1 -> x4, starting transfers between devices: 3.48 us -> 16.4 us  [exchange(): lax.all_to_all(x, 'store', 0, 0, axis_index_groups=groups, tiled=True)]
    ppermute x3 -> x4, waiting for transfers between devices: 5.74 us -> 11.4 us  [ring(): lax.ppermute(block, 'store', forward)]
    ppermute x3 -> x4, starting transfers between devices: 8.25 us -> 13.2 us  [ring(): lax.ppermute(block, 'store', backward)]
    pallas_call x3, Pallas kernels: 5.17 us -> 7.09 us  [the longest x1 3.17 us: shards(): call(final_second, outs, [ANY] + [VMEM] * 14, scratch + [pltpu.SemaphoreT...]
    ppermute x2, starting transfers between devices: 0.91 us -> 2.39 us  [across(): parts.append(lax.ppermute(x, 'store', pairs))]
  transfers between devices with their start and end apart: 9 -> 14, of which waited for: 3 -> 9; matrix products, arithmetic and copies ran while one was open for 0% -> 0% of each run, Pallas kernels for 11% -> 10%
where the time goes in v21:
time: 101 us; the launch traced here: 100 us
  starting transfers between devices  32.2 us (32%)
  waiting for transfers between devices  26.7 us (26%)
  local copies, waits for them, and re-layouts  20.9 us (21%)
  Pallas kernels  19.4 us (19%)
    unnamed x76, local copies, waits for them, and re-layouts  20.8 us
    all_to_all x4, starting transfers between devices, exchange(): lax.all_to_all(x, 'store', 0, 0, axis_index_groups=groups, tiled=True)  16.4 us
    all_to_all x4, waiting for transfers between devices, exchange(): lax.all_to_all(x, 'store', 0, 0, axis_index_groups=groups, tiled=True)  13.7 us
    ppermute x4, starting transfers between devices, ring(): lax.ppermute(block, 'store', backward)  13.2 us
    ppermute x4, waiting for transfers between devices, ring(): lax.ppermute(block, 'store', forward)  11.4 us
    pallas_call x1, Pallas kernels, shards(): call(functools.partial(order_tiles, all_blocks), sds((blocks, ops * size,...  3.46 us
    pallas_call x1, Pallas kernels, shards(): call(final_second, outs, [ANY] + [VMEM] * 14, scratch + [pltpu.SemaphoreT...  3.17 us
    pallas_call x1, Pallas kernels, shards(): call(final_first, [outs, sds((ops, columns), F32), sds((ops, columns), F3...  3.11 us
  transfers between devices with their start and end apart: 14, of which 9 were waited for; matrix products, arithmetic and copies ran while one was open for 0% of the time, Pallas kernels for 10%

profile of v21, /device:TPU:0, one launch (start us, length us, event | category | flops | bytes accessed | tf_op | source)
XLA Modules:
  0.0 100.1 jit_solution(8854632374748600941)
XLA Ops:
  0.6 2.3 %shard_map.112 = (bf16[8,240,128]{2,1,0:T(8,128)(2,1)}, bf16[512,512]{1,0:T(8,128)(2,1)}) custom-call(s32[2,6]{1,0:T(2,128)} %far_cols.1, bf16[512,512]{1,0:T(8,128)(2,1)} %uown.3, bf16[2,32,256]{2,1,0:T(8,128)(2,1)} %bitcast.7, bf16[2,2,6,32,32]{4,3,2,1,0:T(8,128)(2,1)} %coup.1), custom_call_target="tpu_custom_call" | custom-call | tf_op jit(solution)/shard_map/pallas_call | solution.py:523
  2.9 5.4 %collective-permute-start.1 = (bf16[512,512]{1,0:T(8,128)(2,1)}, bf16[512,512]{1,0:T(8,128)(2,1)S(1)}, u32[]{:S(2)}, u32[]{:S(2)}) collective-permute-start(bf16[512,512]{1,0:T(8,128)(2,1)} %get-tuple-element.17), channel_id=1, source_target_pairs={{1,0},{2,1},{3,2},{4,3},{5,4},{6,5},{7,6},{8,7},{9,8},{10,9},{11,1... | collective-permute-start | bytes 1572872 | tf_op jit(solution)/shard_map/ppermute | solution.py:481
  8.4 0.0 collective-permute-start
  8.4 3.5 %all-to-all-start = ((bf16[8,240,128]{2,1,0:T(8,128)(2,1)}), bf16[8,240,128]{2,1,0:T(8,128)(2,1)S(1)}, u32[]{:S(2)}, u32[]{:S(2)}) async-start(bf16[8,240,128]{2,1,0:T(8,128)(2,1)} %get-tuple-element.16.after), calls=%async_computation | async-start | bytes 983040 | tf_op jit(solution)/shard_map/all_to_all | solution.py:507
  11.9 0.0 copy-start.2
  11.9 0.0 copy-start.33
  11.9 3.5 %shard_map.113.w = bf16[2,512,1280]{2,1,0:T(8,128)(2,1)} custom-call(s32[2,5]{1,0:T(2,128)} %cols.1, s32[2]{0:T(128)} %count.1, s32[1]{0:T(128)} %bitcast.row0, bf16[2,2,5,256,256]{4,3,2,1,0:T(8,128)(2,1)} %tiles.1, bf16[8,240,128]{2,1,0:T(8,128)(2,1)} %get-tuple-element.16.after), custom_call_target="tpu_custom_call" | custom-call | tf_op jit(solution)/shard_map/pallas_call | solution.py:533
  15.4 0.5 collective-permute-done.1.high.uhigh
  15.8 5.7 %collective-permute-done.low.ulow = bf16[512,512]{1,0:T(8,128)(2,1)S(1)} collective-permute-done((bf16[512,512]{1,0:T(8,128)(2,1)}, bf16[512,512]{1,0:T(8,128)(2,1)S(1)}, u32[]{:S(2)}, u32[]{:S(2)}) %collective-permute-start) | collective-permute-done | bytes 524320 | tf_op jit(solution)/shard_map/ppermute | solution.py:481
  21.6 1.7 %copy-done = bf16[2,512,1280]{2,1,0:T(8,128)(2,1)S(1)} copy-done((bf16[2,512,1280]{2,1,0:T(8,128)(2,1)S(1)}, bf16[2,512,1280]{2,1,0:T(8,128)(2,1)}, u32[]{:S(2)}) %copy-start) | copy-done | bytes 2621464
  23.3 1.8 %shard_map.114 = (f32[2,512,512]{2,1,0:T(8,128)S(1)}, f32[8,128]{1,0:T(8,128)S(1)}, bf16[528,512]{1,0:T(8,128)(2,1)S(1)}) custom-call(bf16[2,512,1280]{2,1,0:T(8,128)(2,1)S(1)} %copy-done, bf16[512,512]{1,0:T(8,128)(2,1)S(1)} %collective-permute-done.low.ulow, bf16[512,512]{1,0:T(8,128)(2,1)S(1)} %copy-done.2, ...), custom_call_target="tpu_custom_call" | custom-call | flops 11500000256 | tf_op jit(solution)/shard_map/pallas_call | solution.py:539
  25.2 0.0 copy-start.36
  25.2 1.3 %copy-done.36 = f32[2,512,512]{2,1,0:T(8,128)} copy-done((f32[2,512,512]{2,1,0:T(8,128)}, f32[2,512,512]{2,1,0:T(8,128)S(1)}, u32[]{:S(2)}) %copy-start.36) | copy-done | bytes 2097176
  26.5 0.4 collective-permute-start.4
  26.8 0.2 collective-permute-start.2
  27.0 0.0 all-to-all-done.held
  27.0 2.4 %collective-permute-start.3 = (bf16[8,32,128]{2,1,0:T(8,128)(2,1)S(1)}, bf16[8,32,128]{2,1,0:T(8,128)(2,1)S(1)}, u32[]{:S(2)}, u32[]{:S(2)}) collective-permute-start(bf16[8,32,128]{2,1,0:T(8,128)(2,1)S(1)} %shard_map.115.refs_0_), channel_id=1, source_target_pairs={{0,1},{1,0},{2,3},{3,2},{4,5},{5,4},{6,7},{7,6},{8,9},{9,8},{10,11... | collective-permute-start | bytes 196616 | tf_op jit(solution)/shard_map/ppermute | solution.py:513
  29.4 0.1 reshape.18.cols
  29.5 0.8 collective-permute-done.3.refs_1_
  30.3 1.8 %shard_map.116 = bf16[8,64,128]{2,1,0:T(8,128)(2,1)} custom-call(s32[96]{0:T(128)S(1)} %reshape.18.cols, s32[1]{0:T(128)} %bitcast.3.group, bf16[8,240,128]{2,1,0:T(8,128)(2,1)S(1)} %all-to-all-done.held, bf16[8,32,128]{2,1,0:T(8,128)(2,1)S(1)} %shard_map.115.refs_0_, bf16[8,32,128]{2,1,0:T(8,128)(2,1)S(1)} %collective-permute-done.3.refs_1_), custom_call_target="tpu_custom_call" | custom-call | flops 34500001792 | tf_op jit(solution)/shard_map/pallas_call | solution.py:552
  32.1 0.0 copy-done.30
  32.1 5.7 %all-to-all-start.1 = ((bf16[8,64,128]{2,1,0:T(8,128)(2,1)}), bf16[8,64,128]{2,1,0:T(8,128)(2,1)S(1)}, u32[]{:S(2)}, u32[]{:S(2)}) async-start(bf16[8,64,128]{2,1,0:T(8,128)(2,1)} %shard_map.116), calls=%async_computation.1 | async-start | bytes 262144 | tf_op jit(solution)/shard_map/all_to_all | solution.py:507
  37.9 0.0 collective-permute-done.4.after_high.ehigh
  37.9 0.0 copy-start.16
  37.9 1.1 %collective-permute-done.2.after_low.elow = bf16[528,512]{1,0:T(8,128)(2,1)S(1)} collective-permute-done((bf16[528,512]{1,0:T(8,128)(2,1)S(1)}, bf16[528,512]{1,0:T(8,128)(2,1)S(1)}, u32[]{:S(2)}, u32[]{:S(2)}) %collective-permute-start.2) | collective-permute-done | bytes 540704 | tf_op jit(solution)/shard_map/ppermute | solution.py:481
  39.0 6.4 %all-to-all-done.1.cmsg = bf16[8,64,128]{2,1,0:T(8,128)(2,1)S(1)} async-done(((bf16[8,64,128]{2,1,0:T(8,128)(2,1)}), bf16[8,64,128]{2,1,0:T(8,128)(2,1)S(1)}, u32[]{:S(2)}, u32[]{:S(2)}) %all-to-all-start.1) | async-done | bytes 131104 | tf_op jit(solution)/shard_map/all_to_all | solution.py:507
  45.4 1.6 %copy-done.37 = f32[2,512,512]{2,1,0:T(8,128)S(1)} copy-done((f32[2,512,512]{2,1,0:T(8,128)S(1)}, f32[2,512,512]{2,1,0:T(8,128)}, u32[]{:S(2)}) %copy-start.37) | copy-done | bytes 2097176
  47.0 2.1 %shard_map.117 = (bf16[528,512]{1,0:T(8,128)(2,1)S(1)}, bf16[352,512]{1,0:T(8,128)(2,1)S(1)}, bf16[272,512]{1,0:T(8,128)(2,1)S(1)}, bf16[8,80,128]{2,1,0:T(8,128)(2,1)}) custom-call(bf16[512,512]{1,0:T(8,128)(2,1)S(1)} %copy-done.2, f32[2,512,512]{2,1,0:T(8,128)S(1)} %copy-done.37, bf16[2,32,256]{2,1,0:T(8,128)(2,1)S(1)} %bitcast.4, ...), custom_call_target="tpu_custom_call" | custom-call | flops 2300000000 | tf_op jit(solution)/shard_map/pallas_call | solution.py:561
  49.1 0.8 copy-done.20
  49.9 0.7 copy-done.24
  50.6 3.6 %all-to-all-start.2 = ((bf16[8,80,128]{2,1,0:T(8,128)(2,1)}), bf16[8,80,128]{2,1,0:T(8,128)(2,1)S(1)}, u32[]{:S(2)}, u32[]{:S(2)}) async-start(bf16[8,80,128]{2,1,0:T(8,128)(2,1)} %get-tuple-element.23), calls=%async_computation.2 | async-start | bytes 327680 | tf_op jit(solution)/shard_map/all_to_all | solution.py:507
  54.2 3.8 %collective-permute-start.6 = (bf16[352,512]{1,0:T(8,128)(2,1)S(1)}, bf16[352,512]{1,0:T(8,128)(2,1)S(1)}, u32[]{:S(2)}, u32[]{:S(2)}) collective-permute-start(bf16[352,512]{1,0:T(8,128)(2,1)S(1)} %get-tuple-element.22.own0), channel_id=1, source_target_pairs={{1,0},{2,1},{3,2},{4,3},{5,4},{6,5},{7,6},{8,7},{9,8},{10,9},{11,1... | collective-permute-start | bytes 1081352 | tf_op jit(solution)/shard_map/ppermute | solution.py:481
  58.0 0.0 collective-permute-start.5
  58.0 0.7 copy-done.22
  58.8 3.2 %all-to-all-done.2.refs_2_ = bf16[8,80,128]{2,1,0:T(8,128)(2,1)S(1)} async-done(((bf16[8,80,128]{2,1,0:T(8,128)(2,1)}), bf16[8,80,128]{2,1,0:T(8,128)(2,1)S(1)}, u32[]{:S(2)}, u32[]{:S(2)}) %all-to-all-start.2) | async-done | bytes 163872 | tf_op jit(solution)/shard_map/all_to_all | solution.py:507
  62.0 0.0 collective-permute-start.7
  62.0 0.7 copy-done.26
  62.7 0.3 collective-permute-done.6.after_high.halfhigh.high0
  63.0 4.6 %collective-permute-done.5.after_low.halflow.low0 = bf16[352,512]{1,0:T(8,128)(2,1)S(1)} collective-permute-done((bf16[352,512]{1,0:T(8,128)(2,1)S(1)}, bf16[352,512]{1,0:T(8,128)(2,1)S(1)}, u32[]{:S(2)}, u32[]{:S(2)}) %collective-permute-start.5) | collective-permute-done | bytes 360480 | tf_op jit(solution)/shard_map/ppermute | solution.py:481
  67.6 0.7 copy-done.12
  68.3 0.0 collective-permute-done.7.refs_3_
  68.3 1.0 %copy-done.8 = bf16[8,240,128]{2,1,0:T(8,128)(2,1)S(1)} copy-done((bf16[8,240,128]{2,1,0:T(8,128)(2,1)S(1)}, bf16[8,240,128]{2,1,0:T(8,128)(2,1)}, u32[]{:S(2)}) %copy-start.8) | copy-done | bytes 491544
  69.4 1.0 copy-done.13
  70.3 0.9 copy-done.27
  71.3 0.8 copy-done.31
  72.1 0.8 copy-done.35
  72.9 1.6 %shard_map.118 = bf16[8,80,128]{2,1,0:T(8,128)(2,1)S(1)} custom-call(s32[96]{0:T(128)S(1)} %reshape.18.cols, s32[1]{0:T(128)} %bitcast.3.group, bf16[352,512]{1,0:T(8,128)(2,1)S(1)} %copy-done.13, bf16[352,512]{1,0:T(8,128)(2,1)S(1)} %collective-permute-done.6.after_high.halfhigh.high0, bf16[8,240,128]{2,1,0:T(8,128)(2,1)S(1)} %copy-done.8, ...), custom_call_target="tpu_custom_call" | custom-call | flops 34500001792 | tf_op jit(solution)/shard_map/pallas_call | solution.py:580
  74.5 0.0 copy-done.9
  74.6 0.7 copy-done.28
  75.2 3.6 %all-to-all-start.3 = ((bf16[8,80,128]{2,1,0:T(8,128)(2,1)}), bf16[8,80,128]{2,1,0:T(8,128)(2,1)S(1)}, u32[]{:S(2)}, u32[]{:S(2)}) async-start(bf16[8,80,128]{2,1,0:T(8,128)(2,1)} %copy-done.28), calls=%async_computation.3 | async-start | bytes 327680 | tf_op jit(solution)/shard_map/all_to_all | solution.py:507
  78.8 3.6 %collective-permute-start.9 = (bf16[272,512]{1,0:T(8,128)(2,1)}, bf16[272,512]{1,0:T(8,128)(2,1)}, u32[]{:S(2)}, u32[]{:S(2)}) collective-permute-start(bf16[272,512]{1,0:T(8,128)(2,1)} %copy-done.24), channel_id=1, source_target_pairs={{1,0},{2,1},{3,2},{4,3},{5,4},{6,5},{7,6},{8,7},{9,8},{10,9},{11,1... | collective-permute-start | bytes 835592 | tf_op jit(solution)/shard_map/ppermute | solution.py:481
  82.4 0.0 collective-permute-start.8
  82.4 4.1 %all-to-all-done.3.cmsg = bf16[8,80,128]{2,1,0:T(8,128)(2,1)S(1)} async-done(((bf16[8,80,128]{2,1,0:T(8,128)(2,1)}), bf16[8,80,128]{2,1,0:T(8,128)(2,1)S(1)}, u32[]{:S(2)}, u32[]{:S(2)}) %all-to-all-start.3) | async-done | bytes 163872 | tf_op jit(solution)/shard_map/all_to_all | solution.py:507
  86.5 1.0 %copy-done.4 = bf16[512,512]{1,0:T(8,128)(2,1)S(1)} copy-done((bf16[512,512]{1,0:T(8,128)(2,1)S(1)}, bf16[512,512]{1,0:T(8,128)(2,1)}, u32[]{:S(2)}) %copy-start.4) | copy-done | bytes 524312
  87.5 1.0 %copy-done.6 = bf16[512,512]{1,0:T(8,128)(2,1)S(1)} copy-done((bf16[512,512]{1,0:T(8,128)(2,1)S(1)}, bf16[512,512]{1,0:T(8,128)(2,1)}, u32[]{:S(2)}) %copy-start.6) | copy-done | bytes 524312
  88.6 1.0 copy-done.10
  89.6 1.0 copy-done.14
  90.6 1.0 %copy-done.17 = bf16[528,512]{1,0:T(8,128)(2,1)S(1)} copy-done((bf16[528,512]{1,0:T(8,128)(2,1)S(1)}, bf16[528,512]{1,0:T(8,128)(2,1)}, u32[]{:S(2)}) %copy-start.17) | copy-done | bytes 540696
  91.6 1.0 %copy-done.19 = bf16[528,512]{1,0:T(8,128)(2,1)S(1)} copy-done((bf16[528,512]{1,0:T(8,128)(2,1)S(1)}, bf16[528,512]{1,0:T(8,128)(2,1)}, u32[]{:S(2)}) %copy-start.19) | copy-done | bytes 540696
  92.7 1.0 %copy-done.21 = bf16[528,512]{1,0:T(8,128)(2,1)S(1)} copy-done((bf16[528,512]{1,0:T(8,128)(2,1)S(1)}, bf16[528,512]{1,0:T(8,128)(2,1)}, u32[]{:S(2)}) %copy-start.21) | copy-done | bytes 540696
  93.7 3.1 %shard_map.119 = (f32[2,512,512]{2,1,0:T(8,128)}, f32[2,512]{1,0:T(2,128)}, f32[2,512]{1,0:T(2,128)}, f32[8,512]{1,0:T(8,128)S(1)}) custom-call(bf16[2,512,1280]{2,1,0:T(8,128)(2,1)S(1)} %copy-done.1, bf16[512,512]{1,0:T(8,128)(2,1)S(1)} %copy-done.6, bf16[512,512]{1,0:T(8,128)(2,1)S(1)} %copy-done.2, bf16[512,512]{1,0:T(8,128)(2,1)S(1)} %copy-done.4, ...), custom_call_target="tpu_custom_call" | custom-call | tf_op jit(solution)/shard_map/pallas_call | solution.py:598
  96.8 0.0 collective-permute-done.9.high1
  96.8 0.0 collective-permute-done.8.low1
  96.9 3.2 %shard_map.120 = f32[2,512,512]{2,1,0:T(8,128)} custom-call(f32[2,512,512]{2,1,0:T(8,128)} %get-tuple-element.24.begun, bf16[2,512,1280]{2,1,0:T(8,128)(2,1)S(1)} %copy-done.1, bf16[512,512]{1,0:T(8,128)(2,1)S(1)} %copy-done.6, bf16[512,512]{1,0:T(8,128)(2,1)S(1)} %copy-done.2, bf16[512,512]{1,0:T(8,128)(2,1)S(1)} %copy-done.4, ...), custom_call_target="tpu_custom_call", output_to_operand_aliasing={{}: (0, {})} | custom-call | tf_op jit(solution)/shard_map/pallas_call | solution.py:605
  (51 shorter events, 0.1 us)
Async XLA Ops:
  2.9 12.9 %collective-permute-start.1 = (bf16[512,512]{1,0:T(8,128)(2,1)}, bf16[512,512]{1,0:T(8,128)(2,1)S(1)}, u32[]{:S(2)}, u32[]{:S(2)}) collective-permute-start(bf16[512,512]{1,0:T(8,128)(2,1)} %get-tuple-element.17), channel_id=1, source_target_pairs={{1,0},{2,1},{3,2},{4,3},{5,4},{6,5},{7,6},{8,7},{9,8},{10,9},{11,1... | collective-permute-start | bytes 1572872 | tf_op jit(solution)/shard_map/ppermute | solution.py:481
  8.4 13.2 %collective-permute-start = (bf16[512,512]{1,0:T(8,128)(2,1)}, bf16[512,512]{1,0:T(8,128)(2,1)S(1)}, u32[]{:S(2)}, u32[]{:S(2)}) collective-permute-start(bf16[512,512]{1,0:T(8,128)(2,1)} %get-tuple-element.17), channel_id=1, source_target_pairs={{0,1},{1,2},{2,3},{3,4},{4,5},{5,6},{6,7},{7,8},{8,9},{9,10},{10,1... | collective-permute-start | bytes 1572872 | tf_op jit(solution)/shard_map/ppermute | solution.py:481
  8.4 18.6 %all-to-all-start = ((bf16[8,240,128]{2,1,0:T(8,128)(2,1)}), bf16[8,240,128]{2,1,0:T(8,128)(2,1)S(1)}, u32[]{:S(2)}, u32[]{:S(2)}) async-start(bf16[8,240,128]{2,1,0:T(8,128)(2,1)} %get-tuple-element.16.after), calls=%async_computation | async-start | bytes 983040 | tf_op jit(solution)/shard_map/all_to_all | solution.py:507
  11.9 9.7 %copy-start.2 = (bf16[512,512]{1,0:T(8,128)(2,1)S(1)}, bf16[512,512]{1,0:T(8,128)(2,1)}, u32[]{:S(2)}) copy-start(bf16[512,512]{1,0:T(8,128)(2,1)} %uown.3) | copy-start | bytes 1572868
  11.9 9.7 %copy-start.33 = (f32[2,512]{1,0:T(2,128)S(1)}, f32[2,512]{1,0:T(2,128)}, u32[]{:S(2)}) copy-start(f32[2,512]{1,0:T(2,128)} %diag.5) | copy-start | bytes 12292
  15.8 9.3 %copy-start.3 = (bf16[512,512]{1,0:T(8,128)(2,1)}, bf16[512,512]{1,0:T(8,128)(2,1)S(1)}, u32[]{:S(2)}) copy-start(bf16[512,512]{1,0:T(8,128)(2,1)S(1)} %collective-permute-done.1.high.uhigh) | copy-start | bytes 1572868
  21.6 1.7 %copy-start = (bf16[2,512,1280]{2,1,0:T(8,128)(2,1)S(1)}, bf16[2,512,1280]{2,1,0:T(8,128)(2,1)}, u32[]{:S(2)}) copy-start(bf16[2,512,1280]{2,1,0:T(8,128)(2,1)} %shard_map.113.w) | copy-start | bytes 7864324
  23.3 1.8 %copy-start.5 = (bf16[512,512]{1,0:T(8,128)(2,1)}, bf16[512,512]{1,0:T(8,128)(2,1)S(1)}, u32[]{:S(2)}) copy-start(bf16[512,512]{1,0:T(8,128)(2,1)S(1)} %collective-permute-done.low.ulow) | copy-start | bytes 1572868
  25.2 1.3 %copy-start.36 = (f32[2,512,512]{2,1,0:T(8,128)}, f32[2,512,512]{2,1,0:T(8,128)S(1)}, u32[]{:S(2)}) copy-start(f32[2,512,512]{2,1,0:T(8,128)S(1)} %get-tuple-element.19.near) | copy-start | bytes 6291460
  26.5 11.4 %collective-permute-start.4 = (bf16[528,512]{1,0:T(8,128)(2,1)S(1)}, bf16[528,512]{1,0:T(8,128)(2,1)S(1)}, u32[]{:S(2)}, u32[]{:S(2)}) collective-permute-start(bf16[528,512]{1,0:T(8,128)(2,1)S(1)} %get-tuple-element.18), channel_id=1, source_target_pairs={{1,0},{2,1},{3,2},{4,3},{5,4},{6,5},{7,6},{8,7},{9,8},{10,9},{11,1... | collective-permute-start | bytes 1622024 | tf_op jit(solution)/shard_map/ppermute | solution.py:481
  26.8 12.1 %collective-permute-start.2 = (bf16[528,512]{1,0:T(8,128)(2,1)S(1)}, bf16[528,512]{1,0:T(8,128)(2,1)S(1)}, u32[]{:S(2)}, u32[]{:S(2)}) collective-permute-start(bf16[528,512]{1,0:T(8,128)(2,1)S(1)} %get-tuple-element.18), channel_id=1, source_target_pairs={{0,1},{1,2},{2,3},{3,4},{4,5},{5,6},{6,7},{7,8},{8,9},{9,10},{10,1... | collective-permute-start | bytes 1622024 | tf_op jit(solution)/shard_map/ppermute | solution.py:481
  27.0 5.1 %copy-start.7 = (bf16[8,240,128]{2,1,0:T(8,128)(2,1)}, bf16[8,240,128]{2,1,0:T(8,128)(2,1)S(1)}, u32[]{:S(2)}) copy-start(bf16[8,240,128]{2,1,0:T(8,128)(2,1)S(1)} %all-to-all-done.held) | copy-start | bytes 1474564
  27.0 5.1 %copy-start.30 = (bf16[8,32,128]{2,1,0:T(8,128)(2,1)}, bf16[8,32,128]{2,1,0:T(8,128)(2,1)S(1)}, u32[]{:S(2)}) copy-start(bf16[8,32,128]{2,1,0:T(8,128)(2,1)S(1)} %shard_map.115.refs_0_) | copy-start | bytes 196612
  27.0 3.3 %collective-permute-start.3 = (bf16[8,32,128]{2,1,0:T(8,128)(2,1)S(1)}, bf16[8,32,128]{2,1,0:T(8,128)(2,1)S(1)}, u32[]{:S(2)}, u32[]{:S(2)}) collective-permute-start(bf16[8,32,128]{2,1,0:T(8,128)(2,1)S(1)} %shard_map.115.refs_0_), channel_id=1, source_target_pairs={{0,1},{1,0},{2,3},{3,2},{4,5},{5,4},{6,7},{7,6},{8,9},{9,8},{10,11... | collective-permute-start | bytes 196616 | tf_op jit(solution)/shard_map/ppermute | solution.py:513
  30.3 1.8 %copy-start.34 = (bf16[8,32,128]{2,1,0:T(8,128)(2,1)}, bf16[8,32,128]{2,1,0:T(8,128)(2,1)S(1)}, u32[]{:S(2)}) copy-start(bf16[8,32,128]{2,1,0:T(8,128)(2,1)S(1)} %collective-permute-done.3.refs_1_) | copy-start | bytes 196612
  30.3 15.0 %copy-start.29 = (bf16[2,256,32]{1,2,0:T(8,128)(2,1)S(1)}, bf16[2,256,32]{1,2,0:T(8,128)(2,1)}, u32[]{:S(2)}) copy-start(bf16[2,256,32]{1,2,0:T(8,128)(2,1)} %param.15) | copy-start | bytes 98308
  30.3 15.0 %copy-start.32 = (bf16[2,256,32]{1,2,0:T(8,128)(2,1)S(1)}, bf16[2,256,32]{1,2,0:T(8,128)(2,1)}, u32[]{:S(2)}) copy-start(bf16[2,256,32]{1,2,0:T(8,128)(2,1)} %param.16) | copy-start | bytes 98308
  32.1 13.3 %all-to-all-start.1 = ((bf16[8,64,128]{2,1,0:T(8,128)(2,1)}), bf16[8,64,128]{2,1,0:T(8,128)(2,1)S(1)}, u32[]{:S(2)}, u32[]{:S(2)}) async-start(bf16[8,64,128]{2,1,0:T(8,128)(2,1)} %shard_map.116), calls=%async_computation.1 | async-start | bytes 262144 | tf_op jit(solution)/shard_map/all_to_all | solution.py:507
  37.9 11.2 %copy-start.16 = (bf16[528,512]{1,0:T(8,128)(2,1)}, bf16[528,512]{1,0:T(8,128)(2,1)S(1)}, u32[]{:S(2)}) copy-start(bf16[528,512]{1,0:T(8,128)(2,1)S(1)} %collective-permute-done.4.after_high.ehigh) | copy-start | bytes 1622020
  39.0 10.1 %copy-start.18 = (bf16[528,512]{1,0:T(8,128)(2,1)}, bf16[528,512]{1,0:T(8,128)(2,1)S(1)}, u32[]{:S(2)}) copy-start(bf16[528,512]{1,0:T(8,128)(2,1)S(1)} %collective-permute-done.2.after_low.elow) | copy-start | bytes 1622020
  45.4 1.6 %copy-start.37 = (f32[2,512,512]{2,1,0:T(8,128)S(1)}, f32[2,512,512]{2,1,0:T(8,128)}, u32[]{:S(2)}) copy-start(f32[2,512,512]{2,1,0:T(8,128)} %copy-done.36) | copy-start | bytes 6291460
  49.1 0.8 copy-start.20
  49.9 0.7 copy-start.24
  50.6 11.4 %all-to-all-start.2 = ((bf16[8,80,128]{2,1,0:T(8,128)(2,1)}), bf16[8,80,128]{2,1,0:T(8,128)(2,1)S(1)}, u32[]{:S(2)}, u32[]{:S(2)}) async-start(bf16[8,80,128]{2,1,0:T(8,128)(2,1)} %get-tuple-element.23), calls=%async_computation.2 | async-start | bytes 327680 | tf_op jit(solution)/shard_map/all_to_all | solution.py:507
  54.2 8.8 %collective-permute-start.6 = (bf16[352,512]{1,0:T(8,128)(2,1)S(1)}, bf16[352,512]{1,0:T(8,128)(2,1)S(1)}, u32[]{:S(2)}, u32[]{:S(2)}) collective-permute-start(bf16[352,512]{1,0:T(8,128)(2,1)S(1)} %get-tuple-element.22.own0), channel_id=1, source_target_pairs={{1,0},{2,1},{3,2},{4,3},{5,4},{6,5},{7,6},{8,7},{9,8},{10,9},{11,1... | collective-permute-start | bytes 1081352 | tf_op jit(solution)/shard_map/ppermute | solution.py:481
  58.0 9.5 %collective-permute-start.5 = (bf16[352,512]{1,0:T(8,128)(2,1)S(1)}, bf16[352,512]{1,0:T(8,128)(2,1)S(1)}, u32[]{:S(2)}, u32[]{:S(2)}) collective-permute-start(bf16[352,512]{1,0:T(8,128)(2,1)S(1)} %get-tuple-element.22.own0), channel_id=1, source_target_pairs={{0,1},{1,2},{2,3},{3,4},{4,5},{5,6},{6,7},{7,8},{8,9},{9,10},{10,1... | collective-permute-start | bytes 1081352 | tf_op jit(solution)/shard_map/ppermute | solution.py:481
  58.0 0.7 copy-start.22
  62.0 6.3 %collective-permute-start.7 = (bf16[8,80,128]{2,1,0:T(8,128)(2,1)S(1)}, bf16[8,80,128]{2,1,0:T(8,128)(2,1)S(1)}, u32[]{:S(2)}, u32[]{:S(2)}) collective-permute-start(bf16[8,80,128]{2,1,0:T(8,128)(2,1)S(1)} %all-to-all-done.2.refs_2_), channel_id=1, source_target_pairs={{0,1},{1,0},{2,3},{3,2},{4,5},{5,4},{6,7},{7,6},{8,9},{9,8},{10,11... | collective-permute-start | bytes 491528 | tf_op jit(solution)/shard_map/ppermute | solution.py:513
  62.0 0.7 copy-start.26
  63.0 11.6 %copy-start.9 = (bf16[352,512]{1,0:T(8,128)(2,1)}, bf16[352,512]{1,0:T(8,128)(2,1)S(1)}, u32[]{:S(2)}) copy-start(bf16[352,512]{1,0:T(8,128)(2,1)S(1)} %collective-permute-done.6.after_high.halfhigh.high0) | copy-start | bytes 1081348
  67.6 0.7 copy-start.12
  68.3 1.0 %copy-start.8 = (bf16[8,240,128]{2,1,0:T(8,128)(2,1)S(1)}, bf16[8,240,128]{2,1,0:T(8,128)(2,1)}, u32[]{:S(2)}) copy-start(bf16[8,240,128]{2,1,0:T(8,128)(2,1)} %copy-done.7) | copy-start | bytes 1474564
  69.4 1.0 copy-start.13
  70.3 0.9 copy-start.27
  71.3 0.8 copy-start.31
  72.1 0.8 copy-start.35
  72.9 13.6 %copy-start.1 = (bf16[2,512,1280]{2,1,0:T(8,128)(2,1)S(1)}, bf16[2,512,1280]{2,1,0:T(8,128)(2,1)}, u32[]{:S(2)}) copy-start(bf16[2,512,1280]{2,1,0:T(8,128)(2,1)} %shard_map.113.w) | copy-start | bytes 7864324
  74.6 0.7 copy-start.28
  75.2 11.3 %all-to-all-start.3 = ((bf16[8,80,128]{2,1,0:T(8,128)(2,1)}), bf16[8,80,128]{2,1,0:T(8,128)(2,1)S(1)}, u32[]{:S(2)}, u32[]{:S(2)}) async-start(bf16[8,80,128]{2,1,0:T(8,128)(2,1)} %copy-done.28), calls=%async_computation.3 | async-start | bytes 327680 | tf_op jit(solution)/shard_map/all_to_all | solution.py:507
  78.8 18.0 %collective-permute-start.9 = (bf16[272,512]{1,0:T(8,128)(2,1)}, bf16[272,512]{1,0:T(8,128)(2,1)}, u32[]{:S(2)}, u32[]{:S(2)}) collective-permute-start(bf16[272,512]{1,0:T(8,128)(2,1)} %copy-done.24), channel_id=1, source_target_pairs={{1,0},{2,1},{3,2},{4,3},{5,4},{6,5},{7,6},{8,7},{9,8},{10,9},{11,1... | collective-permute-start | bytes 835592 | tf_op jit(solution)/shard_map/ppermute | solution.py:481
  82.4 14.4 %collective-permute-start.8 = (bf16[272,512]{1,0:T(8,128)(2,1)}, bf16[272,512]{1,0:T(8,128)(2,1)}, u32[]{:S(2)}, u32[]{:S(2)}) collective-permute-start(bf16[272,512]{1,0:T(8,128)(2,1)} %copy-done.24), channel_id=1, source_target_pairs={{0,1},{1,2},{2,3},{3,4},{4,5},{5,6},{6,7},{7,8},{8,9},{9,10},{10,1... | collective-permute-start | bytes 835592 | tf_op jit(solution)/shard_map/ppermute | solution.py:481
  86.5 1.0 %copy-start.4 = (bf16[512,512]{1,0:T(8,128)(2,1)S(1)}, bf16[512,512]{1,0:T(8,128)(2,1)}, u32[]{:S(2)}) copy-start(bf16[512,512]{1,0:T(8,128)(2,1)} %copy-done.3) | copy-start | bytes 1572868
  87.5 1.0 %copy-start.6 = (bf16[512,512]{1,0:T(8,128)(2,1)S(1)}, bf16[512,512]{1,0:T(8,128)(2,1)}, u32[]{:S(2)}) copy-start(bf16[512,512]{1,0:T(8,128)(2,1)} %copy-done.5) | copy-start | bytes 1572868
  88.6 1.0 copy-start.10
  89.6 1.0 copy-start.14
  90.6 1.0 %copy-start.17 = (bf16[528,512]{1,0:T(8,128)(2,1)S(1)}, bf16[528,512]{1,0:T(8,128)(2,1)}, u32[]{:S(2)}) copy-start(bf16[528,512]{1,0:T(8,128)(2,1)} %copy-done.16) | copy-start | bytes 1622020
  91.6 1.0 %copy-start.19 = (bf16[528,512]{1,0:T(8,128)(2,1)S(1)}, bf16[528,512]{1,0:T(8,128)(2,1)}, u32[]{:S(2)}) copy-start(bf16[528,512]{1,0:T(8,128)(2,1)} %copy-done.18) | copy-start | bytes 1622020
  92.6 1.0 %copy-start.21 = (bf16[528,512]{1,0:T(8,128)(2,1)S(1)}, bf16[528,512]{1,0:T(8,128)(2,1)}, u32[]{:S(2)}) copy-start(bf16[528,512]{1,0:T(8,128)(2,1)} %copy-done.20) | copy-start | bytes 1622020
  93.7 3.2 %copy-start.11 = (bf16[352,512]{1,0:T(8,128)(2,1)S(1)}, bf16[352,512]{1,0:T(8,128)(2,1)}, u32[]{:S(2)}) copy-start(bf16[352,512]{1,0:T(8,128)(2,1)} %copy-done.9) | copy-start | bytes 1081348
  93.7 3.2 %copy-start.15 = (bf16[352,512]{1,0:T(8,128)(2,1)S(1)}, bf16[352,512]{1,0:T(8,128)(2,1)}, u32[]{:S(2)}) copy-start(bf16[352,512]{1,0:T(8,128)(2,1)} %copy-done.12) | copy-start | bytes 1081348
  93.7 3.2 %copy-start.23 = (bf16[352,512]{1,0:T(8,128)(2,1)S(1)}, bf16[352,512]{1,0:T(8,128)(2,1)}, u32[]{:S(2)}) copy-start(bf16[352,512]{1,0:T(8,128)(2,1)} %copy-done.22) | copy-start | bytes 1081348
  93.7 3.2 %copy-start.25 = (bf16[272,512]{1,0:T(8,128)(2,1)S(1)}, bf16[272,512]{1,0:T(8,128)(2,1)}, u32[]{:S(2)}) copy-start(bf16[272,512]{1,0:T(8,128)(2,1)} %copy-done.24) | copy-start | bytes 835588

commit v22 on v18

--- a/solution.py
+++ b/solution.py
@@ -86,10 +86,9 @@
                 )
 
 
-def coeff_kernel(count, far_cols, u, right, coup, out, u_out):
+def coeff_kernel(count, far_cols, u, right, coup, out):
     ops, blocks, far, rank, _ = coup.shape
     size = right.shape[2]
-    u_out[...] = u[...]
     z = [dot(right[b], u[b * size:(b + 1) * size, :]) for b in range(blocks)]
     at = 3 * ops * rank + STATS
     for pair in range(SLICES // 2):
@@ -457,13 +456,13 @@
     right = jnp.transpose(basis_right, (0, 2, 1))
 
     shared = (blocks + 1) * body
-    mine, own = call(
+    low, high = ring(sources)
+    mine = call(
         functools.partial(coeff_kernel, count),
-        [sds((SLICES, shared + STATS + rank, LANES), BF16), sds(sources.shape, BF16)],
+        sds((SLICES, shared + STATS + rank, LANES), BF16),
         [SMEM] + [VMEM] * 3,
         megabytes=60,
     )(far_cols, sources, right, couplings)
-    low, high = ring(own)
     held = exchange(mine)
     cols = held[:, shared, :blocks * far].astype(jnp.int32).reshape(-1)
 

time: 83 us -> 80.9 us (0.975)
  blocking collectives: 40.8 us -> 39.1 us
    ppermute x3, waiting for transfers between devices: 5.74 us -> 2.48 us  [ring(): lax.ppermute(block, 'store', forward)]
    all_to_all x1, waiting for transfers between devices: 0.01 us -> 3 us  [exchange(): lax.all_to_all(x, 'store', 0, 0, axis_index_groups=groups, tiled=True)]
    all_to_all x3, blocking collectives: 40.8 us -> 39.1 us  [exchange(): lax.all_to_all(x, 'store', 0, 0, axis_index_groups=groups, tiled=True)]
  transfers between devices with their start and end apart: 9 -> 9, of which waited for: 3 -> 3; matrix products, arithmetic and copies ran while one was open for 0% -> 0% of each run, Pallas kernels for 11% -> 15%
where the time goes in v22:
time: 80.9 us; the launch traced here: 80.5 us
  blocking collectives  39.1 us (48%)
  Pallas kernels  16.5 us (20%)
  starting transfers between devices  13.1 us (16%)
  waiting for transfers between devices  6.28 us (8%)
  local copies, waits for them, and re-layouts  4.76 us (6%)
    all_to_all x3, blocking collectives, exchange(): lax.all_to_all(x, 'store', 0, 0, axis_index_groups=groups, tiled=True)  39.1 us
    ppermute x3, starting transfers between devices, ring(): lax.ppermute(block, 'store', backward)  8.32 us
    unnamed x16, local copies, waits for them, and re-layouts  4.68 us
    pallas_call x1, Pallas kernels, shards(): call(functools.partial(order_tiles, all_blocks), sds((blocks, ops * size,...  3.48 us
    all_to_all x1, starting transfers between devices, exchange(): lax.all_to_all(x, 'store', 0, 0, axis_index_groups=groups, tiled=True)  3.48 us
    all_to_all x1, waiting for transfers between devices, exchange(): lax.all_to_all(x, 'store', 0, 0, axis_index_groups=groups, tiled=True)  3 us
    pallas_call x1, Pallas kernels, shards(): call(final_first, [outs, sds((ops, columns), F32), sds((ops, columns), F3...  2.86 us
    ppermute x3, waiting for transfers between devices, ring(): lax.ppermute(block, 'store', forward)  2.48 us
  transfers between devices with their start and end apart: 9, of which 3 were waited for; matrix products, arithmetic and copies ran while one was open for 0% of the time, Pallas kernels for 15%

profile of v22, /device:TPU:0, one launch (start us, length us, event | category | flops | bytes accessed | tf_op | source)
XLA Modules:
  0.0 80.5 jit_solution(1058913412582391903)
XLA Ops:
  0.6 5.5 %collective-permute-start.1 = (bf16[512,512]{1,0:T(8,128)(2,1)}, bf16[512,512]{1,0:T(8,128)(2,1)S(1)}, u32[]{:S(2)}, u32[]{:S(2)}) collective-permute-start(bf16[512,512]{1,0:T(8,128)(2,1)} %uown.3), channel_id=1, source_target_pairs={{1,0},{2,1},{3,2},{4,3},{5,4},{6,5},{7,6},{8,7},{9,8},{10,9},{11,1... | collective-permute-start | bytes 1572872 | tf_op jit(solution)/shard_map/ppermute | solution.py:417
  6.1 0.0 collective-permute-start
  6.1 2.2 %shard_map.112.after = bf16[8,240,128]{2,1,0:T(8,128)(2,1)} custom-call(s32[2,6]{1,0:T(2,128)} %far_cols.1, bf16[512,512]{1,0:T(8,128)(2,1)} %uown.3, bf16[2,32,256]{2,1,0:T(8,128)(2,1)} %bitcast.7, bf16[2,2,6,32,32]{4,3,2,1,0:T(8,128)(2,1)} %coup.1), custom_call_target="tpu_custom_call" | custom-call | tf_op jit(solution)/shard_map/pallas_call | solution.py:460
  8.3 3.5 %all-to-all-start = ((bf16[8,240,128]{2,1,0:T(8,128)(2,1)}), bf16[8,240,128]{2,1,0:T(8,128)(2,1)S(1)}, u32[]{:S(2)}, u32[]{:S(2)}) async-start(bf16[8,240,128]{2,1,0:T(8,128)(2,1)} %shard_map.112.after), calls=%async_computation | async-start | bytes 983040 | tf_op jit(solution)/shard_map/all_to_all | solution.py:443
  11.8 0.0 copy-start.2
  11.8 0.0 copy-start.5
  11.8 0.0 copy-start.3
  11.9 0.0 copy-start.4
  11.9 3.5 %shard_map.113.w = bf16[2,512,1280]{2,1,0:T(8,128)(2,1)} custom-call(s32[2,5]{1,0:T(2,128)} %cols.1, s32[2]{0:T(128)} %count.1, s32[1]{0:T(128)} %bitcast.row0, bf16[2,2,5,256,256]{4,3,2,1,0:T(8,128)(2,1)} %tiles.1, bf16[8,240,128]{2,1,0:T(8,128)(2,1)} %shard_map.112.after), custom_call_target="tpu_custom_call" | custom-call | tf_op jit(solution)/shard_map/pallas_call | solution.py:469
  15.4 0.0 collective-permute-done.1.high.uhigh
  15.4 2.5 %collective-permute-done.low.ulow = bf16[512,512]{1,0:T(8,128)(2,1)S(1)} collective-permute-done((bf16[512,512]{1,0:T(8,128)(2,1)}, bf16[512,512]{1,0:T(8,128)(2,1)S(1)}, u32[]{:S(2)}, u32[]{:S(2)}) %collective-permute-start) | collective-permute-done | bytes 524320 | tf_op jit(solution)/shard_map/ppermute | solution.py:417
  17.8 0.0 copy-done.2
  17.8 0.0 copy-done.5
  17.8 0.0 copy-start
  17.8 1.7 %copy-done = bf16[2,512,1280]{2,1,0:T(8,128)(2,1)S(1)} copy-done((bf16[2,512,1280]{2,1,0:T(8,128)(2,1)S(1)}, bf16[2,512,1280]{2,1,0:T(8,128)(2,1)}, u32[]{:S(2)}) %copy-start) | copy-done | bytes 2621464
  19.6 1.5 %shard_map.114 = (f32[2,512,512]{2,1,0:T(8,128)S(1)}, f32[8,128]{1,0:T(8,128)S(1)}) custom-call(bf16[2,512,1280]{2,1,0:T(8,128)(2,1)S(1)} %copy-done, bf16[512,512]{1,0:T(8,128)(2,1)S(1)} %collective-permute-done.low.ulow, bf16[512,512]{1,0:T(8,128)(2,1)S(1)} %copy-done.2, bf16[512,512]{1,0:T(8,128)(2,1)S(1)} %collective-permute-done.1.high.uhigh, ...), custom_call_target="tpu_custom_call" | custom-call | flops 11500000256 | tf_op jit(solution)/shard_map/pallas_call | solution.py:475
  21.1 0.0 copy-start.6
  21.1 1.3 %copy-done.6 = f32[2,512,512]{2,1,0:T(8,128)} copy-done((f32[2,512,512]{2,1,0:T(8,128)}, f32[2,512,512]{2,1,0:T(8,128)S(1)}, u32[]{:S(2)}) %copy-start.6) | copy-done | bytes 2097176
  22.4 3.0 %all-to-all-done.held = bf16[8,240,128]{2,1,0:T(8,128)(2,1)S(1)} async-done(((bf16[8,240,128]{2,1,0:T(8,128)(2,1)}), bf16[8,240,128]{2,1,0:T(8,128)(2,1)S(1)}, u32[]{:S(2)}, u32[]{:S(2)}) %all-to-all-start) | async-done | bytes 491552 | tf_op jit(solution)/shard_map/all_to_all | solution.py:443
  25.4 1.3 %collective-permute-start.2 = (bf16[8,32,128]{2,1,0:T(8,128)(2,1)S(1)}, bf16[8,32,128]{2,1,0:T(8,128)(2,1)S(1)}, u32[]{:S(2)}, u32[]{:S(2)}) collective-permute-start(bf16[8,32,128]{2,1,0:T(8,128)(2,1)S(1)} %shard_map.115.refs_0_), channel_id=1, source_target_pairs={{0,1},{1,0},{2,3},{3,2},{4,5},{5,4},{6,7},{7,6},{8,9},{9,8},{10,11... | collective-permute-start | bytes 196616 | tf_op jit(solution)/shard_map/ppermute | solution.py:449
  26.8 0.1 reshape.18.cols
  26.9 0.8 collective-permute-done.2.refs_1_
  27.7 1.1 %shard_map.116 = bf16[8,64,128]{2,1,0:T(8,128)(2,1)S(1)} custom-call(s32[96]{0:T(128)S(1)} %reshape.18.cols, s32[1]{0:T(128)} %bitcast.3.group, bf16[8,240,128]{2,1,0:T(8,128)(2,1)S(1)} %all-to-all-done.held, bf16[8,32,128]{2,1,0:T(8,128)(2,1)S(1)} %shard_map.115.refs_0_, bf16[8,32,128]{2,1,0:T(8,128)(2,1)S(1)} %collective-permute-done.2.refs_1_), custom_call_target="tpu_custom_call" | custom-call | tf_op jit(solution)/shard_map/pallas_call | solution.py:483
  28.8 11.6 %all_to_all.20.cmsg = bf16[8,64,128]{2,1,0:T(8,128)(2,1)S(1)} all-to-all(bf16[8,64,128]{2,1,0:T(8,128)(2,1)S(1)} %shard_map.116), channel_id=1, replica_groups={{0,2,4,6,8,10,12,14},{1,3,5,7,9,11,13,15},{16,18,20,22,24,26,28,30},{17..., dimensions={0} | all-to-all | bytes 262144 | tf_op jit(solution)/shard_map/all_to_all | solution.py:443
  40.4 0.0 copy-done.3
  40.4 0.0 copy-done.4
  40.4 0.0 copy-start.7
  40.4 1.6 %copy-done.7 = f32[2,512,512]{2,1,0:T(8,128)S(1)} copy-done((f32[2,512,512]{2,1,0:T(8,128)S(1)}, f32[2,512,512]{2,1,0:T(8,128)}, u32[]{:S(2)}) %copy-start.7) | copy-done | bytes 2097176
  42.0 1.5 %shard_map.117 = (bf16[528,512]{1,0:T(8,128)(2,1)S(1)}, bf16[512,512]{1,0:T(8,128)(2,1)S(1)}, bf16[8,80,128]{2,1,0:T(8,128)(2,1)S(1)}) custom-call(bf16[512,512]{1,0:T(8,128)(2,1)S(1)} %copy-done.2, f32[2,512,512]{2,1,0:T(8,128)S(1)} %copy-done.7, bf16[2,32,256]{2,1,0:T(8,128)(2,1)S(1)} %bitcast.4, bf16[2,32,256]{2,1,0:T(8,128)(2,1)S(1)} %bitcast.8, ...), custom_call_target="tpu_custom_call" | custom-call | flops 2300000000 | tf_op jit(solution)/shard_map/pallas_call | solution.py:491
  43.5 0.8 collective-permute-start.4
  44.3 0.0 collective-permute-start.3
  44.3 14.5 %all_to_all.21.refs_2_ = bf16[8,80,128]{2,1,0:T(8,128)(2,1)S(1)} all-to-all(bf16[8,80,128]{2,1,0:T(8,128)(2,1)S(1)} %get-tuple-element.15), channel_id=1, replica_groups={{0,2,4,6,8,10,12,14},{1,3,5,7,9,11,13,15},{16,18,20,22,24,26,28,30},{17..., dimensions={0} | all-to-all | bytes 327680 | tf_op jit(solution)/shard_map/all_to_all | solution.py:443
  58.8 0.0 collective-permute-start.5
  58.8 2.0 %collective-permute-start.7 = (bf16[512,512]{1,0:T(8,128)(2,1)S(1)}, bf16[512,512]{1,0:T(8,128)(2,1)S(1)}, u32[]{:S(2)}, u32[]{:S(2)}) collective-permute-start(bf16[512,512]{1,0:T(8,128)(2,1)S(1)} %get-tuple-element.17.vown), channel_id=1, source_target_pairs={{1,0},{2,1},{3,2},{4,3},{5,4},{6,5},{7,6},{8,7},{9,8},{10,9},{11,1... | collective-permute-start | bytes 1572872 | tf_op jit(solution)/shard_map/ppermute | solution.py:417
  60.9 0.0 collective-permute-start.6
  60.9 0.0 collective-permute-done.5.refs_3_
  60.9 0.0 collective-permute-done.4.after_high.vhigh
  60.9 0.0 collective-permute-done.3.after_low.vlow
  60.9 0.0 copy-start.1
  60.9 1.6 %shard_map.118 = bf16[8,80,128]{2,1,0:T(8,128)(2,1)S(1)} custom-call(s32[96]{0:T(128)S(1)} %reshape.18.cols, s32[1]{0:T(128)} %bitcast.3.group, bf16[528,512]{1,0:T(8,128)(2,1)S(1)} %collective-permute-done.3.after_low.vlow, bf16[528,512]{1,0:T(8,128)(2,1)S(1)} %collective-permute-done.4.after_high.vhigh, bf16[8,240,128]{2,1,0:T(8,128)(2,1)S(1)} %all-to-all-done.held, ...), custom_call_target="tpu_custom_call" | custom-call | flops 34500001792 | tf_op jit(solution)/shard_map/pallas_call | solution.py:509
  62.5 13.0 %all_to_all.22.cmsg = bf16[8,80,128]{2,1,0:T(8,128)(2,1)S(1)} all-to-all(bf16[8,80,128]{2,1,0:T(8,128)(2,1)S(1)} %shard_map.118), channel_id=1, replica_groups={{0,2,4,6,8,10,12,14},{1,3,5,7,9,11,13,15},{16,18,20,22,24,26,28,30},{17..., dimensions={0} | all-to-all | bytes 327680 | tf_op jit(solution)/shard_map/all_to_all | solution.py:443
  75.5 0.0 copy-done.1
  75.5 2.9 %shard_map.119 = (f32[2,512,512]{2,1,0:T(8,128)}, f32[2,512]{1,0:T(2,128)}, f32[2,512]{1,0:T(2,128)}, f32[8,512]{1,0:T(8,128)S(1)}) custom-call(bf16[2,512,1280]{2,1,0:T(8,128)(2,1)S(1)} %copy-done.1, bf16[512,512]{1,0:T(8,128)(2,1)S(1)} %collective-permute-done.low.ulow, bf16[512,512]{1,0:T(8,128)(2,1)S(1)} %copy-done.2, ...), custom_call_target="tpu_custom_call" | custom-call | tf_op jit(solution)/shard_map/pallas_call | solution.py:527
  78.4 0.0 collective-permute-done.7.vhigh
  78.4 0.0 collective-permute-done.6.vlow
  78.4 2.2 %shard_map.120 = f32[2,512,512]{2,1,0:T(8,128)} custom-call(f32[2,512,512]{2,1,0:T(8,128)} %get-tuple-element.16.begun, bf16[2,512,1280]{2,1,0:T(8,128)(2,1)S(1)} %copy-done.1, bf16[512,512]{1,0:T(8,128)(2,1)S(1)} %collective-permute-done.low.ulow, bf16[512,512]{1,0:T(8,128)(2,1)S(1)} %copy-done.2, ...), custom_call_target="tpu_custom_call", output_to_operand_aliasing={{}: (0, {})} | custom-call | tf_op jit(solution)/shard_map/pallas_call | solution.py:534
  (2 shorter events, 0.0 us)
Async XLA Ops:
  0.6 14.7 %collective-permute-start.1 = (bf16[512,512]{1,0:T(8,128)(2,1)}, bf16[512,512]{1,0:T(8,128)(2,1)S(1)}, u32[]{:S(2)}, u32[]{:S(2)}) collective-permute-start(bf16[512,512]{1,0:T(8,128)(2,1)} %uown.3), channel_id=1, source_target_pairs={{1,0},{2,1},{3,2},{4,3},{5,4},{6,5},{7,6},{8,7},{9,8},{10,9},{11,1... | collective-permute-start | bytes 1572872 | tf_op jit(solution)/shard_map/ppermute | solution.py:417
  6.1 11.7 %collective-permute-start = (bf16[512,512]{1,0:T(8,128)(2,1)}, bf16[512,512]{1,0:T(8,128)(2,1)S(1)}, u32[]{:S(2)}, u32[]{:S(2)}) collective-permute-start(bf16[512,512]{1,0:T(8,128)(2,1)} %uown.3), channel_id=1, source_target_pairs={{0,1},{1,2},{2,3},{3,4},{4,5},{5,6},{6,7},{7,8},{8,9},{9,10},{10,1... | collective-permute-start | bytes 1572872 | tf_op jit(solution)/shard_map/ppermute | solution.py:417
  8.3 17.1 %all-to-all-start = ((bf16[8,240,128]{2,1,0:T(8,128)(2,1)}), bf16[8,240,128]{2,1,0:T(8,128)(2,1)S(1)}, u32[]{:S(2)}, u32[]{:S(2)}) async-start(bf16[8,240,128]{2,1,0:T(8,128)(2,1)} %shard_map.112.after), calls=%async_computation | async-start | bytes 983040 | tf_op jit(solution)/shard_map/all_to_all | solution.py:443
  11.8 6.0 %copy-start.2 = (bf16[512,512]{1,0:T(8,128)(2,1)S(1)}, bf16[512,512]{1,0:T(8,128)(2,1)}, u32[]{:S(2)}) copy-start(bf16[512,512]{1,0:T(8,128)(2,1)} %uown.3) | copy-start | bytes 1572868
  11.8 6.0 %copy-start.5 = (f32[2,512]{1,0:T(2,128)S(1)}, f32[2,512]{1,0:T(2,128)}, u32[]{:S(2)}) copy-start(f32[2,512]{1,0:T(2,128)} %diag.5) | copy-start | bytes 12292
  11.8 28.6 %copy-start.3 = (bf16[2,256,32]{1,2,0:T(8,128)(2,1)S(1)}, bf16[2,256,32]{1,2,0:T(8,128)(2,1)}, u32[]{:S(2)}) copy-start(bf16[2,256,32]{1,2,0:T(8,128)(2,1)} %param.15) | copy-start | bytes 98308
  11.9 28.6 %copy-start.4 = (bf16[2,256,32]{1,2,0:T(8,128)(2,1)S(1)}, bf16[2,256,32]{1,2,0:T(8,128)(2,1)}, u32[]{:S(2)}) copy-start(bf16[2,256,32]{1,2,0:T(8,128)(2,1)} %param.16) | copy-start | bytes 98308
  17.8 1.7 %copy-start = (bf16[2,512,1280]{2,1,0:T(8,128)(2,1)S(1)}, bf16[2,512,1280]{2,1,0:T(8,128)(2,1)}, u32[]{:S(2)}) copy-start(bf16[2,512,1280]{2,1,0:T(8,128)(2,1)} %shard_map.113.w) | copy-start | bytes 7864324
  21.1 1.3 %copy-start.6 = (f32[2,512,512]{2,1,0:T(8,128)}, f32[2,512,512]{2,1,0:T(8,128)S(1)}, u32[]{:S(2)}) copy-start(f32[2,512,512]{2,1,0:T(8,128)S(1)} %get-tuple-element.12.near) | copy-start | bytes 6291460
  25.4 2.2 %collective-permute-start.2 = (bf16[8,32,128]{2,1,0:T(8,128)(2,1)S(1)}, bf16[8,32,128]{2,1,0:T(8,128)(2,1)S(1)}, u32[]{:S(2)}, u32[]{:S(2)}) collective-permute-start(bf16[8,32,128]{2,1,0:T(8,128)(2,1)S(1)} %shard_map.115.refs_0_), channel_id=1, source_target_pairs={{0,1},{1,0},{2,3},{3,2},{4,5},{5,4},{6,7},{7,6},{8,9},{9,8},{10,11... | collective-permute-start | bytes 196616 | tf_op jit(solution)/shard_map/ppermute | solution.py:449
  40.4 1.6 %copy-start.7 = (f32[2,512,512]{2,1,0:T(8,128)S(1)}, f32[2,512,512]{2,1,0:T(8,128)}, u32[]{:S(2)}) copy-start(f32[2,512,512]{2,1,0:T(8,128)} %copy-done.6) | copy-start | bytes 6291460
  43.5 17.4 %collective-permute-start.4 = (bf16[528,512]{1,0:T(8,128)(2,1)S(1)}, bf16[528,512]{1,0:T(8,128)(2,1)S(1)}, u32[]{:S(2)}, u32[]{:S(2)}) collective-permute-start(bf16[528,512]{1,0:T(8,128)(2,1)S(1)} %get-tuple-element.14.vown), channel_id=1, source_target_pairs={{1,0},{2,1},{3,2},{4,3},{5,4},{6,5},{7,6},{8,7},{9,8},{10,9},{11,1... | collective-permute-start | bytes 1622024 | tf_op jit(solution)/shard_map/ppermute | solution.py:417
  44.3 16.6 %collective-permute-start.3 = (bf16[528,512]{1,0:T(8,128)(2,1)S(1)}, bf16[528,512]{1,0:T(8,128)(2,1)S(1)}, u32[]{:S(2)}, u32[]{:S(2)}) collective-permute-start(bf16[528,512]{1,0:T(8,128)(2,1)S(1)} %get-tuple-element.14.vown), channel_id=1, source_target_pairs={{0,1},{1,2},{2,3},{3,4},{4,5},{5,6},{6,7},{7,8},{8,9},{9,10},{10,1... | collective-permute-start | bytes 1622024 | tf_op jit(solution)/shard_map/ppermute | solution.py:417
  58.8 2.1 %collective-permute-start.5 = (bf16[8,80,128]{2,1,0:T(8,128)(2,1)S(1)}, bf16[8,80,128]{2,1,0:T(8,128)(2,1)S(1)}, u32[]{:S(2)}, u32[]{:S(2)}) collective-permute-start(bf16[8,80,128]{2,1,0:T(8,128)(2,1)S(1)} %all_to_all.21.refs_2_), channel_id=1, source_target_pairs={{0,1},{1,0},{2,3},{3,2},{4,5},{5,4},{6,7},{7,6},{8,9},{9,8},{10,11... | collective-permute-start | bytes 491528 | tf_op jit(solution)/shard_map/ppermute | solution.py:449
  58.8 19.5 %collective-permute-start.7 = (bf16[512,512]{1,0:T(8,128)(2,1)S(1)}, bf16[512,512]{1,0:T(8,128)(2,1)S(1)}, u32[]{:S(2)}, u32[]{:S(2)}) collective-permute-start(bf16[512,512]{1,0:T(8,128)(2,1)S(1)} %get-tuple-element.17.vown), channel_id=1, source_target_pairs={{1,0},{2,1},{3,2},{4,3},{5,4},{6,5},{7,6},{8,7},{9,8},{10,9},{11,1... | collective-permute-start | bytes 1572872 | tf_op jit(solution)/shard_map/ppermute | solution.py:417
  60.9 17.5 %collective-permute-start.6 = (bf16[512,512]{1,0:T(8,128)(2,1)S(1)}, bf16[512,512]{1,0:T(8,128)(2,1)S(1)}, u32[]{:S(2)}, u32[]{:S(2)}) collective-permute-start(bf16[512,512]{1,0:T(8,128)(2,1)S(1)} %get-tuple-element.17.vown), channel_id=1, source_target_pairs={{0,1},{1,2},{2,3},{3,4},{4,5},{5,6},{6,7},{7,8},{8,9},{9,10},{10,1... | collective-permute-start | bytes 1572872 | tf_op jit(solution)/shard_map/ppermute | solution.py:417
  60.9 14.6 %copy-start.1 = (bf16[2,512,1280]{2,1,0:T(8,128)(2,1)S(1)}, bf16[2,512,1280]{2,1,0:T(8,128)(2,1)}, u32[]{:S(2)}) copy-start(bf16[2,512,1280]{2,1,0:T(8,128)(2,1)} %shard_map.113.w) | copy-start | bytes 7864324

commit v23 on v22

--- a/solution.py
+++ b/solution.py
@@ -198,9 +198,11 @@
     return jnp.concatenate([column] * (columns // LANES), axis=1)
 
 
-def near_kernel(w, low, own, high, diag, image, token):
+def near_kernel(w, low, own, high, diag, image0, image1, token):
     token[...] = jnp.zeros_like(token)
-    ops, rows, columns = image.shape
+    images = (image0, image1)
+    ops = len(images)
+    rows, columns = own.shape
     size = w.shape[1] // ops
     blocks = rows // size
     for b in range(blocks):
@@ -208,63 +210,67 @@
         here = slice(b * size, (b + 1) * size)
         ub = own[here, :].astype(F32)
         for o in range(ops):
-            image[o, here, :] = (
+            images[o][here, :] = (
                 product[o * size:(o + 1) * size] + diagonal_of(diag, o, b, size, columns) * ub
             )
 
 
-def image_kernel(own, near, left, right, cmsg, out0, out1, mout, image, coef):
-    ops = image.shape[0]
+def image_part(own, near, left, right, cmsg, out, z_out, image, coef, o):
     blocks, rank, size = right.shape
     rows, columns = own.shape
-    take_coefs(cmsg, coef, ops * rank)
-    inner = [None] * ops
-    squares = None
+    take_coefs(cmsg, coef, cmsg.shape[1])
+    squares, inner = 0.0, 0.0
     for b in range(blocks):
         here = slice(b * size, (b + 1) * size)
         ub = own[here, :].astype(F32)
-        part = jnp.sum(ub * ub, axis=0, keepdims=True)
-        squares = part if squares is None else squares + part
-        for o in range(ops):
-            far = dot(left[b], coef[b, o * rank:(o + 1) * rank, :], ((0,), (0,)))
-            value = near[o, here, :] + far.astype(BF16).astype(F32)
-            image[o, here, :] = value
-            part = jnp.sum(ub * value, axis=0, keepdims=True)
-            inner[o] = part if inner[o] is None else inner[o] + part
+        squares = squares + jnp.sum(ub * ub, axis=0, keepdims=True)
+        far = dot(left[b], coef[b, o * rank:(o + 1) * rank, :], ((0,), (0,)))
+        value = near[here, :] + far.astype(BF16).astype(F32)
+        image[here, :] = value
+        inner = inner + jnp.sum(ub * value, axis=0, keepdims=True)
+    good = squares > 0
+    pieces = split3(jnp.where(good, inner / jnp.where(good, squares, 1.0), 0.0))
+    shift = pieces[0].astype(F32) + pieces[1].astype(F32) + pieces[2].astype(F32)
+    spread = 0.0
+    z = []
+    for b in range(blocks):
+        here = slice(b * size, (b + 1) * size)
+        v = image[here, :] - shift * own[here, :].astype(F32)
+        spread = spread + jnp.sum(v * v, axis=0, keepdims=True)
+        v = v.astype(BF16)
+        out[here, :] = v
+        z.append(dot(right[b], v))
+    for pair in range(SLICES // 2):
+        first, second = halves(chunk(z[0], pair), chunk(z[1], pair))
+        z_out[2 * pair, o * rank:(o + 1) * rank, :] = first.astype(BF16)
+        z_out[2 * pair + 1, o * rank:(o + 1) * rank, :] = second.astype(BF16)
+    zero = jnp.zeros((1, columns), BF16)
+    out[rows:, :] = jnp.concatenate(pieces + [zero] * (STATS - len(pieces)), axis=0)
+    return shift, squares, spread
+
+
+def image_first(own, near, left, right, cmsg, out, z_out, keep, image, coef):
+    shift, squares, spread = image_part(own, near, left, right, cmsg, out, z_out, image, coef, 0)
+    keep[0:1, :] = shift
+    keep[1:2, :] = spread
+
+
+def image_second(own, near, left, right, cmsg, z_first, keep, out, mout, image, coef):
+    shift, squares, spread = image_part(own, near, left, right, cmsg, out, mout, image, coef, 1)
+    blocks, rank, size = right.shape
+    columns = own.shape[1]
+    body = 2 * rank
+    mout[:, 0:rank, :] = z_first[...]
     stats = []
-    spreads = []
-    good = squares > 0
-    for o in range(ops):
-        shift = jnp.where(good, inner[o] / jnp.where(good, squares, 1.0), 0.0)
-        pieces = split3(shift)
-        stats += pieces
-        shift = pieces[0].astype(F32) + pieces[1].astype(F32) + pieces[2].astype(F32)
-        spread = None
-        z = []
-        for b in range(blocks):
-            ub = own[b * size:(b + 1) * size, :].astype(F32)
-            v = image[o, b * size:(b + 1) * size, :] - shift * ub
-            part = jnp.sum(v * v, axis=0, keepdims=True)
-            spread = part if spread is None else spread + part
-            v = v.astype(BF16)
-            (out0, out1)[o][b * size:(b + 1) * size, :] = v
-            z.append(dot(right[b], v))
-        for pair in range(SLICES // 2):
-            first, second = halves(chunk(z[0], pair), chunk(z[1], pair))
-            mout[2 * pair, o * rank:(o + 1) * rank, :] = first.astype(BF16)
-            mout[2 * pair + 1, o * rank:(o + 1) * rank, :] = second.astype(BF16)
-        spreads.append(spread)
+    for row in (keep[0:1, :], shift, squares, keep[1:2, :], spread):
+        stats += split3(row)
     zero = jnp.zeros((1, columns), BF16)
-    out0[rows:, :] = jnp.concatenate(stats + [zero] * (STATS - len(stats)), axis=0)
-    stats += split3(squares)
-    for spread in spreads:
-        stats += split3(spread)
     stats = jnp.concatenate(stats + [zero] * (STATS - len(stats)), axis=0).astype(F32)
     for pair in range(SLICES // 2):
         part = chunk(stats, pair)
         first, second = halves(part, part)
-        mout[2 * pair, ops * rank:ops * rank + STATS, :] = first.astype(BF16)
-        mout[2 * pair + 1, ops * rank:ops * rank + STATS, :] = second.astype(BF16)
+        mout[2 * pair, body:body + STATS, :] = first.astype(BF16)
+        mout[2 * pair + 1, body:body + STATS, :] = second.astype(BF16)
 
 
 def second_couple(panels, ops, rank, far, cols, group, after_low, after_high, held, *refs):
@@ -309,6 +315,12 @@
         out[s, body:body + STATS, :] = rows
 
 
+def shift_changes(parts, height, factor):
+    return [
+        (row3(v[v.shape[0] - STATS:, :].astype(F32), 0) - height) * factor for v in parts
+    ]
+
+
 def apply_second(o, factor, changes, u3, v3, w, diag, left, cmsg, images, ext, coef, out, sems):
     blocks, rank, size = left.shape
     rows, columns = u3[1].shape
@@ -366,22 +378,13 @@
         )[0]
     st = stat[...]
     reverse = row3(st, 2 * ops)
-    scales = []
     for o in range(ops):
-        height = row3(st, o)
-        norm = row3(st, ops + o)
-        heights[o:o + 1, :] = height
-        norms[o:o + 1, :] = norm
-        factor = reverse / norm
-        changes = [
-            (row3(v[rows:, :].astype(F32), o) - height) * factor for v in (vlow, vown, vhigh)
-        ]
-        scales.append((factor, changes))
-    factor, changes = scales[1]
-    aux[0:1, :] = factor
-    for at in range(3):
-        aux[1 + at:2 + at, :] = changes[at]
-    factor, changes = scales[0]
+        heights[o:o + 1, :] = row3(st, o)
+        norms[o:o + 1, :] = row3(st, ops + o)
+    aux[0:1, :] = reverse / row3(st, ops + 1)
+    aux[1:2, :] = row3(st, 1)
+    factor = reverse / row3(st, ops)
+    changes = shift_changes((vlow, vown, vhigh), row3(st, 0), factor)
     u3, v3 = (ulow, uown, uhigh), (vlow, vown, vhigh)
     apply_second(0, factor, changes, u3, v3, w, diag, left, cmsg, images, ext, coef, out, sems)
 
@@ -405,7 +408,8 @@
     out,
     sems,
 ):
-    factor, changes = aux[0:1, :], [aux[1 + at:2 + at, :] for at in range(3)]
+    factor = aux[0:1, :]
+    changes = shift_changes((vlow, vown, vhigh), aux[1:2, :], factor)
     u3, v3 = (ulow, uown, uhigh), (vlow, vown, vhigh)
     apply_second(1, factor, changes, u3, v3, w, diag, left, cmsg, images, ext, coef, out, sems)
 
@@ -472,9 +476,9 @@
         [SMEM, SMEM, SMEM, VMEM, ANY],
         megabytes=60,
     )(near_cols, near_count, row0, near_tiles, mine)
-    image, token = call(
+    image0, image1, token = call(
         near_kernel,
-        [sds((ops, rows, columns), F32), sds((8, LANES), F32)],
+        [sds((rows, columns), F32), sds((rows, columns), F32), sds((8, LANES), F32)],
         [VMEM] * 5,
         micros=10.0,
     )(w, low, sources, high, self_terms)
@@ -488,21 +492,21 @@
     )(cols, group, held, *z1)
     c1 = exchange(c1)
 
-    first, second, msg = call(
-        image_kernel,
-        [
-            sds((rows + STATS, columns), BF16),
-            sds((rows, columns), BF16),
-            sds((SLICES, body + STATS, LANES), BF16),
-        ],
+    piece = sds((rows + STATS, columns), BF16)
+    scratch = [pltpu.VMEM((rows, columns), F32), pltpu.VMEM((blocks, body, columns), BF16)]
+    first, z_first, keep = call(
+        image_first,
+        [piece, sds((SLICES, rank, LANES), BF16), sds((8, columns), F32)],
         [VMEM] * 5,
-        [
-            pltpu.VMEM((ops, rows, columns), F32),
-            pltpu.VMEM((blocks, body, columns), BF16),
-        ],
-        micros=2.0,
-    )(sources, image, left, right, c1)
+        scratch,
+    )(sources, image0, left, right, c1)
     low0, high0 = ring(first)
+    second, msg = call(
+        image_second,
+        [piece, sds((SLICES, body + STATS, LANES), BF16)],
+        [VMEM] * 7,
+        scratch,
+    )(sources, image1, left, right, c1, z_first, keep)
     low1, high1 = ring(second)
     msgs = across(exchange(msg))
 

time: 80.9 us -> 80.1 us (level)
  blocking collectives: 39.1 us -> 38.1 us
    all_to_all x3, blocking collectives: 39.1 us -> 38.1 us  [exchange(): lax.all_to_all(x, 'store', 0, 0, axis_index_groups=groups, tiled=True)]
    pallas_call x2 -> x3, Pallas kernels: 3.02 us -> 3.53 us  [the longest x1 1.52 us: shards(): call(near_kernel, [sds((rows, columns), F32), sds((rows, columns), F32),...]
  transfers between devices with their start and end apart: 9 -> 9, of which waited for: 3 -> 3; matrix products, arithmetic and copies ran while one was open for 0% -> 0% of each run, Pallas kernels for 15% -> 16%
where the time goes in v23:
time: 80.1 us; the launch traced here: 79.7 us
  blocking collectives  38.1 us (48%)
  Pallas kernels  17 us (21%)
  starting transfers between devices  13.1 us (16%)
  waiting for transfers between devices  6.64 us (8%)
  local copies, waits for them, and re-layouts  4.04 us (5%)
    all_to_all x3, blocking collectives, exchange(): lax.all_to_all(x, 'store', 0, 0, axis_index_groups=groups, tiled=True)  38.1 us
    ppermute x3, starting transfers between devices, ring(): lax.ppermute(block, 'store', backward)  8.3 us
    unnamed x16, local copies, waits for them, and re-layouts  3.96 us
    all_to_all x1, starting transfers between devices, exchange(): lax.all_to_all(x, 'store', 0, 0, axis_index_groups=groups, tiled=True)  3.48 us
    pallas_call x1, Pallas kernels, shards(): call(functools.partial(order_tiles, all_blocks), sds((blocks, ops * size,...  3.48 us
    all_to_all x1, waiting for transfers between devices, exchange(): lax.all_to_all(x, 'store', 0, 0, axis_index_groups=groups, tiled=True)  3.34 us
    pallas_call x1, Pallas kernels, shards(): call(final_first, [outs, sds((ops, columns), F32), sds((ops, columns), F3...  2.85 us
    ppermute x3, waiting for transfers between devices, ring(): lax.ppermute(block, 'store', forward)  2.48 us
  transfers between devices with their start and end apart: 9, of which 3 were waited for; matrix products, arithmetic and copies ran while one was open for 0% of the time, Pallas kernels for 16%

profile of v23, /device:TPU:0, one launch (start us, length us, event | category | flops | bytes accessed | tf_op | source)
XLA Modules:
  0.0 79.7 jit_solution(16094267921960405726)
XLA Ops:
  0.6 5.5 %collective-permute-start.1 = (bf16[512,512]{1,0:T(8,128)(2,1)}, bf16[512,512]{1,0:T(8,128)(2,1)S(1)}, u32[]{:S(2)}, u32[]{:S(2)}) collective-permute-start(bf16[512,512]{1,0:T(8,128)(2,1)} %uown.3), channel_id=1, source_target_pairs={{1,0},{2,1},{3,2},{4,3},{5,4},{6,5},{7,6},{8,7},{9,8},{10,9},{11,1... | collective-permute-start | bytes 1572872 | tf_op jit(solution)/shard_map/ppermute | solution.py:421
  6.1 0.0 collective-permute-start
  6.1 2.2 %shard_map.112.after = bf16[8,240,128]{2,1,0:T(8,128)(2,1)} custom-call(s32[2,6]{1,0:T(2,128)} %far_cols.1, bf16[512,512]{1,0:T(8,128)(2,1)} %uown.3, bf16[2,32,256]{2,1,0:T(8,128)(2,1)} %bitcast.8, bf16[2,2,6,32,32]{4,3,2,1,0:T(8,128)(2,1)} %coup.1), custom_call_target="tpu_custom_call" | custom-call | tf_op jit(solution)/shard_map/pallas_call | solution.py:464
  8.3 3.5 %all-to-all-start = ((bf16[8,240,128]{2,1,0:T(8,128)(2,1)}), bf16[8,240,128]{2,1,0:T(8,128)(2,1)S(1)}, u32[]{:S(2)}, u32[]{:S(2)}) async-start(bf16[8,240,128]{2,1,0:T(8,128)(2,1)} %shard_map.112.after), calls=%async_computation | async-start | bytes 983040 | tf_op jit(solution)/shard_map/all_to_all | solution.py:447
  11.8 0.0 copy-start.2
  11.8 0.0 copy-start.7
  11.8 0.0 copy-start.5
  11.9 0.0 copy-start.6
  11.9 3.5 %shard_map.113.w = bf16[2,512,1280]{2,1,0:T(8,128)(2,1)} custom-call(s32[2,5]{1,0:T(2,128)} %cols.1, s32[2]{0:T(128)} %count.1, s32[1]{0:T(128)} %bitcast.row0, bf16[2,2,5,256,256]{4,3,2,1,0:T(8,128)(2,1)} %tiles.1, bf16[8,240,128]{2,1,0:T(8,128)(2,1)} %shard_map.112.after), custom_call_target="tpu_custom_call" | custom-call | tf_op jit(solution)/shard_map/pallas_call | solution.py:473
  15.3 0.0 collective-permute-done.1.high.uhigh
  15.3 2.5 %collective-permute-done.low.ulow = bf16[512,512]{1,0:T(8,128)(2,1)S(1)} collective-permute-done((bf16[512,512]{1,0:T(8,128)(2,1)}, bf16[512,512]{1,0:T(8,128)(2,1)S(1)}, u32[]{:S(2)}, u32[]{:S(2)}) %collective-permute-start) | collective-permute-done | bytes 524320 | tf_op jit(solution)/shard_map/ppermute | solution.py:421
  17.8 0.0 copy-done.2
  17.8 0.0 copy-done.7
  17.8 0.0 copy-start
  17.8 1.7 %copy-done = bf16[2,512,1280]{2,1,0:T(8,128)(2,1)S(1)} copy-done((bf16[2,512,1280]{2,1,0:T(8,128)(2,1)S(1)}, bf16[2,512,1280]{2,1,0:T(8,128)(2,1)}, u32[]{:S(2)}) %copy-start) | copy-done | bytes 2621464
  19.6 1.5 %shard_map.114 = (f32[512,512]{1,0:T(8,128)S(1)}, f32[512,512]{1,0:T(8,128)S(1)}, f32[8,128]{1,0:T(8,128)S(1)}) custom-call(bf16[2,512,1280]{2,1,0:T(8,128)(2,1)S(1)} %copy-done, bf16[512,512]{1,0:T(8,128)(2,1)S(1)} %collective-permute-done.low.ulow, bf16[512,512]{1,0:T(8,128)(2,1)S(1)} %copy-done.2, bf16[512,512]{1,0:T(8,128)(2,1)S(1)} %collective-permute-done.1.high.uhigh, ...), custom_call_target="tpu_custom_call" | custom-call | flops 11500000256 | tf_op jit(solution)/shard_map/pallas_call | solution.py:479
  21.1 0.0 copy-start.3
  21.1 1.0 %copy-done.3 = f32[512,512]{1,0:T(8,128)} copy-done((f32[512,512]{1,0:T(8,128)}, f32[512,512]{1,0:T(8,128)S(1)}, u32[]{:S(2)}) %copy-start.3) | copy-done | bytes 1048600
  22.1 3.3 %all-to-all-done.held = bf16[8,240,128]{2,1,0:T(8,128)(2,1)S(1)} async-done(((bf16[8,240,128]{2,1,0:T(8,128)(2,1)}), bf16[8,240,128]{2,1,0:T(8,128)(2,1)S(1)}, u32[]{:S(2)}, u32[]{:S(2)}) %all-to-all-start) | async-done | bytes 491552 | tf_op jit(solution)/shard_map/all_to_all | solution.py:447
  25.4 1.3 %collective-permute-start.2 = (bf16[8,32,128]{2,1,0:T(8,128)(2,1)S(1)}, bf16[8,32,128]{2,1,0:T(8,128)(2,1)S(1)}, u32[]{:S(2)}, u32[]{:S(2)}) collective-permute-start(bf16[8,32,128]{2,1,0:T(8,128)(2,1)S(1)} %shard_map.115.refs_0_), channel_id=1, source_target_pairs={{0,1},{1,0},{2,3},{3,2},{4,5},{5,4},{6,7},{7,6},{8,9},{9,8},{10,11... | collective-permute-start | bytes 196616 | tf_op jit(solution)/shard_map/ppermute | solution.py:453
  26.8 0.1 reshape.18.cols
  26.9 0.8 %collective-permute-done.2.refs_1_ = bf16[8,32,128]{2,1,0:T(8,128)(2,1)S(1)} collective-permute-done((bf16[8,32,128]{2,1,0:T(8,128)(2,1)S(1)}, bf16[8,32,128]{2,1,0:T(8,128)(2,1)S(1)}, u32[]{:S(2)}, u32[]{:S(2)}) %collective-permute-start.2) | collective-permute-done | bytes 65568 | tf_op jit(solution)/shard_map/ppermute | solution.py:453
  27.7 1.1 %shard_map.116 = bf16[8,64,128]{2,1,0:T(8,128)(2,1)S(1)} custom-call(s32[96]{0:T(128)S(1)} %reshape.18.cols, s32[1]{0:T(128)} %bitcast.3.group, bf16[8,240,128]{2,1,0:T(8,128)(2,1)S(1)} %all-to-all-done.held, bf16[8,32,128]{2,1,0:T(8,128)(2,1)S(1)} %shard_map.115.refs_0_, bf16[8,32,128]{2,1,0:T(8,128)(2,1)S(1)} %collective-permute-done.2.refs_1_), custom_call_target="tpu_custom_call" | custom-call | tf_op jit(solution)/shard_map/pallas_call | solution.py:487
  28.8 11.3 %all_to_all.20.cmsg = bf16[8,64,128]{2,1,0:T(8,128)(2,1)S(1)} all-to-all(bf16[8,64,128]{2,1,0:T(8,128)(2,1)S(1)} %shard_map.116), channel_id=1, replica_groups={{0,2,4,6,8,10,12,14},{1,3,5,7,9,11,13,15},{16,18,20,22,24,26,28,30},{17..., dimensions={0} | all-to-all | bytes 262144 | tf_op jit(solution)/shard_map/all_to_all | solution.py:447
  40.1 0.0 copy-done.5
  40.1 0.0 copy-done.6
  40.1 0.0 copy-start.4
  40.1 1.2 %copy-done.4 = f32[512,512]{1,0:T(8,128)S(1)} copy-done((f32[512,512]{1,0:T(8,128)S(1)}, f32[512,512]{1,0:T(8,128)}, u32[]{:S(2)}) %copy-start.4) | copy-done | bytes 1048600
  41.3 1.0 %shard_map.117 = (bf16[528,512]{1,0:T(8,128)(2,1)S(1)}, bf16[8,32,128]{2,1,0:T(8,128)(2,1)S(1)}, f32[8,512]{1,0:T(8,128)S(1)}) custom-call(bf16[512,512]{1,0:T(8,128)(2,1)S(1)} %copy-done.2, f32[512,512]{1,0:T(8,128)S(1)} %copy-done.4, bf16[2,32,256]{2,1,0:T(8,128)(2,1)S(1)} %bitcast.4, bf16[2,32,256]{2,1,0:T(8,128)(2,1)S(1)} %bitcast.9, ...), custom_call_target="tpu_custom_call" | custom-call | tf_op jit(solution)/shard_map/pallas_call | solution.py:497
  42.3 0.8 collective-permute-start.4
  43.1 0.0 collective-permute-start.3
  43.1 1.0 %shard_map.118 = (bf16[528,512]{1,0:T(8,128)(2,1)S(1)}, bf16[8,80,128]{2,1,0:T(8,128)(2,1)S(1)}) custom-call(bf16[512,512]{1,0:T(8,128)(2,1)S(1)} %copy-done.2, f32[512,512]{1,0:T(8,128)S(1)} %get-tuple-element.18.near, bf16[2,32,256]{2,1,0:T(8,128)(2,1)S(1)} %bitcast.5, bf16[2,32,256]{2,1,0:T(8,128)(2,1)S(1)} %bitcast.10, ...), custom_call_target="tpu_custom_call" | custom-call | tf_op jit(solution)/shard_map/pallas_call | solution.py:504
  44.1 13.5 %all_to_all.21.refs_2_ = bf16[8,80,128]{2,1,0:T(8,128)(2,1)S(1)} all-to-all(bf16[8,80,128]{2,1,0:T(8,128)(2,1)S(1)} %get-tuple-element.21), channel_id=1, replica_groups={{0,2,4,6,8,10,12,14},{1,3,5,7,9,11,13,15},{16,18,20,22,24,26,28,30},{17..., dimensions={0} | all-to-all | bytes 327680 | tf_op jit(solution)/shard_map/all_to_all | solution.py:447
  57.6 0.0 collective-permute-start.5
  57.6 0.0 copy-start.1
  57.6 2.0 %collective-permute-start.7 = (bf16[528,512]{1,0:T(8,128)(2,1)S(1)}, bf16[528,512]{1,0:T(8,128)(2,1)S(1)}, u32[]{:S(2)}, u32[]{:S(2)}) collective-permute-start(bf16[528,512]{1,0:T(8,128)(2,1)S(1)} %get-tuple-element.23.vown), channel_id=1, source_target_pairs={{1,0},{2,1},{3,2},{4,3},{5,4},{6,5},{7,6},{8,7},{9,8},{10,9},{11,1... | collective-permute-start | bytes 1622024 | tf_op jit(solution)/shard_map/ppermute | solution.py:421
  59.7 0.0 collective-permute-start.6
  59.7 0.0 collective-permute-done.5.refs_3_
  59.7 0.0 collective-permute-done.4.after_high.vhigh
  59.7 0.0 collective-permute-done.3.after_low.vlow
  59.7 1.6 %shard_map.119 = bf16[8,80,128]{2,1,0:T(8,128)(2,1)S(1)} custom-call(s32[96]{0:T(128)S(1)} %reshape.18.cols, s32[1]{0:T(128)} %bitcast.3.group, bf16[528,512]{1,0:T(8,128)(2,1)S(1)} %collective-permute-done.3.after_low.vlow, bf16[528,512]{1,0:T(8,128)(2,1)S(1)} %collective-permute-done.4.after_high.vhigh, bf16[8,240,128]{2,1,0:T(8,128)(2,1)S(1)} %all-to-all-done.held, ...), custom_call_target="tpu_custom_call" | custom-call | flops 34500001792 | tf_op jit(solution)/shard_map/pallas_call | solution.py:513
  61.3 13.3 %all_to_all.22.cmsg = bf16[8,80,128]{2,1,0:T(8,128)(2,1)S(1)} all-to-all(bf16[8,80,128]{2,1,0:T(8,128)(2,1)S(1)} %shard_map.119), channel_id=1, replica_groups={{0,2,4,6,8,10,12,14},{1,3,5,7,9,11,13,15},{16,18,20,22,24,26,28,30},{17..., dimensions={0} | all-to-all | bytes 327680 | tf_op jit(solution)/shard_map/all_to_all | solution.py:447
  74.6 0.0 copy-done.1
  74.6 2.9 %shard_map.120 = (f32[2,512,512]{2,1,0:T(8,128)}, f32[2,512]{1,0:T(2,128)}, f32[2,512]{1,0:T(2,128)}, f32[8,512]{1,0:T(8,128)S(1)}) custom-call(bf16[2,512,1280]{2,1,0:T(8,128)(2,1)S(1)} %copy-done.1, bf16[512,512]{1,0:T(8,128)(2,1)S(1)} %collective-permute-done.low.ulow, bf16[512,512]{1,0:T(8,128)(2,1)S(1)} %copy-done.2, ...), custom_call_target="tpu_custom_call" | custom-call | tf_op jit(solution)/shard_map/pallas_call | solution.py:531
  77.5 0.0 collective-permute-done.7.vhigh
  77.5 0.0 collective-permute-done.6.vlow
  77.5 2.2 %shard_map.121 = f32[2,512,512]{2,1,0:T(8,128)} custom-call(f32[2,512,512]{2,1,0:T(8,128)} %get-tuple-element.22.begun, bf16[2,512,1280]{2,1,0:T(8,128)(2,1)S(1)} %copy-done.1, bf16[512,512]{1,0:T(8,128)(2,1)S(1)} %collective-permute-done.low.ulow, bf16[512,512]{1,0:T(8,128)(2,1)S(1)} %copy-done.2, ...), custom_call_target="tpu_custom_call", output_to_operand_aliasing={{}: (0, {})} | custom-call | tf_op jit(solution)/shard_map/pallas_call | solution.py:538
  (2 shorter events, 0.0 us)
Async XLA Ops:
  0.6 14.7 %collective-permute-start.1 = (bf16[512,512]{1,0:T(8,128)(2,1)}, bf16[512,512]{1,0:T(8,128)(2,1)S(1)}, u32[]{:S(2)}, u32[]{:S(2)}) collective-permute-start(bf16[512,512]{1,0:T(8,128)(2,1)} %uown.3), channel_id=1, source_target_pairs={{1,0},{2,1},{3,2},{4,3},{5,4},{6,5},{7,6},{8,7},{9,8},{10,9},{11,1... | collective-permute-start | bytes 1572872 | tf_op jit(solution)/shard_map/ppermute | solution.py:421
  6.1 11.7 %collective-permute-start = (bf16[512,512]{1,0:T(8,128)(2,1)}, bf16[512,512]{1,0:T(8,128)(2,1)S(1)}, u32[]{:S(2)}, u32[]{:S(2)}) collective-permute-start(bf16[512,512]{1,0:T(8,128)(2,1)} %uown.3), channel_id=1, source_target_pairs={{0,1},{1,2},{2,3},{3,4},{4,5},{5,6},{6,7},{7,8},{8,9},{9,10},{10,1... | collective-permute-start | bytes 1572872 | tf_op jit(solution)/shard_map/ppermute | solution.py:421
  8.3 17.1 %all-to-all-start = ((bf16[8,240,128]{2,1,0:T(8,128)(2,1)}), bf16[8,240,128]{2,1,0:T(8,128)(2,1)S(1)}, u32[]{:S(2)}, u32[]{:S(2)}) async-start(bf16[8,240,128]{2,1,0:T(8,128)(2,1)} %shard_map.112.after), calls=%async_computation | async-start | bytes 983040 | tf_op jit(solution)/shard_map/all_to_all | solution.py:447
  11.8 6.0 %copy-start.2 = (bf16[512,512]{1,0:T(8,128)(2,1)S(1)}, bf16[512,512]{1,0:T(8,128)(2,1)}, u32[]{:S(2)}) copy-start(bf16[512,512]{1,0:T(8,128)(2,1)} %uown.3) | copy-start | bytes 1572868
  11.8 6.0 %copy-start.7 = (f32[2,512]{1,0:T(2,128)S(1)}, f32[2,512]{1,0:T(2,128)}, u32[]{:S(2)}) copy-start(f32[2,512]{1,0:T(2,128)} %diag.5) | copy-start | bytes 12292
  11.8 28.2 %copy-start.5 = (bf16[2,256,32]{1,2,0:T(8,128)(2,1)S(1)}, bf16[2,256,32]{1,2,0:T(8,128)(2,1)}, u32[]{:S(2)}) copy-start(bf16[2,256,32]{1,2,0:T(8,128)(2,1)} %param.15) | copy-start | bytes 98308
  11.9 28.2 %copy-start.6 = (bf16[2,256,32]{1,2,0:T(8,128)(2,1)S(1)}, bf16[2,256,32]{1,2,0:T(8,128)(2,1)}, u32[]{:S(2)}) copy-start(bf16[2,256,32]{1,2,0:T(8,128)(2,1)} %param.16) | copy-start | bytes 98308
  17.8 1.7 %copy-start = (bf16[2,512,1280]{2,1,0:T(8,128)(2,1)S(1)}, bf16[2,512,1280]{2,1,0:T(8,128)(2,1)}, u32[]{:S(2)}) copy-start(bf16[2,512,1280]{2,1,0:T(8,128)(2,1)} %shard_map.113.w) | copy-start | bytes 7864324
  21.1 1.0 %copy-start.3 = (f32[512,512]{1,0:T(8,128)}, f32[512,512]{1,0:T(8,128)S(1)}, u32[]{:S(2)}) copy-start(f32[512,512]{1,0:T(8,128)S(1)} %get-tuple-element.15.near) | copy-start | bytes 3145732
  25.4 2.2 %collective-permute-start.2 = (bf16[8,32,128]{2,1,0:T(8,128)(2,1)S(1)}, bf16[8,32,128]{2,1,0:T(8,128)(2,1)S(1)}, u32[]{:S(2)}, u32[]{:S(2)}) collective-permute-start(bf16[8,32,128]{2,1,0:T(8,128)(2,1)S(1)} %shard_map.115.refs_0_), channel_id=1, source_target_pairs={{0,1},{1,0},{2,3},{3,2},{4,5},{5,4},{6,7},{7,6},{8,9},{9,8},{10,11... | collective-permute-start | bytes 196616 | tf_op jit(solution)/shard_map/ppermute | solution.py:453
  40.1 1.2 %copy-start.4 = (f32[512,512]{1,0:T(8,128)S(1)}, f32[512,512]{1,0:T(8,128)}, u32[]{:S(2)}) copy-start(f32[512,512]{1,0:T(8,128)} %copy-done.3) | copy-start | bytes 3145732
  42.3 17.4 %collective-permute-start.4 = (bf16[528,512]{1,0:T(8,128)(2,1)S(1)}, bf16[528,512]{1,0:T(8,128)(2,1)S(1)}, u32[]{:S(2)}, u32[]{:S(2)}) collective-permute-start(bf16[528,512]{1,0:T(8,128)(2,1)S(1)} %get-tuple-element.17.vown), channel_id=1, source_target_pairs={{1,0},{2,1},{3,2},{4,3},{5,4},{6,5},{7,6},{8,7},{9,8},{10,9},{11,1... | collective-permute-start | bytes 1622024 | tf_op jit(solution)/shard_map/ppermute | solution.py:421
  43.1 16.6 %collective-permute-start.3 = (bf16[528,512]{1,0:T(8,128)(2,1)S(1)}, bf16[528,512]{1,0:T(8,128)(2,1)S(1)}, u32[]{:S(2)}, u32[]{:S(2)}) collective-permute-start(bf16[528,512]{1,0:T(8,128)(2,1)S(1)} %get-tuple-element.17.vown), channel_id=1, source_target_pairs={{0,1},{1,2},{2,3},{3,4},{4,5},{5,6},{6,7},{7,8},{8,9},{9,10},{10,1... | collective-permute-start | bytes 1622024 | tf_op jit(solution)/shard_map/ppermute | solution.py:421
  57.6 2.1 %collective-permute-start.5 = (bf16[8,80,128]{2,1,0:T(8,128)(2,1)S(1)}, bf16[8,80,128]{2,1,0:T(8,128)(2,1)S(1)}, u32[]{:S(2)}, u32[]{:S(2)}) collective-permute-start(bf16[8,80,128]{2,1,0:T(8,128)(2,1)S(1)} %all_to_all.21.refs_2_), channel_id=1, source_target_pairs={{0,1},{1,0},{2,3},{3,2},{4,5},{5,4},{6,7},{7,6},{8,9},{9,8},{10,11... | collective-permute-start | bytes 491528 | tf_op jit(solution)/shard_map/ppermute | solution.py:453
  57.6 17.0 %copy-start.1 = (bf16[2,512,1280]{2,1,0:T(8,128)(2,1)S(1)}, bf16[2,512,1280]{2,1,0:T(8,128)(2,1)}, u32[]{:S(2)}) copy-start(bf16[2,512,1280]{2,1,0:T(8,128)(2,1)} %shard_map.113.w) | copy-start | bytes 7864324
  57.6 19.9 %collective-permute-start.7 = (bf16[528,512]{1,0:T(8,128)(2,1)S(1)}, bf16[528,512]{1,0:T(8,128)(2,1)S(1)}, u32[]{:S(2)}, u32[]{:S(2)}) collective-permute-start(bf16[528,512]{1,0:T(8,128)(2,1)S(1)} %get-tuple-element.23.vown), channel_id=1, source_target_pairs={{1,0},{2,1},{3,2},{4,3},{5,4},{6,5},{7,6},{8,7},{9,8},{10,9},{11,1... | collective-permute-start | bytes 1622024 | tf_op jit(solution)/shard_map/ppermute | solution.py:421
  59.7 17.9 %collective-permute-start.6 = (bf16[528,512]{1,0:T(8,128)(2,1)S(1)}, bf16[528,512]{1,0:T(8,128)(2,1)S(1)}, u32[]{:S(2)}, u32[]{:S(2)}) collective-permute-start(bf16[528,512]{1,0:T(8,128)(2,1)S(1)} %get-tuple-element.23.vown), channel_id=1, source_target_pairs={{0,1},{1,2},{2,3},{3,4},{4,5},{5,6},{6,7},{7,8},{8,9},{9,10},{10,1... | collective-permute-start | bytes 1622024 | tf_op jit(solution)/shard_map/ppermute | solution.py:421

commit v24 on v23

--- a/solution.py
+++ b/solution.py
@@ -291,7 +291,7 @@
         shift = join3(every, o)
         height = jnp.sum(shift * squares, axis=0, keepdims=True) / panels / scale_sq
         delta = shift - height
-        spread = join3(every, ops + 1 + o) + delta * delta * squares
+        spread = join3(every, ops + 1 + o) + delta * (delta * squares)
         norm = jnp.sqrt(jnp.sum(spread, axis=0, keepdims=True) / panels / scale_sq + EPSILON)
         heights.append(height)
         norms.append(norm)

time: 80.1 us -> 80.1 us (level)
  no operation moved by 1% of the time
where the time goes in v24:
time: 80.1 us; the launch traced here: 79.7 us
  blocking collectives  38.1 us (48%)
  Pallas kernels  17 us (21%)
  starting transfers between devices  13.1 us (16%)
  waiting for transfers between devices  6.64 us (8%)
  local copies, waits for them, and re-layouts  4.04 us (5%)
    all_to_all x3, blocking collectives, exchange(): lax.all_to_all(x, 'store', 0, 0, axis_index_groups=groups, tiled=True)  38.1 us
    ppermute x3, starting transfers between devices, ring(): lax.ppermute(block, 'store', backward)  8.31 us
    unnamed x16, local copies, waits for them, and re-layouts  3.96 us
    all_to_all x1, starting transfers between devices, exchange(): lax.all_to_all(x, 'store', 0, 0, axis_index_groups=groups, tiled=True)  3.48 us
    pallas_call x1, Pallas kernels, shards(): call(functools.partial(order_tiles, all_blocks), sds((blocks, ops * size,...  3.48 us
    all_to_all x1, waiting for transfers between devices, exchange(): lax.all_to_all(x, 'store', 0, 0, axis_index_groups=groups, tiled=True)  3.34 us
    pallas_call x1, Pallas kernels, shards(): call(final_first, [outs, sds((ops, columns), F32), sds((ops, columns), F3...  2.85 us
    ppermute x3, waiting for transfers between devices, ring(): lax.ppermute(block, 'store', forward)  2.48 us
  transfers between devices with their start and end apart: 9, of which 3 were waited for; matrix products, arithmetic and copies ran while one was open for 0% of the time, Pallas kernels for 16%

profile of v24, /device:TPU:0, one launch (start us, length us, event | category | flops | bytes accessed | tf_op | source)
XLA Modules:
  0.0 79.7 jit_solution(4107643928593046663)
XLA Ops:
  0.6 5.5 %collective-permute-start.1 = (bf16[512,512]{1,0:T(8,128)(2,1)}, bf16[512,512]{1,0:T(8,128)(2,1)S(1)}, u32[]{:S(2)}, u32[]{:S(2)}) collective-permute-start(bf16[512,512]{1,0:T(8,128)(2,1)} %uown.3), channel_id=1, source_target_pairs={{1,0},{2,1},{3,2},{4,3},{5,4},{6,5},{7,6},{8,7},{9,8},{10,9},{11,1... | collective-permute-start | bytes 1572872 | tf_op jit(solution)/shard_map/ppermute | solution.py:421
  6.1 0.0 collective-permute-start
  6.1 2.2 %shard_map.112.after = bf16[8,240,128]{2,1,0:T(8,128)(2,1)} custom-call(s32[2,6]{1,0:T(2,128)} %far_cols.1, bf16[512,512]{1,0:T(8,128)(2,1)} %uown.3, bf16[2,32,256]{2,1,0:T(8,128)(2,1)} %bitcast.8, bf16[2,2,6,32,32]{4,3,2,1,0:T(8,128)(2,1)} %coup.1), custom_call_target="tpu_custom_call" | custom-call | tf_op jit(solution)/shard_map/pallas_call | solution.py:464
  8.3 3.5 %all-to-all-start = ((bf16[8,240,128]{2,1,0:T(8,128)(2,1)}), bf16[8,240,128]{2,1,0:T(8,128)(2,1)S(1)}, u32[]{:S(2)}, u32[]{:S(2)}) async-start(bf16[8,240,128]{2,1,0:T(8,128)(2,1)} %shard_map.112.after), calls=%async_computation | async-start | bytes 983040 | tf_op jit(solution)/shard_map/all_to_all | solution.py:447
  11.8 0.0 copy-start.2
  11.8 0.0 copy-start.7
  11.8 0.0 copy-start.5
  11.9 0.0 copy-start.6
  11.9 3.5 %shard_map.113.w = bf16[2,512,1280]{2,1,0:T(8,128)(2,1)} custom-call(s32[2,5]{1,0:T(2,128)} %cols.1, s32[2]{0:T(128)} %count.1, s32[1]{0:T(128)} %bitcast.row0, bf16[2,2,5,256,256]{4,3,2,1,0:T(8,128)(2,1)} %tiles.1, bf16[8,240,128]{2,1,0:T(8,128)(2,1)} %shard_map.112.after), custom_call_target="tpu_custom_call" | custom-call | tf_op jit(solution)/shard_map/pallas_call | solution.py:473
  15.3 0.0 collective-permute-done.1.high.uhigh
  15.3 2.5 %collective-permute-done.low.ulow = bf16[512,512]{1,0:T(8,128)(2,1)S(1)} collective-permute-done((bf16[512,512]{1,0:T(8,128)(2,1)}, bf16[512,512]{1,0:T(8,128)(2,1)S(1)}, u32[]{:S(2)}, u32[]{:S(2)}) %collective-permute-start) | collective-permute-done | bytes 524320 | tf_op jit(solution)/shard_map/ppermute | solution.py:421
  17.8 0.0 copy-done.2
  17.8 0.0 copy-done.7
  17.8 0.0 copy-start
  17.8 1.7 %copy-done = bf16[2,512,1280]{2,1,0:T(8,128)(2,1)S(1)} copy-done((bf16[2,512,1280]{2,1,0:T(8,128)(2,1)S(1)}, bf16[2,512,1280]{2,1,0:T(8,128)(2,1)}, u32[]{:S(2)}) %copy-start) | copy-done | bytes 2621464
  19.6 1.5 %shard_map.114 = (f32[512,512]{1,0:T(8,128)S(1)}, f32[512,512]{1,0:T(8,128)S(1)}, f32[8,128]{1,0:T(8,128)S(1)}) custom-call(bf16[2,512,1280]{2,1,0:T(8,128)(2,1)S(1)} %copy-done, bf16[512,512]{1,0:T(8,128)(2,1)S(1)} %collective-permute-done.low.ulow, bf16[512,512]{1,0:T(8,128)(2,1)S(1)} %copy-done.2, bf16[512,512]{1,0:T(8,128)(2,1)S(1)} %collective-permute-done.1.high.uhigh, ...), custom_call_target="tpu_custom_call" | custom-call | flops 11500000256 | tf_op jit(solution)/shard_map/pallas_call | solution.py:479
  21.1 0.0 copy-start.3
  21.1 1.0 %copy-done.3 = f32[512,512]{1,0:T(8,128)} copy-done((f32[512,512]{1,0:T(8,128)}, f32[512,512]{1,0:T(8,128)S(1)}, u32[]{:S(2)}) %copy-start.3) | copy-done | bytes 1048600
  22.1 3.3 %all-to-all-done.held = bf16[8,240,128]{2,1,0:T(8,128)(2,1)S(1)} async-done(((bf16[8,240,128]{2,1,0:T(8,128)(2,1)}), bf16[8,240,128]{2,1,0:T(8,128)(2,1)S(1)}, u32[]{:S(2)}, u32[]{:S(2)}) %all-to-all-start) | async-done | bytes 491552 | tf_op jit(solution)/shard_map/all_to_all | solution.py:447
  25.4 1.3 %collective-permute-start.2 = (bf16[8,32,128]{2,1,0:T(8,128)(2,1)S(1)}, bf16[8,32,128]{2,1,0:T(8,128)(2,1)S(1)}, u32[]{:S(2)}, u32[]{:S(2)}) collective-permute-start(bf16[8,32,128]{2,1,0:T(8,128)(2,1)S(1)} %shard_map.115.refs_0_), channel_id=1, source_target_pairs={{0,1},{1,0},{2,3},{3,2},{4,5},{5,4},{6,7},{7,6},{8,9},{9,8},{10,11... | collective-permute-start | bytes 196616 | tf_op jit(solution)/shard_map/ppermute | solution.py:453
  26.8 0.1 reshape.18.cols
  26.9 0.8 %collective-permute-done.2.refs_1_ = bf16[8,32,128]{2,1,0:T(8,128)(2,1)S(1)} collective-permute-done((bf16[8,32,128]{2,1,0:T(8,128)(2,1)S(1)}, bf16[8,32,128]{2,1,0:T(8,128)(2,1)S(1)}, u32[]{:S(2)}, u32[]{:S(2)}) %collective-permute-start.2) | collective-permute-done | bytes 65568 | tf_op jit(solution)/shard_map/ppermute | solution.py:453
  27.7 1.1 %shard_map.116 = bf16[8,64,128]{2,1,0:T(8,128)(2,1)S(1)} custom-call(s32[96]{0:T(128)S(1)} %reshape.18.cols, s32[1]{0:T(128)} %bitcast.3.group, bf16[8,240,128]{2,1,0:T(8,128)(2,1)S(1)} %all-to-all-done.held, bf16[8,32,128]{2,1,0:T(8,128)(2,1)S(1)} %shard_map.115.refs_0_, bf16[8,32,128]{2,1,0:T(8,128)(2,1)S(1)} %collective-permute-done.2.refs_1_), custom_call_target="tpu_custom_call" | custom-call | tf_op jit(solution)/shard_map/pallas_call | solution.py:487
  28.8 11.3 %all_to_all.20.cmsg = bf16[8,64,128]{2,1,0:T(8,128)(2,1)S(1)} all-to-all(bf16[8,64,128]{2,1,0:T(8,128)(2,1)S(1)} %shard_map.116), channel_id=1, replica_groups={{0,2,4,6,8,10,12,14},{1,3,5,7,9,11,13,15},{16,18,20,22,24,26,28,30},{17..., dimensions={0} | all-to-all | bytes 262144 | tf_op jit(solution)/shard_map/all_to_all | solution.py:447
  40.1 0.0 copy-done.5
  40.1 0.0 copy-done.6
  40.1 0.0 copy-start.4
  40.1 1.2 %copy-done.4 = f32[512,512]{1,0:T(8,128)S(1)} copy-done((f32[512,512]{1,0:T(8,128)S(1)}, f32[512,512]{1,0:T(8,128)}, u32[]{:S(2)}) %copy-start.4) | copy-done | bytes 1048600
  41.3 1.0 %shard_map.117 = (bf16[528,512]{1,0:T(8,128)(2,1)S(1)}, bf16[8,32,128]{2,1,0:T(8,128)(2,1)S(1)}, f32[8,512]{1,0:T(8,128)S(1)}) custom-call(bf16[512,512]{1,0:T(8,128)(2,1)S(1)} %copy-done.2, f32[512,512]{1,0:T(8,128)S(1)} %copy-done.4, bf16[2,32,256]{2,1,0:T(8,128)(2,1)S(1)} %bitcast.4, bf16[2,32,256]{2,1,0:T(8,128)(2,1)S(1)} %bitcast.9, ...), custom_call_target="tpu_custom_call" | custom-call | tf_op jit(solution)/shard_map/pallas_call | solution.py:497
  42.3 0.8 collective-permute-start.4
  43.1 0.0 collective-permute-start.3
  43.1 1.0 %shard_map.118 = (bf16[528,512]{1,0:T(8,128)(2,1)S(1)}, bf16[8,80,128]{2,1,0:T(8,128)(2,1)S(1)}) custom-call(bf16[512,512]{1,0:T(8,128)(2,1)S(1)} %copy-done.2, f32[512,512]{1,0:T(8,128)S(1)} %get-tuple-element.18.near, bf16[2,32,256]{2,1,0:T(8,128)(2,1)S(1)} %bitcast.5, bf16[2,32,256]{2,1,0:T(8,128)(2,1)S(1)} %bitcast.10, ...), custom_call_target="tpu_custom_call" | custom-call | tf_op jit(solution)/shard_map/pallas_call | solution.py:504
  44.1 13.5 %all_to_all.21.refs_2_ = bf16[8,80,128]{2,1,0:T(8,128)(2,1)S(1)} all-to-all(bf16[8,80,128]{2,1,0:T(8,128)(2,1)S(1)} %get-tuple-element.21), channel_id=1, replica_groups={{0,2,4,6,8,10,12,14},{1,3,5,7,9,11,13,15},{16,18,20,22,24,26,28,30},{17..., dimensions={0} | all-to-all | bytes 327680 | tf_op jit(solution)/shard_map/all_to_all | solution.py:447
  57.6 0.0 collective-permute-start.5
  57.6 0.0 copy-start.1
  57.6 2.0 %collective-permute-start.7 = (bf16[528,512]{1,0:T(8,128)(2,1)S(1)}, bf16[528,512]{1,0:T(8,128)(2,1)S(1)}, u32[]{:S(2)}, u32[]{:S(2)}) collective-permute-start(bf16[528,512]{1,0:T(8,128)(2,1)S(1)} %get-tuple-element.23.vown), channel_id=1, source_target_pairs={{1,0},{2,1},{3,2},{4,3},{5,4},{6,5},{7,6},{8,7},{9,8},{10,9},{11,1... | collective-permute-start | bytes 1622024 | tf_op jit(solution)/shard_map/ppermute | solution.py:421
  59.7 0.0 collective-permute-start.6
  59.7 0.0 collective-permute-done.5.refs_3_
  59.7 0.0 collective-permute-done.4.after_high.vhigh
  59.7 0.0 collective-permute-done.3.after_low.vlow
  59.7 1.6 %shard_map.119 = bf16[8,80,128]{2,1,0:T(8,128)(2,1)S(1)} custom-call(s32[96]{0:T(128)S(1)} %reshape.18.cols, s32[1]{0:T(128)} %bitcast.3.group, bf16[528,512]{1,0:T(8,128)(2,1)S(1)} %collective-permute-done.3.after_low.vlow, bf16[528,512]{1,0:T(8,128)(2,1)S(1)} %collective-permute-done.4.after_high.vhigh, bf16[8,240,128]{2,1,0:T(8,128)(2,1)S(1)} %all-to-all-done.held, ...), custom_call_target="tpu_custom_call" | custom-call | flops 34500001792 | tf_op jit(solution)/shard_map/pallas_call | solution.py:513
  61.3 13.3 %all_to_all.22.cmsg = bf16[8,80,128]{2,1,0:T(8,128)(2,1)S(1)} all-to-all(bf16[8,80,128]{2,1,0:T(8,128)(2,1)S(1)} %shard_map.119), channel_id=1, replica_groups={{0,2,4,6,8,10,12,14},{1,3,5,7,9,11,13,15},{16,18,20,22,24,26,28,30},{17..., dimensions={0} | all-to-all | bytes 327680 | tf_op jit(solution)/shard_map/all_to_all | solution.py:447
  74.6 0.0 copy-done.1
  74.6 2.9 %shard_map.120 = (f32[2,512,512]{2,1,0:T(8,128)}, f32[2,512]{1,0:T(2,128)}, f32[2,512]{1,0:T(2,128)}, f32[8,512]{1,0:T(8,128)S(1)}) custom-call(bf16[2,512,1280]{2,1,0:T(8,128)(2,1)S(1)} %copy-done.1, bf16[512,512]{1,0:T(8,128)(2,1)S(1)} %collective-permute-done.low.ulow, bf16[512,512]{1,0:T(8,128)(2,1)S(1)} %copy-done.2, ...), custom_call_target="tpu_custom_call" | custom-call | tf_op jit(solution)/shard_map/pallas_call | solution.py:531
  77.5 0.0 collective-permute-done.7.vhigh
  77.5 0.0 collective-permute-done.6.vlow
  77.5 2.2 %shard_map.121 = f32[2,512,512]{2,1,0:T(8,128)} custom-call(f32[2,512,512]{2,1,0:T(8,128)} %get-tuple-element.22.begun, bf16[2,512,1280]{2,1,0:T(8,128)(2,1)S(1)} %copy-done.1, bf16[512,512]{1,0:T(8,128)(2,1)S(1)} %collective-permute-done.low.ulow, bf16[512,512]{1,0:T(8,128)(2,1)S(1)} %copy-done.2, ...), custom_call_target="tpu_custom_call", output_to_operand_aliasing={{}: (0, {})} | custom-call | tf_op jit(solution)/shard_map/pallas_call | solution.py:538
  (2 shorter events, 0.0 us)
Async XLA Ops:
  0.6 14.7 %collective-permute-start.1 = (bf16[512,512]{1,0:T(8,128)(2,1)}, bf16[512,512]{1,0:T(8,128)(2,1)S(1)}, u32[]{:S(2)}, u32[]{:S(2)}) collective-permute-start(bf16[512,512]{1,0:T(8,128)(2,1)} %uown.3), channel_id=1, source_target_pairs={{1,0},{2,1},{3,2},{4,3},{5,4},{6,5},{7,6},{8,7},{9,8},{10,9},{11,1... | collective-permute-start | bytes 1572872 | tf_op jit(solution)/shard_map/ppermute | solution.py:421
  6.1 11.7 %collective-permute-start = (bf16[512,512]{1,0:T(8,128)(2,1)}, bf16[512,512]{1,0:T(8,128)(2,1)S(1)}, u32[]{:S(2)}, u32[]{:S(2)}) collective-permute-start(bf16[512,512]{1,0:T(8,128)(2,1)} %uown.3), channel_id=1, source_target_pairs={{0,1},{1,2},{2,3},{3,4},{4,5},{5,6},{6,7},{7,8},{8,9},{9,10},{10,1... | collective-permute-start | bytes 1572872 | tf_op jit(solution)/shard_map/ppermute | solution.py:421
  8.3 17.1 %all-to-all-start = ((bf16[8,240,128]{2,1,0:T(8,128)(2,1)}), bf16[8,240,128]{2,1,0:T(8,128)(2,1)S(1)}, u32[]{:S(2)}, u32[]{:S(2)}) async-start(bf16[8,240,128]{2,1,0:T(8,128)(2,1)} %shard_map.112.after), calls=%async_computation | async-start | bytes 983040 | tf_op jit(solution)/shard_map/all_to_all | solution.py:447
  11.8 6.0 %copy-start.2 = (bf16[512,512]{1,0:T(8,128)(2,1)S(1)}, bf16[512,512]{1,0:T(8,128)(2,1)}, u32[]{:S(2)}) copy-start(bf16[512,512]{1,0:T(8,128)(2,1)} %uown.3) | copy-start | bytes 1572868
  11.8 6.0 %copy-start.7 = (f32[2,512]{1,0:T(2,128)S(1)}, f32[2,512]{1,0:T(2,128)}, u32[]{:S(2)}) copy-start(f32[2,512]{1,0:T(2,128)} %diag.5) | copy-start | bytes 12292
  11.8 28.2 %copy-start.5 = (bf16[2,256,32]{1,2,0:T(8,128)(2,1)S(1)}, bf16[2,256,32]{1,2,0:T(8,128)(2,1)}, u32[]{:S(2)}) copy-start(bf16[2,256,32]{1,2,0:T(8,128)(2,1)} %param.15) | copy-start | bytes 98308
  11.9 28.2 %copy-start.6 = (bf16[2,256,32]{1,2,0:T(8,128)(2,1)S(1)}, bf16[2,256,32]{1,2,0:T(8,128)(2,1)}, u32[]{:S(2)}) copy-start(bf16[2,256,32]{1,2,0:T(8,128)(2,1)} %param.16) | copy-start | bytes 98308
  17.8 1.7 %copy-start = (bf16[2,512,1280]{2,1,0:T(8,128)(2,1)S(1)}, bf16[2,512,1280]{2,1,0:T(8,128)(2,1)}, u32[]{:S(2)}) copy-start(bf16[2,512,1280]{2,1,0:T(8,128)(2,1)} %shard_map.113.w) | copy-start | bytes 7864324
  21.1 1.0 %copy-start.3 = (f32[512,512]{1,0:T(8,128)}, f32[512,512]{1,0:T(8,128)S(1)}, u32[]{:S(2)}) copy-start(f32[512,512]{1,0:T(8,128)S(1)} %get-tuple-element.15.near) | copy-start | bytes 3145732
  25.4 2.2 %collective-permute-start.2 = (bf16[8,32,128]{2,1,0:T(8,128)(2,1)S(1)}, bf16[8,32,128]{2,1,0:T(8,128)(2,1)S(1)}, u32[]{:S(2)}, u32[]{:S(2)}) collective-permute-start(bf16[8,32,128]{2,1,0:T(8,128)(2,1)S(1)} %shard_map.115.refs_0_), channel_id=1, source_target_pairs={{0,1},{1,0},{2,3},{3,2},{4,5},{5,4},{6,7},{7,6},{8,9},{9,8},{10,11... | collective-permute-start | bytes 196616 | tf_op jit(solution)/shard_map/ppermute | solution.py:453
  40.1 1.2 %copy-start.4 = (f32[512,512]{1,0:T(8,128)S(1)}, f32[512,512]{1,0:T(8,128)}, u32[]{:S(2)}) copy-start(f32[512,512]{1,0:T(8,128)} %copy-done.3) | copy-start | bytes 3145732
  42.3 17.4 %collective-permute-start.4 = (bf16[528,512]{1,0:T(8,128)(2,1)S(1)}, bf16[528,512]{1,0:T(8,128)(2,1)S(1)}, u32[]{:S(2)}, u32[]{:S(2)}) collective-permute-start(bf16[528,512]{1,0:T(8,128)(2,1)S(1)} %get-tuple-element.17.vown), channel_id=1, source_target_pairs={{1,0},{2,1},{3,2},{4,3},{5,4},{6,5},{7,6},{8,7},{9,8},{10,9},{11,1... | collective-permute-start | bytes 1622024 | tf_op jit(solution)/shard_map/ppermute | solution.py:421
  43.1 16.6 %collective-permute-start.3 = (bf16[528,512]{1,0:T(8,128)(2,1)S(1)}, bf16[528,512]{1,0:T(8,128)(2,1)S(1)}, u32[]{:S(2)}, u32[]{:S(2)}) collective-permute-start(bf16[528,512]{1,0:T(8,128)(2,1)S(1)} %get-tuple-element.17.vown), channel_id=1, source_target_pairs={{0,1},{1,2},{2,3},{3,4},{4,5},{5,6},{6,7},{7,8},{8,9},{9,10},{10,1... | collective-permute-start | bytes 1622024 | tf_op jit(solution)/shard_map/ppermute | solution.py:421
  57.6 2.1 %collective-permute-start.5 = (bf16[8,80,128]{2,1,0:T(8,128)(2,1)S(1)}, bf16[8,80,128]{2,1,0:T(8,128)(2,1)S(1)}, u32[]{:S(2)}, u32[]{:S(2)}) collective-permute-start(bf16[8,80,128]{2,1,0:T(8,128)(2,1)S(1)} %all_to_all.21.refs_2_), channel_id=1, source_target_pairs={{0,1},{1,0},{2,3},{3,2},{4,5},{5,4},{6,7},{7,6},{8,9},{9,8},{10,11... | collective-permute-start | bytes 491528 | tf_op jit(solution)/shard_map/ppermute | solution.py:453
  57.6 17.0 %copy-start.1 = (bf16[2,512,1280]{2,1,0:T(8,128)(2,1)S(1)}, bf16[2,512,1280]{2,1,0:T(8,128)(2,1)}, u32[]{:S(2)}) copy-start(bf16[2,512,1280]{2,1,0:T(8,128)(2,1)} %shard_map.113.w) | copy-start | bytes 7864324
  57.6 19.9 %collective-permute-start.7 = (bf16[528,512]{1,0:T(8,128)(2,1)S(1)}, bf16[528,512]{1,0:T(8,128)(2,1)S(1)}, u32[]{:S(2)}, u32[]{:S(2)}) collective-permute-start(bf16[528,512]{1,0:T(8,128)(2,1)S(1)} %get-tuple-element.23.vown), channel_id=1, source_target_pairs={{1,0},{2,1},{3,2},{4,3},{5,4},{6,5},{7,6},{8,7},{9,8},{10,9},{11,1... | collective-permute-start | bytes 1622024 | tf_op jit(solution)/shard_map/ppermute | solution.py:421
  59.7 17.9 %collective-permute-start.6 = (bf16[528,512]{1,0:T(8,128)(2,1)S(1)}, bf16[528,512]{1,0:T(8,128)(2,1)S(1)}, u32[]{:S(2)}, u32[]{:S(2)}) collective-permute-start(bf16[528,512]{1,0:T(8,128)(2,1)S(1)} %get-tuple-element.23.vown), channel_id=1, source_target_pairs={{0,1},{1,2},{2,3},{3,4},{4,5},{5,6},{6,7},{7,8},{8,9},{9,10},{10,1... | collective-permute-start | bytes 1622024 | tf_op jit(solution)/shard_map/ppermute | solution.py:421

commit v25 on v24

--- a/solution.py
+++ b/solution.py
@@ -166,13 +166,14 @@
         out[s] = halves(c[0], c[1])[0].astype(BF16)
 
 
-def take_coefs(cmsg, coef, rows):
+def take_coefs(cmsg, coef, o, rank):
+    rows = slice(o * rank, (o + 1) * rank)
     for pair in range(SLICES // 2):
         parts = halves(
-            cmsg[2 * pair, 0:rows, :].astype(F32), cmsg[2 * pair + 1, 0:rows, :].astype(F32)
+            cmsg[2 * pair, rows, :].astype(F32), cmsg[2 * pair + 1, rows, :].astype(F32)
         )
         for b in range(2):
-            coef[b, :, pair * LANES:(pair + 1) * LANES] = parts[b].astype(BF16)
+            coef[b, rows, pair * LANES:(pair + 1) * LANES] = parts[b].astype(BF16)
 
 
 def near_product(tiles, parts, b, blocks, size):
@@ -218,7 +219,7 @@
 def image_part(own, near, left, right, cmsg, out, z_out, image, coef, o):
     blocks, rank, size = right.shape
     rows, columns = own.shape
-    take_coefs(cmsg, coef, cmsg.shape[1])
+    take_coefs(cmsg, coef, o, rank)
     squares, inner = 0.0, 0.0
     for b in range(blocks):
         here = slice(b * size, (b + 1) * size)
@@ -325,7 +326,7 @@
     blocks, rank, size = left.shape
     rows, columns = u3[1].shape
     ops = w.shape[1] // size
-    take_coefs(cmsg, coef, ops * rank)
+    take_coefs(cmsg, coef, o, rank)
     for at, (u, v) in enumerate(zip(u3, v3)):
         value = v[0:rows, :].astype(F32) * factor + u[...].astype(F32) * changes[at]
         ext[at] = value.astype(BF16)

time: 80.1 us -> 80.1 us (level)
  no operation moved by 1% of the time
where the time goes in v25:
time: 80.1 us; the launch traced here: 79.7 us
  blocking collectives  38.1 us (48%)
  Pallas kernels  16.9 us (21%)
  starting transfers between devices  13.1 us (16%)
  waiting for transfers between devices  6.64 us (8%)
  local copies, waits for them, and re-layouts  4.04 us (5%)
    all_to_all x3, blocking collectives, exchange(): lax.all_to_all(x, 'store', 0, 0, axis_index_groups=groups, tiled=True)  38.1 us
    ppermute x3, starting transfers between devices, ring(): lax.ppermute(block, 'store', backward)  8.3 us
    unnamed x16, local copies, waits for them, and re-layouts  3.96 us
    all_to_all x1, starting transfers between devices, exchange(): lax.all_to_all(x, 'store', 0, 0, axis_index_groups=groups, tiled=True)  3.48 us
    pallas_call x1, Pallas kernels, shards(): call(functools.partial(order_tiles, all_blocks), sds((blocks, ops * size,...  3.48 us
    all_to_all x1, waiting for transfers between devices, exchange(): lax.all_to_all(x, 'store', 0, 0, axis_index_groups=groups, tiled=True)  3.34 us
    pallas_call x1, Pallas kernels, shards(): call(final_first, [outs, sds((ops, columns), F32), sds((ops, columns), F3...  2.85 us
    ppermute x3, waiting for transfers between devices, ring(): lax.ppermute(block, 'store', forward)  2.48 us
  transfers between devices with their start and end apart: 9, of which 3 were waited for; matrix products, arithmetic and copies ran while one was open for 0% of the time, Pallas kernels for 16%

profile of v25, /device:TPU:0, one launch (start us, length us, event | category | flops | bytes accessed | tf_op | source)
XLA Modules:
  0.0 79.7 jit_solution(9853766725015055178)
XLA Ops:
  0.6 5.5 %collective-permute-start.1 = (bf16[512,512]{1,0:T(8,128)(2,1)}, bf16[512,512]{1,0:T(8,128)(2,1)S(1)}, u32[]{:S(2)}, u32[]{:S(2)}) collective-permute-start(bf16[512,512]{1,0:T(8,128)(2,1)} %uown.3), channel_id=1, source_target_pairs={{1,0},{2,1},{3,2},{4,3},{5,4},{6,5},{7,6},{8,7},{9,8},{10,9},{11,1... | collective-permute-start | bytes 1572872 | tf_op jit(solution)/shard_map/ppermute | solution.py:422
  6.1 0.0 collective-permute-start
  6.1 2.2 %shard_map.112.after = bf16[8,240,128]{2,1,0:T(8,128)(2,1)} custom-call(s32[2,6]{1,0:T(2,128)} %far_cols.1, bf16[512,512]{1,0:T(8,128)(2,1)} %uown.3, bf16[2,32,256]{2,1,0:T(8,128)(2,1)} %bitcast.8, bf16[2,2,6,32,32]{4,3,2,1,0:T(8,128)(2,1)} %coup.1), custom_call_target="tpu_custom_call" | custom-call | tf_op jit(solution)/shard_map/pallas_call | solution.py:465
  8.3 3.5 %all-to-all-start = ((bf16[8,240,128]{2,1,0:T(8,128)(2,1)}), bf16[8,240,128]{2,1,0:T(8,128)(2,1)S(1)}, u32[]{:S(2)}, u32[]{:S(2)}) async-start(bf16[8,240,128]{2,1,0:T(8,128)(2,1)} %shard_map.112.after), calls=%async_computation | async-start | bytes 983040 | tf_op jit(solution)/shard_map/all_to_all | solution.py:448
  11.8 0.0 copy-start.2
  11.8 0.0 copy-start.7
  11.8 0.0 copy-start.5
  11.9 0.0 copy-start.6
  11.9 3.5 %shard_map.113.w = bf16[2,512,1280]{2,1,0:T(8,128)(2,1)} custom-call(s32[2,5]{1,0:T(2,128)} %cols.1, s32[2]{0:T(128)} %count.1, s32[1]{0:T(128)} %bitcast.row0, bf16[2,2,5,256,256]{4,3,2,1,0:T(8,128)(2,1)} %tiles.1, bf16[8,240,128]{2,1,0:T(8,128)(2,1)} %shard_map.112.after), custom_call_target="tpu_custom_call" | custom-call | tf_op jit(solution)/shard_map/pallas_call | solution.py:474
  15.3 0.0 collective-permute-done.1.high.uhigh
  15.3 2.5 %collective-permute-done.low.ulow = bf16[512,512]{1,0:T(8,128)(2,1)S(1)} collective-permute-done((bf16[512,512]{1,0:T(8,128)(2,1)}, bf16[512,512]{1,0:T(8,128)(2,1)S(1)}, u32[]{:S(2)}, u32[]{:S(2)}) %collective-permute-start) | collective-permute-done | bytes 524320 | tf_op jit(solution)/shard_map/ppermute | solution.py:422
  17.8 0.0 copy-done.2
  17.8 0.0 copy-done.7
  17.8 0.0 copy-start
  17.8 1.7 %copy-done = bf16[2,512,1280]{2,1,0:T(8,128)(2,1)S(1)} copy-done((bf16[2,512,1280]{2,1,0:T(8,128)(2,1)S(1)}, bf16[2,512,1280]{2,1,0:T(8,128)(2,1)}, u32[]{:S(2)}) %copy-start) | copy-done | bytes 2621464
  19.6 1.5 %shard_map.114 = (f32[512,512]{1,0:T(8,128)S(1)}, f32[512,512]{1,0:T(8,128)S(1)}, f32[8,128]{1,0:T(8,128)S(1)}) custom-call(bf16[2,512,1280]{2,1,0:T(8,128)(2,1)S(1)} %copy-done, bf16[512,512]{1,0:T(8,128)(2,1)S(1)} %collective-permute-done.low.ulow, bf16[512,512]{1,0:T(8,128)(2,1)S(1)} %copy-done.2, bf16[512,512]{1,0:T(8,128)(2,1)S(1)} %collective-permute-done.1.high.uhigh, ...), custom_call_target="tpu_custom_call" | custom-call | flops 11500000256 | tf_op jit(solution)/shard_map/pallas_call | solution.py:480
  21.1 0.0 copy-start.3
  21.1 1.0 %copy-done.3 = f32[512,512]{1,0:T(8,128)} copy-done((f32[512,512]{1,0:T(8,128)}, f32[512,512]{1,0:T(8,128)S(1)}, u32[]{:S(2)}) %copy-start.3) | copy-done | bytes 1048600
  22.1 3.3 %all-to-all-done.held = bf16[8,240,128]{2,1,0:T(8,128)(2,1)S(1)} async-done(((bf16[8,240,128]{2,1,0:T(8,128)(2,1)}), bf16[8,240,128]{2,1,0:T(8,128)(2,1)S(1)}, u32[]{:S(2)}, u32[]{:S(2)}) %all-to-all-start) | async-done | bytes 491552 | tf_op jit(solution)/shard_map/all_to_all | solution.py:448
  25.4 1.3 %collective-permute-start.2 = (bf16[8,32,128]{2,1,0:T(8,128)(2,1)S(1)}, bf16[8,32,128]{2,1,0:T(8,128)(2,1)S(1)}, u32[]{:S(2)}, u32[]{:S(2)}) collective-permute-start(bf16[8,32,128]{2,1,0:T(8,128)(2,1)S(1)} %shard_map.115.refs_0_), channel_id=1, source_target_pairs={{0,1},{1,0},{2,3},{3,2},{4,5},{5,4},{6,7},{7,6},{8,9},{9,8},{10,11... | collective-permute-start | bytes 196616 | tf_op jit(solution)/shard_map/ppermute | solution.py:454
  26.8 0.1 reshape.18.cols
  26.9 0.8 %collective-permute-done.2.refs_1_ = bf16[8,32,128]{2,1,0:T(8,128)(2,1)S(1)} collective-permute-done((bf16[8,32,128]{2,1,0:T(8,128)(2,1)S(1)}, bf16[8,32,128]{2,1,0:T(8,128)(2,1)S(1)}, u32[]{:S(2)}, u32[]{:S(2)}) %collective-permute-start.2) | collective-permute-done | bytes 65568 | tf_op jit(solution)/shard_map/ppermute | solution.py:454
  27.7 1.1 %shard_map.116 = bf16[8,64,128]{2,1,0:T(8,128)(2,1)S(1)} custom-call(s32[96]{0:T(128)S(1)} %reshape.18.cols, s32[1]{0:T(128)} %bitcast.3.group, bf16[8,240,128]{2,1,0:T(8,128)(2,1)S(1)} %all-to-all-done.held, bf16[8,32,128]{2,1,0:T(8,128)(2,1)S(1)} %shard_map.115.refs_0_, bf16[8,32,128]{2,1,0:T(8,128)(2,1)S(1)} %collective-permute-done.2.refs_1_), custom_call_target="tpu_custom_call" | custom-call | tf_op jit(solution)/shard_map/pallas_call | solution.py:488
  28.8 11.3 %all_to_all.20.cmsg = bf16[8,64,128]{2,1,0:T(8,128)(2,1)S(1)} all-to-all(bf16[8,64,128]{2,1,0:T(8,128)(2,1)S(1)} %shard_map.116), channel_id=1, replica_groups={{0,2,4,6,8,10,12,14},{1,3,5,7,9,11,13,15},{16,18,20,22,24,26,28,30},{17..., dimensions={0} | all-to-all | bytes 262144 | tf_op jit(solution)/shard_map/all_to_all | solution.py:448
  40.1 0.0 copy-done.5
  40.1 0.0 copy-done.6
  40.1 0.0 copy-start.4
  40.1 1.2 %copy-done.4 = f32[512,512]{1,0:T(8,128)S(1)} copy-done((f32[512,512]{1,0:T(8,128)S(1)}, f32[512,512]{1,0:T(8,128)}, u32[]{:S(2)}) %copy-start.4) | copy-done | bytes 1048600
  41.3 1.0 %shard_map.117 = (bf16[528,512]{1,0:T(8,128)(2,1)S(1)}, bf16[8,32,128]{2,1,0:T(8,128)(2,1)S(1)}, f32[8,512]{1,0:T(8,128)S(1)}) custom-call(bf16[512,512]{1,0:T(8,128)(2,1)S(1)} %copy-done.2, f32[512,512]{1,0:T(8,128)S(1)} %copy-done.4, bf16[2,32,256]{2,1,0:T(8,128)(2,1)S(1)} %bitcast.4, bf16[2,32,256]{2,1,0:T(8,128)(2,1)S(1)} %bitcast.9, ...), custom_call_target="tpu_custom_call" | custom-call | tf_op jit(solution)/shard_map/pallas_call | solution.py:498
  42.3 0.8 collective-permute-start.4
  43.1 0.0 collective-permute-start.3
  43.1 1.0 %shard_map.118 = (bf16[528,512]{1,0:T(8,128)(2,1)S(1)}, bf16[8,80,128]{2,1,0:T(8,128)(2,1)S(1)}) custom-call(bf16[512,512]{1,0:T(8,128)(2,1)S(1)} %copy-done.2, f32[512,512]{1,0:T(8,128)S(1)} %get-tuple-element.18.near, bf16[2,32,256]{2,1,0:T(8,128)(2,1)S(1)} %bitcast.5, bf16[2,32,256]{2,1,0:T(8,128)(2,1)S(1)} %bitcast.10, ...), custom_call_target="tpu_custom_call" | custom-call | tf_op jit(solution)/shard_map/pallas_call | solution.py:505
  44.1 13.5 %all_to_all.21.refs_2_ = bf16[8,80,128]{2,1,0:T(8,128)(2,1)S(1)} all-to-all(bf16[8,80,128]{2,1,0:T(8,128)(2,1)S(1)} %get-tuple-element.21), channel_id=1, replica_groups={{0,2,4,6,8,10,12,14},{1,3,5,7,9,11,13,15},{16,18,20,22,24,26,28,30},{17..., dimensions={0} | all-to-all | bytes 327680 | tf_op jit(solution)/shard_map/all_to_all | solution.py:448
  57.6 0.0 collective-permute-start.5
  57.6 0.0 copy-start.1
  57.6 2.0 %collective-permute-start.7 = (bf16[528,512]{1,0:T(8,128)(2,1)S(1)}, bf16[528,512]{1,0:T(8,128)(2,1)S(1)}, u32[]{:S(2)}, u32[]{:S(2)}) collective-permute-start(bf16[528,512]{1,0:T(8,128)(2,1)S(1)} %get-tuple-element.23.vown), channel_id=1, source_target_pairs={{1,0},{2,1},{3,2},{4,3},{5,4},{6,5},{7,6},{8,7},{9,8},{10,9},{11,1... | collective-permute-start | bytes 1622024 | tf_op jit(solution)/shard_map/ppermute | solution.py:422
  59.6 0.0 collective-permute-start.6
  59.7 0.0 collective-permute-done.5.refs_3_
  59.7 0.0 collective-permute-done.4.after_high.vhigh
  59.7 0.0 collective-permute-done.3.after_low.vlow
  59.7 1.6 %shard_map.119 = bf16[8,80,128]{2,1,0:T(8,128)(2,1)S(1)} custom-call(s32[96]{0:T(128)S(1)} %reshape.18.cols, s32[1]{0:T(128)} %bitcast.3.group, bf16[528,512]{1,0:T(8,128)(2,1)S(1)} %collective-permute-done.3.after_low.vlow, bf16[528,512]{1,0:T(8,128)(2,1)S(1)} %collective-permute-done.4.after_high.vhigh, bf16[8,240,128]{2,1,0:T(8,128)(2,1)S(1)} %all-to-all-done.held, ...), custom_call_target="tpu_custom_call" | custom-call | flops 34500001792 | tf_op jit(solution)/shard_map/pallas_call | solution.py:514
  61.3 13.3 %all_to_all.22.cmsg = bf16[8,80,128]{2,1,0:T(8,128)(2,1)S(1)} all-to-all(bf16[8,80,128]{2,1,0:T(8,128)(2,1)S(1)} %shard_map.119), channel_id=1, replica_groups={{0,2,4,6,8,10,12,14},{1,3,5,7,9,11,13,15},{16,18,20,22,24,26,28,30},{17..., dimensions={0} | all-to-all | bytes 327680 | tf_op jit(solution)/shard_map/all_to_all | solution.py:448
  74.6 0.0 copy-done.1
  74.6 2.8 %shard_map.120 = (f32[2,512,512]{2,1,0:T(8,128)}, f32[2,512]{1,0:T(2,128)}, f32[2,512]{1,0:T(2,128)}, f32[8,512]{1,0:T(8,128)S(1)}) custom-call(bf16[2,512,1280]{2,1,0:T(8,128)(2,1)S(1)} %copy-done.1, bf16[512,512]{1,0:T(8,128)(2,1)S(1)} %collective-permute-done.low.ulow, bf16[512,512]{1,0:T(8,128)(2,1)S(1)} %copy-done.2, ...), custom_call_target="tpu_custom_call" | custom-call | tf_op jit(solution)/shard_map/pallas_call | solution.py:532
  77.5 0.0 collective-permute-done.7.vhigh
  77.5 0.0 collective-permute-done.6.vlow
  77.5 2.2 %shard_map.121 = f32[2,512,512]{2,1,0:T(8,128)} custom-call(f32[2,512,512]{2,1,0:T(8,128)} %get-tuple-element.22.begun, bf16[2,512,1280]{2,1,0:T(8,128)(2,1)S(1)} %copy-done.1, bf16[512,512]{1,0:T(8,128)(2,1)S(1)} %collective-permute-done.low.ulow, bf16[512,512]{1,0:T(8,128)(2,1)S(1)} %copy-done.2, ...), custom_call_target="tpu_custom_call", output_to_operand_aliasing={{}: (0, {})} | custom-call | tf_op jit(solution)/shard_map/pallas_call | solution.py:539
  (2 shorter events, 0.0 us)
Async XLA Ops:
  0.6 14.7 %collective-permute-start.1 = (bf16[512,512]{1,0:T(8,128)(2,1)}, bf16[512,512]{1,0:T(8,128)(2,1)S(1)}, u32[]{:S(2)}, u32[]{:S(2)}) collective-permute-start(bf16[512,512]{1,0:T(8,128)(2,1)} %uown.3), channel_id=1, source_target_pairs={{1,0},{2,1},{3,2},{4,3},{5,4},{6,5},{7,6},{8,7},{9,8},{10,9},{11,1... | collective-permute-start | bytes 1572872 | tf_op jit(solution)/shard_map/ppermute | solution.py:422
  6.1 11.7 %collective-permute-start = (bf16[512,512]{1,0:T(8,128)(2,1)}, bf16[512,512]{1,0:T(8,128)(2,1)S(1)}, u32[]{:S(2)}, u32[]{:S(2)}) collective-permute-start(bf16[512,512]{1,0:T(8,128)(2,1)} %uown.3), channel_id=1, source_target_pairs={{0,1},{1,2},{2,3},{3,4},{4,5},{5,6},{6,7},{7,8},{8,9},{9,10},{10,1... | collective-permute-start | bytes 1572872 | tf_op jit(solution)/shard_map/ppermute | solution.py:422
  8.3 17.1 %all-to-all-start = ((bf16[8,240,128]{2,1,0:T(8,128)(2,1)}), bf16[8,240,128]{2,1,0:T(8,128)(2,1)S(1)}, u32[]{:S(2)}, u32[]{:S(2)}) async-start(bf16[8,240,128]{2,1,0:T(8,128)(2,1)} %shard_map.112.after), calls=%async_computation | async-start | bytes 983040 | tf_op jit(solution)/shard_map/all_to_all | solution.py:448
  11.8 6.0 %copy-start.2 = (bf16[512,512]{1,0:T(8,128)(2,1)S(1)}, bf16[512,512]{1,0:T(8,128)(2,1)}, u32[]{:S(2)}) copy-start(bf16[512,512]{1,0:T(8,128)(2,1)} %uown.3) | copy-start | bytes 1572868
  11.8 6.0 %copy-start.7 = (f32[2,512]{1,0:T(2,128)S(1)}, f32[2,512]{1,0:T(2,128)}, u32[]{:S(2)}) copy-start(f32[2,512]{1,0:T(2,128)} %diag.5) | copy-start | bytes 12292
  11.8 28.2 %copy-start.5 = (bf16[2,256,32]{1,2,0:T(8,128)(2,1)S(1)}, bf16[2,256,32]{1,2,0:T(8,128)(2,1)}, u32[]{:S(2)}) copy-start(bf16[2,256,32]{1,2,0:T(8,128)(2,1)} %param.15) | copy-start | bytes 98308
  11.9 28.2 %copy-start.6 = (bf16[2,256,32]{1,2,0:T(8,128)(2,1)S(1)}, bf16[2,256,32]{1,2,0:T(8,128)(2,1)}, u32[]{:S(2)}) copy-start(bf16[2,256,32]{1,2,0:T(8,128)(2,1)} %param.16) | copy-start | bytes 98308
  17.8 1.7 %copy-start = (bf16[2,512,1280]{2,1,0:T(8,128)(2,1)S(1)}, bf16[2,512,1280]{2,1,0:T(8,128)(2,1)}, u32[]{:S(2)}) copy-start(bf16[2,512,1280]{2,1,0:T(8,128)(2,1)} %shard_map.113.w) | copy-start | bytes 7864324
  21.1 1.0 %copy-start.3 = (f32[512,512]{1,0:T(8,128)}, f32[512,512]{1,0:T(8,128)S(1)}, u32[]{:S(2)}) copy-start(f32[512,512]{1,0:T(8,128)S(1)} %get-tuple-element.15.near) | copy-start | bytes 3145732
  25.4 2.2 %collective-permute-start.2 = (bf16[8,32,128]{2,1,0:T(8,128)(2,1)S(1)}, bf16[8,32,128]{2,1,0:T(8,128)(2,1)S(1)}, u32[]{:S(2)}, u32[]{:S(2)}) collective-permute-start(bf16[8,32,128]{2,1,0:T(8,128)(2,1)S(1)} %shard_map.115.refs_0_), channel_id=1, source_target_pairs={{0,1},{1,0},{2,3},{3,2},{4,5},{5,4},{6,7},{7,6},{8,9},{9,8},{10,11... | collective-permute-start | bytes 196616 | tf_op jit(solution)/shard_map/ppermute | solution.py:454
  40.1 1.2 %copy-start.4 = (f32[512,512]{1,0:T(8,128)S(1)}, f32[512,512]{1,0:T(8,128)}, u32[]{:S(2)}) copy-start(f32[512,512]{1,0:T(8,128)} %copy-done.3) | copy-start | bytes 3145732
  42.3 17.4 %collective-permute-start.4 = (bf16[528,512]{1,0:T(8,128)(2,1)S(1)}, bf16[528,512]{1,0:T(8,128)(2,1)S(1)}, u32[]{:S(2)}, u32[]{:S(2)}) collective-permute-start(bf16[528,512]{1,0:T(8,128)(2,1)S(1)} %get-tuple-element.17.vown), channel_id=1, source_target_pairs={{1,0},{2,1},{3,2},{4,3},{5,4},{6,5},{7,6},{8,7},{9,8},{10,9},{11,1... | collective-permute-start | bytes 1622024 | tf_op jit(solution)/shard_map/ppermute | solution.py:422
  43.1 16.6 %collective-permute-start.3 = (bf16[528,512]{1,0:T(8,128)(2,1)S(1)}, bf16[528,512]{1,0:T(8,128)(2,1)S(1)}, u32[]{:S(2)}, u32[]{:S(2)}) collective-permute-start(bf16[528,512]{1,0:T(8,128)(2,1)S(1)} %get-tuple-element.17.vown), channel_id=1, source_target_pairs={{0,1},{1,2},{2,3},{3,4},{4,5},{5,6},{6,7},{7,8},{8,9},{9,10},{10,1... | collective-permute-start | bytes 1622024 | tf_op jit(solution)/shard_map/ppermute | solution.py:422
  57.6 2.1 %collective-permute-start.5 = (bf16[8,80,128]{2,1,0:T(8,128)(2,1)S(1)}, bf16[8,80,128]{2,1,0:T(8,128)(2,1)S(1)}, u32[]{:S(2)}, u32[]{:S(2)}) collective-permute-start(bf16[8,80,128]{2,1,0:T(8,128)(2,1)S(1)} %all_to_all.21.refs_2_), channel_id=1, source_target_pairs={{0,1},{1,0},{2,3},{3,2},{4,5},{5,4},{6,7},{7,6},{8,9},{9,8},{10,11... | collective-permute-start | bytes 491528 | tf_op jit(solution)/shard_map/ppermute | solution.py:454
  57.6 17.0 %copy-start.1 = (bf16[2,512,1280]{2,1,0:T(8,128)(2,1)S(1)}, bf16[2,512,1280]{2,1,0:T(8,128)(2,1)}, u32[]{:S(2)}) copy-start(bf16[2,512,1280]{2,1,0:T(8,128)(2,1)} %shard_map.113.w) | copy-start | bytes 7864324
  57.6 19.9 %collective-permute-start.7 = (bf16[528,512]{1,0:T(8,128)(2,1)S(1)}, bf16[528,512]{1,0:T(8,128)(2,1)S(1)}, u32[]{:S(2)}, u32[]{:S(2)}) collective-permute-start(bf16[528,512]{1,0:T(8,128)(2,1)S(1)} %get-tuple-element.23.vown), channel_id=1, source_target_pairs={{1,0},{2,1},{3,2},{4,3},{5,4},{6,5},{7,6},{8,7},{9,8},{10,9},{11,1... | collective-permute-start | bytes 1622024 | tf_op jit(solution)/shard_map/ppermute | solution.py:422
  59.6 17.8 %collective-permute-start.6 = (bf16[528,512]{1,0:T(8,128)(2,1)S(1)}, bf16[528,512]{1,0:T(8,128)(2,1)S(1)}, u32[]{:S(2)}, u32[]{:S(2)}) collective-permute-start(bf16[528,512]{1,0:T(8,128)(2,1)S(1)} %get-tuple-element.23.vown), channel_id=1, source_target_pairs={{0,1},{1,2},{2,3},{3,4},{4,5},{5,6},{6,7},{7,8},{8,9},{9,10},{10,1... | collective-permute-start | bytes 1622024 | tf_op jit(solution)/shard_map/ppermute | solution.py:422
